TPU v7x, 32 devices: a whole 2x2x4 slice. The times are simulated.
32 devices in a mesh: grp: 8 (over y, x, core), fft: 4 (over z).
Axes of the slice: x: 2, y: 2, z: 4, core: 2. Of those that a mesh axis runs over, the one named last changes fastest.
Arguments:
- patches: bfloat16 [48, 16, 16, 2560], P('grp', 'fft'), may hold values from -6 to 6
- targets: bfloat16 [48, 16, 16, 256], P('grp', 'fft'), may hold values from -6 to 6
- grid_side: int32 [48], replicated, may hold values from 4 to 16, as said below
- dest_group: int32 [48], replicated, may hold values from 0 to 7, as said below
- embed_w: bfloat16 [2560, 1024], replicated, may hold values from -0.125 to 0.125
- embed_b: float32 [1024], replicated, may hold values from -3 to 3
- gain: float32 [1024], replicated, may hold values from 0.5 to 1.5
- spec_w: bfloat16 [2, 2, 8, 128, 128], replicated, may hold values from -0.375 to 0.375
- spec_b: float32 [2, 2, 8, 128], replicated, may hold values from -3 to 3
- head_w: bfloat16 [1024, 256], replicated, may hold values from -0.1875 to 0.1875
- head_b: float32 [256], replicated, may hold values from -3 to 3
Outputs:
- predictions: bfloat16 [48, 16, 16, 256], P('grp', 'fft')
- embed_grad: float32 [2560, 1024], P(('grp', 'fft'))
- embed_bias_grad: float32 [1024], replicated
- gain_grad: float32 [1024], replicated
- spec_w_grad: float32 [2, 2, 8, 128, 128], replicated
- spec_b_grad: float32 [2, 2, 8, 128], replicated
- head_grad: float32 [1024, 256], replicated
- head_bias_grad: float32 [256], replicated
Inputs may be any that keep to these rules, and one draw needn't show every extreme that they name: `grid_side`: each entry is 16, 8 or 4, and 16 occurs in every draw. `dest_group`: every group index occurs exactly 6 times; the 6 samples held by one loader (indices q * 6 to q * 6 + 5) go to 6 different groups.
All inputs are finite; a program needn't handle non-finite values.
Results may differ from a plain program's by a relative error of at most 0.014.
The roundings to bfloat16 on the way count: a program that leaves them out, or rounds other values in their place, can miss the bound.
Values may be sent and summed in bfloat16 or wider, within the bound.
No kernel may reach another device: no remote copies, remote signals or barrier semaphores. Data moves between devices by JAX's collectives and lax.ppermute only.
A program may use at most 128 MiB of HBM per device.

v0:
```python
import jax
import jax.numpy as jnp
from jax import lax
from jax.sharding import PartitionSpec as P

EPSILON = 1e-05
SHRINK = 0.01
PRECISE = lax.Precision.HIGHEST


def to_half(values):
    return lax.optimization_barrier(values.astype(jnp.bfloat16))


def grid_valid(slot_edges, row_index, col_index):
    inside = (row_index[None, :, None] < slot_edges[:, None, None]) & (
        col_index[None, None, :] < slot_edges[:, None, None]
    )
    return jnp.where(inside, 1.0, 0.0).astype(jnp.float32)


def slot_tables(slot_edges, grid_cells):
    positions = jnp.arange(grid_cells, dtype=jnp.int32)
    product = positions[None, :, None] * positions[None, None, :] % slot_edges[:, None, None]
    inside = (positions[None, :, None] < slot_edges[:, None, None]) & (
        positions[None, None, :] < slot_edges[:, None, None]
    )
    edge_float = slot_edges.astype(jnp.float32)[:, None, None]
    angles = 2.0 * jnp.pi * product.astype(jnp.float32) / edge_float
    weights = jnp.where(inside, 1.0, 0.0).astype(jnp.float32) / jnp.sqrt(edge_float)
    return (jnp.cos(angles) * weights, jnp.sin(angles) * weights)


def embed_tokens(patch_grid, embed_w, embed_b, valid_mask):
    flat_rows = patch_grid.reshape(-1, patch_grid.shape[-1])
    mapped = jnp.dot(flat_rows, embed_w, preferred_element_type=jnp.float32) + embed_b
    mapped = mapped.reshape(valid_mask.shape + (embed_w.shape[1],)) * valid_mask[..., None]
    return to_half(mapped)


def normalize(embedded, gain):
    values = embedded.astype(jnp.float32)
    centered = values - jnp.mean(values, axis=-1, keepdims=True)
    inv_std = lax.rsqrt(jnp.mean(centered * centered, axis=-1, keepdims=True) + EPSILON)
    unit_norm = centered * inv_std
    return (unit_norm, inv_std, to_half(unit_norm * gain))


def normalize_back(normed_grad, unit_norm, inv_std, gain):
    unit_grad = normed_grad * gain
    mean_grad = jnp.mean(unit_grad, axis=-1, keepdims=True)
    mean_cross = jnp.mean(unit_grad * unit_norm, axis=-1, keepdims=True)
    return inv_std * (unit_grad - mean_grad - unit_norm * mean_cross)


def column_transform(cosines, sines, normed):
    values = normed.astype(jnp.float32)
    real_part = jnp.einsum("skc,srcd->srkd", cosines, values, precision=PRECISE)
    imag_part = -jnp.einsum("skc,srcd->srkd", sines, values, precision=PRECISE)
    return to_half(jnp.stack([real_part, imag_part]))


def row_transform(cosines, sines, columns):
    values = columns.astype(jnp.float32)

    def contract(table, operand):
        return jnp.einsum("smr,srkd->smkd", table, operand, precision=PRECISE)

    real_part = contract(cosines, values[0]) + contract(sines, values[1])
    imag_part = contract(cosines, values[1]) - contract(sines, values[0])
    return to_half(jnp.stack([real_part, imag_part]))


def row_inverse(cosines, sines, filtered):

    def contract(table, operand):
        return jnp.einsum("srm,smkd->srkd", table, operand, precision=PRECISE)

    real_part = contract(cosines, filtered[0]) - contract(sines, filtered[1])
    imag_part = contract(cosines, filtered[1]) + contract(sines, filtered[0])
    return to_half(jnp.stack([real_part, imag_part]))


def column_inverse(cosines, sines, inverse):
    values = inverse.astype(jnp.float32)

    def contract(table, operand):
        return jnp.einsum("sck,srkd->srcd", table, operand, precision=PRECISE)

    return contract(cosines, values[0]) - contract(sines, values[1])


def column_inverse_back(cosines, sines, gradient):

    def contract(table, operand):
        return jnp.einsum("sck,srcd->srkd", table, operand, precision=PRECISE)

    return to_half(jnp.stack([contract(cosines, gradient), -contract(sines, gradient)]))


def row_inverse_back(cosines, sines, gradient):
    values = gradient.astype(jnp.float32)

    def contract(table, operand):
        return jnp.einsum("srm,srkd->smkd", table, operand, precision=PRECISE)

    real_part = contract(cosines, values[0]) + contract(sines, values[1])
    imag_part = contract(cosines, values[1]) - contract(sines, values[0])
    return jnp.stack([real_part, imag_part])


def row_transform_back(cosines, sines, gradient):

    def contract(table, operand):
        return jnp.einsum("smr,smkd->srkd", table, operand, precision=PRECISE)

    real_part = contract(cosines, gradient[0]) - contract(sines, gradient[1])
    imag_part = contract(sines, gradient[0]) + contract(cosines, gradient[1])
    return to_half(jnp.stack([real_part, imag_part]))


def column_transform_back(cosines, sines, gradient):
    values = gradient.astype(jnp.float32)

    def contract(table, operand):
        return jnp.einsum("skc,srkd->srcd", table, operand, precision=PRECISE)

    return contract(cosines, values[0]) - contract(sines, values[1])


def block_mult(left_side, weights):
    return jnp.einsum("pbc,bce->pbe", left_side, weights, preferred_element_type=jnp.float32)


def block_outer(left_side, gradient):
    return jnp.einsum("pbc,pbe->bce", left_side, gradient, preferred_element_type=jnp.float32)


def block_back(gradient, weights):
    return jnp.einsum("pbe,bce->pbc", gradient, weights, preferred_element_type=jnp.float32)


def complex_block(real_part, imag_part, weight_re, weight_im):
    return (
        block_mult(real_part, weight_re) - block_mult(imag_part, weight_im),
        block_mult(imag_part, weight_re) + block_mult(real_part, weight_im),
    )


def spectral_mlp(spectrum, spec_w, spec_b):
    layer_one = complex_block(spectrum[0], spectrum[1], spec_w[0, 0], spec_w[0, 1])
    pre_one = jnp.stack([layer_one[0] + spec_b[0, 0], layer_one[1] + spec_b[0, 1]])
    hidden = to_half(jnp.maximum(pre_one, 0.0))
    layer_two = complex_block(hidden[0], hidden[1], spec_w[1, 0], spec_w[1, 1])
    pre_two = jnp.stack([layer_two[0] + spec_b[1, 0], layer_two[1] + spec_b[1, 1]])
    filtered = jnp.sign(pre_two) * jnp.maximum(jnp.abs(pre_two) - SHRINK, 0.0)
    return (pre_one, hidden, pre_two, filtered)


def layer_grads(inputs, gradient):
    weight_re = block_outer(inputs[0], gradient[0]) + block_outer(inputs[1], gradient[1])
    weight_im = block_outer(inputs[0], gradient[1]) - block_outer(inputs[1], gradient[0])
    return (jnp.stack([weight_re, weight_im]), jnp.sum(gradient.astype(jnp.float32), axis=1))


def input_grads(gradient, weight_re, weight_im):
    real_part = block_back(gradient[0], weight_re) + block_back(gradient[1], weight_im)
    imag_part = block_back(gradient[1], weight_re) - block_back(gradient[0], weight_im)
    return jnp.stack([real_part, imag_part])


def spectral_mlp_back(filtered_grad, spectrum, pre_one, hidden, pre_two, spec_w):
    two_grad = to_half(jnp.where(jnp.abs(pre_two) > SHRINK, filtered_grad, 0.0))
    weights_two, biases_two = layer_grads(hidden, two_grad)
    hidden_grad = input_grads(two_grad, spec_w[1, 0], spec_w[1, 1])
    one_grad = to_half(jnp.where(pre_one > 0.0, hidden_grad, 0.0))
    weights_one, biases_one = layer_grads(spectrum, one_grad)
    spectrum_grad = input_grads(one_grad, spec_w[0, 0], spec_w[0, 1])
    return (
        spectrum_grad,
        jnp.stack([weights_one, weights_two]),
        jnp.stack([biases_one, biases_two]),
    )


def head_pass(embedded, normed, mixed, valid_mask, head_w, head_b, target_grid, loss_scale):
    updated = to_half(embedded.astype(jnp.float32) + normed.astype(jnp.float32) + mixed)
    flat_rows = updated.reshape(-1, updated.shape[-1])
    output = jnp.dot(flat_rows, head_w, preferred_element_type=jnp.float32) + head_b
    output = output.reshape(valid_mask.shape + (head_w.shape[1],)) * valid_mask[..., None]
    residual_grad = to_half(
        loss_scale[:, None, None, None]
        * valid_mask[..., None]
        * (output - target_grid.astype(jnp.float32))
    )
    return (updated, output.astype(jnp.bfloat16), residual_grad)


def head_back(updated, residual_grad, head_w):
    flat_up = updated.reshape(-1, updated.shape[-1])
    flat_res = residual_grad.reshape(-1, residual_grad.shape[-1])
    head_grad = lax.dot_general(
        flat_up, flat_res, (((0,), (0,)), ((), ())), preferred_element_type=jnp.float32
    )
    bias_grad = jnp.sum(flat_res.astype(jnp.float32), axis=0)
    updated_grad = lax.dot_general(
        flat_res, head_w, (((1,), (1,)), ((), ())), preferred_element_type=jnp.float32
    )
    return (head_grad, bias_grad, to_half(updated_grad.reshape(updated.shape)))


def embedded_back(normed_spec_grad, updated_grad, unit_norm, inv_std, gain, valid_mask):
    direct = updated_grad.astype(jnp.float32)
    normed_grad = normed_spec_grad + direct
    gain_grad = jnp.sum(normed_grad * unit_norm, axis=(0, 1, 2))
    input_grad = normalize_back(normed_grad, unit_norm, inv_std, gain)
    return (gain_grad, to_half((input_grad + direct) * valid_mask[..., None]))


def route_blocks(tensor, chosen, filled):
    picked = jnp.take(tensor, chosen, axis=0)
    keep_mask = filled.reshape((-1,) + (1,) * (tensor.ndim - 1))
    return jnp.where(keep_mask, picked, jnp.zeros_like(picked))


def to_frequency(stacked):
    return lax.all_to_all(stacked, "fft", split_axis=3, concat_axis=2, tiled=True)


def to_rows(stacked):
    return lax.all_to_all(stacked, "fft", split_axis=2, concat_axis=3, tiled=True)


def on_device(
    patches, targets, grid_side, dest_group, embed_w, embed_b, gain, spec_w, spec_b, head_w, head_b
):
    slot_count = patches.shape[0]
    row_count = patches.shape[1]
    grid_cells = patches.shape[2]
    samples = dest_group.shape[0]
    groups = lax.axis_size("grp")
    group_at = lax.axis_index("grp")
    blocks = spec_w.shape[2]
    block_width = spec_w.shape[3]
    row_index = lax.axis_index("fft") * row_count + jnp.arange(row_count, dtype=jnp.int32)
    col_index = jnp.arange(grid_cells, dtype=jnp.int32)
    group_ids = jnp.arange(groups, dtype=jnp.int32)
    slot_ids = jnp.arange(slot_count, dtype=jnp.int32)
    own_dest = lax.dynamic_slice_in_dim(dest_group, group_at * slot_count, slot_count)
    matches = own_dest[None, :] == group_ids[:, None]
    chosen = jnp.sum(jnp.where(matches, slot_ids[None, :], 0), axis=1)
    filled = jnp.any(matches, axis=1)
    slot_order = jnp.argsort(dest_group, stable=True)
    slot_samples = lax.dynamic_slice_in_dim(slot_order, group_at * slot_count, slot_count)
    sources = slot_samples // slot_count
    slot_edges = jnp.take(grid_side, slot_samples)
    valid_mask = grid_valid(slot_edges, row_index, col_index)
    moved_patches, moved_targets = (
        lax.all_to_all(
            route_blocks(patches, chosen, filled), "grp", split_axis=0, concat_axis=0, tiled=True
        ),
        lax.all_to_all(
            route_blocks(targets, chosen, filled), "grp", split_axis=0, concat_axis=0, tiled=True
        ),
    )
    patch_slots = jnp.take(moved_patches, sources, axis=0)
    embedded = embed_tokens(patch_slots, embed_w, embed_b, valid_mask)
    target_slots = jnp.take(moved_targets, sources, axis=0)
    cosines, sines = slot_tables(slot_edges, grid_cells)
    unit_norm, inv_std, normed = normalize(embedded, gain)
    columns = to_frequency(column_transform(cosines, sines, normed))
    spectrum = row_transform(cosines, sines, columns)
    grid_shape = spectrum.shape
    flat_spectrum = spectrum.reshape(2, -1, blocks, block_width)
    pre_one, hidden, pre_two, filtered = spectral_mlp(flat_spectrum, spec_w, spec_b)
    inverse = to_rows(row_inverse(cosines, sines, filtered.reshape(grid_shape)))
    mixed = column_inverse(cosines, sines, inverse)
    loss_scale = 2.0 / (slot_edges.astype(jnp.float32) * jnp.sqrt(jnp.float32(samples)))
    updated, predicted, residual_grad = head_pass(
        embedded, normed, mixed, valid_mask, head_w, head_b, target_slots, loss_scale
    )
    head_grad, head_bias_grad, updated_grad = head_back(updated, residual_grad, head_w)
    inverse_grad = to_frequency(
        column_inverse_back(cosines, sines, updated_grad.astype(jnp.float32))
    )
    filtered_grad = row_inverse_back(cosines, sines, inverse_grad)
    spectrum_grad, spec_w_grad, spec_b_grad = spectral_mlp_back(
        filtered_grad.reshape(2, -1, blocks, block_width),
        flat_spectrum,
        pre_one,
        hidden,
        pre_two,
        spec_w,
    )
    columns_grad = to_rows(row_transform_back(cosines, sines, spectrum_grad.reshape(grid_shape)))
    normed_spec_grad = column_transform_back(cosines, sines, columns_grad)
    gain_grad, embedded_grad = embedded_back(
        normed_spec_grad, updated_grad, unit_norm, inv_std, gain, valid_mask
    )
    flat_patches = patch_slots.reshape(-1, patch_slots.shape[-1])
    flat_grads = embedded_grad.reshape(-1, embedded_grad.shape[-1])
    embed_bias_grad = jnp.sum(flat_grads.astype(jnp.float32), axis=0)
    devices = lax.axis_size(("grp", "fft"))
    row_share = flat_patches.shape[1] // devices
    whole_grad = lax.dot_general(
        flat_patches, flat_grads, (((0,), (0,)), ((), ())), preferred_element_type=jnp.float32
    )
    summed = lax.psum(
        (
            whole_grad,
            embed_bias_grad,
            gain_grad,
            spec_w_grad,
            spec_b_grad,
            head_grad,
            head_bias_grad,
        ),
        ("grp", "fft"),
    )
    embed_grad = lax.dynamic_slice_in_dim(
        summed[0], lax.axis_index(("grp", "fft")) * row_share, row_share
    )
    summed_rest = summed[1:]
    return (
        predicted,
        embed_grad,
        summed_rest[0],
        summed_rest[1],
        summed_rest[2],
        summed_rest[3],
        summed_rest[4],
        summed_rest[5],
    )


def solution(mesh):
    return jax.shard_map(
        on_device,
        mesh=mesh,
        in_specs=(
            P("grp", "fft", None, None),
            P("grp", "fft", None, None),
            P(),
            P(),
            P(),
            P(),
            P(),
            P(),
            P(),
            P(),
            P(),
        ),
        out_specs=(
            P("grp", "fft", None, None),
            P(("grp", "fft"), None),
            P(),
            P(),
            P(),
            P(),
            P(),
            P(),
        ),
        check_vma=False,
    )
```

profile of v0, /device:TPU:0, one launch (start us, length us, event | category | flops | bytes accessed | tf_op | source)
XLA Modules:
  0.0 623.6 jit_solution(11650878868742149831)
XLA Ops:
  8.7 2.2 gather_fusion
  11.0 3.6 select_select_fusion
  14.6 5.3 all-to-all-start
  19.9 2.0 sort.17
  23.9 28.3 %all-to-all-done = bf16[8,4,16,2560]{3,2,1,0:T(8,128)(2,1)} async-done(((bf16[8,4,16,2560]{3,2,1,0:T(8,128)(2,1)}), bf16[8,4,16,2560]{3,2,1,0:T(8,128)(2,1)}, u32[]{:S(2)}, u32[]{:S(2)}) %all-to-all-start) | async-done | bytes 2621472 | tf_op jit(solution)/shard_map/all_to_all | solution.py:259
  52.2 2.4 gather_fusion.1
  56.0 4.7 convolution_add_fusion.1
  64.9 2.4 copy.149
  67.3 5.6 all-to-all-start.1
  74.4 32.5 %all-to-all-done.1 = bf16[2,6,4,16,1024]{4,2,1,0,3:T(4,128)(2,1)S(1)} async-done(((bf16[2,6,4,16,1024]{4,2,1,0,3:T(4,128)(2,1)}), bf16[2,6,4,16,1024]{4,2,1,0,3:T(4,128)(2,1)S(1)}, u32[]{:S(2)}, u32[]{:S(2)}) %all-to-all-start.1) | async-done | bytes 1572896 | tf_op jit(solution)/shard_map/all_to_all | solution.py:227
  106.9 5.2 all-to-all-start.3
  135.5 2.1 copy.161
  137.5 1.8 squeeze.114
  139.3 3.9 fusion.30
  143.2 2.1 copy.164
  145.3 3.0 squeeze.115
  148.3 4.3 fusion.26
  152.6 2.8 fusion.32
  155.4 2.8 fusion.35
  158.3 2.4 copy.171
  160.7 3.8 all-to-all-start.2
  166.1 36.2 %all-to-all-done.2 = bf16[2,6,16,4,1024]{4,3,1,0,2:T(4,128)(2,1)S(1)} async-done(((bf16[2,6,16,4,1024]{4,3,1,0,2:T(4,128)(2,1)}), bf16[2,6,16,4,1024]{4,3,1,0,2:T(4,128)(2,1)S(1)}, u32[]{:S(2)}, u32[]{:S(2)}) %all-to-all-start.2) | async-done | bytes 1572896 | tf_op jit(solution)/shard_map/all_to_all | solution.py:231
  214.2 39.6 %all_to_all.70 = bf16[2,6,4,16,1024]{4,2,1,0,3:T(4,128)(2,1)S(1)} all-to-all(bf16[2,6,4,16,1024]{4,2,1,0,3:T(4,128)(2,1)S(1)} %copy.175), channel_id=1, replica_groups=mesh['grp'=8,'fft'=4] {'fft'}, dimensions={3} | all-to-all | bytes 3145728 | tf_op jit(solution)/shard_map/all_to_all | solution.py:227
  261.9 2.1 copy.180
  268.0 1.8 fusion
  275.8 2.1 copy.181
  277.9 2.8 squeeze.124
  280.6 5.4 fusion.22
  286.0 3.9 fusion.24
  291.2 2.1 copy.183
  293.2 3.0 squeeze.125
  296.2 4.7 fusion.41
  301.0 2.8 fusion.38
  304.0 2.4 copy.187
  306.3 4.3 all-to-all-start.5
  310.8 2.7 convolution_bitcast_fusion.1
  320.1 27.1 %all-to-all-done.5 = bf16[2,6,16,4,1024]{4,3,1,0,2:T(4,128)(2,1)} async-done(((bf16[2,6,16,4,1024]{4,3,1,0,2:T(4,128)(2,1)}), bf16[2,6,16,4,1024]{4,3,1,0,2:T(4,128)(2,1)}, u32[]{:S(2)}, u32[]{:S(2)}) %all-to-all-start.5) | async-done | bytes 1572896 | tf_op jit(solution)/shard_map/all_to_all | solution.py:231
  347.2 2.3 copy.270
  349.5 1.9 fusion.235
  351.5 2.5 squeeze.127
  354.0 2.3 squeeze.126
  356.2 2.7 fusion.115
  359.0 2.2 fusion.14
  362.9 5.6 convolution_bitcast_fusion
  369.8 39.6 %all-reduce = (f32[1024]{0:T(1024)}, f32[1024]{0:T(1024)}, f32[2,2,8,128]{3,2,1,0:T(8,128)}, f32[256]{0:T(256)}) all-reduce(f32[1024]{0:T(1024)S(1)} %convert_reduce_fusion.3, f32[1024]{0:T(1024)S(1)} %get-tuple-element.10, f32[2,2,8,128]{3,2,1,0:T(8,128)S(1)} %pad_maximum_fusion.8, ...), channel_id=1, replica_groups=mesh['grp'=8,'fft'=4] {'grp','fft'}, use_global_device_ids=true, to_apply=%region_9.10 | all-reduce | flops 6400 | bytes 51200 | tf_op jit(solution)/shard_map/psum | solution.py:308
  409.4 200.9 %all-reduce.4.cloned.1.call-done = (f32[2560,1024]{1,0:T(8,128)}, f32[2,2,8,128,128]{4,3,2,1,0:T(8,128)}, f32[1024,256]{1,0:T(8,128)}) async-done(((f32[2560,1024]{1,0:T(8,128)}, f32[2,2,8,128,128]{4,3,2,1,0:T(8,128)}, f32[1024,256]{1,0:T(8,128)}), (f32[2560,1024]{1,0:T(8,128)}, f32[2,2,8,128,128]{4,3,2,1,0:T(8,128)}, f32[1024,256]{1,0:T(8,128)})) %all-reduce.4.cloned.1.call-update) | async-done | bytes 13631504 | tf_op jit(solution)/shard_map/psum | solution.py:308
  610.3 1.7 constant_dynamic-slice_fusion
  612.0 3.3 copy.277
  (282 shorter events, 76.9 us)
Async XLA Ops:
  8.3 2.7 copy-start.73
  8.3 2.6 copy-start.75
  8.7 2.2 copy-start.69
  14.6 5.3 copy-start.79
  14.6 7.7 %copy-start.2 = (s32[48]{0:T(128)S(1)}, s32[48]{0:T(128)}, u32[]{:S(2)}) copy-start(s32[48]{0:T(128)} %param.13) | copy-start | bytes 580
  14.6 37.7 %all-to-all-start = ((bf16[8,4,16,2560]{3,2,1,0:T(8,128)(2,1)}), bf16[8,4,16,2560]{3,2,1,0:T(8,128)(2,1)}, u32[]{:S(2)}, u32[]{:S(2)}) async-start(bf16[8,4,16,2560]{3,2,1,0:T(8,128)(2,1)} %select_select_fusion), calls=%async_computation | async-start | bytes 5242880 | tf_op jit(solution)/shard_map/all_to_all | solution.py:259
  22.0 1.9 copy-start.70
  22.9 31.7 %copy-start.68 = (s32[1024]{0:T(1024)}, s32[1024]{0:T(1024)S(1)}, u32[]{:S(2)}) copy-start(s32[1024]{0:T(1024)S(1)} %pad_clamp_fusion.1) | copy-start | bytes 12292
  23.1 40.2 %copy-start.42 = (f32[6]{0:T(128)}, f32[6]{0:T(128)S(1)}, u32[]{:S(2)}) copy-start(f32[6]{0:T(128)S(1)} %convert_sqrt_fusion) | copy-start | bytes 76
  23.2 40.1 %copy-start.47 = (s32[6]{0:T(128)}, s32[6]{0:T(128)S(1)}, u32[]{:S(2)}) copy-start(s32[6]{0:T(128)S(1)} %get-tuple-element.44) | copy-start | bytes 76
  23.2 40.1 %copy-start.52 = (f32[6]{0:T(128)}, f32[6]{0:T(128)S(1)}, u32[]{:S(2)}) copy-start(f32[6]{0:T(128)S(1)} %get-tuple-element.45) | copy-start | bytes 76
  23.9 36.7 %copy-start.57 = (f32[6,4,16]{2,1,0:T(4,128)}, f32[6,4,16]{2,1,0:T(4,128)S(1)}, u32[]{:S(2)}) copy-start(f32[6,4,16]{2,1,0:T(4,128)S(1)} %get-tuple-element.43) | copy-start | bytes 4612
  60.8 145.3 %copy-start.5 = (bf16[6,4,16,1024]{3,2,1,0:T(8,128)(2,1)}, bf16[6,4,16,1024]{3,2,1,0:T(8,128)(2,1)S(1)}, u32[]{:S(2)}) copy-start(bf16[6,4,16,1024]{3,2,1,0:T(8,128)(2,1)S(1)} %multiply_convert_fusion) | copy-start | bytes 2359300
  61.0 2.2 copy-start.60
  61.4 1.8 copy-start.62
  61.7 3.0 copy-start.26
  67.3 5.6 copy-start.41
  67.3 6.3 %copy-start.65 = (f32[2,2,8,128]{3,2,1,0:T(8,128)S(1)}, f32[2,2,8,128]{3,2,1,0:T(8,128)}, u32[]{:S(2)}) copy-start(f32[2,2,8,128]{3,2,1,0:T(8,128)} %param.19) | copy-start | bytes 49156
  67.3 6.3 %copy-start.74 = (pred[8]{0:T(512)(128)(4,1)S(1)}, pred[8]{0:T(512)(128)(4,1)}, u32[]{:S(2)}) copy-start(pred[8]{0:T(512)(128)(4,1)} %copy-done.73) | copy-start | bytes 28
  67.3 6.3 %copy-start.76 = (pred[8]{0:T(512)(128)(4,1)S(1)}, pred[8]{0:T(512)(128)(4,1)}, u32[]{:S(2)}) copy-start(pred[8]{0:T(512)(128)(4,1)} %copy-done.75) | copy-start | bytes 28
  67.3 39.6 %all-to-all-start.1 = ((bf16[2,6,4,16,1024]{4,2,1,0,3:T(4,128)(2,1)}), bf16[2,6,4,16,1024]{4,2,1,0,3:T(4,128)(2,1)S(1)}, u32[]{:S(2)}, u32[]{:S(2)}) async-start(bf16[2,6,4,16,1024]{4,2,1,0,3:T(4,128)(2,1)} %copy.149), calls=%async_computation.1 | async-start | bytes 3145728 | tf_op jit(solution)/shard_map/all_to_all | solution.py:227
  106.9 53.8 %all-to-all-start.3 = ((bf16[8,4,16,256]{3,2,1,0:T(8,128)(2,1)}), bf16[8,4,16,256]{3,2,1,0:T(8,128)(2,1)}, u32[]{:S(2)}, u32[]{:S(2)}) async-start(bf16[8,4,16,256]{3,2,1,0:T(8,128)(2,1)} %select_select_fusion.1), calls=%async_computation.3 | async-start | bytes 524288 | tf_op jit(solution)/shard_map/all_to_all | solution.py:262
  123.0 4.8 copy-start.9
  124.2 2.8 copy-start.11
  139.3 3.9 copy-start.33
  148.3 4.3 copy-start.14
  148.3 4.3 copy-start.31
  160.7 41.7 %all-to-all-start.2 = ((bf16[2,6,16,4,1024]{4,3,1,0,2:T(4,128)(2,1)}), bf16[2,6,16,4,1024]{4,3,1,0,2:T(4,128)(2,1)S(1)}, u32[]{:S(2)}, u32[]{:S(2)}) async-start(bf16[2,6,16,4,1024]{4,3,1,0,2:T(4,128)(2,1)} %copy.171), calls=%async_computation.2 | async-start | bytes 3145728 | tf_op jit(solution)/shard_map/all_to_all | solution.py:231
  207.9 2.1 copy-start.35
  210.0 2.8 copy-start.24
  268.0 1.8 copy-start.12
  271.0 1.9 copy-start.19
  280.6 5.4 copy-start.15
  286.0 3.9 copy-start.32
  296.2 4.8 copy-start.13
  296.2 4.8 copy-start.30
  306.3 40.9 %all-to-all-start.5 = ((bf16[2,6,16,4,1024]{4,3,1,0,2:T(4,128)(2,1)}), bf16[2,6,16,4,1024]{4,3,1,0,2:T(4,128)(2,1)}, u32[]{:S(2)}, u32[]{:S(2)}) async-start(bf16[2,6,16,4,1024]{4,3,1,0,2:T(4,128)(2,1)} %copy.187), calls=%async_computation.5 | async-start | bytes 3145728 | tf_op jit(solution)/shard_map/all_to_all | solution.py:231
  310.7 299.6 %all-reduce.4.cloned.1.call-start = ((), (), s32[]{:S(2)}) async-start(), calls=%async_computation.6 | async-start | bytes 27262976 | tf_op jit(solution)/shard_map/psum | solution.py:308
  310.7 2.7 copy-start.10
  349.5 9.4 %copy-start.63 = (f32[6,4,16]{2,1,0:T(4,128)S(1)}, f32[6,4,16]{2,1,0:T(4,128)}, u32[]{:S(2)}) copy-start(f32[6,4,16]{2,1,0:T(4,128)} %copy-done.62) | copy-start | bytes 4612
  349.5 9.4 %copy-start.67 = (f32[1024]{0:T(1024)S(1)}, f32[1024]{0:T(1024)}, u32[]{:S(2)}) copy-start(f32[1024]{0:T(1024)} %param.17) | copy-start | bytes 12292
  356.2 2.7 copy-start.6
  356.2 2.7 copy-start.25
  356.2 2.7 copy-start.40
  356.2 2.7 copy-start.61
  359.0 2.2 copy-start.59
  612.0 3.3 copy-start.39
  612.0 4.3 copy-start.1
  (38 other events, 43.7 us)
Sparse Core Ops, SparseCore 0:
  368.6 241.6 all-reduce.3
where the time goes:
time: 631 us; the launch traced here: 624 us
  waiting for transfers between devices  325 us (52%)
  matrix products  80.8 us (13%)
  local copies, waits for them, and re-layouts  80.5 us (13%)
  blocking collectives  79.1 us (13%)
  starting transfers between devices  24.2 us (4%)
  other arithmetic  17.9 us (3%)
  between operations  16 us (3%)
    psum x1, waiting for transfers between devices, on_device(): lax.psum((whole_grad, embed_bias_grad, gain_grad, spec_w_grad, spec_b_gra...  201 us
    all_to_all x2, waiting for transfers between devices, to_rows(): lax.all_to_all(stacked, 'fft', split_axis=2, concat_axis=3, tiled=True)  63.3 us
    all_to_all x1, blocking collectives, to_frequency(): lax.all_to_all(stacked, 'fft', split_axis=3, concat_axis=2, tiled=True)  39.6 us
    psum x1, blocking collectives, on_device(): lax.psum((whole_grad, embed_bias_grad, gain_grad, spec_w_grad, spec_b_gra...  39.6 us
    all_to_all x1, waiting for transfers between devices, to_frequency(): lax.all_to_all(stacked, 'fft', split_axis=3, concat_axis=2, tiled=True)  32.5 us
    all_to_all x1, waiting for transfers between devices, on_device(): lax.all_to_all(route_blocks(patches, chosen, filled), 'grp', split_axis=0...  28.3 us
    dot_general x4, matrix products, contract(): return jnp.einsum('smr,smkd->srkd', table, operand, precision=PRECISE)  16.8 us
    unnamed x162, local copies, waits for them, and re-layouts  15.9 us
  transfers between devices with their start and end apart: 6, of which 5 were waited for; matrix products, arithmetic and copies ran while one was open for 10% of the time, Pallas kernels for 0%

commit v1 on v0

v1 whole, which is shorter than its diff:
```python
import jax
import jax.numpy as jnp
import ml_dtypes
import numpy as np
from jax import lax
from jax.experimental import pallas as pl
from jax.experimental.pallas import tpu as pltpu
from jax.sharding import PartitionSpec as P

EPSILON = 1e-05
SHRINK = 0.01
CHUNKS = 2
VMEM_BYTES = 48 * 1024 * 1024
HALF = jnp.bfloat16
FULL = jnp.float32


def dft_tables(cells):
    levels = []
    for side in (cells, cells // 2, cells // 4):
        k = np.arange(cells)
        inside = (k < side).astype(np.float64)
        keep = inside[:, None] * inside[None, :]
        angle = 2.0 * np.pi * ((k[:, None] * k[None, :]) % side) / side
        one = np.exp(-1j * angle) * keep / np.sqrt(side)
        two = np.kron(one, one)
        levels.append(np.concatenate([two.real, two.imag], axis=0))
    table = np.stack(levels)
    table[np.abs(table) < 1e-12] = 0.0
    high = table.astype(np.float32).astype(ml_dtypes.bfloat16)
    low = (table - high.astype(np.float64)).astype(np.float32).astype(ml_dtypes.bfloat16)
    size = cells * cells

    def back(values):
        return np.concatenate([values[:, :size], values[:, size:]], axis=2)

    return high, low, back(high), back(low)


def dot(left, right):
    return jnp.dot(left, right, preferred_element_type=FULL)


def dot_tn(left, right):
    return lax.dot_general(left, right, (((0,), (0,)), ((), ())), preferred_element_type=FULL)


def dot_nt(left, right):
    return lax.dot_general(left, right, (((1,), (1,)), ((), ())), preferred_element_type=FULL)


def params():
    return pltpu.CompilerParams(vmem_limit_bytes=VMEM_BYTES)


def token_sides(scal_ref, first, count, per_sample, cells):
    token = lax.broadcasted_iota(jnp.int32, (count * per_sample, 1), 0)
    sample = token // per_sample
    side = jnp.zeros_like(token)
    for i in range(count):
        side = jnp.where(sample == i, scal_ref[1 + first + i], side)
    row = scal_ref[0] + (token % per_sample) // cells
    col = token % cells
    valid = jnp.where((row < side) & (col < side), 1.0, 0.0).astype(FULL)
    return side, valid


def layer_norm(values):
    centered = values - jnp.mean(values, axis=-1, keepdims=True)
    inv_std = lax.rsqrt(jnp.mean(centered * centered, axis=-1, keepdims=True) + EPSILON)
    return centered * inv_std, inv_std


def gather_features(ref, rows):
    parts = [ref[z].reshape(rows, ref.shape[-1]) for z in range(ref.shape[0])]
    return jnp.concatenate(parts, axis=1)


def embed_chunk(scal, patches, embed_w, embed_b, gain, first, count, per_sample, cells, shards):
    rows = count * per_sample
    depth, width = embed_w.shape
    share = width // shards
    steps = 4
    tile = depth // steps

    def body(scal_ref, x_ref, w_ref, b_ref, gain_ref, emb_ref, out_ref, acc):
        step = pl.program_id(0)
        part = dot(x_ref[...], w_ref[...])

        @pl.when(step == 0)
        def _():
            acc[...] = part

        @pl.when(step > 0)
        def _():
            acc[...] += part

        @pl.when(step == steps - 1)
        def _():
            _, valid = token_sides(scal_ref, first, count, per_sample, cells)
            embedded = ((acc[...] + b_ref[...]) * valid).astype(HALF)
            emb_ref[...] = embedded
            unit, _ = layer_norm(embedded.astype(FULL))
            normed = (unit * gain_ref[...]).astype(HALF)
            for z in range(shards):
                out_ref[z] = normed[:, z * share : (z + 1) * share].reshape(count, per_sample, share)

    at = first // count
    return pl.pallas_call(
        body,
        grid_spec=pltpu.PrefetchScalarGridSpec(
            num_scalar_prefetch=1,
            grid=(steps,),
            in_specs=[
                pl.BlockSpec((rows, tile), lambda k, s: (at, k)),
                pl.BlockSpec((tile, width), lambda k, s: (k, 0)),
                pl.BlockSpec((1, width), lambda k, s: (0, 0)),
                pl.BlockSpec((1, width), lambda k, s: (0, 0)),
            ],
            out_specs=[
                pl.BlockSpec((rows, width), lambda k, s: (0, 0)),
                pl.BlockSpec((shards, count, per_sample, share), lambda k, s: (0, 0, 0, 0)),
            ],
            scratch_shapes=[pltpu.VMEM((rows, width), FULL)],
        ),
        out_shape=[
            jax.ShapeDtypeStruct((rows, width), HALF),
            jax.ShapeDtypeStruct((shards, count, per_sample, share), HALF),
        ],
        compiler_params=params(),
        cost_estimate=pl.CostEstimate(
            flops=2 * rows * depth * width, bytes_accessed=2 * depth * (rows + width), transcendentals=0
        ),
        name="embed",
    )(scal, patches, embed_w, embed_b, gain)


def to_blocks(values, blocks, width):
    half = values.shape[0] // 2
    return [
        jnp.concatenate(
            [values[:half, b * width : (b + 1) * width], values[half:, b * width : (b + 1) * width]], axis=1
        )
        for b in range(blocks)
    ]


def from_blocks(parts, width):
    real = jnp.concatenate([p[:, :width] for p in parts], axis=1)
    imag = jnp.concatenate([p[:, width:] for p in parts], axis=1)
    return jnp.concatenate([real, imag], axis=0)


def inverse_table(high_ref, low_ref, values):
    top = values.astype(HALF)
    rest = (values - top.astype(FULL)).astype(HALF)
    return dot(high_ref[0], top) + (dot(low_ref[0], top) + dot(high_ref[0], rest))


def level_specs(first, size):
    forward = pl.BlockSpec((1, 2 * size, size), lambda i, s: (s[1 + first + i], 0, 0))
    backward = pl.BlockSpec((1, size, 2 * size), lambda i, s: (s[1 + first + i], 0, 0))
    return [forward, forward, backward, backward]


def spectral_chunk(scal, tables, moved, weights, biases, first):
    shards, count, per_sample, share = moved.shape
    size = shards * per_sample
    blocks, wide = weights.shape[1], weights.shape[2]
    width = wide // 2

    def body(s_ref, th, tl, bh, bl, x_ref, w_ref, b_ref, out_ref, spec_ref, hid_ref, fil_ref):
        grid = jnp.concatenate([x_ref[z, 0] for z in range(shards)], axis=0)
        spectrum = (dot(th[0], grid) + dot(tl[0], grid)).astype(HALF)
        kept = []
        for b, entry in enumerate(to_blocks(spectrum, blocks, width)):
            spec_ref[0, b] = entry
            pre_one = dot(entry, w_ref[0, b]) + b_ref[0, b : b + 1]
            hidden = jnp.maximum(pre_one, 0.0).astype(HALF)
            hid_ref[0, b] = hidden
            pre_two = dot(hidden, w_ref[1, b]) + b_ref[1, b : b + 1]
            filtered = jnp.where(
                pre_two > SHRINK, pre_two - SHRINK, jnp.where(pre_two < -SHRINK, pre_two + SHRINK, 0.0)
            )
            fil_ref[0, b] = filtered.astype(HALF)
            kept.append(filtered)
        mixed = inverse_table(bh, bl, from_blocks(kept, width)).astype(HALF)
        for z in range(shards):
            out_ref[z, 0] = mixed[z * per_sample : (z + 1) * per_sample]

    grid_block = pl.BlockSpec((shards, 1, per_sample, share), lambda i, s: (0, i, 0, 0))
    saved = pl.BlockSpec((1, blocks, size, wide), lambda i, s: (i, 0, 0, 0))
    saved_shape = jax.ShapeDtypeStruct((count, blocks, size, wide), HALF)
    return pl.pallas_call(
        body,
        grid_spec=pltpu.PrefetchScalarGridSpec(
            num_scalar_prefetch=1,
            grid=(count,),
            in_specs=level_specs(first, size)
            + [
                grid_block,
                pl.BlockSpec(weights.shape, lambda i, s: (0, 0, 0, 0)),
                pl.BlockSpec(biases.shape, lambda i, s: (0, 0, 0)),
            ],
            out_specs=[grid_block, saved, saved, saved],
        ),
        out_shape=[jax.ShapeDtypeStruct(moved.shape, HALF), saved_shape, saved_shape, saved_shape],
        compiler_params=params(),
        cost_estimate=pl.CostEstimate(
            flops=count * size * share * size * 20, bytes_accessed=count * size * share * 16, transcendentals=0
        ),
        name="spectral",
    )(scal[1], *tables, moved, weights, biases)


def head_chunk(scal, embedded, gain, mixed, targets, head_w, head_b, first, samples, cells):
    shards, count, per_sample, share = mixed.shape
    rows = count * per_sample
    width, outs = head_w.shape
    at = first // count
    scale_root = float(np.sqrt(np.float32(samples)))

    def body(scal_ref, emb_ref, gain_ref, mix_ref, tgt_ref, w_ref, b_ref, pred_ref, res_ref, grad_ref, bias_ref):
        side, valid = token_sides(scal_ref, first, count, per_sample, cells)
        embedded = emb_ref[...].astype(FULL)
        unit, _ = layer_norm(embedded)
        normed = (unit * gain_ref[...]).astype(HALF)
        mixed = gather_features(mix_ref, rows)
        updated = (embedded + normed.astype(FULL) + mixed.astype(FULL)).astype(HALF)
        output = (dot(updated, w_ref[...]) + b_ref[...]) * valid
        pred_ref[...] = output.astype(HALF)
        scale = 2.0 / (side.astype(FULL) * scale_root)
        residual = (scale * valid * (output - tgt_ref[...].astype(FULL))).astype(HALF)
        res_ref[...] = residual
        grad_ref[...] = dot_tn(updated, residual)
        total = jnp.sum(residual.astype(FULL), axis=0, keepdims=True)
        bias_ref[...] = jnp.broadcast_to(total, bias_ref.shape)

    def whole(shape):
        return pl.BlockSpec(shape, lambda i, s: (0,) * len(shape))

    return pl.pallas_call(
        body,
        grid_spec=pltpu.PrefetchScalarGridSpec(
            num_scalar_prefetch=1,
            grid=(1,),
            in_specs=[
                whole((rows, width)),
                whole((1, width)),
                whole(mixed.shape),
                pl.BlockSpec((rows, outs), lambda i, s: (at, 0)),
                whole((width, outs)),
                whole((1, outs)),
            ],
            out_specs=[whole((rows, outs)), whole((rows, outs)), whole((width, outs)), whole((8, outs))],
        ),
        out_shape=[
            jax.ShapeDtypeStruct((rows, outs), HALF),
            jax.ShapeDtypeStruct((rows, outs), HALF),
            jax.ShapeDtypeStruct((width, outs), FULL),
            jax.ShapeDtypeStruct((8, outs), FULL),
        ],
        compiler_params=params(),
        cost_estimate=pl.CostEstimate(
            flops=4 * rows * width * outs, bytes_accessed=rows * width * 4 + width * outs * 6, transcendentals=0
        ),
        name="head",
    )(scal, embedded, gain, mixed, targets, head_w, head_b)


def spectral_back_chunk(scal, tables, residual, head_w, weights_t, spectrum, hidden, filtered, first):
    shards, count, per_sample, outs = residual.shape
    size = shards * per_sample
    blocks, wide = weights_t.shape[1], weights_t.shape[2]
    width = wide // 2
    share = blocks * width

    def body(s_ref, th, tl, bh, bl, r_ref, h_ref, w_ref, spec_ref, hid_ref, fil_ref, out_ref, grad_ref, bias_ref):
        @pl.when(pl.program_id(0) == 0)
        def _():
            grad_ref[...] = jnp.zeros_like(grad_ref)
            bias_ref[...] = jnp.zeros_like(bias_ref)

        residual = jnp.concatenate([r_ref[z, 0] for z in range(shards)], axis=0)
        updated_grad = dot_nt(residual, h_ref[...]).astype(HALF)
        filtered_grad = dot(th[0], updated_grad) + dot(tl[0], updated_grad)
        kept = []
        for b, entry in enumerate(to_blocks(filtered_grad, blocks, width)):
            two_grad = jnp.where(fil_ref[0, b].astype(FULL) != 0.0, entry, 0.0).astype(HALF)
            hidden = hid_ref[0, b]
            grad_ref[1, b] += dot_tn(hidden, two_grad)
            bias_ref[1, b : b + 1] += jnp.sum(two_grad.astype(FULL), axis=0, keepdims=True)
            hidden_grad = dot(two_grad, w_ref[1, b])
            one_grad = jnp.where(hidden.astype(FULL) > 0.0, hidden_grad, 0.0).astype(HALF)
            grad_ref[0, b] += dot_tn(spec_ref[0, b], one_grad)
            bias_ref[0, b : b + 1] += jnp.sum(one_grad.astype(FULL), axis=0, keepdims=True)
            kept.append(dot(one_grad, w_ref[0, b]))
        grad = inverse_table(bh, bl, from_blocks(kept, width)).astype(HALF)
        for z in range(shards):
            out_ref[z, 0] = grad[z * per_sample : (z + 1) * per_sample]

    saved = pl.BlockSpec((1, blocks, size, wide), lambda i, s: (i, 0, 0, 0))
    return pl.pallas_call(
        body,
        grid_spec=pltpu.PrefetchScalarGridSpec(
            num_scalar_prefetch=1,
            grid=(count,),
            in_specs=level_specs(first, size)
            + [
                pl.BlockSpec((shards, 1, per_sample, outs), lambda i, s: (0, i, 0, 0)),
                pl.BlockSpec((share, outs), lambda i, s: (s[0], 0)),
                pl.BlockSpec(weights_t.shape, lambda i, s: (0, 0, 0, 0)),
                saved,
                saved,
                saved,
            ],
            out_specs=[
                pl.BlockSpec((shards, 1, per_sample, share), lambda i, s: (0, i, 0, 0)),
                pl.BlockSpec((2, blocks, wide, wide), lambda i, s: (0, 0, 0, 0)),
                pl.BlockSpec((2, blocks, wide), lambda i, s: (0, 0, 0)),
            ],
        ),
        out_shape=[
            jax.ShapeDtypeStruct((shards, count, per_sample, share), HALF),
            jax.ShapeDtypeStruct((2, blocks, wide, wide), FULL),
            jax.ShapeDtypeStruct((2, blocks, wide), FULL),
        ],
        compiler_params=params(),
        cost_estimate=pl.CostEstimate(
            flops=count * size * share * size * 24, bytes_accessed=count * size * share * 16, transcendentals=0
        ),
        name="spectral_back",
    )(scal[1], *tables, residual, head_w, weights_t, spectrum, hidden, filtered)


def embedded_back_chunk(scal, embedded, residual, head_w, gain, spec_grad, first, cells):
    shards, count, per_sample, share = spec_grad.shape
    rows = count * per_sample
    width, outs = head_w.shape

    def body(scal_ref, emb_ref, res_ref, w_ref, gain_ref, grad_ref, out_ref, sums_ref):
        _, valid = token_sides(scal_ref, first, count, per_sample, cells)
        unit, inv_std = layer_norm(emb_ref[...].astype(FULL))
        direct = dot_nt(res_ref[...], w_ref[...]).astype(HALF).astype(FULL)
        normed_grad = gather_features(grad_ref, rows).astype(FULL) + direct
        gain_grad = jnp.sum(normed_grad * unit, axis=0, keepdims=True)
        unit_grad = normed_grad * gain_ref[...]
        mean_grad = jnp.mean(unit_grad, axis=-1, keepdims=True)
        mean_cross = jnp.mean(unit_grad * unit, axis=-1, keepdims=True)
        input_grad = inv_std * (unit_grad - mean_grad - unit * mean_cross)
        result = ((input_grad + direct) * valid).astype(HALF)
        out_ref[...] = result
        bias_grad = jnp.sum(result.astype(FULL), axis=0, keepdims=True)
        sums_ref[0:4] = jnp.broadcast_to(gain_grad, (4, width))
        sums_ref[4:8] = jnp.broadcast_to(bias_grad, (4, width))

    def whole(shape):
        return pl.BlockSpec(shape, lambda i, s: (0,) * len(shape))

    return pl.pallas_call(
        body,
        grid_spec=pltpu.PrefetchScalarGridSpec(
            num_scalar_prefetch=1,
            grid=(1,),
            in_specs=[
                whole((rows, width)),
                whole((rows, outs)),
                whole((width, outs)),
                whole((1, width)),
                whole(spec_grad.shape),
            ],
            out_specs=[whole((rows, width)), whole((8, width))],
        ),
        out_shape=[jax.ShapeDtypeStruct((rows, width), HALF), jax.ShapeDtypeStruct((8, width), FULL)],
        compiler_params=params(),
        cost_estimate=pl.CostEstimate(
            flops=2 * rows * width * outs, bytes_accessed=rows * width * 6, transcendentals=0
        ),
        name="embedded_back",
    )(scal, embedded, residual, head_w, gain, spec_grad)


def embed_grad_parts(group_at, patches, grads, groups):
    tokens, depth = patches.shape
    width = grads[0].shape[1]
    block = depth // groups
    tile = 256
    piece = int(np.gcd(tile, block))
    per_block = block // piece
    count = len(grads)

    def body(at_ref, x_ref, *refs):
        grad_refs, (send_ref, keep_ref) = refs[:count], refs[count:]
        total, row = None, 0
        for ref in grad_refs:
            part = dot_tn(x_ref[row : row + ref.shape[0]], ref[...])
            total = part if total is None else total + part
            row += ref.shape[0]
        total = total.astype(HALF)
        for i in range(tile // piece):
            place = pl.program_id(0) * (tile // piece) + i
            relative = jnp.bitwise_xor(place // per_block, at_ref[0])
            at = relative // 2
            rows = pl.ds(pl.multiple_of((place % per_block) * piece, piece), piece)
            values = total[i * piece : (i + 1) * piece]

            @pl.when(relative % 2 == 1)
            def _(at=at, rows=rows, values=values):
                send_ref[at, rows] = values

            @pl.when(relative % 2 == 0)
            def _(at=at, rows=rows, values=values):
                keep_ref[at, rows] = values

    shape = (groups // 2, block, width)
    out = pl.BlockSpec(shape, lambda i, s: (0, 0, 0))
    return pl.pallas_call(
        body,
        grid_spec=pltpu.PrefetchScalarGridSpec(
            num_scalar_prefetch=1,
            grid=(depth // tile,),
            in_specs=[pl.BlockSpec((tokens, tile), lambda i, s: (0, i))]
            + [pl.BlockSpec(g.shape, lambda i, s: (0, 0)) for g in grads],
            out_specs=[out, out],
        ),
        out_shape=[jax.ShapeDtypeStruct(shape, HALF)] * 2,
        compiler_params=params(),
        cost_estimate=pl.CostEstimate(
            flops=2 * tokens * depth * width, bytes_accessed=depth * (tokens + width) * 2, transcendentals=0
        ),
        name="embed_grad",
    )(group_at, patches, *grads)


def swap_bit(values, bit, groups):
    return lax.ppermute(values, "grp", [(g, g ^ (1 << bit)) for g in range(groups)])


def add_half(left, right):
    return (left.astype(FULL) + right.astype(FULL)).astype(HALF)


def scatter_sum(send, keep, groups):
    bits = groups.bit_length() - 1
    shards = lax.axis_size("fft")
    total = add_half(keep, swap_bit(send, 0, groups))
    block, width = total.shape[1:]
    total = total.reshape((2,) * (bits - 1) + (block, width))
    done = []
    for turn in range(2):
        part = total[..., turn * (width // 2) : (turn + 1) * (width // 2)]
        left = list(range(1, bits))
        order = list(left) if turn == 0 else left[::-1]
        for bit in order:
            axis = len(left) - 1 - left.index(bit)
            left.remove(bit)
            moving = lax.index_in_dim(part, 1, axis, keepdims=False)
            staying = lax.index_in_dim(part, 0, axis, keepdims=False)
            part = add_half(staying, swap_bit(moving, bit, groups))
        done.append(part)
    part = jnp.concatenate(done, axis=-1).reshape(shards, block // shards, width)
    moved = lax.all_to_all(part, "fft", split_axis=0, concat_axis=0, tiled=True)
    return jnp.sum(moved.astype(FULL), axis=0)


def across(values):
    return lax.all_to_all(values, "fft", split_axis=0, concat_axis=0, tiled=True)


def route_predictions(predicted, dest_group, group_at, groups, slot_count):
    own_dest = lax.dynamic_slice_in_dim(dest_group, group_at * slot_count, slot_count)
    matches = own_dest[None, :] == jnp.arange(groups, dtype=jnp.int32)[:, None]
    chosen = jnp.sum(jnp.where(matches, jnp.arange(slot_count, dtype=jnp.int32)[None, :], 0), axis=1)
    outgoing = jnp.take(predicted, chosen, axis=0)
    moved = lax.all_to_all(outgoing, "grp", split_axis=0, concat_axis=0, tiled=True)
    slot_order = jnp.argsort(dest_group, stable=True)
    slot_samples = lax.dynamic_slice_in_dim(slot_order, group_at * slot_count, slot_count)
    return jnp.take(moved, slot_samples // slot_count, axis=0)


def on_device(
    patches, targets, grid_side, dest_group, embed_w, embed_b, gain, spec_w, spec_b, head_w, head_b
):
    slot_count, row_count, cells, depth = patches.shape
    samples = dest_group.shape[0]
    groups = lax.axis_size("grp")
    shards = lax.axis_size("fft")
    group_at = lax.axis_index("grp")
    shard_at = lax.axis_index("fft")
    outs = targets.shape[-1]
    width = embed_w.shape[1]
    blocks = spec_w.shape[2] // shards
    per_sample = row_count * cells
    count = slot_count // CHUNKS
    firsts = [c * count for c in range(CHUNKS)]

    sides = lax.dynamic_slice_in_dim(grid_side, group_at * slot_count, slot_count)
    level = jnp.where(sides == cells, 0, jnp.where(sides == cells // 2, 1, 2)).astype(jnp.int32)
    row_scal = jnp.concatenate([jnp.reshape(shard_at * row_count, (1,)).astype(jnp.int32), sides])
    level_scal = jnp.concatenate([jnp.reshape(shard_at, (1,)).astype(jnp.int32), level])
    tables = [jnp.asarray(t) for t in dft_tables(cells)]
    both = (row_scal, level_scal)
    flat_patches = patches.reshape(-1, depth)
    flat_targets = targets.reshape(-1, outs)
    gain_row, embed_b_row, head_b_row = gain[None], embed_b[None], head_b[None]

    own_w = lax.dynamic_slice_in_dim(spec_w, shard_at * blocks, blocks, axis=2)
    real, imag = own_w[:, 0], own_w[:, 1]
    weights = jnp.concatenate(
        [jnp.concatenate([real, imag], axis=-1), jnp.concatenate([-imag, real], axis=-1)], axis=-2
    )
    weights_t = jnp.swapaxes(weights, -1, -2)
    own_b = lax.dynamic_slice_in_dim(spec_b, shard_at * blocks, blocks, axis=2)
    biases = jnp.concatenate([own_b[:, 0], own_b[:, 1]], axis=-1)

    embedded, moved = [], []
    for first in firsts:
        emb, normed = embed_chunk(
            row_scal, flat_patches, embed_w, embed_b_row, gain_row, first, count, per_sample, cells, shards
        )
        embedded.append(emb)
        moved.append(across(normed))
    mixed, saved = [], []
    for first, values in zip(firsts, moved):
        out, *rest = spectral_chunk(both, tables, values, weights, biases, first)
        mixed.append(across(out))
        saved.append(rest)
    predicted, residual, head_grads, head_sums, gathered = [], [], [], [], []
    for first, emb, mix in zip(firsts, embedded, mixed):
        pred, res, grad, sums = head_chunk(
            row_scal, emb, gain_row, mix, flat_targets, head_w, head_b_row, first, samples, cells
        )
        predicted.append(pred)
        residual.append(res)
        head_grads.append(grad)
        head_sums.append(sums[0])
        gathered.append(lax.all_gather(res.reshape(count, per_sample, outs), "fft"))
    spec_back, weight_sums, bias_sums = [], [], []
    for first, res, rest in zip(firsts, gathered, saved):
        back, grad, sums = spectral_back_chunk(both, tables, res, head_w, weights_t, *rest, first)
        spec_back.append(across(back))
        weight_sums.append(grad)
        bias_sums.append(sums)
    embedded_grads, row_sums = [], []
    for first, emb, res, back in zip(firsts, embedded, residual, spec_back):
        grad, sums = embedded_back_chunk(row_scal, emb, res, head_w, gain_row, back, first, cells)
        embedded_grads.append(grad)
        row_sums.append(sums)
    send, keep = embed_grad_parts(
        jnp.reshape(group_at, (1,)).astype(jnp.int32), flat_patches, embedded_grads, groups
    )
    embed_grad = scatter_sum(send, keep, groups)

    predictions = route_predictions(
        jnp.concatenate(predicted, axis=0).reshape(slot_count, per_sample, outs),
        dest_group,
        group_at,
        groups,
        slot_count,
    ).reshape(targets.shape)

    head_grad, head_bias_grad = lax.psum((sum(head_grads), sum(head_sums)), ("grp", "fft"))
    raw = sum(weight_sums)
    half = raw.shape[-1] // 2
    spec_real = raw[:, :, :half, :half] + raw[:, :, half:, half:]
    spec_imag = raw[:, :, :half, half:] - raw[:, :, half:, :half]
    raw_b = sum(bias_sums)
    spec_part = jnp.stack([spec_real, spec_imag], axis=1)
    bias_part = jnp.stack([raw_b[..., :half], raw_b[..., half:]], axis=1)
    spec_part, bias_part = lax.psum((spec_part, bias_part), "grp")
    spec_w_grad = lax.all_gather(spec_part, "fft", axis=2, tiled=True)
    spec_b_grad = lax.all_gather(bias_part, "fft", axis=2, tiled=True)
    rows = sum(row_sums)
    gain_grad, embed_bias_grad = lax.psum((rows[0], rows[4]), ("grp", "fft"))
    return (
        predictions,
        embed_grad,
        embed_bias_grad,
        gain_grad,
        spec_w_grad,
        spec_b_grad,
        head_grad,
        head_bias_grad,
    )


def solution(mesh):
    return jax.shard_map(
        on_device,
        mesh=mesh,
        in_specs=(
            P("grp", "fft", None, None),
            P("grp", "fft", None, None),
            P(),
            P(),
            P(),
            P(),
            P(),
            P(),
            P(),
            P(),
            P(),
        ),
        out_specs=(
            P("grp", "fft", None, None),
            P(("grp", "fft"), None),
            P(),
            P(),
            P(),
            P(),
            P(),
            P(),
        ),
        check_vma=False,
    )
```

time: 631 us -> 439 us (0.70)
  waiting for transfers between devices: 325 us -> 162 us
  matrix products: 80.8 us -> 0 us
  Pallas kernels: 0 us -> 55.1 us
  local copies, waits for them, and re-layouts: 80.5 us -> 48.2 us
  blocking collectives: 79.1 us -> 96.5 us
  starting transfers between devices: 24.2 us -> 40.8 us
    all_to_all x5 -> x8, waiting for transfers between devices: 124 us -> 11.1 us  [the longest x6 8.45 us: across(): lax.all_to_all(values, 'fft', split_axis=0, concat_axis=0, tiled=True)]
    dot_general x53 -> x0, matrix products: 80.8 us -> none  [the longest x4 16.8 us: contract(): return jnp.einsum('smr,smkd->srkd', table, operand, precision=PRECISE)]
    psum x1 -> x2, waiting for transfers between devices: 201 us -> 136 us  [the longest x1 84 us: on_device(): lax.psum((sum(head_grads), sum(head_sums)), ('grp', 'fft'))]
    pallas_call x0 -> x11, Pallas kernels: none -> 55.1 us  [the longest x2 15.1 us: spectral_back_chunk(): pl.pallas_call(body, grid_spec=pltpu.PrefetchScalarGridSpec(num_scalar_pr...]
    all_gather x0 -> x3, blocking collectives: none -> 45 us  [the longest x2 31 us: on_device(): gathered.append(lax.all_gather(res.reshape(count, per_sample, outs), 'fft'))]
    all_to_all x1 -> x0, blocking collectives: 39.6 us -> none  [to_frequency(): lax.all_to_all(stacked, 'fft', split_axis=3, concat_axis=2, tiled=True)]
    unnamed x162 -> x125, local copies, waits for them, and re-layouts: 15.9 us -> 40.8 us
    squeeze x16 -> x5, local copies, waits for them, and re-layouts: 19.9 us -> 3.32 us  [the longest x4 2.6 us: scatter_sum(): moving = lax.index_in_dim(part, 1, axis, keepdims=False)]
  transfers between devices with their start and end apart: 6 -> 16, of which waited for: 5 -> 8; matrix products, arithmetic and copies ran while one was open for 10% -> 7% of each run, Pallas kernels for 0% -> 9%
where the time goes in v1:
time: 439 us; the launch traced here: 437 us
  waiting for transfers between devices  162 us (37%)
  blocking collectives  96.5 us (22%)
  Pallas kernels  55.1 us (13%)
  local copies, waits for them, and re-layouts  48.2 us (11%)
  starting transfers between devices  40.8 us (9%)
  other arithmetic  18.5 us (4%)
  between operations  16 us (4%)
    psum x1, waiting for transfers between devices, on_device(): lax.psum((sum(head_grads), sum(head_sums)), ('grp', 'fft'))  84 us
    psum x1, waiting for transfers between devices, on_device(): spec_part, bias_part = lax.psum((spec_part, bias_part), 'grp')  51.8 us
    unnamed x125, local copies, waits for them, and re-layouts  40.8 us
    psum x1, blocking collectives, on_device(): gain_grad, embed_bias_grad = lax.psum((rows[0], rows[4]), ('grp', 'fft'))  39.6 us
    all_gather x2, blocking collectives, on_device(): gathered.append(lax.all_gather(res.reshape(count, per_sample, outs), 'fft'))  31 us
    all_to_all x6, starting transfers between devices, across(): lax.all_to_all(values, 'fft', split_axis=0, concat_axis=0, tiled=True)  29.3 us
    pallas_call x2, Pallas kernels, spectral_back_chunk(): pl.pallas_call(body, grid_spec=pltpu.PrefetchScalarGridSpec(num_scalar_pr...  15.1 us
    ppermute x5, waiting for transfers between devices, swap_bit(): lax.ppermute(values, 'grp', [(g, g ^ 1 << bit) for g in range(groups)])  15.1 us
  transfers between devices with their start and end apart: 16, of which 8 were waited for; matrix products, arithmetic and copies ran while one was open for 7% of the time, Pallas kernels for 9%

profile of v1, /device:TPU:0, one launch (start us, length us, event | category | flops | bytes accessed | tf_op | source)
XLA Modules:
  0.0 437.2 jit_solution(8309008030347171630)
XLA Ops:
  8.8 1.5 copy-done.8
  11.7 6.2 %embed.2 = (bf16[192,1024]{1,0:T(8,128)(2,1)S(1)}, bf16[4,3,64,256]{3,2,1,0:T(8,128)(2,1)}) custom-call(s32[7]{0:T(128)S(1)} %pad_add_fusion.scal_ref, bf16[384,2560]{1,0:T(8,128)(2,1)S(1)} %bitcast.74, bf16[2560,1024]{1,0:T(8,128)(2,1)} %w_ref.8, f32[1,1024]{1,0:T(1,128)S(1)} %bitcast.87, f32[1,1024]{1,0:T(1,128)S(1)} %bitcast.81), custom_call_target="tpu_custom_call" | custom-call | flops 1006632960 | bytes 6225920 | tf_op jit(solution)/shard_map/embed/pallas_call | solution.py:109
  18.7 6.3 %all-to-all-start = ((bf16[4,3,64,256]{3,2,1,0:T(8,128)(2,1)}), bf16[4,3,64,256]{3,2,1,0:T(8,128)(2,1)S(1)}, u32[]{:S(2)}, u32[]{:S(2)}) async-start(bf16[4,3,64,256]{3,2,1,0:T(8,128)(2,1)} %get-tuple-element.43), calls=%async_computation | async-start | bytes 786432 | tf_op jit(solution)/shard_map/all_to_all | solution.py:467
  25.0 1.6 constant_dynamic-slice_fusion.1
  26.8 5.4 %embed.3 = (bf16[192,1024]{1,0:T(8,128)(2,1)S(1)}, bf16[4,3,64,256]{3,2,1,0:T(8,128)(2,1)S(1)}) custom-call(s32[7]{0:T(128)S(1)} %pad_add_fusion.scal_ref, bf16[384,2560]{1,0:T(8,128)(2,1)S(1)} %bitcast.75, bf16[2560,1024]{1,0:T(8,128)(2,1)} %w_ref.8, f32[1,1024]{1,0:T(1,128)S(1)} %bitcast.88, f32[1,1024]{1,0:T(1,128)S(1)} %bitcast.82), custom_call_target="tpu_custom_call" | custom-call | flops 1006632960 | bytes 6225920 | tf_op jit(solution)/shard_map/embed/pallas_call | solution.py:109
  33.7 3.0 all-to-all-done.x_ref
  36.7 3.5 all-to-all-start.2
  40.2 1.7 copy.50
  41.8 2.0 fusion.7
  43.9 1.2 copy.42.w_ref
  46.9 5.6 %spectral.2 = (bf16[4,3,64,256]{3,2,1,0:T(8,128)(2,1)S(1)}, bf16[3,2,256,256]{3,2,1,0:T(8,128)(2,1)S(1)}, bf16[3,2,256,256]{3,2,1,0:T(8,128)(2,1)S(1)}, bf16[3,2,256,256]{3,2,1,0:T(8,128)(2,1)S(1)}) custom-call(s32[7]{0:T(128)S(1)} %pad_add_fusion.1.s_ref, bf16[3,512,256]{2,1,0:T(8,128)(2,1)S(1)} %copy-done.4, bf16[3,512,256]{2,1,0:T(8,128)(2,1)S(1)} %copy-done.3, ...), custom_call_target="tpu_custom_call" | custom-call | flops 1006632960 | bytes 3145728 | tf_op jit(solution)/shard_map/spectral/pallas_call | solution.py:194
  56.7 5.1 %all-to-all-start.1 = ((bf16[4,3,64,256]{3,2,1,0:T(8,128)(2,1)}), bf16[4,3,64,256]{3,2,1,0:T(8,128)(2,1)}, u32[]{:S(2)}, u32[]{:S(2)}) async-start(bf16[4,3,64,256]{3,2,1,0:T(8,128)(2,1)} %copy-done.40), calls=%async_computation.1 | async-start | bytes 786432 | tf_op jit(solution)/shard_map/all_to_all | solution.py:467
  61.8 1.1 copy-done.5
  63.9 5.6 %spectral.3 = (bf16[4,3,64,256]{3,2,1,0:T(8,128)(2,1)S(1)}, bf16[3,2,256,256]{3,2,1,0:T(8,128)(2,1)S(1)}, bf16[3,2,256,256]{3,2,1,0:T(8,128)(2,1)S(1)}, bf16[3,2,256,256]{3,2,1,0:T(8,128)(2,1)S(1)}) custom-call(s32[7]{0:T(128)S(1)} %pad_add_fusion.1.s_ref, bf16[3,512,256]{2,1,0:T(8,128)(2,1)S(1)} %copy-done.5, bf16[3,512,256]{2,1,0:T(8,128)(2,1)S(1)} %copy-done.3, ...), custom_call_target="tpu_custom_call" | custom-call | flops 1006632960 | bytes 3145728 | tf_op jit(solution)/shard_map/spectral/pallas_call | solution.py:194
  73.0 5.2 %all-to-all-start.3 = ((bf16[4,3,64,256]{3,2,1,0:T(8,128)(2,1)}), bf16[4,3,64,256]{3,2,1,0:T(8,128)(2,1)}, u32[]{:S(2)}, u32[]{:S(2)}) async-start(bf16[4,3,64,256]{3,2,1,0:T(8,128)(2,1)} %copy-done.38), calls=%async_computation.3 | async-start | bytes 786432 | tf_op jit(solution)/shard_map/all_to_all | solution.py:467
  80.2 2.5 head.2
  83.7 15.8 %all_gather.12.r_ref = bf16[4,3,64,256]{3,2,1,0:T(8,128)(2,1)S(1)} all-gather(bf16[1,3,64,256]{3,2,1,0:T(8,128)(2,1)S(1)} %bitcast.79), channel_id=1, replica_groups=mesh['grp'=8,'fft'=4] {'fft'}, dimensions={0}, use_global_device_ids=true | all-gather | bytes 491520 | tf_op jit(solution)/shard_map/all_gather | solution.py:537
  100.6 1.1 copy-done.33
  101.8 7.6 %spectral_back.2 = (bf16[4,3,64,256]{3,2,1,0:T(8,128)(2,1)S(1)}, f32[2,2,256,256]{3,2,1,0:T(8,128)}, f32[2,2,256]{2,1,0:T(2,128)S(1)}) custom-call(s32[7]{0:T(128)S(1)} %pad_add_fusion.1.s_ref, bf16[3,512,256]{2,1,0:T(8,128)(2,1)S(1)} %copy-done.6, bf16[3,512,256]{2,1,0:T(8,128)(2,1)S(1)} %copy-done.3, bf16[3,256,512]{2,1,0:T(8,128)(2,1)S(1)} %copy-done.2, ...), custom_call_target="tpu_custom_call" | custom-call | flops 1207959552 | bytes 3145728 | tf_op jit(solution)/shard_map/spectral_back/pallas_call | solution.py:303
  110.1 4.1 all-to-all-start.5
  116.2 2.5 head.3
  119.6 15.2 %all_gather.13.r_ref = bf16[4,3,64,256]{3,2,1,0:T(8,128)(2,1)S(1)} all-gather(bf16[1,3,64,256]{3,2,1,0:T(8,128)(2,1)S(1)} %bitcast.80), channel_id=1, replica_groups=mesh['grp'=8,'fft'=4] {'fft'}, dimensions={0}, use_global_device_ids=true | all-gather | bytes 491520 | tf_op jit(solution)/shard_map/all_gather | solution.py:537
  136.0 1.1 copy-done.29
  137.2 7.6 %spectral_back.3 = (bf16[4,3,64,256]{3,2,1,0:T(8,128)(2,1)S(1)}, f32[2,2,256,256]{3,2,1,0:T(8,128)}, f32[2,2,256]{2,1,0:T(2,128)S(1)}) custom-call(s32[7]{0:T(128)S(1)} %pad_add_fusion.1.s_ref, bf16[3,512,256]{2,1,0:T(8,128)(2,1)S(1)} %copy-done.7, bf16[3,512,256]{2,1,0:T(8,128)(2,1)S(1)} %copy-done.3, bf16[3,256,512]{2,1,0:T(8,128)(2,1)S(1)} %copy-done.2, ...), custom_call_target="tpu_custom_call" | custom-call | flops 1207959552 | bytes 3145728 | tf_op jit(solution)/shard_map/spectral_back/pallas_call | solution.py:303
  145.5 5.1 %all-to-all-start.6 = ((bf16[4,3,64,256]{3,2,1,0:T(8,128)(2,1)}), bf16[4,3,64,256]{3,2,1,0:T(8,128)(2,1)S(1)}, u32[]{:S(2)}, u32[]{:S(2)}) async-start(bf16[4,3,64,256]{3,2,1,0:T(8,128)(2,1)} %copy-done.39), calls=%async_computation.6 | async-start | bytes 786432 | tf_op jit(solution)/shard_map/all_to_all | solution.py:467
  151.6 2.4 embedded_back.2
  154.0 5.5 %all-to-all-done.6.grad_ref = bf16[4,3,64,256]{3,2,1,0:T(8,128)(2,1)S(1)} async-done(((bf16[4,3,64,256]{3,2,1,0:T(8,128)(2,1)}), bf16[4,3,64,256]{3,2,1,0:T(8,128)(2,1)S(1)}, u32[]{:S(2)}, u32[]{:S(2)}) %all-to-all-start.6) | async-done | bytes 393248 | tf_op jit(solution)/shard_map/all_to_all | solution.py:467
  161.3 1.4 embedded_back.3
  162.8 8.4 %embed_grad.1 = (bf16[4,320,1024]{2,1,0:T(8,128)(2,1)}, bf16[4,320,1024]{2,1,0:T(8,128)(2,1)}) custom-call(s32[1]{0:T(128)} %bitcast.15.at_ref, bf16[384,2560]{1,0:T(8,128)(2,1)S(1)} %bitcast.76, bf16[192,1024]{1,0:T(8,128)(2,1)S(1)} %get-tuple-element.55.refs_0_, bf16[192,1024]{1,0:T(8,128)(2,1)S(1)} %get-tuple-element.61.refs_1_), custom_call_target="tpu_custom_call" | custom-call | flops 2013265920 | bytes 7208960 | tf_op jit(solution)/shard_map/embed_grad/pallas_call | solution.py:417
  172.5 2.0 sort.17
  174.6 51.8 %all-reduce.4.cloned.1.call-done = f32[2,2,2,128,128]{4,3,2,0,1:T(8,128)} async-done(((f32[2,2,2,128,128]{4,3,2,0,1:T(8,128)}), f32[2,2,2,128,128]{4,3,2,0,1:T(8,128)}) %all-reduce.4.cloned.1.call-update) | async-done | bytes 524304 | tf_op jit(solution)/shard_map/psum | solution.py:570
  226.4 1.5 copy-done.52
  227.9 3.9 add_convert_fusion
  235.6 12.9 %collective-permute-done.1 = bf16[2,320,512]{2,1,0:T(8,128)(2,1)} collective-permute-done((bf16[2,320,512]{2,1,0:T(8,128)(2,1)}, bf16[2,320,512]{2,1,0:T(8,128)(2,1)}, u32[]{:S(2)}, u32[]{:S(2)}) %collective-permute-start.1) | collective-permute-done | bytes 655392 | tf_op jit(solution)/shard_map/ppermute | solution.py:436
  248.5 1.3 collective-permute-done.3
  249.7 1.6 fusion.1
  252.2 1.4 collective-permute-start.4
  255.2 3.5 all-to-all-start.4
  259.7 1.2 fusion.2
  260.9 1.2 fusion.3
  263.0 2.7 all-to-all-done.4
  266.3 4.5 %all-to-all-start.7 = ((bf16[4,80,1024]{2,1,0:T(8,128)(2,1)}), bf16[4,80,1024]{2,1,0:T(8,128)(2,1)S(1)}, u32[]{:S(2)}, u32[]{:S(2)}) async-start(bf16[4,80,1024]{2,1,0:T(8,128)(2,1)} %bitcast.28), calls=%async_computation.7 | async-start | bytes 1310720 | tf_op jit(solution)/shard_map/all_to_all | solution.py:462
  270.9 12.0 %psum.45 = f32[2,2,2,128]{3,2,0,1:T(2,128)S(1)} all-reduce(f32[2,2,2,128]{3,2,0,1:T(2,128)S(1)} %pad_maximum_fusion.4), channel_id=1, replica_groups=mesh['grp'=8,'fft'=4] {'grp'}, use_global_device_ids=true, to_apply=%region_6.7 | all-reduce | flops 1024 | bytes 8192 | tf_op jit(solution)/shard_map/psum | solution.py:570
  282.9 14.0 %all_gather.15 = f32[2,2,8,128]{3,1,0,2:T(2,128)S(1)} all-gather(f32[2,2,2,128]{3,1,0,2:T(2,128)S(1)} %copy.46), channel_id=1, replica_groups=mesh['grp'=8,'fft'=4] {'fft'}, dimensions={2}, use_global_device_ids=true | all-gather | bytes 20480 | tf_op jit(solution)/shard_map/all_gather | solution.py:572
  300.0 39.6 %all-reduce = (f32[1024]{0:T(1024)}, f32[1024]{0:T(1024)}, f32[256]{0:T(256)}) all-reduce(f32[1024]{0:T(1024)S(1)} %bitcast.99, f32[1024]{0:T(1024)S(1)} %bitcast.98, f32[256]{0:T(256)S(1)} %bitcast.100), channel_id=1, replica_groups=mesh['grp'=8,'fft'=4] {'grp','fft'}, use_global_device_ids=true, to_apply=%region_3.4 | all-reduce | flops 2304 | bytes 18432 | tf_op jit(solution)/shard_map/psum | solution.py:574
  339.5 3.2 copy.47
  343.5 84.0 %all-reduce.6.cloned.1.call-done = f32[1024,256]{1,0:T(8,128)} async-done(((f32[1024,256]{1,0:T(8,128)}), f32[1024,256]{1,0:T(8,128)}) %all-reduce.6.cloned.1.call-update) | async-done | bytes 1048592 | tf_op jit(solution)/shard_map/psum | solution.py:562
  427.5 2.3 copy.59
  (172 shorter events, 41.5 us)
Async XLA Ops:
  8.8 1.5 copy-start.8
  11.7 15.0 %copy-start.9 = (bf16[6,4,16,2560]{3,2,1,0:T(8,128)(2,1)S(1)}, bf16[6,4,16,2560]{3,2,1,0:T(8,128)(2,1)}, u32[]{:S(2)}) copy-start(bf16[6,4,16,2560]{3,2,1,0:T(8,128)(2,1)} %param.15) | copy-start | bytes 5898244
  11.7 15.0 %copy-start.44 = (f32[1024]{0:T(1024)S(1)}, f32[1024]{0:T(1024)}, u32[]{:S(2)}) copy-start(f32[1024]{0:T(1024)} %param.21) | copy-start | bytes 12292
  11.7 15.1 %copy-start.50 = (f32[1024]{0:T(1024)S(1)}, f32[1024]{0:T(1024)}, u32[]{:S(2)}) copy-start(f32[1024]{0:T(1024)} %param.20) | copy-start | bytes 12292
  18.7 18.0 %all-to-all-start = ((bf16[4,3,64,256]{3,2,1,0:T(8,128)(2,1)}), bf16[4,3,64,256]{3,2,1,0:T(8,128)(2,1)S(1)}, u32[]{:S(2)}, u32[]{:S(2)}) async-start(bf16[4,3,64,256]{3,2,1,0:T(8,128)(2,1)} %get-tuple-element.43), calls=%async_computation | async-start | bytes 786432 | tf_op jit(solution)/shard_map/all_to_all | solution.py:467
  33.7 12.2 %copy-start.2 = (bf16[3,256,512]{2,1,0:T(8,128)(2,1)S(1)}, bf16[3,256,512]{2,1,0:T(8,128)(2,1)}, u32[]{:S(2)}) copy-start(bf16[3,256,512]{2,1,0:T(8,128)(2,1)} %constant.72.clone.bh) | copy-start | bytes 2359300
  33.7 12.2 %copy-start.3 = (bf16[3,512,256]{2,1,0:T(8,128)(2,1)S(1)}, bf16[3,512,256]{2,1,0:T(8,128)(2,1)}, u32[]{:S(2)}) copy-start(bf16[3,512,256]{2,1,0:T(8,128)(2,1)} %constant.71.clone.tl) | copy-start | bytes 2359300
  33.7 12.2 %copy-start.4 = (bf16[3,512,256]{2,1,0:T(8,128)(2,1)S(1)}, bf16[3,512,256]{2,1,0:T(8,128)(2,1)}, u32[]{:S(2)}) copy-start(bf16[3,512,256]{2,1,0:T(8,128)(2,1)} %constant.70.clone.th) | copy-start | bytes 2359300
  36.7 7.2 %copy-start.12 = (bf16[4,3,64,256]{3,2,1,0:T(8,128)(2,1)}, bf16[4,3,64,256]{3,2,1,0:T(8,128)(2,1)S(1)}, u32[]{:S(2)}) copy-start(bf16[4,3,64,256]{3,2,1,0:T(8,128)(2,1)S(1)} %all-to-all-done.x_ref) | copy-start | bytes 1179652
  36.7 19.3 %all-to-all-start.2 = ((bf16[4,3,64,256]{3,2,1,0:T(8,128)(2,1)}), bf16[4,3,64,256]{3,2,1,0:T(8,128)(2,1)S(1)}, u32[]{:S(2)}, u32[]{:S(2)}) async-start(bf16[4,3,64,256]{3,2,1,0:T(8,128)(2,1)} %copy-done.36), calls=%async_computation.2 | async-start | bytes 786432 | tf_op jit(solution)/shard_map/all_to_all | solution.py:467
  56.7 16.3 %all-to-all-start.1 = ((bf16[4,3,64,256]{3,2,1,0:T(8,128)(2,1)}), bf16[4,3,64,256]{3,2,1,0:T(8,128)(2,1)}, u32[]{:S(2)}, u32[]{:S(2)}) async-start(bf16[4,3,64,256]{3,2,1,0:T(8,128)(2,1)} %copy-done.40), calls=%async_computation.1 | async-start | bytes 786432 | tf_op jit(solution)/shard_map/all_to_all | solution.py:467
  61.8 1.1 copy-start.5
  63.9 14.3 %copy-start = (bf16[1024,256]{1,0:T(8,128)(2,1)S(1)}, bf16[1024,256]{1,0:T(8,128)(2,1)}, u32[]{:S(2)}) copy-start(bf16[1024,256]{1,0:T(8,128)(2,1)} %w_ref.11) | copy-start | bytes 1572868
  63.9 14.3 %copy-start.51 = (f32[256]{0:T(256)S(1)}, f32[256]{0:T(256)}, u32[]{:S(2)}) copy-start(f32[256]{0:T(256)} %param.25) | copy-start | bytes 3076
  63.9 35.6 %copy-start.1 = (bf16[3,256,512]{2,1,0:T(8,128)(2,1)S(1)}, bf16[3,256,512]{2,1,0:T(8,128)(2,1)}, u32[]{:S(2)}) copy-start(bf16[3,256,512]{2,1,0:T(8,128)(2,1)} %constant.73.clone.bl) | copy-start | bytes 2359300
  73.0 26.5 %copy-start.11 = (bf16[2,2,256,256]{3,2,1,0:T(8,128)(2,1)S(1)}, bf16[2,2,256,256]{3,2,1,0:T(8,128)(2,1)}, u32[]{:S(2)}) copy-start(bf16[2,2,256,256]{3,2,1,0:T(8,128)(2,1)} %get-tuple-element.111.w_ref) | copy-start | bytes 1572868
  73.0 37.1 %all-to-all-start.3 = ((bf16[4,3,64,256]{3,2,1,0:T(8,128)(2,1)}), bf16[4,3,64,256]{3,2,1,0:T(8,128)(2,1)}, u32[]{:S(2)}, u32[]{:S(2)}) async-start(bf16[4,3,64,256]{3,2,1,0:T(8,128)(2,1)} %copy-done.38), calls=%async_computation.3 | async-start | bytes 786432 | tf_op jit(solution)/shard_map/all_to_all | solution.py:467
  83.7 15.8 %copy-start.45 = (bf16[192,256]{1,0:T(8,128)(2,1)}, bf16[192,256]{1,0:T(8,128)(2,1)S(1)}, u32[]{:S(2)}) copy-start(bf16[192,256]{1,0:T(8,128)(2,1)S(1)} %get-tuple-element.45) | copy-start | bytes 294916
  99.5 1.1 copy-start.6
  100.6 1.1 copy-start.33
  110.1 35.4 %all-to-all-start.5 = ((bf16[4,3,64,256]{3,2,1,0:T(8,128)(2,1)}), bf16[4,3,64,256]{3,2,1,0:T(8,128)(2,1)}, u32[]{:S(2)}, u32[]{:S(2)}) async-start(bf16[4,3,64,256]{3,2,1,0:T(8,128)(2,1)} %copy-done.37), calls=%async_computation.5 | async-start | bytes 786432 | tf_op jit(solution)/shard_map/all_to_all | solution.py:467
  119.6 15.3 %copy-start.41 = (bf16[192,256]{1,0:T(8,128)(2,1)}, bf16[192,256]{1,0:T(8,128)(2,1)S(1)}, u32[]{:S(2)}) copy-start(bf16[192,256]{1,0:T(8,128)(2,1)S(1)} %get-tuple-element.56.res_ref) | copy-start | bytes 294916
  119.6 15.3 %copy-start.47 = (bf16[192,256]{1,0:T(8,128)(2,1)}, bf16[192,256]{1,0:T(8,128)(2,1)S(1)}, u32[]{:S(2)}) copy-start(bf16[192,256]{1,0:T(8,128)(2,1)S(1)} %get-tuple-element.49) | copy-start | bytes 294916
  134.9 1.1 copy-start.7
  136.0 1.1 copy-start.29
  145.5 17.3 %copy-start.10 = (bf16[6,4,16,2560]{3,2,1,0:T(8,128)(2,1)S(1)}, bf16[6,4,16,2560]{3,2,1,0:T(8,128)(2,1)}, u32[]{:S(2)}) copy-start(bf16[6,4,16,2560]{3,2,1,0:T(8,128)(2,1)} %param.15) | copy-start | bytes 5898244
  145.5 14.0 %all-to-all-start.6 = ((bf16[4,3,64,256]{3,2,1,0:T(8,128)(2,1)}), bf16[4,3,64,256]{3,2,1,0:T(8,128)(2,1)S(1)}, u32[]{:S(2)}, u32[]{:S(2)}) async-start(bf16[4,3,64,256]{3,2,1,0:T(8,128)(2,1)} %copy-done.39), calls=%async_computation.6 | async-start | bytes 786432 | tf_op jit(solution)/shard_map/all_to_all | solution.py:467
  150.6 75.8 %all-reduce.4.cloned.1.call-start = ((), (), s32[]{:S(2)}) async-start(), calls=%async_computation.8 | async-start | bytes 1048576 | tf_op jit(solution)/shard_map/psum | solution.py:570
  162.8 8.5 %copy-start.59 = (s32[48]{0:T(128)S(1)}, s32[48]{0:T(128)}, u32[]{:S(2)}) copy-start(s32[48]{0:T(128)} %param.18) | copy-start | bytes 580
  162.8 8.5 %copy-start.55 = (f32[2,2,256,256]{3,2,1,0:T(8,128)S(1)}, f32[2,2,256,256]{3,2,1,0:T(8,128)}, u32[]{:S(2)}) copy-start(f32[2,2,256,256]{3,2,1,0:T(8,128)} %get-tuple-element.66) | copy-start | bytes 3145732
  162.8 8.5 %copy-start.56 = (f32[2,2,256,256]{3,2,1,0:T(8,128)S(1)}, f32[2,2,256,256]{3,2,1,0:T(8,128)}, u32[]{:S(2)}) copy-start(f32[2,2,256,256]{3,2,1,0:T(8,128)} %get-tuple-element.67) | copy-start | bytes 3145732
  171.2 55.2 %collective-permute-start = (bf16[4,320,1024]{2,1,0:T(8,128)(2,1)}, bf16[4,320,1024]{2,1,0:T(8,128)(2,1)S(1)}, u32[]{:S(2)}, u32[]{:S(2)}) collective-permute-start(bf16[4,320,1024]{2,1,0:T(8,128)(2,1)} %get-tuple-element.63), channel_id=1, source_target_pairs={{0,4},{4,0},{8,12},{12,8},{16,20},{20,16},{24,28},{28,24},{1,5},{5... | collective-permute-start | bytes 7864328 | tf_op jit(solution)/shard_map/ppermute | solution.py:436
  172.4 167.2 %all-gather.2.cloned.1.call-start = ((), (), s32[]{:S(2)}) async-start(), calls=%async_computation.9 | async-start | bytes 2621440 | tf_op jit(solution)/shard_map/all_gather | solution.py:571
  226.4 1.5 copy-start.52
  231.8 3.2 copy-start.46
  231.8 3.2 copy-start.48
  232.7 15.8 %collective-permute-start.1 = (bf16[2,320,512]{2,1,0:T(8,128)(2,1)}, bf16[2,320,512]{2,1,0:T(8,128)(2,1)}, u32[]{:S(2)}, u32[]{:S(2)}) collective-permute-start(bf16[2,320,512]{2,1,0:T(8,128)(2,1)} %slice_bitcast_fusion.2), channel_id=1, source_target_pairs={{0,8},{4,12},{8,0},{12,4},{16,24},{20,28},{24,16},{28,20},{1,9},{5... | collective-permute-start | bytes 1966088 | tf_op jit(solution)/shard_map/ppermute | solution.py:436
  234.3 15.4 %collective-permute-start.3 = (bf16[2,320,512]{2,1,0:T(8,128)(2,1)}, bf16[2,320,512]{2,1,0:T(8,128)(2,1)}, u32[]{:S(2)}, u32[]{:S(2)}) collective-permute-start(bf16[2,320,512]{2,1,0:T(8,128)(2,1)} %slice_bitcast_fusion), channel_id=1, source_target_pairs={{0,16},{4,20},{8,24},{12,28},{16,0},{20,4},{24,8},{28,12},{1,17},{... | collective-permute-start | bytes 1966088 | tf_op jit(solution)/shard_map/ppermute | solution.py:436
  251.4 3.0 copy-start.53
  251.4 3.0 copy-start.54
  252.2 7.5 %collective-permute-start.4 = (bf16[320,512]{1,0:T(8,128)(2,1)}, bf16[320,512]{1,0:T(8,128)(2,1)}, u32[]{:S(2)}, u32[]{:S(2)}) collective-permute-start(bf16[320,512]{1,0:T(8,128)(2,1)} %slice_bitcast_fusion.4), channel_id=1, source_target_pairs={{0,8},{4,12},{8,0},{12,4},{16,24},{20,28},{24,16},{28,20},{1,9},{5... | collective-permute-start | bytes 983048 | tf_op jit(solution)/shard_map/ppermute | solution.py:436
  253.6 7.2 %collective-permute-start.2 = (bf16[320,512]{1,0:T(8,128)(2,1)S(1)}, bf16[320,512]{1,0:T(8,128)(2,1)}, u32[]{:S(2)}, u32[]{:S(2)}) collective-permute-start(bf16[320,512]{1,0:T(8,128)(2,1)S(1)} %slice_bitcast_fusion.6), channel_id=1, source_target_pairs={{0,16},{4,20},{8,24},{12,28},{16,0},{20,4},{24,8},{28,12},{1,17},{... | collective-permute-start | bytes 983048 | tf_op jit(solution)/shard_map/ppermute | solution.py:436
  255.2 42.3 %copy-start.23 = (f32[1024,256]{1,0:T(8,128)S(1)}, f32[1024,256]{1,0:T(8,128)}, u32[]{:S(2)}) copy-start(f32[1024,256]{1,0:T(8,128)} %copy-done.22) | copy-start | bytes 3145732
  255.2 42.3 %copy-start.25 = (f32[1024,256]{1,0:T(8,128)S(1)}, f32[1024,256]{1,0:T(8,128)}, u32[]{:S(2)}) copy-start(f32[1024,256]{1,0:T(8,128)} %copy-done.24) | copy-start | bytes 3145732
  255.2 10.4 %all-to-all-start.4 = ((bf16[8,64,256]{2,1,0:T(8,128)(2,1)}), bf16[8,64,256]{2,1,0:T(8,128)(2,1)S(1)}, u32[]{:S(2)}, u32[]{:S(2)}) async-start(bf16[8,64,256]{2,1,0:T(8,128)(2,1)} %broadcast_select_fusion), calls=%async_computation.4 | async-start | bytes 524288 | tf_op jit(solution)/shard_map/all_to_all | solution.py:475
  266.3 76.4 %all-to-all-start.7 = ((bf16[4,80,1024]{2,1,0:T(8,128)(2,1)}), bf16[4,80,1024]{2,1,0:T(8,128)(2,1)S(1)}, u32[]{:S(2)}, u32[]{:S(2)}) async-start(bf16[4,80,1024]{2,1,0:T(8,128)(2,1)} %bitcast.28), calls=%async_computation.7 | async-start | bytes 1310720 | tf_op jit(solution)/shard_map/all_to_all | solution.py:462
  270.9 27.7 %copy-start.58 = (bf16[8,64,256]{2,1,0:T(8,128)(2,1)S(1)}, bf16[8,64,256]{2,1,0:T(8,128)(2,1)}, u32[]{:S(2)}) copy-start(bf16[8,64,256]{2,1,0:T(8,128)(2,1)} %copy-done.57) | copy-start | bytes 786436
  270.9 156.6 %all-reduce.6.cloned.1.call-start = ((), (), s32[]{:S(2)}) async-start(), calls=%async_computation.10 | async-start | bytes 2097152 | tf_op jit(solution)/shard_map/psum | solution.py:562
  (28 other events, 24.2 us)
Sparse Core Ops, SparseCore 0:
  172.5 53.8 all-reduce.3
  228.0 45.2 all-gather.1
Sparse Core Ops, SparseCore 1:
  298.7 128.8 all-reduce.5

commit v2 on v1

v2 whole, which is shorter than its diff:
```python
import jax
import jax.numpy as jnp
import ml_dtypes
import numpy as np
from jax import lax
from jax.experimental import pallas as pl
from jax.experimental.pallas import tpu as pltpu
from jax.sharding import PartitionSpec as P

EPSILON = 1e-05
SHRINK = 0.01
CHUNKS = 2
VMEM_BYTES = 60 * 1024 * 1024
SLOTS = 6
SHARD, FIRST_ROW, GROUP, SIDES = 0, 1, 2, 3
HALF = jnp.bfloat16
FULL = jnp.float32


def dft_tables(cells):
    levels, factors = [], []
    for side, scale in ((cells, 1.1305), (cells // 2, 1.8633), (cells // 4, 1.0)):
        k = np.arange(cells)
        inside = (k < side).astype(np.float64)
        keep = inside[:, None] * inside[None, :]
        angle = 2.0 * np.pi * ((k[:, None] * k[None, :]) % side) / side
        one = np.exp(-1j * angle) * keep / np.sqrt(side)
        two = np.kron(one, one)
        table = np.concatenate([two.real, two.imag], axis=0)
        table[np.abs(table) < 1e-12] = 0.0
        rounded = (table * scale).astype(np.float32).astype(ml_dtypes.bfloat16)
        held = rounded.astype(np.float64)
        factors.append(float(np.sum(table * table) / np.sum(table * held)))
        levels.append(rounded)
    return np.stack(levels), factors


def dot(left, right):
    return jnp.dot(left, right, preferred_element_type=FULL)


def dot_tn(left, right):
    return lax.dot_general(left, right, (((0,), (0,)), ((), ())), preferred_element_type=FULL)


def dot_nt(left, right):
    return lax.dot_general(left, right, (((1,), (1,)), ((), ())), preferred_element_type=FULL)


def params():
    return pltpu.CompilerParams(vmem_limit_bytes=VMEM_BYTES)


def token_sides(scal_ref, first, count, per_sample, cells):
    token = lax.broadcasted_iota(jnp.int32, (count * per_sample, 1), 0)
    sample = token // per_sample
    side = jnp.zeros_like(token)
    for i in range(count):
        side = jnp.where(sample == i, scal_ref[SIDES + first + i], side)
    row = scal_ref[FIRST_ROW] + (token % per_sample) // cells
    col = token % cells
    valid = jnp.where((row < side) & (col < side), 1.0, 0.0).astype(FULL)
    return side, valid


def layer_norm(values):
    centered = values - jnp.mean(values, axis=-1, keepdims=True)
    inv_std = lax.rsqrt(jnp.mean(centered * centered, axis=-1, keepdims=True) + EPSILON)
    return centered * inv_std, inv_std


def whole(shape):
    return pl.BlockSpec(tuple(shape), lambda i, s: (0,) * len(shape))


def part_of(scal_ref, k, size):
    at = jnp.bitwise_xor(scal_ref[SHARD], k)
    return pl.ds(pl.multiple_of(at * size, size), size)


def fill_lanes(scal_ref, refs, held):
    share = refs[0].shape[-1]
    for k, ref in enumerate(refs):
        held[:, part_of(scal_ref, k, share)] = ref[...].reshape(held.shape[0], share)


def fill_rows(scal_ref, refs, held):
    rows = refs[0].shape[1]
    for k, ref in enumerate(refs):
        held[part_of(scal_ref, k, rows), :] = ref[0]


def split_lanes(scal_ref, held, refs):
    share = refs[0].shape[-1]
    for k, ref in enumerate(refs):
        ref[...] = held[:, part_of(scal_ref, k, share)].reshape(ref.shape)


def split_rows(scal_ref, held, refs):
    rows = refs[0].shape[1]
    for k, ref in enumerate(refs):
        ref[0] = held[part_of(scal_ref, k, rows), :]


def embed_chunk(scal, patches, embed_w, embed_b, gain, first, count, per_sample, cells, shards):
    rows = count * per_sample
    depth, width = embed_w.shape
    share = width // shards
    steps = 4
    tile = depth // steps

    def body(scal_ref, x_ref, w_ref, b_ref, gain_ref, emb_ref, *refs):
        outs, (acc, held) = refs[:shards], refs[shards:]
        step = pl.program_id(0)
        part = dot(x_ref[...], w_ref[...])

        @pl.when(step == 0)
        def _():
            acc[...] = part

        @pl.when(step > 0)
        def _():
            acc[...] += part

        @pl.when(step == steps - 1)
        def _():
            _, valid = token_sides(scal_ref, first, count, per_sample, cells)
            embedded = ((acc[...] + b_ref[...]) * valid).astype(HALF)
            emb_ref[...] = embedded
            unit, _ = layer_norm(embedded.astype(FULL))
            held[...] = (unit * gain_ref[...]).astype(HALF)
            split_lanes(scal_ref, held, outs)

    at = first // count
    piece = (count, per_sample, share)
    emb, *pieces = pl.pallas_call(
        body,
        grid_spec=pltpu.PrefetchScalarGridSpec(
            num_scalar_prefetch=1,
            grid=(steps,),
            in_specs=[
                pl.BlockSpec((rows, tile), lambda k, s: (at, k)),
                pl.BlockSpec((tile, width), lambda k, s: (k, 0)),
                whole((1, width)),
                whole((1, width)),
            ],
            out_specs=[whole((rows, width))] + [whole(piece)] * shards,
            scratch_shapes=[pltpu.VMEM((rows, width), FULL), pltpu.VMEM((rows, width), HALF)],
        ),
        out_shape=[jax.ShapeDtypeStruct((rows, width), HALF)] + [jax.ShapeDtypeStruct(piece, HALF)] * shards,
        compiler_params=params(),
        cost_estimate=pl.CostEstimate(
            flops=2 * rows * depth * width, bytes_accessed=2 * depth * (rows + width), transcendentals=0
        ),
        name="embed",
    )(scal, patches, embed_w, embed_b, gain)
    return emb, pieces


def to_blocks(values, blocks, width):
    half = values.shape[0] // 2
    return [
        jnp.concatenate(
            [values[:half, b * width : (b + 1) * width], values[half:, b * width : (b + 1) * width]], axis=1
        )
        for b in range(blocks)
    ]


def from_blocks(parts, width):
    real = jnp.concatenate([p[:, :width] for p in parts], axis=1)
    imag = jnp.concatenate([p[:, width:] for p in parts], axis=1)
    return real, imag


def table_factor(scal_ref, at, factors):
    level = scal_ref[at]
    return jnp.where(level == 0, factors[0], jnp.where(level == 1, factors[1], factors[2])).astype(FULL)


def table_back(table_ref, pair, factor):
    size = table_ref.shape[2]
    total = None
    for at, values in enumerate(pair):
        table = table_ref[0, at * size : (at + 1) * size]
        top = values.astype(HALF)
        rest = (values - top.astype(FULL)).astype(HALF)
        part = dot(table, top) + dot(table, rest)
        total = part if total is None else total + part
    return total * factor


def complex_weights(w_ref, held, blocks, width):
    for layer in range(2):
        for b in range(blocks):
            real, imag = w_ref[layer, 0, b], w_ref[layer, 1, b]
            held[layer, b, :width, :width] = real
            held[layer, b, :width, width:] = imag
            held[layer, b, width:, :width] = -imag
            held[layer, b, width:, width:] = real


def spectral_chunk(scal, table, factors, pieces, spec_w, spec_b, first):
    shards = len(pieces)
    count, per_sample, share = pieces[0].shape
    size = shards * per_sample
    width = spec_w.shape[-1]
    blocks = share // width
    wide = 2 * width

    def body(scal_ref, t_ref, w_ref, b_ref, *refs):
        ins, outs = refs[:shards], refs[shards : 2 * shards]
        spec_ref, hid_ref, fil_ref, weights, held = refs[2 * shards :]

        @pl.when(pl.program_id(0) == 0)
        def _():
            complex_weights(w_ref, weights, blocks, width)

        def bias(layer, b):
            row = pl.ds(scal_ref[SHARD] * blocks + b, 1)
            return jnp.concatenate([b_ref[layer, 0, row], b_ref[layer, 1, row]], axis=1)

        factor = table_factor(scal_ref, SIDES + SLOTS + first + pl.program_id(0), factors)
        fill_rows(scal_ref, ins, held)
        spectrum = (dot(t_ref[0], held[...]) * factor).astype(HALF)
        kept = []
        for b, entry in enumerate(to_blocks(spectrum, blocks, width)):
            spec_ref[0, b] = entry
            pre_one = dot(entry, weights[0, b]) + bias(0, b)
            hidden = jnp.maximum(pre_one, 0.0).astype(HALF)
            hid_ref[0, b] = hidden
            pre_two = dot(hidden, weights[1, b]) + bias(1, b)
            filtered = jnp.where(
                pre_two > SHRINK, pre_two - SHRINK, jnp.where(pre_two < -SHRINK, pre_two + SHRINK, 0.0)
            )
            fil_ref[0, b] = filtered.astype(HALF)
            kept.append(filtered)
        held[...] = table_back(t_ref, from_blocks(kept, width), factor).astype(HALF)
        split_rows(scal_ref, held, outs)

    piece = pl.BlockSpec((1, per_sample, share), lambda i, s: (i, 0, 0))
    saved = pl.BlockSpec((1, blocks, size, wide), lambda i, s: (i, 0, 0, 0))
    saved_shape = jax.ShapeDtypeStruct((count, blocks, size, wide), HALF)
    outs = pl.pallas_call(
        body,
        grid_spec=pltpu.PrefetchScalarGridSpec(
            num_scalar_prefetch=1,
            grid=(count,),
            in_specs=[
                pl.BlockSpec((1, 2 * size, size), lambda i, s: (s[SIDES + SLOTS + first + i], 0, 0)),
                pl.BlockSpec((2, 2, blocks, width, width), lambda i, s: (0, 0, s[SHARD], 0, 0)),
                whole(spec_b.shape),
            ]
            + [piece] * shards,
            out_specs=[piece] * shards + [saved] * 3,
            scratch_shapes=[pltpu.VMEM((2, blocks, wide, wide), HALF), pltpu.VMEM((size, share), HALF)],
        ),
        out_shape=[jax.ShapeDtypeStruct(pieces[0].shape, HALF)] * shards + [saved_shape] * 3,
        compiler_params=params(),
        cost_estimate=pl.CostEstimate(
            flops=count * size * share * size * 14, bytes_accessed=count * size * share * 16, transcendentals=0
        ),
        name="spectral",
    )(scal, table, spec_w, spec_b, *pieces)
    return outs[:shards], outs[shards:]


def head_chunk(scal, embedded, gain, mixed, targets, head_w, head_b, first, samples, cells):
    shards = len(mixed)
    count, per_sample, share = mixed[0].shape
    rows = count * per_sample
    width, outs = head_w.shape
    at = first // count
    scale_root = float(np.sqrt(np.float32(samples)))

    def body(scal_ref, emb_ref, gain_ref, tgt_ref, w_ref, b_ref, *refs):
        mix_refs, (pred_ref, res_ref, grad_ref, bias_ref, held) = refs[:shards], refs[shards:]
        fill_lanes(scal_ref, mix_refs, held)
        side, valid = token_sides(scal_ref, first, count, per_sample, cells)
        embedded = emb_ref[...].astype(FULL)
        unit, _ = layer_norm(embedded)
        normed = (unit * gain_ref[...]).astype(HALF)
        updated = (embedded + normed.astype(FULL) + held[...].astype(FULL)).astype(HALF)
        output = (dot(updated, w_ref[...]) + b_ref[...]) * valid
        pred_ref[...] = output.astype(HALF).reshape(pred_ref.shape)
        scale = 2.0 / (side.astype(FULL) * scale_root)
        residual = (scale * valid * (output - tgt_ref[...].astype(FULL))).astype(HALF)
        res_ref[...] = residual.reshape(res_ref.shape)
        grad_ref[...] = dot_tn(updated, residual)
        total = jnp.sum(residual.astype(FULL), axis=0, keepdims=True)
        bias_ref[...] = jnp.broadcast_to(total, bias_ref.shape)

    token_shape = (count, per_sample, outs)
    return pl.pallas_call(
        body,
        grid_spec=pltpu.PrefetchScalarGridSpec(
            num_scalar_prefetch=1,
            grid=(1,),
            in_specs=[
                whole((rows, width)),
                whole((1, width)),
                pl.BlockSpec((rows, outs), lambda i, s: (at, 0)),
                whole((width, outs)),
                whole((1, outs)),
            ]
            + [whole(mixed[0].shape)] * shards,
            out_specs=[whole(token_shape), whole(token_shape), whole((width, outs)), whole((8, outs))],
            scratch_shapes=[pltpu.VMEM((rows, width), HALF)],
        ),
        out_shape=[
            jax.ShapeDtypeStruct(token_shape, HALF),
            jax.ShapeDtypeStruct(token_shape, HALF),
            jax.ShapeDtypeStruct((width, outs), FULL),
            jax.ShapeDtypeStruct((8, outs), FULL),
        ],
        compiler_params=params(),
        cost_estimate=pl.CostEstimate(
            flops=4 * rows * width * outs, bytes_accessed=rows * width * 4 + width * outs * 6, transcendentals=0
        ),
        name="head",
    )(scal, embedded, gain, targets, head_w, head_b, *mixed)


def spectral_back_chunk(scal, table, factors, residual, head_w, spec_w, saved, first, before, last):
    shards = len(residual)
    count, per_sample, outs = residual[0].shape
    size = shards * per_sample
    width = spec_w.shape[-1]
    wide = 2 * width
    share = head_w.shape[0] // shards
    blocks = share // width
    raw_shape = (2, blocks, wide, wide)
    bias_shape = (2 * blocks, wide)
    has_before = before is not None

    def body(scal_ref, t_ref, h_ref, w_ref, spec_ref, hid_ref, fil_ref, *refs):
        ins, refs = refs[:shards], refs[shards:]
        if has_before:
            (old_ref, old_bias_ref), refs = refs[:2], refs[2:]
        pieces, (grad_ref, bias_ref, weights, held, gathered, total) = refs[:shards], refs[shards:]

        @pl.when(pl.program_id(0) == 0)
        def _():
            complex_weights(w_ref, weights, blocks, width)
            if has_before:
                total[...] = old_ref[...]
                bias_ref[...] = old_bias_ref[...]
            else:
                total[...] = jnp.zeros_like(total)
                bias_ref[...] = jnp.zeros_like(bias_ref)

        factor = table_factor(scal_ref, SIDES + SLOTS + first + pl.program_id(0), factors)
        fill_rows(scal_ref, ins, gathered)
        updated_grad = dot_nt(gathered[...], h_ref[...]).astype(HALF)
        filtered_grad = dot(t_ref[0], updated_grad) * factor
        kept = []
        for b, entry in enumerate(to_blocks(filtered_grad, blocks, width)):
            two_grad = jnp.where(fil_ref[0, b].astype(FULL) != 0.0, entry, 0.0).astype(HALF)
            hidden = hid_ref[0, b]
            total[1, b] += dot_tn(hidden, two_grad)
            bias_ref[blocks + b : blocks + b + 1] += jnp.sum(two_grad.astype(FULL), axis=0, keepdims=True)
            hidden_grad = dot_nt(two_grad, weights[1, b])
            one_grad = jnp.where(hidden.astype(FULL) > 0.0, hidden_grad, 0.0).astype(HALF)
            total[0, b] += dot_tn(spec_ref[0, b], one_grad)
            bias_ref[b : b + 1] += jnp.sum(one_grad.astype(FULL), axis=0, keepdims=True)
            kept.append(dot_nt(one_grad, weights[0, b]))
        held[...] = table_back(t_ref, from_blocks(kept, width), factor).astype(HALF)
        split_rows(scal_ref, held, pieces)

        @pl.when(pl.program_id(0) == count - 1)
        def _():
            if not last:
                grad_ref[...] = total[...]
                return
            for layer in range(2):
                for b in range(blocks):
                    raw = total[layer, b]
                    real = raw[:width, :width] + raw[width:, width:]
                    imag = raw[:width, width:] - raw[width:, :width]
                    row = (layer * blocks + b) * width
                    grad_ref[row : row + width] = jnp.concatenate([real, imag], axis=1).astype(HALF)

    saved_spec = pl.BlockSpec((1, blocks, size, wide), lambda i, s: (i, 0, 0, 0))
    piece = pl.BlockSpec((1, per_sample, share), lambda i, s: (i, 0, 0))
    if last:
        grad_out = jax.ShapeDtypeStruct((2 * blocks * width, wide), HALF)
    else:
        grad_out = jax.ShapeDtypeStruct(raw_shape, FULL)
    result = pl.pallas_call(
        body,
        grid_spec=pltpu.PrefetchScalarGridSpec(
            num_scalar_prefetch=1,
            grid=(count,),
            in_specs=[
                pl.BlockSpec((1, 2 * size, size), lambda i, s: (s[SIDES + SLOTS + first + i], 0, 0)),
                pl.BlockSpec((share, outs), lambda i, s: (s[SHARD], 0)),
                pl.BlockSpec((2, 2, blocks, width, width), lambda i, s: (0, 0, s[SHARD], 0, 0)),
                saved_spec,
                saved_spec,
                saved_spec,
            ]
            + [pl.BlockSpec((1, per_sample, outs), lambda i, s: (i, 0, 0))] * shards
            + ([whole(raw_shape), whole(bias_shape)] if has_before else []),
            out_specs=[piece] * shards + [whole(grad_out.shape), whole(bias_shape)],
            scratch_shapes=[
                pltpu.VMEM((2, blocks, wide, wide), HALF),
                pltpu.VMEM((size, share), HALF),
                pltpu.VMEM((size, outs), HALF),
                pltpu.VMEM(raw_shape, FULL),
            ],
        ),
        out_shape=[jax.ShapeDtypeStruct((count, per_sample, share), HALF)] * shards
        + [grad_out, jax.ShapeDtypeStruct(bias_shape, FULL)],
        compiler_params=params(),
        cost_estimate=pl.CostEstimate(
            flops=count * size * share * size * 20, bytes_accessed=count * size * share * 16, transcendentals=0
        ),
        name="spectral_back",
    )(scal, table, head_w, spec_w, *saved, *residual, *(before or ()))
    return result[:shards], result[shards:]


def embedded_back_chunk(scal, embedded, residual, head_w, gain, spec_grad, first, cells):
    shards = len(spec_grad)
    count, per_sample, share = spec_grad[0].shape
    rows = count * per_sample
    width, outs = head_w.shape

    def body(scal_ref, emb_ref, res_ref, w_ref, gain_ref, *refs):
        grad_refs, (out_ref, sums_ref, held) = refs[:shards], refs[shards:]
        fill_lanes(scal_ref, grad_refs, held)
        _, valid = token_sides(scal_ref, first, count, per_sample, cells)
        unit, inv_std = layer_norm(emb_ref[...].astype(FULL))
        direct = dot_nt(res_ref[...].reshape(rows, outs), w_ref[...]).astype(HALF).astype(FULL)
        normed_grad = held[...].astype(FULL) + direct
        gain_grad = jnp.sum(normed_grad * unit, axis=0, keepdims=True)
        unit_grad = normed_grad * gain_ref[...]
        mean_grad = jnp.mean(unit_grad, axis=-1, keepdims=True)
        mean_cross = jnp.mean(unit_grad * unit, axis=-1, keepdims=True)
        input_grad = inv_std * (unit_grad - mean_grad - unit * mean_cross)
        result = ((input_grad + direct) * valid).astype(HALF)
        out_ref[...] = result
        bias_grad = jnp.sum(result.astype(FULL), axis=0, keepdims=True)
        sums_ref[0:4] = jnp.broadcast_to(gain_grad, (4, width))
        sums_ref[4:8] = jnp.broadcast_to(bias_grad, (4, width))

    return pl.pallas_call(
        body,
        grid_spec=pltpu.PrefetchScalarGridSpec(
            num_scalar_prefetch=1,
            grid=(1,),
            in_specs=[
                whole((rows, width)),
                whole((count, per_sample, outs)),
                whole((width, outs)),
                whole((1, width)),
            ]
            + [whole(spec_grad[0].shape)] * shards,
            out_specs=[whole((rows, width)), whole((8, width))],
            scratch_shapes=[pltpu.VMEM((rows, width), HALF)],
        ),
        out_shape=[jax.ShapeDtypeStruct((rows, width), HALF), jax.ShapeDtypeStruct((8, width), FULL)],
        compiler_params=params(),
        cost_estimate=pl.CostEstimate(
            flops=2 * rows * width * outs, bytes_accessed=rows * width * 6, transcendentals=0
        ),
        name="embedded_back",
    )(scal, embedded, residual, head_w, gain, *spec_grad)


def turned_patches(scal, patches, groups):
    tokens, depth = patches.shape
    block = depth // groups
    tile = 256
    piece = int(np.gcd(tile, block))
    per_block = block // piece

    def body(scal_ref, x_ref, send_ref, keep_ref):
        turned = x_ref[...].T
        for i in range(tile // piece):
            place = pl.program_id(0) * (tile // piece) + i
            group = place // per_block
            rows = pl.ds(pl.multiple_of((place % per_block) * piece, piece), piece)
            values = turned[i * piece : (i + 1) * piece]
            away = jnp.bitwise_xor(group, scal_ref[GROUP]) % 2

            @pl.when(away == 1)
            def _(group=group, rows=rows, values=values):
                send_ref[group // 2, rows] = values

            @pl.when(away == 0)
            def _(group=group, rows=rows, values=values):
                keep_ref[group // 2, rows] = values

    shape = (groups // 2, block, tokens)
    return pl.pallas_call(
        body,
        grid_spec=pltpu.PrefetchScalarGridSpec(
            num_scalar_prefetch=1,
            grid=(depth // tile,),
            in_specs=[pl.BlockSpec((tokens, tile), lambda i, s: (0, i))],
            out_specs=[whole(shape)] * 2,
        ),
        out_shape=[jax.ShapeDtypeStruct(shape, HALF)] * 2,
        compiler_params=params(),
        cost_estimate=pl.CostEstimate(flops=0, bytes_accessed=4 * tokens * depth, transcendentals=0),
        name="turned_patches",
    )(scal, patches)


def embed_grad_parts(scal, turned, grads, groups):
    pairs, block, tokens = turned[0].shape
    width = grads[0].shape[1]
    half = width // 2
    top = pairs // 2
    count = len(turned)
    depth = tokens * count

    def body(scal_ref, *refs):
        turned_refs, grad_refs = refs[:count], refs[count : count + len(grads)]
        left_send, left_keep, right_send, right_keep, held = refs[count + len(grads) :]
        step = pl.program_id(0)

        @pl.when(step == 0)
        def _():
            row = 0
            for ref in grad_refs:
                held[row : row + ref.shape[0]] = ref[...]
                row += ref.shape[0]

        rows = jnp.concatenate([ref[0] for ref in turned_refs], axis=1)
        total = dot(rows, held[...]).astype(HALF)

        @pl.when(step % 2 == 1)
        def _():
            left_send[step // 2] = total[:, :half]

        @pl.when(step % 2 == 0)
        def _():
            left_keep[step // 2] = total[:, :half]

        @pl.when(step >= top)
        def _():
            right_send[step - top] = total[:, half:]

        @pl.when(step < top)
        def _():
            right_keep[step] = total[:, half:]

    shape = (top, block, half)
    return pl.pallas_call(
        body,
        grid_spec=pltpu.PrefetchScalarGridSpec(
            num_scalar_prefetch=1,
            grid=(pairs,),
            in_specs=[
                pl.BlockSpec((1, block, tokens), lambda i, s: (jnp.bitwise_xor(s[GROUP] // 2, i), 0, 0))
                for _ in turned
            ]
            + [whole(g.shape) for g in grads],
            out_specs=[whole(shape)] * 4,
            scratch_shapes=[pltpu.VMEM((depth, width), HALF)],
        ),
        out_shape=[jax.ShapeDtypeStruct(shape, HALF)] * 4,
        compiler_params=params(),
        cost_estimate=pl.CostEstimate(
            flops=2 * depth * pairs * block * width,
            bytes_accessed=2 * (pairs * block * (depth + width) + depth * width),
            transcendentals=0,
        ),
        name="embed_grad",
    )(scal, *turned, *grads)


def swap_bit(values, bit, groups):
    return lax.ppermute(values, "grp", [(g, g ^ (1 << bit)) for g in range(groups)])


def across(pieces):
    shards = len(pieces)
    return [pieces[0]] + [
        lax.ppermute(pieces[k], "fft", [(z, z ^ k) for z in range(shards)]) for k in range(1, shards)
    ]


def add_half(left, right):
    return (left.astype(FULL) + right.astype(FULL)).astype(HALF)


def scatter_sum(parts, groups, shard_at):
    bits = groups.bit_length() - 1
    shards = lax.axis_size("fft")
    ends = []
    for send, keep, order, low in (
        (parts[0], parts[1], list(range(1, bits)), True),
        (parts[2], parts[3], list(range(bits - 1, 0, -1)), False),
    ):
        total = add_half(keep, swap_bit(send, order[0], groups))
        for bit in order[1:]:
            count, block, width = total.shape
            if low:
                split = total.reshape(count // 2, 2, block, width)
                keep, send = split[:, 0], split[:, 1]
            else:
                split = total.reshape(2, count // 2, block, width)
                keep, send = split[0], split[1]
            total = add_half(keep, swap_bit(send, bit, groups))
        ends.append(total[0])
    block = ends[0].shape[0]
    share = block // shards
    part = jnp.concatenate(ends, axis=-1).reshape(shards, share, -1)
    moved = lax.all_to_all(part, "fft", split_axis=0, concat_axis=0, tiled=True)
    return jnp.sum(moved.astype(FULL), axis=0)


def to_all(values, axes, count):
    return lax.all_to_all(
        jnp.broadcast_to(values[None], (count,) + values.shape), axes, split_axis=0, concat_axis=0, tiled=True
    )


def small_grads(head_grad, head_bias, spec_grad, spec_bias, groups, shards, shard_at):
    outs = head_grad.shape[1]
    head_rows = head_grad.shape[0] // groups
    spec_rows = spec_grad.shape[0] // groups
    small = jnp.concatenate([spec_bias, head_bias[None], jnp.zeros((7 - spec_bias.shape[0], outs), FULL)], axis=0)
    high = lax.optimization_barrier(small.astype(HALF))
    small = jnp.concatenate([high, (small - high.astype(FULL)).astype(HALF)], axis=0)
    packed = jnp.concatenate(
        [
            head_grad.astype(HALF).reshape(groups, head_rows, outs),
            spec_grad.reshape(groups, spec_rows, outs),
            jnp.broadcast_to(small[None], (groups,) + small.shape),
        ],
        axis=1,
    )
    moved = lax.all_to_all(packed, "grp", split_axis=0, concat_axis=0, tiled=True)
    summed = jnp.sum(moved.astype(FULL), axis=0)
    small = summed[head_rows + spec_rows :]
    small = small[:8] + small[8:]
    high = lax.optimization_barrier(small.astype(HALF))
    small = jnp.concatenate([high, (small - high.astype(FULL)).astype(HALF)], axis=0)
    summed = jnp.concatenate([summed[: head_rows + spec_rows].astype(HALF), small], axis=0)
    rows = across([summed] * shards)
    head_part = sum(r[:head_rows].astype(FULL) for r in rows).astype(HALF)
    order = jnp.bitwise_xor(jnp.arange(shards, dtype=jnp.int32), shard_at)
    rest = jnp.take(jnp.stack([r[head_rows:] for r in rows]), order, axis=0)
    small = rest[:, spec_rows:].astype(FULL)
    small = small[:, :8] + small[:, 8:]
    spec_bias_all = small[:, : spec_bias.shape[0]]
    head_bias_all = jnp.sum(small[:, spec_bias.shape[0]], axis=0)
    spec_part = rest[:, :spec_rows].reshape(shards * spec_rows, outs)
    gathered = to_all(jnp.concatenate([head_part, spec_part], axis=0), "grp", groups)
    head_all = gathered[:, :head_rows].reshape(groups * head_rows, outs).astype(FULL)
    spec_all = gathered[:, head_rows:].reshape(groups, shards, spec_rows, outs)
    return head_all, head_bias_all, jnp.swapaxes(spec_all, 0, 1), spec_bias_all


def route_predictions(predicted, dest_group, group_at, groups, slot_count):
    own_dest = lax.dynamic_slice_in_dim(dest_group, group_at * slot_count, slot_count)
    matches = own_dest[None, :] == jnp.arange(groups, dtype=jnp.int32)[:, None]
    chosen = jnp.sum(jnp.where(matches, jnp.arange(slot_count, dtype=jnp.int32)[None, :], 0), axis=1)
    outgoing = jnp.take(predicted, chosen, axis=0)
    moved = lax.all_to_all(outgoing, "grp", split_axis=0, concat_axis=0, tiled=True)
    loaders = jnp.arange(groups, dtype=jnp.int32)
    holds = jnp.any(dest_group.reshape(groups, slot_count) == group_at, axis=1)
    rank = jnp.sum(jnp.where(holds[None, :] & (loaders[None, :] < loaders[:, None]), 1, 0), axis=1)
    slots = jnp.arange(slot_count, dtype=jnp.int32)
    sources = jnp.sum(jnp.where(holds[None, :] & (rank[None, :] == slots[:, None]), loaders[None, :], 0), axis=1)
    return jnp.take(moved, sources, axis=0)


def on_device(
    patches, targets, grid_side, dest_group, embed_w, embed_b, gain, spec_w, spec_b, head_w, head_b
):
    slot_count, row_count, cells, depth = patches.shape
    samples = dest_group.shape[0]
    groups = lax.axis_size("grp")
    shards = lax.axis_size("fft")
    group_at = lax.axis_index("grp").astype(jnp.int32)
    shard_at = lax.axis_index("fft").astype(jnp.int32)
    outs = targets.shape[-1]
    per_sample = row_count * cells
    count = slot_count // CHUNKS
    firsts = [c * count for c in range(CHUNKS)]
    assert slot_count == SLOTS

    sides = lax.dynamic_slice_in_dim(grid_side, group_at * slot_count, slot_count)
    level = jnp.where(sides == cells, 0, jnp.where(sides == cells // 2, 1, 2)).astype(jnp.int32)
    scal = jnp.concatenate([jnp.stack([shard_at, shard_at * row_count, group_at]), sides, level])
    table_values, factors = dft_tables(cells)
    table = jnp.asarray(table_values)
    flat_patches = patches.reshape(-1, depth)
    flat_targets = targets.reshape(-1, outs)
    gain_row, embed_b_row, head_b_row = gain[None], embed_b[None], head_b[None]

    embedded, moved = [], []
    for first in firsts:
        emb, pieces = embed_chunk(
            scal, flat_patches, embed_w, embed_b_row, gain_row, first, count, per_sample, cells, shards
        )
        embedded.append(emb)
        moved.append(across(pieces))
    turned_send, turned_keep = turned_patches(scal, flat_patches, groups)
    turned = [turned_keep, swap_bit(turned_send, 0, groups)]
    mixed, saved = [], []
    for first, pieces in zip(firsts, moved):
        out, rest = spectral_chunk(scal, table, factors, pieces, spec_w, spec_b, first)
        mixed.append(across(out))
        saved.append(rest)
    predicted, residual, head_grads, head_sums, gathered = [], [], [], [], []
    for first, emb, mix in zip(firsts, embedded, mixed):
        pred, res, grad, sums = head_chunk(
            scal, emb, gain_row, mix, flat_targets, head_w, head_b_row, first, samples, cells
        )
        predicted.append(pred)
        residual.append(res)
        head_grads.append(grad)
        head_sums.append(sums[0])
        gathered.append(across([res] * shards))
    spec_back, sums = [], None
    for first, res, rest in zip(firsts, gathered, saved):
        pieces, sums = spectral_back_chunk(
            scal, table, factors, res, head_w, spec_w, rest, first, sums, first == firsts[-1]
        )
        spec_back.append(across(pieces))
    own_grads, other_grads, row_sums = [], [], []
    for first, emb, res, back in zip(firsts, embedded, residual, spec_back):
        grad, row_sum = embedded_back_chunk(scal, emb, res, head_w, gain_row, back, first, cells)
        own_grads.append(grad)
        other_grads.append(swap_bit(grad, 0, groups))
        row_sums.append(row_sum)
    parts = embed_grad_parts(scal, turned, own_grads + other_grads, groups)
    embed_grad = scatter_sum(parts, groups, shard_at)

    predictions = route_predictions(
        jnp.concatenate(predicted, axis=0), dest_group, group_at, groups, slot_count
    ).reshape(targets.shape)
    spec_grad, spec_bias = sums
    head_grad, head_bias_grad, spec_all, spec_bias_all = small_grads(
        sum(head_grads), sum(head_sums), spec_grad, spec_bias, groups, shards, shard_at
    )
    width = spec_w.shape[-1]
    blocks = spec_w.shape[2] // shards
    spec_all = spec_all.reshape(shards, 2, blocks, width, 2, width)
    spec_w_grad = jnp.transpose(spec_all, (1, 4, 0, 2, 3, 5)).reshape(spec_w.shape).astype(FULL)
    spec_bias_all = spec_bias_all.reshape(shards, 2, blocks, 2, width)
    spec_b_grad = jnp.transpose(spec_bias_all, (1, 3, 0, 2, 4)).reshape(spec_b.shape)
    rows = sum(row_sums)
    rows = jnp.sum(to_all(rows.reshape(2, 4, -1)[:, 0], ("grp", "fft"), groups * shards), axis=0)
    gain_grad, embed_bias_grad = rows[0], rows[1]
    return (
        predictions,
        embed_grad,
        embed_bias_grad,
        gain_grad,
        spec_w_grad,
        spec_b_grad,
        head_grad,
        head_bias_grad,
    )


def solution(mesh):
    return jax.shard_map(
        on_device,
        mesh=mesh,
        in_specs=(
            P("grp", "fft", None, None),
            P("grp", "fft", None, None),
            P(),
            P(),
            P(),
            P(),
            P(),
            P(),
            P(),
            P(),
            P(),
        ),
        out_specs=(
            P("grp", "fft", None, None),
            P(("grp", "fft"), None),
            P(),
            P(),
            P(),
            P(),
            P(),
            P(),
        ),
        check_vma=False,
    )
```

time: 439 us -> 227 us (0.52)
  waiting for transfers between devices: 162 us -> 56.1 us
  blocking collectives: 96.5 us -> 0 us
  local copies, waits for them, and re-layouts: 48.2 us -> 17.6 us
  starting transfers between devices: 40.8 us -> 67.4 us
  Pallas kernels: 55.1 us -> 71 us
  between operations: 16 us -> 1.35 us
  other arithmetic: 18.5 us -> 12.3 us
    psum x2 -> x0, waiting for transfers between devices: 136 us -> none  [the longest x1 84 us: on_device(): lax.psum((sum(head_grads), sum(head_sums)), ('grp', 'fft'))]
    psum x2 -> x0, blocking collectives: 51.5 us -> none  [the longest x1 39.6 us: on_device(): gain_grad, embed_bias_grad = lax.psum((rows[0], rows[4]), ('grp', 'fft'))]
    all_gather x3 -> x0, blocking collectives: 45 us -> none  [the longest x2 31 us: on_device(): gathered.append(lax.all_gather(res.reshape(count, per_sample, outs), 'fft'))]
    ppermute x0 -> x27, starting transfers between devices: none -> 41.4 us  [across(): lax.ppermute(pieces[k], 'fft', [(z, z ^ k) for z in range(shards)])]
    unnamed x125 -> x83, local copies, waits for them, and re-layouts: 40.8 us -> 6.15 us
    all_to_all x6 -> x3, starting transfers between devices: 29.3 us -> 11.3 us  [the longest x2 7.72 us: to_all(): lax.all_to_all(jnp.broadcast_to(values[None], (count,) + values.shape), a...]
    ppermute x0 -> x27, waiting for transfers between devices: none -> 16.1 us  [across(): lax.ppermute(pieces[k], 'fft', [(z, z ^ k) for z in range(shards)])]
    all_to_all x1, waiting for transfers between devices: 0.01 us -> 9.19 us  [scatter_sum(): moved = lax.all_to_all(part, 'fft', split_axis=0, concat_axis=0, tiled=True)]
  transfers between devices with their start and end apart: 16 -> 39, of which waited for: 8 -> 9; matrix products, arithmetic and copies ran while one was open for 7% -> 10% of each run, Pallas kernels for 9% -> 29%
where the time goes in v2:
time: 227 us; the launch traced here: 226 us
  Pallas kernels  71 us (31%)
  starting transfers between devices  67.4 us (30%)
  waiting for transfers between devices  56.1 us (25%)
  local copies, waits for them, and re-layouts  17.6 us (8%)
  other arithmetic  12.3 us (5%)
    ppermute x27, starting transfers between devices, across(): lax.ppermute(pieces[k], 'fft', [(z, z ^ k) for z in range(shards)])  41.4 us
    ppermute x7, waiting for transfers between devices, swap_bit(): lax.ppermute(values, 'grp', [(g, g ^ 1 << bit) for g in range(groups)])  21.8 us
    ppermute x27, waiting for transfers between devices, across(): lax.ppermute(pieces[k], 'fft', [(z, z ^ k) for z in range(shards)])  16.1 us
    pallas_call x2, Pallas kernels, spectral_back_chunk(): pl.pallas_call(body, grid_spec=pltpu.PrefetchScalarGridSpec(num_scalar_pr...  15.3 us
    pallas_call x2, Pallas kernels, embed_chunk(): pl.pallas_call(body, grid_spec=pltpu.PrefetchScalarGridSpec(num_scalar_pr...  13.3 us
    pallas_call x2, Pallas kernels, spectral_chunk(): pl.pallas_call(body, grid_spec=pltpu.PrefetchScalarGridSpec(num_scalar_pr...  11.8 us
    all_to_all x1, waiting for transfers between devices, scatter_sum(): moved = lax.all_to_all(part, 'fft', split_axis=0, concat_axis=0, tiled=True)  9.19 us
    all_to_all x2, waiting for transfers between devices, to_all(): lax.all_to_all(jnp.broadcast_to(values[None], (count,) + values.shape), a...  9.04 us
  transfers between devices with their start and end apart: 39, of which 9 were waited for; matrix products, arithmetic and copies ran while one was open for 10% of the time, Pallas kernels for 29%

profile of v2, /device:TPU:0, one launch (start us, length us, event | category | flops | bytes accessed | tf_op | source)
XLA Modules:
  0.0 225.8 jit_solution(6246212542726554922)
XLA Ops:
  2.0 6.6 %embed.3 = (bf16[192,1024]{1,0:T(8,128)(2,1)}, bf16[3,64,256]{2,1,0:T(8,128)(2,1)}, bf16[3,64,256]{2,1,0:T(8,128)(2,1)}, bf16[3,64,256]{2,1,0:T(8,128)(2,1)}, bf16[3,64,256]{2,1,0:T(8,128)(2,1)}) custom-call(s32[15]{0:T(128)} %concatenate.29.scal_ref, bf16[384,2560]{1,0:T(8,128)(2,1)} %bitcast.59, bf16[2560,1024]{1,0:T(8,128)(2,1)} %w_ref.13, ...), custom_call_target="tpu_custom_call" | custom-call | flops 1006632960 | bytes 6225920 | tf_op jit(solution)/shard_map/embed/pallas_call | solution.py:136
  8.6 3.1 %collective-permute-start.6 = (bf16[3,64,256]{2,1,0:T(8,128)(2,1)}, bf16[3,64,256]{2,1,0:T(8,128)(2,1)S(1)}, u32[]{:S(2)}, u32[]{:S(2)}) collective-permute-start(bf16[3,64,256]{2,1,0:T(8,128)(2,1)} %get-tuple-element.74), channel_id=1, source_target_pairs={{0,1},{1,0},{2,3},{3,2},{4,5},{5,4},{6,7},{7,6},{8,9},{9,8},{10,11... | collective-permute-start | bytes 294920 | tf_op jit(solution)/shard_map/ppermute | solution.py:582
  11.7 2.6 %collective-permute-start.7 = (bf16[3,64,256]{2,1,0:T(8,128)(2,1)}, bf16[3,64,256]{2,1,0:T(8,128)(2,1)S(1)}, u32[]{:S(2)}, u32[]{:S(2)}) collective-permute-start(bf16[3,64,256]{2,1,0:T(8,128)(2,1)} %get-tuple-element.75), channel_id=1, source_target_pairs={{0,2},{1,3},{2,0},{3,1},{4,6},{5,7},{6,4},{7,5},{8,10},{9,11},{10,... | collective-permute-start | bytes 294920 | tf_op jit(solution)/shard_map/ppermute | solution.py:582
  14.3 6.7 %embed.2 = (bf16[192,1024]{1,0:T(8,128)(2,1)}, bf16[3,64,256]{2,1,0:T(8,128)(2,1)}, bf16[3,64,256]{2,1,0:T(8,128)(2,1)}, bf16[3,64,256]{2,1,0:T(8,128)(2,1)}, bf16[3,64,256]{2,1,0:T(8,128)(2,1)}) custom-call(s32[15]{0:T(128)} %concatenate.29.scal_ref, bf16[384,2560]{1,0:T(8,128)(2,1)} %bitcast.60, bf16[2560,1024]{1,0:T(8,128)(2,1)} %w_ref.13, ...), custom_call_target="tpu_custom_call" | custom-call | flops 1006632960 | bytes 6225920 | tf_op jit(solution)/shard_map/embed/pallas_call | solution.py:136
  21.6 3.8 %collective-permute-start.2 = (bf16[3,64,256]{2,1,0:T(8,128)(2,1)}, bf16[3,64,256]{2,1,0:T(8,128)(2,1)S(1)}, u32[]{:S(2)}, u32[]{:S(2)}) collective-permute-start(bf16[3,64,256]{2,1,0:T(8,128)(2,1)} %get-tuple-element.66), channel_id=1, source_target_pairs={{0,3},{1,2},{2,1},{3,0},{4,7},{5,6},{6,5},{7,4},{8,11},{9,10},{10,... | collective-permute-start | bytes 294920 | tf_op jit(solution)/shard_map/ppermute | solution.py:582
  26.7 7.4 %collective-permute-done.1.refs_2_ = bf16[3,64,256]{2,1,0:T(8,128)(2,1)S(1)} collective-permute-done((bf16[3,64,256]{2,1,0:T(8,128)(2,1)}, bf16[3,64,256]{2,1,0:T(8,128)(2,1)S(1)}, u32[]{:S(2)}, u32[]{:S(2)}) %collective-permute-start.1) | collective-permute-done | bytes 98336 | tf_op jit(solution)/shard_map/ppermute | solution.py:582
  34.8 5.9 %spectral.2 = (bf16[3,64,256]{2,1,0:T(8,128)(2,1)}, bf16[3,64,256]{2,1,0:T(8,128)(2,1)}, bf16[3,64,256]{2,1,0:T(8,128)(2,1)}, bf16[3,64,256]{2,1,0:T(8,128)(2,1)...) custom-call(s32[15]{0:T(128)} %concatenate.29.scal_ref, ...), custom_call_target="tpu_custom_call" | custom-call | flops 704643072 | bytes 3145728 | tf_op jit(solution)/shard_map/spectral/pallas_call | solution.py:244
  40.7 2.2 collective-permute-start.3
  42.9 8.0 %turned_patches.1 = (bf16[4,320,384]{2,1,0:T(8,128)(2,1)}, bf16[4,320,384]{2,1,0:T(8,128)(2,1)}) custom-call(s32[15]{0:T(128)} %concatenate.29.scal_ref, bf16[384,2560]{1,0:T(8,128)(2,1)} %bitcast.61), custom_call_target="tpu_custom_call" | custom-call | bytes 3932160 | tf_op jit(solution)/shard_map/turned_patches/pallas_call | solution.py:496
  51.0 2.4 %collective-permute-start.5 = (bf16[3,64,256]{2,1,0:T(8,128)(2,1)S(1)}, bf16[3,64,256]{2,1,0:T(8,128)(2,1)S(1)}, u32[]{:S(2)}, u32[]{:S(2)}) collective-permute-start(bf16[3,64,256]{2,1,0:T(8,128)(2,1)S(1)} %copy-done.33), channel_id=1, source_target_pairs={{0,3},{1,2},{2,1},{3,0},{4,7},{5,6},{6,5},{7,4},{8,11},{9,10},{10,... | collective-permute-start | bytes 294920 | tf_op jit(solution)/shard_map/ppermute | solution.py:582
  54.1 5.9 %spectral.3 = (bf16[3,64,256]{2,1,0:T(8,128)(2,1)}, bf16[3,64,256]{2,1,0:T(8,128)(2,1)}, bf16[3,64,256]{2,1,0:T(8,128)(2,1)}, bf16[3,64,256]{2,1,0:T(8,128)(2,1)...) custom-call(s32[15]{0:T(128)} %concatenate.29.scal_ref, ...), custom_call_target="tpu_custom_call" | custom-call | flops 704643072 | bytes 3145728 | tf_op jit(solution)/shard_map/spectral/pallas_call | solution.py:244
  60.1 1.2 collective-permute-start.9
  62.2 2.3 %collective-permute-start.11 = (bf16[3,64,256]{2,1,0:T(8,128)(2,1)}, bf16[3,64,256]{2,1,0:T(8,128)(2,1)S(1)}, u32[]{:S(2)}, u32[]{:S(2)}) collective-permute-start(bf16[3,64,256]{2,1,0:T(8,128)(2,1)} %get-tuple-element.80), channel_id=1, source_target_pairs={{0,3},{1,2},{2,1},{3,0},{4,7},{5,6},{6,5},{7,4},{8,11},{9,10},{10,... | collective-permute-start | bytes 294920 | tf_op jit(solution)/shard_map/ppermute | solution.py:582
  65.2 3.9 %head.2 = (bf16[3,64,256]{2,1,0:T(8,128)(2,1)}, bf16[3,64,256]{2,1,0:T(8,128)(2,1)}, f32[1024,256]{1,0:T(8,128)}, f32[8,256]{1,0:T(8,128)}) custom-call(s32[15]{0:T(128)} %concatenate.29.scal_ref, bf16[192,1024]{1,0:T(8,128)(2,1)} %get-tuple-element.62.emb_ref, f32[1,1024]{1,0:T(1,128)} %bitcast.75, bf16[384,256]{1,0:T(8,128)(2,1)} %bitcast.68, ...), custom_call_target="tpu_custom_call" | custom-call | flops 201326592 | bytes 2359296 | tf_op jit(solution)/shard_map/head/pallas_call | solution.py:294
  69.1 1.5 collective-permute-start.15
  70.8 2.7 %collective-permute-start.13 = (bf16[3,64,256]{2,1,0:T(8,128)(2,1)}, bf16[3,64,256]{2,1,0:T(8,128)(2,1)S(1)}, u32[]{:S(2)}, u32[]{:S(2)}) collective-permute-start(bf16[3,64,256]{2,1,0:T(8,128)(2,1)} %get-tuple-element.84.refs_0_.res_ref), channel_id=1, source_target_pairs={{0,1},{1,0},{2,3},{3,2},{4,5},{5,4},{6,7},{7,6},{8,9},{9,8},{10,11... | collective-permute-start | bytes 294920 | tf_op jit(solution)/shard_map/ppermute | solution.py:582
  74.2 3.9 %head.3 = (bf16[3,64,256]{2,1,0:T(8,128)(2,1)}, bf16[3,64,256]{2,1,0:T(8,128)(2,1)}, f32[1024,256]{1,0:T(8,128)}, f32[8,256]{1,0:T(8,128)}) custom-call(s32[15]{0:T(128)} %concatenate.29.scal_ref, bf16[192,1024]{1,0:T(8,128)(2,1)} %get-tuple-element.72.emb_ref, f32[1,1024]{1,0:T(1,128)} %bitcast.76, bf16[384,256]{1,0:T(8,128)(2,1)} %bitcast.69, ...), custom_call_target="tpu_custom_call" | custom-call | flops 201326592 | bytes 2359296 | tf_op jit(solution)/shard_map/head/pallas_call | solution.py:294
  78.1 1.5 collective-permute-start.21
  82.7 3.7 %all-to-all-start = ((bf16[8,64,256]{2,1,0:T(8,128)(2,1)}), bf16[8,64,256]{2,1,0:T(8,128)(2,1)S(1)}, u32[]{:S(2)}, u32[]{:S(2)}) async-start(bf16[8,64,256]{2,1,0:T(8,128)(2,1)} %broadcast_select_fusion), calls=%async_computation | async-start | bytes 524288 | tf_op jit(solution)/shard_map/all_to_all | solution.py:664
  86.5 2.2 collective-permute-start.19
  89.3 7.7 %spectral_back.2 = (bf16[3,64,256]{2,1,0:T(8,128)(2,1)}, bf16[3,64,256]{2,1,0:T(8,128)(2,1)}, bf16[3,64,256]{2,1,0:T(8,128)(2,1)}, bf16[3,64,256]{2,1,0:T(8,128)...) custom-call(s32[15]{0:T(128)} %concatenate.29.scal_ref, bf16[3,512,256]{2,1,0:T(8,128)(2,1)} %constant.72.clone.t_ref, ...), custom_call_target="tpu_custom_call" | custom-call | flops 1006632960 | bytes 3145728 | tf_op jit(solution)/shard_map/spectral_back/pallas_call | solution.py:389
  97.9 1.5 collective-permute-start.17
  99.4 2.4 %collective-permute-start.18 = (bf16[3,64,256]{2,1,0:T(8,128)(2,1)S(1)}, bf16[3,64,256]{2,1,0:T(8,128)(2,1)S(1)}, u32[]{:S(2)}, u32[]{:S(2)}) collective-permute-start(bf16[3,64,256]{2,1,0:T(8,128)(2,1)S(1)} %copy-done.32), channel_id=1, source_target_pairs={{0,3},{1,2},{2,1},{3,0},{4,7},{5,6},{6,5},{7,4},{8,11},{9,10},{10,... | collective-permute-start | bytes 294920 | tf_op jit(solution)/shard_map/ppermute | solution.py:582
  102.5 7.6 %spectral_back.3 = (bf16[3,64,256]{2,1,0:T(8,128)(2,1)}, bf16[3,64,256]{2,1,0:T(8,128)(2,1)}, bf16[3,64,256]{2,1,0:T(8,128)(2,1)}, bf16[3,64,256]{2,1,0:T(8,128)...) custom-call(s32[15]{0:T(128)} %concatenate.29.scal_ref, bf16[3,512,256]{2,1,0:T(8,128)(2,1)} %constant.72.clone.t_ref, ...), custom_call_target="tpu_custom_call" | custom-call | flops 1006632960 | bytes 3145728 | tf_op jit(solution)/shard_map/spectral_back/pallas_call | solution.py:389
  110.2 2.1 collective-permute-start.23
  112.2 2.3 %collective-permute-start.24 = (bf16[3,64,256]{2,1,0:T(8,128)(2,1)}, bf16[3,64,256]{2,1,0:T(8,128)(2,1)S(1)}, u32[]{:S(2)}, u32[]{:S(2)}) collective-permute-start(bf16[3,64,256]{2,1,0:T(8,128)(2,1)} %get-tuple-element.102), channel_id=1, source_target_pairs={{0,3},{1,2},{2,1},{3,0},{4,7},{5,6},{6,5},{7,4},{8,11},{9,10},{10,... | collective-permute-start | bytes 294920 | tf_op jit(solution)/shard_map/ppermute | solution.py:582
  116.0 3.8 %embedded_back.2 = (bf16[192,1024]{1,0:T(8,128)(2,1)}, f32[8,1024]{1,0:T(8,128)}) custom-call(s32[15]{0:T(128)} %concatenate.29.scal_ref, bf16[192,1024]{1,0:T(8,128)(2,1)} %get-tuple-element.62.emb_ref, bf16[3,64,256]{2,1,0:T(8,128)(2,1)} %get-tuple-element.84.refs_0_.res_ref, bf16[1024,256]{1,0:T(8,128)(2,1)} %w_ref.19, f32[1,1024]{1,0:T(1,128)} %bitcast.77, ...), custom_call_target="tpu_custom_call" | custom-call | flops 100663296 | bytes 1179648 | tf_op jit(solution)/shard_map/embedded_back/pallas_call | solution.py:447
  121.4 3.6 %embedded_back.3 = (bf16[192,1024]{1,0:T(8,128)(2,1)}, f32[8,1024]{1,0:T(8,128)}) custom-call(s32[15]{0:T(128)} %concatenate.29.scal_ref, bf16[192,1024]{1,0:T(8,128)(2,1)} %get-tuple-element.72.emb_ref, bf16[3,64,256]{2,1,0:T(8,128)(2,1)} %get-tuple-element.93.refs_0_.res_ref, bf16[1024,256]{1,0:T(8,128)(2,1)} %w_ref.19, f32[1,1024]{1,0:T(1,128)} %bitcast.78, ...), custom_call_target="tpu_custom_call" | custom-call | flops 100663296 | bytes 1179648 | tf_op jit(solution)/shard_map/embedded_back/pallas_call | solution.py:447
  126.7 4.0 %all-to-all-start.2 = ((f32[32,2,1024]{2,1,0:T(2,128)}), f32[32,2,1024]{2,1,0:T(2,128)S(1)}, u32[]{:S(2)}, u32[]{:S(2)}) async-start(f32[32,2,1024]{2,1,0:T(2,128)} %broadcast_in_dim.130), calls=%async_computation.2 | async-start | bytes 524288 | tf_op jit(solution)/shard_map/all_to_all | solution.py:617
  131.8 9.0 %all-to-all-done.2 = f32[32,2,1024]{2,1,0:T(2,128)S(1)} async-done(((f32[32,2,1024]{2,1,0:T(2,128)}), f32[32,2,1024]{2,1,0:T(2,128)S(1)}, u32[]{:S(2)}, u32[]{:S(2)}) %all-to-all-start.2) | async-done | bytes 262176 | tf_op jit(solution)/shard_map/all_to_all | solution.py:617
  140.9 3.6 %all-to-all-start.3 = ((bf16[8,208,256]{2,1,0:T(8,128)(2,1)}), bf16[8,208,256]{2,1,0:T(8,128)(2,1)S(1)}, u32[]{:S(2)}, u32[]{:S(2)}) async-start(bf16[8,208,256]{2,1,0:T(8,128)(2,1)} %pad_maximum_fusion), calls=%async_computation.3 | async-start | bytes 1703936 | tf_op jit(solution)/shard_map/all_to_all | solution.py:637
  147.2 7.4 %embed_grad.1 = (bf16[2,320,512]{2,1,0:T(8,128)(2,1)}, bf16[2,320,512]{2,1,0:T(8,128)(2,1)}, bf16[2,320,512]{2,1,0:T(8,128)(2,1)}, bf16[2,320,512]{2,1,0:T(8,128)(2,1)}) custom-call(s32[15]{0:T(128)} %concatenate.29.scal_ref, bf16[4,320,384]{2,1,0:T(8,128)(2,1)} %get-tuple-element.82.refs_0_, bf16[4,320,384]{2,1,0:T(8,128)(2,1)} %collective-permute-done.12.refs_1_, ...), custom_call_target="tpu_custom_call" | custom-call | flops 2013265920 | bytes 6160384 | tf_op jit(solution)/shard_map/embed_grad/pallas_call | solution.py:551
  154.6 1.9 collective-permute-start.27
  156.5 1.5 collective-permute-start.29
  158.2 1.8 collective-permute-start.33
  160.8 1.8 collective-permute-start.31
  162.7 3.3 %collective-permute-done.33 = bf16[208,256]{1,0:T(8,128)(2,1)S(1)} collective-permute-done((bf16[208,256]{1,0:T(8,128)(2,1)S(1)}, bf16[208,256]{1,0:T(8,128)(2,1)S(1)}, u32[]{:S(2)}, u32[]{:S(2)}) %collective-permute-start.33) | collective-permute-done | bytes 106528 | tf_op jit(solution)/shard_map/ppermute | solution.py:582
  166.0 4.2 %collective-permute-done.32 = bf16[208,256]{1,0:T(8,128)(2,1)S(1)} collective-permute-done((bf16[208,256]{1,0:T(8,128)(2,1)S(1)}, bf16[208,256]{1,0:T(8,128)(2,1)S(1)}, u32[]{:S(2)}, u32[]{:S(2)}) %collective-permute-start.32) | collective-permute-done | bytes 106528 | tf_op jit(solution)/shard_map/ppermute | solution.py:582
  171.0 1.2 broadcast_in_dim.135
  172.3 3.7 %all-to-all-start.4 = ((bf16[8,384,256]{2,1,0:T(8,128)(2,1)}), bf16[8,384,256]{2,1,0:T(8,128)(2,1)S(1)}, u32[]{:S(2)}, u32[]{:S(2)}) async-start(bf16[8,384,256]{2,1,0:T(8,128)(2,1)} %broadcast_in_dim.135), calls=%async_computation.4 | async-start | bytes 3145728 | tf_op jit(solution)/shard_map/all_to_all | solution.py:617
  176.0 1.3 fusion
  177.4 2.0 collective-permute-start.28
  179.6 1.5 collective-permute-start.30
  181.7 21.3 %collective-permute-done.28 = bf16[1,320,512]{2,1,0:T(8,128)(2,1)S(1)} collective-permute-done((bf16[1,320,512]{2,1,0:T(8,128)(2,1)S(1)}, bf16[1,320,512]{2,1,0:T(8,128)(2,1)S(1)}, u32[]{:S(2)}, u32[]{:S(2)}) %collective-permute-start.28) | collective-permute-done | bytes 327712 | tf_op jit(solution)/shard_map/ppermute | solution.py:576
  204.2 3.5 %all-to-all-start.1 = ((bf16[4,80,1024]{2,1,0:T(8,128)(2,1)}), bf16[4,80,1024]{2,1,0:T(8,128)(2,1)S(1)}, u32[]{:S(2)}, u32[]{:S(2)}) async-start(bf16[4,80,1024]{2,1,0:T(8,128)(2,1)} %pad_maximum_fusion.1), calls=%async_computation.1 | async-start | bytes 1310720 | tf_op jit(solution)/shard_map/all_to_all | solution.py:612
  209.4 2.1 reshape.162
  211.5 3.2 %copy.28 = f32[2,2,4,2,128,128]{5,4,3,2,1,0:T(8,128)} copy(f32[2,2,4,2,128,128]{5,1,4,3,0,2:T(2,128)} %bitcast.62) | data formatting | bytes 4194304 | tf_op jit(solution)/shard_map/convert_element_type | solution.py:746
  215.8 9.2 %all-to-all-done.1 = bf16[4,80,1024]{2,1,0:T(8,128)(2,1)S(1)} async-done(((bf16[4,80,1024]{2,1,0:T(8,128)(2,1)}), bf16[4,80,1024]{2,1,0:T(8,128)(2,1)S(1)}, u32[]{:S(2)}, u32[]{:S(2)}) %all-to-all-start.1) | async-done | bytes 655392 | tf_op jit(solution)/shard_map/all_to_all | solution.py:612
  (202 shorter events, 28.3 us)
Async XLA Ops:
  8.6 42.4 %collective-permute-start.6 = (bf16[3,64,256]{2,1,0:T(8,128)(2,1)}, bf16[3,64,256]{2,1,0:T(8,128)(2,1)S(1)}, u32[]{:S(2)}, u32[]{:S(2)}) collective-permute-start(bf16[3,64,256]{2,1,0:T(8,128)(2,1)} %get-tuple-element.74), channel_id=1, source_target_pairs={{0,1},{1,0},{2,3},{3,2},{4,5},{5,4},{6,7},{7,6},{8,9},{9,8},{10,11... | collective-permute-start | bytes 294920 | tf_op jit(solution)/shard_map/ppermute | solution.py:582
  11.7 13.7 %copy-start.40 = (s32[48]{0:T(128)S(1)}, s32[48]{0:T(128)}, u32[]{:S(2)}) copy-start(s32[48]{0:T(128)} %param.15) | copy-start | bytes 580
  11.7 14.6 %copy-start.31 = (bf16[3,64,256]{2,1,0:T(8,128)(2,1)S(1)}, bf16[3,64,256]{2,1,0:T(8,128)(2,1)}, u32[]{:S(2)}) copy-start(bf16[3,64,256]{2,1,0:T(8,128)(2,1)} %get-tuple-element.76) | copy-start | bytes 294916
  11.7 41.7 %collective-permute-start.7 = (bf16[3,64,256]{2,1,0:T(8,128)(2,1)}, bf16[3,64,256]{2,1,0:T(8,128)(2,1)S(1)}, u32[]{:S(2)}, u32[]{:S(2)}) collective-permute-start(bf16[3,64,256]{2,1,0:T(8,128)(2,1)} %get-tuple-element.75), channel_id=1, source_target_pairs={{0,2},{1,3},{2,0},{3,1},{4,6},{5,7},{6,4},{7,5},{8,10},{9,11},{10,... | collective-permute-start | bytes 294920 | tf_op jit(solution)/shard_map/ppermute | solution.py:582
  21.0 5.3 %collective-permute-start = (bf16[3,64,256]{2,1,0:T(8,128)(2,1)}, bf16[3,64,256]{2,1,0:T(8,128)(2,1)S(1)}, u32[]{:S(2)}, u32[]{:S(2)}) collective-permute-start(bf16[3,64,256]{2,1,0:T(8,128)(2,1)} %get-tuple-element.64), channel_id=1, source_target_pairs={{0,1},{1,0},{2,3},{3,2},{4,5},{5,4},{6,7},{7,6},{8,9},{9,8},{10,11... | collective-permute-start | bytes 294920 | tf_op jit(solution)/shard_map/ppermute | solution.py:582
  21.5 12.6 %collective-permute-start.1 = (bf16[3,64,256]{2,1,0:T(8,128)(2,1)}, bf16[3,64,256]{2,1,0:T(8,128)(2,1)S(1)}, u32[]{:S(2)}, u32[]{:S(2)}) collective-permute-start(bf16[3,64,256]{2,1,0:T(8,128)(2,1)} %get-tuple-element.65), channel_id=1, source_target_pairs={{0,2},{1,3},{2,0},{3,1},{4,6},{5,7},{6,4},{7,5},{8,10},{9,11},{10,... | collective-permute-start | bytes 294920 | tf_op jit(solution)/shard_map/ppermute | solution.py:582
  21.6 12.5 %collective-permute-start.2 = (bf16[3,64,256]{2,1,0:T(8,128)(2,1)}, bf16[3,64,256]{2,1,0:T(8,128)(2,1)S(1)}, u32[]{:S(2)}, u32[]{:S(2)}) collective-permute-start(bf16[3,64,256]{2,1,0:T(8,128)(2,1)} %get-tuple-element.66), channel_id=1, source_target_pairs={{0,3},{1,2},{2,1},{3,0},{4,7},{5,6},{6,5},{7,4},{8,11},{9,10},{10,... | collective-permute-start | bytes 294920 | tf_op jit(solution)/shard_map/ppermute | solution.py:582
  26.3 27.2 %collective-permute-start.8 = (bf16[3,64,256]{2,1,0:T(8,128)(2,1)S(1)}, bf16[3,64,256]{2,1,0:T(8,128)(2,1)S(1)}, u32[]{:S(2)}, u32[]{:S(2)}) collective-permute-start(bf16[3,64,256]{2,1,0:T(8,128)(2,1)S(1)} %copy-done.31), channel_id=1, source_target_pairs={{0,3},{1,2},{2,1},{3,0},{4,7},{5,6},{6,5},{7,4},{8,11},{9,10},{10,... | collective-permute-start | bytes 294920 | tf_op jit(solution)/shard_map/ppermute | solution.py:582
  40.7 10.3 %copy-start.34 = (bf16[3,64,256]{2,1,0:T(8,128)(2,1)S(1)}, bf16[3,64,256]{2,1,0:T(8,128)(2,1)}, u32[]{:S(2)}) copy-start(bf16[3,64,256]{2,1,0:T(8,128)(2,1)} %get-tuple-element.69) | copy-start | bytes 294916
  40.7 10.4 %copy-start.33 = (bf16[3,64,256]{2,1,0:T(8,128)(2,1)S(1)}, bf16[3,64,256]{2,1,0:T(8,128)(2,1)}, u32[]{:S(2)}) copy-start(bf16[3,64,256]{2,1,0:T(8,128)(2,1)} %get-tuple-element.70) | copy-start | bytes 294916
  40.7 21.5 %collective-permute-start.3 = (bf16[3,64,256]{2,1,0:T(8,128)(2,1)}, bf16[3,64,256]{2,1,0:T(8,128)(2,1)S(1)}, u32[]{:S(2)}, u32[]{:S(2)}) collective-permute-start(bf16[3,64,256]{2,1,0:T(8,128)(2,1)} %get-tuple-element.68), channel_id=1, source_target_pairs={{0,1},{1,0},{2,3},{3,2},{4,5},{5,4},{6,7},{7,6},{8,9},{9,8},{10,11... | collective-permute-start | bytes 294920 | tf_op jit(solution)/shard_map/ppermute | solution.py:582
  51.0 13.5 %collective-permute-start.4 = (bf16[3,64,256]{2,1,0:T(8,128)(2,1)S(1)}, bf16[3,64,256]{2,1,0:T(8,128)(2,1)S(1)}, u32[]{:S(2)}, u32[]{:S(2)}) collective-permute-start(bf16[3,64,256]{2,1,0:T(8,128)(2,1)S(1)} %copy-done.34), channel_id=1, source_target_pairs={{0,2},{1,3},{2,0},{3,1},{4,6},{5,7},{6,4},{7,5},{8,10},{9,11},{10,... | collective-permute-start | bytes 294920 | tf_op jit(solution)/shard_map/ppermute | solution.py:582
  51.0 13.5 %collective-permute-start.5 = (bf16[3,64,256]{2,1,0:T(8,128)(2,1)S(1)}, bf16[3,64,256]{2,1,0:T(8,128)(2,1)S(1)}, u32[]{:S(2)}, u32[]{:S(2)}) collective-permute-start(bf16[3,64,256]{2,1,0:T(8,128)(2,1)S(1)} %copy-done.33), channel_id=1, source_target_pairs={{0,3},{1,2},{2,1},{3,0},{4,7},{5,6},{6,5},{7,4},{8,11},{9,10},{10,... | collective-permute-start | bytes 294920 | tf_op jit(solution)/shard_map/ppermute | solution.py:582
  60.1 10.8 %collective-permute-start.9 = (bf16[3,64,256]{2,1,0:T(8,128)(2,1)}, bf16[3,64,256]{2,1,0:T(8,128)(2,1)S(1)}, u32[]{:S(2)}, u32[]{:S(2)}) collective-permute-start(bf16[3,64,256]{2,1,0:T(8,128)(2,1)} %get-tuple-element.78), channel_id=1, source_target_pairs={{0,1},{1,0},{2,3},{3,2},{4,5},{5,4},{6,7},{7,6},{8,9},{9,8},{10,11... | collective-permute-start | bytes 294920 | tf_op jit(solution)/shard_map/ppermute | solution.py:582
  61.2 12.3 %collective-permute-start.10 = (bf16[3,64,256]{2,1,0:T(8,128)(2,1)}, bf16[3,64,256]{2,1,0:T(8,128)(2,1)S(1)}, u32[]{:S(2)}, u32[]{:S(2)}) collective-permute-start(bf16[3,64,256]{2,1,0:T(8,128)(2,1)} %get-tuple-element.79), channel_id=1, source_target_pairs={{0,2},{1,3},{2,0},{3,1},{4,6},{5,7},{6,4},{7,5},{8,10},{9,11},{10,... | collective-permute-start | bytes 294920 | tf_op jit(solution)/shard_map/ppermute | solution.py:582
  62.2 11.4 %collective-permute-start.11 = (bf16[3,64,256]{2,1,0:T(8,128)(2,1)}, bf16[3,64,256]{2,1,0:T(8,128)(2,1)S(1)}, u32[]{:S(2)}, u32[]{:S(2)}) collective-permute-start(bf16[3,64,256]{2,1,0:T(8,128)(2,1)} %get-tuple-element.80), channel_id=1, source_target_pairs={{0,3},{1,2},{2,1},{3,0},{4,7},{5,6},{6,5},{7,4},{8,11},{9,10},{10,... | collective-permute-start | bytes 294920 | tf_op jit(solution)/shard_map/ppermute | solution.py:582
  69.1 17.3 %collective-permute-start.15 = (bf16[3,64,256]{2,1,0:T(8,128)(2,1)}, bf16[3,64,256]{2,1,0:T(8,128)(2,1)S(1)}, u32[]{:S(2)}, u32[]{:S(2)}) collective-permute-start(bf16[3,64,256]{2,1,0:T(8,128)(2,1)} %get-tuple-element.84.refs_0_.res_ref), channel_id=1, source_target_pairs={{0,3},{1,2},{2,1},{3,0},{4,7},{5,6},{6,5},{7,4},{8,11},{9,10},{10,... | collective-permute-start | bytes 294920 | tf_op jit(solution)/shard_map/ppermute | solution.py:582
  70.6 18.0 %collective-permute-start.14 = (bf16[3,64,256]{2,1,0:T(8,128)(2,1)}, bf16[3,64,256]{2,1,0:T(8,128)(2,1)S(1)}, u32[]{:S(2)}, u32[]{:S(2)}) collective-permute-start(bf16[3,64,256]{2,1,0:T(8,128)(2,1)} %get-tuple-element.84.refs_0_.res_ref), channel_id=1, source_target_pairs={{0,2},{1,3},{2,0},{3,1},{4,6},{5,7},{6,4},{7,5},{8,10},{9,11},{10,... | collective-permute-start | bytes 294920 | tf_op jit(solution)/shard_map/ppermute | solution.py:582
  70.8 17.9 %collective-permute-start.13 = (bf16[3,64,256]{2,1,0:T(8,128)(2,1)}, bf16[3,64,256]{2,1,0:T(8,128)(2,1)S(1)}, u32[]{:S(2)}, u32[]{:S(2)}) collective-permute-start(bf16[3,64,256]{2,1,0:T(8,128)(2,1)} %get-tuple-element.84.refs_0_.res_ref), channel_id=1, source_target_pairs={{0,1},{1,0},{2,3},{3,2},{4,5},{5,4},{6,7},{7,6},{8,9},{9,8},{10,11... | collective-permute-start | bytes 294920 | tf_op jit(solution)/shard_map/ppermute | solution.py:582
  78.1 8.4 %copy-start.5 = (bf16[3,64,256]{2,1,0:T(8,128)(2,1)S(1)}, bf16[3,64,256]{2,1,0:T(8,128)(2,1)}, u32[]{:S(2)}) copy-start(bf16[3,64,256]{2,1,0:T(8,128)(2,1)} %get-tuple-element.93.refs_0_.res_ref) | copy-start | bytes 294916
  78.1 21.3 %collective-permute-start.21 = (bf16[3,64,256]{2,1,0:T(8,128)(2,1)}, bf16[3,64,256]{2,1,0:T(8,128)(2,1)S(1)}, u32[]{:S(2)}, u32[]{:S(2)}) collective-permute-start(bf16[3,64,256]{2,1,0:T(8,128)(2,1)} %get-tuple-element.93.refs_0_.res_ref), channel_id=1, source_target_pairs={{0,3},{1,2},{2,1},{3,0},{4,7},{5,6},{6,5},{7,4},{8,11},{9,10},{10,... | collective-permute-start | bytes 294920 | tf_op jit(solution)/shard_map/ppermute | solution.py:582
  79.6 22.2 %collective-permute-start.20 = (bf16[3,64,256]{2,1,0:T(8,128)(2,1)}, bf16[3,64,256]{2,1,0:T(8,128)(2,1)S(1)}, u32[]{:S(2)}, u32[]{:S(2)}) collective-permute-start(bf16[3,64,256]{2,1,0:T(8,128)(2,1)} %get-tuple-element.93.refs_0_.res_ref), channel_id=1, source_target_pairs={{0,2},{1,3},{2,0},{3,1},{4,6},{5,7},{6,4},{7,5},{8,10},{9,11},{10,... | collective-permute-start | bytes 294920 | tf_op jit(solution)/shard_map/ppermute | solution.py:582
  82.7 43.1 %all-to-all-start = ((bf16[8,64,256]{2,1,0:T(8,128)(2,1)}), bf16[8,64,256]{2,1,0:T(8,128)(2,1)S(1)}, u32[]{:S(2)}, u32[]{:S(2)}) async-start(bf16[8,64,256]{2,1,0:T(8,128)(2,1)} %broadcast_select_fusion), calls=%async_computation | async-start | bytes 524288 | tf_op jit(solution)/shard_map/all_to_all | solution.py:664
  86.5 15.3 %collective-permute-start.19 = (bf16[3,64,256]{2,1,0:T(8,128)(2,1)S(1)}, bf16[3,64,256]{2,1,0:T(8,128)(2,1)S(1)}, u32[]{:S(2)}, u32[]{:S(2)}) collective-permute-start(bf16[3,64,256]{2,1,0:T(8,128)(2,1)S(1)} %copy-done.5), channel_id=1, source_target_pairs={{0,1},{1,0},{2,3},{3,2},{4,5},{5,4},{6,7},{7,6},{8,9},{9,8},{10,11... | collective-permute-start | bytes 294920 | tf_op jit(solution)/shard_map/ppermute | solution.py:582
  97.1 15.2 %collective-permute-start.16 = (bf16[3,64,256]{2,1,0:T(8,128)(2,1)}, bf16[3,64,256]{2,1,0:T(8,128)(2,1)S(1)}, u32[]{:S(2)}, u32[]{:S(2)}) collective-permute-start(bf16[3,64,256]{2,1,0:T(8,128)(2,1)} %get-tuple-element.89), channel_id=1, source_target_pairs={{0,1},{1,0},{2,3},{3,2},{4,5},{5,4},{6,7},{7,6},{8,9},{9,8},{10,11... | collective-permute-start | bytes 294920 | tf_op jit(solution)/shard_map/ppermute | solution.py:582
  97.9 17.4 %collective-permute-start.17 = (bf16[3,64,256]{2,1,0:T(8,128)(2,1)S(1)}, bf16[3,64,256]{2,1,0:T(8,128)(2,1)S(1)}, u32[]{:S(2)}, u32[]{:S(2)}) collective-permute-start(bf16[3,64,256]{2,1,0:T(8,128)(2,1)S(1)} %copy-done.35), channel_id=1, source_target_pairs={{0,2},{1,3},{2,0},{3,1},{4,6},{5,7},{6,4},{7,5},{8,10},{9,11},{10,... | collective-permute-start | bytes 294920 | tf_op jit(solution)/shard_map/ppermute | solution.py:582
  99.4 15.9 %collective-permute-start.18 = (bf16[3,64,256]{2,1,0:T(8,128)(2,1)S(1)}, bf16[3,64,256]{2,1,0:T(8,128)(2,1)S(1)}, u32[]{:S(2)}, u32[]{:S(2)}) collective-permute-start(bf16[3,64,256]{2,1,0:T(8,128)(2,1)S(1)} %copy-done.32), channel_id=1, source_target_pairs={{0,3},{1,2},{2,1},{3,0},{4,7},{5,6},{6,5},{7,4},{8,11},{9,10},{10,... | collective-permute-start | bytes 294920 | tf_op jit(solution)/shard_map/ppermute | solution.py:582
  110.1 9.7 %collective-permute-start.22 = (bf16[3,64,256]{2,1,0:T(8,128)(2,1)}, bf16[3,64,256]{2,1,0:T(8,128)(2,1)S(1)}, u32[]{:S(2)}, u32[]{:S(2)}) collective-permute-start(bf16[3,64,256]{2,1,0:T(8,128)(2,1)} %get-tuple-element.100), channel_id=1, source_target_pairs={{0,1},{1,0},{2,3},{3,2},{4,5},{5,4},{6,7},{7,6},{8,9},{9,8},{10,11... | collective-permute-start | bytes 294920 | tf_op jit(solution)/shard_map/ppermute | solution.py:582
  110.2 10.5 %collective-permute-start.23 = (bf16[3,64,256]{2,1,0:T(8,128)(2,1)}, bf16[3,64,256]{2,1,0:T(8,128)(2,1)S(1)}, u32[]{:S(2)}, u32[]{:S(2)}) collective-permute-start(bf16[3,64,256]{2,1,0:T(8,128)(2,1)} %get-tuple-element.101), channel_id=1, source_target_pairs={{0,2},{1,3},{2,0},{3,1},{4,6},{5,7},{6,4},{7,5},{8,10},{9,11},{10,... | collective-permute-start | bytes 294920 | tf_op jit(solution)/shard_map/ppermute | solution.py:582
  112.2 8.5 %collective-permute-start.24 = (bf16[3,64,256]{2,1,0:T(8,128)(2,1)}, bf16[3,64,256]{2,1,0:T(8,128)(2,1)S(1)}, u32[]{:S(2)}, u32[]{:S(2)}) collective-permute-start(bf16[3,64,256]{2,1,0:T(8,128)(2,1)} %get-tuple-element.102), channel_id=1, source_target_pairs={{0,3},{1,2},{2,1},{3,0},{4,7},{5,6},{6,5},{7,4},{8,11},{9,10},{10,... | collective-permute-start | bytes 294920 | tf_op jit(solution)/shard_map/ppermute | solution.py:582
  115.3 31.7 %collective-permute-start.12 = (bf16[4,320,384]{2,1,0:T(8,128)(2,1)}, bf16[4,320,384]{2,1,0:T(8,128)(2,1)}, u32[]{:S(2)}, u32[]{:S(2)}) collective-permute-start(bf16[4,320,384]{2,1,0:T(8,128)(2,1)} %get-tuple-element.83), channel_id=1, source_target_pairs={{0,4},{4,0},{8,12},{12,8},{16,20},{20,16},{24,28},{28,24},{1,5},{5... | collective-permute-start | bytes 2949128 | tf_op jit(solution)/shard_map/ppermute | solution.py:576
  116.0 14.7 %copy-start.25 = (f32[4,256]{1,0:T(4,128)S(1)}, f32[4,256]{1,0:T(4,128)}, u32[]{:S(2)}) copy-start(f32[4,256]{1,0:T(4,128)} %get-tuple-element.113) | copy-start | bytes 12292
  116.0 14.8 %copy-start.6 = (bf16[512,256]{1,0:T(8,128)(2,1)S(1)}, bf16[512,256]{1,0:T(8,128)(2,1)}, u32[]{:S(2)}) copy-start(bf16[512,256]{1,0:T(8,128)(2,1)} %get-tuple-element.112) | copy-start | bytes 786436
  126.7 14.2 %all-to-all-start.2 = ((f32[32,2,1024]{2,1,0:T(2,128)}), f32[32,2,1024]{2,1,0:T(2,128)S(1)}, u32[]{:S(2)}, u32[]{:S(2)}) async-start(f32[32,2,1024]{2,1,0:T(2,128)} %broadcast_in_dim.130), calls=%async_computation.2 | async-start | bytes 524288 | tf_op jit(solution)/shard_map/all_to_all | solution.py:617
  130.8 13.6 %copy-start.26 = (bf16[192,1024]{1,0:T(8,128)(2,1)S(1)}, bf16[192,1024]{1,0:T(8,128)(2,1)}, u32[]{:S(2)}) copy-start(bf16[192,1024]{1,0:T(8,128)(2,1)} %get-tuple-element.92.refs_2_) | copy-start | bytes 1179652
  130.9 14.1 %copy-start.27 = (bf16[192,1024]{1,0:T(8,128)(2,1)S(1)}, bf16[192,1024]{1,0:T(8,128)(2,1)}, u32[]{:S(2)}) copy-start(bf16[192,1024]{1,0:T(8,128)(2,1)} %get-tuple-element.103.refs_3_) | copy-start | bytes 1179652
  140.9 17.1 %all-to-all-start.3 = ((bf16[8,208,256]{2,1,0:T(8,128)(2,1)}), bf16[8,208,256]{2,1,0:T(8,128)(2,1)S(1)}, u32[]{:S(2)}, u32[]{:S(2)}) async-start(bf16[8,208,256]{2,1,0:T(8,128)(2,1)} %pad_maximum_fusion), calls=%async_computation.3 | async-start | bytes 1703936 | tf_op jit(solution)/shard_map/all_to_all | solution.py:637
  144.4 2.0 collective-permute-start.25
  144.9 2.0 collective-permute-start.26
  154.6 21.4 %collective-permute-start.27 = (bf16[2,320,512]{2,1,0:T(8,128)(2,1)}, bf16[2,320,512]{2,1,0:T(8,128)(2,1)}, u32[]{:S(2)}, u32[]{:S(2)}) collective-permute-start(bf16[2,320,512]{2,1,0:T(8,128)(2,1)} %get-tuple-element.105), channel_id=1, source_target_pairs={{0,8},{4,12},{8,0},{12,4},{16,24},{20,28},{24,16},{28,20},{1,9},{5... | collective-permute-start | bytes 1966088 | tf_op jit(solution)/shard_map/ppermute | solution.py:576
  156.5 22.9 %collective-permute-start.29 = (bf16[2,320,512]{2,1,0:T(8,128)(2,1)}, bf16[2,320,512]{2,1,0:T(8,128)(2,1)S(1)}, u32[]{:S(2)}, u32[]{:S(2)}) collective-permute-start(bf16[2,320,512]{2,1,0:T(8,128)(2,1)} %get-tuple-element.107), channel_id=1, source_target_pairs={{0,16},{4,20},{8,24},{12,28},{16,0},{20,4},{24,8},{28,12},{1,17},{... | collective-permute-start | bytes 1966088 | tf_op jit(solution)/shard_map/ppermute | solution.py:576
  158.2 7.8 %collective-permute-start.33 = (bf16[208,256]{1,0:T(8,128)(2,1)S(1)}, bf16[208,256]{1,0:T(8,128)(2,1)S(1)}, u32[]{:S(2)}, u32[]{:S(2)}) collective-permute-start(bf16[208,256]{1,0:T(8,128)(2,1)S(1)} %pad_maximum_fusion.5), channel_id=1, source_target_pairs={{0,3},{1,2},{2,1},{3,0},{4,7},{5,6},{6,5},{7,4},{8,11},{9,10},{10,... | collective-permute-start | bytes 319496 | tf_op jit(solution)/shard_map/ppermute | solution.py:582
  160.0 10.2 %collective-permute-start.32 = (bf16[208,256]{1,0:T(8,128)(2,1)S(1)}, bf16[208,256]{1,0:T(8,128)(2,1)S(1)}, u32[]{:S(2)}, u32[]{:S(2)}) collective-permute-start(bf16[208,256]{1,0:T(8,128)(2,1)S(1)} %pad_maximum_fusion.5), channel_id=1, source_target_pairs={{0,2},{1,3},{2,0},{3,1},{4,6},{5,7},{6,4},{7,5},{8,10},{9,11},{10,... | collective-permute-start | bytes 319496 | tf_op jit(solution)/shard_map/ppermute | solution.py:582
  160.8 9.4 %collective-permute-start.31 = (bf16[208,256]{1,0:T(8,128)(2,1)S(1)}, bf16[208,256]{1,0:T(8,128)(2,1)S(1)}, u32[]{:S(2)}, u32[]{:S(2)}) collective-permute-start(bf16[208,256]{1,0:T(8,128)(2,1)S(1)} %pad_maximum_fusion.5), channel_id=1, source_target_pairs={{0,1},{1,0},{2,3},{3,2},{4,5},{5,4},{6,7},{7,6},{8,9},{9,8},{10,11... | collective-permute-start | bytes 319496 | tf_op jit(solution)/shard_map/ppermute | solution.py:582
  172.3 31.9 %all-to-all-start.4 = ((bf16[8,384,256]{2,1,0:T(8,128)(2,1)}), bf16[8,384,256]{2,1,0:T(8,128)(2,1)S(1)}, u32[]{:S(2)}, u32[]{:S(2)}) async-start(bf16[8,384,256]{2,1,0:T(8,128)(2,1)} %broadcast_in_dim.135), calls=%async_computation.4 | async-start | bytes 3145728 | tf_op jit(solution)/shard_map/all_to_all | solution.py:617
  177.4 25.6 %collective-permute-start.28 = (bf16[1,320,512]{2,1,0:T(8,128)(2,1)S(1)}, bf16[1,320,512]{2,1,0:T(8,128)(2,1)S(1)}, u32[]{:S(2)}, u32[]{:S(2)}) collective-permute-start(bf16[1,320,512]{2,1,0:T(8,128)(2,1)S(1)} %slice_bitcast_fusion), channel_id=1, source_target_pairs={{0,16},{4,20},{8,24},{12,28},{16,0},{20,4},{24,8},{28,12},{1,17},{... | collective-permute-start | bytes 983048 | tf_op jit(solution)/shard_map/ppermute | solution.py:576
  179.6 23.5 %collective-permute-start.30 = (bf16[1,320,512]{2,1,0:T(8,128)(2,1)S(1)}, bf16[1,320,512]{2,1,0:T(8,128)(2,1)S(1)}, u32[]{:S(2)}, u32[]{:S(2)}) collective-permute-start(bf16[1,320,512]{2,1,0:T(8,128)(2,1)S(1)} %slice.128), channel_id=1, source_target_pairs={{0,8},{4,12},{8,0},{12,4},{16,24},{20,28},{24,16},{28,20},{1,9},{5... | collective-permute-start | bytes 983048 | tf_op jit(solution)/shard_map/ppermute | solution.py:576
  204.2 20.8 %all-to-all-start.1 = ((bf16[4,80,1024]{2,1,0:T(8,128)(2,1)}), bf16[4,80,1024]{2,1,0:T(8,128)(2,1)S(1)}, u32[]{:S(2)}, u32[]{:S(2)}) async-start(bf16[4,80,1024]{2,1,0:T(8,128)(2,1)} %pad_maximum_fusion.1), calls=%async_computation.1 | async-start | bytes 1310720 | tf_op jit(solution)/shard_map/all_to_all | solution.py:612
  (33 other events, 69.4 us)

commit v3 on v2

--- a/solution.py
+++ b/solution.py
@@ -63,12 +63,6 @@
     return side, valid
 
 
-def layer_norm(values):
-    centered = values - jnp.mean(values, axis=-1, keepdims=True)
-    inv_std = lax.rsqrt(jnp.mean(centered * centered, axis=-1, keepdims=True) + EPSILON)
-    return centered * inv_std, inv_std
-
-
 def whole(shape):
     return pl.BlockSpec(tuple(shape), lambda i, s: (0,) * len(shape))
 
@@ -87,7 +81,7 @@
 def fill_rows(scal_ref, refs, held):
     rows = refs[0].shape[1]
     for k, ref in enumerate(refs):
-        held[part_of(scal_ref, k, rows), :] = ref[0]
+        held[:, part_of(scal_ref, k, rows), :] = ref[...]
 
 
 def split_lanes(scal_ref, held, refs):
@@ -99,18 +93,20 @@
 def split_rows(scal_ref, held, refs):
     rows = refs[0].shape[1]
     for k, ref in enumerate(refs):
-        ref[0] = held[part_of(scal_ref, k, rows), :]
-
-
-def embed_chunk(scal, patches, embed_w, embed_b, gain, first, count, per_sample, cells, shards):
-    rows = count * per_sample
-    depth, width = embed_w.shape
+        ref[...] = held[:, part_of(scal_ref, k, rows), :]
+
+
+def embed(scal, patches, embed_w, embed_b, gain, firsts, count, per_sample, cells, shards):
+    rows, depth = patches.shape
+    width = embed_w.shape[1]
     share = width // shards
+    chunk_rows = count * per_sample
+    chunks = len(firsts)
     steps = 4
     tile = depth // steps
 
-    def body(scal_ref, x_ref, w_ref, b_ref, gain_ref, emb_ref, *refs):
-        outs, (acc, held) = refs[:shards], refs[shards:]
+    def body(scal_ref, x_ref, w_ref, b_ref, gain_ref, emb_ref, norm_ref, stat_ref, *refs):
+        outs, acc = refs[:-1], refs[-1]
         step = pl.program_id(0)
         part = dot(x_ref[...], w_ref[...])
 
@@ -124,37 +120,51 @@
 
         @pl.when(step == steps - 1)
         def _():
-            _, valid = token_sides(scal_ref, first, count, per_sample, cells)
-            embedded = ((acc[...] + b_ref[...]) * valid).astype(HALF)
-            emb_ref[...] = embedded
-            unit, _ = layer_norm(embedded.astype(FULL))
-            held[...] = (unit * gain_ref[...]).astype(HALF)
-            split_lanes(scal_ref, held, outs)
-
-    at = first // count
+            for c, first in enumerate(firsts):
+                at = slice(c * chunk_rows, (c + 1) * chunk_rows)
+                _, valid = token_sides(scal_ref, first, count, per_sample, cells)
+                embedded = ((acc[at] + b_ref[...]) * valid).astype(HALF)
+                emb_ref[at] = embedded
+                values = embedded.astype(FULL)
+                mean = jnp.mean(values, axis=-1, keepdims=True)
+                centered = values - mean
+                inv_std = lax.rsqrt(jnp.mean(centered * centered, axis=-1, keepdims=True) + EPSILON)
+                norm_ref[at] = (centered * inv_std * gain_ref[...]).astype(HALF)
+                stat_ref[at, :128] = jnp.broadcast_to(mean, (chunk_rows, 128))
+                stat_ref[at, 128:] = jnp.broadcast_to(inv_std, (chunk_rows, 128))
+                for k in range(shards):
+                    piece = norm_ref[at, part_of(scal_ref, k, share)]
+                    outs[c * shards + k][...] = piece.reshape(count, per_sample, share)
+
     piece = (count, per_sample, share)
-    emb, *pieces = pl.pallas_call(
+    emb, normed, stats, *pieces = pl.pallas_call(
         body,
         grid_spec=pltpu.PrefetchScalarGridSpec(
             num_scalar_prefetch=1,
             grid=(steps,),
             in_specs=[
-                pl.BlockSpec((rows, tile), lambda k, s: (at, k)),
+                pl.BlockSpec((rows, tile), lambda k, s: (0, k)),
                 pl.BlockSpec((tile, width), lambda k, s: (k, 0)),
                 whole((1, width)),
                 whole((1, width)),
             ],
-            out_specs=[whole((rows, width))] + [whole(piece)] * shards,
-            scratch_shapes=[pltpu.VMEM((rows, width), FULL), pltpu.VMEM((rows, width), HALF)],
-        ),
-        out_shape=[jax.ShapeDtypeStruct((rows, width), HALF)] + [jax.ShapeDtypeStruct(piece, HALF)] * shards,
+            out_specs=[whole((rows, width)), whole((rows, width)), whole((rows, 256))]
+            + [whole(piece)] * (shards * chunks),
+            scratch_shapes=[pltpu.VMEM((rows, width), FULL)],
+        ),
+        out_shape=[
+            jax.ShapeDtypeStruct((rows, width), HALF),
+            jax.ShapeDtypeStruct((rows, width), HALF),
+            jax.ShapeDtypeStruct((rows, 256), FULL),
+        ]
+        + [jax.ShapeDtypeStruct(piece, HALF)] * (shards * chunks),
         compiler_params=params(),
         cost_estimate=pl.CostEstimate(
             flops=2 * rows * depth * width, bytes_accessed=2 * depth * (rows + width), transcendentals=0
         ),
         name="embed",
     )(scal, patches, embed_w, embed_b, gain)
-    return emb, pieces
+    return emb, normed, stats, [pieces[c * shards : (c + 1) * shards] for c in range(chunks)]
 
 
 def to_blocks(values, blocks, width):
@@ -173,21 +183,23 @@
     return real, imag
 
 
-def table_factor(scal_ref, at, factors):
-    level = scal_ref[at]
+def table_factor(level, factors):
     return jnp.where(level == 0, factors[0], jnp.where(level == 1, factors[1], factors[2])).astype(FULL)
 
 
-def table_back(table_ref, pair, factor):
+def table_back(table_ref, level, tops, rests, factor):
     size = table_ref.shape[2]
     total = None
-    for at, values in enumerate(pair):
-        table = table_ref[0, at * size : (at + 1) * size]
-        top = values.astype(HALF)
-        rest = (values - top.astype(FULL)).astype(HALF)
+    for at, (top, rest) in enumerate(zip(tops, rests)):
+        table = table_ref[level, at * size : (at + 1) * size]
         part = dot(table, top) + dot(table, rest)
         total = part if total is None else total + part
     return total * factor
+
+
+def two_terms(values):
+    top = values.astype(HALF)
+    return top, (values - top.astype(FULL)).astype(HALF)
 
 
 def complex_weights(w_ref, held, blocks, width):
@@ -212,50 +224,52 @@
         ins, outs = refs[:shards], refs[shards : 2 * shards]
         spec_ref, hid_ref, fil_ref, weights, held = refs[2 * shards :]
 
-        @pl.when(pl.program_id(0) == 0)
-        def _():
-            complex_weights(w_ref, weights, blocks, width)
-
         def bias(layer, b):
             row = pl.ds(scal_ref[SHARD] * blocks + b, 1)
             return jnp.concatenate([b_ref[layer, 0, row], b_ref[layer, 1, row]], axis=1)
 
-        factor = table_factor(scal_ref, SIDES + SLOTS + first + pl.program_id(0), factors)
+        complex_weights(w_ref, weights, blocks, width)
         fill_rows(scal_ref, ins, held)
-        spectrum = (dot(t_ref[0], held[...]) * factor).astype(HALF)
+        levels = [scal_ref[SIDES + SLOTS + first + i] for i in range(count)]
+        for i, level in enumerate(levels):
+            spectrum = (dot(t_ref[level], held[i]) * table_factor(level, factors)).astype(HALF)
+            for b, entry in enumerate(to_blocks(spectrum, blocks, width)):
+                spec_ref[b, i * size : (i + 1) * size] = entry
         kept = []
-        for b, entry in enumerate(to_blocks(spectrum, blocks, width)):
-            spec_ref[0, b] = entry
-            pre_one = dot(entry, weights[0, b]) + bias(0, b)
+        for b in range(blocks):
+            pre_one = dot(spec_ref[b], weights[0, b]) + bias(0, b)
             hidden = jnp.maximum(pre_one, 0.0).astype(HALF)
-            hid_ref[0, b] = hidden
+            hid_ref[b] = hidden
             pre_two = dot(hidden, weights[1, b]) + bias(1, b)
             filtered = jnp.where(
                 pre_two > SHRINK, pre_two - SHRINK, jnp.where(pre_two < -SHRINK, pre_two + SHRINK, 0.0)
             )
-            fil_ref[0, b] = filtered.astype(HALF)
-            kept.append(filtered)
-        held[...] = table_back(t_ref, from_blocks(kept, width), factor).astype(HALF)
+            top, rest = two_terms(filtered)
+            fil_ref[b] = top
+            kept.append((top, rest))
+        for i, level in enumerate(levels):
+            at = slice(i * size, (i + 1) * size)
+            tops = from_blocks([top[at] for top, _ in kept], width)
+            rests = from_blocks([rest[at] for _, rest in kept], width)
+            held[i] = table_back(t_ref, level, tops, rests, table_factor(level, factors)).astype(HALF)
         split_rows(scal_ref, held, outs)
 
-    piece = pl.BlockSpec((1, per_sample, share), lambda i, s: (i, 0, 0))
-    saved = pl.BlockSpec((1, blocks, size, wide), lambda i, s: (i, 0, 0, 0))
-    saved_shape = jax.ShapeDtypeStruct((count, blocks, size, wide), HALF)
+    saved = (blocks, count * size, wide)
     outs = pl.pallas_call(
         body,
         grid_spec=pltpu.PrefetchScalarGridSpec(
             num_scalar_prefetch=1,
-            grid=(count,),
+            grid=(1,),
             in_specs=[
-                pl.BlockSpec((1, 2 * size, size), lambda i, s: (s[SIDES + SLOTS + first + i], 0, 0)),
+                whole(table.shape),
                 pl.BlockSpec((2, 2, blocks, width, width), lambda i, s: (0, 0, s[SHARD], 0, 0)),
                 whole(spec_b.shape),
             ]
-            + [piece] * shards,
-            out_specs=[piece] * shards + [saved] * 3,
-            scratch_shapes=[pltpu.VMEM((2, blocks, wide, wide), HALF), pltpu.VMEM((size, share), HALF)],
-        ),
-        out_shape=[jax.ShapeDtypeStruct(pieces[0].shape, HALF)] * shards + [saved_shape] * 3,
+            + [whole(pieces[0].shape)] * shards,
+            out_specs=[whole(pieces[0].shape)] * shards + [whole(saved)] * 3,
+            scratch_shapes=[pltpu.VMEM((2, blocks, wide, wide), HALF), pltpu.VMEM((count, size, share), HALF)],
+        ),
+        out_shape=[jax.ShapeDtypeStruct(pieces[0].shape, HALF)] * shards + [jax.ShapeDtypeStruct(saved, HALF)] * 3,
         compiler_params=params(),
         cost_estimate=pl.CostEstimate(
             flops=count * size * share * size * 14, bytes_accessed=count * size * share * 16, transcendentals=0
@@ -265,7 +279,7 @@
     return outs[:shards], outs[shards:]
 
 
-def head_chunk(scal, embedded, gain, mixed, targets, head_w, head_b, first, samples, cells):
+def head_chunk(scal, embedded, normed, mixed, targets, head_w, head_b, first, samples, cells):
     shards = len(mixed)
     count, per_sample, share = mixed[0].shape
     rows = count * per_sample
@@ -273,14 +287,11 @@
     at = first // count
     scale_root = float(np.sqrt(np.float32(samples)))
 
-    def body(scal_ref, emb_ref, gain_ref, tgt_ref, w_ref, b_ref, *refs):
+    def body(scal_ref, emb_ref, norm_ref, tgt_ref, w_ref, b_ref, *refs):
         mix_refs, (pred_ref, res_ref, grad_ref, bias_ref, held) = refs[:shards], refs[shards:]
         fill_lanes(scal_ref, mix_refs, held)
         side, valid = token_sides(scal_ref, first, count, per_sample, cells)
-        embedded = emb_ref[...].astype(FULL)
-        unit, _ = layer_norm(embedded)
-        normed = (unit * gain_ref[...]).astype(HALF)
-        updated = (embedded + normed.astype(FULL) + held[...].astype(FULL)).astype(HALF)
+        updated = (emb_ref[...].astype(FULL) + norm_ref[...].astype(FULL) + held[...].astype(FULL)).astype(HALF)
         output = (dot(updated, w_ref[...]) + b_ref[...]) * valid
         pred_ref[...] = output.astype(HALF).reshape(pred_ref.shape)
         scale = 2.0 / (side.astype(FULL) * scale_root)
@@ -297,8 +308,8 @@
             num_scalar_prefetch=1,
             grid=(1,),
             in_specs=[
-                whole((rows, width)),
-                whole((1, width)),
+                pl.BlockSpec((rows, width), lambda i, s: (at, 0)),
+                pl.BlockSpec((rows, width), lambda i, s: (at, 0)),
                 pl.BlockSpec((rows, outs), lambda i, s: (at, 0)),
                 whole((width, outs)),
                 whole((1, outs)),
@@ -318,7 +329,7 @@
             flops=4 * rows * width * outs, bytes_accessed=rows * width * 4 + width * outs * 6, transcendentals=0
         ),
         name="head",
-    )(scal, embedded, gain, targets, head_w, head_b, *mixed)
+    )(scal, embedded, normed, targets, head_w, head_b, *mixed)
 
 
 def spectral_back_chunk(scal, table, factors, residual, head_w, spec_w, saved, first, before, last):
@@ -337,51 +348,49 @@
         ins, refs = refs[:shards], refs[shards:]
         if has_before:
             (old_ref, old_bias_ref), refs = refs[:2], refs[2:]
-        pieces, (grad_ref, bias_ref, weights, held, gathered, total) = refs[:shards], refs[shards:]
-
-        @pl.when(pl.program_id(0) == 0)
-        def _():
-            complex_weights(w_ref, weights, blocks, width)
+        pieces, (grad_ref, bias_ref, weights, held, gathered) = refs[:shards], refs[shards:]
+
+        def weight_sums(layer, b, inputs, grads):
+            raw = dot_tn(inputs, grads)
+            sums = jnp.sum(grads.astype(FULL), axis=0, keepdims=True)
+            at = layer * blocks + b
             if has_before:
-                total[...] = old_ref[...]
-                bias_ref[...] = old_bias_ref[...]
-            else:
-                total[...] = jnp.zeros_like(total)
-                bias_ref[...] = jnp.zeros_like(bias_ref)
-
-        factor = table_factor(scal_ref, SIDES + SLOTS + first + pl.program_id(0), factors)
+                raw = raw + old_ref[layer, b]
+                sums = sums + old_bias_ref[at : at + 1]
+            bias_ref[at : at + 1] = sums
+            if not last:
+                grad_ref[layer, b] = raw
+                return
+            real = raw[:width, :width] + raw[width:, width:]
+            imag = raw[:width, width:] - raw[width:, :width]
+            grad_ref[at * width : (at + 1) * width] = jnp.concatenate([real, imag], axis=1).astype(HALF)
+
+        complex_weights(w_ref, weights, blocks, width)
         fill_rows(scal_ref, ins, gathered)
-        updated_grad = dot_nt(gathered[...], h_ref[...]).astype(HALF)
-        filtered_grad = dot(t_ref[0], updated_grad) * factor
+        levels = [scal_ref[SIDES + SLOTS + first + i] for i in range(count)]
+        updated_grad = dot_nt(gathered[...].reshape(count * size, outs), h_ref[...]).astype(HALF)
+        entries = []
+        for i, level in enumerate(levels):
+            filtered_grad = dot(t_ref[level], updated_grad[i * size : (i + 1) * size]) * table_factor(level, factors)
+            entries.append(to_blocks(filtered_grad, blocks, width))
         kept = []
-        for b, entry in enumerate(to_blocks(filtered_grad, blocks, width)):
-            two_grad = jnp.where(fil_ref[0, b].astype(FULL) != 0.0, entry, 0.0).astype(HALF)
-            hidden = hid_ref[0, b]
-            total[1, b] += dot_tn(hidden, two_grad)
-            bias_ref[blocks + b : blocks + b + 1] += jnp.sum(two_grad.astype(FULL), axis=0, keepdims=True)
+        for b in range(blocks):
+            entry = jnp.concatenate([e[b] for e in entries], axis=0)
+            two_grad = jnp.where(fil_ref[b].astype(FULL) != 0.0, entry, 0.0).astype(HALF)
+            hidden = hid_ref[b]
             hidden_grad = dot_nt(two_grad, weights[1, b])
             one_grad = jnp.where(hidden.astype(FULL) > 0.0, hidden_grad, 0.0).astype(HALF)
-            total[0, b] += dot_tn(spec_ref[0, b], one_grad)
-            bias_ref[b : b + 1] += jnp.sum(one_grad.astype(FULL), axis=0, keepdims=True)
-            kept.append(dot_nt(one_grad, weights[0, b]))
-        held[...] = table_back(t_ref, from_blocks(kept, width), factor).astype(HALF)
+            kept.append(two_terms(dot_nt(one_grad, weights[0, b])))
+            weight_sums(1, b, hidden, two_grad)
+            weight_sums(0, b, spec_ref[b], one_grad)
+        for i, level in enumerate(levels):
+            at = slice(i * size, (i + 1) * size)
+            tops = from_blocks([top[at] for top, _ in kept], width)
+            rests = from_blocks([rest[at] for _, rest in kept], width)
+            held[i] = table_back(t_ref, level, tops, rests, table_factor(level, factors)).astype(HALF)
         split_rows(scal_ref, held, pieces)
 
-        @pl.when(pl.program_id(0) == count - 1)
-        def _():
-            if not last:
-                grad_ref[...] = total[...]
-                return
-            for layer in range(2):
-                for b in range(blocks):
-                    raw = total[layer, b]
-                    real = raw[:width, :width] + raw[width:, width:]
-                    imag = raw[:width, width:] - raw[width:, :width]
-                    row = (layer * blocks + b) * width
-                    grad_ref[row : row + width] = jnp.concatenate([real, imag], axis=1).astype(HALF)
-
-    saved_spec = pl.BlockSpec((1, blocks, size, wide), lambda i, s: (i, 0, 0, 0))
-    piece = pl.BlockSpec((1, per_sample, share), lambda i, s: (i, 0, 0))
+    piece = (count, per_sample, share)
     if last:
         grad_out = jax.ShapeDtypeStruct((2 * blocks * width, wide), HALF)
     else:
@@ -390,26 +399,23 @@
         body,
         grid_spec=pltpu.PrefetchScalarGridSpec(
             num_scalar_prefetch=1,
-            grid=(count,),
+            grid=(1,),
             in_specs=[
-                pl.BlockSpec((1, 2 * size, size), lambda i, s: (s[SIDES + SLOTS + first + i], 0, 0)),
+                whole(table.shape),
                 pl.BlockSpec((share, outs), lambda i, s: (s[SHARD], 0)),
                 pl.BlockSpec((2, 2, blocks, width, width), lambda i, s: (0, 0, s[SHARD], 0, 0)),
-                saved_spec,
-                saved_spec,
-                saved_spec,
             ]
-            + [pl.BlockSpec((1, per_sample, outs), lambda i, s: (i, 0, 0))] * shards
+            + [whole(saved[0].shape)] * 3
+            + [whole(residual[0].shape)] * shards
             + ([whole(raw_shape), whole(bias_shape)] if has_before else []),
-            out_specs=[piece] * shards + [whole(grad_out.shape), whole(bias_shape)],
+            out_specs=[whole(piece)] * shards + [whole(grad_out.shape), whole(bias_shape)],
             scratch_shapes=[
                 pltpu.VMEM((2, blocks, wide, wide), HALF),
-                pltpu.VMEM((size, share), HALF),
-                pltpu.VMEM((size, outs), HALF),
-                pltpu.VMEM(raw_shape, FULL),
+                pltpu.VMEM((count, size, share), HALF),
+                pltpu.VMEM((count, size, outs), HALF),
             ],
         ),
-        out_shape=[jax.ShapeDtypeStruct((count, per_sample, share), HALF)] * shards
+        out_shape=[jax.ShapeDtypeStruct(piece, HALF)] * shards
         + [grad_out, jax.ShapeDtypeStruct(bias_shape, FULL)],
         compiler_params=params(),
         cost_estimate=pl.CostEstimate(
@@ -420,17 +426,19 @@
     return result[:shards], result[shards:]
 
 
-def embedded_back_chunk(scal, embedded, residual, head_w, gain, spec_grad, first, cells):
+def embedded_back_chunk(scal, embedded, stats, residual, head_w, gain, spec_grad, first, cells):
     shards = len(spec_grad)
     count, per_sample, share = spec_grad[0].shape
     rows = count * per_sample
     width, outs = head_w.shape
-
-    def body(scal_ref, emb_ref, res_ref, w_ref, gain_ref, *refs):
+    at = first // count
+
+    def body(scal_ref, emb_ref, stat_ref, res_ref, w_ref, gain_ref, *refs):
         grad_refs, (out_ref, sums_ref, held) = refs[:shards], refs[shards:]
         fill_lanes(scal_ref, grad_refs, held)
         _, valid = token_sides(scal_ref, first, count, per_sample, cells)
-        unit, inv_std = layer_norm(emb_ref[...].astype(FULL))
+        inv_std = stat_ref[:, 128:129]
+        unit = (emb_ref[...].astype(FULL) - stat_ref[:, 0:1]) * inv_std
         direct = dot_nt(res_ref[...].reshape(rows, outs), w_ref[...]).astype(HALF).astype(FULL)
         normed_grad = held[...].astype(FULL) + direct
         gain_grad = jnp.sum(normed_grad * unit, axis=0, keepdims=True)
@@ -450,7 +458,8 @@
             num_scalar_prefetch=1,
             grid=(1,),
             in_specs=[
-                whole((rows, width)),
+                pl.BlockSpec((rows, width), lambda i, s: (at, 0)),
+                pl.BlockSpec((rows, 256), lambda i, s: (at, 0)),
                 whole((count, per_sample, outs)),
                 whole((width, outs)),
                 whole((1, width)),
@@ -465,7 +474,7 @@
             flops=2 * rows * width * outs, bytes_accessed=rows * width * 6, transcendentals=0
         ),
         name="embedded_back",
-    )(scal, embedded, residual, head_w, gain, *spec_grad)
+    )(scal, embedded, stats, residual, head_w, gain, *spec_grad)
 
 
 def turned_patches(scal, patches, groups):
@@ -587,9 +596,8 @@
     return (left.astype(FULL) + right.astype(FULL)).astype(HALF)
 
 
-def scatter_sum(parts, groups, shard_at):
+def scatter_start(parts, groups):
     bits = groups.bit_length() - 1
-    shards = lax.axis_size("fft")
     ends = []
     for send, keep, order, low in (
         (parts[0], parts[1], list(range(1, bits)), True),
@@ -606,9 +614,11 @@
                 keep, send = split[0], split[1]
             total = add_half(keep, swap_bit(send, bit, groups))
         ends.append(total[0])
-    block = ends[0].shape[0]
-    share = block // shards
-    part = jnp.concatenate(ends, axis=-1).reshape(shards, share, -1)
+    return jnp.concatenate(ends, axis=-1)
+
+
+def scatter_end(part, shards):
+    part = part.reshape(shards, part.shape[0] // shards, -1)
     moved = lax.all_to_all(part, "fft", split_axis=0, concat_axis=0, tiled=True)
     return jnp.sum(moved.astype(FULL), axis=0)
 
@@ -619,41 +629,60 @@
     )
 
 
-def small_grads(head_grad, head_bias, spec_grad, spec_bias, groups, shards, shard_at):
+def hi_lo(values):
+    high = lax.optimization_barrier(values.astype(HALF))
+    return jnp.concatenate([high, (values - high.astype(FULL)).astype(HALF)], axis=-2)
+
+
+def from_hi_lo(values):
+    half = values.shape[-2] // 2
+    values = values.astype(FULL)
+    return values[..., :half, :] + values[..., half:, :]
+
+
+def sum_over_groups(head_grad, spec_grad, groups):
     outs = head_grad.shape[1]
-    head_rows = head_grad.shape[0] // groups
-    spec_rows = spec_grad.shape[0] // groups
-    small = jnp.concatenate([spec_bias, head_bias[None], jnp.zeros((7 - spec_bias.shape[0], outs), FULL)], axis=0)
-    high = lax.optimization_barrier(small.astype(HALF))
-    small = jnp.concatenate([high, (small - high.astype(FULL)).astype(HALF)], axis=0)
     packed = jnp.concatenate(
-        [
-            head_grad.astype(HALF).reshape(groups, head_rows, outs),
-            spec_grad.reshape(groups, spec_rows, outs),
-            jnp.broadcast_to(small[None], (groups,) + small.shape),
-        ],
-        axis=1,
+        [head_grad.astype(HALF).reshape(groups, -1, outs), spec_grad.reshape(groups, -1, outs)], axis=1
     )
-    moved = lax.all_to_all(packed, "grp", split_axis=0, concat_axis=0, tiled=True)
-    summed = jnp.sum(moved.astype(FULL), axis=0)
-    small = summed[head_rows + spec_rows :]
-    small = small[:8] + small[8:]
-    high = lax.optimization_barrier(small.astype(HALF))
-    small = jnp.concatenate([high, (small - high.astype(FULL)).astype(HALF)], axis=0)
-    summed = jnp.concatenate([summed[: head_rows + spec_rows].astype(HALF), small], axis=0)
-    rows = across([summed] * shards)
+    return lax.all_to_all(packed, "grp", split_axis=0, concat_axis=0, tiled=True)
+
+
+def over_shards(moved, small, head_rows, shards, shard_at):
+    summed = jnp.sum(moved.astype(FULL), axis=0).astype(HALF)
+    rows = across([jnp.concatenate([summed, hi_lo(small)], axis=0)] * shards)
     head_part = sum(r[:head_rows].astype(FULL) for r in rows).astype(HALF)
     order = jnp.bitwise_xor(jnp.arange(shards, dtype=jnp.int32), shard_at)
     rest = jnp.take(jnp.stack([r[head_rows:] for r in rows]), order, axis=0)
-    small = rest[:, spec_rows:].astype(FULL)
-    small = small[:, :8] + small[:, 8:]
-    spec_bias_all = small[:, : spec_bias.shape[0]]
-    head_bias_all = jnp.sum(small[:, spec_bias.shape[0]], axis=0)
-    spec_part = rest[:, :spec_rows].reshape(shards * spec_rows, outs)
-    gathered = to_all(jnp.concatenate([head_part, spec_part], axis=0), "grp", groups)
-    head_all = gathered[:, :head_rows].reshape(groups * head_rows, outs).astype(FULL)
-    spec_all = gathered[:, head_rows:].reshape(groups, shards, spec_rows, outs)
-    return head_all, head_bias_all, jnp.swapaxes(spec_all, 0, 1), spec_bias_all
+    spec_rows = summed.shape[0] - head_rows
+    return head_part, rest[:, :spec_rows], from_hi_lo(rest[:, spec_rows:])
+
+
+def assembled(gathered, head_rows, shards, blocks, width):
+    groups = gathered.shape[0]
+    total_blocks = shards * blocks
+    spec_rows = 2 * blocks * width // groups
+
+    def body(x_ref, head_ref, spec_ref):
+        for g in range(groups):
+            head_ref[g * head_rows : (g + 1) * head_rows] = x_ref[g, :head_rows].astype(FULL)
+            start = g * spec_rows
+            layer, b = start // (blocks * width), (start // width) % blocks
+            rows = slice(start % width, start % width + spec_rows)
+            for z in range(shards):
+                values = x_ref[g, head_rows + z * spec_rows : head_rows + (z + 1) * spec_rows].astype(FULL)
+                spec_ref[layer, 0, z * blocks + b, rows] = values[:, :width]
+                spec_ref[layer, 1, z * blocks + b, rows] = values[:, width:]
+
+    return pl.pallas_call(
+        body,
+        out_shape=[
+            jax.ShapeDtypeStruct((groups * head_rows, 2 * width), FULL),
+            jax.ShapeDtypeStruct((2, 2, total_blocks, width, width), FULL),
+        ],
+        compiler_params=params(),
+        name="assembled",
+    )(gathered)
 
 
 def route_predictions(predicted, dest_group, group_at, groups, slot_count):
@@ -694,24 +723,21 @@
     flat_targets = targets.reshape(-1, outs)
     gain_row, embed_b_row, head_b_row = gain[None], embed_b[None], head_b[None]
 
-    embedded, moved = [], []
-    for first in firsts:
-        emb, pieces = embed_chunk(
-            scal, flat_patches, embed_w, embed_b_row, gain_row, first, count, per_sample, cells, shards
-        )
-        embedded.append(emb)
-        moved.append(across(pieces))
+    embedded, normed, stats, pieces = embed(
+        scal, flat_patches, embed_w, embed_b_row, gain_row, firsts, count, per_sample, cells, shards
+    )
+    moved = [across(p) for p in pieces]
     turned_send, turned_keep = turned_patches(scal, flat_patches, groups)
     turned = [turned_keep, swap_bit(turned_send, 0, groups)]
     mixed, saved = [], []
-    for first, pieces in zip(firsts, moved):
-        out, rest = spectral_chunk(scal, table, factors, pieces, spec_w, spec_b, first)
+    for first, values in zip(firsts, moved):
+        out, rest = spectral_chunk(scal, table, factors, values, spec_w, spec_b, first)
         mixed.append(across(out))
         saved.append(rest)
     predicted, residual, head_grads, head_sums, gathered = [], [], [], [], []
-    for first, emb, mix in zip(firsts, embedded, mixed):
+    for first, mix in zip(firsts, mixed):
         pred, res, grad, sums = head_chunk(
-            scal, emb, gain_row, mix, flat_targets, head_w, head_b_row, first, samples, cells
+            scal, embedded, normed, mix, flat_targets, head_w, head_b_row, first, samples, cells
         )
         predicted.append(pred)
         residual.append(res)
@@ -720,35 +746,46 @@
         gathered.append(across([res] * shards))
     spec_back, sums = [], None
     for first, res, rest in zip(firsts, gathered, saved):
-        pieces, sums = spectral_back_chunk(
+        values, sums = spectral_back_chunk(
             scal, table, factors, res, head_w, spec_w, rest, first, sums, first == firsts[-1]
         )
-        spec_back.append(across(pieces))
+        spec_back.append(across(values))
+    spec_grad, spec_bias = sums
+    width = spec_w.shape[-1]
+    blocks = spec_w.shape[2] // shards
+    head_rows = head_w.shape[0] // groups
+    weight_sums = sum_over_groups(sum(head_grads), spec_grad, groups)
     own_grads, other_grads, row_sums = [], [], []
-    for first, emb, res, back in zip(firsts, embedded, residual, spec_back):
-        grad, row_sum = embedded_back_chunk(scal, emb, res, head_w, gain_row, back, first, cells)
+    for first, res, back in zip(firsts, residual, spec_back):
+        grad, row_sum = embedded_back_chunk(scal, embedded, stats, res, head_w, gain_row, back, first, cells)
         own_grads.append(grad)
         other_grads.append(swap_bit(grad, 0, groups))
         row_sums.append(row_sum)
     parts = embed_grad_parts(scal, turned, own_grads + other_grads, groups)
-    embed_grad = scatter_sum(parts, groups, shard_at)
-
+    parts, weight_sums, predicted, row_sums = lax.optimization_barrier((parts, weight_sums, predicted, row_sums))
+    part = scatter_start(parts, groups)
     predictions = route_predictions(
         jnp.concatenate(predicted, axis=0), dest_group, group_at, groups, slot_count
     ).reshape(targets.shape)
-    spec_grad, spec_bias = sums
-    head_grad, head_bias_grad, spec_all, spec_bias_all = small_grads(
-        sum(head_grads), sum(head_sums), spec_grad, spec_bias, groups, shards, shard_at
-    )
-    width = spec_w.shape[-1]
-    blocks = spec_w.shape[2] // shards
-    spec_all = spec_all.reshape(shards, 2, blocks, width, 2, width)
-    spec_w_grad = jnp.transpose(spec_all, (1, 4, 0, 2, 3, 5)).reshape(spec_w.shape).astype(FULL)
-    spec_bias_all = spec_bias_all.reshape(shards, 2, blocks, 2, width)
+    rows = sum(row_sums)
+    vectors = jnp.concatenate([rows[0].reshape(-1, outs), rows[4].reshape(-1, outs), sum(head_sums)[None]], axis=0)
+    own_rows, all_rows = spec_bias.shape[0], vectors.shape[0]
+    small = jnp.concatenate([spec_bias, vectors, jnp.zeros((16 - own_rows - all_rows, outs), FULL)], axis=0)
+    head_part, spec_part, small = over_shards(weight_sums, small, head_rows, shards, shard_at)
+    small = jnp.concatenate([small[:, :own_rows].reshape(-1, outs), jnp.sum(small[:, own_rows:], axis=0)], axis=0)
+    small = jnp.concatenate([small, jnp.zeros((-small.shape[0] % 16, outs), FULL)], axis=0)
+    outgoing = jnp.concatenate([head_part, spec_part.reshape(-1, outs), hi_lo(small)], axis=0)
+    part, outgoing = lax.optimization_barrier((part, outgoing))
+    embed_grad = scatter_end(part, shards)
+    gathered = to_all(outgoing, "grp", groups)
+    head_grad, spec_w_grad = assembled(gathered, head_rows, shards, blocks, width)
+    small = jnp.sum(from_hi_lo(gathered[:, head_rows + shards * (2 * blocks * width // groups) :]), axis=0)
+    spec_bias_all = small[: shards * own_rows].reshape(shards, 2, blocks, 2, width)
     spec_b_grad = jnp.transpose(spec_bias_all, (1, 3, 0, 2, 4)).reshape(spec_b.shape)
-    rows = sum(row_sums)
-    rows = jnp.sum(to_all(rows.reshape(2, 4, -1)[:, 0], ("grp", "fft"), groups * shards), axis=0)
-    gain_grad, embed_bias_grad = rows[0], rows[1]
+    vectors = small[shards * own_rows : shards * own_rows + all_rows]
+    quarter = (all_rows - 1) // 2
+    gain_grad, embed_bias_grad = vectors[:quarter].reshape(-1), vectors[quarter : 2 * quarter].reshape(-1)
+    head_bias_grad = vectors[2 * quarter]
     return (
         predictions,
         embed_grad,

time: 227 us -> 227 us (level)
  blocking collectives: 0 us -> 19.1 us
  Pallas kernels: 71 us -> 65.3 us
  local copies, waits for them, and re-layouts: 17.6 us -> 12.7 us
  other arithmetic: 12.3 us -> 8.83 us
    all_to_all x0 -> x1, blocking collectives: none -> 19.1 us  [scatter_end(): moved = lax.all_to_all(part, 'fft', split_axis=0, concat_axis=0, tiled=True)]
    all_to_all x2 -> x1, waiting for transfers between devices: 9.04 us -> 21.1 us  [to_all(): lax.all_to_all(jnp.broadcast_to(values[None], (count,) + values.shape), a...]
    all_to_all x2 -> x1, waiting for transfers between devices: 9.2 us -> 0.01 us  [sum_over_groups(): lax.all_to_all(packed, 'grp', split_axis=0, concat_axis=0, tiled=True)]
    ppermute x27, starting transfers between devices: 41.4 us -> 48.9 us  [across(): lax.ppermute(pieces[k], 'fft', [(z, z ^ k) for z in range(shards)])]
    ppermute x7, waiting for transfers between devices: 21.8 us -> 16 us  [swap_bit(): lax.ppermute(values, 'grp', [(g, g ^ 1 << bit) for g in range(groups)])]
    convert_element_type x3 -> x0, local copies, waits for them, and re-layouts: 5.45 us -> none  [on_device(): jnp.transpose(spec_all, (1, 4, 0, 2, 3, 5)).reshape(spec_w.shape)]
    all_to_all x2 -> x1, starting transfers between devices: 7.72 us -> 3.59 us  [to_all(): lax.all_to_all(jnp.broadcast_to(values[None], (count,) + values.shape), a...]
    all_to_all x2 -> x1, starting transfers between devices: 7.03 us -> 3.77 us  [sum_over_groups(): lax.all_to_all(packed, 'grp', split_axis=0, concat_axis=0, tiled=True)]
  transfers between devices with their start and end apart: 39 -> 37, of which waited for: 9 -> 13; matrix products, arithmetic and copies ran while one was open for 10% -> 4% of each run, Pallas kernels for 29% -> 23%
where the time goes in v3:
time: 227 us; the launch traced here: 226 us
  Pallas kernels  65.3 us (29%)
  starting transfers between devices  65.2 us (29%)
  waiting for transfers between devices  54 us (24%)
  blocking collectives  19.1 us (8%)
  local copies, waits for them, and re-layouts  12.7 us (6%)
  other arithmetic  8.83 us (4%)
    ppermute x27, starting transfers between devices, across(): lax.ppermute(pieces[k], 'fft', [(z, z ^ k) for z in range(shards)])  48.9 us
    all_to_all x1, waiting for transfers between devices, to_all(): lax.all_to_all(jnp.broadcast_to(values[None], (count,) + values.shape), a...  21.1 us
    all_to_all x1, blocking collectives, scatter_end(): moved = lax.all_to_all(part, 'fft', split_axis=0, concat_axis=0, tiled=True)  19.1 us
    ppermute x27, waiting for transfers between devices, across(): lax.ppermute(pieces[k], 'fft', [(z, z ^ k) for z in range(shards)])  16.9 us
    ppermute x7, waiting for transfers between devices, swap_bit(): lax.ppermute(values, 'grp', [(g, g ^ 1 << bit) for g in range(groups)])  16 us
    pallas_call x2, Pallas kernels, spectral_back_chunk(): pl.pallas_call(body, grid_spec=pltpu.PrefetchScalarGridSpec(num_scalar_pr...  12.3 us
    pallas_call x2, Pallas kernels, spectral_chunk(): pl.pallas_call(body, grid_spec=pltpu.PrefetchScalarGridSpec(num_scalar_pr...  9.83 us
    pallas_call x1, Pallas kernels, embed(): pl.pallas_call(body, grid_spec=pltpu.PrefetchScalarGridSpec(num_scalar_pr...  8.97 us
  transfers between devices with their start and end apart: 37, of which 13 were waited for; matrix products, arithmetic and copies ran while one was open for 4% of the time, Pallas kernels for 23%

profile of v3, /device:TPU:0, one launch (start us, length us, event | category | flops | bytes accessed | tf_op | source)
XLA Modules:
  0.0 226.3 jit_solution(9664165923620621195)
XLA Ops:
  2.0 9.0 %embed.1 = (bf16[384,1024]{1,0:T(8,128)(2,1)}, bf16[384,1024]{1,0:T(8,128)(2,1)}, f32[384,256]{1,0:T(8,128)}, bf16[3,64,256]{2,1,0:T(8,128)(2,1)}, bf16[3,64,256...) custom-call(s32[15]{0:T(128)} %concatenate.24.scal_ref, ...), custom_call_target="tpu_custom_call" | custom-call | flops 2013265920 | bytes 7208960 | tf_op jit(solution)/shard_map/embed/pallas_call | solution.py:140
  11.0 3.1 %collective-permute-start.13 = (bf16[3,64,256]{2,1,0:T(8,128)(2,1)}, bf16[3,64,256]{2,1,0:T(8,128)(2,1)S(1)}, u32[]{:S(2)}, u32[]{:S(2)}) collective-permute-start(bf16[3,64,256]{2,1,0:T(8,128)(2,1)} %get-tuple-element.99), channel_id=1, source_target_pairs={{0,1},{1,0},{2,3},{3,2},{4,5},{5,4},{6,7},{7,6},{8,9},{9,8},{10,11... | collective-permute-start | bytes 294920 | tf_op jit(solution)/shard_map/ppermute | solution.py:591
  14.0 2.6 %collective-permute-start.14 = (bf16[3,64,256]{2,1,0:T(8,128)(2,1)}, bf16[3,64,256]{2,1,0:T(8,128)(2,1)S(1)}, u32[]{:S(2)}, u32[]{:S(2)}) collective-permute-start(bf16[3,64,256]{2,1,0:T(8,128)(2,1)} %get-tuple-element.100), channel_id=1, source_target_pairs={{0,2},{1,3},{2,0},{3,1},{4,6},{5,7},{6,4},{7,5},{8,10},{9,11},{10,... | collective-permute-start | bytes 294920 | tf_op jit(solution)/shard_map/ppermute | solution.py:591
  17.1 3.9 %collective-permute-start.3 = (bf16[3,64,256]{2,1,0:T(8,128)(2,1)}, bf16[3,64,256]{2,1,0:T(8,128)(2,1)S(1)}, u32[]{:S(2)}, u32[]{:S(2)}) collective-permute-start(bf16[3,64,256]{2,1,0:T(8,128)(2,1)} %get-tuple-element.84), channel_id=1, source_target_pairs={{0,3},{1,2},{2,1},{3,0},{4,7},{5,6},{6,5},{7,4},{8,11},{9,10},{10,... | collective-permute-start | bytes 294920 | tf_op jit(solution)/shard_map/ppermute | solution.py:591
  21.2 1.7 collective-permute-done.1.refs_1_
  22.9 2.7 %collective-permute-start.15 = (bf16[3,64,256]{2,1,0:T(8,128)(2,1)}, bf16[3,64,256]{2,1,0:T(8,128)(2,1)S(1)}, u32[]{:S(2)}, u32[]{:S(2)}) collective-permute-start(bf16[3,64,256]{2,1,0:T(8,128)(2,1)} %get-tuple-element.101), channel_id=1, source_target_pairs={{0,3},{1,2},{2,1},{3,0},{4,7},{5,6},{6,5},{7,4},{8,11},{9,10},{10,... | collective-permute-start | bytes 294920 | tf_op jit(solution)/shard_map/ppermute | solution.py:591
  25.6 5.0 %collective-permute-done.2.refs_2_ = bf16[3,64,256]{2,1,0:T(8,128)(2,1)S(1)} collective-permute-done((bf16[3,64,256]{2,1,0:T(8,128)(2,1)}, bf16[3,64,256]{2,1,0:T(8,128)(2,1)S(1)}, u32[]{:S(2)}, u32[]{:S(2)}) %collective-permute-start.2) | collective-permute-done | bytes 98336 | tf_op jit(solution)/shard_map/ppermute | solution.py:591
  31.3 4.9 %spectral.2 = (bf16[3,64,256]{2,1,0:T(8,128)(2,1)}, bf16[3,64,256]{2,1,0:T(8,128)(2,1)}, bf16[3,64,256]{2,1,0:T(8,128)(2,1)}, bf16[3,64,256]{2,1,0:T(8,128)(2,1)...) custom-call(s32[15]{0:T(128)} %concatenate.24.scal_ref, ...), custom_call_target="tpu_custom_call" | custom-call | flops 704643072 | bytes 3145728 | tf_op jit(solution)/shard_map/spectral/pallas_call | solution.py:258
  36.2 2.6 %collective-permute-start.4 = (bf16[3,64,256]{2,1,0:T(8,128)(2,1)}, bf16[3,64,256]{2,1,0:T(8,128)(2,1)S(1)}, u32[]{:S(2)}, u32[]{:S(2)}) collective-permute-start(bf16[3,64,256]{2,1,0:T(8,128)(2,1)} %get-tuple-element.86), channel_id=1, source_target_pairs={{0,1},{1,0},{2,3},{3,2},{4,5},{5,4},{6,7},{7,6},{8,9},{9,8},{10,11... | collective-permute-start | bytes 294920 | tf_op jit(solution)/shard_map/ppermute | solution.py:591
  38.8 1.5 collective-permute-start.5
  40.4 1.5 collective-permute-start.6
  41.8 8.0 %turned_patches.1 = (bf16[4,320,384]{2,1,0:T(8,128)(2,1)}, bf16[4,320,384]{2,1,0:T(8,128)(2,1)}) custom-call(s32[15]{0:T(128)} %concatenate.24.scal_ref, bf16[384,2560]{1,0:T(8,128)(2,1)} %bitcast.56), custom_call_target="tpu_custom_call" | custom-call | bytes 3932160 | tf_op jit(solution)/shard_map/turned_patches/pallas_call | solution.py:505
  50.5 4.9 %spectral.3 = (bf16[3,64,256]{2,1,0:T(8,128)(2,1)}, bf16[3,64,256]{2,1,0:T(8,128)(2,1)}, bf16[3,64,256]{2,1,0:T(8,128)(2,1)}, bf16[3,64,256]{2,1,0:T(8,128)(2,1)...) custom-call(s32[15]{0:T(128)} %concatenate.24.scal_ref, ...), custom_call_target="tpu_custom_call" | custom-call | flops 704643072 | bytes 3145728 | tf_op jit(solution)/shard_map/spectral/pallas_call | solution.py:258
  56.0 2.4 %collective-permute-start.17 = (bf16[3,64,256]{2,1,0:T(8,128)(2,1)}, bf16[3,64,256]{2,1,0:T(8,128)(2,1)S(1)}, u32[]{:S(2)}, u32[]{:S(2)}) collective-permute-start(bf16[3,64,256]{2,1,0:T(8,128)(2,1)} %get-tuple-element.104), channel_id=1, source_target_pairs={{0,2},{1,3},{2,0},{3,1},{4,6},{5,7},{6,4},{7,5},{8,10},{9,11},{10,... | collective-permute-start | bytes 294920 | tf_op jit(solution)/shard_map/ppermute | solution.py:591
  58.4 1.5 collective-permute-start.18
  60.5 4.0 %head.2 = (bf16[3,64,256]{2,1,0:T(8,128)(2,1)}, bf16[3,64,256]{2,1,0:T(8,128)(2,1)}, f32[1024,256]{1,0:T(8,128)}, f32[8,256]{1,0:T(8,128)}) custom-call(s32[15]{0:T(128)} %concatenate.24.scal_ref, bf16[384,1024]{1,0:T(8,128)(2,1)} %get-tuple-element.78.emb_ref, bf16[384,1024]{1,0:T(8,128)(2,1)} %get-tuple-element.80.norm_ref, bf16[384,256]{1,0:T(8,128)(2,1)} %bitcast.59, ...), custom_call_target="tpu_custom_call" | custom-call | flops 201326592 | bytes 2359296 | tf_op jit(solution)/shard_map/head/pallas_call | solution.py:305
  64.5 2.9 %collective-permute-start.8 = (bf16[3,64,256]{2,1,0:T(8,128)(2,1)}, bf16[3,64,256]{2,1,0:T(8,128)(2,1)S(1)}, u32[]{:S(2)}, u32[]{:S(2)}) collective-permute-start(bf16[3,64,256]{2,1,0:T(8,128)(2,1)} %get-tuple-element.89.refs_0_.res_ref), channel_id=1, source_target_pairs={{0,2},{1,3},{2,0},{3,1},{4,6},{5,7},{6,4},{7,5},{8,10},{9,11},{10,... | collective-permute-start | bytes 294920 | tf_op jit(solution)/shard_map/ppermute | solution.py:591
  68.2 4.0 %head.3 = (bf16[3,64,256]{2,1,0:T(8,128)(2,1)}, bf16[3,64,256]{2,1,0:T(8,128)(2,1)}, f32[1024,256]{1,0:T(8,128)}, f32[8,256]{1,0:T(8,128)}) custom-call(s32[15]{0:T(128)} %concatenate.24.scal_ref, bf16[384,1024]{1,0:T(8,128)(2,1)} %get-tuple-element.78.emb_ref, bf16[384,1024]{1,0:T(8,128)(2,1)} %get-tuple-element.80.norm_ref, bf16[384,256]{1,0:T(8,128)(2,1)} %bitcast.60, ...), custom_call_target="tpu_custom_call" | custom-call | flops 201326592 | bytes 2359296 | tf_op jit(solution)/shard_map/head/pallas_call | solution.py:305
  72.3 1.9 collective-permute-start.20
  74.2 2.4 %collective-permute-start.21 = (bf16[3,64,256]{2,1,0:T(8,128)(2,1)}, bf16[3,64,256]{2,1,0:T(8,128)(2,1)S(1)}, u32[]{:S(2)}, u32[]{:S(2)}) collective-permute-start(bf16[3,64,256]{2,1,0:T(8,128)(2,1)} %get-tuple-element.106.refs_0_.res_ref), channel_id=1, source_target_pairs={{0,3},{1,2},{2,1},{3,0},{4,7},{5,6},{6,5},{7,4},{8,11},{9,10},{10,... | collective-permute-start | bytes 294920 | tf_op jit(solution)/shard_map/ppermute | solution.py:591
  76.6 1.5 collective-permute-start.9
  78.1 1.3 add_convert_fusion.2
  79.5 4.6 %collective-permute-done.9.refs_3_ = bf16[3,64,256]{2,1,0:T(8,128)(2,1)S(1)} collective-permute-done((bf16[3,64,256]{2,1,0:T(8,128)(2,1)S(1)}, bf16[3,64,256]{2,1,0:T(8,128)(2,1)S(1)}, u32[]{:S(2)}, u32[]{:S(2)}) %collective-permute-start.9) | collective-permute-done | bytes 98336 | tf_op jit(solution)/shard_map/ppermute | solution.py:591
  84.7 6.1 %spectral_back.2 = (bf16[3,64,256]{2,1,0:T(8,128)(2,1)}, bf16[3,64,256]{2,1,0:T(8,128)(2,1)}, bf16[3,64,256]{2,1,0:T(8,128)(2,1)}, bf16[3,64,256]{2,1,0:T(8,128)...) custom-call(s32[15]{0:T(128)} %concatenate.24.scal_ref, bf16[3,512,256]{2,1,0:T(8,128)(2,1)} %constant.75.clone.t_ref, ...), custom_call_target="tpu_custom_call" | custom-call | flops 1006632960 | bytes 3145728 | tf_op jit(solution)/shard_map/spectral_back/pallas_call | solution.py:398
  91.5 6.2 %spectral_back.3 = (bf16[3,64,256]{2,1,0:T(8,128)(2,1)}, bf16[3,64,256]{2,1,0:T(8,128)(2,1)}, bf16[3,64,256]{2,1,0:T(8,128)(2,1)}, bf16[3,64,256]{2,1,0:T(8,128)...) custom-call(s32[15]{0:T(128)} %concatenate.24.scal_ref, bf16[3,512,256]{2,1,0:T(8,128)(2,1)} %constant.75.clone.t_ref, ...), custom_call_target="tpu_custom_call" | custom-call | flops 1006632960 | bytes 3145728 | tf_op jit(solution)/shard_map/spectral_back/pallas_call | solution.py:398
  97.7 5.7 %collective-permute-start.22 = (bf16[3,64,256]{2,1,0:T(8,128)(2,1)}, bf16[3,64,256]{2,1,0:T(8,128)(2,1)S(1)}, u32[]{:S(2)}, u32[]{:S(2)}) collective-permute-start(bf16[3,64,256]{2,1,0:T(8,128)(2,1)} %get-tuple-element.113), channel_id=1, source_target_pairs={{0,1},{1,0},{2,3},{3,2},{4,5},{5,4},{6,7},{7,6},{8,9},{9,8},{10,11... | collective-permute-start | bytes 294920 | tf_op jit(solution)/shard_map/ppermute | solution.py:591
  103.6 1.9 pad_maximum_fusion
  105.5 3.8 %all-to-all-start = ((bf16[8,192,256]{2,1,0:T(8,128)(2,1)}), bf16[8,192,256]{2,1,0:T(8,128)(2,1)S(1)}, u32[]{:S(2)}, u32[]{:S(2)}) async-start(bf16[8,192,256]{2,1,0:T(8,128)(2,1)} %pad_maximum_fusion), calls=%async_computation | async-start | bytes 1572864 | tf_op jit(solution)/shard_map/all_to_all | solution.py:648
  109.3 2.4 %collective-permute-start.24 = (bf16[3,64,256]{2,1,0:T(8,128)(2,1)S(1)}, bf16[3,64,256]{2,1,0:T(8,128)(2,1)S(1)}, u32[]{:S(2)}, u32[]{:S(2)}) collective-permute-start(bf16[3,64,256]{2,1,0:T(8,128)(2,1)S(1)} %copy-done.38), channel_id=1, source_target_pairs={{0,3},{1,2},{2,1},{3,0},{4,7},{5,6},{6,5},{7,4},{8,11},{9,10},{10,... | collective-permute-start | bytes 294920 | tf_op jit(solution)/shard_map/ppermute | solution.py:591
  113.9 2.3 %collective-permute-start.12 = (bf16[3,64,256]{2,1,0:T(8,128)(2,1)S(1)}, bf16[3,64,256]{2,1,0:T(8,128)(2,1)S(1)}, u32[]{:S(2)}, u32[]{:S(2)}) collective-permute-start(bf16[3,64,256]{2,1,0:T(8,128)(2,1)S(1)} %copy-done.32), channel_id=1, source_target_pairs={{0,3},{1,2},{2,1},{3,0},{4,7},{5,6},{6,5},{7,4},{8,11},{9,10},{10,... | collective-permute-start | bytes 294920 | tf_op jit(solution)/shard_map/ppermute | solution.py:591
  117.5 3.7 %embedded_back.3 = (bf16[192,1024]{1,0:T(8,128)(2,1)}, f32[8,1024]{1,0:T(8,128)}) custom-call(s32[15]{0:T(128)} %concatenate.24.scal_ref, bf16[384,1024]{1,0:T(8,128)(2,1)} %get-tuple-element.78.emb_ref, f32[384,256]{1,0:T(8,128)} %get-tuple-element.79.stat_ref, bf16[3,64,256]{2,1,0:T(8,128)(2,1)} %get-tuple-element.106.refs_0_.res_ref, ...), custom_call_target="tpu_custom_call" | custom-call | flops 100663296 | bytes 1179648 | tf_op jit(solution)/shard_map/embedded_back/pallas_call | solution.py:455
  121.2 3.5 %collective-permute-done.11.refs_2_ = bf16[3,64,256]{2,1,0:T(8,128)(2,1)S(1)} collective-permute-done((bf16[3,64,256]{2,1,0:T(8,128)(2,1)S(1)}, bf16[3,64,256]{2,1,0:T(8,128)(2,1)S(1)}, u32[]{:S(2)}, u32[]{:S(2)}) %collective-permute-start.11) | collective-permute-done | bytes 98336 | tf_op jit(solution)/shard_map/ppermute | solution.py:591
  125.4 3.7 %embedded_back.2 = (bf16[192,1024]{1,0:T(8,128)(2,1)}, f32[8,1024]{1,0:T(8,128)}) custom-call(s32[15]{0:T(128)} %concatenate.24.scal_ref, bf16[384,1024]{1,0:T(8,128)(2,1)} %get-tuple-element.78.emb_ref, f32[384,256]{1,0:T(8,128)} %get-tuple-element.79.stat_ref, bf16[3,64,256]{2,1,0:T(8,128)(2,1)} %get-tuple-element.89.refs_0_.res_ref, ...), custom_call_target="tpu_custom_call" | custom-call | flops 100663296 | bytes 1179648 | tf_op jit(solution)/shard_map/embedded_back/pallas_call | solution.py:455
  131.8 7.5 %embed_grad.1 = (bf16[2,320,512]{2,1,0:T(8,128)(2,1)}, bf16[2,320,512]{2,1,0:T(8,128)(2,1)}, bf16[2,320,512]{2,1,0:T(8,128)(2,1)}, bf16[2,320,512]{2,1,0:T(8,128)(2,1)}) custom-call(s32[15]{0:T(128)} %concatenate.24.scal_ref, bf16[4,320,384]{2,1,0:T(8,128)(2,1)} %get-tuple-element.76.refs_0_, bf16[4,320,384]{2,1,0:T(8,128)(2,1)} %collective-permute-done.refs_1_, ...), custom_call_target="tpu_custom_call" | custom-call | flops 2013265920 | bytes 6160384 | tf_op jit(solution)/shard_map/embed_grad/pallas_call | solution.py:560
  139.6 2.2 collective-permute-start.31
  142.7 1.5 collective-permute-start.33
  144.3 1.7 collective-permute-start.27
  146.0 1.5 collective-permute-start.29
  148.8 3.4 %all-to-all-start.1 = ((bf16[8,64,256]{2,1,0:T(8,128)(2,1)}), bf16[8,64,256]{2,1,0:T(8,128)(2,1)S(1)}, u32[]{:S(2)}, u32[]{:S(2)}) async-start(bf16[8,64,256]{2,1,0:T(8,128)(2,1)} %broadcast_select_fusion), calls=%async_computation.1 | async-start | bytes 524288 | tf_op jit(solution)/shard_map/all_to_all | solution.py:693
  152.3 1.4 collective-permute-done.32
  154.7 7.4 %collective-permute-done.27 = bf16[2,320,512]{2,1,0:T(8,128)(2,1)S(1)} collective-permute-done((bf16[2,320,512]{2,1,0:T(8,128)(2,1)}, bf16[2,320,512]{2,1,0:T(8,128)(2,1)S(1)}, u32[]{:S(2)}, u32[]{:S(2)}) %collective-permute-start.27) | collective-permute-done | bytes 655392 | tf_op jit(solution)/shard_map/ppermute | solution.py:585
  162.4 1.7 collective-permute-start.28
  165.8 6.1 %collective-permute-done.28 = bf16[1,320,512]{2,1,0:T(8,128)(2,1)S(1)} collective-permute-done((bf16[1,320,512]{2,1,0:T(8,128)(2,1)S(1)}, bf16[1,320,512]{2,1,0:T(8,128)(2,1)S(1)}, u32[]{:S(2)}, u32[]{:S(2)}) %collective-permute-start.28) | collective-permute-done | bytes 327712 | tf_op jit(solution)/shard_map/ppermute | solution.py:585
  172.6 19.1 %all_to_all.20 = bf16[4,80,1024]{2,1,0:T(8,128)(2,1)S(1)} all-to-all(bf16[4,80,1024]{2,1,0:T(8,128)(2,1)S(1)} %bitcast.53), channel_id=1, replica_groups=mesh['grp'=8,'fft'=4] {'fft'}, dimensions={0} | all-to-all | bytes 1310720 | tf_op jit(solution)/shard_map/all_to_all | solution.py:622
  191.6 1.3 broadcast_in_dim.123
  193.0 3.6 %all-to-all-start.3 = ((bf16[8,448,256]{2,1,0:T(8,128)(2,1)}), bf16[8,448,256]{2,1,0:T(8,128)(2,1)S(1)}, u32[]{:S(2)}, u32[]{:S(2)}) async-start(bf16[8,448,256]{2,1,0:T(8,128)(2,1)} %broadcast_in_dim.123), calls=%async_computation.3 | async-start | bytes 3670016 | tf_op jit(solution)/shard_map/all_to_all | solution.py:627
  199.2 21.1 %all-to-all-done.3.x_ref = bf16[8,448,256]{2,1,0:T(8,128)(2,1)S(1)} async-done(((bf16[8,448,256]{2,1,0:T(8,128)(2,1)}), bf16[8,448,256]{2,1,0:T(8,128)(2,1)S(1)}, u32[]{:S(2)}, u32[]{:S(2)}) %all-to-all-start.3) | async-done | bytes 1835040 | tf_op jit(solution)/shard_map/all_to_all | solution.py:627
  223.0 3.4 %assembled.1 = (f32[1024,256]{1,0:T(8,128)}, f32[2,2,8,128,128]{4,3,2,1,0:T(8,128)}) custom-call(bf16[8,448,256]{2,1,0:T(8,128)(2,1)} %copy-done), custom_call_target="tpu_custom_call" | custom-call | tf_op jit(solution)/shard_map/assembled/pallas_call | solution.py:677
  (199 shorter events, 25.1 us)
Async XLA Ops:
  2.0 19.0 %copy-start.42 = (s32[48]{0:T(128)S(1)}, s32[48]{0:T(128)}, u32[]{:S(2)}) copy-start(s32[48]{0:T(128)} %param.15) | copy-start | bytes 580
  11.0 29.4 %collective-permute-start.13 = (bf16[3,64,256]{2,1,0:T(8,128)(2,1)}, bf16[3,64,256]{2,1,0:T(8,128)(2,1)S(1)}, u32[]{:S(2)}, u32[]{:S(2)}) collective-permute-start(bf16[3,64,256]{2,1,0:T(8,128)(2,1)} %get-tuple-element.99), channel_id=1, source_target_pairs={{0,1},{1,0},{2,3},{3,2},{4,5},{5,4},{6,7},{7,6},{8,9},{9,8},{10,11... | collective-permute-start | bytes 294920 | tf_op jit(solution)/shard_map/ppermute | solution.py:591
  14.0 35.8 %collective-permute-start.14 = (bf16[3,64,256]{2,1,0:T(8,128)(2,1)}, bf16[3,64,256]{2,1,0:T(8,128)(2,1)S(1)}, u32[]{:S(2)}, u32[]{:S(2)}) collective-permute-start(bf16[3,64,256]{2,1,0:T(8,128)(2,1)} %get-tuple-element.100), channel_id=1, source_target_pairs={{0,2},{1,3},{2,0},{3,1},{4,6},{5,7},{6,4},{7,5},{8,10},{9,11},{10,... | collective-permute-start | bytes 294920 | tf_op jit(solution)/shard_map/ppermute | solution.py:591
  16.6 6.3 %collective-permute-start.1 = (bf16[3,64,256]{2,1,0:T(8,128)(2,1)}, bf16[3,64,256]{2,1,0:T(8,128)(2,1)S(1)}, u32[]{:S(2)}, u32[]{:S(2)}) collective-permute-start(bf16[3,64,256]{2,1,0:T(8,128)(2,1)} %get-tuple-element.82), channel_id=1, source_target_pairs={{0,1},{1,0},{2,3},{3,2},{4,5},{5,4},{6,7},{7,6},{8,9},{9,8},{10,11... | collective-permute-start | bytes 294920 | tf_op jit(solution)/shard_map/ppermute | solution.py:591
  17.1 13.5 %collective-permute-start.2 = (bf16[3,64,256]{2,1,0:T(8,128)(2,1)}, bf16[3,64,256]{2,1,0:T(8,128)(2,1)S(1)}, u32[]{:S(2)}, u32[]{:S(2)}) collective-permute-start(bf16[3,64,256]{2,1,0:T(8,128)(2,1)} %get-tuple-element.83), channel_id=1, source_target_pairs={{0,2},{1,3},{2,0},{3,1},{4,6},{5,7},{6,4},{7,5},{8,10},{9,11},{10,... | collective-permute-start | bytes 294920 | tf_op jit(solution)/shard_map/ppermute | solution.py:591
  17.1 13.5 %collective-permute-start.3 = (bf16[3,64,256]{2,1,0:T(8,128)(2,1)}, bf16[3,64,256]{2,1,0:T(8,128)(2,1)S(1)}, u32[]{:S(2)}, u32[]{:S(2)}) collective-permute-start(bf16[3,64,256]{2,1,0:T(8,128)(2,1)} %get-tuple-element.84), channel_id=1, source_target_pairs={{0,3},{1,2},{2,1},{3,0},{4,7},{5,6},{6,5},{7,4},{8,11},{9,10},{10,... | collective-permute-start | bytes 294920 | tf_op jit(solution)/shard_map/ppermute | solution.py:591
  22.9 26.9 %collective-permute-start.15 = (bf16[3,64,256]{2,1,0:T(8,128)(2,1)}, bf16[3,64,256]{2,1,0:T(8,128)(2,1)S(1)}, u32[]{:S(2)}, u32[]{:S(2)}) collective-permute-start(bf16[3,64,256]{2,1,0:T(8,128)(2,1)} %get-tuple-element.101), channel_id=1, source_target_pairs={{0,3},{1,2},{2,1},{3,0},{4,7},{5,6},{6,5},{7,4},{8,11},{9,10},{10,... | collective-permute-start | bytes 294920 | tf_op jit(solution)/shard_map/ppermute | solution.py:591
  36.2 22.2 %collective-permute-start.4 = (bf16[3,64,256]{2,1,0:T(8,128)(2,1)}, bf16[3,64,256]{2,1,0:T(8,128)(2,1)S(1)}, u32[]{:S(2)}, u32[]{:S(2)}) collective-permute-start(bf16[3,64,256]{2,1,0:T(8,128)(2,1)} %get-tuple-element.86), channel_id=1, source_target_pairs={{0,1},{1,0},{2,3},{3,2},{4,5},{5,4},{6,7},{7,6},{8,9},{9,8},{10,11... | collective-permute-start | bytes 294920 | tf_op jit(solution)/shard_map/ppermute | solution.py:591
  38.8 21.0 %collective-permute-start.5 = (bf16[3,64,256]{2,1,0:T(8,128)(2,1)}, bf16[3,64,256]{2,1,0:T(8,128)(2,1)S(1)}, u32[]{:S(2)}, u32[]{:S(2)}) collective-permute-start(bf16[3,64,256]{2,1,0:T(8,128)(2,1)} %get-tuple-element.87), channel_id=1, source_target_pairs={{0,2},{1,3},{2,0},{3,1},{4,6},{5,7},{6,4},{7,5},{8,10},{9,11},{10,... | collective-permute-start | bytes 294920 | tf_op jit(solution)/shard_map/ppermute | solution.py:591
  40.4 9.5 %copy-start.35 = (bf16[3,64,256]{2,1,0:T(8,128)(2,1)}, bf16[3,64,256]{2,1,0:T(8,128)(2,1)S(1)}, u32[]{:S(2)}) copy-start(bf16[3,64,256]{2,1,0:T(8,128)(2,1)S(1)} %collective-permute-done.13.refs_1_) | copy-start | bytes 294916
  40.4 19.5 %collective-permute-start.6 = (bf16[3,64,256]{2,1,0:T(8,128)(2,1)}, bf16[3,64,256]{2,1,0:T(8,128)(2,1)S(1)}, u32[]{:S(2)}, u32[]{:S(2)}) collective-permute-start(bf16[3,64,256]{2,1,0:T(8,128)(2,1)} %get-tuple-element.88), channel_id=1, source_target_pairs={{0,3},{1,2},{2,1},{3,0},{4,7},{5,6},{6,5},{7,4},{8,11},{9,10},{10,... | collective-permute-start | bytes 294920 | tf_op jit(solution)/shard_map/ppermute | solution.py:591
  55.4 12.0 %collective-permute-start.16 = (bf16[3,64,256]{2,1,0:T(8,128)(2,1)}, bf16[3,64,256]{2,1,0:T(8,128)(2,1)S(1)}, u32[]{:S(2)}, u32[]{:S(2)}) collective-permute-start(bf16[3,64,256]{2,1,0:T(8,128)(2,1)} %get-tuple-element.103), channel_id=1, source_target_pairs={{0,1},{1,0},{2,3},{3,2},{4,5},{5,4},{6,7},{7,6},{8,9},{9,8},{10,11... | collective-permute-start | bytes 294920 | tf_op jit(solution)/shard_map/ppermute | solution.py:591
  56.0 11.6 %collective-permute-start.17 = (bf16[3,64,256]{2,1,0:T(8,128)(2,1)}, bf16[3,64,256]{2,1,0:T(8,128)(2,1)S(1)}, u32[]{:S(2)}, u32[]{:S(2)}) collective-permute-start(bf16[3,64,256]{2,1,0:T(8,128)(2,1)} %get-tuple-element.104), channel_id=1, source_target_pairs={{0,2},{1,3},{2,0},{3,1},{4,6},{5,7},{6,4},{7,5},{8,10},{9,11},{10,... | collective-permute-start | bytes 294920 | tf_op jit(solution)/shard_map/ppermute | solution.py:591
  58.4 9.2 %collective-permute-start.18 = (bf16[3,64,256]{2,1,0:T(8,128)(2,1)}, bf16[3,64,256]{2,1,0:T(8,128)(2,1)S(1)}, u32[]{:S(2)}, u32[]{:S(2)}) collective-permute-start(bf16[3,64,256]{2,1,0:T(8,128)(2,1)} %get-tuple-element.105), channel_id=1, source_target_pairs={{0,3},{1,2},{2,1},{3,0},{4,7},{5,6},{6,5},{7,4},{8,11},{9,10},{10,... | collective-permute-start | bytes 294920 | tf_op jit(solution)/shard_map/ppermute | solution.py:591
  64.5 9.7 %collective-permute-start.7 = (bf16[3,64,256]{2,1,0:T(8,128)(2,1)}, bf16[3,64,256]{2,1,0:T(8,128)(2,1)S(1)}, u32[]{:S(2)}, u32[]{:S(2)}) collective-permute-start(bf16[3,64,256]{2,1,0:T(8,128)(2,1)} %get-tuple-element.89.refs_0_.res_ref), channel_id=1, source_target_pairs={{0,1},{1,0},{2,3},{3,2},{4,5},{5,4},{6,7},{7,6},{8,9},{9,8},{10,11... | collective-permute-start | bytes 294920 | tf_op jit(solution)/shard_map/ppermute | solution.py:591
  64.5 12.1 %collective-permute-start.8 = (bf16[3,64,256]{2,1,0:T(8,128)(2,1)}, bf16[3,64,256]{2,1,0:T(8,128)(2,1)S(1)}, u32[]{:S(2)}, u32[]{:S(2)}) collective-permute-start(bf16[3,64,256]{2,1,0:T(8,128)(2,1)} %get-tuple-element.89.refs_0_.res_ref), channel_id=1, source_target_pairs={{0,2},{1,3},{2,0},{3,1},{4,6},{5,7},{6,4},{7,5},{8,10},{9,11},{10,... | collective-permute-start | bytes 294920 | tf_op jit(solution)/shard_map/ppermute | solution.py:591
  67.4 63.6 %collective-permute-start = (bf16[4,320,384]{2,1,0:T(8,128)(2,1)S(1)}, bf16[4,320,384]{2,1,0:T(8,128)(2,1)}, u32[]{:S(2)}, u32[]{:S(2)}) collective-permute-start(bf16[4,320,384]{2,1,0:T(8,128)(2,1)S(1)} %copy-done.29), channel_id=1, source_target_pairs={{0,4},{4,0},{8,12},{12,8},{16,20},{20,16},{24,28},{28,24},{1,5},{5... | collective-permute-start | bytes 2949128 | tf_op jit(solution)/shard_map/ppermute | solution.py:585
  68.2 8.4 %copy-start.5 = (bf16[3,64,256]{2,1,0:T(8,128)(2,1)S(1)}, bf16[3,64,256]{2,1,0:T(8,128)(2,1)}, u32[]{:S(2)}) copy-start(bf16[3,64,256]{2,1,0:T(8,128)(2,1)} %get-tuple-element.89.refs_0_.res_ref) | copy-start | bytes 294916
  68.2 9.9 %copy-start.1 = (f32[1024,256]{1,0:T(8,128)S(1)}, f32[1024,256]{1,0:T(8,128)}, u32[]{:S(2)}) copy-start(f32[1024,256]{1,0:T(8,128)} %get-tuple-element.121) | copy-start | bytes 3145732
  72.2 18.6 %collective-permute-start.19 = (bf16[3,64,256]{2,1,0:T(8,128)(2,1)}, bf16[3,64,256]{2,1,0:T(8,128)(2,1)S(1)}, u32[]{:S(2)}, u32[]{:S(2)}) collective-permute-start(bf16[3,64,256]{2,1,0:T(8,128)(2,1)} %get-tuple-element.106.refs_0_.res_ref), channel_id=1, source_target_pairs={{0,1},{1,0},{2,3},{3,2},{4,5},{5,4},{6,7},{7,6},{8,9},{9,8},{10,11... | collective-permute-start | bytes 294920 | tf_op jit(solution)/shard_map/ppermute | solution.py:591
  72.3 18.5 %collective-permute-start.20 = (bf16[3,64,256]{2,1,0:T(8,128)(2,1)}, bf16[3,64,256]{2,1,0:T(8,128)(2,1)S(1)}, u32[]{:S(2)}, u32[]{:S(2)}) collective-permute-start(bf16[3,64,256]{2,1,0:T(8,128)(2,1)} %get-tuple-element.106.refs_0_.res_ref), channel_id=1, source_target_pairs={{0,2},{1,3},{2,0},{3,1},{4,6},{5,7},{6,4},{7,5},{8,10},{9,11},{10,... | collective-permute-start | bytes 294920 | tf_op jit(solution)/shard_map/ppermute | solution.py:591
  74.2 16.6 %collective-permute-start.21 = (bf16[3,64,256]{2,1,0:T(8,128)(2,1)}, bf16[3,64,256]{2,1,0:T(8,128)(2,1)S(1)}, u32[]{:S(2)}, u32[]{:S(2)}) collective-permute-start(bf16[3,64,256]{2,1,0:T(8,128)(2,1)} %get-tuple-element.106.refs_0_.res_ref), channel_id=1, source_target_pairs={{0,3},{1,2},{2,1},{3,0},{4,7},{5,6},{6,5},{7,4},{8,11},{9,10},{10,... | collective-permute-start | bytes 294920 | tf_op jit(solution)/shard_map/ppermute | solution.py:591
  76.6 7.5 %collective-permute-start.9 = (bf16[3,64,256]{2,1,0:T(8,128)(2,1)S(1)}, bf16[3,64,256]{2,1,0:T(8,128)(2,1)S(1)}, u32[]{:S(2)}, u32[]{:S(2)}) collective-permute-start(bf16[3,64,256]{2,1,0:T(8,128)(2,1)S(1)} %copy-done.5), channel_id=1, source_target_pairs={{0,3},{1,2},{2,1},{3,0},{4,7},{5,6},{6,5},{7,4},{8,11},{9,10},{10,... | collective-permute-start | bytes 294920 | tf_op jit(solution)/shard_map/ppermute | solution.py:591
  97.7 15.0 %collective-permute-start.22 = (bf16[3,64,256]{2,1,0:T(8,128)(2,1)}, bf16[3,64,256]{2,1,0:T(8,128)(2,1)S(1)}, u32[]{:S(2)}, u32[]{:S(2)}) collective-permute-start(bf16[3,64,256]{2,1,0:T(8,128)(2,1)} %get-tuple-element.113), channel_id=1, source_target_pairs={{0,1},{1,0},{2,3},{3,2},{4,5},{5,4},{6,7},{7,6},{8,9},{9,8},{10,11... | collective-permute-start | bytes 294920 | tf_op jit(solution)/shard_map/ppermute | solution.py:591
  103.4 10.4 %collective-permute-start.23 = (bf16[3,64,256]{2,1,0:T(8,128)(2,1)}, bf16[3,64,256]{2,1,0:T(8,128)(2,1)S(1)}, u32[]{:S(2)}, u32[]{:S(2)}) collective-permute-start(bf16[3,64,256]{2,1,0:T(8,128)(2,1)} %get-tuple-element.114), channel_id=1, source_target_pairs={{0,2},{1,3},{2,0},{3,1},{4,6},{5,7},{6,4},{7,5},{8,10},{9,11},{10,... | collective-permute-start | bytes 294920 | tf_op jit(solution)/shard_map/ppermute | solution.py:591
  103.6 8.1 %copy-start.34 = (bf16[3,64,256]{2,1,0:T(8,128)(2,1)S(1)}, bf16[3,64,256]{2,1,0:T(8,128)(2,1)}, u32[]{:S(2)}) copy-start(bf16[3,64,256]{2,1,0:T(8,128)(2,1)} %get-tuple-element.94) | copy-start | bytes 294916
  103.6 9.1 %copy-start.33 = (bf16[3,64,256]{2,1,0:T(8,128)(2,1)S(1)}, bf16[3,64,256]{2,1,0:T(8,128)(2,1)}, u32[]{:S(2)}) copy-start(bf16[3,64,256]{2,1,0:T(8,128)(2,1)} %get-tuple-element.95) | copy-start | bytes 294916
  103.6 10.3 %copy-start.32 = (bf16[3,64,256]{2,1,0:T(8,128)(2,1)S(1)}, bf16[3,64,256]{2,1,0:T(8,128)(2,1)}, u32[]{:S(2)}) copy-start(bf16[3,64,256]{2,1,0:T(8,128)(2,1)} %get-tuple-element.96) | copy-start | bytes 294916
  105.5 33.8 %all-to-all-start = ((bf16[8,192,256]{2,1,0:T(8,128)(2,1)}), bf16[8,192,256]{2,1,0:T(8,128)(2,1)S(1)}, u32[]{:S(2)}, u32[]{:S(2)}) async-start(bf16[8,192,256]{2,1,0:T(8,128)(2,1)} %pad_maximum_fusion), calls=%async_computation | async-start | bytes 1572864 | tf_op jit(solution)/shard_map/all_to_all | solution.py:648
  109.3 7.5 %collective-permute-start.24 = (bf16[3,64,256]{2,1,0:T(8,128)(2,1)S(1)}, bf16[3,64,256]{2,1,0:T(8,128)(2,1)S(1)}, u32[]{:S(2)}, u32[]{:S(2)}) collective-permute-start(bf16[3,64,256]{2,1,0:T(8,128)(2,1)S(1)} %copy-done.38), channel_id=1, source_target_pairs={{0,3},{1,2},{2,1},{3,0},{4,7},{5,6},{6,5},{7,4},{8,11},{9,10},{10,... | collective-permute-start | bytes 294920 | tf_op jit(solution)/shard_map/ppermute | solution.py:591
  111.7 9.5 %collective-permute-start.10 = (bf16[3,64,256]{2,1,0:T(8,128)(2,1)S(1)}, bf16[3,64,256]{2,1,0:T(8,128)(2,1)S(1)}, u32[]{:S(2)}, u32[]{:S(2)}) collective-permute-start(bf16[3,64,256]{2,1,0:T(8,128)(2,1)S(1)} %copy-done.34), channel_id=1, source_target_pairs={{0,1},{1,0},{2,3},{3,2},{4,5},{5,4},{6,7},{7,6},{8,9},{9,8},{10,11... | collective-permute-start | bytes 294920 | tf_op jit(solution)/shard_map/ppermute | solution.py:591
  112.7 12.0 %collective-permute-start.11 = (bf16[3,64,256]{2,1,0:T(8,128)(2,1)S(1)}, bf16[3,64,256]{2,1,0:T(8,128)(2,1)S(1)}, u32[]{:S(2)}, u32[]{:S(2)}) collective-permute-start(bf16[3,64,256]{2,1,0:T(8,128)(2,1)S(1)} %copy-done.33), channel_id=1, source_target_pairs={{0,2},{1,3},{2,0},{3,1},{4,6},{5,7},{6,4},{7,5},{8,10},{9,11},{10,... | collective-permute-start | bytes 294920 | tf_op jit(solution)/shard_map/ppermute | solution.py:591
  113.9 10.9 %collective-permute-start.12 = (bf16[3,64,256]{2,1,0:T(8,128)(2,1)S(1)}, bf16[3,64,256]{2,1,0:T(8,128)(2,1)S(1)}, u32[]{:S(2)}, u32[]{:S(2)}) collective-permute-start(bf16[3,64,256]{2,1,0:T(8,128)(2,1)S(1)} %copy-done.32), channel_id=1, source_target_pairs={{0,3},{1,2},{2,1},{3,0},{4,7},{5,6},{6,5},{7,4},{8,11},{9,10},{10,... | collective-permute-start | bytes 294920 | tf_op jit(solution)/shard_map/ppermute | solution.py:591
  121.2 8.7 %collective-permute-start.26 = (bf16[192,1024]{1,0:T(8,128)(2,1)}, bf16[192,1024]{1,0:T(8,128)(2,1)S(1)}, u32[]{:S(2)}, u32[]{:S(2)}) collective-permute-start(bf16[192,1024]{1,0:T(8,128)(2,1)} %get-tuple-element.116.refs_3_), channel_id=1, source_target_pairs={{0,4},{4,0},{8,12},{12,8},{16,20},{20,16},{24,28},{28,24},{1,5},{5... | collective-permute-start | bytes 1179656 | tf_op jit(solution)/shard_map/ppermute | solution.py:585
  129.1 1.9 collective-permute-start.25
  139.3 8.1 %copy-start.18 = (bf16[3,64,256]{2,1,0:T(8,128)(2,1)S(1)}, bf16[3,64,256]{2,1,0:T(8,128)(2,1)}, u32[]{:S(2)}) copy-start(bf16[3,64,256]{2,1,0:T(8,128)(2,1)} %get-tuple-element.128) | copy-start | bytes 294916
  139.3 8.1 %copy-start.19 = (bf16[3,64,256]{2,1,0:T(8,128)(2,1)S(1)}, bf16[3,64,256]{2,1,0:T(8,128)(2,1)}, u32[]{:S(2)}) copy-start(bf16[3,64,256]{2,1,0:T(8,128)(2,1)} %get-tuple-element.129) | copy-start | bytes 294916
  139.6 14.1 %collective-permute-start.31 = (bf16[224,256]{1,0:T(8,128)(2,1)S(1)}, bf16[224,256]{1,0:T(8,128)(2,1)S(1)}, u32[]{:S(2)}, u32[]{:S(2)}) collective-permute-start(bf16[224,256]{1,0:T(8,128)(2,1)S(1)} %pad_maximum_fusion.5), channel_id=1, source_target_pairs={{0,1},{1,0},{2,3},{3,2},{4,5},{5,4},{6,7},{7,6},{8,9},{9,8},{10,11... | collective-permute-start | bytes 344072 | tf_op jit(solution)/shard_map/ppermute | solution.py:591
  141.9 11.8 %collective-permute-start.32 = (bf16[224,256]{1,0:T(8,128)(2,1)S(1)}, bf16[224,256]{1,0:T(8,128)(2,1)S(1)}, u32[]{:S(2)}, u32[]{:S(2)}) collective-permute-start(bf16[224,256]{1,0:T(8,128)(2,1)S(1)} %pad_maximum_fusion.5), channel_id=1, source_target_pairs={{0,2},{1,3},{2,0},{3,1},{4,6},{5,7},{6,4},{7,5},{8,10},{9,11},{10,... | collective-permute-start | bytes 344072 | tf_op jit(solution)/shard_map/ppermute | solution.py:591
  142.7 9.6 %collective-permute-start.33 = (bf16[224,256]{1,0:T(8,128)(2,1)S(1)}, bf16[224,256]{1,0:T(8,128)(2,1)S(1)}, u32[]{:S(2)}, u32[]{:S(2)}) collective-permute-start(bf16[224,256]{1,0:T(8,128)(2,1)S(1)} %pad_maximum_fusion.5), channel_id=1, source_target_pairs={{0,3},{1,2},{2,1},{3,0},{4,7},{5,6},{6,5},{7,4},{8,11},{9,10},{10,... | collective-permute-start | bytes 344072 | tf_op jit(solution)/shard_map/ppermute | solution.py:591
  144.3 17.8 %collective-permute-start.27 = (bf16[2,320,512]{2,1,0:T(8,128)(2,1)}, bf16[2,320,512]{2,1,0:T(8,128)(2,1)S(1)}, u32[]{:S(2)}, u32[]{:S(2)}) collective-permute-start(bf16[2,320,512]{2,1,0:T(8,128)(2,1)} %get-tuple-element.131), channel_id=1, source_target_pairs={{0,8},{4,12},{8,0},{12,4},{16,24},{20,28},{24,16},{28,20},{1,9},{5... | collective-permute-start | bytes 1966088 | tf_op jit(solution)/shard_map/ppermute | solution.py:585
  146.0 19.1 %collective-permute-start.29 = (bf16[2,320,512]{2,1,0:T(8,128)(2,1)}, bf16[2,320,512]{2,1,0:T(8,128)(2,1)S(1)}, u32[]{:S(2)}, u32[]{:S(2)}) collective-permute-start(bf16[2,320,512]{2,1,0:T(8,128)(2,1)} %get-tuple-element.133), channel_id=1, source_target_pairs={{0,16},{4,20},{8,24},{12,28},{16,0},{20,4},{24,8},{28,12},{1,17},{... | collective-permute-start | bytes 1966088 | tf_op jit(solution)/shard_map/ppermute | solution.py:585
  148.8 23.7 %all-to-all-start.1 = ((bf16[8,64,256]{2,1,0:T(8,128)(2,1)}), bf16[8,64,256]{2,1,0:T(8,128)(2,1)S(1)}, u32[]{:S(2)}, u32[]{:S(2)}) async-start(bf16[8,64,256]{2,1,0:T(8,128)(2,1)} %broadcast_select_fusion), calls=%async_computation.1 | async-start | bytes 524288 | tf_op jit(solution)/shard_map/all_to_all | solution.py:693
  152.3 9.8 %copy-start.4 = (bf16[2,320,512]{2,1,0:T(8,128)(2,1)S(1)}, bf16[2,320,512]{2,1,0:T(8,128)(2,1)}, u32[]{:S(2)}) copy-start(bf16[2,320,512]{2,1,0:T(8,128)(2,1)} %get-tuple-element.130) | copy-start | bytes 1966084
  154.7 10.3 %copy-start.3 = (bf16[2,320,512]{2,1,0:T(8,128)(2,1)S(1)}, bf16[2,320,512]{2,1,0:T(8,128)(2,1)}, u32[]{:S(2)}) copy-start(bf16[2,320,512]{2,1,0:T(8,128)(2,1)} %get-tuple-element.132) | copy-start | bytes 1966084
  162.4 9.6 %collective-permute-start.28 = (bf16[1,320,512]{2,1,0:T(8,128)(2,1)S(1)}, bf16[1,320,512]{2,1,0:T(8,128)(2,1)S(1)}, u32[]{:S(2)}, u32[]{:S(2)}) collective-permute-start(bf16[1,320,512]{2,1,0:T(8,128)(2,1)S(1)} %slice_bitcast_fusion), channel_id=1, source_target_pairs={{0,16},{4,20},{8,24},{12,28},{16,0},{20,4},{24,8},{28,12},{1,17},{... | collective-permute-start | bytes 983048 | tf_op jit(solution)/shard_map/ppermute | solution.py:585
  165.2 7.1 %collective-permute-start.30 = (bf16[1,320,512]{2,1,0:T(8,128)(2,1)S(1)}, bf16[1,320,512]{2,1,0:T(8,128)(2,1)S(1)}, u32[]{:S(2)}, u32[]{:S(2)}) collective-permute-start(bf16[1,320,512]{2,1,0:T(8,128)(2,1)S(1)} %slice.131), channel_id=1, source_target_pairs={{0,8},{4,12},{8,0},{12,4},{16,24},{20,28},{24,16},{28,20},{1,9},{5... | collective-permute-start | bytes 983048 | tf_op jit(solution)/shard_map/ppermute | solution.py:585
  193.0 27.4 %all-to-all-start.3 = ((bf16[8,448,256]{2,1,0:T(8,128)(2,1)}), bf16[8,448,256]{2,1,0:T(8,128)(2,1)S(1)}, u32[]{:S(2)}, u32[]{:S(2)}) async-start(bf16[8,448,256]{2,1,0:T(8,128)(2,1)} %broadcast_in_dim.123), calls=%async_computation.3 | async-start | bytes 3670016 | tf_op jit(solution)/shard_map/all_to_all | solution.py:627
  (33 other events, 89.5 us)

commit v4 on v3

--- a/solution.py
+++ b/solution.py
@@ -10,7 +10,7 @@
 EPSILON = 1e-05
 SHRINK = 0.01
 CHUNKS = 2
-VMEM_BYTES = 60 * 1024 * 1024
+VMEM_BYTES = 24 * 1024 * 1024
 SLOTS = 6
 SHARD, FIRST_ROW, GROUP, SIDES = 0, 1, 2, 3
 HALF = jnp.bfloat16
@@ -288,7 +288,7 @@
     scale_root = float(np.sqrt(np.float32(samples)))
 
     def body(scal_ref, emb_ref, norm_ref, tgt_ref, w_ref, b_ref, *refs):
-        mix_refs, (pred_ref, res_ref, grad_ref, bias_ref, held) = refs[:shards], refs[shards:]
+        mix_refs, (pred_ref, res_ref, up_ref, bias_ref, held) = refs[:shards], refs[shards:]
         fill_lanes(scal_ref, mix_refs, held)
         side, valid = token_sides(scal_ref, first, count, per_sample, cells)
         updated = (emb_ref[...].astype(FULL) + norm_ref[...].astype(FULL) + held[...].astype(FULL)).astype(HALF)
@@ -297,7 +297,7 @@
         scale = 2.0 / (side.astype(FULL) * scale_root)
         residual = (scale * valid * (output - tgt_ref[...].astype(FULL))).astype(HALF)
         res_ref[...] = residual.reshape(res_ref.shape)
-        grad_ref[...] = dot_tn(updated, residual)
+        up_ref[...] = updated
         total = jnp.sum(residual.astype(FULL), axis=0, keepdims=True)
         bias_ref[...] = jnp.broadcast_to(total, bias_ref.shape)
 
@@ -315,21 +315,44 @@
                 whole((1, outs)),
             ]
             + [whole(mixed[0].shape)] * shards,
-            out_specs=[whole(token_shape), whole(token_shape), whole((width, outs)), whole((8, outs))],
+            out_specs=[whole(token_shape), whole(token_shape), whole((rows, width)), whole((8, outs))],
             scratch_shapes=[pltpu.VMEM((rows, width), HALF)],
         ),
         out_shape=[
             jax.ShapeDtypeStruct(token_shape, HALF),
             jax.ShapeDtypeStruct(token_shape, HALF),
-            jax.ShapeDtypeStruct((width, outs), FULL),
+            jax.ShapeDtypeStruct((rows, width), HALF),
             jax.ShapeDtypeStruct((8, outs), FULL),
         ],
         compiler_params=params(),
         cost_estimate=pl.CostEstimate(
-            flops=4 * rows * width * outs, bytes_accessed=rows * width * 4 + width * outs * 6, transcendentals=0
+            flops=2 * rows * width * outs, bytes_accessed=rows * width * 4 + width * outs * 6, transcendentals=0
         ),
         name="head",
     )(scal, embedded, normed, targets, head_w, head_b, *mixed)
+
+
+def head_gradient(updated, residual):
+    width = updated[0].shape[1]
+    outs = residual[0].shape[-1]
+    count = len(updated)
+
+    def body(*refs):
+        total = None
+        for up_ref, res_ref in zip(refs[:count], refs[count : 2 * count]):
+            part = dot_tn(up_ref[...], res_ref[...].reshape(up_ref.shape[0], outs))
+            total = part if total is None else total + part
+        refs[-1][...] = total.astype(HALF)
+
+    return pl.pallas_call(
+        body,
+        out_shape=jax.ShapeDtypeStruct((width, outs), HALF),
+        compiler_params=params(),
+        cost_estimate=pl.CostEstimate(
+            flops=2 * count * updated[0].size * outs, bytes_accessed=2 * count * updated[0].size, transcendentals=0
+        ),
+        name="head_gradient",
+    )(*updated, *residual)
 
 
 def spectral_back_chunk(scal, table, factors, residual, head_w, spec_w, saved, first, before, last):
@@ -517,44 +540,37 @@
     )(scal, patches)
 
 
-def embed_grad_parts(scal, turned, grads, groups):
+def embed_grad_parts(scal, turned, grads, groups, away):
     pairs, block, tokens = turned[0].shape
-    width = grads[0].shape[1]
+    chunk_rows, width = grads[0].shape
     half = width // 2
     top = pairs // 2
     count = len(turned)
     depth = tokens * count
 
+    def relative(unit):
+        return jnp.where(unit < top, 2 * unit + away, unit - top + away * top)
+
     def body(scal_ref, *refs):
         turned_refs, grad_refs = refs[:count], refs[count : count + len(grads)]
-        left_send, left_keep, right_send, right_keep, held = refs[count + len(grads) :]
-        step = pl.program_id(0)
-
-        @pl.when(step == 0)
+        left_ref, right_ref, held = refs[count + len(grads) :]
+        unit = pl.program_id(0)
+
+        @pl.when(unit % top == 0)
         def _():
-            row = 0
-            for ref in grad_refs:
-                held[row : row + ref.shape[0]] = ref[...]
-                row += ref.shape[0]
+            for i, ref in enumerate(grad_refs):
+                held[i * chunk_rows : (i + 1) * chunk_rows] = ref[...]
 
         rows = jnp.concatenate([ref[0] for ref in turned_refs], axis=1)
         total = dot(rows, held[...]).astype(HALF)
 
-        @pl.when(step % 2 == 1)
+        @pl.when(unit < top)
         def _():
-            left_send[step // 2] = total[:, :half]
-
-        @pl.when(step % 2 == 0)
+            left_ref[0] = total
+
+        @pl.when(unit >= top)
         def _():
-            left_keep[step // 2] = total[:, :half]
-
-        @pl.when(step >= top)
-        def _():
-            right_send[step - top] = total[:, half:]
-
-        @pl.when(step < top)
-        def _():
-            right_keep[step] = total[:, half:]
+            right_ref[0] = total
 
     shape = (top, block, half)
     return pl.pallas_call(
@@ -563,18 +579,21 @@
             num_scalar_prefetch=1,
             grid=(pairs,),
             in_specs=[
-                pl.BlockSpec((1, block, tokens), lambda i, s: (jnp.bitwise_xor(s[GROUP] // 2, i), 0, 0))
+                pl.BlockSpec((1, block, tokens), lambda i, s: (jnp.bitwise_xor(s[GROUP] // 2, relative(i)), 0, 0))
                 for _ in turned
             ]
-            + [whole(g.shape) for g in grads],
-            out_specs=[whole(shape)] * 4,
-            scratch_shapes=[pltpu.VMEM((depth, width), HALF)],
-        ),
-        out_shape=[jax.ShapeDtypeStruct(shape, HALF)] * 4,
+            + [pl.BlockSpec((chunk_rows, half), lambda i, s: (0, i // top)) for _ in grads],
+            out_specs=[
+                pl.BlockSpec((1, block, half), lambda i, s: (jnp.minimum(i, top - 1), 0, 0)),
+                pl.BlockSpec((1, block, half), lambda i, s: (jnp.maximum(i - top, 0), 0, 0)),
+            ],
+            scratch_shapes=[pltpu.VMEM((depth, half), HALF)],
+        ),
+        out_shape=[jax.ShapeDtypeStruct(shape, HALF)] * 2,
         compiler_params=params(),
         cost_estimate=pl.CostEstimate(
-            flops=2 * depth * pairs * block * width,
-            bytes_accessed=2 * (pairs * block * (depth + width) + depth * width),
+            flops=depth * pairs * block * width,
+            bytes_accessed=pairs * block * (2 * depth + width) + depth * width,
             transcendentals=0,
         ),
         name="embed_grad",
@@ -596,15 +615,15 @@
     return (left.astype(FULL) + right.astype(FULL)).astype(HALF)
 
 
-def scatter_start(parts, groups):
+def scatter_start(received, kept, groups):
     bits = groups.bit_length() - 1
     ends = []
-    for send, keep, order, low in (
-        (parts[0], parts[1], list(range(1, bits)), True),
-        (parts[2], parts[3], list(range(bits - 1, 0, -1)), False),
+    for first, keep, order, low in (
+        (received[0], kept[0], list(range(2, bits)), True),
+        (received[1], kept[1], list(range(bits - 2, 0, -1)), False),
     ):
-        total = add_half(keep, swap_bit(send, order[0], groups))
-        for bit in order[1:]:
+        total = add_half(keep, first)
+        for bit in order:
             count, block, width = total.shape
             if low:
                 split = total.reshape(count // 2, 2, block, width)
@@ -614,19 +633,25 @@
                 keep, send = split[0], split[1]
             total = add_half(keep, swap_bit(send, bit, groups))
         ends.append(total[0])
-    return jnp.concatenate(ends, axis=-1)
-
-
-def scatter_end(part, shards):
-    part = part.reshape(shards, part.shape[0] // shards, -1)
-    moved = lax.all_to_all(part, "fft", split_axis=0, concat_axis=0, tiled=True)
-    return jnp.sum(moved.astype(FULL), axis=0)
-
-
-def to_all(values, axes, count):
-    return lax.all_to_all(
-        jnp.broadcast_to(values[None], (count,) + values.shape), axes, split_axis=0, concat_axis=0, tiled=True
-    )
+    return ends
+
+
+def scatter_end(ends, shards, shard_at):
+    share = ends[0].shape[0] // shards
+
+    def piece(k):
+        at = jnp.bitwise_xor(shard_at, k) * share
+        return jnp.concatenate([lax.dynamic_slice_in_dim(e, at, share) for e in ends], axis=-1)
+
+    return sum(p.astype(FULL) for p in across([piece(k) for k in range(shards)]))
+
+
+def from_all_groups(values, groups):
+    even = [values] + [
+        lax.ppermute(values, "grp", [(g, g ^ k) for g in range(groups)]) for k in range(2, groups, 2)
+    ]
+    odd = [swap_bit(v, 0, groups) for v in even]
+    return [v for pair in zip(even, odd) for v in pair]
 
 
 def hi_lo(values):
@@ -643,7 +668,7 @@
 def sum_over_groups(head_grad, spec_grad, groups):
     outs = head_grad.shape[1]
     packed = jnp.concatenate(
-        [head_grad.astype(HALF).reshape(groups, -1, outs), spec_grad.reshape(groups, -1, outs)], axis=1
+        [head_grad.reshape(groups, -1, outs), spec_grad.reshape(groups, -1, outs)], axis=1
     )
     return lax.all_to_all(packed, "grp", split_axis=0, concat_axis=0, tiled=True)
 
@@ -658,31 +683,48 @@
     return head_part, rest[:, :spec_rows], from_hi_lo(rest[:, spec_rows:])
 
 
-def assembled(gathered, head_rows, shards, blocks, width):
-    groups = gathered.shape[0]
+def assembled(scal, gathered, head_rows, shards, blocks, width):
+    groups = len(gathered)
     total_blocks = shards * blocks
     spec_rows = 2 * blocks * width // groups
-
-    def body(x_ref, head_ref, spec_ref):
-        for g in range(groups):
-            head_ref[g * head_rows : (g + 1) * head_rows] = x_ref[g, :head_rows].astype(FULL)
-            start = g * spec_rows
+    small_at = head_rows + shards * spec_rows
+    small_rows = (gathered[0].shape[0] - small_at) // 2
+
+    def body(scal_ref, *refs):
+        ins, (head_ref, spec_ref, small_ref) = refs[:groups], refs[groups:]
+        small = None
+        for k, ref in enumerate(ins):
+            group = jnp.bitwise_xor(scal_ref[GROUP], k)
+            at = pl.ds(pl.multiple_of(group * head_rows, head_rows), head_rows)
+            head_ref[at, :] = ref[:head_rows].astype(FULL)
+            start = group * spec_rows
             layer, b = start // (blocks * width), (start // width) % blocks
-            rows = slice(start % width, start % width + spec_rows)
+            rows = pl.ds(pl.multiple_of(start % width, spec_rows), spec_rows)
             for z in range(shards):
-                values = x_ref[g, head_rows + z * spec_rows : head_rows + (z + 1) * spec_rows].astype(FULL)
+                values = ref[head_rows + z * spec_rows : head_rows + (z + 1) * spec_rows].astype(FULL)
                 spec_ref[layer, 0, z * blocks + b, rows] = values[:, :width]
                 spec_ref[layer, 1, z * blocks + b, rows] = values[:, width:]
-
+            part = ref[small_at : small_at + small_rows].astype(FULL) + ref[small_at + small_rows :].astype(FULL)
+            small = part if small is None else small + part
+        small_ref[...] = small
+
+    out_shape = [
+        jax.ShapeDtypeStruct((groups * head_rows, 2 * width), FULL),
+        jax.ShapeDtypeStruct((2, 2, total_blocks, width, width), FULL),
+        jax.ShapeDtypeStruct((small_rows, 2 * width), FULL),
+    ]
     return pl.pallas_call(
         body,
-        out_shape=[
-            jax.ShapeDtypeStruct((groups * head_rows, 2 * width), FULL),
-            jax.ShapeDtypeStruct((2, 2, total_blocks, width, width), FULL),
-        ],
+        grid_spec=pltpu.PrefetchScalarGridSpec(
+            num_scalar_prefetch=1,
+            grid=(1,),
+            in_specs=[whole(gathered[0].shape)] * groups,
+            out_specs=[whole(o.shape) for o in out_shape],
+        ),
+        out_shape=out_shape,
         compiler_params=params(),
         name="assembled",
-    )(gathered)
+    )(scal, *gathered)
 
 
 def route_predictions(predicted, dest_group, group_at, groups, slot_count):
@@ -729,21 +771,24 @@
     moved = [across(p) for p in pieces]
     turned_send, turned_keep = turned_patches(scal, flat_patches, groups)
     turned = [turned_keep, swap_bit(turned_send, 0, groups)]
+    moved[0], turned_keep = lax.optimization_barrier((moved[0], turned_keep))
+    turned[0] = turned_keep
     mixed, saved = [], []
     for first, values in zip(firsts, moved):
         out, rest = spectral_chunk(scal, table, factors, values, spec_w, spec_b, first)
         mixed.append(across(out))
         saved.append(rest)
-    predicted, residual, head_grads, head_sums, gathered = [], [], [], [], []
+    predicted, residual, updated, head_sums, gathered = [], [], [], [], []
     for first, mix in zip(firsts, mixed):
-        pred, res, grad, sums = head_chunk(
+        pred, res, up, sums = head_chunk(
             scal, embedded, normed, mix, flat_targets, head_w, head_b_row, first, samples, cells
         )
         predicted.append(pred)
         residual.append(res)
-        head_grads.append(grad)
+        updated.append(up)
         head_sums.append(sums[0])
         gathered.append(across([res] * shards))
+    head_grad, gathered[0] = lax.optimization_barrier((head_gradient(updated, residual), gathered[0]))
     spec_back, sums = [], None
     for first, res, rest in zip(firsts, gathered, saved):
         values, sums = spectral_back_chunk(
@@ -754,16 +799,20 @@
     width = spec_w.shape[-1]
     blocks = spec_w.shape[2] // shards
     head_rows = head_w.shape[0] // groups
-    weight_sums = sum_over_groups(sum(head_grads), spec_grad, groups)
+    weight_sums = sum_over_groups(head_grad, spec_grad, groups)
     own_grads, other_grads, row_sums = [], [], []
     for first, res, back in zip(firsts, residual, spec_back):
         grad, row_sum = embedded_back_chunk(scal, embedded, stats, res, head_w, gain_row, back, first, cells)
         own_grads.append(grad)
         other_grads.append(swap_bit(grad, 0, groups))
         row_sums.append(row_sum)
-    parts = embed_grad_parts(scal, turned, own_grads + other_grads, groups)
-    parts, weight_sums, predicted, row_sums = lax.optimization_barrier((parts, weight_sums, predicted, row_sums))
-    part = scatter_start(parts, groups)
+    grads = own_grads + other_grads
+    sent = embed_grad_parts(scal, turned, grads, groups, 1)
+    top_bit = groups.bit_length() - 2
+    received = [swap_bit(sent[0], 1, groups), swap_bit(sent[1], top_bit, groups)]
+    kept = embed_grad_parts(scal, turned, grads, groups, 0)
+    kept, weight_sums, predicted, row_sums = lax.optimization_barrier((kept, weight_sums, predicted, row_sums))
+    ends = scatter_start(received, kept, groups)
     predictions = route_predictions(
         jnp.concatenate(predicted, axis=0), dest_group, group_at, groups, slot_count
     ).reshape(targets.shape)
@@ -775,11 +824,10 @@
     small = jnp.concatenate([small[:, :own_rows].reshape(-1, outs), jnp.sum(small[:, own_rows:], axis=0)], axis=0)
     small = jnp.concatenate([small, jnp.zeros((-small.shape[0] % 16, outs), FULL)], axis=0)
     outgoing = jnp.concatenate([head_part, spec_part.reshape(-1, outs), hi_lo(small)], axis=0)
-    part, outgoing = lax.optimization_barrier((part, outgoing))
-    embed_grad = scatter_end(part, shards)
-    gathered = to_all(outgoing, "grp", groups)
-    head_grad, spec_w_grad = assembled(gathered, head_rows, shards, blocks, width)
-    small = jnp.sum(from_hi_lo(gathered[:, head_rows + shards * (2 * blocks * width // groups) :]), axis=0)
+    ends, outgoing = lax.optimization_barrier((ends, outgoing))
+    gathered = from_all_groups(outgoing, groups)
+    embed_grad = scatter_end(ends, shards, shard_at)
+    head_grad, spec_w_grad, small = assembled(scal, gathered, head_rows, shards, blocks, width)
     spec_bias_all = small[: shards * own_rows].reshape(shards, 2, blocks, 2, width)
     spec_b_grad = jnp.transpose(spec_bias_all, (1, 3, 0, 2, 4)).reshape(spec_b.shape)
     vectors = small[shards * own_rows : shards * own_rows + all_rows]

time: 227 us -> 189 us (0.83)
  Pallas kernels: 65.3 us -> 39 us
  waiting for transfers between devices: 54 us -> 32.1 us
  blocking collectives: 19.1 us -> 0 us
  local copies, waits for them, and re-layouts: 12.7 us -> 25.9 us
  starting transfers between devices: 65.2 us -> 75.7 us
  other arithmetic: 8.83 us -> 14.1 us
    all_to_all x1 -> x0, waiting for transfers between devices: 21.1 us -> none  [to_all(): lax.all_to_all(jnp.broadcast_to(values[None], (count,) + values.shape), a...]
    all_to_all x1 -> x0, blocking collectives: 19.1 us -> none  [scatter_end(): moved = lax.all_to_all(part, 'fft', split_axis=0, concat_axis=0, tiled=True)]
    unnamed x89 -> x105, local copies, waits for them, and re-layouts: 7.26 us -> 18.2 us
    ppermute x27 -> x30, starting transfers between devices: 48.9 us -> 55.6 us  [across(): lax.ppermute(pieces[k], 'fft', [(z, z ^ k) for z in range(shards)])]
    pallas_call x2, Pallas kernels: 7.91 us -> 1.83 us  [head_chunk(): pl.pallas_call(body, grid_spec=pltpu.PrefetchScalarGridSpec(num_scalar_pr...]
    pallas_call x2, Pallas kernels: 12.3 us -> 6.79 us  [spectral_back_chunk(): pl.pallas_call(body, grid_spec=pltpu.PrefetchScalarGridSpec(num_scalar_pr...]
    pallas_call x2, Pallas kernels: 7.45 us -> 2.9 us  [embedded_back_chunk(): pl.pallas_call(body, grid_spec=pltpu.PrefetchScalarGridSpec(num_scalar_pr...]
    pallas_call x2, Pallas kernels: 9.83 us -> 5.63 us  [spectral_chunk(): pl.pallas_call(body, grid_spec=pltpu.PrefetchScalarGridSpec(num_scalar_pr...]
  transfers between devices with their start and end apart: 37 -> 46, of which waited for: 13 -> 10; matrix products, arithmetic and copies ran while one was open for 4% -> 9% of each run, Pallas kernels for 23% -> 16%
where the time goes in v4:
time: 189 us; the launch traced here: 188 us
  starting transfers between devices  75.7 us (40%)
  Pallas kernels  39 us (21%)
  waiting for transfers between devices  32.1 us (17%)
  local copies, waits for them, and re-layouts  25.9 us (14%)
  other arithmetic  14.1 us (7%)
    ppermute x30, starting transfers between devices, across(): lax.ppermute(pieces[k], 'fft', [(z, z ^ k) for z in range(shards)])  55.6 us
    unnamed x105, local copies, waits for them, and re-layouts  18.2 us
    ppermute x30, waiting for transfers between devices, across(): lax.ppermute(pieces[k], 'fft', [(z, z ^ k) for z in range(shards)])  16.6 us
    ppermute x11, waiting for transfers between devices, swap_bit(): lax.ppermute(values, 'grp', [(g, g ^ 1 << bit) for g in range(groups)])  15.5 us
    pallas_call x2, Pallas kernels, embed_grad_parts(): pl.pallas_call(body, grid_spec=pltpu.PrefetchScalarGridSpec(num_scalar_pr...  8.99 us
    ppermute x11, starting transfers between devices, swap_bit(): lax.ppermute(values, 'grp', [(g, g ^ 1 << bit) for g in range(groups)])  7.91 us
    pallas_call x2, Pallas kernels, spectral_back_chunk(): pl.pallas_call(body, grid_spec=pltpu.PrefetchScalarGridSpec(num_scalar_pr...  6.79 us
    pallas_call x1, Pallas kernels, embed(): pl.pallas_call(body, grid_spec=pltpu.PrefetchScalarGridSpec(num_scalar_pr...  6.05 us
  transfers between devices with their start and end apart: 46, of which 10 were waited for; matrix products, arithmetic and copies ran while one was open for 9% of the time, Pallas kernels for 16%

profile of v4, /device:TPU:0, one launch (start us, length us, event | category | flops | bytes accessed | tf_op | source)
XLA Modules:
  0.0 188.1 jit_solution(14942427594196478074)
XLA Ops:
  1.5 1.6 copy-done.4
  3.7 2.5 %copy-done.19 = bf16[2560,1024]{1,0:T(8,128)(2,1)S(1)} copy-done((bf16[2560,1024]{1,0:T(8,128)(2,1)S(1)}, bf16[2560,1024]{1,0:T(8,128)(2,1)}, u32[]{:S(2)}) %copy-start.19) | copy-done | bytes 5242904
  6.9 6.0 %embed.1 = (bf16[384,1024]{1,0:T(8,128)(2,1)S(1)}, bf16[384,1024]{1,0:T(8,128)(2,1)S(1)}, f32[384,256]{1,0:T(8,128)S(1)}, bf16[3,64,256]{2,1,0:T(8,128)(2,1)S(1)...) custom-call(s32[15]{0:T(128)S(1)} %concatenate.33.scal_ref, ...), custom_call_target="tpu_custom_call" | custom-call | flops 2013265920 | bytes 7208960 | tf_op jit(solution)/shard_map/embed/pallas_call | solution.py:140
  14.2 3.0 %collective-permute-start = (bf16[3,64,256]{2,1,0:T(8,128)(2,1)}, bf16[3,64,256]{2,1,0:T(8,128)(2,1)S(1)}, u32[]{:S(2)}, u32[]{:S(2)}) collective-permute-start(bf16[3,64,256]{2,1,0:T(8,128)(2,1)} %get-tuple-element.87), channel_id=1, source_target_pairs={{0,1},{1,0},{2,3},{3,2},{4,5},{5,4},{6,7},{7,6},{8,9},{9,8},{10,11... | collective-permute-start | bytes 294920 | tf_op jit(solution)/shard_map/ppermute | solution.py:610
  17.2 2.6 %collective-permute-start.1 = (bf16[3,64,256]{2,1,0:T(8,128)(2,1)S(1)}, bf16[3,64,256]{2,1,0:T(8,128)(2,1)S(1)}, u32[]{:S(2)}, u32[]{:S(2)}) collective-permute-start(bf16[3,64,256]{2,1,0:T(8,128)(2,1)S(1)} %get-tuple-element.88), channel_id=1, source_target_pairs={{0,2},{1,3},{2,0},{3,1},{4,6},{5,7},{6,4},{7,5},{8,10},{9,11},{10,... | collective-permute-start | bytes 294920 | tf_op jit(solution)/shard_map/ppermute | solution.py:610
  20.7 3.5 %collective-permute-start.8 = (bf16[3,64,256]{2,1,0:T(8,128)(2,1)}, bf16[3,64,256]{2,1,0:T(8,128)(2,1)}, u32[]{:S(2)}, u32[]{:S(2)}) collective-permute-start(bf16[3,64,256]{2,1,0:T(8,128)(2,1)} %get-tuple-element.111), channel_id=1, source_target_pairs={{0,2},{1,3},{2,0},{3,1},{4,6},{5,7},{6,4},{7,5},{8,10},{9,11},{10,... | collective-permute-start | bytes 294920 | tf_op jit(solution)/shard_map/ppermute | solution.py:610
  26.2 1.5 copy-done.5
  27.7 3.9 %turned_patches.1 = (bf16[4,320,384]{2,1,0:T(8,128)(2,1)}, bf16[4,320,384]{2,1,0:T(8,128)(2,1)S(1)}) custom-call(s32[15]{0:T(128)S(1)} %concatenate.33.scal_ref, bf16[384,2560]{1,0:T(8,128)(2,1)S(1)} %bitcast.54), custom_call_target="tpu_custom_call" | custom-call | bytes 3932160 | tf_op jit(solution)/shard_map/turned_patches/pallas_call | solution.py:528
  31.6 1.4 copy-done.2
  33.1 2.3 %spectral.2 = (bf16[3,64,256]{2,1,0:T(8,128)(2,1)S(1)}, bf16[3,64,256]{2,1,0:T(8,128)(2,1)S(1)}, bf16[3,64,256]{2,1,0:T(8,128)(2,1)S(1)}, bf16[3,64,256]{2,1,0:T...) custom-call(s32[15]{0:T(128)S(1)} %concatenate.33.scal_ref, ...), custom_call_target="tpu_custom_call" | custom-call | flops 704643072 | bytes 3145728 | tf_op jit(solution)/shard_map/spectral/pallas_call | solution.py:258
  35.5 2.8 %collective-permute-start.4 = (bf16[3,64,256]{2,1,0:T(8,128)(2,1)S(1)}, bf16[3,64,256]{2,1,0:T(8,128)(2,1)S(1)}, u32[]{:S(2)}, u32[]{:S(2)}) collective-permute-start(bf16[3,64,256]{2,1,0:T(8,128)(2,1)S(1)} %get-tuple-element.101), channel_id=1, source_target_pairs={{0,1},{1,0},{2,3},{3,2},{4,5},{5,4},{6,7},{7,6},{8,9},{9,8},{10,11... | collective-permute-start | bytes 294920 | tf_op jit(solution)/shard_map/ppermute | solution.py:610
  38.3 1.6 collective-permute-start.5
  40.8 3.3 %spectral.3 = (bf16[3,64,256]{2,1,0:T(8,128)(2,1)S(1)}, bf16[3,64,256]{2,1,0:T(8,128)(2,1)S(1)}, bf16[3,64,256]{2,1,0:T(8,128)(2,1)S(1)}, bf16[3,64,256]{2,1,0:T...) custom-call(s32[15]{0:T(128)S(1)} %concatenate.33.scal_ref, ...), custom_call_target="tpu_custom_call" | custom-call | flops 704643072 | bytes 3145728 | tf_op jit(solution)/shard_map/spectral/pallas_call | solution.py:258
  45.2 2.5 %collective-permute-start.11 = (bf16[3,64,256]{2,1,0:T(8,128)(2,1)S(1)}, bf16[3,64,256]{2,1,0:T(8,128)(2,1)S(1)}, u32[]{:S(2)}, u32[]{:S(2)}) collective-permute-start(bf16[3,64,256]{2,1,0:T(8,128)(2,1)S(1)} %get-tuple-element.115), channel_id=1, source_target_pairs={{0,2},{1,3},{2,0},{3,1},{4,6},{5,7},{6,4},{7,5},{8,10},{9,11},{10,... | collective-permute-start | bytes 294920 | tf_op jit(solution)/shard_map/ppermute | solution.py:610
  50.2 2.3 %collective-permute-start.13 = (bf16[3,64,256]{2,1,0:T(8,128)(2,1)S(1)}, bf16[3,64,256]{2,1,0:T(8,128)(2,1)S(1)}, u32[]{:S(2)}, u32[]{:S(2)}) collective-permute-start(bf16[3,64,256]{2,1,0:T(8,128)(2,1)S(1)} %get-tuple-element.119.refs_2_.refs_0_.res_ref), channel_id=1, source_target_pairs={{0,1},{1,0},{2,3},{3,2},{4,5},{5,4},{6,7},{7,6},{8,9},{9,8},{10,11... | collective-permute-start | bytes 294920 | tf_op jit(solution)/shard_map/ppermute | solution.py:610
  55.3 1.5 collective-permute-done.11.refs_2_
  57.8 4.8 %collective-permute-start.19 = (bf16[3,64,256]{2,1,0:T(8,128)(2,1)S(1)}, bf16[3,64,256]{2,1,0:T(8,128)(2,1)S(1)}, u32[]{:S(2)}, u32[]{:S(2)}) collective-permute-start(bf16[3,64,256]{2,1,0:T(8,128)(2,1)S(1)} %get-tuple-element.118.refs_3_.refs_0_.res_ref), channel_id=1, source_target_pairs={{0,1},{1,0},{2,3},{3,2},{4,5},{5,4},{6,7},{7,6},{8,9},{9,8},{10,11... | collective-permute-start | bytes 294920 | tf_op jit(solution)/shard_map/ppermute | solution.py:610
  63.3 1.8 collective-permute-start.21
  65.7 3.7 %spectral_back.2 = (bf16[3,64,256]{2,1,0:T(8,128)(2,1)S(1)}, bf16[3,64,256]{2,1,0:T(8,128)(2,1)}, bf16[3,64,256]{2,1,0:T(8,128)(2,1)}, bf16[3,64,256]{2,1,0:T(8,...) custom-call(s32[15]{0:T(128)S(1)} %concatenate.33.scal_ref, bf16[3,512,256]{2,1,0:T(8,128)(2,1)S(1)} %copy-done.3, ...), custom_call_target="tpu_custom_call" | custom-call | flops 1006632960 | bytes 3145728 | tf_op jit(solution)/shard_map/spectral_back/pallas_call | solution.py:421
  69.4 2.3 %collective-permute-start.16 = (bf16[3,64,256]{2,1,0:T(8,128)(2,1)}, bf16[3,64,256]{2,1,0:T(8,128)(2,1)S(1)}, u32[]{:S(2)}, u32[]{:S(2)}) collective-permute-start(bf16[3,64,256]{2,1,0:T(8,128)(2,1)} %get-tuple-element.124), channel_id=1, source_target_pairs={{0,1},{1,0},{2,3},{3,2},{4,5},{5,4},{6,7},{7,6},{8,9},{9,8},{10,11... | collective-permute-start | bytes 294920 | tf_op jit(solution)/shard_map/ppermute | solution.py:610
  71.7 2.8 %collective-permute-start.17 = (bf16[3,64,256]{2,1,0:T(8,128)(2,1)}, bf16[3,64,256]{2,1,0:T(8,128)(2,1)S(1)}, u32[]{:S(2)}, u32[]{:S(2)}) collective-permute-start(bf16[3,64,256]{2,1,0:T(8,128)(2,1)} %get-tuple-element.125), channel_id=1, source_target_pairs={{0,2},{1,3},{2,0},{3,1},{4,6},{5,7},{6,4},{7,5},{8,10},{9,11},{10,... | collective-permute-start | bytes 294920 | tf_op jit(solution)/shard_map/ppermute | solution.py:610
  74.5 3.1 %spectral_back.3 = (bf16[3,64,256]{2,1,0:T(8,128)(2,1)S(1)}, bf16[3,64,256]{2,1,0:T(8,128)(2,1)S(1)}, bf16[3,64,256]{2,1,0:T(8,128)(2,1)S(1)}, bf16[3,64,256]{2,...) custom-call(s32[15]{0:T(128)S(1)} %concatenate.33.scal_ref, ...), custom_call_target="tpu_custom_call" | custom-call | flops 1006632960 | bytes 3145728 | tf_op jit(solution)/shard_map/spectral_back/pallas_call | solution.py:421
  79.9 4.6 %all-to-all-start = ((bf16[8,192,256]{2,1,0:T(8,128)(2,1)}), bf16[8,192,256]{2,1,0:T(8,128)(2,1)}, u32[]{:S(2)}, u32[]{:S(2)}) async-start(bf16[8,192,256]{2,1,0:T(8,128)(2,1)} %pad_maximum_fusion), calls=%async_computation | async-start | bytes 1572864 | tf_op jit(solution)/shard_map/all_to_all | solution.py:673
  84.6 1.4 collective-permute-start.18
  86.6 2.4 %collective-permute-start.23 = (bf16[3,64,256]{2,1,0:T(8,128)(2,1)S(1)}, bf16[3,64,256]{2,1,0:T(8,128)(2,1)S(1)}, u32[]{:S(2)}, u32[]{:S(2)}) collective-permute-start(bf16[3,64,256]{2,1,0:T(8,128)(2,1)S(1)} %copy-done.36), channel_id=1, source_target_pairs={{0,2},{1,3},{2,0},{3,1},{4,6},{5,7},{6,4},{7,5},{8,10},{9,11},{10,... | collective-permute-start | bytes 294920 | tf_op jit(solution)/shard_map/ppermute | solution.py:610
  90.4 1.7 collective-permute-done.18.refs_3_
  92.1 1.5 embedded_back.2
  93.7 6.1 %collective-permute-done.23.refs_2_ = bf16[3,64,256]{2,1,0:T(8,128)(2,1)S(1)} collective-permute-done((bf16[3,64,256]{2,1,0:T(8,128)(2,1)S(1)}, bf16[3,64,256]{2,1,0:T(8,128)(2,1)S(1)}, u32[]{:S(2)}, u32[]{:S(2)}) %collective-permute-start.23) | collective-permute-done | bytes 98336 | tf_op jit(solution)/shard_map/ppermute | solution.py:610
  99.8 1.4 embedded_back.3
  103.0 4.1 %embed_grad.2 = (bf16[2,320,512]{2,1,0:T(8,128)(2,1)S(1)}, bf16[2,320,512]{2,1,0:T(8,128)(2,1)S(1)}) custom-call(s32[15]{0:T(128)S(1)} %concatenate.33.scal_ref, bf16[4,320,384]{2,1,0:T(8,128)(2,1)S(1)} %copy-done.21, bf16[4,320,384]{2,1,0:T(8,128)(2,1)} %collective-permute-done.3.refs_1_, bf16[192,1024]{1,0:T(8,128)(2,1)S(1)} %get-tuple-element.127.refs_2_, ...), custom_call_target="tpu_custom_call" | custom-call | flops 1006632960 | bytes 4063232 | tf_op jit(solution)/shard_map/embed_grad/pallas_call | solution.py:576
  112.7 2.5 %collective-permute-start.32 = (bf16[224,256]{1,0:T(8,128)(2,1)}, bf16[224,256]{1,0:T(8,128)(2,1)}, u32[]{:S(2)}, u32[]{:S(2)}) collective-permute-start(bf16[224,256]{1,0:T(8,128)(2,1)} %pad_maximum_fusion.7), channel_id=1, source_target_pairs={{0,2},{1,3},{2,0},{3,1},{4,6},{5,7},{6,4},{7,5},{8,10},{9,11},{10,... | collective-permute-start | bytes 344072 | tf_op jit(solution)/shard_map/ppermute | solution.py:610
  117.5 4.1 %all-to-all-start.1 = ((bf16[8,64,256]{2,1,0:T(8,128)(2,1)}), bf16[8,64,256]{2,1,0:T(8,128)(2,1)}, u32[]{:S(2)}, u32[]{:S(2)}) async-start(bf16[8,64,256]{2,1,0:T(8,128)(2,1)} %broadcast_select_fusion), calls=%async_computation.1 | async-start | bytes 524288 | tf_op jit(solution)/shard_map/all_to_all | solution.py:735
  124.6 4.9 %embed_grad.3 = (bf16[2,320,512]{2,1,0:T(8,128)(2,1)}, bf16[2,320,512]{2,1,0:T(8,128)(2,1)S(1)}) custom-call(s32[15]{0:T(128)S(1)} %concatenate.33.scal_ref, bf16[4,320,384]{2,1,0:T(8,128)(2,1)S(1)} %copy-done.22, bf16[4,320,384]{2,1,0:T(8,128)(2,1)} %collective-permute-done.3.refs_1_, bf16[192,1024]{1,0:T(8,128)(2,1)S(1)} %copy-done.24, ...), custom_call_target="tpu_custom_call" | custom-call | flops 1006632960 | bytes 4063232 | tf_op jit(solution)/shard_map/embed_grad/pallas_call | solution.py:576
  129.5 1.9 %collective-permute-start.27 = (bf16[2,320,512]{2,1,0:T(8,128)(2,1)}, bf16[2,320,512]{2,1,0:T(8,128)(2,1)}, u32[]{:S(2)}, u32[]{:S(2)}) collective-permute-start(bf16[2,320,512]{2,1,0:T(8,128)(2,1)} %get-tuple-element.149), channel_id=1, source_target_pairs={{0,8},{4,12},{8,0},{12,4},{16,24},{20,28},{24,16},{28,20},{1,9},{5... | collective-permute-start | bytes 1966088 | tf_op jit(solution)/shard_map/ppermute | solution.py:604
  131.3 1.5 collective-permute-start.29
  137.9 8.8 %collective-permute-done.27 = bf16[2,320,512]{2,1,0:T(8,128)(2,1)} collective-permute-done((bf16[2,320,512]{2,1,0:T(8,128)(2,1)}, bf16[2,320,512]{2,1,0:T(8,128)(2,1)}, u32[]{:S(2)}, u32[]{:S(2)}) %collective-permute-start.27) | collective-permute-done | bytes 655392 | tf_op jit(solution)/shard_map/ppermute | solution.py:604
  148.1 1.8 collective-permute-start.28
  151.2 1.5 collective-permute-start.30
  152.8 1.5 gather_fusion.1
  154.3 3.0 %collective-permute-done.28 = bf16[1,320,512]{2,1,0:T(8,128)(2,1)S(1)} collective-permute-done((bf16[1,320,512]{2,1,0:T(8,128)(2,1)S(1)}, bf16[1,320,512]{2,1,0:T(8,128)(2,1)S(1)}, u32[]{:S(2)}, u32[]{:S(2)}) %collective-permute-start.28) | collective-permute-done | bytes 327712 | tf_op jit(solution)/shard_map/ppermute | solution.py:604
  157.4 2.6 %collective-permute-done.30 = bf16[1,320,512]{2,1,0:T(8,128)(2,1)} collective-permute-done((bf16[1,320,512]{2,1,0:T(8,128)(2,1)S(1)}, bf16[1,320,512]{2,1,0:T(8,128)(2,1)}, u32[]{:S(2)}, u32[]{:S(2)}) %collective-permute-start.30) | collective-permute-done | bytes 327712 | tf_op jit(solution)/shard_map/ppermute | solution.py:604
  161.1 1.5 collective-permute-start.38
  163.2 1.5 collective-permute-start.42
  166.0 1.6 collective-permute-start.35
  167.6 4.3 %collective-permute-done.36 = bf16[80,1024]{1,0:T(8,128)(2,1)S(1)} collective-permute-done((bf16[80,1024]{1,0:T(8,128)(2,1)S(1)}, bf16[80,1024]{1,0:T(8,128)(2,1)S(1)}, u32[]{:S(2)}, u32[]{:S(2)}) %collective-permute-start.36) | collective-permute-done | bytes 163872 | tf_op jit(solution)/shard_map/ppermute | solution.py:610
  172.0 5.8 %collective-permute-start.34 = (bf16[80,1024]{1,0:T(8,128)(2,1)S(1)}, bf16[80,1024]{1,0:T(8,128)(2,1)S(1)}, u32[]{:S(2)}, u32[]{:S(2)}) collective-permute-start(bf16[80,1024]{1,0:T(8,128)(2,1)S(1)} %pad_maximum_fusion.4), channel_id=1, source_target_pairs={{0,1},{1,0},{2,3},{3,2},{4,5},{5,4},{6,7},{7,6},{8,9},{9,8},{10,11... | collective-permute-start | bytes 491528 | tf_op jit(solution)/shard_map/ppermute | solution.py:610
  180.6 1.9 %collective-permute-done.34 = bf16[80,1024]{1,0:T(8,128)(2,1)S(1)} collective-permute-done((bf16[80,1024]{1,0:T(8,128)(2,1)S(1)}, bf16[80,1024]{1,0:T(8,128)(2,1)S(1)}, u32[]{:S(2)}, u32[]{:S(2)}) %collective-permute-start.34) | collective-permute-done | bytes 163872 | tf_op jit(solution)/shard_map/ppermute | solution.py:610
  183.3 2.5 %assembled.1 = (f32[1024,256]{1,0:T(8,128)}, f32[2,2,8,128,128]{4,3,2,1,0:T(8,128)}, f32[32,256]{1,0:T(8,128)S(1)}) custom-call(s32[15]{0:T(128)S(1)} %concatenate.33.scal_ref, bf16[448,256]{1,0:T(8,128)(2,1)S(1)} %pad_maximum_fusion.1.refs_0_, bf16[448,256]{1,0:T(8,128)(2,1)S(1)} %collective-permute-done.37.refs_1_, ...), custom_call_target="tpu_custom_call" | custom-call | tf_op jit(solution)/shard_map/assembled/pallas_call | solution.py:716
  (233 shorter events, 49.6 us)
Async XLA Ops:
  6.9 24.7 %copy-start.38 = (f32[2,2,8,128]{3,2,1,0:T(8,128)S(1)}, f32[2,2,8,128]{3,2,1,0:T(8,128)}, u32[]{:S(2)}) copy-start(f32[2,2,8,128]{3,2,1,0:T(8,128)} %b_ref.3) | copy-start | bytes 49156
  14.2 11.3 %collective-permute-start = (bf16[3,64,256]{2,1,0:T(8,128)(2,1)}, bf16[3,64,256]{2,1,0:T(8,128)(2,1)S(1)}, u32[]{:S(2)}, u32[]{:S(2)}) collective-permute-start(bf16[3,64,256]{2,1,0:T(8,128)(2,1)} %get-tuple-element.87), channel_id=1, source_target_pairs={{0,1},{1,0},{2,3},{3,2},{4,5},{5,4},{6,7},{7,6},{8,9},{9,8},{10,11... | collective-permute-start | bytes 294920 | tf_op jit(solution)/shard_map/ppermute | solution.py:610
  17.2 14.4 %collective-permute-start.1 = (bf16[3,64,256]{2,1,0:T(8,128)(2,1)S(1)}, bf16[3,64,256]{2,1,0:T(8,128)(2,1)S(1)}, u32[]{:S(2)}, u32[]{:S(2)}) collective-permute-start(bf16[3,64,256]{2,1,0:T(8,128)(2,1)S(1)} %get-tuple-element.88), channel_id=1, source_target_pairs={{0,2},{1,3},{2,0},{3,1},{4,6},{5,7},{6,4},{7,5},{8,10},{9,11},{10,... | collective-permute-start | bytes 294920 | tf_op jit(solution)/shard_map/ppermute | solution.py:610
  19.8 11.8 %collective-permute-start.2 = (bf16[3,64,256]{2,1,0:T(8,128)(2,1)S(1)}, bf16[3,64,256]{2,1,0:T(8,128)(2,1)S(1)}, u32[]{:S(2)}, u32[]{:S(2)}) collective-permute-start(bf16[3,64,256]{2,1,0:T(8,128)(2,1)S(1)} %get-tuple-element.89), channel_id=1, source_target_pairs={{0,3},{1,2},{2,1},{3,0},{4,7},{5,6},{6,5},{7,4},{8,11},{9,10},{10,... | collective-permute-start | bytes 294920 | tf_op jit(solution)/shard_map/ppermute | solution.py:610
  19.8 20.1 %collective-permute-start.7 = (bf16[3,64,256]{2,1,0:T(8,128)(2,1)}, bf16[3,64,256]{2,1,0:T(8,128)(2,1)}, u32[]{:S(2)}, u32[]{:S(2)}) collective-permute-start(bf16[3,64,256]{2,1,0:T(8,128)(2,1)} %get-tuple-element.110), channel_id=1, source_target_pairs={{0,1},{1,0},{2,3},{3,2},{4,5},{5,4},{6,7},{7,6},{8,9},{9,8},{10,11... | collective-permute-start | bytes 294920 | tf_op jit(solution)/shard_map/ppermute | solution.py:610
  20.7 20.1 %collective-permute-start.8 = (bf16[3,64,256]{2,1,0:T(8,128)(2,1)}, bf16[3,64,256]{2,1,0:T(8,128)(2,1)}, u32[]{:S(2)}, u32[]{:S(2)}) collective-permute-start(bf16[3,64,256]{2,1,0:T(8,128)(2,1)} %get-tuple-element.111), channel_id=1, source_target_pairs={{0,2},{1,3},{2,0},{3,1},{4,6},{5,7},{6,4},{7,5},{8,10},{9,11},{10,... | collective-permute-start | bytes 294920 | tf_op jit(solution)/shard_map/ppermute | solution.py:610
  25.5 15.3 %collective-permute-start.9 = (bf16[3,64,256]{2,1,0:T(8,128)(2,1)}, bf16[3,64,256]{2,1,0:T(8,128)(2,1)S(1)}, u32[]{:S(2)}, u32[]{:S(2)}) collective-permute-start(bf16[3,64,256]{2,1,0:T(8,128)(2,1)} %get-tuple-element.112), channel_id=1, source_target_pairs={{0,3},{1,2},{2,1},{3,0},{4,7},{5,6},{6,5},{7,4},{8,11},{9,10},{10,... | collective-permute-start | bytes 294920 | tf_op jit(solution)/shard_map/ppermute | solution.py:610
  35.5 12.2 %collective-permute-start.4 = (bf16[3,64,256]{2,1,0:T(8,128)(2,1)S(1)}, bf16[3,64,256]{2,1,0:T(8,128)(2,1)S(1)}, u32[]{:S(2)}, u32[]{:S(2)}) collective-permute-start(bf16[3,64,256]{2,1,0:T(8,128)(2,1)S(1)} %get-tuple-element.101), channel_id=1, source_target_pairs={{0,1},{1,0},{2,3},{3,2},{4,5},{5,4},{6,7},{7,6},{8,9},{9,8},{10,11... | collective-permute-start | bytes 294920 | tf_op jit(solution)/shard_map/ppermute | solution.py:610
  38.3 10.3 %collective-permute-start.5 = (bf16[3,64,256]{2,1,0:T(8,128)(2,1)S(1)}, bf16[3,64,256]{2,1,0:T(8,128)(2,1)S(1)}, u32[]{:S(2)}, u32[]{:S(2)}) collective-permute-start(bf16[3,64,256]{2,1,0:T(8,128)(2,1)S(1)} %get-tuple-element.102), channel_id=1, source_target_pairs={{0,2},{1,3},{2,0},{3,1},{4,6},{5,7},{6,4},{7,5},{8,10},{9,11},{10,... | collective-permute-start | bytes 294920 | tf_op jit(solution)/shard_map/ppermute | solution.py:610
  39.9 8.6 %collective-permute-start.6 = (bf16[3,64,256]{2,1,0:T(8,128)(2,1)S(1)}, bf16[3,64,256]{2,1,0:T(8,128)(2,1)S(1)}, u32[]{:S(2)}, u32[]{:S(2)}) collective-permute-start(bf16[3,64,256]{2,1,0:T(8,128)(2,1)S(1)} %get-tuple-element.103), channel_id=1, source_target_pairs={{0,3},{1,2},{2,1},{3,0},{4,7},{5,6},{6,5},{7,4},{8,11},{9,10},{10,... | collective-permute-start | bytes 294920 | tf_op jit(solution)/shard_map/ppermute | solution.py:610
  44.1 9.6 %collective-permute-start.10 = (bf16[3,64,256]{2,1,0:T(8,128)(2,1)S(1)}, bf16[3,64,256]{2,1,0:T(8,128)(2,1)S(1)}, u32[]{:S(2)}, u32[]{:S(2)}) collective-permute-start(bf16[3,64,256]{2,1,0:T(8,128)(2,1)S(1)} %get-tuple-element.114), channel_id=1, source_target_pairs={{0,1},{1,0},{2,3},{3,2},{4,5},{5,4},{6,7},{7,6},{8,9},{9,8},{10,11... | collective-permute-start | bytes 294920 | tf_op jit(solution)/shard_map/ppermute | solution.py:610
  45.2 11.7 %collective-permute-start.11 = (bf16[3,64,256]{2,1,0:T(8,128)(2,1)S(1)}, bf16[3,64,256]{2,1,0:T(8,128)(2,1)S(1)}, u32[]{:S(2)}, u32[]{:S(2)}) collective-permute-start(bf16[3,64,256]{2,1,0:T(8,128)(2,1)S(1)} %get-tuple-element.115), channel_id=1, source_target_pairs={{0,2},{1,3},{2,0},{3,1},{4,6},{5,7},{6,4},{7,5},{8,10},{9,11},{10,... | collective-permute-start | bytes 294920 | tf_op jit(solution)/shard_map/ppermute | solution.py:610
  47.7 9.1 %collective-permute-start.12 = (bf16[3,64,256]{2,1,0:T(8,128)(2,1)S(1)}, bf16[3,64,256]{2,1,0:T(8,128)(2,1)S(1)}, u32[]{:S(2)}, u32[]{:S(2)}) collective-permute-start(bf16[3,64,256]{2,1,0:T(8,128)(2,1)S(1)} %get-tuple-element.116), channel_id=1, source_target_pairs={{0,3},{1,2},{2,1},{3,0},{4,7},{5,6},{6,5},{7,4},{8,11},{9,10},{10,... | collective-permute-start | bytes 294920 | tf_op jit(solution)/shard_map/ppermute | solution.py:610
  50.2 13.1 %collective-permute-start.13 = (bf16[3,64,256]{2,1,0:T(8,128)(2,1)S(1)}, bf16[3,64,256]{2,1,0:T(8,128)(2,1)S(1)}, u32[]{:S(2)}, u32[]{:S(2)}) collective-permute-start(bf16[3,64,256]{2,1,0:T(8,128)(2,1)S(1)} %get-tuple-element.119.refs_2_.refs_0_.res_ref), channel_id=1, source_target_pairs={{0,1},{1,0},{2,3},{3,2},{4,5},{5,4},{6,7},{7,6},{8,9},{9,8},{10,11... | collective-permute-start | bytes 294920 | tf_op jit(solution)/shard_map/ppermute | solution.py:610
  52.4 13.2 %collective-permute-start.14 = (bf16[3,64,256]{2,1,0:T(8,128)(2,1)S(1)}, bf16[3,64,256]{2,1,0:T(8,128)(2,1)S(1)}, u32[]{:S(2)}, u32[]{:S(2)}) collective-permute-start(bf16[3,64,256]{2,1,0:T(8,128)(2,1)S(1)} %get-tuple-element.119.refs_2_.refs_0_.res_ref), channel_id=1, source_target_pairs={{0,2},{1,3},{2,0},{3,1},{4,6},{5,7},{6,4},{7,5},{8,10},{9,11},{10,... | collective-permute-start | bytes 294920 | tf_op jit(solution)/shard_map/ppermute | solution.py:610
  53.7 12.0 %collective-permute-start.15 = (bf16[3,64,256]{2,1,0:T(8,128)(2,1)S(1)}, bf16[3,64,256]{2,1,0:T(8,128)(2,1)S(1)}, u32[]{:S(2)}, u32[]{:S(2)}) collective-permute-start(bf16[3,64,256]{2,1,0:T(8,128)(2,1)S(1)} %get-tuple-element.119.refs_2_.refs_0_.res_ref), channel_id=1, source_target_pairs={{0,3},{1,2},{2,1},{3,0},{4,7},{5,6},{6,5},{7,4},{8,11},{9,10},{10,... | collective-permute-start | bytes 294920 | tf_op jit(solution)/shard_map/ppermute | solution.py:610
  57.8 13.9 %collective-permute-start.19 = (bf16[3,64,256]{2,1,0:T(8,128)(2,1)S(1)}, bf16[3,64,256]{2,1,0:T(8,128)(2,1)S(1)}, u32[]{:S(2)}, u32[]{:S(2)}) collective-permute-start(bf16[3,64,256]{2,1,0:T(8,128)(2,1)S(1)} %get-tuple-element.118.refs_3_.refs_0_.res_ref), channel_id=1, source_target_pairs={{0,1},{1,0},{2,3},{3,2},{4,5},{5,4},{6,7},{7,6},{8,9},{9,8},{10,11... | collective-permute-start | bytes 294920 | tf_op jit(solution)/shard_map/ppermute | solution.py:610
  62.6 11.9 %collective-permute-start.20 = (bf16[3,64,256]{2,1,0:T(8,128)(2,1)S(1)}, bf16[3,64,256]{2,1,0:T(8,128)(2,1)S(1)}, u32[]{:S(2)}, u32[]{:S(2)}) collective-permute-start(bf16[3,64,256]{2,1,0:T(8,128)(2,1)S(1)} %get-tuple-element.118.refs_3_.refs_0_.res_ref), channel_id=1, source_target_pairs={{0,2},{1,3},{2,0},{3,1},{4,6},{5,7},{6,4},{7,5},{8,10},{9,11},{10,... | collective-permute-start | bytes 294920 | tf_op jit(solution)/shard_map/ppermute | solution.py:610
  63.3 11.2 %collective-permute-start.21 = (bf16[3,64,256]{2,1,0:T(8,128)(2,1)S(1)}, bf16[3,64,256]{2,1,0:T(8,128)(2,1)S(1)}, u32[]{:S(2)}, u32[]{:S(2)}) collective-permute-start(bf16[3,64,256]{2,1,0:T(8,128)(2,1)S(1)} %get-tuple-element.118.refs_3_.refs_0_.res_ref), channel_id=1, source_target_pairs={{0,3},{1,2},{2,1},{3,0},{4,7},{5,6},{6,5},{7,4},{8,11},{9,10},{10,... | collective-permute-start | bytes 294920 | tf_op jit(solution)/shard_map/ppermute | solution.py:610
  65.6 37.4 %collective-permute-start.3 = (bf16[4,320,384]{2,1,0:T(8,128)(2,1)}, bf16[4,320,384]{2,1,0:T(8,128)(2,1)}, u32[]{:S(2)}, u32[]{:S(2)}) collective-permute-start(bf16[4,320,384]{2,1,0:T(8,128)(2,1)} %get-tuple-element.92), channel_id=1, source_target_pairs={{0,4},{4,0},{8,12},{12,8},{16,20},{20,16},{24,28},{28,24},{1,5},{5... | collective-permute-start | bytes 2949128 | tf_op jit(solution)/shard_map/ppermute | solution.py:604
  69.4 17.2 %collective-permute-start.16 = (bf16[3,64,256]{2,1,0:T(8,128)(2,1)}, bf16[3,64,256]{2,1,0:T(8,128)(2,1)S(1)}, u32[]{:S(2)}, u32[]{:S(2)}) collective-permute-start(bf16[3,64,256]{2,1,0:T(8,128)(2,1)} %get-tuple-element.124), channel_id=1, source_target_pairs={{0,1},{1,0},{2,3},{3,2},{4,5},{5,4},{6,7},{7,6},{8,9},{9,8},{10,11... | collective-permute-start | bytes 294920 | tf_op jit(solution)/shard_map/ppermute | solution.py:610
  71.7 17.3 %collective-permute-start.17 = (bf16[3,64,256]{2,1,0:T(8,128)(2,1)}, bf16[3,64,256]{2,1,0:T(8,128)(2,1)S(1)}, u32[]{:S(2)}, u32[]{:S(2)}) collective-permute-start(bf16[3,64,256]{2,1,0:T(8,128)(2,1)} %get-tuple-element.125), channel_id=1, source_target_pairs={{0,2},{1,3},{2,0},{3,1},{4,6},{5,7},{6,4},{7,5},{8,10},{9,11},{10,... | collective-permute-start | bytes 294920 | tf_op jit(solution)/shard_map/ppermute | solution.py:610
  79.9 19.9 %copy-start.9 = (bf16[3,64,256]{2,1,0:T(8,128)(2,1)S(1)}, bf16[3,64,256]{2,1,0:T(8,128)(2,1)}, u32[]{:S(2)}) copy-start(bf16[3,64,256]{2,1,0:T(8,128)(2,1)} %copy-done.8) | copy-start | bytes 294916
  79.9 29.5 %all-to-all-start = ((bf16[8,192,256]{2,1,0:T(8,128)(2,1)}), bf16[8,192,256]{2,1,0:T(8,128)(2,1)}, u32[]{:S(2)}, u32[]{:S(2)}) async-start(bf16[8,192,256]{2,1,0:T(8,128)(2,1)} %pad_maximum_fusion), calls=%async_computation | async-start | bytes 1572864 | tf_op jit(solution)/shard_map/all_to_all | solution.py:673
  84.6 7.5 %collective-permute-start.18 = (bf16[3,64,256]{2,1,0:T(8,128)(2,1)S(1)}, bf16[3,64,256]{2,1,0:T(8,128)(2,1)S(1)}, u32[]{:S(2)}, u32[]{:S(2)}) collective-permute-start(bf16[3,64,256]{2,1,0:T(8,128)(2,1)S(1)} %copy-done.32), channel_id=1, source_target_pairs={{0,3},{1,2},{2,1},{3,0},{4,7},{5,6},{6,5},{7,4},{8,11},{9,10},{10,... | collective-permute-start | bytes 294920 | tf_op jit(solution)/shard_map/ppermute | solution.py:610
  86.0 7.7 %collective-permute-start.22 = (bf16[3,64,256]{2,1,0:T(8,128)(2,1)}, bf16[3,64,256]{2,1,0:T(8,128)(2,1)S(1)}, u32[]{:S(2)}, u32[]{:S(2)}) collective-permute-start(bf16[3,64,256]{2,1,0:T(8,128)(2,1)} %copy-done.37), channel_id=1, source_target_pairs={{0,1},{1,0},{2,3},{3,2},{4,5},{5,4},{6,7},{7,6},{8,9},{9,8},{10,11... | collective-permute-start | bytes 294920 | tf_op jit(solution)/shard_map/ppermute | solution.py:610
  86.6 13.1 %collective-permute-start.23 = (bf16[3,64,256]{2,1,0:T(8,128)(2,1)S(1)}, bf16[3,64,256]{2,1,0:T(8,128)(2,1)S(1)}, u32[]{:S(2)}, u32[]{:S(2)}) collective-permute-start(bf16[3,64,256]{2,1,0:T(8,128)(2,1)S(1)} %copy-done.36), channel_id=1, source_target_pairs={{0,2},{1,3},{2,0},{3,1},{4,6},{5,7},{6,4},{7,5},{8,10},{9,11},{10,... | collective-permute-start | bytes 294920 | tf_op jit(solution)/shard_map/ppermute | solution.py:610
  89.0 10.7 %collective-permute-start.24 = (bf16[3,64,256]{2,1,0:T(8,128)(2,1)S(1)}, bf16[3,64,256]{2,1,0:T(8,128)(2,1)S(1)}, u32[]{:S(2)}, u32[]{:S(2)}) collective-permute-start(bf16[3,64,256]{2,1,0:T(8,128)(2,1)S(1)} %copy-done.34), channel_id=1, source_target_pairs={{0,3},{1,2},{2,1},{3,0},{4,7},{5,6},{6,5},{7,4},{8,11},{9,10},{10,... | collective-permute-start | bytes 294920 | tf_op jit(solution)/shard_map/ppermute | solution.py:610
  93.6 8.4 %collective-permute-start.25 = (bf16[192,1024]{1,0:T(8,128)(2,1)S(1)}, bf16[192,1024]{1,0:T(8,128)(2,1)S(1)}, u32[]{:S(2)}, u32[]{:S(2)}) collective-permute-start(bf16[192,1024]{1,0:T(8,128)(2,1)S(1)} %get-tuple-element.127.refs_2_), channel_id=1, source_target_pairs={{0,4},{4,0},{8,12},{12,8},{16,20},{20,16},{24,28},{28,24},{1,5},{5... | collective-permute-start | bytes 1179656 | tf_op jit(solution)/shard_map/ppermute | solution.py:604
  101.2 1.8 collective-permute-start.26
  111.6 22.1 %collective-permute-start.33 = (bf16[224,256]{1,0:T(8,128)(2,1)}, bf16[224,256]{1,0:T(8,128)(2,1)}, u32[]{:S(2)}, u32[]{:S(2)}) collective-permute-start(bf16[224,256]{1,0:T(8,128)(2,1)} %pad_maximum_fusion.7), channel_id=1, source_target_pairs={{0,3},{1,2},{2,1},{3,0},{4,7},{5,6},{6,5},{7,4},{8,11},{9,10},{10,... | collective-permute-start | bytes 344072 | tf_op jit(solution)/shard_map/ppermute | solution.py:610
  112.7 21.7 %collective-permute-start.32 = (bf16[224,256]{1,0:T(8,128)(2,1)}, bf16[224,256]{1,0:T(8,128)(2,1)}, u32[]{:S(2)}, u32[]{:S(2)}) collective-permute-start(bf16[224,256]{1,0:T(8,128)(2,1)} %pad_maximum_fusion.7), channel_id=1, source_target_pairs={{0,2},{1,3},{2,0},{3,1},{4,6},{5,7},{6,4},{7,5},{8,10},{9,11},{10,... | collective-permute-start | bytes 344072 | tf_op jit(solution)/shard_map/ppermute | solution.py:610
  115.2 20.0 %collective-permute-start.31 = (bf16[224,256]{1,0:T(8,128)(2,1)}, bf16[224,256]{1,0:T(8,128)(2,1)}, u32[]{:S(2)}, u32[]{:S(2)}) collective-permute-start(bf16[224,256]{1,0:T(8,128)(2,1)} %pad_maximum_fusion.7), channel_id=1, source_target_pairs={{0,1},{1,0},{2,3},{3,2},{4,5},{5,4},{6,7},{7,6},{8,9},{9,8},{10,11... | collective-permute-start | bytes 344072 | tf_op jit(solution)/shard_map/ppermute | solution.py:610
  117.5 35.3 %all-to-all-start.1 = ((bf16[8,64,256]{2,1,0:T(8,128)(2,1)}), bf16[8,64,256]{2,1,0:T(8,128)(2,1)}, u32[]{:S(2)}, u32[]{:S(2)}) async-start(bf16[8,64,256]{2,1,0:T(8,128)(2,1)} %broadcast_select_fusion), calls=%async_computation.1 | async-start | bytes 524288 | tf_op jit(solution)/shard_map/all_to_all | solution.py:735
  129.5 17.3 %collective-permute-start.27 = (bf16[2,320,512]{2,1,0:T(8,128)(2,1)}, bf16[2,320,512]{2,1,0:T(8,128)(2,1)}, u32[]{:S(2)}, u32[]{:S(2)}) collective-permute-start(bf16[2,320,512]{2,1,0:T(8,128)(2,1)} %get-tuple-element.149), channel_id=1, source_target_pairs={{0,8},{4,12},{8,0},{12,4},{16,24},{20,28},{24,16},{28,20},{1,9},{5... | collective-permute-start | bytes 1966088 | tf_op jit(solution)/shard_map/ppermute | solution.py:604
  131.3 18.5 %collective-permute-start.29 = (bf16[2,320,512]{2,1,0:T(8,128)(2,1)S(1)}, bf16[2,320,512]{2,1,0:T(8,128)(2,1)}, u32[]{:S(2)}, u32[]{:S(2)}) collective-permute-start(bf16[2,320,512]{2,1,0:T(8,128)(2,1)S(1)} %get-tuple-element.151), channel_id=1, source_target_pairs={{0,16},{4,20},{8,24},{12,28},{16,0},{20,4},{24,8},{28,12},{1,17},{... | collective-permute-start | bytes 1966088 | tf_op jit(solution)/shard_map/ppermute | solution.py:604
  148.1 9.2 %collective-permute-start.28 = (bf16[1,320,512]{2,1,0:T(8,128)(2,1)S(1)}, bf16[1,320,512]{2,1,0:T(8,128)(2,1)S(1)}, u32[]{:S(2)}, u32[]{:S(2)}) collective-permute-start(bf16[1,320,512]{2,1,0:T(8,128)(2,1)S(1)} %slice_bitcast_fusion), channel_id=1, source_target_pairs={{0,16},{4,20},{8,24},{12,28},{16,0},{20,4},{24,8},{28,12},{1,17},{... | collective-permute-start | bytes 983048 | tf_op jit(solution)/shard_map/ppermute | solution.py:604
  151.2 8.8 %collective-permute-start.30 = (bf16[1,320,512]{2,1,0:T(8,128)(2,1)S(1)}, bf16[1,320,512]{2,1,0:T(8,128)(2,1)}, u32[]{:S(2)}, u32[]{:S(2)}) collective-permute-start(bf16[1,320,512]{2,1,0:T(8,128)(2,1)S(1)} %slice.119), channel_id=1, source_target_pairs={{0,8},{4,12},{8,0},{12,4},{16,24},{20,28},{24,16},{28,20},{1,9},{5... | collective-permute-start | bytes 983048 | tf_op jit(solution)/shard_map/ppermute | solution.py:604
  161.1 18.4 %collective-permute-start.38 = (bf16[448,256]{1,0:T(8,128)(2,1)S(1)}, bf16[448,256]{1,0:T(8,128)(2,1)S(1)}, u32[]{:S(2)}, u32[]{:S(2)}) collective-permute-start(bf16[448,256]{1,0:T(8,128)(2,1)S(1)} %pad_maximum_fusion.1.refs_0_), channel_id=1, source_target_pairs={{0,8},{4,12},{8,0},{12,4},{16,24},{20,28},{24,16},{28,20},{1,9},{5... | collective-permute-start | bytes 688136 | tf_op jit(solution)/shard_map/ppermute | solution.py:651
  162.7 17.4 %collective-permute-start.40 = (bf16[448,256]{1,0:T(8,128)(2,1)S(1)}, bf16[448,256]{1,0:T(8,128)(2,1)S(1)}, u32[]{:S(2)}, u32[]{:S(2)}) collective-permute-start(bf16[448,256]{1,0:T(8,128)(2,1)S(1)} %pad_maximum_fusion.1.refs_0_), channel_id=1, source_target_pairs={{0,16},{4,20},{8,24},{12,28},{16,0},{20,4},{24,8},{28,12},{1,17},{... | collective-permute-start | bytes 688136 | tf_op jit(solution)/shard_map/ppermute | solution.py:651
  163.2 16.9 %collective-permute-start.42 = (bf16[448,256]{1,0:T(8,128)(2,1)S(1)}, bf16[448,256]{1,0:T(8,128)(2,1)S(1)}, u32[]{:S(2)}, u32[]{:S(2)}) collective-permute-start(bf16[448,256]{1,0:T(8,128)(2,1)S(1)} %pad_maximum_fusion.1.refs_0_), channel_id=1, source_target_pairs={{0,24},{4,28},{8,16},{12,20},{16,8},{20,12},{24,0},{28,4},{1,25},{... | collective-permute-start | bytes 688136 | tf_op jit(solution)/shard_map/ppermute | solution.py:651
  164.7 7.2 %collective-permute-start.36 = (bf16[80,1024]{1,0:T(8,128)(2,1)S(1)}, bf16[80,1024]{1,0:T(8,128)(2,1)S(1)}, u32[]{:S(2)}, u32[]{:S(2)}) collective-permute-start(bf16[80,1024]{1,0:T(8,128)(2,1)S(1)} %pad_maximum_fusion.6), channel_id=1, source_target_pairs={{0,3},{1,2},{2,1},{3,0},{4,7},{5,6},{6,5},{7,4},{8,11},{9,10},{10,... | collective-permute-start | bytes 491528 | tf_op jit(solution)/shard_map/ppermute | solution.py:610
  166.0 13.5 %collective-permute-start.35 = (bf16[80,1024]{1,0:T(8,128)(2,1)S(1)}, bf16[80,1024]{1,0:T(8,128)(2,1)S(1)}, u32[]{:S(2)}, u32[]{:S(2)}) collective-permute-start(bf16[80,1024]{1,0:T(8,128)(2,1)S(1)} %pad_maximum_fusion.5), channel_id=1, source_target_pairs={{0,2},{1,3},{2,0},{3,1},{4,6},{5,7},{6,4},{7,5},{8,10},{9,11},{10,... | collective-permute-start | bytes 491528 | tf_op jit(solution)/shard_map/ppermute | solution.py:610
  172.0 10.5 %collective-permute-start.34 = (bf16[80,1024]{1,0:T(8,128)(2,1)S(1)}, bf16[80,1024]{1,0:T(8,128)(2,1)S(1)}, u32[]{:S(2)}, u32[]{:S(2)}) collective-permute-start(bf16[80,1024]{1,0:T(8,128)(2,1)S(1)} %pad_maximum_fusion.4), channel_id=1, source_target_pairs={{0,1},{1,0},{2,3},{3,2},{4,5},{5,4},{6,7},{7,6},{8,9},{9,8},{10,11... | collective-permute-start | bytes 491528 | tf_op jit(solution)/shard_map/ppermute | solution.py:610
  179.5 3.7 %collective-permute-start.37 = (bf16[448,256]{1,0:T(8,128)(2,1)S(1)}, bf16[448,256]{1,0:T(8,128)(2,1)S(1)}, u32[]{:S(2)}, u32[]{:S(2)}) collective-permute-start(bf16[448,256]{1,0:T(8,128)(2,1)S(1)} %pad_maximum_fusion.1.refs_0_), channel_id=1, source_target_pairs={{0,4},{4,0},{8,12},{12,8},{16,20},{20,16},{24,28},{28,24},{1,5},{5... | collective-permute-start | bytes 688136 | tf_op jit(solution)/shard_map/ppermute | solution.py:604
  179.6 3.7 %collective-permute-start.39 = (bf16[448,256]{1,0:T(8,128)(2,1)S(1)}, bf16[448,256]{1,0:T(8,128)(2,1)S(1)}, u32[]{:S(2)}, u32[]{:S(2)}) collective-permute-start(bf16[448,256]{1,0:T(8,128)(2,1)S(1)} %collective-permute-done.38.refs_2_), channel_id=1, source_target_pairs={{0,4},{4,0},{8,12},{12,8},{16,20},{20,16},{24,28},{28,24},{1,5},{5... | collective-permute-start | bytes 688136 | tf_op jit(solution)/shard_map/ppermute | solution.py:604
  180.1 3.2 %collective-permute-start.41 = (bf16[448,256]{1,0:T(8,128)(2,1)S(1)}, bf16[448,256]{1,0:T(8,128)(2,1)S(1)}, u32[]{:S(2)}, u32[]{:S(2)}) collective-permute-start(bf16[448,256]{1,0:T(8,128)(2,1)S(1)} %collective-permute-done.40.refs_4_), channel_id=1, source_target_pairs={{0,4},{4,0},{8,12},{12,8},{16,20},{20,16},{24,28},{28,24},{1,5},{5... | collective-permute-start | bytes 688136 | tf_op jit(solution)/shard_map/ppermute | solution.py:604
  180.1 3.2 %collective-permute-start.43 = (bf16[448,256]{1,0:T(8,128)(2,1)S(1)}, bf16[448,256]{1,0:T(8,128)(2,1)S(1)}, u32[]{:S(2)}, u32[]{:S(2)}) collective-permute-start(bf16[448,256]{1,0:T(8,128)(2,1)S(1)} %collective-permute-done.42.refs_6_), channel_id=1, source_target_pairs={{0,4},{4,0},{8,12},{12,8},{16,20},{20,16},{24,28},{28,24},{1,5},{5... | collective-permute-start | bytes 688136 | tf_op jit(solution)/shard_map/ppermute | solution.py:604
  (50 other events, 366.0 us)

commit v5 on v4

--- a/solution.py
+++ b/solution.py
@@ -47,8 +47,8 @@
     return lax.dot_general(left, right, (((1,), (1,)), ((), ())), preferred_element_type=FULL)
 
 
-def params():
-    return pltpu.CompilerParams(vmem_limit_bytes=VMEM_BYTES)
+def params(limit=VMEM_BYTES):
+    return pltpu.CompilerParams(vmem_limit_bytes=limit)
 
 
 def token_sides(scal_ref, first, count, per_sample, cells):
@@ -96,8 +96,9 @@
         ref[...] = held[:, part_of(scal_ref, k, rows), :]
 
 
-def embed(scal, patches, embed_w, embed_b, gain, firsts, count, per_sample, cells, shards):
+def embed(scal, patches, embed_w, embed_b, gain, firsts, count, per_sample, cells, shards, groups):
     rows, depth = patches.shape
+    block = depth // groups
     width = embed_w.shape[1]
     share = width // shards
     chunk_rows = count * per_sample
@@ -106,8 +107,21 @@
     tile = depth // steps
 
     def body(scal_ref, x_ref, w_ref, b_ref, gain_ref, emb_ref, norm_ref, stat_ref, *refs):
-        outs, acc = refs[:-1], refs[-1]
+        (send_ref, keep_ref), outs, acc = refs[:2], refs[2:-1], refs[-1]
         step = pl.program_id(0)
+        turned = x_ref[...].T
+        for i in range(tile // block):
+            values = turned[i * block : (i + 1) * block]
+            away = (scal_ref[GROUP] + i) % 2
+
+            @pl.when(away == 1)
+            def _(i=i, values=values):
+                send_ref[i // 2] = values
+
+            @pl.when(away == 0)
+            def _(i=i, values=values):
+                keep_ref[i // 2] = values
+
         part = dot(x_ref[...], w_ref[...])
 
         @pl.when(step == 0)
@@ -137,7 +151,9 @@
                     outs[c * shards + k][...] = piece.reshape(count, per_sample, share)
 
     piece = (count, per_sample, share)
-    emb, normed, stats, *pieces = pl.pallas_call(
+    turned_spec = pl.BlockSpec((tile // (2 * block), block, rows), lambda k, s: (k, 0, 0))
+    turned_shape = jax.ShapeDtypeStruct((groups // 2, block, rows), HALF)
+    emb, normed, stats, send, keep, *pieces = pl.pallas_call(
         body,
         grid_spec=pltpu.PrefetchScalarGridSpec(
             num_scalar_prefetch=1,
@@ -148,7 +164,7 @@
                 whole((1, width)),
                 whole((1, width)),
             ],
-            out_specs=[whole((rows, width)), whole((rows, width)), whole((rows, 256))]
+            out_specs=[whole((rows, width)), whole((rows, width)), whole((rows, 256)), turned_spec, turned_spec]
             + [whole(piece)] * (shards * chunks),
             scratch_shapes=[pltpu.VMEM((rows, width), FULL)],
         ),
@@ -156,15 +172,17 @@
             jax.ShapeDtypeStruct((rows, width), HALF),
             jax.ShapeDtypeStruct((rows, width), HALF),
             jax.ShapeDtypeStruct((rows, 256), FULL),
+            turned_shape,
+            turned_shape,
         ]
         + [jax.ShapeDtypeStruct(piece, HALF)] * (shards * chunks),
-        compiler_params=params(),
+        compiler_params=params(60 * 1024 * 1024),
         cost_estimate=pl.CostEstimate(
             flops=2 * rows * depth * width, bytes_accessed=2 * depth * (rows + width), transcendentals=0
         ),
         name="embed",
     )(scal, patches, embed_w, embed_b, gain)
-    return emb, normed, stats, [pieces[c * shards : (c + 1) * shards] for c in range(chunks)]
+    return emb, normed, stats, send, keep, [pieces[c * shards : (c + 1) * shards] for c in range(chunks)]
 
 
 def to_blocks(values, blocks, width):
@@ -288,7 +306,7 @@
     scale_root = float(np.sqrt(np.float32(samples)))
 
     def body(scal_ref, emb_ref, norm_ref, tgt_ref, w_ref, b_ref, *refs):
-        mix_refs, (pred_ref, res_ref, up_ref, bias_ref, held) = refs[:shards], refs[shards:]
+        mix_refs, (pred_ref, res_ref, all_ref, up_ref, bias_ref, held) = refs[:shards], refs[shards:]
         fill_lanes(scal_ref, mix_refs, held)
         side, valid = token_sides(scal_ref, first, count, per_sample, cells)
         updated = (emb_ref[...].astype(FULL) + norm_ref[...].astype(FULL) + held[...].astype(FULL)).astype(HALF)
@@ -297,6 +315,8 @@
         scale = 2.0 / (side.astype(FULL) * scale_root)
         residual = (scale * valid * (output - tgt_ref[...].astype(FULL))).astype(HALF)
         res_ref[...] = residual.reshape(res_ref.shape)
+        for z in range(shards):
+            all_ref[z] = residual.reshape(res_ref.shape)
         up_ref[...] = updated
         total = jnp.sum(residual.astype(FULL), axis=0, keepdims=True)
         bias_ref[...] = jnp.broadcast_to(total, bias_ref.shape)
@@ -315,12 +335,19 @@
                 whole((1, outs)),
             ]
             + [whole(mixed[0].shape)] * shards,
-            out_specs=[whole(token_shape), whole(token_shape), whole((rows, width)), whole((8, outs))],
+            out_specs=[
+                whole(token_shape),
+                whole(token_shape),
+                whole((shards,) + token_shape),
+                whole((rows, width)),
+                whole((8, outs)),
+            ],
             scratch_shapes=[pltpu.VMEM((rows, width), HALF)],
         ),
         out_shape=[
             jax.ShapeDtypeStruct(token_shape, HALF),
             jax.ShapeDtypeStruct(token_shape, HALF),
+            jax.ShapeDtypeStruct((shards,) + token_shape, HALF),
             jax.ShapeDtypeStruct((rows, width), HALF),
             jax.ShapeDtypeStruct((8, outs), FULL),
         ],
@@ -356,8 +383,7 @@
 
 
 def spectral_back_chunk(scal, table, factors, residual, head_w, spec_w, saved, first, before, last):
-    shards = len(residual)
-    count, per_sample, outs = residual[0].shape
+    shards, count, per_sample, outs = residual.shape
     size = shards * per_sample
     width = spec_w.shape[-1]
     wide = 2 * width
@@ -368,7 +394,7 @@
     has_before = before is not None
 
     def body(scal_ref, t_ref, h_ref, w_ref, spec_ref, hid_ref, fil_ref, *refs):
-        ins, refs = refs[:shards], refs[shards:]
+        in_ref, refs = refs[0], refs[1:]
         if has_before:
             (old_ref, old_bias_ref), refs = refs[:2], refs[2:]
         pieces, (grad_ref, bias_ref, weights, held, gathered) = refs[:shards], refs[shards:]
@@ -389,7 +415,8 @@
             grad_ref[at * width : (at + 1) * width] = jnp.concatenate([real, imag], axis=1).astype(HALF)
 
         complex_weights(w_ref, weights, blocks, width)
-        fill_rows(scal_ref, ins, gathered)
+        for z in range(shards):
+            gathered[:, z * per_sample : (z + 1) * per_sample, :] = in_ref[z]
         levels = [scal_ref[SIDES + SLOTS + first + i] for i in range(count)]
         updated_grad = dot_nt(gathered[...].reshape(count * size, outs), h_ref[...]).astype(HALF)
         entries = []
@@ -429,7 +456,7 @@
                 pl.BlockSpec((2, 2, blocks, width, width), lambda i, s: (0, 0, s[SHARD], 0, 0)),
             ]
             + [whole(saved[0].shape)] * 3
-            + [whole(residual[0].shape)] * shards
+            + [whole(residual.shape)]
             + ([whole(raw_shape), whole(bias_shape)] if has_before else []),
             out_specs=[whole(piece)] * shards + [whole(grad_out.shape), whole(bias_shape)],
             scratch_shapes=[
@@ -445,7 +472,7 @@
             flops=count * size * share * size * 20, bytes_accessed=count * size * share * 16, transcendentals=0
         ),
         name="spectral_back",
-    )(scal, table, head_w, spec_w, *saved, *residual, *(before or ()))
+    )(scal, table, head_w, spec_w, *saved, residual, *(before or ()))
     return result[:shards], result[shards:]
 
 
@@ -498,46 +525,6 @@
         ),
         name="embedded_back",
     )(scal, embedded, stats, residual, head_w, gain, *spec_grad)
-
-
-def turned_patches(scal, patches, groups):
-    tokens, depth = patches.shape
-    block = depth // groups
-    tile = 256
-    piece = int(np.gcd(tile, block))
-    per_block = block // piece
-
-    def body(scal_ref, x_ref, send_ref, keep_ref):
-        turned = x_ref[...].T
-        for i in range(tile // piece):
-            place = pl.program_id(0) * (tile // piece) + i
-            group = place // per_block
-            rows = pl.ds(pl.multiple_of((place % per_block) * piece, piece), piece)
-            values = turned[i * piece : (i + 1) * piece]
-            away = jnp.bitwise_xor(group, scal_ref[GROUP]) % 2
-
-            @pl.when(away == 1)
-            def _(group=group, rows=rows, values=values):
-                send_ref[group // 2, rows] = values
-
-            @pl.when(away == 0)
-            def _(group=group, rows=rows, values=values):
-                keep_ref[group // 2, rows] = values
-
-    shape = (groups // 2, block, tokens)
-    return pl.pallas_call(
-        body,
-        grid_spec=pltpu.PrefetchScalarGridSpec(
-            num_scalar_prefetch=1,
-            grid=(depth // tile,),
-            in_specs=[pl.BlockSpec((tokens, tile), lambda i, s: (0, i))],
-            out_specs=[whole(shape)] * 2,
-        ),
-        out_shape=[jax.ShapeDtypeStruct(shape, HALF)] * 2,
-        compiler_params=params(),
-        cost_estimate=pl.CostEstimate(flops=0, bytes_accessed=4 * tokens * depth, transcendentals=0),
-        name="turned_patches",
-    )(scal, patches)
 
 
 def embed_grad_parts(scal, turned, grads, groups, away):
@@ -637,13 +624,20 @@
 
 
 def scatter_end(ends, shards, shard_at):
-    share = ends[0].shape[0] // shards
-
-    def piece(k):
-        at = jnp.bitwise_xor(shard_at, k) * share
-        return jnp.concatenate([lax.dynamic_slice_in_dim(e, at, share) for e in ends], axis=-1)
-
-    return sum(p.astype(FULL) for p in across([piece(k) for k in range(shards)]))
+    part = jnp.concatenate(ends, axis=-1)
+    part = part.reshape(shards, part.shape[0] // shards, -1)
+    bit = 1
+    while bit < shards:
+        split = part.reshape(part.shape[0] // 2, 2, *part.shape[1:])
+        mine = (shard_at // bit) % 2
+        keep = lax.dynamic_index_in_dim(split, mine, 1, keepdims=False)
+        send = lax.dynamic_index_in_dim(split, 1 - mine, 1, keepdims=False)
+        received = lax.ppermute(send, "fft", [(z, z ^ bit) for z in range(shards)])
+        part = keep.astype(FULL) + received.astype(FULL)
+        bit *= 2
+        if bit < shards:
+            part = part.astype(HALF)
+    return part[0]
 
 
 def from_all_groups(values, groups):
@@ -678,9 +672,8 @@
     rows = across([jnp.concatenate([summed, hi_lo(small)], axis=0)] * shards)
     head_part = sum(r[:head_rows].astype(FULL) for r in rows).astype(HALF)
     order = jnp.bitwise_xor(jnp.arange(shards, dtype=jnp.int32), shard_at)
-    rest = jnp.take(jnp.stack([r[head_rows:] for r in rows]), order, axis=0)
-    spec_rows = summed.shape[0] - head_rows
-    return head_part, rest[:, :spec_rows], from_hi_lo(rest[:, spec_rows:])
+    small = jnp.take(jnp.stack([from_hi_lo(r[summed.shape[0] :]) for r in rows]), order, axis=0)
+    return head_part, [r[head_rows : summed.shape[0]] for r in rows], small
 
 
 def assembled(scal, gathered, head_rows, shards, blocks, width):
@@ -691,7 +684,7 @@
     small_rows = (gathered[0].shape[0] - small_at) // 2
 
     def body(scal_ref, *refs):
-        ins, (head_ref, spec_ref, small_ref) = refs[:groups], refs[groups:]
+        ins, (head_ref, spec_ref, bias_ref, gain_ref, embed_ref, out_ref) = refs[:groups], refs[groups:]
         small = None
         for k, ref in enumerate(ins):
             group = jnp.bitwise_xor(scal_ref[GROUP], k)
@@ -700,18 +693,36 @@
             start = group * spec_rows
             layer, b = start // (blocks * width), (start // width) % blocks
             rows = pl.ds(pl.multiple_of(start % width, spec_rows), spec_rows)
-            for z in range(shards):
-                values = ref[head_rows + z * spec_rows : head_rows + (z + 1) * spec_rows].astype(FULL)
+            for j in range(shards):
+                values = ref[head_rows + j * spec_rows : head_rows + (j + 1) * spec_rows].astype(FULL)
+                z = jnp.bitwise_xor(scal_ref[SHARD], j)
                 spec_ref[layer, 0, z * blocks + b, rows] = values[:, :width]
                 spec_ref[layer, 1, z * blocks + b, rows] = values[:, width:]
             part = ref[small_at : small_at + small_rows].astype(FULL) + ref[small_at + small_rows :].astype(FULL)
             small = part if small is None else small + part
-        small_ref[...] = small
+        for z in range(shards):
+            for layer in range(2):
+                for b in range(blocks):
+                    row = (z * 2 + layer) * blocks + b
+                    for p in range(2):
+                        bias_ref[layer, p, z * blocks + b : z * blocks + b + 1] = small[
+                            row : row + 1, p * width : (p + 1) * width
+                        ]
+        row = shards * 2 * blocks
+        quarter = gain_ref.shape[1] // (2 * width)
+        for ref in (gain_ref, embed_ref):
+            for i in range(quarter):
+                ref[:, i * 2 * width : (i + 1) * 2 * width] = small[row + i : row + i + 1]
+            row += quarter
+        out_ref[...] = small[row : row + 1]
 
     out_shape = [
         jax.ShapeDtypeStruct((groups * head_rows, 2 * width), FULL),
         jax.ShapeDtypeStruct((2, 2, total_blocks, width, width), FULL),
-        jax.ShapeDtypeStruct((small_rows, 2 * width), FULL),
+        jax.ShapeDtypeStruct((2, 2, total_blocks, width), FULL),
+        jax.ShapeDtypeStruct((1, groups * head_rows), FULL),
+        jax.ShapeDtypeStruct((1, groups * head_rows), FULL),
+        jax.ShapeDtypeStruct((1, 2 * width), FULL),
     ]
     return pl.pallas_call(
         body,
@@ -765,14 +776,11 @@
     flat_targets = targets.reshape(-1, outs)
     gain_row, embed_b_row, head_b_row = gain[None], embed_b[None], head_b[None]
 
-    embedded, normed, stats, pieces = embed(
-        scal, flat_patches, embed_w, embed_b_row, gain_row, firsts, count, per_sample, cells, shards
+    embedded, normed, stats, turned_send, turned_keep, pieces = embed(
+        scal, flat_patches, embed_w, embed_b_row, gain_row, firsts, count, per_sample, cells, shards, groups
     )
     moved = [across(p) for p in pieces]
-    turned_send, turned_keep = turned_patches(scal, flat_patches, groups)
     turned = [turned_keep, swap_bit(turned_send, 0, groups)]
-    moved[0], turned_keep = lax.optimization_barrier((moved[0], turned_keep))
-    turned[0] = turned_keep
     mixed, saved = [], []
     for first, values in zip(firsts, moved):
         out, rest = spectral_chunk(scal, table, factors, values, spec_w, spec_b, first)
@@ -780,14 +788,14 @@
         saved.append(rest)
     predicted, residual, updated, head_sums, gathered = [], [], [], [], []
     for first, mix in zip(firsts, mixed):
-        pred, res, up, sums = head_chunk(
+        pred, res, copies, up, sums = head_chunk(
             scal, embedded, normed, mix, flat_targets, head_w, head_b_row, first, samples, cells
         )
         predicted.append(pred)
         residual.append(res)
         updated.append(up)
         head_sums.append(sums[0])
-        gathered.append(across([res] * shards))
+        gathered.append(lax.all_to_all(copies, "fft", split_axis=0, concat_axis=0, tiled=True))
     head_grad, gathered[0] = lax.optimization_barrier((head_gradient(updated, residual), gathered[0]))
     spec_back, sums = [], None
     for first, res, rest in zip(firsts, gathered, saved):
@@ -799,18 +807,21 @@
     width = spec_w.shape[-1]
     blocks = spec_w.shape[2] // shards
     head_rows = head_w.shape[0] // groups
-    weight_sums = sum_over_groups(head_grad, spec_grad, groups)
     own_grads, other_grads, row_sums = [], [], []
     for first, res, back in zip(firsts, residual, spec_back):
         grad, row_sum = embedded_back_chunk(scal, embedded, stats, res, head_w, gain_row, back, first, cells)
+        if first == firsts[0]:
+            grad, head_grad, spec_grad = lax.optimization_barrier((grad, head_grad, spec_grad))
+            weight_sums = sum_over_groups(head_grad, spec_grad, groups)
         own_grads.append(grad)
         other_grads.append(swap_bit(grad, 0, groups))
         row_sums.append(row_sum)
     grads = own_grads + other_grads
     sent = embed_grad_parts(scal, turned, grads, groups, 1)
+    sent, kept_turned = lax.optimization_barrier((sent, turned))
     top_bit = groups.bit_length() - 2
     received = [swap_bit(sent[0], 1, groups), swap_bit(sent[1], top_bit, groups)]
-    kept = embed_grad_parts(scal, turned, grads, groups, 0)
+    kept = embed_grad_parts(scal, kept_turned, grads, groups, 0)
     kept, weight_sums, predicted, row_sums = lax.optimization_barrier((kept, weight_sums, predicted, row_sums))
     ends = scatter_start(received, kept, groups)
     predictions = route_predictions(
@@ -820,20 +831,17 @@
     vectors = jnp.concatenate([rows[0].reshape(-1, outs), rows[4].reshape(-1, outs), sum(head_sums)[None]], axis=0)
     own_rows, all_rows = spec_bias.shape[0], vectors.shape[0]
     small = jnp.concatenate([spec_bias, vectors, jnp.zeros((16 - own_rows - all_rows, outs), FULL)], axis=0)
-    head_part, spec_part, small = over_shards(weight_sums, small, head_rows, shards, shard_at)
+    head_part, spec_parts, small = over_shards(weight_sums, small, head_rows, shards, shard_at)
     small = jnp.concatenate([small[:, :own_rows].reshape(-1, outs), jnp.sum(small[:, own_rows:], axis=0)], axis=0)
     small = jnp.concatenate([small, jnp.zeros((-small.shape[0] % 16, outs), FULL)], axis=0)
-    outgoing = jnp.concatenate([head_part, spec_part.reshape(-1, outs), hi_lo(small)], axis=0)
+    outgoing = jnp.concatenate([head_part, *spec_parts, hi_lo(small)], axis=0)
     ends, outgoing = lax.optimization_barrier((ends, outgoing))
     gathered = from_all_groups(outgoing, groups)
     embed_grad = scatter_end(ends, shards, shard_at)
-    head_grad, spec_w_grad, small = assembled(scal, gathered, head_rows, shards, blocks, width)
-    spec_bias_all = small[: shards * own_rows].reshape(shards, 2, blocks, 2, width)
-    spec_b_grad = jnp.transpose(spec_bias_all, (1, 3, 0, 2, 4)).reshape(spec_b.shape)
-    vectors = small[shards * own_rows : shards * own_rows + all_rows]
-    quarter = (all_rows - 1) // 2
-    gain_grad, embed_bias_grad = vectors[:quarter].reshape(-1), vectors[quarter : 2 * quarter].reshape(-1)
-    head_bias_grad = vectors[2 * quarter]
+    head_grad, spec_w_grad, spec_b_grad, gain_grad, embed_bias_grad, head_bias_grad = assembled(
+        scal, gathered, head_rows, shards, blocks, width
+    )
+    gain_grad, embed_bias_grad, head_bias_grad = gain_grad[0], embed_bias_grad[0], head_bias_grad[0]
     return (
         predictions,
         embed_grad,

time: 189 us -> 201 us (1.063)
  starting transfers between devices: 75.7 us -> 60 us
  local copies, waits for them, and re-layouts: 25.9 us -> 37.3 us
  waiting for transfers between devices: 32.1 us -> 41.9 us
  other arithmetic: 14.1 us -> 17.3 us
  Pallas kernels: 39 us -> 41.6 us
    ppermute x30 -> x21, starting transfers between devices: 55.6 us -> 33.2 us  [across(): lax.ppermute(pieces[k], 'fft', [(z, z ^ k) for z in range(shards)])]
    unnamed x105 -> x143, local copies, waits for them, and re-layouts: 18.2 us -> 33.8 us
    all_to_all x0 -> x2, starting transfers between devices: none -> 7.1 us  [on_device(): lax.all_to_all(copies, 'fft', split_axis=0, concat_axis=0, tiled=True)]
    ppermute x3, waiting for transfers between devices: 0.01 us -> 6.99 us  [from_all_groups(): lax.ppermute(values, 'grp', [(g, g ^ k) for g in range(groups)])]
    ppermute x11, waiting for transfers between devices: 15.5 us -> 8.73 us  [swap_bit(): lax.ppermute(values, 'grp', [(g, g ^ 1 << bit) for g in range(groups)])]
    ppermute x0 -> x2, waiting for transfers between devices: none -> 5.09 us  [scatter_end(): received = lax.ppermute(send, 'fft', [(z, z ^ bit) for z in range(shards)])]
    ppermute x30 -> x21, waiting for transfers between devices: 16.6 us -> 21 us  [across(): lax.ppermute(pieces[k], 'fft', [(z, z ^ k) for z in range(shards)])]
    pallas_call x1, Pallas kernels: 6.05 us -> 10 us  [embed(): pl.pallas_call(body, grid_spec=pltpu.PrefetchScalarGridSpec(num_scalar_pr...]
  transfers between devices with their start and end apart: 46 -> 41, of which waited for: 10 -> 13; matrix products, arithmetic and copies ran while one was open for 9% -> 10% of each run, Pallas kernels for 16% -> 16%
where the time goes in v5:
time: 201 us; the launch traced here: 199 us
  starting transfers between devices  60 us (30%)
  waiting for transfers between devices  41.9 us (21%)
  Pallas kernels  41.6 us (21%)
  local copies, waits for them, and re-layouts  37.3 us (19%)
  other arithmetic  17.3 us (9%)
    unnamed x143, local copies, waits for them, and re-layouts  33.8 us
    ppermute x21, starting transfers between devices, across(): lax.ppermute(pieces[k], 'fft', [(z, z ^ k) for z in range(shards)])  33.2 us
    ppermute x21, waiting for transfers between devices, across(): lax.ppermute(pieces[k], 'fft', [(z, z ^ k) for z in range(shards)])  21 us
    pallas_call x1, Pallas kernels, embed(): pl.pallas_call(body, grid_spec=pltpu.PrefetchScalarGridSpec(num_scalar_pr...  10 us
    ppermute x11, waiting for transfers between devices, swap_bit(): lax.ppermute(values, 'grp', [(g, g ^ 1 << bit) for g in range(groups)])  8.73 us
    pallas_call x2, Pallas kernels, embed_grad_parts(): pl.pallas_call(body, grid_spec=pltpu.PrefetchScalarGridSpec(num_scalar_pr...  8.18 us
    pallas_call x2, Pallas kernels, spectral_back_chunk(): pl.pallas_call(body, grid_spec=pltpu.PrefetchScalarGridSpec(num_scalar_pr...  7.41 us
    all_to_all x2, starting transfers between devices, on_device(): lax.all_to_all(copies, 'fft', split_axis=0, concat_axis=0, tiled=True)  7.1 us
  transfers between devices with their start and end apart: 41, of which 13 were waited for; matrix products, arithmetic and copies ran while one was open for 10% of the time, Pallas kernels for 16%

profile of v5, /device:TPU:0, one launch (start us, length us, event | category | flops | bytes accessed | tf_op | source)
XLA Modules:
  0.0 199.5 jit_solution(13669597882356505156)
XLA Ops:
  2.0 10.0 %embed.1 = (bf16[384,1024]{1,0:T(8,128)(2,1)}, bf16[384,1024]{1,0:T(8,128)(2,1)}, f32[384,256]{1,0:T(8,128)}, bf16[4,320,384]{2,1,0:T(8,128)(2,1)}, bf16[4,320,3...) custom-call(s32[15]{0:T(128)} %concatenate.28.scal_ref, ...), custom_call_target="tpu_custom_call" | custom-call | flops 2013265920 | bytes 7208960 | tf_op jit(solution)/shard_map/embed/pallas_call | solution.py:156
  12.0 3.1 %collective-permute-start.1 = (bf16[3,64,256]{2,1,0:T(8,128)(2,1)}, bf16[3,64,256]{2,1,0:T(8,128)(2,1)S(1)}, u32[]{:S(2)}, u32[]{:S(2)}) collective-permute-start(bf16[3,64,256]{2,1,0:T(8,128)(2,1)} %get-tuple-element.96), channel_id=1, source_target_pairs={{0,1},{1,0},{2,3},{3,2},{4,5},{5,4},{6,7},{7,6},{8,9},{9,8},{10,11... | collective-permute-start | bytes 294920 | tf_op jit(solution)/shard_map/ppermute | solution.py:597
  15.1 2.6 %collective-permute-start.2 = (bf16[3,64,256]{2,1,0:T(8,128)(2,1)}, bf16[3,64,256]{2,1,0:T(8,128)(2,1)S(1)}, u32[]{:S(2)}, u32[]{:S(2)}) collective-permute-start(bf16[3,64,256]{2,1,0:T(8,128)(2,1)} %get-tuple-element.97), channel_id=1, source_target_pairs={{0,2},{1,3},{2,0},{3,1},{4,6},{5,7},{6,4},{7,5},{8,10},{9,11},{10,... | collective-permute-start | bytes 294920 | tf_op jit(solution)/shard_map/ppermute | solution.py:597
  18.6 7.1 %collective-permute-done.2.refs_2_ = bf16[3,64,256]{2,1,0:T(8,128)(2,1)S(1)} collective-permute-done((bf16[3,64,256]{2,1,0:T(8,128)(2,1)}, bf16[3,64,256]{2,1,0:T(8,128)(2,1)S(1)}, u32[]{:S(2)}, u32[]{:S(2)}) %collective-permute-start.2) | collective-permute-done | bytes 98336 | tf_op jit(solution)/shard_map/ppermute | solution.py:597
  27.8 3.0 %spectral.2 = (bf16[3,64,256]{2,1,0:T(8,128)(2,1)S(1)}, bf16[3,64,256]{2,1,0:T(8,128)(2,1)}, bf16[3,64,256]{2,1,0:T(8,128)(2,1)}, bf16[3,64,256]{2,1,0:T(8,128)(...) custom-call(s32[15]{0:T(128)S(1)} %copy-done.50, ...), custom_call_target="tpu_custom_call" | custom-call | flops 704643072 | bytes 3145728 | tf_op jit(solution)/shard_map/spectral/pallas_call | solution.py:276
  33.5 1.6 collective-permute-start.4
  35.1 1.4 collective-permute-start.5
  36.6 1.3 collective-permute-start.6
  39.3 2.8 %collective-permute-start.8 = (bf16[3,64,256]{2,1,0:T(8,128)(2,1)}, bf16[3,64,256]{2,1,0:T(8,128)(2,1)}, u32[]{:S(2)}, u32[]{:S(2)}) collective-permute-start(bf16[3,64,256]{2,1,0:T(8,128)(2,1)} %get-tuple-element.110), channel_id=1, source_target_pairs={{0,2},{1,3},{2,0},{3,1},{4,6},{5,7},{6,4},{7,5},{8,10},{9,11},{10,... | collective-permute-start | bytes 294920 | tf_op jit(solution)/shard_map/ppermute | solution.py:597
  42.1 5.2 %collective-permute-done.5.refs_2_ = bf16[3,64,256]{2,1,0:T(8,128)(2,1)} collective-permute-done((bf16[3,64,256]{2,1,0:T(8,128)(2,1)}, bf16[3,64,256]{2,1,0:T(8,128)(2,1)}, u32[]{:S(2)}, u32[]{:S(2)}) %collective-permute-start.5) | collective-permute-done | bytes 98336 | tf_op jit(solution)/shard_map/ppermute | solution.py:597
  47.2 1.9 collective-permute-start.9
  49.2 1.8 head.2
  54.5 3.5 %all-to-all-start = ((bf16[4,3,64,256]{3,2,1,0:T(8,128)(2,1)}), bf16[4,3,64,256]{3,2,1,0:T(8,128)(2,1)S(1)}, u32[]{:S(2)}, u32[]{:S(2)}) async-start(bf16[4,3,64,256]{3,2,1,0:T(8,128)(2,1)} %copy-done.36), calls=%async_computation | async-start | bytes 786432 | tf_op jit(solution)/shard_map/all_to_all | solution.py:798
  61.3 3.3 %spectral.3 = (bf16[3,64,256]{2,1,0:T(8,128)(2,1)S(1)}, bf16[3,64,256]{2,1,0:T(8,128)(2,1)S(1)}, bf16[3,64,256]{2,1,0:T(8,128)(2,1)S(1)}, bf16[3,64,256]{2,1,0:T...) custom-call(s32[15]{0:T(128)S(1)} %copy-done.50, ...), custom_call_target="tpu_custom_call" | custom-call | flops 704643072 | bytes 3145728 | tf_op jit(solution)/shard_map/spectral/pallas_call | solution.py:276
  67.3 2.0 collective-permute-start.10
  69.3 2.4 %collective-permute-start.11 = (bf16[3,64,256]{2,1,0:T(8,128)(2,1)S(1)}, bf16[3,64,256]{2,1,0:T(8,128)(2,1)S(1)}, u32[]{:S(2)}, u32[]{:S(2)}) collective-permute-start(bf16[3,64,256]{2,1,0:T(8,128)(2,1)S(1)} %get-tuple-element.114), channel_id=1, source_target_pairs={{0,2},{1,3},{2,0},{3,1},{4,6},{5,7},{6,4},{7,5},{8,10},{9,11},{10,... | collective-permute-start | bytes 294920 | tf_op jit(solution)/shard_map/ppermute | solution.py:597
  72.3 3.6 %collective-permute-done.11.refs_2_ = bf16[3,64,256]{2,1,0:T(8,128)(2,1)S(1)} collective-permute-done((bf16[3,64,256]{2,1,0:T(8,128)(2,1)S(1)}, bf16[3,64,256]{2,1,0:T(8,128)(2,1)S(1)}, u32[]{:S(2)}, u32[]{:S(2)}) %collective-permute-start.11) | collective-permute-done | bytes 98336 | tf_op jit(solution)/shard_map/ppermute | solution.py:597
  75.9 2.2 %collective-permute-done.12.refs_3_ = bf16[3,64,256]{2,1,0:T(8,128)(2,1)S(1)} collective-permute-done((bf16[3,64,256]{2,1,0:T(8,128)(2,1)S(1)}, bf16[3,64,256]{2,1,0:T(8,128)(2,1)S(1)}, u32[]{:S(2)}, u32[]{:S(2)}) %collective-permute-start.12) | collective-permute-done | bytes 98336 | tf_op jit(solution)/shard_map/ppermute | solution.py:597
  83.2 3.6 %all-to-all-start.1 = ((bf16[4,3,64,256]{3,2,1,0:T(8,128)(2,1)}), bf16[4,3,64,256]{3,2,1,0:T(8,128)(2,1)S(1)}, u32[]{:S(2)}, u32[]{:S(2)}) async-start(bf16[4,3,64,256]{3,2,1,0:T(8,128)(2,1)} %copy-done.37), calls=%async_computation.1 | async-start | bytes 786432 | tf_op jit(solution)/shard_map/all_to_all | solution.py:798
  93.0 1.3 copy-done.19
  95.4 3.6 %spectral_back.2 = (bf16[3,64,256]{2,1,0:T(8,128)(2,1)S(1)}, bf16[3,64,256]{2,1,0:T(8,128)(2,1)}, bf16[3,64,256]{2,1,0:T(8,128)(2,1)}, bf16[3,64,256]{2,1,0:T(8,...) custom-call(s32[15]{0:T(128)S(1)} %copy-done.50, bf16[3,512,256]{2,1,0:T(8,128)(2,1)S(1)} %copy-done.6, ...), custom_call_target="tpu_custom_call" | custom-call | flops 1006632960 | bytes 3145728 | tf_op jit(solution)/shard_map/spectral_back/pallas_call | solution.py:448
  100.6 1.8 collective-permute-start.13
  102.4 2.4 %collective-permute-start.14 = (bf16[3,64,256]{2,1,0:T(8,128)(2,1)}, bf16[3,64,256]{2,1,0:T(8,128)(2,1)}, u32[]{:S(2)}, u32[]{:S(2)}) collective-permute-start(bf16[3,64,256]{2,1,0:T(8,128)(2,1)} %get-tuple-element.122), channel_id=1, source_target_pairs={{0,2},{1,3},{2,0},{3,1},{4,6},{5,7},{6,4},{7,5},{8,10},{9,11},{10,... | collective-permute-start | bytes 294920 | tf_op jit(solution)/shard_map/ppermute | solution.py:597
  112.0 3.8 %spectral_back.3 = (bf16[3,64,256]{2,1,0:T(8,128)(2,1)S(1)}, bf16[3,64,256]{2,1,0:T(8,128)(2,1)}, bf16[3,64,256]{2,1,0:T(8,128)(2,1)}, bf16[3,64,256]{2,1,0:T(8,...) custom-call(s32[15]{0:T(128)S(1)} %copy-done.50, bf16[3,512,256]{2,1,0:T(8,128)(2,1)S(1)} %copy-done.6, ...), custom_call_target="tpu_custom_call" | custom-call | flops 1006632960 | bytes 3145728 | tf_op jit(solution)/shard_map/spectral_back/pallas_call | solution.py:448
  116.7 3.3 %collective-permute-start.17 = (bf16[3,64,256]{2,1,0:T(8,128)(2,1)}, bf16[3,64,256]{2,1,0:T(8,128)(2,1)S(1)}, u32[]{:S(2)}, u32[]{:S(2)}) collective-permute-start(bf16[3,64,256]{2,1,0:T(8,128)(2,1)} %get-tuple-element.136), channel_id=1, source_target_pairs={{0,2},{1,3},{2,0},{3,1},{4,6},{5,7},{6,4},{7,5},{8,10},{9,11},{10,... | collective-permute-start | bytes 294920 | tf_op jit(solution)/shard_map/ppermute | solution.py:597
  120.2 2.4 %embedded_back.2 = (bf16[192,1024]{1,0:T(8,128)(2,1)S(1)}, f32[8,1024]{1,0:T(8,128)S(1)}) custom-call(s32[15]{0:T(128)S(1)} %copy-done.50, bf16[384,1024]{1,0:T(8,128)(2,1)S(1)} %copy-done.1, f32[384,256]{1,0:T(8,128)S(1)} %copy-done.9, bf16[3,64,256]{2,1,0:T(8,128)(2,1)S(1)} %copy-done.32, bf16[1024,256]{1,0:T(8,128)(2,1)S(1)} %copy-done, ...), custom_call_target="tpu_custom_call" | custom-call | flops 100663296 | bytes 1179648 | tf_op jit(solution)/shard_map/embedded_back/pallas_call | solution.py:505
  123.6 4.2 %all-to-all-start.2 = ((bf16[8,192,256]{2,1,0:T(8,128)(2,1)}), bf16[8,192,256]{2,1,0:T(8,128)(2,1)}, u32[]{:S(2)}, u32[]{:S(2)}) async-start(bf16[8,192,256]{2,1,0:T(8,128)(2,1)} %pad_maximum_fusion), calls=%async_computation.2 | async-start | bytes 1572864 | tf_op jit(solution)/shard_map/all_to_all | solution.py:667
  128.9 1.4 embedded_back.3
  132.2 4.1 %embed_grad.2 = (bf16[2,320,512]{2,1,0:T(8,128)(2,1)S(1)}, bf16[2,320,512]{2,1,0:T(8,128)(2,1)S(1)}) custom-call(s32[15]{0:T(128)S(1)} %copy-done.50, bf16[4,320,384]{2,1,0:T(8,128)(2,1)S(1)} %copy-done.59, bf16[4,320,384]{2,1,0:T(8,128)(2,1)} %collective-permute-done.refs_1_, bf16[192,1024]{1,0:T(8,128)(2,1)S(1)} %copy-done.56, ...), custom_call_target="tpu_custom_call" | custom-call | flops 1006632960 | bytes 4063232 | tf_op jit(solution)/shard_map/embed_grad/pallas_call | solution.py:563
  136.3 1.7 collective-permute-start.21
  138.0 1.5 collective-permute-start.23
  139.5 4.1 %embed_grad.3 = (bf16[2,320,512]{2,1,0:T(8,128)(2,1)S(1)}, bf16[2,320,512]{2,1,0:T(8,128)(2,1)S(1)}) custom-call(s32[15]{0:T(128)S(1)} %copy-done.50, bf16[4,320,384]{2,1,0:T(8,128)(2,1)S(1)} %copy-done.59, bf16[4,320,384]{2,1,0:T(8,128)(2,1)} %collective-permute-done.refs_1_, bf16[192,1024]{1,0:T(8,128)(2,1)S(1)} %copy-done.56, ...), custom_call_target="tpu_custom_call" | custom-call | flops 1006632960 | bytes 4063232 | tf_op jit(solution)/shard_map/embed_grad/pallas_call | solution.py:563
  143.8 1.2 reduce_sum.57
  145.7 3.6 %collective-permute-start.27 = (bf16[224,256]{1,0:T(8,128)(2,1)}, bf16[224,256]{1,0:T(8,128)(2,1)S(1)}, u32[]{:S(2)}, u32[]{:S(2)}) collective-permute-start(bf16[224,256]{1,0:T(8,128)(2,1)} %pad_maximum_fusion.3), channel_id=1, source_target_pairs={{0,3},{1,2},{2,1},{3,0},{4,7},{5,6},{6,5},{7,4},{8,11},{9,10},{10,... | collective-permute-start | bytes 344072 | tf_op jit(solution)/shard_map/ppermute | solution.py:597
  150.8 1.4 broadcast_select_fusion
  152.2 3.4 %all-to-all-start.3 = ((bf16[8,64,256]{2,1,0:T(8,128)(2,1)}), bf16[8,64,256]{2,1,0:T(8,128)(2,1)S(1)}, u32[]{:S(2)}, u32[]{:S(2)}) async-start(bf16[8,64,256]{2,1,0:T(8,128)(2,1)} %broadcast_select_fusion), calls=%async_computation.3 | async-start | bytes 524288 | tf_op jit(solution)/shard_map/all_to_all | solution.py:746
  155.7 2.3 %collective-permute-done.26 = bf16[224,256]{1,0:T(8,128)(2,1)} collective-permute-done((bf16[224,256]{1,0:T(8,128)(2,1)}, bf16[224,256]{1,0:T(8,128)(2,1)}, u32[]{:S(2)}, u32[]{:S(2)}) %collective-permute-start.26) | collective-permute-done | bytes 114720 | tf_op jit(solution)/shard_map/ppermute | solution.py:597
  162.9 1.3 fusion
  164.8 1.3 add_convert_fusion
  166.8 6.9 %collective-permute-done.22 = bf16[1,320,512]{2,1,0:T(8,128)(2,1)S(1)} collective-permute-done((bf16[1,320,512]{2,1,0:T(8,128)(2,1)S(1)}, bf16[1,320,512]{2,1,0:T(8,128)(2,1)S(1)}, u32[]{:S(2)}, u32[]{:S(2)}) %collective-permute-start.22) | collective-permute-done | bytes 327712 | tf_op jit(solution)/shard_map/ppermute | solution.py:591
  173.8 1.5 collective-permute-done.24
  177.5 1.4 collective-permute-start.35
  180.5 3.5 %collective-permute-done.31.refs_2_ = bf16[448,256]{1,0:T(8,128)(2,1)S(1)} collective-permute-done((bf16[448,256]{1,0:T(8,128)(2,1)S(1)}, bf16[448,256]{1,0:T(8,128)(2,1)S(1)}, u32[]{:S(2)}, u32[]{:S(2)}) %collective-permute-start.31) | collective-permute-done | bytes 229408 | tf_op jit(solution)/shard_map/ppermute | solution.py:645
  184.0 1.8 collective-permute-done.33.refs_4_
  185.9 1.6 collective-permute-done.35.refs_6_
  187.6 2.7 %collective-permute-start.29 = (bf16[1,80,1024]{2,1,0:T(8,128)(2,1)S(1)}, bf16[1,80,1024]{2,1,0:T(8,128)(2,1)S(1)}, u32[]{:S(2)}, u32[]{:S(2)}) collective-permute-start(bf16[1,80,1024]{2,1,0:T(8,128)(2,1)S(1)} %constant_dynamic-slice_fusion), channel_id=1, source_target_pairs={{0,2},{1,3},{2,0},{3,1},{4,6},{5,7},{6,4},{7,5},{8,10},{9,11},{10,... | collective-permute-start | bytes 491528 | tf_op jit(solution)/shard_map/ppermute | solution.py:635
  191.1 2.5 %assembled.1 = (f32[1024,256]{1,0:T(8,128)}, f32[2,2,8,128,128]{4,3,2,1,0:T(8,128)}, f32[2,2,8,128]{3,2,1,0:T(8,128)}, f32[1,1024]{1,0:T(1,128)}, f32[1,1024]{1,0:T(1,128)}, /*index=5*/f32[1,256]{1,0:T(1,128)}) custom-call(s32[15]{0:T(128)S(1)} %copy-done.50, bf16[448,256]{1,0:T(8,128)(2,1)S(1)} %fusion.7.refs_0_, ...), custom_call_target="tpu_custom_call" | custom-call | tf_op jit(solution)/shard_map/assembled/pallas_call | solution.py:727
  193.6 5.1 %collective-permute-done.29 = bf16[1,80,1024]{2,1,0:T(8,128)(2,1)S(1)} collective-permute-done((bf16[1,80,1024]{2,1,0:T(8,128)(2,1)S(1)}, bf16[1,80,1024]{2,1,0:T(8,128)(2,1)S(1)}, u32[]{:S(2)}, u32[]{:S(2)}) %collective-permute-start.29) | collective-permute-done | bytes 163872 | tf_op jit(solution)/shard_map/ppermute | solution.py:635
  (255 shorter events, 58.2 us)
Async XLA Ops:
  2.0 23.8 %copy-start.2 = (bf16[2,2,8,128,128]{4,3,2,1,0:T(8,128)(2,1)S(1)}, bf16[2,2,8,128,128]{4,3,2,1,0:T(8,128)(2,1)}, u32[]{:S(2)}) copy-start(bf16[2,2,8,128,128]{4,3,2,1,0:T(8,128)(2,1)} %w_ref.16) | copy-start | bytes 3145732
  2.0 23.8 %copy-start.50 = (s32[15]{0:T(128)S(1)}, s32[15]{0:T(128)}, u32[]{:S(2)}) copy-start(s32[15]{0:T(128)} %concatenate.28.scal_ref) | copy-start | bytes 184
  2.0 23.8 %copy-start.57 = (f32[2,2,8,128]{3,2,1,0:T(8,128)S(1)}, f32[2,2,8,128]{3,2,1,0:T(8,128)}, u32[]{:S(2)}) copy-start(f32[2,2,8,128]{3,2,1,0:T(8,128)} %b_ref.3) | copy-start | bytes 49156
  12.0 6.6 %collective-permute-start.1 = (bf16[3,64,256]{2,1,0:T(8,128)(2,1)}, bf16[3,64,256]{2,1,0:T(8,128)(2,1)S(1)}, u32[]{:S(2)}, u32[]{:S(2)}) collective-permute-start(bf16[3,64,256]{2,1,0:T(8,128)(2,1)} %get-tuple-element.96), channel_id=1, source_target_pairs={{0,1},{1,0},{2,3},{3,2},{4,5},{5,4},{6,7},{7,6},{8,9},{9,8},{10,11... | collective-permute-start | bytes 294920 | tf_op jit(solution)/shard_map/ppermute | solution.py:597
  15.1 22.8 %copy-start.64 = (s32[48]{0:T(128)S(1)}, s32[48]{0:T(128)}, u32[]{:S(2)}) copy-start(s32[48]{0:T(128)} %param.15) | copy-start | bytes 580
  15.1 10.6 %collective-permute-start.2 = (bf16[3,64,256]{2,1,0:T(8,128)(2,1)}, bf16[3,64,256]{2,1,0:T(8,128)(2,1)S(1)}, u32[]{:S(2)}, u32[]{:S(2)}) collective-permute-start(bf16[3,64,256]{2,1,0:T(8,128)(2,1)} %get-tuple-element.97), channel_id=1, source_target_pairs={{0,2},{1,3},{2,0},{3,1},{4,6},{5,7},{6,4},{7,5},{8,10},{9,11},{10,... | collective-permute-start | bytes 294920 | tf_op jit(solution)/shard_map/ppermute | solution.py:597
  17.7 8.0 %collective-permute-start.3 = (bf16[3,64,256]{2,1,0:T(8,128)(2,1)}, bf16[3,64,256]{2,1,0:T(8,128)(2,1)S(1)}, u32[]{:S(2)}, u32[]{:S(2)}) collective-permute-start(bf16[3,64,256]{2,1,0:T(8,128)(2,1)} %get-tuple-element.98), channel_id=1, source_target_pairs={{0,3},{1,2},{2,1},{3,0},{4,7},{5,6},{6,5},{7,4},{8,11},{9,10},{10,... | collective-permute-start | bytes 294920 | tf_op jit(solution)/shard_map/ppermute | solution.py:597
  17.7 114.2 %collective-permute-start = (bf16[4,320,384]{2,1,0:T(8,128)(2,1)}, bf16[4,320,384]{2,1,0:T(8,128)(2,1)}, u32[]{:S(2)}, u32[]{:S(2)}) collective-permute-start(bf16[4,320,384]{2,1,0:T(8,128)(2,1)} %get-tuple-element.91), channel_id=1, source_target_pairs={{0,4},{4,0},{8,12},{12,8},{16,20},{20,16},{24,28},{28,24},{1,5},{5... | collective-permute-start | bytes 2949128 | tf_op jit(solution)/shard_map/ppermute | solution.py:591
  17.7 40.5 %collective-permute-start.7 = (bf16[3,64,256]{2,1,0:T(8,128)(2,1)}, bf16[3,64,256]{2,1,0:T(8,128)(2,1)}, u32[]{:S(2)}, u32[]{:S(2)}) collective-permute-start(bf16[3,64,256]{2,1,0:T(8,128)(2,1)} %get-tuple-element.109), channel_id=1, source_target_pairs={{0,1},{1,0},{2,3},{3,2},{4,5},{5,4},{6,7},{7,6},{8,9},{9,8},{10,11... | collective-permute-start | bytes 294920 | tf_op jit(solution)/shard_map/ppermute | solution.py:597
  27.8 21.4 %copy-start.3 = (bf16[384,1024]{1,0:T(8,128)(2,1)S(1)}, bf16[384,1024]{1,0:T(8,128)(2,1)}, u32[]{:S(2)}) copy-start(bf16[384,1024]{1,0:T(8,128)(2,1)} %get-tuple-element.94.norm_ref) | copy-start | bytes 2359300
  27.8 21.4 %copy-start.28 = (bf16[6,4,16,256]{3,2,1,0:T(8,128)(2,1)S(1)}, bf16[6,4,16,256]{3,2,1,0:T(8,128)(2,1)}, u32[]{:S(2)}) copy-start(bf16[6,4,16,256]{3,2,1,0:T(8,128)(2,1)} %param.13) | copy-start | bytes 589828
  27.8 21.4 %copy-start.52 = (f32[256]{0:T(256)S(1)}, f32[256]{0:T(256)}, u32[]{:S(2)}) copy-start(f32[256]{0:T(256)} %param.22) | copy-start | bytes 3076
  33.5 5.8 %collective-permute-start.4 = (bf16[3,64,256]{2,1,0:T(8,128)(2,1)}, bf16[3,64,256]{2,1,0:T(8,128)(2,1)S(1)}, u32[]{:S(2)}, u32[]{:S(2)}) collective-permute-start(bf16[3,64,256]{2,1,0:T(8,128)(2,1)} %get-tuple-element.100), channel_id=1, source_target_pairs={{0,1},{1,0},{2,3},{3,2},{4,5},{5,4},{6,7},{7,6},{8,9},{9,8},{10,11... | collective-permute-start | bytes 294920 | tf_op jit(solution)/shard_map/ppermute | solution.py:597
  35.1 12.1 %collective-permute-start.5 = (bf16[3,64,256]{2,1,0:T(8,128)(2,1)}, bf16[3,64,256]{2,1,0:T(8,128)(2,1)}, u32[]{:S(2)}, u32[]{:S(2)}) collective-permute-start(bf16[3,64,256]{2,1,0:T(8,128)(2,1)} %get-tuple-element.101), channel_id=1, source_target_pairs={{0,2},{1,3},{2,0},{3,1},{4,6},{5,7},{6,4},{7,5},{8,10},{9,11},{10,... | collective-permute-start | bytes 294920 | tf_op jit(solution)/shard_map/ppermute | solution.py:597
  36.6 12.6 %collective-permute-start.6 = (bf16[3,64,256]{2,1,0:T(8,128)(2,1)}, bf16[3,64,256]{2,1,0:T(8,128)(2,1)}, u32[]{:S(2)}, u32[]{:S(2)}) collective-permute-start(bf16[3,64,256]{2,1,0:T(8,128)(2,1)} %get-tuple-element.102), channel_id=1, source_target_pairs={{0,3},{1,2},{2,1},{3,0},{4,7},{5,6},{6,5},{7,4},{8,11},{9,10},{10,... | collective-permute-start | bytes 294920 | tf_op jit(solution)/shard_map/ppermute | solution.py:597
  39.3 18.9 %collective-permute-start.8 = (bf16[3,64,256]{2,1,0:T(8,128)(2,1)}, bf16[3,64,256]{2,1,0:T(8,128)(2,1)}, u32[]{:S(2)}, u32[]{:S(2)}) collective-permute-start(bf16[3,64,256]{2,1,0:T(8,128)(2,1)} %get-tuple-element.110), channel_id=1, source_target_pairs={{0,2},{1,3},{2,0},{3,1},{4,6},{5,7},{6,4},{7,5},{8,10},{9,11},{10,... | collective-permute-start | bytes 294920 | tf_op jit(solution)/shard_map/ppermute | solution.py:597
  47.2 11.0 %collective-permute-start.9 = (bf16[3,64,256]{2,1,0:T(8,128)(2,1)}, bf16[3,64,256]{2,1,0:T(8,128)(2,1)}, u32[]{:S(2)}, u32[]{:S(2)}) collective-permute-start(bf16[3,64,256]{2,1,0:T(8,128)(2,1)} %get-tuple-element.111), channel_id=1, source_target_pairs={{0,3},{1,2},{2,1},{3,0},{4,7},{5,6},{6,5},{7,4},{8,11},{9,10},{10,... | collective-permute-start | bytes 294920 | tf_op jit(solution)/shard_map/ppermute | solution.py:597
  54.5 27.9 %all-to-all-start = ((bf16[4,3,64,256]{3,2,1,0:T(8,128)(2,1)}), bf16[4,3,64,256]{3,2,1,0:T(8,128)(2,1)S(1)}, u32[]{:S(2)}, u32[]{:S(2)}) async-start(bf16[4,3,64,256]{3,2,1,0:T(8,128)(2,1)} %copy-done.36), calls=%async_computation | async-start | bytes 786432 | tf_op jit(solution)/shard_map/all_to_all | solution.py:798
  67.3 5.0 %collective-permute-start.10 = (bf16[3,64,256]{2,1,0:T(8,128)(2,1)S(1)}, bf16[3,64,256]{2,1,0:T(8,128)(2,1)S(1)}, u32[]{:S(2)}, u32[]{:S(2)}) collective-permute-start(bf16[3,64,256]{2,1,0:T(8,128)(2,1)S(1)} %get-tuple-element.113), channel_id=1, source_target_pairs={{0,1},{1,0},{2,3},{3,2},{4,5},{5,4},{6,7},{7,6},{8,9},{9,8},{10,11... | collective-permute-start | bytes 294920 | tf_op jit(solution)/shard_map/ppermute | solution.py:597
  69.3 6.6 %collective-permute-start.11 = (bf16[3,64,256]{2,1,0:T(8,128)(2,1)S(1)}, bf16[3,64,256]{2,1,0:T(8,128)(2,1)S(1)}, u32[]{:S(2)}, u32[]{:S(2)}) collective-permute-start(bf16[3,64,256]{2,1,0:T(8,128)(2,1)S(1)} %get-tuple-element.114), channel_id=1, source_target_pairs={{0,2},{1,3},{2,0},{3,1},{4,6},{5,7},{6,4},{7,5},{8,10},{9,11},{10,... | collective-permute-start | bytes 294920 | tf_op jit(solution)/shard_map/ppermute | solution.py:597
  71.7 6.4 %collective-permute-start.12 = (bf16[3,64,256]{2,1,0:T(8,128)(2,1)S(1)}, bf16[3,64,256]{2,1,0:T(8,128)(2,1)S(1)}, u32[]{:S(2)}, u32[]{:S(2)}) collective-permute-start(bf16[3,64,256]{2,1,0:T(8,128)(2,1)S(1)} %get-tuple-element.115), channel_id=1, source_target_pairs={{0,3},{1,2},{2,1},{3,0},{4,7},{5,6},{6,5},{7,4},{8,11},{9,10},{10,... | collective-permute-start | bytes 294920 | tf_op jit(solution)/shard_map/ppermute | solution.py:597
  83.2 22.5 %all-to-all-start.1 = ((bf16[4,3,64,256]{3,2,1,0:T(8,128)(2,1)}), bf16[4,3,64,256]{3,2,1,0:T(8,128)(2,1)S(1)}, u32[]{:S(2)}, u32[]{:S(2)}) async-start(bf16[4,3,64,256]{3,2,1,0:T(8,128)(2,1)} %copy-done.37), calls=%async_computation.1 | async-start | bytes 786432 | tf_op jit(solution)/shard_map/all_to_all | solution.py:798
  100.6 16.0 %collective-permute-start.13 = (bf16[3,64,256]{2,1,0:T(8,128)(2,1)}, bf16[3,64,256]{2,1,0:T(8,128)(2,1)}, u32[]{:S(2)}, u32[]{:S(2)}) collective-permute-start(bf16[3,64,256]{2,1,0:T(8,128)(2,1)} %get-tuple-element.121), channel_id=1, source_target_pairs={{0,1},{1,0},{2,3},{3,2},{4,5},{5,4},{6,7},{7,6},{8,9},{9,8},{10,11... | collective-permute-start | bytes 294920 | tf_op jit(solution)/shard_map/ppermute | solution.py:597
  102.4 17.5 %collective-permute-start.14 = (bf16[3,64,256]{2,1,0:T(8,128)(2,1)}, bf16[3,64,256]{2,1,0:T(8,128)(2,1)}, u32[]{:S(2)}, u32[]{:S(2)}) collective-permute-start(bf16[3,64,256]{2,1,0:T(8,128)(2,1)} %get-tuple-element.122), channel_id=1, source_target_pairs={{0,2},{1,3},{2,0},{3,1},{4,6},{5,7},{6,4},{7,5},{8,10},{9,11},{10,... | collective-permute-start | bytes 294920 | tf_op jit(solution)/shard_map/ppermute | solution.py:597
  104.8 15.4 %collective-permute-start.15 = (bf16[3,64,256]{2,1,0:T(8,128)(2,1)}, bf16[3,64,256]{2,1,0:T(8,128)(2,1)}, u32[]{:S(2)}, u32[]{:S(2)}) collective-permute-start(bf16[3,64,256]{2,1,0:T(8,128)(2,1)} %get-tuple-element.123), channel_id=1, source_target_pairs={{0,3},{1,2},{2,1},{3,0},{4,7},{5,6},{6,5},{7,4},{8,11},{9,10},{10,... | collective-permute-start | bytes 294920 | tf_op jit(solution)/shard_map/ppermute | solution.py:597
  115.8 13.1 %collective-permute-start.16 = (bf16[3,64,256]{2,1,0:T(8,128)(2,1)}, bf16[3,64,256]{2,1,0:T(8,128)(2,1)S(1)}, u32[]{:S(2)}, u32[]{:S(2)}) collective-permute-start(bf16[3,64,256]{2,1,0:T(8,128)(2,1)} %get-tuple-element.135), channel_id=1, source_target_pairs={{0,1},{1,0},{2,3},{3,2},{4,5},{5,4},{6,7},{7,6},{8,9},{9,8},{10,11... | collective-permute-start | bytes 294920 | tf_op jit(solution)/shard_map/ppermute | solution.py:597
  116.7 12.2 %collective-permute-start.17 = (bf16[3,64,256]{2,1,0:T(8,128)(2,1)}, bf16[3,64,256]{2,1,0:T(8,128)(2,1)S(1)}, u32[]{:S(2)}, u32[]{:S(2)}) collective-permute-start(bf16[3,64,256]{2,1,0:T(8,128)(2,1)} %get-tuple-element.136), channel_id=1, source_target_pairs={{0,2},{1,3},{2,0},{3,1},{4,6},{5,7},{6,4},{7,5},{8,10},{9,11},{10,... | collective-permute-start | bytes 294920 | tf_op jit(solution)/shard_map/ppermute | solution.py:597
  119.9 9.0 %collective-permute-start.18 = (bf16[3,64,256]{2,1,0:T(8,128)(2,1)}, bf16[3,64,256]{2,1,0:T(8,128)(2,1)S(1)}, u32[]{:S(2)}, u32[]{:S(2)}) collective-permute-start(bf16[3,64,256]{2,1,0:T(8,128)(2,1)} %get-tuple-element.137), channel_id=1, source_target_pairs={{0,3},{1,2},{2,1},{3,0},{4,7},{5,6},{6,5},{7,4},{8,11},{9,10},{10,... | collective-permute-start | bytes 294920 | tf_op jit(solution)/shard_map/ppermute | solution.py:597
  123.6 20.0 %all-to-all-start.2 = ((bf16[8,192,256]{2,1,0:T(8,128)(2,1)}), bf16[8,192,256]{2,1,0:T(8,128)(2,1)}, u32[]{:S(2)}, u32[]{:S(2)}) async-start(bf16[8,192,256]{2,1,0:T(8,128)(2,1)} %pad_maximum_fusion), calls=%async_computation.2 | async-start | bytes 1572864 | tf_op jit(solution)/shard_map/all_to_all | solution.py:667
  128.5 3.4 %collective-permute-start.19 = (bf16[192,1024]{1,0:T(8,128)(2,1)S(1)}, bf16[192,1024]{1,0:T(8,128)(2,1)S(1)}, u32[]{:S(2)}, u32[]{:S(2)}) collective-permute-start(bf16[192,1024]{1,0:T(8,128)(2,1)S(1)} %get-tuple-element.133.refs_2_), channel_id=1, source_target_pairs={{0,4},{4,0},{8,12},{12,8},{16,20},{20,16},{24,28},{28,24},{1,5},{5... | collective-permute-start | bytes 1179656 | tf_op jit(solution)/shard_map/ppermute | solution.py:591
  130.4 1.8 collective-permute-start.20
  136.3 26.6 %collective-permute-start.21 = (bf16[2,320,512]{2,1,0:T(8,128)(2,1)S(1)}, bf16[2,320,512]{2,1,0:T(8,128)(2,1)}, u32[]{:S(2)}, u32[]{:S(2)}) collective-permute-start(bf16[2,320,512]{2,1,0:T(8,128)(2,1)S(1)} %get-tuple-element.154), channel_id=1, source_target_pairs={{0,8},{4,12},{8,0},{12,4},{16,24},{20,28},{24,16},{28,20},{1,9},{5... | collective-permute-start | bytes 1966088 | tf_op jit(solution)/shard_map/ppermute | solution.py:591
  138.0 26.8 %collective-permute-start.23 = (bf16[2,320,512]{2,1,0:T(8,128)(2,1)S(1)}, bf16[2,320,512]{2,1,0:T(8,128)(2,1)}, u32[]{:S(2)}, u32[]{:S(2)}) collective-permute-start(bf16[2,320,512]{2,1,0:T(8,128)(2,1)S(1)} %get-tuple-element.156), channel_id=1, source_target_pairs={{0,16},{4,20},{8,24},{12,28},{16,0},{20,4},{24,8},{28,12},{1,17},{... | collective-permute-start | bytes 1966088 | tf_op jit(solution)/shard_map/ppermute | solution.py:591
  145.7 10.0 %collective-permute-start.27 = (bf16[224,256]{1,0:T(8,128)(2,1)}, bf16[224,256]{1,0:T(8,128)(2,1)S(1)}, u32[]{:S(2)}, u32[]{:S(2)}) collective-permute-start(bf16[224,256]{1,0:T(8,128)(2,1)} %pad_maximum_fusion.3), channel_id=1, source_target_pairs={{0,3},{1,2},{2,1},{3,0},{4,7},{5,6},{6,5},{7,4},{8,11},{9,10},{10,... | collective-permute-start | bytes 344072 | tf_op jit(solution)/shard_map/ppermute | solution.py:597
  149.3 8.8 %collective-permute-start.26 = (bf16[224,256]{1,0:T(8,128)(2,1)}, bf16[224,256]{1,0:T(8,128)(2,1)}, u32[]{:S(2)}, u32[]{:S(2)}) collective-permute-start(bf16[224,256]{1,0:T(8,128)(2,1)} %pad_maximum_fusion.3), channel_id=1, source_target_pairs={{0,2},{1,3},{2,0},{3,1},{4,6},{5,7},{6,4},{7,5},{8,10},{9,11},{10,... | collective-permute-start | bytes 344072 | tf_op jit(solution)/shard_map/ppermute | solution.py:597
  149.3 8.8 %collective-permute-start.25 = (bf16[224,256]{1,0:T(8,128)(2,1)}, bf16[224,256]{1,0:T(8,128)(2,1)}, u32[]{:S(2)}, u32[]{:S(2)}) collective-permute-start(bf16[224,256]{1,0:T(8,128)(2,1)} %pad_maximum_fusion.3), channel_id=1, source_target_pairs={{0,1},{1,0},{2,3},{3,2},{4,5},{5,4},{6,7},{7,6},{8,9},{9,8},{10,11... | collective-permute-start | bytes 344072 | tf_op jit(solution)/shard_map/ppermute | solution.py:597
  152.2 27.6 %all-to-all-start.3 = ((bf16[8,64,256]{2,1,0:T(8,128)(2,1)}), bf16[8,64,256]{2,1,0:T(8,128)(2,1)S(1)}, u32[]{:S(2)}, u32[]{:S(2)}) async-start(bf16[8,64,256]{2,1,0:T(8,128)(2,1)} %broadcast_select_fusion), calls=%async_computation.3 | async-start | bytes 524288 | tf_op jit(solution)/shard_map/all_to_all | solution.py:746
  164.2 9.5 %collective-permute-start.22 = (bf16[1,320,512]{2,1,0:T(8,128)(2,1)S(1)}, bf16[1,320,512]{2,1,0:T(8,128)(2,1)S(1)}, u32[]{:S(2)}, u32[]{:S(2)}) collective-permute-start(bf16[1,320,512]{2,1,0:T(8,128)(2,1)S(1)} %slice_bitcast_fusion), channel_id=1, source_target_pairs={{0,16},{4,20},{8,24},{12,28},{16,0},{20,4},{24,8},{28,12},{1,17},{... | collective-permute-start | bytes 983048 | tf_op jit(solution)/shard_map/ppermute | solution.py:591
  166.1 9.2 %collective-permute-start.24 = (bf16[1,320,512]{2,1,0:T(8,128)(2,1)S(1)}, bf16[1,320,512]{2,1,0:T(8,128)(2,1)S(1)}, u32[]{:S(2)}, u32[]{:S(2)}) collective-permute-start(bf16[1,320,512]{2,1,0:T(8,128)(2,1)S(1)} %slice.127), channel_id=1, source_target_pairs={{0,8},{4,12},{8,0},{12,4},{16,24},{20,28},{24,16},{28,20},{1,9},{5... | collective-permute-start | bytes 983048 | tf_op jit(solution)/shard_map/ppermute | solution.py:591
  175.4 8.6 %collective-permute-start.31 = (bf16[448,256]{1,0:T(8,128)(2,1)S(1)}, bf16[448,256]{1,0:T(8,128)(2,1)S(1)}, u32[]{:S(2)}, u32[]{:S(2)}) collective-permute-start(bf16[448,256]{1,0:T(8,128)(2,1)S(1)} %fusion.7.refs_0_), channel_id=1, source_target_pairs={{0,8},{4,12},{8,0},{12,4},{16,24},{20,28},{24,16},{28,20},{1,9},{5... | collective-permute-start | bytes 688136 | tf_op jit(solution)/shard_map/ppermute | solution.py:645
  176.3 9.5 %collective-permute-start.33 = (bf16[448,256]{1,0:T(8,128)(2,1)S(1)}, bf16[448,256]{1,0:T(8,128)(2,1)S(1)}, u32[]{:S(2)}, u32[]{:S(2)}) collective-permute-start(bf16[448,256]{1,0:T(8,128)(2,1)S(1)} %fusion.7.refs_0_), channel_id=1, source_target_pairs={{0,16},{4,20},{8,24},{12,28},{16,0},{20,4},{24,8},{28,12},{1,17},{... | collective-permute-start | bytes 688136 | tf_op jit(solution)/shard_map/ppermute | solution.py:645
  177.5 10.0 %collective-permute-start.35 = (bf16[448,256]{1,0:T(8,128)(2,1)S(1)}, bf16[448,256]{1,0:T(8,128)(2,1)S(1)}, u32[]{:S(2)}, u32[]{:S(2)}) collective-permute-start(bf16[448,256]{1,0:T(8,128)(2,1)S(1)} %fusion.7.refs_0_), channel_id=1, source_target_pairs={{0,24},{4,28},{8,16},{12,20},{16,8},{20,12},{24,0},{28,4},{1,25},{... | collective-permute-start | bytes 688136 | tf_op jit(solution)/shard_map/ppermute | solution.py:645
  179.1 8.4 %collective-permute-start.28 = (bf16[2,80,1024]{2,1,0:T(8,128)(2,1)S(1)}, bf16[2,80,1024]{2,1,0:T(8,128)(2,1)S(1)}, u32[]{:S(2)}, u32[]{:S(2)}) collective-permute-start(bf16[2,80,1024]{2,1,0:T(8,128)(2,1)S(1)} %dynamic-slice_bitcast_fusion), channel_id=1, source_target_pairs={{0,1},{1,0},{2,3},{3,2},{4,5},{5,4},{6,7},{7,6},{8,9},{9,8},{10,11... | collective-permute-start | bytes 983048 | tf_op jit(solution)/shard_map/ppermute | solution.py:635
  180.4 10.7 %collective-permute-start.30 = (bf16[448,256]{1,0:T(8,128)(2,1)S(1)}, bf16[448,256]{1,0:T(8,128)(2,1)S(1)}, u32[]{:S(2)}, u32[]{:S(2)}) collective-permute-start(bf16[448,256]{1,0:T(8,128)(2,1)S(1)} %fusion.7.refs_0_), channel_id=1, source_target_pairs={{0,4},{4,0},{8,12},{12,8},{16,20},{20,16},{24,28},{28,24},{1,5},{5... | collective-permute-start | bytes 688136 | tf_op jit(solution)/shard_map/ppermute | solution.py:591
  184.0 7.1 %collective-permute-start.32 = (bf16[448,256]{1,0:T(8,128)(2,1)S(1)}, bf16[448,256]{1,0:T(8,128)(2,1)S(1)}, u32[]{:S(2)}, u32[]{:S(2)}) collective-permute-start(bf16[448,256]{1,0:T(8,128)(2,1)S(1)} %collective-permute-done.31.refs_2_), channel_id=1, source_target_pairs={{0,4},{4,0},{8,12},{12,8},{16,20},{20,16},{24,28},{28,24},{1,5},{5... | collective-permute-start | bytes 688136 | tf_op jit(solution)/shard_map/ppermute | solution.py:591
  185.9 5.2 %collective-permute-start.34 = (bf16[448,256]{1,0:T(8,128)(2,1)S(1)}, bf16[448,256]{1,0:T(8,128)(2,1)S(1)}, u32[]{:S(2)}, u32[]{:S(2)}) collective-permute-start(bf16[448,256]{1,0:T(8,128)(2,1)S(1)} %collective-permute-done.33.refs_4_), channel_id=1, source_target_pairs={{0,4},{4,0},{8,12},{12,8},{16,20},{20,16},{24,28},{28,24},{1,5},{5... | collective-permute-start | bytes 688136 | tf_op jit(solution)/shard_map/ppermute | solution.py:591
  187.5 3.6 %collective-permute-start.36 = (bf16[448,256]{1,0:T(8,128)(2,1)S(1)}, bf16[448,256]{1,0:T(8,128)(2,1)S(1)}, u32[]{:S(2)}, u32[]{:S(2)}) collective-permute-start(bf16[448,256]{1,0:T(8,128)(2,1)S(1)} %collective-permute-done.35.refs_6_), channel_id=1, source_target_pairs={{0,4},{4,0},{8,12},{12,8},{16,20},{20,16},{24,28},{28,24},{1,5},{5... | collective-permute-start | bytes 688136 | tf_op jit(solution)/shard_map/ppermute | solution.py:591
  187.6 11.1 %collective-permute-start.29 = (bf16[1,80,1024]{2,1,0:T(8,128)(2,1)S(1)}, bf16[1,80,1024]{2,1,0:T(8,128)(2,1)S(1)}, u32[]{:S(2)}, u32[]{:S(2)}) collective-permute-start(bf16[1,80,1024]{2,1,0:T(8,128)(2,1)S(1)} %constant_dynamic-slice_fusion), channel_id=1, source_target_pairs={{0,2},{1,3},{2,0},{3,1},{4,6},{5,7},{6,4},{7,5},{8,10},{9,11},{10,... | collective-permute-start | bytes 491528 | tf_op jit(solution)/shard_map/ppermute | solution.py:635
  (62 other events, 240.1 us)

commit v6 on v5

--- a/solution.py
+++ b/solution.py
@@ -13,6 +13,7 @@
 VMEM_BYTES = 24 * 1024 * 1024
 SLOTS = 6
 SHARD, FIRST_ROW, GROUP, SIDES = 0, 1, 2, 3
+ROUTES = 3
 HALF = jnp.bfloat16
 FULL = jnp.float32
 
@@ -306,7 +307,7 @@
     scale_root = float(np.sqrt(np.float32(samples)))
 
     def body(scal_ref, emb_ref, norm_ref, tgt_ref, w_ref, b_ref, *refs):
-        mix_refs, (pred_ref, res_ref, all_ref, up_ref, bias_ref, held) = refs[:shards], refs[shards:]
+        mix_refs, (pred_ref, res_ref, up_ref, bias_ref, held) = refs[:shards], refs[shards:]
         fill_lanes(scal_ref, mix_refs, held)
         side, valid = token_sides(scal_ref, first, count, per_sample, cells)
         updated = (emb_ref[...].astype(FULL) + norm_ref[...].astype(FULL) + held[...].astype(FULL)).astype(HALF)
@@ -315,8 +316,6 @@
         scale = 2.0 / (side.astype(FULL) * scale_root)
         residual = (scale * valid * (output - tgt_ref[...].astype(FULL))).astype(HALF)
         res_ref[...] = residual.reshape(res_ref.shape)
-        for z in range(shards):
-            all_ref[z] = residual.reshape(res_ref.shape)
         up_ref[...] = updated
         total = jnp.sum(residual.astype(FULL), axis=0, keepdims=True)
         bias_ref[...] = jnp.broadcast_to(total, bias_ref.shape)
@@ -335,19 +334,12 @@
                 whole((1, outs)),
             ]
             + [whole(mixed[0].shape)] * shards,
-            out_specs=[
-                whole(token_shape),
-                whole(token_shape),
-                whole((shards,) + token_shape),
-                whole((rows, width)),
-                whole((8, outs)),
-            ],
+            out_specs=[whole(token_shape), whole(token_shape), whole((rows, width)), whole((8, outs))],
             scratch_shapes=[pltpu.VMEM((rows, width), HALF)],
         ),
         out_shape=[
             jax.ShapeDtypeStruct(token_shape, HALF),
             jax.ShapeDtypeStruct(token_shape, HALF),
-            jax.ShapeDtypeStruct((shards,) + token_shape, HALF),
             jax.ShapeDtypeStruct((rows, width), HALF),
             jax.ShapeDtypeStruct((8, outs), FULL),
         ],
@@ -383,7 +375,8 @@
 
 
 def spectral_back_chunk(scal, table, factors, residual, head_w, spec_w, saved, first, before, last):
-    shards, count, per_sample, outs = residual.shape
+    shards = len(residual)
+    count, per_sample, outs = residual[0].shape
     size = shards * per_sample
     width = spec_w.shape[-1]
     wide = 2 * width
@@ -394,7 +387,7 @@
     has_before = before is not None
 
     def body(scal_ref, t_ref, h_ref, w_ref, spec_ref, hid_ref, fil_ref, *refs):
-        in_ref, refs = refs[0], refs[1:]
+        ins, refs = refs[:shards], refs[shards:]
         if has_before:
             (old_ref, old_bias_ref), refs = refs[:2], refs[2:]
         pieces, (grad_ref, bias_ref, weights, held, gathered) = refs[:shards], refs[shards:]
@@ -415,8 +408,7 @@
             grad_ref[at * width : (at + 1) * width] = jnp.concatenate([real, imag], axis=1).astype(HALF)
 
         complex_weights(w_ref, weights, blocks, width)
-        for z in range(shards):
-            gathered[:, z * per_sample : (z + 1) * per_sample, :] = in_ref[z]
+        fill_rows(scal_ref, ins, gathered)
         levels = [scal_ref[SIDES + SLOTS + first + i] for i in range(count)]
         updated_grad = dot_nt(gathered[...].reshape(count * size, outs), h_ref[...]).astype(HALF)
         entries = []
@@ -456,7 +448,7 @@
                 pl.BlockSpec((2, 2, blocks, width, width), lambda i, s: (0, 0, s[SHARD], 0, 0)),
             ]
             + [whole(saved[0].shape)] * 3
-            + [whole(residual.shape)]
+            + [whole(residual[0].shape)] * shards
             + ([whole(raw_shape), whole(bias_shape)] if has_before else []),
             out_specs=[whole(piece)] * shards + [whole(grad_out.shape), whole(bias_shape)],
             scratch_shapes=[
@@ -472,7 +464,7 @@
             flops=count * size * share * size * 20, bytes_accessed=count * size * share * 16, transcendentals=0
         ),
         name="spectral_back",
-    )(scal, table, head_w, spec_w, *saved, residual, *(before or ()))
+    )(scal, table, head_w, spec_w, *saved, *residual, *(before or ()))
     return result[:shards], result[shards:]
 
 
@@ -649,31 +641,112 @@
 
 
 def hi_lo(values):
-    high = lax.optimization_barrier(values.astype(HALF))
-    return jnp.concatenate([high, (values - high.astype(FULL)).astype(HALF)], axis=-2)
+    high = values.astype(HALF)
+    return jnp.concatenate([high, (values - high.astype(FULL)).astype(HALF)], axis=0)
 
 
 def from_hi_lo(values):
-    half = values.shape[-2] // 2
+    half = values.shape[0] // 2
     values = values.astype(FULL)
-    return values[..., :half, :] + values[..., half:, :]
-
-
-def sum_over_groups(head_grad, spec_grad, groups):
+    return values[:half] + values[half:]
+
+
+def one_step(body, name, operands, out_shape):
+    return pl.pallas_call(
+        body,
+        grid_spec=pltpu.PrefetchScalarGridSpec(
+            num_scalar_prefetch=1,
+            grid=(1,),
+            in_specs=[whole(o.shape) for o in operands[1:]],
+            out_specs=[whole(o.shape) for o in out_shape],
+        ),
+        out_shape=out_shape,
+        compiler_params=params(),
+        name=name,
+    )(*operands)
+
+
+def packed(routes, head_grad, spec_grad, predicted, groups):
     outs = head_grad.shape[1]
-    packed = jnp.concatenate(
-        [head_grad.reshape(groups, -1, outs), spec_grad.reshape(groups, -1, outs)], axis=1
+    head_rows, spec_rows = head_grad.shape[0] // groups, spec_grad.shape[0] // groups
+    count, per_sample, _ = predicted[0].shape
+
+    def body(routes_ref, head_ref, spec_ref, *refs):
+        pred_refs, out_ref = refs[:-1], refs[-1]
+        for g in range(groups):
+            out_ref[g, :head_rows] = head_ref[g * head_rows : (g + 1) * head_rows]
+            out_ref[g, head_rows : head_rows + spec_rows] = spec_ref[g * spec_rows : (g + 1) * spec_rows]
+            chosen = routes_ref[ROUTES + g]
+            for c, ref in enumerate(pred_refs):
+
+                @pl.when(chosen // count == c)
+                def _(g=g, c=c, ref=ref, chosen=chosen):
+                    out_ref[g, head_rows + spec_rows :] = ref[chosen - c * count]
+
+    shape = (groups, head_rows + spec_rows + per_sample, outs)
+    return one_step(
+        body, "packed", (routes, head_grad, spec_grad, *predicted), [jax.ShapeDtypeStruct(shape, HALF)]
+    )[0]
+
+
+def group_sums(routes, moved, spec_bias, head_sums, row_sums, slot_count, per_sample):
+    groups, rows, outs = moved.shape
+    weight_rows = rows - per_sample
+    own_rows = spec_bias.shape[0]
+    chunks = len(head_sums)
+    parts = row_sums[0].shape[1] // outs
+    spare = 16 - own_rows - 2 * parts - 1
+
+    def body(routes_ref, moved_ref, bias_ref, *refs):
+        head_refs, row_refs, (out_ref, pred_ref) = refs[:chunks], refs[chunks : 2 * chunks], refs[2 * chunks :]
+        total = moved_ref[0, :weight_rows].astype(FULL)
+        for g in range(1, groups):
+            total = total + moved_ref[g, :weight_rows].astype(FULL)
+        out_ref[:weight_rows] = total.astype(HALF)
+        lines = [bias_ref[...]]
+        for row in (0, 4):
+            line = sum(ref[row : row + 1] for ref in row_refs)
+            lines += [line[:, i * outs : (i + 1) * outs] for i in range(parts)]
+        lines += [sum(ref[0:1] for ref in head_refs), jnp.zeros((spare, outs), FULL)]
+        out_ref[weight_rows:] = hi_lo(jnp.concatenate(lines, axis=0))
+        for i in range(slot_count):
+            pred_ref[i] = moved_ref[routes_ref[ROUTES + groups + i], weight_rows:]
+
+    return one_step(
+        body,
+        "group_sums",
+        (routes, moved, spec_bias, *head_sums, *row_sums),
+        [
+            jax.ShapeDtypeStruct((weight_rows + 32, outs), HALF),
+            jax.ShapeDtypeStruct((slot_count, per_sample, outs), HALF),
+        ],
     )
-    return lax.all_to_all(packed, "grp", split_axis=0, concat_axis=0, tiled=True)
-
-
-def over_shards(moved, small, head_rows, shards, shard_at):
-    summed = jnp.sum(moved.astype(FULL), axis=0).astype(HALF)
-    rows = across([jnp.concatenate([summed, hi_lo(small)], axis=0)] * shards)
-    head_part = sum(r[:head_rows].astype(FULL) for r in rows).astype(HALF)
-    order = jnp.bitwise_xor(jnp.arange(shards, dtype=jnp.int32), shard_at)
-    small = jnp.take(jnp.stack([from_hi_lo(r[summed.shape[0] :]) for r in rows]), order, axis=0)
-    return head_part, [r[head_rows : summed.shape[0]] for r in rows], small
+
+
+def shard_sums(routes, rows, head_rows, spec_rows, own_rows):
+    shards = len(rows)
+    outs = rows[0].shape[1]
+    small_rows = 32
+
+    def body(routes_ref, *refs):
+        ins, out_ref = refs[:-1], refs[-1]
+        total = sum(ref[:head_rows].astype(FULL) for ref in ins)
+        out_ref[:head_rows] = total.astype(HALF)
+        for k, ref in enumerate(ins):
+            at = head_rows + k * spec_rows
+            out_ref[at : at + spec_rows] = ref[head_rows : head_rows + spec_rows]
+        smalls = [from_hi_lo(ref[head_rows + spec_rows :]) for ref in ins]
+        lines = []
+        for z in range(shards):
+            here = [jnp.bitwise_xor(routes_ref[SHARD], k) == z for k in range(shards)]
+            lines.append(sum(jnp.where(h, v[:own_rows], 0.0) for h, v in zip(here, smalls)))
+        lines.append(sum(v[own_rows:] for v in smalls))
+        have = shards * own_rows + 16 - own_rows
+        lines.append(jnp.zeros((small_rows - have, outs), FULL))
+        out_ref[head_rows + shards * spec_rows :] = hi_lo(jnp.concatenate(lines, axis=0))
+
+    shape = (head_rows + shards * spec_rows + 2 * small_rows, outs)
+    return one_step(body, "shard_sums", (routes, *rows), [jax.ShapeDtypeStruct(shape, HALF)])[0]
 
 
 def assembled(scal, gathered, head_rows, shards, blocks, width):
@@ -738,18 +811,15 @@
     )(scal, *gathered)
 
 
-def route_predictions(predicted, dest_group, group_at, groups, slot_count):
+def prediction_routes(dest_group, group_at, groups, slot_count):
     own_dest = lax.dynamic_slice_in_dim(dest_group, group_at * slot_count, slot_count)
-    matches = own_dest[None, :] == jnp.arange(groups, dtype=jnp.int32)[:, None]
-    chosen = jnp.sum(jnp.where(matches, jnp.arange(slot_count, dtype=jnp.int32)[None, :], 0), axis=1)
-    outgoing = jnp.take(predicted, chosen, axis=0)
-    moved = lax.all_to_all(outgoing, "grp", split_axis=0, concat_axis=0, tiled=True)
     loaders = jnp.arange(groups, dtype=jnp.int32)
+    slots = jnp.arange(slot_count, dtype=jnp.int32)
+    chosen = jnp.sum(jnp.where(own_dest[None, :] == loaders[:, None], slots[None, :], 0), axis=1)
     holds = jnp.any(dest_group.reshape(groups, slot_count) == group_at, axis=1)
     rank = jnp.sum(jnp.where(holds[None, :] & (loaders[None, :] < loaders[:, None]), 1, 0), axis=1)
-    slots = jnp.arange(slot_count, dtype=jnp.int32)
     sources = jnp.sum(jnp.where(holds[None, :] & (rank[None, :] == slots[:, None]), loaders[None, :], 0), axis=1)
-    return jnp.take(moved, sources, axis=0)
+    return jnp.concatenate([chosen, sources]).astype(jnp.int32)
 
 
 def on_device(
@@ -769,7 +839,9 @@
 
     sides = lax.dynamic_slice_in_dim(grid_side, group_at * slot_count, slot_count)
     level = jnp.where(sides == cells, 0, jnp.where(sides == cells // 2, 1, 2)).astype(jnp.int32)
-    scal = jnp.concatenate([jnp.stack([shard_at, shard_at * row_count, group_at]), sides, level])
+    place = jnp.stack([shard_at, shard_at * row_count, group_at])
+    scal = jnp.concatenate([place, sides, level])
+    routes = jnp.concatenate([place, prediction_routes(dest_group, group_at, groups, slot_count)])
     table_values, factors = dft_tables(cells)
     table = jnp.asarray(table_values)
     flat_patches = patches.reshape(-1, depth)
@@ -780,7 +852,6 @@
         scal, flat_patches, embed_w, embed_b_row, gain_row, firsts, count, per_sample, cells, shards, groups
     )
     moved = [across(p) for p in pieces]
-    turned = [turned_keep, swap_bit(turned_send, 0, groups)]
     mixed, saved = [], []
     for first, values in zip(firsts, moved):
         out, rest = spectral_chunk(scal, table, factors, values, spec_w, spec_b, first)
@@ -788,21 +859,24 @@
         saved.append(rest)
     predicted, residual, updated, head_sums, gathered = [], [], [], [], []
     for first, mix in zip(firsts, mixed):
-        pred, res, copies, up, sums = head_chunk(
+        pred, res, up, sums = head_chunk(
             scal, embedded, normed, mix, flat_targets, head_w, head_b_row, first, samples, cells
         )
         predicted.append(pred)
         residual.append(res)
         updated.append(up)
-        head_sums.append(sums[0])
-        gathered.append(lax.all_to_all(copies, "fft", split_axis=0, concat_axis=0, tiled=True))
+        head_sums.append(sums)
+        gathered.append(across([res] * shards))
     head_grad, gathered[0] = lax.optimization_barrier((head_gradient(updated, residual), gathered[0]))
     spec_back, sums = [], None
     for first, res, rest in zip(firsts, gathered, saved):
         values, sums = spectral_back_chunk(
             scal, table, factors, res, head_w, spec_w, rest, first, sums, first == firsts[-1]
         )
+        if first == firsts[-1]:
+            values, turned_send = lax.optimization_barrier((values, turned_send))
         spec_back.append(across(values))
+    turned = [turned_keep, swap_bit(turned_send, 0, groups)]
     spec_grad, spec_bias = sums
     width = spec_w.shape[-1]
     blocks = spec_w.shape[2] // shards
@@ -812,7 +886,9 @@
         grad, row_sum = embedded_back_chunk(scal, embedded, stats, res, head_w, gain_row, back, first, cells)
         if first == firsts[0]:
             grad, head_grad, spec_grad = lax.optimization_barrier((grad, head_grad, spec_grad))
-            weight_sums = sum_over_groups(head_grad, spec_grad, groups)
+            weight_sums = lax.all_to_all(
+                packed(routes, head_grad, spec_grad, predicted, groups), "grp", split_axis=0, concat_axis=0, tiled=True
+            )
         own_grads.append(grad)
         other_grads.append(swap_bit(grad, 0, groups))
         row_sums.append(row_sum)
@@ -822,19 +898,12 @@
     top_bit = groups.bit_length() - 2
     received = [swap_bit(sent[0], 1, groups), swap_bit(sent[1], top_bit, groups)]
     kept = embed_grad_parts(scal, kept_turned, grads, groups, 0)
-    kept, weight_sums, predicted, row_sums = lax.optimization_barrier((kept, weight_sums, predicted, row_sums))
+    kept, weight_sums = lax.optimization_barrier((kept, weight_sums))
     ends = scatter_start(received, kept, groups)
-    predictions = route_predictions(
-        jnp.concatenate(predicted, axis=0), dest_group, group_at, groups, slot_count
-    ).reshape(targets.shape)
-    rows = sum(row_sums)
-    vectors = jnp.concatenate([rows[0].reshape(-1, outs), rows[4].reshape(-1, outs), sum(head_sums)[None]], axis=0)
-    own_rows, all_rows = spec_bias.shape[0], vectors.shape[0]
-    small = jnp.concatenate([spec_bias, vectors, jnp.zeros((16 - own_rows - all_rows, outs), FULL)], axis=0)
-    head_part, spec_parts, small = over_shards(weight_sums, small, head_rows, shards, shard_at)
-    small = jnp.concatenate([small[:, :own_rows].reshape(-1, outs), jnp.sum(small[:, own_rows:], axis=0)], axis=0)
-    small = jnp.concatenate([small, jnp.zeros((-small.shape[0] % 16, outs), FULL)], axis=0)
-    outgoing = jnp.concatenate([head_part, *spec_parts, hi_lo(small)], axis=0)
+    small, predictions = group_sums(routes, weight_sums, spec_bias, head_sums, row_sums, slot_count, per_sample)
+    predictions = predictions.reshape(targets.shape)
+    spec_rows = spec_grad.shape[0] // groups
+    outgoing = shard_sums(routes, across([small] * shards), head_rows, spec_rows, spec_bias.shape[0])
     ends, outgoing = lax.optimization_barrier((ends, outgoing))
     gathered = from_all_groups(outgoing, groups)
     embed_grad = scatter_end(ends, shards, shard_at)

time: 201 us -> 169 us (0.84)
  local copies, waits for them, and re-layouts: 37.3 us -> 1.89 us
  other arithmetic: 17.3 us -> 4.84 us
  waiting for transfers between devices: 41.9 us -> 50.3 us
  starting transfers between devices: 60 us -> 66.8 us
  Pallas kernels: 41.6 us -> 43.7 us
    unnamed x143 -> x32, local copies, waits for them, and re-layouts: 33.8 us -> 0.95 us
    ppermute x21 -> x27, starting transfers between devices: 33.2 us -> 49.6 us  [across(): lax.ppermute(pieces[k], 'fft', [(z, z ^ k) for z in range(shards)])]
    all_to_all x4 -> x1, starting transfers between devices: 14.7 us -> 3.98 us  [on_device(): lax.all_to_all(packed(routes, head_grad, spec_grad, predicted, groups), '...]
    ppermute x11, waiting for transfers between devices: 8.73 us -> 15.4 us  [swap_bit(): lax.ppermute(values, 'grp', [(g, g ^ 1 << bit) for g in range(groups)])]
    pallas_call x0 -> x3, Pallas kernels: none -> 3.58 us  [one_step(): pl.pallas_call(body, grid_spec=pltpu.PrefetchScalarGridSpec(num_scalar_pr...]
    select_n x6 -> x0, other arithmetic: 2.86 us -> none  [the longest x2 1.43 us: route_predictions(): outgoing = jnp.take(predicted, chosen, axis=0)]
    ppermute x21 -> x27, waiting for transfers between devices: 21 us -> 18.3 us  [across(): lax.ppermute(pieces[k], 'fft', [(z, z ^ k) for z in range(shards)])]
    all_to_all x4 -> x1, waiting for transfers between devices: 0.01 us -> 2.34 us  [on_device(): lax.all_to_all(packed(routes, head_grad, spec_grad, predicted, groups), '...]
  transfers between devices with their start and end apart: 41 -> 44, of which waited for: 13 -> 13; matrix products, arithmetic and copies ran while one was open for 10% -> 2% of each run, Pallas kernels for 16% -> 18%
where the time goes in v6:
time: 169 us; the launch traced here: 168 us
  starting transfers between devices  66.8 us (40%)
  waiting for transfers between devices  50.3 us (30%)
  Pallas kernels  43.7 us (26%)
  other arithmetic  4.84 us (3%)
  local copies, waits for them, and re-layouts  1.89 us (1%)
    ppermute x27, starting transfers between devices, across(): lax.ppermute(pieces[k], 'fft', [(z, z ^ k) for z in range(shards)])  49.6 us
    ppermute x27, waiting for transfers between devices, across(): lax.ppermute(pieces[k], 'fft', [(z, z ^ k) for z in range(shards)])  18.3 us
    ppermute x11, waiting for transfers between devices, swap_bit(): lax.ppermute(values, 'grp', [(g, g ^ 1 << bit) for g in range(groups)])  15.4 us
    pallas_call x2, Pallas kernels, embed_grad_parts(): pl.pallas_call(body, grid_spec=pltpu.PrefetchScalarGridSpec(num_scalar_pr...  10.1 us
    pallas_call x1, Pallas kernels, embed(): pl.pallas_call(body, grid_spec=pltpu.PrefetchScalarGridSpec(num_scalar_pr...  10 us
    ppermute x3, waiting for transfers between devices, from_all_groups(): lax.ppermute(values, 'grp', [(g, g ^ k) for g in range(groups)])  7.58 us
    ppermute x2, waiting for transfers between devices, scatter_end(): received = lax.ppermute(send, 'fft', [(z, z ^ bit) for z in range(shards)])  6.68 us
    ppermute x11, starting transfers between devices, swap_bit(): lax.ppermute(values, 'grp', [(g, g ^ 1 << bit) for g in range(groups)])  6.53 us
  transfers between devices with their start and end apart: 44, of which 13 were waited for; matrix products, arithmetic and copies ran while one was open for 2% of the time, Pallas kernels for 18%

profile of v6, /device:TPU:0, one launch (start us, length us, event | category | flops | bytes accessed | tf_op | source)
XLA Modules:
  0.0 168.5 jit_solution(12310250723453050751)
XLA Ops:
  2.0 10.0 %embed.1 = (bf16[384,1024]{1,0:T(8,128)(2,1)}, bf16[384,1024]{1,0:T(8,128)(2,1)}, f32[384,256]{1,0:T(8,128)}, bf16[4,320,384]{2,1,0:T(8,128)(2,1)}, bf16[4,320,3...) custom-call(s32[15]{0:T(128)} %concatenate.12.scal_ref, ...), custom_call_target="tpu_custom_call" | custom-call | flops 2013265920 | bytes 7208960 | tf_op jit(solution)/shard_map/embed/pallas_call | solution.py:157
  12.0 4.1 %collective-permute-start.10 = (bf16[3,64,256]{2,1,0:T(8,128)(2,1)}, bf16[3,64,256]{2,1,0:T(8,128)(2,1)S(1)}, u32[]{:S(2)}, u32[]{:S(2)}) collective-permute-start(bf16[3,64,256]{2,1,0:T(8,128)(2,1)} %get-tuple-element.111), channel_id=1, source_target_pairs={{0,2},{1,3},{2,0},{3,1},{4,6},{5,7},{6,4},{7,5},{8,10},{9,11},{10,... | collective-permute-start | bytes 294920 | tf_op jit(solution)/shard_map/ppermute | solution.py:589
  16.1 1.3 collective-permute-start.11
  17.7 1.8 %collective-permute-start = (bf16[3,64,256]{2,1,0:T(8,128)(2,1)}, bf16[3,64,256]{2,1,0:T(8,128)(2,1)S(1)}, u32[]{:S(2)}, u32[]{:S(2)}) collective-permute-start(bf16[3,64,256]{2,1,0:T(8,128)(2,1)} %get-tuple-element.96), channel_id=1, source_target_pairs={{0,1},{1,0},{2,3},{3,2},{4,5},{5,4},{6,7},{7,6},{8,9},{9,8},{10,11... | collective-permute-start | bytes 294920 | tf_op jit(solution)/shard_map/ppermute | solution.py:589
  19.5 1.7 %collective-permute-start.1 = (bf16[3,64,256]{2,1,0:T(8,128)(2,1)}, bf16[3,64,256]{2,1,0:T(8,128)(2,1)S(1)}, u32[]{:S(2)}, u32[]{:S(2)}) collective-permute-start(bf16[3,64,256]{2,1,0:T(8,128)(2,1)} %get-tuple-element.97), channel_id=1, source_target_pairs={{0,2},{1,3},{2,0},{3,1},{4,6},{5,7},{6,4},{7,5},{8,10},{9,11},{10,... | collective-permute-start | bytes 294920 | tf_op jit(solution)/shard_map/ppermute | solution.py:589
  21.2 3.0 %collective-permute-done.10.refs_2_ = bf16[3,64,256]{2,1,0:T(8,128)(2,1)S(1)} collective-permute-done((bf16[3,64,256]{2,1,0:T(8,128)(2,1)}, bf16[3,64,256]{2,1,0:T(8,128)(2,1)S(1)}, u32[]{:S(2)}, u32[]{:S(2)}) %collective-permute-start.10) | collective-permute-done | bytes 98336 | tf_op jit(solution)/shard_map/ppermute | solution.py:589
  24.2 2.8 %collective-permute-start.2 = (bf16[3,64,256]{2,1,0:T(8,128)(2,1)}, bf16[3,64,256]{2,1,0:T(8,128)(2,1)S(1)}, u32[]{:S(2)}, u32[]{:S(2)}) collective-permute-start(bf16[3,64,256]{2,1,0:T(8,128)(2,1)} %get-tuple-element.98), channel_id=1, source_target_pairs={{0,3},{1,2},{2,1},{3,0},{4,7},{5,6},{6,5},{7,4},{8,11},{9,10},{10,... | collective-permute-start | bytes 294920 | tf_op jit(solution)/shard_map/ppermute | solution.py:589
  27.9 2.3 %spectral.3 = (bf16[3,64,256]{2,1,0:T(8,128)(2,1)S(1)}, bf16[3,64,256]{2,1,0:T(8,128)(2,1)S(1)}, bf16[3,64,256]{2,1,0:T(8,128)(2,1)S(1)}, bf16[3,64,256]{2,1,0:T...) custom-call(s32[15]{0:T(128)S(1)} %copy-done.7, ...), custom_call_target="tpu_custom_call" | custom-call | flops 704643072 | bytes 3145728 | tf_op jit(solution)/shard_map/spectral/pallas_call | solution.py:277
  31.3 1.6 collective-permute-start.13
  32.8 1.9 %collective-permute-start.14 = (bf16[3,64,256]{2,1,0:T(8,128)(2,1)S(1)}, bf16[3,64,256]{2,1,0:T(8,128)(2,1)S(1)}, u32[]{:S(2)}, u32[]{:S(2)}) collective-permute-start(bf16[3,64,256]{2,1,0:T(8,128)(2,1)S(1)} %get-tuple-element.119), channel_id=1, source_target_pairs={{0,3},{1,2},{2,1},{3,0},{4,7},{5,6},{6,5},{7,4},{8,11},{9,10},{10,... | collective-permute-start | bytes 294920 | tf_op jit(solution)/shard_map/ppermute | solution.py:589
  34.8 2.3 %spectral.2 = (bf16[3,64,256]{2,1,0:T(8,128)(2,1)S(1)}, bf16[3,64,256]{2,1,0:T(8,128)(2,1)S(1)}, bf16[3,64,256]{2,1,0:T(8,128)(2,1)S(1)}, bf16[3,64,256]{2,1,0:T...) custom-call(s32[15]{0:T(128)S(1)} %copy-done.7, ...), custom_call_target="tpu_custom_call" | custom-call | flops 704643072 | bytes 3145728 | tf_op jit(solution)/shard_map/spectral/pallas_call | solution.py:277
  37.5 2.2 %collective-permute-start.4 = (bf16[3,64,256]{2,1,0:T(8,128)(2,1)S(1)}, bf16[3,64,256]{2,1,0:T(8,128)(2,1)S(1)}, u32[]{:S(2)}, u32[]{:S(2)}) collective-permute-start(bf16[3,64,256]{2,1,0:T(8,128)(2,1)S(1)} %get-tuple-element.106), channel_id=1, source_target_pairs={{0,2},{1,3},{2,0},{3,1},{4,6},{5,7},{6,4},{7,5},{8,10},{9,11},{10,... | collective-permute-start | bytes 294920 | tf_op jit(solution)/shard_map/ppermute | solution.py:589
  39.7 1.8 %collective-permute-start.5 = (bf16[3,64,256]{2,1,0:T(8,128)(2,1)S(1)}, bf16[3,64,256]{2,1,0:T(8,128)(2,1)S(1)}, u32[]{:S(2)}, u32[]{:S(2)}) collective-permute-start(bf16[3,64,256]{2,1,0:T(8,128)(2,1)S(1)} %get-tuple-element.107), channel_id=1, source_target_pairs={{0,3},{1,2},{2,1},{3,0},{4,7},{5,6},{6,5},{7,4},{8,11},{9,10},{10,... | collective-permute-start | bytes 294920 | tf_op jit(solution)/shard_map/ppermute | solution.py:589
  42.8 6.9 %collective-permute-start.15 = (bf16[3,64,256]{2,1,0:T(8,128)(2,1)S(1)}, bf16[3,64,256]{2,1,0:T(8,128)(2,1)S(1)}, u32[]{:S(2)}, u32[]{:S(2)}) collective-permute-start(bf16[3,64,256]{2,1,0:T(8,128)(2,1)S(1)} %get-tuple-element.123.refs_2_.refs_0_.res_ref), channel_id=1, source_target_pairs={{0,1},{1,0},{2,3},{3,2},{4,5},{5,4},{6,7},{7,6},{8,9},{9,8},{10,11... | collective-permute-start | bytes 294920 | tf_op jit(solution)/shard_map/ppermute | solution.py:589
  50.7 1.5 collective-permute-start.17
  54.2 1.8 %collective-permute-start.7 = (bf16[3,64,256]{2,1,0:T(8,128)(2,1)S(1)}, bf16[3,64,256]{2,1,0:T(8,128)(2,1)S(1)}, u32[]{:S(2)}, u32[]{:S(2)}) collective-permute-start(bf16[3,64,256]{2,1,0:T(8,128)(2,1)S(1)} %get-tuple-element.108.refs_3_.refs_0_.res_ref), channel_id=1, source_target_pairs={{0,2},{1,3},{2,0},{3,1},{4,6},{5,7},{6,4},{7,5},{8,10},{9,11},{10,... | collective-permute-start | bytes 294920 | tf_op jit(solution)/shard_map/ppermute | solution.py:589
  56.0 1.5 collective-permute-start.8
  58.1 2.4 %collective-permute-done.16.refs_2_ = bf16[3,64,256]{2,1,0:T(8,128)(2,1)S(1)} collective-permute-done((bf16[3,64,256]{2,1,0:T(8,128)(2,1)S(1)}, bf16[3,64,256]{2,1,0:T(8,128)(2,1)S(1)}, u32[]{:S(2)}, u32[]{:S(2)}) %collective-permute-start.16) | collective-permute-done | bytes 98336 | tf_op jit(solution)/shard_map/ppermute | solution.py:589
  60.5 3.0 %spectral_back.2 = (bf16[3,64,256]{2,1,0:T(8,128)(2,1)S(1)}, bf16[3,64,256]{2,1,0:T(8,128)(2,1)S(1)}, bf16[3,64,256]{2,1,0:T(8,128)(2,1)S(1)}, bf16[3,64,256]{2,...) custom-call(s32[15]{0:T(128)S(1)} %copy-done.7, bf16[3,512,256]{2,1,0:T(8,128)(2,1)S(1)} %copy-done.4, ...), custom_call_target="tpu_custom_call" | custom-call | flops 1006632960 | bytes 3145728 | tf_op jit(solution)/shard_map/spectral_back/pallas_call | solution.py:440
  63.5 4.3 %collective-permute-done.7.refs_2_ = bf16[3,64,256]{2,1,0:T(8,128)(2,1)S(1)} collective-permute-done((bf16[3,64,256]{2,1,0:T(8,128)(2,1)S(1)}, bf16[3,64,256]{2,1,0:T(8,128)(2,1)S(1)}, u32[]{:S(2)}, u32[]{:S(2)}) %collective-permute-start.7) | collective-permute-done | bytes 98336 | tf_op jit(solution)/shard_map/ppermute | solution.py:589
  67.8 3.1 %spectral_back.3 = (bf16[3,64,256]{2,1,0:T(8,128)(2,1)S(1)}, bf16[3,64,256]{2,1,0:T(8,128)(2,1)S(1)}, bf16[3,64,256]{2,1,0:T(8,128)(2,1)S(1)}, bf16[3,64,256]{2,...) custom-call(s32[15]{0:T(128)S(1)} %copy-done.7, bf16[3,512,256]{2,1,0:T(8,128)(2,1)S(1)} %copy-done.4, ...), custom_call_target="tpu_custom_call" | custom-call | flops 1006632960 | bytes 3145728 | tf_op jit(solution)/shard_map/spectral_back/pallas_call | solution.py:440
  70.9 1.8 %collective-permute-start.19 = (bf16[3,64,256]{2,1,0:T(8,128)(2,1)S(1)}, bf16[3,64,256]{2,1,0:T(8,128)(2,1)S(1)}, u32[]{:S(2)}, u32[]{:S(2)}) collective-permute-start(bf16[3,64,256]{2,1,0:T(8,128)(2,1)S(1)} %get-tuple-element.137), channel_id=1, source_target_pairs={{0,1},{1,0},{2,3},{3,2},{4,5},{5,4},{6,7},{7,6},{8,9},{9,8},{10,11... | collective-permute-start | bytes 294920 | tf_op jit(solution)/shard_map/ppermute | solution.py:589
  73.7 1.7 collective-permute-start.21
  76.3 2.9 %collective-permute-start.23 = (bf16[3,64,256]{2,1,0:T(8,128)(2,1)S(1)}, bf16[3,64,256]{2,1,0:T(8,128)(2,1)S(1)}, u32[]{:S(2)}, u32[]{:S(2)}) collective-permute-start(bf16[3,64,256]{2,1,0:T(8,128)(2,1)S(1)} %get-tuple-element.146), channel_id=1, source_target_pairs={{0,2},{1,3},{2,0},{3,1},{4,6},{5,7},{6,4},{7,5},{8,10},{9,11},{10,... | collective-permute-start | bytes 294920 | tf_op jit(solution)/shard_map/ppermute | solution.py:589
  79.2 4.4 %collective-permute-done.20.refs_2_ = bf16[3,64,256]{2,1,0:T(8,128)(2,1)S(1)} collective-permute-done((bf16[3,64,256]{2,1,0:T(8,128)(2,1)S(1)}, bf16[3,64,256]{2,1,0:T(8,128)(2,1)S(1)}, u32[]{:S(2)}, u32[]{:S(2)}) %collective-permute-start.20) | collective-permute-done | bytes 98336 | tf_op jit(solution)/shard_map/ppermute | solution.py:589
  83.5 2.3 %collective-permute-start.24 = (bf16[3,64,256]{2,1,0:T(8,128)(2,1)S(1)}, bf16[3,64,256]{2,1,0:T(8,128)(2,1)S(1)}, u32[]{:S(2)}, u32[]{:S(2)}) collective-permute-start(bf16[3,64,256]{2,1,0:T(8,128)(2,1)S(1)} %get-tuple-element.147), channel_id=1, source_target_pairs={{0,3},{1,2},{2,1},{3,0},{4,7},{5,6},{6,5},{7,4},{8,11},{9,10},{10,... | collective-permute-start | bytes 294920 | tf_op jit(solution)/shard_map/ppermute | solution.py:589
  85.9 2.2 %embedded_back.2 = (bf16[192,1024]{1,0:T(8,128)(2,1)}, f32[8,1024]{1,0:T(8,128)S(1)}) custom-call(s32[15]{0:T(128)S(1)} %copy-done.7, bf16[384,1024]{1,0:T(8,128)(2,1)S(1)} %copy-done.1, f32[384,256]{1,0:T(8,128)S(1)} %copy-done.5, bf16[3,64,256]{2,1,0:T(8,128)(2,1)S(1)} %get-tuple-element.123.refs_2_.refs_0_.res_ref, bf16[1024,256]{1,0:T(8,128)(2,1)S(1)} %copy-done, ...), custom_call_target="tpu_custom_call" | custom-call | flops 100663296 | bytes 1179648 | tf_op jit(solution)/shard_map/embedded_back/pallas_call | solution.py:497
  88.1 3.8 %collective-permute-done.23.refs_2_ = bf16[3,64,256]{2,1,0:T(8,128)(2,1)S(1)} collective-permute-done((bf16[3,64,256]{2,1,0:T(8,128)(2,1)S(1)}, bf16[3,64,256]{2,1,0:T(8,128)(2,1)S(1)}, u32[]{:S(2)}, u32[]{:S(2)}) %collective-permute-start.23) | collective-permute-done | bytes 98336 | tf_op jit(solution)/shard_map/ppermute | solution.py:589
  92.0 2.4 %embedded_back.3 = (bf16[192,1024]{1,0:T(8,128)(2,1)}, f32[8,1024]{1,0:T(8,128)S(1)}) custom-call(s32[15]{0:T(128)S(1)} %copy-done.7, bf16[384,1024]{1,0:T(8,128)(2,1)S(1)} %copy-done.1, f32[384,256]{1,0:T(8,128)S(1)} %copy-done.5, bf16[3,64,256]{2,1,0:T(8,128)(2,1)S(1)} %get-tuple-element.108.refs_3_.refs_0_.res_ref, bf16[1024,256]{1,0:T(8,128)(2,1)S(1)} %copy-done, ...), custom_call_target="tpu_custom_call" | custom-call | flops 100663296 | bytes 1179648 | tf_op jit(solution)/shard_map/embedded_back/pallas_call | solution.py:497
  95.5 1.7 %packed.1 = bf16[8,256,256]{2,1,0:T(8,128)(2,1)} custom-call(s32[17]{0:T(128)S(1)} %concatenate.11.routes_ref, bf16[1024,256]{1,0:T(8,128)(2,1)S(1)} %head_gradient.1.head_ref, bf16[512,256]{1,0:T(8,128)(2,1)S(1)} %get-tuple-element.156.spec_ref, bf16[3,64,256]{2,1,0:T(8,128)(2,1)S(1)} %get-tuple-element.157.refs_0_, ...), custom_call_target="tpu_custom_call" | custom-call | tf_op jit(solution)/shard_map/packed/pallas_call | solution.py:655
  97.2 4.0 %all-to-all-start = ((bf16[8,256,256]{2,1,0:T(8,128)(2,1)}), bf16[8,256,256]{2,1,0:T(8,128)(2,1)S(1)}, u32[]{:S(2)}, u32[]{:S(2)}) async-start(bf16[8,256,256]{2,1,0:T(8,128)(2,1)} %packed.1), calls=%async_computation | async-start | bytes 2097152 | tf_op jit(solution)/shard_map/all_to_all | solution.py:889
  101.3 5.5 %embed_grad.2 = (bf16[2,320,512]{2,1,0:T(8,128)(2,1)}, bf16[2,320,512]{2,1,0:T(8,128)(2,1)}) custom-call(s32[15]{0:T(128)S(1)} %copy-done.7, bf16[4,320,384]{2,1,0:T(8,128)(2,1)S(1)} %copy-done.11, bf16[4,320,384]{2,1,0:T(8,128)(2,1)S(1)} %collective-permute-done.18.refs_1_, bf16[192,1024]{1,0:T(8,128)(2,1)} %get-tuple-element.143.refs_2_, ...), custom_call_target="tpu_custom_call" | custom-call | flops 1006632960 | bytes 4063232 | tf_op jit(solution)/shard_map/embed_grad/pallas_call | solution.py:555
  106.7 2.0 %collective-permute-start.29 = (bf16[2,320,512]{2,1,0:T(8,128)(2,1)}, bf16[2,320,512]{2,1,0:T(8,128)(2,1)}, u32[]{:S(2)}, u32[]{:S(2)}) collective-permute-start(bf16[2,320,512]{2,1,0:T(8,128)(2,1)} %get-tuple-element.169), channel_id=1, source_target_pairs={{0,16},{4,20},{8,24},{12,28},{16,0},{20,4},{24,8},{28,12},{1,17},{... | collective-permute-start | bytes 1966088 | tf_op jit(solution)/shard_map/ppermute | solution.py:583
  108.8 1.5 collective-permute-start.27
  110.2 4.6 %embed_grad.3 = (bf16[2,320,512]{2,1,0:T(8,128)(2,1)S(1)}, bf16[2,320,512]{2,1,0:T(8,128)(2,1)S(1)}) custom-call(s32[15]{0:T(128)S(1)} %copy-done.7, bf16[4,320,384]{2,1,0:T(8,128)(2,1)S(1)} %copy-done.12, bf16[4,320,384]{2,1,0:T(8,128)(2,1)S(1)} %collective-permute-done.18.refs_1_, bf16[192,1024]{1,0:T(8,128)(2,1)} %get-tuple-element.143.refs_2_, ...), custom_call_target="tpu_custom_call" | custom-call | flops 1006632960 | bytes 4063232 | tf_op jit(solution)/shard_map/embed_grad/pallas_call | solution.py:555
  114.8 2.3 %all-to-all-done.moved_ref = bf16[8,256,256]{2,1,0:T(8,128)(2,1)S(1)} async-done(((bf16[8,256,256]{2,1,0:T(8,128)(2,1)}), bf16[8,256,256]{2,1,0:T(8,128)(2,1)S(1)}, u32[]{:S(2)}, u32[]{:S(2)}) %all-to-all-start) | async-done | bytes 1048608 | tf_op jit(solution)/shard_map/all_to_all | solution.py:889
  118.4 1.9 %collective-permute-start.31 = (bf16[224,256]{1,0:T(8,128)(2,1)S(1)}, bf16[224,256]{1,0:T(8,128)(2,1)S(1)}, u32[]{:S(2)}, u32[]{:S(2)}) collective-permute-start(bf16[224,256]{1,0:T(8,128)(2,1)S(1)} %get-tuple-element.170.refs_0_), channel_id=1, source_target_pairs={{0,1},{1,0},{2,3},{3,2},{4,5},{5,4},{6,7},{7,6},{8,9},{9,8},{10,11... | collective-permute-start | bytes 344072 | tf_op jit(solution)/shard_map/ppermute | solution.py:589
  121.1 1.7 collective-permute-start.33
  122.8 7.0 %collective-permute-done.29 = bf16[2,320,512]{2,1,0:T(8,128)(2,1)} collective-permute-done((bf16[2,320,512]{2,1,0:T(8,128)(2,1)}, bf16[2,320,512]{2,1,0:T(8,128)(2,1)}, u32[]{:S(2)}, u32[]{:S(2)}) %collective-permute-start.29) | collective-permute-done | bytes 655392 | tf_op jit(solution)/shard_map/ppermute | solution.py:583
  131.1 1.5 collective-permute-start.30
  135.0 5.6 %collective-permute-done.30 = bf16[1,320,512]{2,1,0:T(8,128)(2,1)S(1)} collective-permute-done((bf16[1,320,512]{2,1,0:T(8,128)(2,1)S(1)}, bf16[1,320,512]{2,1,0:T(8,128)(2,1)S(1)}, u32[]{:S(2)}, u32[]{:S(2)}) %collective-permute-start.30) | collective-permute-done | bytes 327712 | tf_op jit(solution)/shard_map/ppermute | solution.py:583
  140.7 2.7 %collective-permute-done.28 = bf16[1,320,512]{2,1,0:T(8,128)(2,1)S(1)} collective-permute-done((bf16[1,320,512]{2,1,0:T(8,128)(2,1)S(1)}, bf16[1,320,512]{2,1,0:T(8,128)(2,1)S(1)}, u32[]{:S(2)}, u32[]{:S(2)}) %collective-permute-start.28) | collective-permute-done | bytes 327712 | tf_op jit(solution)/shard_map/ppermute | solution.py:583
  143.6 2.0 %collective-permute-start.34 = (bf16[2,80,1024]{2,1,0:T(8,128)(2,1)S(1)}, bf16[2,80,1024]{2,1,0:T(8,128)(2,1)S(1)}, u32[]{:S(2)}, u32[]{:S(2)}) collective-permute-start(bf16[2,80,1024]{2,1,0:T(8,128)(2,1)S(1)} %dynamic-slice_bitcast_fusion), channel_id=1, source_target_pairs={{0,1},{1,0},{2,3},{3,2},{4,5},{5,4},{6,7},{7,6},{8,9},{9,8},{10,11... | collective-permute-start | bytes 983048 | tf_op jit(solution)/shard_map/ppermute | solution.py:627
  146.4 2.7 %collective-permute-start.41 = (bf16[448,256]{1,0:T(8,128)(2,1)S(1)}, bf16[448,256]{1,0:T(8,128)(2,1)S(1)}, u32[]{:S(2)}, u32[]{:S(2)}) collective-permute-start(bf16[448,256]{1,0:T(8,128)(2,1)S(1)} %shard_sums.1.refs_0_), channel_id=1, source_target_pairs={{0,24},{4,28},{8,16},{12,20},{16,8},{20,12},{24,0},{28,4},{1,25},{... | collective-permute-start | bytes 688136 | tf_op jit(solution)/shard_map/ppermute | solution.py:637
  149.1 5.0 %collective-permute-done.37.refs_2_ = bf16[448,256]{1,0:T(8,128)(2,1)S(1)} collective-permute-done((bf16[448,256]{1,0:T(8,128)(2,1)S(1)}, bf16[448,256]{1,0:T(8,128)(2,1)S(1)}, u32[]{:S(2)}, u32[]{:S(2)}) %collective-permute-start.37) | collective-permute-done | bytes 229408 | tf_op jit(solution)/shard_map/ppermute | solution.py:637
  154.1 2.5 %collective-permute-done.39.refs_4_ = bf16[448,256]{1,0:T(8,128)(2,1)S(1)} collective-permute-done((bf16[448,256]{1,0:T(8,128)(2,1)S(1)}, bf16[448,256]{1,0:T(8,128)(2,1)S(1)}, u32[]{:S(2)}, u32[]{:S(2)}) %collective-permute-start.39) | collective-permute-done | bytes 229408 | tf_op jit(solution)/shard_map/ppermute | solution.py:637
  158.6 2.5 %assembled.1 = (f32[1024,256]{1,0:T(8,128)}, f32[2,2,8,128,128]{4,3,2,1,0:T(8,128)}, f32[2,2,8,128]{3,2,1,0:T(8,128)}, f32[1,1024]{1,0:T(1,128)}, f32[1,1024]{1,0:T(1,128)}, /*index=5*/f32[1,256]{1,0:T(1,128)}) custom-call(s32[15]{0:T(128)S(1)} %copy-done.7, bf16[448,256]{1,0:T(8,128)(2,1)S(1)} %shard_sums.1.refs_0_, ...), custom_call_target="tpu_custom_call" | custom-call | tf_op jit(solution)/shard_map/assembled/pallas_call | solution.py:800
  161.1 6.7 %collective-permute-done.35 = bf16[1,80,1024]{2,1,0:T(8,128)(2,1)S(1)} collective-permute-done((bf16[1,80,1024]{2,1,0:T(8,128)(2,1)S(1)}, bf16[1,80,1024]{2,1,0:T(8,128)(2,1)S(1)}, u32[]{:S(2)}, u32[]{:S(2)}) %collective-permute-start.35) | collective-permute-done | bytes 163872 | tf_op jit(solution)/shard_map/ppermute | solution.py:627
  (109 shorter events, 21.2 us)
Async XLA Ops:
  2.0 25.0 %copy-start.2 = (bf16[2,2,8,128,128]{4,3,2,1,0:T(8,128)(2,1)S(1)}, bf16[2,2,8,128,128]{4,3,2,1,0:T(8,128)(2,1)}, u32[]{:S(2)}) copy-start(bf16[2,2,8,128,128]{4,3,2,1,0:T(8,128)(2,1)} %w_ref.15) | copy-start | bytes 3145732
  2.0 25.0 %copy-start.4 = (bf16[3,512,256]{2,1,0:T(8,128)(2,1)S(1)}, bf16[3,512,256]{2,1,0:T(8,128)(2,1)}, u32[]{:S(2)}) copy-start(bf16[3,512,256]{2,1,0:T(8,128)(2,1)} %constant.76.clone.t_ref) | copy-start | bytes 2359300
  2.0 25.0 %copy-start.7 = (s32[15]{0:T(128)S(1)}, s32[15]{0:T(128)}, u32[]{:S(2)}) copy-start(s32[15]{0:T(128)} %concatenate.12.scal_ref) | copy-start | bytes 184
  2.0 25.1 %copy-start.10 = (f32[2,2,8,128]{3,2,1,0:T(8,128)S(1)}, f32[2,2,8,128]{3,2,1,0:T(8,128)}, u32[]{:S(2)}) copy-start(f32[2,2,8,128]{3,2,1,0:T(8,128)} %b_ref.3) | copy-start | bytes 49156
  12.0 12.2 %collective-permute-start.10 = (bf16[3,64,256]{2,1,0:T(8,128)(2,1)}, bf16[3,64,256]{2,1,0:T(8,128)(2,1)S(1)}, u32[]{:S(2)}, u32[]{:S(2)}) collective-permute-start(bf16[3,64,256]{2,1,0:T(8,128)(2,1)} %get-tuple-element.111), channel_id=1, source_target_pairs={{0,2},{1,3},{2,0},{3,1},{4,6},{5,7},{6,4},{7,5},{8,10},{9,11},{10,... | collective-permute-start | bytes 294920 | tf_op jit(solution)/shard_map/ppermute | solution.py:589
  16.1 10.9 %collective-permute-start.11 = (bf16[3,64,256]{2,1,0:T(8,128)(2,1)}, bf16[3,64,256]{2,1,0:T(8,128)(2,1)S(1)}, u32[]{:S(2)}, u32[]{:S(2)}) collective-permute-start(bf16[3,64,256]{2,1,0:T(8,128)(2,1)} %get-tuple-element.112), channel_id=1, source_target_pairs={{0,3},{1,2},{2,1},{3,0},{4,7},{5,6},{6,5},{7,4},{8,11},{9,10},{10,... | collective-permute-start | bytes 294920 | tf_op jit(solution)/shard_map/ppermute | solution.py:589
  17.5 9.5 %collective-permute-start.9 = (bf16[3,64,256]{2,1,0:T(8,128)(2,1)}, bf16[3,64,256]{2,1,0:T(8,128)(2,1)S(1)}, u32[]{:S(2)}, u32[]{:S(2)}) collective-permute-start(bf16[3,64,256]{2,1,0:T(8,128)(2,1)} %get-tuple-element.110), channel_id=1, source_target_pairs={{0,1},{1,0},{2,3},{3,2},{4,5},{5,4},{6,7},{7,6},{8,9},{9,8},{10,11... | collective-permute-start | bytes 294920 | tf_op jit(solution)/shard_map/ppermute | solution.py:589
  17.7 15.1 %collective-permute-start = (bf16[3,64,256]{2,1,0:T(8,128)(2,1)}, bf16[3,64,256]{2,1,0:T(8,128)(2,1)S(1)}, u32[]{:S(2)}, u32[]{:S(2)}) collective-permute-start(bf16[3,64,256]{2,1,0:T(8,128)(2,1)} %get-tuple-element.96), channel_id=1, source_target_pairs={{0,1},{1,0},{2,3},{3,2},{4,5},{5,4},{6,7},{7,6},{8,9},{9,8},{10,11... | collective-permute-start | bytes 294920 | tf_op jit(solution)/shard_map/ppermute | solution.py:589
  19.5 15.2 %collective-permute-start.1 = (bf16[3,64,256]{2,1,0:T(8,128)(2,1)}, bf16[3,64,256]{2,1,0:T(8,128)(2,1)S(1)}, u32[]{:S(2)}, u32[]{:S(2)}) collective-permute-start(bf16[3,64,256]{2,1,0:T(8,128)(2,1)} %get-tuple-element.97), channel_id=1, source_target_pairs={{0,2},{1,3},{2,0},{3,1},{4,6},{5,7},{6,4},{7,5},{8,10},{9,11},{10,... | collective-permute-start | bytes 294920 | tf_op jit(solution)/shard_map/ppermute | solution.py:589
  24.2 10.5 %collective-permute-start.2 = (bf16[3,64,256]{2,1,0:T(8,128)(2,1)}, bf16[3,64,256]{2,1,0:T(8,128)(2,1)S(1)}, u32[]{:S(2)}, u32[]{:S(2)}) collective-permute-start(bf16[3,64,256]{2,1,0:T(8,128)(2,1)} %get-tuple-element.98), channel_id=1, source_target_pairs={{0,3},{1,2},{2,1},{3,0},{4,7},{5,6},{6,5},{7,4},{8,11},{9,10},{10,... | collective-permute-start | bytes 294920 | tf_op jit(solution)/shard_map/ppermute | solution.py:589
  30.2 9.5 %collective-permute-start.12 = (bf16[3,64,256]{2,1,0:T(8,128)(2,1)S(1)}, bf16[3,64,256]{2,1,0:T(8,128)(2,1)S(1)}, u32[]{:S(2)}, u32[]{:S(2)}) collective-permute-start(bf16[3,64,256]{2,1,0:T(8,128)(2,1)S(1)} %get-tuple-element.117), channel_id=1, source_target_pairs={{0,1},{1,0},{2,3},{3,2},{4,5},{5,4},{6,7},{7,6},{8,9},{9,8},{10,11... | collective-permute-start | bytes 294920 | tf_op jit(solution)/shard_map/ppermute | solution.py:589
  31.3 10.6 %collective-permute-start.13 = (bf16[3,64,256]{2,1,0:T(8,128)(2,1)S(1)}, bf16[3,64,256]{2,1,0:T(8,128)(2,1)S(1)}, u32[]{:S(2)}, u32[]{:S(2)}) collective-permute-start(bf16[3,64,256]{2,1,0:T(8,128)(2,1)S(1)} %get-tuple-element.118), channel_id=1, source_target_pairs={{0,2},{1,3},{2,0},{3,1},{4,6},{5,7},{6,4},{7,5},{8,10},{9,11},{10,... | collective-permute-start | bytes 294920 | tf_op jit(solution)/shard_map/ppermute | solution.py:589
  32.8 9.0 %collective-permute-start.14 = (bf16[3,64,256]{2,1,0:T(8,128)(2,1)S(1)}, bf16[3,64,256]{2,1,0:T(8,128)(2,1)S(1)}, u32[]{:S(2)}, u32[]{:S(2)}) collective-permute-start(bf16[3,64,256]{2,1,0:T(8,128)(2,1)S(1)} %get-tuple-element.119), channel_id=1, source_target_pairs={{0,3},{1,2},{2,1},{3,0},{4,7},{5,6},{6,5},{7,4},{8,11},{9,10},{10,... | collective-permute-start | bytes 294920 | tf_op jit(solution)/shard_map/ppermute | solution.py:589
  37.1 13.6 %collective-permute-start.3 = (bf16[3,64,256]{2,1,0:T(8,128)(2,1)S(1)}, bf16[3,64,256]{2,1,0:T(8,128)(2,1)S(1)}, u32[]{:S(2)}, u32[]{:S(2)}) collective-permute-start(bf16[3,64,256]{2,1,0:T(8,128)(2,1)S(1)} %get-tuple-element.105), channel_id=1, source_target_pairs={{0,1},{1,0},{2,3},{3,2},{4,5},{5,4},{6,7},{7,6},{8,9},{9,8},{10,11... | collective-permute-start | bytes 294920 | tf_op jit(solution)/shard_map/ppermute | solution.py:589
  37.5 14.7 %collective-permute-start.4 = (bf16[3,64,256]{2,1,0:T(8,128)(2,1)S(1)}, bf16[3,64,256]{2,1,0:T(8,128)(2,1)S(1)}, u32[]{:S(2)}, u32[]{:S(2)}) collective-permute-start(bf16[3,64,256]{2,1,0:T(8,128)(2,1)S(1)} %get-tuple-element.106), channel_id=1, source_target_pairs={{0,2},{1,3},{2,0},{3,1},{4,6},{5,7},{6,4},{7,5},{8,10},{9,11},{10,... | collective-permute-start | bytes 294920 | tf_op jit(solution)/shard_map/ppermute | solution.py:589
  39.7 12.4 %collective-permute-start.5 = (bf16[3,64,256]{2,1,0:T(8,128)(2,1)S(1)}, bf16[3,64,256]{2,1,0:T(8,128)(2,1)S(1)}, u32[]{:S(2)}, u32[]{:S(2)}) collective-permute-start(bf16[3,64,256]{2,1,0:T(8,128)(2,1)S(1)} %get-tuple-element.107), channel_id=1, source_target_pairs={{0,3},{1,2},{2,1},{3,0},{4,7},{5,6},{6,5},{7,4},{8,11},{9,10},{10,... | collective-permute-start | bytes 294920 | tf_op jit(solution)/shard_map/ppermute | solution.py:589
  42.8 13.2 %collective-permute-start.15 = (bf16[3,64,256]{2,1,0:T(8,128)(2,1)S(1)}, bf16[3,64,256]{2,1,0:T(8,128)(2,1)S(1)}, u32[]{:S(2)}, u32[]{:S(2)}) collective-permute-start(bf16[3,64,256]{2,1,0:T(8,128)(2,1)S(1)} %get-tuple-element.123.refs_2_.refs_0_.res_ref), channel_id=1, source_target_pairs={{0,1},{1,0},{2,3},{3,2},{4,5},{5,4},{6,7},{7,6},{8,9},{9,8},{10,11... | collective-permute-start | bytes 294920 | tf_op jit(solution)/shard_map/ppermute | solution.py:589
  49.7 10.8 %collective-permute-start.16 = (bf16[3,64,256]{2,1,0:T(8,128)(2,1)S(1)}, bf16[3,64,256]{2,1,0:T(8,128)(2,1)S(1)}, u32[]{:S(2)}, u32[]{:S(2)}) collective-permute-start(bf16[3,64,256]{2,1,0:T(8,128)(2,1)S(1)} %get-tuple-element.123.refs_2_.refs_0_.res_ref), channel_id=1, source_target_pairs={{0,2},{1,3},{2,0},{3,1},{4,6},{5,7},{6,4},{7,5},{8,10},{9,11},{10,... | collective-permute-start | bytes 294920 | tf_op jit(solution)/shard_map/ppermute | solution.py:589
  50.7 9.9 %collective-permute-start.17 = (bf16[3,64,256]{2,1,0:T(8,128)(2,1)S(1)}, bf16[3,64,256]{2,1,0:T(8,128)(2,1)S(1)}, u32[]{:S(2)}, u32[]{:S(2)}) collective-permute-start(bf16[3,64,256]{2,1,0:T(8,128)(2,1)S(1)} %get-tuple-element.123.refs_2_.refs_0_.res_ref), channel_id=1, source_target_pairs={{0,3},{1,2},{2,1},{3,0},{4,7},{5,6},{6,5},{7,4},{8,11},{9,10},{10,... | collective-permute-start | bytes 294920 | tf_op jit(solution)/shard_map/ppermute | solution.py:589
  53.1 10.4 %collective-permute-start.6 = (bf16[3,64,256]{2,1,0:T(8,128)(2,1)S(1)}, bf16[3,64,256]{2,1,0:T(8,128)(2,1)S(1)}, u32[]{:S(2)}, u32[]{:S(2)}) collective-permute-start(bf16[3,64,256]{2,1,0:T(8,128)(2,1)S(1)} %get-tuple-element.108.refs_3_.refs_0_.res_ref), channel_id=1, source_target_pairs={{0,1},{1,0},{2,3},{3,2},{4,5},{5,4},{6,7},{7,6},{8,9},{9,8},{10,11... | collective-permute-start | bytes 294920 | tf_op jit(solution)/shard_map/ppermute | solution.py:589
  54.2 13.6 %collective-permute-start.7 = (bf16[3,64,256]{2,1,0:T(8,128)(2,1)S(1)}, bf16[3,64,256]{2,1,0:T(8,128)(2,1)S(1)}, u32[]{:S(2)}, u32[]{:S(2)}) collective-permute-start(bf16[3,64,256]{2,1,0:T(8,128)(2,1)S(1)} %get-tuple-element.108.refs_3_.refs_0_.res_ref), channel_id=1, source_target_pairs={{0,2},{1,3},{2,0},{3,1},{4,6},{5,7},{6,4},{7,5},{8,10},{9,11},{10,... | collective-permute-start | bytes 294920 | tf_op jit(solution)/shard_map/ppermute | solution.py:589
  56.0 11.8 %collective-permute-start.8 = (bf16[3,64,256]{2,1,0:T(8,128)(2,1)S(1)}, bf16[3,64,256]{2,1,0:T(8,128)(2,1)S(1)}, u32[]{:S(2)}, u32[]{:S(2)}) collective-permute-start(bf16[3,64,256]{2,1,0:T(8,128)(2,1)S(1)} %get-tuple-element.108.refs_3_.refs_0_.res_ref), channel_id=1, source_target_pairs={{0,3},{1,2},{2,1},{3,0},{4,7},{5,6},{6,5},{7,4},{8,11},{9,10},{10,... | collective-permute-start | bytes 294920 | tf_op jit(solution)/shard_map/ppermute | solution.py:589
  70.9 30.4 %collective-permute-start.18 = (bf16[4,320,384]{2,1,0:T(8,128)(2,1)}, bf16[4,320,384]{2,1,0:T(8,128)(2,1)S(1)}, u32[]{:S(2)}, u32[]{:S(2)}) collective-permute-start(bf16[4,320,384]{2,1,0:T(8,128)(2,1)} %get-tuple-element.134), channel_id=1, source_target_pairs={{0,4},{4,0},{8,12},{12,8},{16,20},{20,16},{24,28},{28,24},{1,5},{5... | collective-permute-start | bytes 2949128 | tf_op jit(solution)/shard_map/ppermute | solution.py:583
  70.9 5.3 %collective-permute-start.19 = (bf16[3,64,256]{2,1,0:T(8,128)(2,1)S(1)}, bf16[3,64,256]{2,1,0:T(8,128)(2,1)S(1)}, u32[]{:S(2)}, u32[]{:S(2)}) collective-permute-start(bf16[3,64,256]{2,1,0:T(8,128)(2,1)S(1)} %get-tuple-element.137), channel_id=1, source_target_pairs={{0,1},{1,0},{2,3},{3,2},{4,5},{5,4},{6,7},{7,6},{8,9},{9,8},{10,11... | collective-permute-start | bytes 294920 | tf_op jit(solution)/shard_map/ppermute | solution.py:589
  72.8 10.8 %collective-permute-start.20 = (bf16[3,64,256]{2,1,0:T(8,128)(2,1)S(1)}, bf16[3,64,256]{2,1,0:T(8,128)(2,1)S(1)}, u32[]{:S(2)}, u32[]{:S(2)}) collective-permute-start(bf16[3,64,256]{2,1,0:T(8,128)(2,1)S(1)} %get-tuple-element.138), channel_id=1, source_target_pairs={{0,2},{1,3},{2,0},{3,1},{4,6},{5,7},{6,4},{7,5},{8,10},{9,11},{10,... | collective-permute-start | bytes 294920 | tf_op jit(solution)/shard_map/ppermute | solution.py:589
  73.7 12.2 %collective-permute-start.21 = (bf16[3,64,256]{2,1,0:T(8,128)(2,1)S(1)}, bf16[3,64,256]{2,1,0:T(8,128)(2,1)S(1)}, u32[]{:S(2)}, u32[]{:S(2)}) collective-permute-start(bf16[3,64,256]{2,1,0:T(8,128)(2,1)S(1)} %get-tuple-element.139), channel_id=1, source_target_pairs={{0,3},{1,2},{2,1},{3,0},{4,7},{5,6},{6,5},{7,4},{8,11},{9,10},{10,... | collective-permute-start | bytes 294920 | tf_op jit(solution)/shard_map/ppermute | solution.py:589
  75.4 12.7 %collective-permute-start.22 = (bf16[3,64,256]{2,1,0:T(8,128)(2,1)S(1)}, bf16[3,64,256]{2,1,0:T(8,128)(2,1)S(1)}, u32[]{:S(2)}, u32[]{:S(2)}) collective-permute-start(bf16[3,64,256]{2,1,0:T(8,128)(2,1)S(1)} %get-tuple-element.145), channel_id=1, source_target_pairs={{0,1},{1,0},{2,3},{3,2},{4,5},{5,4},{6,7},{7,6},{8,9},{9,8},{10,11... | collective-permute-start | bytes 294920 | tf_op jit(solution)/shard_map/ppermute | solution.py:589
  76.3 15.7 %collective-permute-start.23 = (bf16[3,64,256]{2,1,0:T(8,128)(2,1)S(1)}, bf16[3,64,256]{2,1,0:T(8,128)(2,1)S(1)}, u32[]{:S(2)}, u32[]{:S(2)}) collective-permute-start(bf16[3,64,256]{2,1,0:T(8,128)(2,1)S(1)} %get-tuple-element.146), channel_id=1, source_target_pairs={{0,2},{1,3},{2,0},{3,1},{4,6},{5,7},{6,4},{7,5},{8,10},{9,11},{10,... | collective-permute-start | bytes 294920 | tf_op jit(solution)/shard_map/ppermute | solution.py:589
  83.5 8.4 %collective-permute-start.24 = (bf16[3,64,256]{2,1,0:T(8,128)(2,1)S(1)}, bf16[3,64,256]{2,1,0:T(8,128)(2,1)S(1)}, u32[]{:S(2)}, u32[]{:S(2)}) collective-permute-start(bf16[3,64,256]{2,1,0:T(8,128)(2,1)S(1)} %get-tuple-element.147), channel_id=1, source_target_pairs={{0,3},{1,2},{2,1},{3,0},{4,7},{5,6},{6,5},{7,4},{8,11},{9,10},{10,... | collective-permute-start | bytes 294920 | tf_op jit(solution)/shard_map/ppermute | solution.py:589
  94.3 6.9 %collective-permute-start.26 = (bf16[192,1024]{1,0:T(8,128)(2,1)}, bf16[192,1024]{1,0:T(8,128)(2,1)}, u32[]{:S(2)}, u32[]{:S(2)}) collective-permute-start(bf16[192,1024]{1,0:T(8,128)(2,1)} %get-tuple-element.148.refs_3_), channel_id=1, source_target_pairs={{0,4},{4,0},{8,12},{12,8},{16,20},{20,16},{24,28},{28,24},{1,5},{5... | collective-permute-start | bytes 1179656 | tf_op jit(solution)/shard_map/ppermute | solution.py:583
  94.4 6.9 %collective-permute-start.25 = (bf16[192,1024]{1,0:T(8,128)(2,1)}, bf16[192,1024]{1,0:T(8,128)(2,1)}, u32[]{:S(2)}, u32[]{:S(2)}) collective-permute-start(bf16[192,1024]{1,0:T(8,128)(2,1)} %get-tuple-element.143.refs_2_), channel_id=1, source_target_pairs={{0,4},{4,0},{8,12},{12,8},{16,20},{20,16},{24,28},{28,24},{1,5},{5... | collective-permute-start | bytes 1179656 | tf_op jit(solution)/shard_map/ppermute | solution.py:583
  97.2 19.9 %all-to-all-start = ((bf16[8,256,256]{2,1,0:T(8,128)(2,1)}), bf16[8,256,256]{2,1,0:T(8,128)(2,1)S(1)}, u32[]{:S(2)}, u32[]{:S(2)}) async-start(bf16[8,256,256]{2,1,0:T(8,128)(2,1)} %packed.1), calls=%async_computation | async-start | bytes 2097152 | tf_op jit(solution)/shard_map/all_to_all | solution.py:889
  106.7 23.1 %collective-permute-start.29 = (bf16[2,320,512]{2,1,0:T(8,128)(2,1)}, bf16[2,320,512]{2,1,0:T(8,128)(2,1)}, u32[]{:S(2)}, u32[]{:S(2)}) collective-permute-start(bf16[2,320,512]{2,1,0:T(8,128)(2,1)} %get-tuple-element.169), channel_id=1, source_target_pairs={{0,16},{4,20},{8,24},{12,28},{16,0},{20,4},{24,8},{28,12},{1,17},{... | collective-permute-start | bytes 1966088 | tf_op jit(solution)/shard_map/ppermute | solution.py:583
  108.8 23.9 %collective-permute-start.27 = (bf16[2,320,512]{2,1,0:T(8,128)(2,1)}, bf16[2,320,512]{2,1,0:T(8,128)(2,1)}, u32[]{:S(2)}, u32[]{:S(2)}) collective-permute-start(bf16[2,320,512]{2,1,0:T(8,128)(2,1)} %get-tuple-element.167), channel_id=1, source_target_pairs={{0,8},{4,12},{8,0},{12,4},{16,24},{20,28},{24,16},{28,20},{1,9},{5... | collective-permute-start | bytes 1966088 | tf_op jit(solution)/shard_map/ppermute | solution.py:583
  118.4 16.0 %collective-permute-start.31 = (bf16[224,256]{1,0:T(8,128)(2,1)S(1)}, bf16[224,256]{1,0:T(8,128)(2,1)S(1)}, u32[]{:S(2)}, u32[]{:S(2)}) collective-permute-start(bf16[224,256]{1,0:T(8,128)(2,1)S(1)} %get-tuple-element.170.refs_0_), channel_id=1, source_target_pairs={{0,1},{1,0},{2,3},{3,2},{4,5},{5,4},{6,7},{7,6},{8,9},{9,8},{10,11... | collective-permute-start | bytes 344072 | tf_op jit(solution)/shard_map/ppermute | solution.py:589
  120.3 14.1 %collective-permute-start.32 = (bf16[224,256]{1,0:T(8,128)(2,1)S(1)}, bf16[224,256]{1,0:T(8,128)(2,1)S(1)}, u32[]{:S(2)}, u32[]{:S(2)}) collective-permute-start(bf16[224,256]{1,0:T(8,128)(2,1)S(1)} %get-tuple-element.170.refs_0_), channel_id=1, source_target_pairs={{0,2},{1,3},{2,0},{3,1},{4,6},{5,7},{6,4},{7,5},{8,10},{9,11},{10,... | collective-permute-start | bytes 344072 | tf_op jit(solution)/shard_map/ppermute | solution.py:589
  121.1 13.3 %collective-permute-start.33 = (bf16[224,256]{1,0:T(8,128)(2,1)S(1)}, bf16[224,256]{1,0:T(8,128)(2,1)S(1)}, u32[]{:S(2)}, u32[]{:S(2)}) collective-permute-start(bf16[224,256]{1,0:T(8,128)(2,1)S(1)} %get-tuple-element.170.refs_0_), channel_id=1, source_target_pairs={{0,3},{1,2},{2,1},{3,0},{4,7},{5,6},{6,5},{7,4},{8,11},{9,10},{10,... | collective-permute-start | bytes 344072 | tf_op jit(solution)/shard_map/ppermute | solution.py:589
  131.1 9.5 %collective-permute-start.30 = (bf16[1,320,512]{2,1,0:T(8,128)(2,1)S(1)}, bf16[1,320,512]{2,1,0:T(8,128)(2,1)S(1)}, u32[]{:S(2)}, u32[]{:S(2)}) collective-permute-start(bf16[1,320,512]{2,1,0:T(8,128)(2,1)S(1)} %slice.21), channel_id=1, source_target_pairs={{0,8},{4,12},{8,0},{12,4},{16,24},{20,28},{24,16},{28,20},{1,9},{5... | collective-permute-start | bytes 983048 | tf_op jit(solution)/shard_map/ppermute | solution.py:583
  133.9 9.5 %collective-permute-start.28 = (bf16[1,320,512]{2,1,0:T(8,128)(2,1)S(1)}, bf16[1,320,512]{2,1,0:T(8,128)(2,1)S(1)}, u32[]{:S(2)}, u32[]{:S(2)}) collective-permute-start(bf16[1,320,512]{2,1,0:T(8,128)(2,1)S(1)} %slice_bitcast_fusion), channel_id=1, source_target_pairs={{0,16},{4,20},{8,24},{12,28},{16,0},{20,4},{24,8},{28,12},{1,17},{... | collective-permute-start | bytes 983048 | tf_op jit(solution)/shard_map/ppermute | solution.py:583
  143.6 13.5 %collective-permute-start.34 = (bf16[2,80,1024]{2,1,0:T(8,128)(2,1)S(1)}, bf16[2,80,1024]{2,1,0:T(8,128)(2,1)S(1)}, u32[]{:S(2)}, u32[]{:S(2)}) collective-permute-start(bf16[2,80,1024]{2,1,0:T(8,128)(2,1)S(1)} %dynamic-slice_bitcast_fusion), channel_id=1, source_target_pairs={{0,1},{1,0},{2,3},{3,2},{4,5},{5,4},{6,7},{7,6},{8,9},{9,8},{10,11... | collective-permute-start | bytes 983048 | tf_op jit(solution)/shard_map/ppermute | solution.py:627
  145.6 8.5 %collective-permute-start.37 = (bf16[448,256]{1,0:T(8,128)(2,1)S(1)}, bf16[448,256]{1,0:T(8,128)(2,1)S(1)}, u32[]{:S(2)}, u32[]{:S(2)}) collective-permute-start(bf16[448,256]{1,0:T(8,128)(2,1)S(1)} %shard_sums.1.refs_0_), channel_id=1, source_target_pairs={{0,8},{4,12},{8,0},{12,4},{16,24},{20,28},{24,16},{28,20},{1,9},{5... | collective-permute-start | bytes 688136 | tf_op jit(solution)/shard_map/ppermute | solution.py:637
  145.9 10.8 %collective-permute-start.39 = (bf16[448,256]{1,0:T(8,128)(2,1)S(1)}, bf16[448,256]{1,0:T(8,128)(2,1)S(1)}, u32[]{:S(2)}, u32[]{:S(2)}) collective-permute-start(bf16[448,256]{1,0:T(8,128)(2,1)S(1)} %shard_sums.1.refs_0_), channel_id=1, source_target_pairs={{0,16},{4,20},{8,24},{12,28},{16,0},{20,4},{24,8},{28,12},{1,17},{... | collective-permute-start | bytes 688136 | tf_op jit(solution)/shard_map/ppermute | solution.py:637
  146.4 10.3 %collective-permute-start.41 = (bf16[448,256]{1,0:T(8,128)(2,1)S(1)}, bf16[448,256]{1,0:T(8,128)(2,1)S(1)}, u32[]{:S(2)}, u32[]{:S(2)}) collective-permute-start(bf16[448,256]{1,0:T(8,128)(2,1)S(1)} %shard_sums.1.refs_0_), channel_id=1, source_target_pairs={{0,24},{4,28},{8,16},{12,20},{16,8},{20,12},{24,0},{28,4},{1,25},{... | collective-permute-start | bytes 688136 | tf_op jit(solution)/shard_map/ppermute | solution.py:637
  149.1 9.5 %collective-permute-start.36 = (bf16[448,256]{1,0:T(8,128)(2,1)S(1)}, bf16[448,256]{1,0:T(8,128)(2,1)S(1)}, u32[]{:S(2)}, u32[]{:S(2)}) collective-permute-start(bf16[448,256]{1,0:T(8,128)(2,1)S(1)} %shard_sums.1.refs_0_), channel_id=1, source_target_pairs={{0,4},{4,0},{8,12},{12,8},{16,20},{20,16},{24,28},{28,24},{1,5},{5... | collective-permute-start | bytes 688136 | tf_op jit(solution)/shard_map/ppermute | solution.py:583
  154.1 4.4 %collective-permute-start.38 = (bf16[448,256]{1,0:T(8,128)(2,1)S(1)}, bf16[448,256]{1,0:T(8,128)(2,1)S(1)}, u32[]{:S(2)}, u32[]{:S(2)}) collective-permute-start(bf16[448,256]{1,0:T(8,128)(2,1)S(1)} %collective-permute-done.37.refs_2_), channel_id=1, source_target_pairs={{0,4},{4,0},{8,12},{12,8},{16,20},{20,16},{24,28},{28,24},{1,5},{5... | collective-permute-start | bytes 688136 | tf_op jit(solution)/shard_map/ppermute | solution.py:583
  156.6 1.9 %collective-permute-start.40 = (bf16[448,256]{1,0:T(8,128)(2,1)S(1)}, bf16[448,256]{1,0:T(8,128)(2,1)S(1)}, u32[]{:S(2)}, u32[]{:S(2)}) collective-permute-start(bf16[448,256]{1,0:T(8,128)(2,1)S(1)} %collective-permute-done.39.refs_4_), channel_id=1, source_target_pairs={{0,4},{4,0},{8,12},{12,8},{16,20},{20,16},{24,28},{28,24},{1,5},{5... | collective-permute-start | bytes 688136 | tf_op jit(solution)/shard_map/ppermute | solution.py:583
  156.6 1.9 %collective-permute-start.42 = (bf16[448,256]{1,0:T(8,128)(2,1)S(1)}, bf16[448,256]{1,0:T(8,128)(2,1)S(1)}, u32[]{:S(2)}, u32[]{:S(2)}) collective-permute-start(bf16[448,256]{1,0:T(8,128)(2,1)S(1)} %collective-permute-done.41.refs_6_), channel_id=1, source_target_pairs={{0,4},{4,0},{8,12},{12,8},{16,20},{20,16},{24,28},{28,24},{1,5},{5... | collective-permute-start | bytes 688136 | tf_op jit(solution)/shard_map/ppermute | solution.py:583
  157.3 10.4 %collective-permute-start.35 = (bf16[1,80,1024]{2,1,0:T(8,128)(2,1)S(1)}, bf16[1,80,1024]{2,1,0:T(8,128)(2,1)S(1)}, u32[]{:S(2)}, u32[]{:S(2)}) collective-permute-start(bf16[1,80,1024]{2,1,0:T(8,128)(2,1)S(1)} %constant_dynamic-slice_fusion), channel_id=1, source_target_pairs={{0,2},{1,3},{2,0},{3,1},{4,6},{5,7},{6,4},{7,5},{8,10},{9,11},{10,... | collective-permute-start | bytes 491528 | tf_op jit(solution)/shard_map/ppermute | solution.py:627
  (12 other events, 120.7 us)

commit v7 on v6

--- a/solution.py
+++ b/solution.py
@@ -615,29 +615,19 @@
     return ends
 
 
-def scatter_end(ends, shards, shard_at):
-    part = jnp.concatenate(ends, axis=-1)
-    part = part.reshape(shards, part.shape[0] // shards, -1)
-    bit = 1
-    while bit < shards:
-        split = part.reshape(part.shape[0] // 2, 2, *part.shape[1:])
-        mine = (shard_at // bit) % 2
-        keep = lax.dynamic_index_in_dim(split, mine, 1, keepdims=False)
-        send = lax.dynamic_index_in_dim(split, 1 - mine, 1, keepdims=False)
-        received = lax.ppermute(send, "fft", [(z, z ^ bit) for z in range(shards)])
-        part = keep.astype(FULL) + received.astype(FULL)
-        bit *= 2
-        if bit < shards:
-            part = part.astype(HALF)
-    return part[0]
-
-
-def from_all_groups(values, groups):
-    even = [values] + [
+def scatter_step(part, bit, shards, shard_at):
+    split = part.reshape(part.shape[0] // 2, 2, *part.shape[1:])
+    mine = (shard_at // bit) % 2
+    keep = lax.dynamic_index_in_dim(split, mine, 1, keepdims=False)
+    send = lax.dynamic_index_in_dim(split, 1 - mine, 1, keepdims=False)
+    received = lax.ppermute(send, "fft", [(z, z ^ bit) for z in range(shards)])
+    return keep.astype(FULL) + received.astype(FULL)
+
+
+def from_same_core(values, groups):
+    return [values] + [
         lax.ppermute(values, "grp", [(g, g ^ k) for g in range(groups)]) for k in range(2, groups, 2)
     ]
-    odd = [swap_bit(v, 0, groups) for v in even]
-    return [v for pair in zip(even, odd) for v in pair]
 
 
 def hi_lo(values):
@@ -881,18 +871,17 @@
     width = spec_w.shape[-1]
     blocks = spec_w.shape[2] // shards
     head_rows = head_w.shape[0] // groups
+    weight_sums = lax.all_to_all(
+        packed(routes, head_grad, spec_grad, predicted, groups), "grp", split_axis=0, concat_axis=0, tiled=True
+    )
     own_grads, other_grads, row_sums = [], [], []
     for first, res, back in zip(firsts, residual, spec_back):
         grad, row_sum = embedded_back_chunk(scal, embedded, stats, res, head_w, gain_row, back, first, cells)
-        if first == firsts[0]:
-            grad, head_grad, spec_grad = lax.optimization_barrier((grad, head_grad, spec_grad))
-            weight_sums = lax.all_to_all(
-                packed(routes, head_grad, spec_grad, predicted, groups), "grp", split_axis=0, concat_axis=0, tiled=True
-            )
         own_grads.append(grad)
         other_grads.append(swap_bit(grad, 0, groups))
         row_sums.append(row_sum)
     grads = own_grads + other_grads
+    grads, weight_sums = lax.optimization_barrier((grads, weight_sums))
     sent = embed_grad_parts(scal, turned, grads, groups, 1)
     sent, kept_turned = lax.optimization_barrier((sent, turned))
     top_bit = groups.bit_length() - 2
@@ -904,9 +893,20 @@
     predictions = predictions.reshape(targets.shape)
     spec_rows = spec_grad.shape[0] // groups
     outgoing = shard_sums(routes, across([small] * shards), head_rows, spec_rows, spec_bias.shape[0])
-    ends, outgoing = lax.optimization_barrier((ends, outgoing))
-    gathered = from_all_groups(outgoing, groups)
-    embed_grad = scatter_end(ends, shards, shard_at)
+    _, outgoing = lax.optimization_barrier((ends, outgoing))
+    part = jnp.concatenate(ends, axis=-1)
+    part = part.reshape(shards, part.shape[0] // shards, -1)
+    part = scatter_step(part, 1, shards, shard_at)
+    even = from_same_core(outgoing, groups)
+    bit = 2
+    while bit < shards:
+        part = part.astype(HALF)
+        if bit == 2:
+            _, even = lax.optimization_barrier((part, even))
+        part = scatter_step(part, bit, shards, shard_at)
+        bit *= 2
+    embed_grad = part[0]
+    gathered = [v for pair in zip(even, [swap_bit(v, 0, groups) for v in even]) for v in pair]
     head_grad, spec_w_grad, spec_b_grad, gain_grad, embed_bias_grad, head_bias_grad = assembled(
         scal, gathered, head_rows, shards, blocks, width
     )

time: 169 us -> 181 us (1.071)
  local copies, waits for them, and re-layouts: 1.89 us -> 17.9 us
  Pallas kernels: 43.7 us -> 41.6 us
  waiting for transfers between devices: 50.3 us -> 48.3 us
    unnamed x32 -> x94, local copies, waits for them, and re-layouts: 0.95 us -> 16.4 us
    ppermute x5, waiting for transfers between devices: 14.3 us -> 7.19 us  [the longest x3 7.19 us: from_same_core(): lax.ppermute(values, 'grp', [(g, g ^ k) for g in range(groups)])]
    ppermute x27, waiting for transfers between devices: 18.3 us -> 24.2 us  [across(): lax.ppermute(pieces[k], 'fft', [(z, z ^ k) for z in range(shards)])]
    all_to_all x1, waiting for transfers between devices: 2.34 us -> 0.01 us  [on_device(): lax.all_to_all(packed(routes, head_grad, spec_grad, predicted, groups), '...]
    pallas_call x2, Pallas kernels: 10.1 us -> 8.18 us  [embed_grad_parts(): pl.pallas_call(body, grid_spec=pltpu.PrefetchScalarGridSpec(num_scalar_pr...]
  transfers between devices with their start and end apart: 44 -> 44, of which waited for: 13 -> 15; matrix products, arithmetic and copies ran while one was open for 2% -> 2% of each run, Pallas kernels for 18% -> 12%
where the time goes in v7:
time: 181 us
  starting transfers between devices  66.5 us (37%)
  waiting for transfers between devices  48.3 us (27%)
  Pallas kernels  41.6 us (23%)
  local copies, waits for them, and re-layouts  17.9 us (10%)
  other arithmetic  5.17 us (3%)
    ppermute x27, starting transfers between devices, across(): lax.ppermute(pieces[k], 'fft', [(z, z ^ k) for z in range(shards)])  49.4 us
    ppermute x27, waiting for transfers between devices, across(): lax.ppermute(pieces[k], 'fft', [(z, z ^ k) for z in range(shards)])  24.2 us
    ppermute x11, waiting for transfers between devices, swap_bit(): lax.ppermute(values, 'grp', [(g, g ^ 1 << bit) for g in range(groups)])  16.9 us
    unnamed x94, local copies, waits for them, and re-layouts  16.4 us
    pallas_call x1, Pallas kernels, embed(): pl.pallas_call(body, grid_spec=pltpu.PrefetchScalarGridSpec(num_scalar_pr...  10 us
    pallas_call x2, Pallas kernels, embed_grad_parts(): pl.pallas_call(body, grid_spec=pltpu.PrefetchScalarGridSpec(num_scalar_pr...  8.18 us
    ppermute x11, starting transfers between devices, swap_bit(): lax.ppermute(values, 'grp', [(g, g ^ 1 << bit) for g in range(groups)])  7.88 us
    pallas_call x2, Pallas kernels, spectral_back_chunk(): pl.pallas_call(body, grid_spec=pltpu.PrefetchScalarGridSpec(num_scalar_pr...  7.4 us
  transfers between devices with their start and end apart: 44, of which 15 were waited for; matrix products, arithmetic and copies ran while one was open for 2% of the time, Pallas kernels for 12%

profile of v7, /device:TPU:0, one launch (start us, length us, event | category | flops | bytes accessed | tf_op | source)
XLA Modules:
  0.0 180.6 jit_solution(15218724417669473904)
XLA Ops:
  2.0 10.0 %embed.1 = (bf16[384,1024]{1,0:T(8,128)(2,1)}, bf16[384,1024]{1,0:T(8,128)(2,1)}, f32[384,256]{1,0:T(8,128)}, bf16[4,320,384]{2,1,0:T(8,128)(2,1)}, bf16[4,320,3...) custom-call(s32[15]{0:T(128)} %concatenate.17.scal_ref, ...), custom_call_target="tpu_custom_call" | custom-call | flops 2013265920 | bytes 7208960 | tf_op jit(solution)/shard_map/embed/pallas_call | solution.py:157
  12.1 4.1 %collective-permute-start.10 = (bf16[3,64,256]{2,1,0:T(8,128)(2,1)}, bf16[3,64,256]{2,1,0:T(8,128)(2,1)S(1)}, u32[]{:S(2)}, u32[]{:S(2)}) collective-permute-start(bf16[3,64,256]{2,1,0:T(8,128)(2,1)} %get-tuple-element.114), channel_id=1, source_target_pairs={{0,2},{1,3},{2,0},{3,1},{4,6},{5,7},{6,4},{7,5},{8,10},{9,11},{10,... | collective-permute-start | bytes 294920 | tf_op jit(solution)/shard_map/ppermute | solution.py:589
  16.2 1.3 collective-permute-start.11
  17.7 1.8 collective-permute-start
  19.5 1.7 collective-permute-start.1
  21.2 3.0 %collective-permute-done.10.refs_2_ = bf16[3,64,256]{2,1,0:T(8,128)(2,1)S(1)} collective-permute-done((bf16[3,64,256]{2,1,0:T(8,128)(2,1)}, bf16[3,64,256]{2,1,0:T(8,128)(2,1)S(1)}, u32[]{:S(2)}, u32[]{:S(2)}) %collective-permute-start.10) | collective-permute-done | bytes 98336 | tf_op jit(solution)/shard_map/ppermute | solution.py:589
  24.3 2.8 %collective-permute-start.2 = (bf16[3,64,256]{2,1,0:T(8,128)(2,1)}, bf16[3,64,256]{2,1,0:T(8,128)(2,1)S(1)}, u32[]{:S(2)}, u32[]{:S(2)}) collective-permute-start(bf16[3,64,256]{2,1,0:T(8,128)(2,1)} %get-tuple-element.101), channel_id=1, source_target_pairs={{0,3},{1,2},{2,1},{3,0},{4,7},{5,6},{6,5},{7,4},{8,11},{9,10},{10,... | collective-permute-start | bytes 294920 | tf_op jit(solution)/shard_map/ppermute | solution.py:589
  28.8 2.3 %spectral.3 = (bf16[3,64,256]{2,1,0:T(8,128)(2,1)S(1)}, bf16[3,64,256]{2,1,0:T(8,128)(2,1)S(1)}, bf16[3,64,256]{2,1,0:T(8,128)(2,1)S(1)}, bf16[3,64,256]{2,1,0:T...) custom-call(s32[15]{0:T(128)S(1)} %copy-done.17, ...), custom_call_target="tpu_custom_call" | custom-call | flops 704643072 | bytes 3145728 | tf_op jit(solution)/shard_map/spectral/pallas_call | solution.py:277
  31.3 1.6 collective-permute-start.13
  32.9 2.7 %collective-permute-start.14 = (bf16[3,64,256]{2,1,0:T(8,128)(2,1)S(1)}, bf16[3,64,256]{2,1,0:T(8,128)(2,1)S(1)}, u32[]{:S(2)}, u32[]{:S(2)}) collective-permute-start(bf16[3,64,256]{2,1,0:T(8,128)(2,1)S(1)} %get-tuple-element.122), channel_id=1, source_target_pairs={{0,3},{1,2},{2,1},{3,0},{4,7},{5,6},{6,5},{7,4},{8,11},{9,10},{10,... | collective-permute-start | bytes 294920 | tf_op jit(solution)/shard_map/ppermute | solution.py:589
  38.8 2.3 %spectral.2 = (bf16[3,64,256]{2,1,0:T(8,128)(2,1)S(1)}, bf16[3,64,256]{2,1,0:T(8,128)(2,1)S(1)}, bf16[3,64,256]{2,1,0:T(8,128)(2,1)S(1)}, bf16[3,64,256]{2,1,0:T...) custom-call(s32[15]{0:T(128)S(1)} %copy-done.17, ...), custom_call_target="tpu_custom_call" | custom-call | flops 704643072 | bytes 3145728 | tf_op jit(solution)/shard_map/spectral/pallas_call | solution.py:277
  41.3 1.7 collective-permute-start.4
  43.0 2.7 %collective-permute-start.5 = (bf16[3,64,256]{2,1,0:T(8,128)(2,1)S(1)}, bf16[3,64,256]{2,1,0:T(8,128)(2,1)S(1)}, u32[]{:S(2)}, u32[]{:S(2)}) collective-permute-start(bf16[3,64,256]{2,1,0:T(8,128)(2,1)S(1)} %get-tuple-element.110), channel_id=1, source_target_pairs={{0,3},{1,2},{2,1},{3,0},{4,7},{5,6},{6,5},{7,4},{8,11},{9,10},{10,... | collective-permute-start | bytes 294920 | tf_op jit(solution)/shard_map/ppermute | solution.py:589
  46.8 1.7 collective-permute-start.16
  48.5 2.7 %collective-permute-start.17 = (bf16[3,64,256]{2,1,0:T(8,128)(2,1)S(1)}, bf16[3,64,256]{2,1,0:T(8,128)(2,1)S(1)}, u32[]{:S(2)}, u32[]{:S(2)}) collective-permute-start(bf16[3,64,256]{2,1,0:T(8,128)(2,1)S(1)} %get-tuple-element.126.refs_2_.refs_0_.res_ref), channel_id=1, source_target_pairs={{0,3},{1,2},{2,1},{3,0},{4,7},{5,6},{6,5},{7,4},{8,11},{9,10},{10,... | collective-permute-start | bytes 294920 | tf_op jit(solution)/shard_map/ppermute | solution.py:589
  53.2 6.5 %collective-permute-start.6 = (bf16[3,64,256]{2,1,0:T(8,128)(2,1)S(1)}, bf16[3,64,256]{2,1,0:T(8,128)(2,1)S(1)}, u32[]{:S(2)}, u32[]{:S(2)}) collective-permute-start(bf16[3,64,256]{2,1,0:T(8,128)(2,1)S(1)} %get-tuple-element.111.refs_3_.refs_0_.res_ref), channel_id=1, source_target_pairs={{0,1},{1,0},{2,3},{3,2},{4,5},{5,4},{6,7},{7,6},{8,9},{9,8},{10,11... | collective-permute-start | bytes 294920 | tf_op jit(solution)/shard_map/ppermute | solution.py:589
  60.6 1.5 collective-permute-start.8
  62.7 3.7 %spectral_back.2 = (bf16[3,64,256]{2,1,0:T(8,128)(2,1)S(1)}, bf16[3,64,256]{2,1,0:T(8,128)(2,1)}, bf16[3,64,256]{2,1,0:T(8,128)(2,1)S(1)}, bf16[3,64,256]{2,1,0:...) custom-call(s32[15]{0:T(128)S(1)} %copy-done.17, bf16[3,512,256]{2,1,0:T(8,128)(2,1)S(1)} %copy-done.4, ...), custom_call_target="tpu_custom_call" | custom-call | flops 1006632960 | bytes 3145728 | tf_op jit(solution)/shard_map/spectral_back/pallas_call | solution.py:440
  67.0 2.1 %collective-permute-done.7.refs_2_ = bf16[3,64,256]{2,1,0:T(8,128)(2,1)S(1)} collective-permute-done((bf16[3,64,256]{2,1,0:T(8,128)(2,1)S(1)}, bf16[3,64,256]{2,1,0:T(8,128)(2,1)S(1)}, u32[]{:S(2)}, u32[]{:S(2)}) %collective-permute-start.7) | collective-permute-done | bytes 98336 | tf_op jit(solution)/shard_map/ppermute | solution.py:589
  69.0 3.7 %spectral_back.3 = (bf16[3,64,256]{2,1,0:T(8,128)(2,1)S(1)}, bf16[3,64,256]{2,1,0:T(8,128)(2,1)S(1)}, bf16[3,64,256]{2,1,0:T(8,128)(2,1)}, bf16[3,64,256]{2,1,0:...) custom-call(s32[15]{0:T(128)S(1)} %copy-done.17, bf16[3,512,256]{2,1,0:T(8,128)(2,1)S(1)} %copy-done.4, ...), custom_call_target="tpu_custom_call" | custom-call | flops 1006632960 | bytes 3145728 | tf_op jit(solution)/shard_map/spectral_back/pallas_call | solution.py:440
  79.0 1.7 packed.1
  80.7 3.9 %all-to-all-start = ((bf16[8,256,256]{2,1,0:T(8,128)(2,1)}), bf16[8,256,256]{2,1,0:T(8,128)(2,1)S(1)}, u32[]{:S(2)}, u32[]{:S(2)}) async-start(bf16[8,256,256]{2,1,0:T(8,128)(2,1)} %packed.1), calls=%async_computation | async-start | bytes 2097152 | tf_op jit(solution)/shard_map/all_to_all | solution.py:874
  84.6 1.7 collective-permute-start.22
  87.4 1.6 collective-permute-start.24
  89.8 3.1 %collective-permute-start.20 = (bf16[3,64,256]{2,1,0:T(8,128)(2,1)}, bf16[3,64,256]{2,1,0:T(8,128)(2,1)S(1)}, u32[]{:S(2)}, u32[]{:S(2)}) collective-permute-start(bf16[3,64,256]{2,1,0:T(8,128)(2,1)} %copy-done.33), channel_id=1, source_target_pairs={{0,2},{1,3},{2,0},{3,1},{4,6},{5,7},{6,4},{7,5},{8,10},{9,11},{10,... | collective-permute-start | bytes 294920 | tf_op jit(solution)/shard_map/ppermute | solution.py:589
  92.8 4.4 %collective-permute-done.23.refs_2_ = bf16[3,64,256]{2,1,0:T(8,128)(2,1)S(1)} collective-permute-done((bf16[3,64,256]{2,1,0:T(8,128)(2,1)}, bf16[3,64,256]{2,1,0:T(8,128)(2,1)S(1)}, u32[]{:S(2)}, u32[]{:S(2)}) %collective-permute-start.23) | collective-permute-done | bytes 98336 | tf_op jit(solution)/shard_map/ppermute | solution.py:589
  97.2 2.5 %collective-permute-start.21 = (bf16[3,64,256]{2,1,0:T(8,128)(2,1)}, bf16[3,64,256]{2,1,0:T(8,128)(2,1)S(1)}, u32[]{:S(2)}, u32[]{:S(2)}) collective-permute-start(bf16[3,64,256]{2,1,0:T(8,128)(2,1)} %copy-done.32), channel_id=1, source_target_pairs={{0,3},{1,2},{2,1},{3,0},{4,7},{5,6},{6,5},{7,4},{8,11},{9,10},{10,... | collective-permute-start | bytes 294920 | tf_op jit(solution)/shard_map/ppermute | solution.py:589
  99.7 1.4 embedded_back.3
  101.2 4.4 %collective-permute-done.20.refs_2_ = bf16[3,64,256]{2,1,0:T(8,128)(2,1)S(1)} collective-permute-done((bf16[3,64,256]{2,1,0:T(8,128)(2,1)}, bf16[3,64,256]{2,1,0:T(8,128)(2,1)S(1)}, u32[]{:S(2)}, u32[]{:S(2)}) %collective-permute-start.20) | collective-permute-done | bytes 98336 | tf_op jit(solution)/shard_map/ppermute | solution.py:589
  105.6 1.4 embedded_back.2
  113.1 4.1 %embed_grad.2 = (bf16[2,320,512]{2,1,0:T(8,128)(2,1)S(1)}, bf16[2,320,512]{2,1,0:T(8,128)(2,1)S(1)}) custom-call(s32[15]{0:T(128)S(1)} %copy-done.17, bf16[4,320,384]{2,1,0:T(8,128)(2,1)S(1)} %copy-done.40, bf16[4,320,384]{2,1,0:T(8,128)(2,1)} %collective-permute-done.18.refs_1_, bf16[192,1024]{1,0:T(8,128)(2,1)S(1)} %copy-done.31, ...), custom_call_target="tpu_custom_call" | custom-call | flops 1006632960 | bytes 4063232 | tf_op jit(solution)/shard_map/embed_grad/pallas_call | solution.py:555
  117.2 1.9 %collective-permute-start.29 = (bf16[2,320,512]{2,1,0:T(8,128)(2,1)S(1)}, bf16[2,320,512]{2,1,0:T(8,128)(2,1)S(1)}, u32[]{:S(2)}, u32[]{:S(2)}) collective-permute-start(bf16[2,320,512]{2,1,0:T(8,128)(2,1)S(1)} %get-tuple-element.174), channel_id=1, source_target_pairs={{0,16},{4,20},{8,24},{12,28},{16,0},{20,4},{24,8},{28,12},{1,17},{... | collective-permute-start | bytes 1966088 | tf_op jit(solution)/shard_map/ppermute | solution.py:583
  119.1 1.5 collective-permute-start.27
  120.5 4.1 %embed_grad.3 = (bf16[2,320,512]{2,1,0:T(8,128)(2,1)S(1)}, bf16[2,320,512]{2,1,0:T(8,128)(2,1)S(1)}) custom-call(s32[15]{0:T(128)S(1)} %copy-done.17, bf16[4,320,384]{2,1,0:T(8,128)(2,1)S(1)} %copy-done.41, bf16[4,320,384]{2,1,0:T(8,128)(2,1)} %collective-permute-done.18.refs_1_, bf16[192,1024]{1,0:T(8,128)(2,1)S(1)} %copy-done.31, ...), custom_call_target="tpu_custom_call" | custom-call | flops 1006632960 | bytes 4063232 | tf_op jit(solution)/shard_map/embed_grad/pallas_call | solution.py:555
  124.6 9.6 %collective-permute-done.29 = bf16[2,320,512]{2,1,0:T(8,128)(2,1)S(1)} collective-permute-done((bf16[2,320,512]{2,1,0:T(8,128)(2,1)S(1)}, bf16[2,320,512]{2,1,0:T(8,128)(2,1)S(1)}, u32[]{:S(2)}, u32[]{:S(2)}) %collective-permute-start.29) | collective-permute-done | bytes 655392 | tf_op jit(solution)/shard_map/ppermute | solution.py:583
  134.5 1.8 collective-permute-start.30
  136.5 1.5 collective-permute-start.28
  138.1 5.8 %collective-permute-done.30 = bf16[1,320,512]{2,1,0:T(8,128)(2,1)} collective-permute-done((bf16[1,320,512]{2,1,0:T(8,128)(2,1)S(1)}, bf16[1,320,512]{2,1,0:T(8,128)(2,1)}, u32[]{:S(2)}, u32[]{:S(2)}) %collective-permute-start.30) | collective-permute-done | bytes 327712 | tf_op jit(solution)/shard_map/ppermute | solution.py:583
  146.7 1.7 collective-permute-start.31
  150.0 2.6 %collective-permute-start.34 = (bf16[224,256]{1,0:T(8,128)(2,1)S(1)}, bf16[224,256]{1,0:T(8,128)(2,1)S(1)}, u32[]{:S(2)}, u32[]{:S(2)}) collective-permute-start(bf16[224,256]{1,0:T(8,128)(2,1)S(1)} %get-tuple-element.175.refs_0_), channel_id=1, source_target_pairs={{0,2},{1,3},{2,0},{3,1},{4,6},{5,7},{6,4},{7,5},{8,10},{9,11},{10,... | collective-permute-start | bytes 344072 | tf_op jit(solution)/shard_map/ppermute | solution.py:589
  152.6 1.4 collective-permute-start.35
  154.1 6.2 %collective-permute-done.33.refs_1_ = bf16[224,256]{1,0:T(8,128)(2,1)S(1)} collective-permute-done((bf16[224,256]{1,0:T(8,128)(2,1)S(1)}, bf16[224,256]{1,0:T(8,128)(2,1)S(1)}, u32[]{:S(2)}, u32[]{:S(2)}) %collective-permute-start.33) | collective-permute-done | bytes 114720 | tf_op jit(solution)/shard_map/ppermute | solution.py:589
  160.3 3.8 %collective-permute-done.35.refs_3_ = bf16[224,256]{1,0:T(8,128)(2,1)S(1)} collective-permute-done((bf16[224,256]{1,0:T(8,128)(2,1)S(1)}, bf16[224,256]{1,0:T(8,128)(2,1)S(1)}, u32[]{:S(2)}, u32[]{:S(2)}) %collective-permute-start.35) | collective-permute-done | bytes 114720 | tf_op jit(solution)/shard_map/ppermute | solution.py:589
  164.6 1.4 collective-permute-start.36
  166.1 1.4 collective-permute-start.37
  168.4 3.5 %collective-permute-done.36.refs_2_ = bf16[448,256]{1,0:T(8,128)(2,1)S(1)} collective-permute-done((bf16[448,256]{1,0:T(8,128)(2,1)S(1)}, bf16[448,256]{1,0:T(8,128)(2,1)S(1)}, u32[]{:S(2)}, u32[]{:S(2)}) %collective-permute-start.36) | collective-permute-done | bytes 229408 | tf_op jit(solution)/shard_map/ppermute | solution.py:629
  171.9 3.7 %collective-permute-done.37.refs_4_ = bf16[448,256]{1,0:T(8,128)(2,1)S(1)} collective-permute-done((bf16[448,256]{1,0:T(8,128)(2,1)S(1)}, bf16[448,256]{1,0:T(8,128)(2,1)S(1)}, u32[]{:S(2)}, u32[]{:S(2)}) %collective-permute-start.37) | collective-permute-done | bytes 229408 | tf_op jit(solution)/shard_map/ppermute | solution.py:629
  178.1 2.5 %assembled.1 = (f32[1024,256]{1,0:T(8,128)}, f32[2,2,8,128,128]{4,3,2,1,0:T(8,128)}, f32[2,2,8,128]{3,2,1,0:T(8,128)}, f32[1,1024]{1,0:T(1,128)}, f32[1,1024]{1,0:T(1,128)}, /*index=5*/f32[1,256]{1,0:T(1,128)}) custom-call(s32[15]{0:T(128)S(1)} %copy-done.17, bf16[448,256]{1,0:T(8,128)(2,1)S(1)} %shard_sums.1.refs_0_, ...), custom_call_target="tpu_custom_call" | custom-call | tf_op jit(solution)/shard_map/assembled/pallas_call | solution.py:790
  (170 shorter events, 34.8 us)
Async XLA Ops:
  2.0 25.9 %copy-start.2 = (bf16[2,2,8,128,128]{4,3,2,1,0:T(8,128)(2,1)S(1)}, bf16[2,2,8,128,128]{4,3,2,1,0:T(8,128)(2,1)}, u32[]{:S(2)}) copy-start(bf16[2,2,8,128,128]{4,3,2,1,0:T(8,128)(2,1)} %w_ref.15) | copy-start | bytes 3145732
  2.0 25.9 %copy-start.4 = (bf16[3,512,256]{2,1,0:T(8,128)(2,1)S(1)}, bf16[3,512,256]{2,1,0:T(8,128)(2,1)}, u32[]{:S(2)}) copy-start(bf16[3,512,256]{2,1,0:T(8,128)(2,1)} %constant.76.clone.t_ref) | copy-start | bytes 2359300
  2.0 25.9 %copy-start.17 = (s32[15]{0:T(128)S(1)}, s32[15]{0:T(128)}, u32[]{:S(2)}) copy-start(s32[15]{0:T(128)} %concatenate.17.scal_ref) | copy-start | bytes 184
  2.0 25.9 %copy-start.38 = (f32[2,2,8,128]{3,2,1,0:T(8,128)S(1)}, f32[2,2,8,128]{3,2,1,0:T(8,128)}, u32[]{:S(2)}) copy-start(f32[2,2,8,128]{3,2,1,0:T(8,128)} %b_ref.3) | copy-start | bytes 49156
  12.1 12.2 %collective-permute-start.10 = (bf16[3,64,256]{2,1,0:T(8,128)(2,1)}, bf16[3,64,256]{2,1,0:T(8,128)(2,1)S(1)}, u32[]{:S(2)}, u32[]{:S(2)}) collective-permute-start(bf16[3,64,256]{2,1,0:T(8,128)(2,1)} %get-tuple-element.114), channel_id=1, source_target_pairs={{0,2},{1,3},{2,0},{3,1},{4,6},{5,7},{6,4},{7,5},{8,10},{9,11},{10,... | collective-permute-start | bytes 294920 | tf_op jit(solution)/shard_map/ppermute | solution.py:589
  16.2 11.7 %collective-permute-start.11 = (bf16[3,64,256]{2,1,0:T(8,128)(2,1)}, bf16[3,64,256]{2,1,0:T(8,128)(2,1)S(1)}, u32[]{:S(2)}, u32[]{:S(2)}) collective-permute-start(bf16[3,64,256]{2,1,0:T(8,128)(2,1)} %get-tuple-element.115), channel_id=1, source_target_pairs={{0,3},{1,2},{2,1},{3,0},{4,7},{5,6},{6,5},{7,4},{8,11},{9,10},{10,... | collective-permute-start | bytes 294920 | tf_op jit(solution)/shard_map/ppermute | solution.py:589
  17.5 10.3 %collective-permute-start.9 = (bf16[3,64,256]{2,1,0:T(8,128)(2,1)}, bf16[3,64,256]{2,1,0:T(8,128)(2,1)S(1)}, u32[]{:S(2)}, u32[]{:S(2)}) collective-permute-start(bf16[3,64,256]{2,1,0:T(8,128)(2,1)} %get-tuple-element.113), channel_id=1, source_target_pairs={{0,1},{1,0},{2,3},{3,2},{4,5},{5,4},{6,7},{7,6},{8,9},{9,8},{10,11... | collective-permute-start | bytes 294920 | tf_op jit(solution)/shard_map/ppermute | solution.py:589
  17.7 15.1 %collective-permute-start = (bf16[3,64,256]{2,1,0:T(8,128)(2,1)}, bf16[3,64,256]{2,1,0:T(8,128)(2,1)S(1)}, u32[]{:S(2)}, u32[]{:S(2)}) collective-permute-start(bf16[3,64,256]{2,1,0:T(8,128)(2,1)} %get-tuple-element.99), channel_id=1, source_target_pairs={{0,1},{1,0},{2,3},{3,2},{4,5},{5,4},{6,7},{7,6},{8,9},{9,8},{10,11... | collective-permute-start | bytes 294920 | tf_op jit(solution)/shard_map/ppermute | solution.py:589
  19.5 16.1 %collective-permute-start.1 = (bf16[3,64,256]{2,1,0:T(8,128)(2,1)}, bf16[3,64,256]{2,1,0:T(8,128)(2,1)S(1)}, u32[]{:S(2)}, u32[]{:S(2)}) collective-permute-start(bf16[3,64,256]{2,1,0:T(8,128)(2,1)} %get-tuple-element.100), channel_id=1, source_target_pairs={{0,2},{1,3},{2,0},{3,1},{4,6},{5,7},{6,4},{7,5},{8,10},{9,11},{10,... | collective-permute-start | bytes 294920 | tf_op jit(solution)/shard_map/ppermute | solution.py:589
  24.3 11.3 %collective-permute-start.2 = (bf16[3,64,256]{2,1,0:T(8,128)(2,1)}, bf16[3,64,256]{2,1,0:T(8,128)(2,1)S(1)}, u32[]{:S(2)}, u32[]{:S(2)}) collective-permute-start(bf16[3,64,256]{2,1,0:T(8,128)(2,1)} %get-tuple-element.101), channel_id=1, source_target_pairs={{0,3},{1,2},{2,1},{3,0},{4,7},{5,6},{6,5},{7,4},{8,11},{9,10},{10,... | collective-permute-start | bytes 294920 | tf_op jit(solution)/shard_map/ppermute | solution.py:589
  31.1 11.9 %collective-permute-start.12 = (bf16[3,64,256]{2,1,0:T(8,128)(2,1)S(1)}, bf16[3,64,256]{2,1,0:T(8,128)(2,1)S(1)}, u32[]{:S(2)}, u32[]{:S(2)}) collective-permute-start(bf16[3,64,256]{2,1,0:T(8,128)(2,1)S(1)} %get-tuple-element.120), channel_id=1, source_target_pairs={{0,1},{1,0},{2,3},{3,2},{4,5},{5,4},{6,7},{7,6},{8,9},{9,8},{10,11... | collective-permute-start | bytes 294920 | tf_op jit(solution)/shard_map/ppermute | solution.py:589
  31.3 14.4 %collective-permute-start.13 = (bf16[3,64,256]{2,1,0:T(8,128)(2,1)S(1)}, bf16[3,64,256]{2,1,0:T(8,128)(2,1)S(1)}, u32[]{:S(2)}, u32[]{:S(2)}) collective-permute-start(bf16[3,64,256]{2,1,0:T(8,128)(2,1)S(1)} %get-tuple-element.121), channel_id=1, source_target_pairs={{0,2},{1,3},{2,0},{3,1},{4,6},{5,7},{6,4},{7,5},{8,10},{9,11},{10,... | collective-permute-start | bytes 294920 | tf_op jit(solution)/shard_map/ppermute | solution.py:589
  32.9 12.9 %collective-permute-start.14 = (bf16[3,64,256]{2,1,0:T(8,128)(2,1)S(1)}, bf16[3,64,256]{2,1,0:T(8,128)(2,1)S(1)}, u32[]{:S(2)}, u32[]{:S(2)}) collective-permute-start(bf16[3,64,256]{2,1,0:T(8,128)(2,1)S(1)} %get-tuple-element.122), channel_id=1, source_target_pairs={{0,3},{1,2},{2,1},{3,0},{4,7},{5,6},{6,5},{7,4},{8,11},{9,10},{10,... | collective-permute-start | bytes 294920 | tf_op jit(solution)/shard_map/ppermute | solution.py:589
  41.1 7.4 %collective-permute-start.3 = (bf16[3,64,256]{2,1,0:T(8,128)(2,1)S(1)}, bf16[3,64,256]{2,1,0:T(8,128)(2,1)S(1)}, u32[]{:S(2)}, u32[]{:S(2)}) collective-permute-start(bf16[3,64,256]{2,1,0:T(8,128)(2,1)S(1)} %get-tuple-element.108), channel_id=1, source_target_pairs={{0,1},{1,0},{2,3},{3,2},{4,5},{5,4},{6,7},{7,6},{8,9},{9,8},{10,11... | collective-permute-start | bytes 294920 | tf_op jit(solution)/shard_map/ppermute | solution.py:589
  41.3 10.6 %collective-permute-start.4 = (bf16[3,64,256]{2,1,0:T(8,128)(2,1)S(1)}, bf16[3,64,256]{2,1,0:T(8,128)(2,1)S(1)}, u32[]{:S(2)}, u32[]{:S(2)}) collective-permute-start(bf16[3,64,256]{2,1,0:T(8,128)(2,1)S(1)} %get-tuple-element.109), channel_id=1, source_target_pairs={{0,2},{1,3},{2,0},{3,1},{4,6},{5,7},{6,4},{7,5},{8,10},{9,11},{10,... | collective-permute-start | bytes 294920 | tf_op jit(solution)/shard_map/ppermute | solution.py:589
  43.0 9.2 %collective-permute-start.5 = (bf16[3,64,256]{2,1,0:T(8,128)(2,1)S(1)}, bf16[3,64,256]{2,1,0:T(8,128)(2,1)S(1)}, u32[]{:S(2)}, u32[]{:S(2)}) collective-permute-start(bf16[3,64,256]{2,1,0:T(8,128)(2,1)S(1)} %get-tuple-element.110), channel_id=1, source_target_pairs={{0,3},{1,2},{2,1},{3,0},{4,7},{5,6},{6,5},{7,4},{8,11},{9,10},{10,... | collective-permute-start | bytes 294920 | tf_op jit(solution)/shard_map/ppermute | solution.py:589
  46.7 13.9 %collective-permute-start.15 = (bf16[3,64,256]{2,1,0:T(8,128)(2,1)S(1)}, bf16[3,64,256]{2,1,0:T(8,128)(2,1)S(1)}, u32[]{:S(2)}, u32[]{:S(2)}) collective-permute-start(bf16[3,64,256]{2,1,0:T(8,128)(2,1)S(1)} %get-tuple-element.126.refs_2_.refs_0_.res_ref), channel_id=1, source_target_pairs={{0,1},{1,0},{2,3},{3,2},{4,5},{5,4},{6,7},{7,6},{8,9},{9,8},{10,11... | collective-permute-start | bytes 294920 | tf_op jit(solution)/shard_map/ppermute | solution.py:589
  46.8 15.8 %collective-permute-start.16 = (bf16[3,64,256]{2,1,0:T(8,128)(2,1)S(1)}, bf16[3,64,256]{2,1,0:T(8,128)(2,1)S(1)}, u32[]{:S(2)}, u32[]{:S(2)}) collective-permute-start(bf16[3,64,256]{2,1,0:T(8,128)(2,1)S(1)} %get-tuple-element.126.refs_2_.refs_0_.res_ref), channel_id=1, source_target_pairs={{0,2},{1,3},{2,0},{3,1},{4,6},{5,7},{6,4},{7,5},{8,10},{9,11},{10,... | collective-permute-start | bytes 294920 | tf_op jit(solution)/shard_map/ppermute | solution.py:589
  48.5 14.2 %collective-permute-start.17 = (bf16[3,64,256]{2,1,0:T(8,128)(2,1)S(1)}, bf16[3,64,256]{2,1,0:T(8,128)(2,1)S(1)}, u32[]{:S(2)}, u32[]{:S(2)}) collective-permute-start(bf16[3,64,256]{2,1,0:T(8,128)(2,1)S(1)} %get-tuple-element.126.refs_2_.refs_0_.res_ref), channel_id=1, source_target_pairs={{0,3},{1,2},{2,1},{3,0},{4,7},{5,6},{6,5},{7,4},{8,11},{9,10},{10,... | collective-permute-start | bytes 294920 | tf_op jit(solution)/shard_map/ppermute | solution.py:589
  53.2 13.8 %collective-permute-start.6 = (bf16[3,64,256]{2,1,0:T(8,128)(2,1)S(1)}, bf16[3,64,256]{2,1,0:T(8,128)(2,1)S(1)}, u32[]{:S(2)}, u32[]{:S(2)}) collective-permute-start(bf16[3,64,256]{2,1,0:T(8,128)(2,1)S(1)} %get-tuple-element.111.refs_3_.refs_0_.res_ref), channel_id=1, source_target_pairs={{0,1},{1,0},{2,3},{3,2},{4,5},{5,4},{6,7},{7,6},{8,9},{9,8},{10,11... | collective-permute-start | bytes 294920 | tf_op jit(solution)/shard_map/ppermute | solution.py:589
  59.7 9.4 %collective-permute-start.7 = (bf16[3,64,256]{2,1,0:T(8,128)(2,1)S(1)}, bf16[3,64,256]{2,1,0:T(8,128)(2,1)S(1)}, u32[]{:S(2)}, u32[]{:S(2)}) collective-permute-start(bf16[3,64,256]{2,1,0:T(8,128)(2,1)S(1)} %get-tuple-element.111.refs_3_.refs_0_.res_ref), channel_id=1, source_target_pairs={{0,2},{1,3},{2,0},{3,1},{4,6},{5,7},{6,4},{7,5},{8,10},{9,11},{10,... | collective-permute-start | bytes 294920 | tf_op jit(solution)/shard_map/ppermute | solution.py:589
  60.6 8.4 %collective-permute-start.8 = (bf16[3,64,256]{2,1,0:T(8,128)(2,1)S(1)}, bf16[3,64,256]{2,1,0:T(8,128)(2,1)S(1)}, u32[]{:S(2)}, u32[]{:S(2)}) collective-permute-start(bf16[3,64,256]{2,1,0:T(8,128)(2,1)S(1)} %get-tuple-element.111.refs_3_.refs_0_.res_ref), channel_id=1, source_target_pairs={{0,3},{1,2},{2,1},{3,0},{4,7},{5,6},{6,5},{7,4},{8,11},{9,10},{10,... | collective-permute-start | bytes 294920 | tf_op jit(solution)/shard_map/ppermute | solution.py:589
  74.8 34.1 %collective-permute-start.18 = (bf16[4,320,384]{2,1,0:T(8,128)(2,1)}, bf16[4,320,384]{2,1,0:T(8,128)(2,1)}, u32[]{:S(2)}, u32[]{:S(2)}) collective-permute-start(bf16[4,320,384]{2,1,0:T(8,128)(2,1)} %get-tuple-element.137), channel_id=1, source_target_pairs={{0,4},{4,0},{8,12},{12,8},{16,20},{20,16},{24,28},{28,24},{1,5},{5... | collective-permute-start | bytes 2949128 | tf_op jit(solution)/shard_map/ppermute | solution.py:583
  80.7 28.2 %all-to-all-start = ((bf16[8,256,256]{2,1,0:T(8,128)(2,1)}), bf16[8,256,256]{2,1,0:T(8,128)(2,1)S(1)}, u32[]{:S(2)}, u32[]{:S(2)}) async-start(bf16[8,256,256]{2,1,0:T(8,128)(2,1)} %packed.1), calls=%async_computation | async-start | bytes 2097152 | tf_op jit(solution)/shard_map/all_to_all | solution.py:874
  84.6 5.2 %collective-permute-start.22 = (bf16[3,64,256]{2,1,0:T(8,128)(2,1)S(1)}, bf16[3,64,256]{2,1,0:T(8,128)(2,1)S(1)}, u32[]{:S(2)}, u32[]{:S(2)}) collective-permute-start(bf16[3,64,256]{2,1,0:T(8,128)(2,1)S(1)} %copy-done.37), channel_id=1, source_target_pairs={{0,1},{1,0},{2,3},{3,2},{4,5},{5,4},{6,7},{7,6},{8,9},{9,8},{10,11... | collective-permute-start | bytes 294920 | tf_op jit(solution)/shard_map/ppermute | solution.py:589
  86.2 11.0 %collective-permute-start.23 = (bf16[3,64,256]{2,1,0:T(8,128)(2,1)}, bf16[3,64,256]{2,1,0:T(8,128)(2,1)S(1)}, u32[]{:S(2)}, u32[]{:S(2)}) collective-permute-start(bf16[3,64,256]{2,1,0:T(8,128)(2,1)} %get-tuple-element.146), channel_id=1, source_target_pairs={{0,2},{1,3},{2,0},{3,1},{4,6},{5,7},{6,4},{7,5},{8,10},{9,11},{10,... | collective-permute-start | bytes 294920 | tf_op jit(solution)/shard_map/ppermute | solution.py:589
  87.4 12.3 %collective-permute-start.24 = (bf16[3,64,256]{2,1,0:T(8,128)(2,1)}, bf16[3,64,256]{2,1,0:T(8,128)(2,1)S(1)}, u32[]{:S(2)}, u32[]{:S(2)}) collective-permute-start(bf16[3,64,256]{2,1,0:T(8,128)(2,1)} %get-tuple-element.147), channel_id=1, source_target_pairs={{0,3},{1,2},{2,1},{3,0},{4,7},{5,6},{6,5},{7,4},{8,11},{9,10},{10,... | collective-permute-start | bytes 294920 | tf_op jit(solution)/shard_map/ppermute | solution.py:589
  89.0 12.2 %collective-permute-start.19 = (bf16[3,64,256]{2,1,0:T(8,128)(2,1)}, bf16[3,64,256]{2,1,0:T(8,128)(2,1)S(1)}, u32[]{:S(2)}, u32[]{:S(2)}) collective-permute-start(bf16[3,64,256]{2,1,0:T(8,128)(2,1)} %get-tuple-element.140), channel_id=1, source_target_pairs={{0,1},{1,0},{2,3},{3,2},{4,5},{5,4},{6,7},{7,6},{8,9},{9,8},{10,11... | collective-permute-start | bytes 294920 | tf_op jit(solution)/shard_map/ppermute | solution.py:589
  89.8 15.9 %collective-permute-start.20 = (bf16[3,64,256]{2,1,0:T(8,128)(2,1)}, bf16[3,64,256]{2,1,0:T(8,128)(2,1)S(1)}, u32[]{:S(2)}, u32[]{:S(2)}) collective-permute-start(bf16[3,64,256]{2,1,0:T(8,128)(2,1)} %copy-done.33), channel_id=1, source_target_pairs={{0,2},{1,3},{2,0},{3,1},{4,6},{5,7},{6,4},{7,5},{8,10},{9,11},{10,... | collective-permute-start | bytes 294920 | tf_op jit(solution)/shard_map/ppermute | solution.py:589
  97.2 8.4 %collective-permute-start.21 = (bf16[3,64,256]{2,1,0:T(8,128)(2,1)}, bf16[3,64,256]{2,1,0:T(8,128)(2,1)S(1)}, u32[]{:S(2)}, u32[]{:S(2)}) collective-permute-start(bf16[3,64,256]{2,1,0:T(8,128)(2,1)} %copy-done.32), channel_id=1, source_target_pairs={{0,3},{1,2},{2,1},{3,0},{4,7},{5,6},{6,5},{7,4},{8,11},{9,10},{10,... | collective-permute-start | bytes 294920 | tf_op jit(solution)/shard_map/ppermute | solution.py:589
  101.2 6.8 %collective-permute-start.26 = (bf16[192,1024]{1,0:T(8,128)(2,1)S(1)}, bf16[192,1024]{1,0:T(8,128)(2,1)S(1)}, u32[]{:S(2)}, u32[]{:S(2)}) collective-permute-start(bf16[192,1024]{1,0:T(8,128)(2,1)S(1)} %get-tuple-element.154.refs_3_), channel_id=1, source_target_pairs={{0,4},{4,0},{8,12},{12,8},{16,20},{20,16},{24,28},{28,24},{1,5},{5... | collective-permute-start | bytes 1179656 | tf_op jit(solution)/shard_map/ppermute | solution.py:583
  107.1 1.8 collective-permute-start.25
  117.2 17.1 %collective-permute-start.29 = (bf16[2,320,512]{2,1,0:T(8,128)(2,1)S(1)}, bf16[2,320,512]{2,1,0:T(8,128)(2,1)S(1)}, u32[]{:S(2)}, u32[]{:S(2)}) collective-permute-start(bf16[2,320,512]{2,1,0:T(8,128)(2,1)S(1)} %get-tuple-element.174), channel_id=1, source_target_pairs={{0,16},{4,20},{8,24},{12,28},{16,0},{20,4},{24,8},{28,12},{1,17},{... | collective-permute-start | bytes 1966088 | tf_op jit(solution)/shard_map/ppermute | solution.py:583
  119.1 17.2 %collective-permute-start.27 = (bf16[2,320,512]{2,1,0:T(8,128)(2,1)S(1)}, bf16[2,320,512]{2,1,0:T(8,128)(2,1)S(1)}, u32[]{:S(2)}, u32[]{:S(2)}) collective-permute-start(bf16[2,320,512]{2,1,0:T(8,128)(2,1)S(1)} %get-tuple-element.172), channel_id=1, source_target_pairs={{0,8},{4,12},{8,0},{12,4},{16,24},{20,28},{24,16},{28,20},{1,9},{5... | collective-permute-start | bytes 1966088 | tf_op jit(solution)/shard_map/ppermute | solution.py:583
  134.5 9.4 %collective-permute-start.30 = (bf16[1,320,512]{2,1,0:T(8,128)(2,1)S(1)}, bf16[1,320,512]{2,1,0:T(8,128)(2,1)}, u32[]{:S(2)}, u32[]{:S(2)}) collective-permute-start(bf16[1,320,512]{2,1,0:T(8,128)(2,1)S(1)} %slice.21), channel_id=1, source_target_pairs={{0,8},{4,12},{8,0},{12,4},{16,24},{20,28},{24,16},{28,20},{1,9},{5... | collective-permute-start | bytes 983048 | tf_op jit(solution)/shard_map/ppermute | solution.py:583
  136.5 9.0 %collective-permute-start.28 = (bf16[1,320,512]{2,1,0:T(8,128)(2,1)S(1)}, bf16[1,320,512]{2,1,0:T(8,128)(2,1)}, u32[]{:S(2)}, u32[]{:S(2)}) collective-permute-start(bf16[1,320,512]{2,1,0:T(8,128)(2,1)S(1)} %slice_bitcast_fusion), channel_id=1, source_target_pairs={{0,16},{4,20},{8,24},{12,28},{16,0},{20,4},{24,8},{28,12},{1,17},{... | collective-permute-start | bytes 983048 | tf_op jit(solution)/shard_map/ppermute | solution.py:583
  146.7 21.5 %collective-permute-start.31 = (bf16[2,80,1024]{2,1,0:T(8,128)(2,1)S(1)}, bf16[2,80,1024]{2,1,0:T(8,128)(2,1)S(1)}, u32[]{:S(2)}, u32[]{:S(2)}) collective-permute-start(bf16[2,80,1024]{2,1,0:T(8,128)(2,1)S(1)} %fusion.4), channel_id=1, source_target_pairs={{0,1},{1,0},{2,3},{3,2},{4,5},{5,4},{6,7},{7,6},{8,9},{9,8},{10,11... | collective-permute-start | bytes 983048 | tf_op jit(solution)/shard_map/ppermute | solution.py:623
  149.7 10.6 %collective-permute-start.33 = (bf16[224,256]{1,0:T(8,128)(2,1)S(1)}, bf16[224,256]{1,0:T(8,128)(2,1)S(1)}, u32[]{:S(2)}, u32[]{:S(2)}) collective-permute-start(bf16[224,256]{1,0:T(8,128)(2,1)S(1)} %get-tuple-element.175.refs_0_), channel_id=1, source_target_pairs={{0,1},{1,0},{2,3},{3,2},{4,5},{5,4},{6,7},{7,6},{8,9},{9,8},{10,11... | collective-permute-start | bytes 344072 | tf_op jit(solution)/shard_map/ppermute | solution.py:589
  150.0 10.2 %collective-permute-start.34 = (bf16[224,256]{1,0:T(8,128)(2,1)S(1)}, bf16[224,256]{1,0:T(8,128)(2,1)S(1)}, u32[]{:S(2)}, u32[]{:S(2)}) collective-permute-start(bf16[224,256]{1,0:T(8,128)(2,1)S(1)} %get-tuple-element.175.refs_0_), channel_id=1, source_target_pairs={{0,2},{1,3},{2,0},{3,1},{4,6},{5,7},{6,4},{7,5},{8,10},{9,11},{10,... | collective-permute-start | bytes 344072 | tf_op jit(solution)/shard_map/ppermute | solution.py:589
  152.6 11.4 %collective-permute-start.35 = (bf16[224,256]{1,0:T(8,128)(2,1)S(1)}, bf16[224,256]{1,0:T(8,128)(2,1)S(1)}, u32[]{:S(2)}, u32[]{:S(2)}) collective-permute-start(bf16[224,256]{1,0:T(8,128)(2,1)S(1)} %get-tuple-element.175.refs_0_), channel_id=1, source_target_pairs={{0,3},{1,2},{2,1},{3,0},{4,7},{5,6},{6,5},{7,4},{8,11},{9,10},{10,... | collective-permute-start | bytes 344072 | tf_op jit(solution)/shard_map/ppermute | solution.py:589
  164.6 7.3 %collective-permute-start.36 = (bf16[448,256]{1,0:T(8,128)(2,1)S(1)}, bf16[448,256]{1,0:T(8,128)(2,1)S(1)}, u32[]{:S(2)}, u32[]{:S(2)}) collective-permute-start(bf16[448,256]{1,0:T(8,128)(2,1)S(1)} %shard_sums.1.refs_0_), channel_id=1, source_target_pairs={{0,8},{4,12},{8,0},{12,4},{16,24},{20,28},{24,16},{28,20},{1,9},{5... | collective-permute-start | bytes 688136 | tf_op jit(solution)/shard_map/ppermute | solution.py:629
  166.1 9.5 %collective-permute-start.37 = (bf16[448,256]{1,0:T(8,128)(2,1)S(1)}, bf16[448,256]{1,0:T(8,128)(2,1)S(1)}, u32[]{:S(2)}, u32[]{:S(2)}) collective-permute-start(bf16[448,256]{1,0:T(8,128)(2,1)S(1)} %shard_sums.1.refs_0_), channel_id=1, source_target_pairs={{0,16},{4,20},{8,24},{12,28},{16,0},{20,4},{24,8},{28,12},{1,17},{... | collective-permute-start | bytes 688136 | tf_op jit(solution)/shard_map/ppermute | solution.py:629
  167.5 8.1 %collective-permute-start.38 = (bf16[448,256]{1,0:T(8,128)(2,1)S(1)}, bf16[448,256]{1,0:T(8,128)(2,1)S(1)}, u32[]{:S(2)}, u32[]{:S(2)}) collective-permute-start(bf16[448,256]{1,0:T(8,128)(2,1)S(1)} %shard_sums.1.refs_0_), channel_id=1, source_target_pairs={{0,24},{4,28},{8,16},{12,20},{16,8},{20,12},{24,0},{28,4},{1,25},{... | collective-permute-start | bytes 688136 | tf_op jit(solution)/shard_map/ppermute | solution.py:629
  168.3 8.3 %collective-permute-start.32 = (bf16[1,80,1024]{2,1,0:T(8,128)(2,1)S(1)}, bf16[1,80,1024]{2,1,0:T(8,128)(2,1)S(1)}, u32[]{:S(2)}, u32[]{:S(2)}) collective-permute-start(bf16[1,80,1024]{2,1,0:T(8,128)(2,1)S(1)} %constant_dynamic-slice_fusion), channel_id=1, source_target_pairs={{0,2},{1,3},{2,0},{3,1},{4,6},{5,7},{6,4},{7,5},{8,10},{9,11},{10,... | collective-permute-start | bytes 491528 | tf_op jit(solution)/shard_map/ppermute | solution.py:623
  175.6 1.8 collective-permute-start.39
  175.6 1.8 %collective-permute-start.40 = (bf16[448,256]{1,0:T(8,128)(2,1)S(1)}, bf16[448,256]{1,0:T(8,128)(2,1)S(1)}, u32[]{:S(2)}, u32[]{:S(2)}) collective-permute-start(bf16[448,256]{1,0:T(8,128)(2,1)S(1)} %collective-permute-done.36.refs_2_), channel_id=1, source_target_pairs={{0,4},{4,0},{8,12},{12,8},{16,20},{20,16},{24,28},{28,24},{1,5},{5... | collective-permute-start | bytes 688136 | tf_op jit(solution)/shard_map/ppermute | solution.py:583
  176.1 1.6 collective-permute-start.41
  176.1 2.0 %collective-permute-start.42 = (bf16[448,256]{1,0:T(8,128)(2,1)S(1)}, bf16[448,256]{1,0:T(8,128)(2,1)S(1)}, u32[]{:S(2)}, u32[]{:S(2)}) collective-permute-start(bf16[448,256]{1,0:T(8,128)(2,1)S(1)} %collective-permute-done.38.refs_6_), channel_id=1, source_target_pairs={{0,4},{4,0},{8,12},{12,8},{16,20},{20,16},{24,28},{28,24},{1,5},{5... | collective-permute-start | bytes 688136 | tf_op jit(solution)/shard_map/ppermute | solution.py:583
  (43 other events, 248.4 us)

commit v8 on v7

--- a/solution.py
+++ b/solution.py
@@ -871,12 +871,14 @@
     width = spec_w.shape[-1]
     blocks = spec_w.shape[2] // shards
     head_rows = head_w.shape[0] // groups
-    weight_sums = lax.all_to_all(
-        packed(routes, head_grad, spec_grad, predicted, groups), "grp", split_axis=0, concat_axis=0, tiled=True
-    )
     own_grads, other_grads, row_sums = [], [], []
     for first, res, back in zip(firsts, residual, spec_back):
         grad, row_sum = embedded_back_chunk(scal, embedded, stats, res, head_w, gain_row, back, first, cells)
+        if first == firsts[0]:
+            grad, head_grad, spec_grad = lax.optimization_barrier((grad, head_grad, spec_grad))
+            weight_sums = lax.all_to_all(
+                packed(routes, head_grad, spec_grad, predicted, groups), "grp", split_axis=0, concat_axis=0, tiled=True
+            )
         own_grads.append(grad)
         other_grads.append(swap_bit(grad, 0, groups))
         row_sums.append(row_sum)
@@ -893,7 +895,7 @@
     predictions = predictions.reshape(targets.shape)
     spec_rows = spec_grad.shape[0] // groups
     outgoing = shard_sums(routes, across([small] * shards), head_rows, spec_rows, spec_bias.shape[0])
-    _, outgoing = lax.optimization_barrier((ends, outgoing))
+    ends, outgoing = lax.optimization_barrier((ends, outgoing))
     part = jnp.concatenate(ends, axis=-1)
     part = part.reshape(shards, part.shape[0] // shards, -1)
     part = scatter_step(part, 1, shards, shard_at)

time: 181 us -> 168 us (0.928)
  waiting for transfers between devices: 48.3 us -> 29.6 us
  starting transfers between devices: 66.5 us -> 71.8 us
    ppermute x27, waiting for transfers between devices: 24.2 us -> 12 us  [across(): lax.ppermute(pieces[k], 'fft', [(z, z ^ k) for z in range(shards)])]
    ppermute x11, waiting for transfers between devices: 16.9 us -> 10.8 us  [swap_bit(): lax.ppermute(values, 'grp', [(g, g ^ 1 << bit) for g in range(groups)])]
    ppermute x3, waiting for transfers between devices: 7.19 us -> 1.2 us  [from_same_core(): lax.ppermute(values, 'grp', [(g, g ^ k) for g in range(groups)])]
    ppermute x2, waiting for transfers between devices: 0.01 us -> 5.6 us  [scatter_step(): received = lax.ppermute(send, 'fft', [(z, z ^ bit) for z in range(shards)])]
    ppermute x2, starting transfers between devices: 1.8 us -> 5.6 us  [scatter_step(): received = lax.ppermute(send, 'fft', [(z, z ^ bit) for z in range(shards)])]
    convert_element_type x3 -> x1, other arithmetic: 2.33 us -> 0.18 us  [add_half(): return (left.astype(FULL) + right.astype(FULL)).astype(HALF)]
    unnamed x94 -> x98, local copies, waits for them, and re-layouts: 16.4 us -> 15 us
  transfers between devices with their start and end apart: 44 -> 44, of which waited for: 15 -> 13; matrix products, arithmetic and copies ran while one was open for 2% -> 2% of each run, Pallas kernels for 12% -> 16%
where the time goes in v8:
time: 168 us; the launch traced here: 167 us
  starting transfers between devices  71.8 us (43%)
  Pallas kernels  42.7 us (25%)
  waiting for transfers between devices  29.6 us (18%)
  local copies, waits for them, and re-layouts  17.1 us (10%)
  other arithmetic  4.24 us (3%)
    ppermute x27, starting transfers between devices, across(): lax.ppermute(pieces[k], 'fft', [(z, z ^ k) for z in range(shards)])  50.9 us
    unnamed x98, local copies, waits for them, and re-layouts  15 us
    ppermute x27, waiting for transfers between devices, across(): lax.ppermute(pieces[k], 'fft', [(z, z ^ k) for z in range(shards)])  12 us
    ppermute x11, waiting for transfers between devices, swap_bit(): lax.ppermute(values, 'grp', [(g, g ^ 1 << bit) for g in range(groups)])  10.8 us
    pallas_call x1, Pallas kernels, embed(): pl.pallas_call(body, grid_spec=pltpu.PrefetchScalarGridSpec(num_scalar_pr...  10.1 us
    pallas_call x2, Pallas kernels, embed_grad_parts(): pl.pallas_call(body, grid_spec=pltpu.PrefetchScalarGridSpec(num_scalar_pr...  8.18 us
    ppermute x11, starting transfers between devices, swap_bit(): lax.ppermute(values, 'grp', [(g, g ^ 1 << bit) for g in range(groups)])  8.02 us
    pallas_call x2, Pallas kernels, spectral_back_chunk(): pl.pallas_call(body, grid_spec=pltpu.PrefetchScalarGridSpec(num_scalar_pr...  7.48 us
  transfers between devices with their start and end apart: 44, of which 13 were waited for; matrix products, arithmetic and copies ran while one was open for 2% of the time, Pallas kernels for 16%

profile of v8, /device:TPU:0, one launch (start us, length us, event | category | flops | bytes accessed | tf_op | source)
XLA Modules:
  0.0 166.7 jit_solution(4856257669023688719)
XLA Ops:
  2.0 10.1 %embed.1 = (bf16[384,1024]{1,0:T(8,128)(2,1)}, bf16[384,1024]{1,0:T(8,128)(2,1)}, f32[384,256]{1,0:T(8,128)}, bf16[4,320,384]{2,1,0:T(8,128)(2,1)}, bf16[4,320,3...) custom-call(s32[15]{0:T(128)} %concatenate.12.scal_ref, ...), custom_call_target="tpu_custom_call" | custom-call | flops 2013265920 | bytes 7208960 | tf_op jit(solution)/shard_map/embed/pallas_call | solution.py:157
  12.1 4.1 %collective-permute-start.10 = (bf16[3,64,256]{2,1,0:T(8,128)(2,1)}, bf16[3,64,256]{2,1,0:T(8,128)(2,1)S(1)}, u32[]{:S(2)}, u32[]{:S(2)}) collective-permute-start(bf16[3,64,256]{2,1,0:T(8,128)(2,1)} %get-tuple-element.120), channel_id=1, source_target_pairs={{0,2},{1,3},{2,0},{3,1},{4,6},{5,7},{6,4},{7,5},{8,10},{9,11},{10,... | collective-permute-start | bytes 294920 | tf_op jit(solution)/shard_map/ppermute | solution.py:589
  16.2 1.3 collective-permute-start.11
  17.8 1.8 %collective-permute-start = (bf16[3,64,256]{2,1,0:T(8,128)(2,1)}, bf16[3,64,256]{2,1,0:T(8,128)(2,1)S(1)}, u32[]{:S(2)}, u32[]{:S(2)}) collective-permute-start(bf16[3,64,256]{2,1,0:T(8,128)(2,1)} %get-tuple-element.105), channel_id=1, source_target_pairs={{0,1},{1,0},{2,3},{3,2},{4,5},{5,4},{6,7},{7,6},{8,9},{9,8},{10,11... | collective-permute-start | bytes 294920 | tf_op jit(solution)/shard_map/ppermute | solution.py:589
  19.5 1.7 %collective-permute-start.1 = (bf16[3,64,256]{2,1,0:T(8,128)(2,1)}, bf16[3,64,256]{2,1,0:T(8,128)(2,1)S(1)}, u32[]{:S(2)}, u32[]{:S(2)}) collective-permute-start(bf16[3,64,256]{2,1,0:T(8,128)(2,1)} %get-tuple-element.106), channel_id=1, source_target_pairs={{0,2},{1,3},{2,0},{3,1},{4,6},{5,7},{6,4},{7,5},{8,10},{9,11},{10,... | collective-permute-start | bytes 294920 | tf_op jit(solution)/shard_map/ppermute | solution.py:589
  21.2 3.0 %collective-permute-done.10.refs_2_ = bf16[3,64,256]{2,1,0:T(8,128)(2,1)S(1)} collective-permute-done((bf16[3,64,256]{2,1,0:T(8,128)(2,1)}, bf16[3,64,256]{2,1,0:T(8,128)(2,1)S(1)}, u32[]{:S(2)}, u32[]{:S(2)}) %collective-permute-start.10) | collective-permute-done | bytes 98336 | tf_op jit(solution)/shard_map/ppermute | solution.py:589
  24.3 2.8 %collective-permute-start.2 = (bf16[3,64,256]{2,1,0:T(8,128)(2,1)}, bf16[3,64,256]{2,1,0:T(8,128)(2,1)S(1)}, u32[]{:S(2)}, u32[]{:S(2)}) collective-permute-start(bf16[3,64,256]{2,1,0:T(8,128)(2,1)} %get-tuple-element.107), channel_id=1, source_target_pairs={{0,3},{1,2},{2,1},{3,0},{4,7},{5,6},{6,5},{7,4},{8,11},{9,10},{10,... | collective-permute-start | bytes 294920 | tf_op jit(solution)/shard_map/ppermute | solution.py:589
  28.8 2.3 %spectral.3 = (bf16[3,64,256]{2,1,0:T(8,128)(2,1)S(1)}, bf16[3,64,256]{2,1,0:T(8,128)(2,1)S(1)}, bf16[3,64,256]{2,1,0:T(8,128)(2,1)S(1)}, bf16[3,64,256]{2,1,0:T...) custom-call(s32[15]{0:T(128)S(1)} %copy-done.23, ...), custom_call_target="tpu_custom_call" | custom-call | flops 704643072 | bytes 3145728 | tf_op jit(solution)/shard_map/spectral/pallas_call | solution.py:277
  31.3 1.6 collective-permute-start.13
  32.9 2.7 %collective-permute-start.14 = (bf16[3,64,256]{2,1,0:T(8,128)(2,1)S(1)}, bf16[3,64,256]{2,1,0:T(8,128)(2,1)S(1)}, u32[]{:S(2)}, u32[]{:S(2)}) collective-permute-start(bf16[3,64,256]{2,1,0:T(8,128)(2,1)S(1)} %get-tuple-element.128), channel_id=1, source_target_pairs={{0,3},{1,2},{2,1},{3,0},{4,7},{5,6},{6,5},{7,4},{8,11},{9,10},{10,... | collective-permute-start | bytes 294920 | tf_op jit(solution)/shard_map/ppermute | solution.py:589
  38.8 2.3 %spectral.2 = (bf16[3,64,256]{2,1,0:T(8,128)(2,1)S(1)}, bf16[3,64,256]{2,1,0:T(8,128)(2,1)S(1)}, bf16[3,64,256]{2,1,0:T(8,128)(2,1)S(1)}, bf16[3,64,256]{2,1,0:T...) custom-call(s32[15]{0:T(128)S(1)} %copy-done.23, ...), custom_call_target="tpu_custom_call" | custom-call | flops 704643072 | bytes 3145728 | tf_op jit(solution)/shard_map/spectral/pallas_call | solution.py:277
  41.3 1.7 %collective-permute-start.4 = (bf16[3,64,256]{2,1,0:T(8,128)(2,1)S(1)}, bf16[3,64,256]{2,1,0:T(8,128)(2,1)S(1)}, u32[]{:S(2)}, u32[]{:S(2)}) collective-permute-start(bf16[3,64,256]{2,1,0:T(8,128)(2,1)S(1)} %get-tuple-element.115), channel_id=1, source_target_pairs={{0,2},{1,3},{2,0},{3,1},{4,6},{5,7},{6,4},{7,5},{8,10},{9,11},{10,... | collective-permute-start | bytes 294920 | tf_op jit(solution)/shard_map/ppermute | solution.py:589
  43.0 2.7 %collective-permute-start.5 = (bf16[3,64,256]{2,1,0:T(8,128)(2,1)S(1)}, bf16[3,64,256]{2,1,0:T(8,128)(2,1)S(1)}, u32[]{:S(2)}, u32[]{:S(2)}) collective-permute-start(bf16[3,64,256]{2,1,0:T(8,128)(2,1)S(1)} %get-tuple-element.116), channel_id=1, source_target_pairs={{0,3},{1,2},{2,1},{3,0},{4,7},{5,6},{6,5},{7,4},{8,11},{9,10},{10,... | collective-permute-start | bytes 294920 | tf_op jit(solution)/shard_map/ppermute | solution.py:589
  46.8 1.7 %collective-permute-start.16 = (bf16[3,64,256]{2,1,0:T(8,128)(2,1)S(1)}, bf16[3,64,256]{2,1,0:T(8,128)(2,1)S(1)}, u32[]{:S(2)}, u32[]{:S(2)}) collective-permute-start(bf16[3,64,256]{2,1,0:T(8,128)(2,1)S(1)} %get-tuple-element.132.refs_2_.refs_0_.res_ref), channel_id=1, source_target_pairs={{0,2},{1,3},{2,0},{3,1},{4,6},{5,7},{6,4},{7,5},{8,10},{9,11},{10,... | collective-permute-start | bytes 294920 | tf_op jit(solution)/shard_map/ppermute | solution.py:589
  48.5 2.7 %collective-permute-start.17 = (bf16[3,64,256]{2,1,0:T(8,128)(2,1)S(1)}, bf16[3,64,256]{2,1,0:T(8,128)(2,1)S(1)}, u32[]{:S(2)}, u32[]{:S(2)}) collective-permute-start(bf16[3,64,256]{2,1,0:T(8,128)(2,1)S(1)} %get-tuple-element.132.refs_2_.refs_0_.res_ref), channel_id=1, source_target_pairs={{0,3},{1,2},{2,1},{3,0},{4,7},{5,6},{6,5},{7,4},{8,11},{9,10},{10,... | collective-permute-start | bytes 294920 | tf_op jit(solution)/shard_map/ppermute | solution.py:589
  53.2 6.5 %collective-permute-start.6 = (bf16[3,64,256]{2,1,0:T(8,128)(2,1)S(1)}, bf16[3,64,256]{2,1,0:T(8,128)(2,1)S(1)}, u32[]{:S(2)}, u32[]{:S(2)}) collective-permute-start(bf16[3,64,256]{2,1,0:T(8,128)(2,1)S(1)} %get-tuple-element.117.refs_3_.refs_0_.res_ref), channel_id=1, source_target_pairs={{0,1},{1,0},{2,3},{3,2},{4,5},{5,4},{6,7},{7,6},{8,9},{9,8},{10,11... | collective-permute-start | bytes 294920 | tf_op jit(solution)/shard_map/ppermute | solution.py:589
  60.7 1.5 collective-permute-start.8
  62.7 3.7 %spectral_back.2 = (bf16[3,64,256]{2,1,0:T(8,128)(2,1)S(1)}, bf16[3,64,256]{2,1,0:T(8,128)(2,1)}, bf16[3,64,256]{2,1,0:T(8,128)(2,1)}, bf16[3,64,256]{2,1,0:T(8,...) custom-call(s32[15]{0:T(128)S(1)} %copy-done.23, bf16[3,512,256]{2,1,0:T(8,128)(2,1)S(1)} %copy-done.4, ...), custom_call_target="tpu_custom_call" | custom-call | flops 1006632960 | bytes 3145728 | tf_op jit(solution)/shard_map/spectral_back/pallas_call | solution.py:440
  67.6 1.9 %collective-permute-start.20 = (bf16[3,64,256]{2,1,0:T(8,128)(2,1)}, bf16[3,64,256]{2,1,0:T(8,128)(2,1)}, u32[]{:S(2)}, u32[]{:S(2)}) collective-permute-start(bf16[3,64,256]{2,1,0:T(8,128)(2,1)} %get-tuple-element.147), channel_id=1, source_target_pairs={{0,2},{1,3},{2,0},{3,1},{4,6},{5,7},{6,4},{7,5},{8,10},{9,11},{10,... | collective-permute-start | bytes 294920 | tf_op jit(solution)/shard_map/ppermute | solution.py:589
  69.4 1.5 collective-permute-start.21
  71.0 3.7 %spectral_back.3 = (bf16[3,64,256]{2,1,0:T(8,128)(2,1)S(1)}, bf16[3,64,256]{2,1,0:T(8,128)(2,1)}, bf16[3,64,256]{2,1,0:T(8,128)(2,1)S(1)}, bf16[3,64,256]{2,1,0:...) custom-call(s32[15]{0:T(128)S(1)} %copy-done.23, bf16[3,512,256]{2,1,0:T(8,128)(2,1)S(1)} %copy-done.4, ...), custom_call_target="tpu_custom_call" | custom-call | flops 1006632960 | bytes 3145728 | tf_op jit(solution)/shard_map/spectral_back/pallas_call | solution.py:440
  80.6 2.4 %embedded_back.2 = (bf16[192,1024]{1,0:T(8,128)(2,1)S(1)}, f32[8,1024]{1,0:T(8,128)S(1)}) custom-call(s32[15]{0:T(128)S(1)} %copy-done.23, bf16[384,1024]{1,0:T(8,128)(2,1)S(1)} %copy-done.1, f32[384,256]{1,0:T(8,128)S(1)} %copy-done.7, bf16[3,64,256]{2,1,0:T(8,128)(2,1)S(1)} %copy-done.11, bf16[1024,256]{1,0:T(8,128)(2,1)S(1)} %copy-done, ...), custom_call_target="tpu_custom_call" | custom-call | flops 100663296 | bytes 1179648 | tf_op jit(solution)/shard_map/embedded_back/pallas_call | solution.py:497
  85.0 1.7 %packed.1 = bf16[8,256,256]{2,1,0:T(8,128)(2,1)} custom-call(s32[17]{0:T(128)S(1)} %concatenate.11.routes_ref, bf16[1024,256]{1,0:T(8,128)(2,1)S(1)} %copy-done.6, bf16[512,256]{1,0:T(8,128)(2,1)S(1)} %copy-done.14, bf16[3,64,256]{2,1,0:T(8,128)(2,1)S(1)} %copy-done.16, bf16[3,64,256]{2,1,0:T(8,128)(2,1)S(1)} %copy-done.18), custom_call_target="tpu_custom_call" | custom-call | tf_op jit(solution)/shard_map/packed/pallas_call | solution.py:645
  86.7 3.9 %all-to-all-start = ((bf16[8,256,256]{2,1,0:T(8,128)(2,1)}), bf16[8,256,256]{2,1,0:T(8,128)(2,1)S(1)}, u32[]{:S(2)}, u32[]{:S(2)}) async-start(bf16[8,256,256]{2,1,0:T(8,128)(2,1)} %packed.1), calls=%async_computation | async-start | bytes 2097152 | tf_op jit(solution)/shard_map/all_to_all | solution.py:879
  90.6 2.3 %collective-permute-start.22 = (bf16[3,64,256]{2,1,0:T(8,128)(2,1)}, bf16[3,64,256]{2,1,0:T(8,128)(2,1)S(1)}, u32[]{:S(2)}, u32[]{:S(2)}) collective-permute-start(bf16[3,64,256]{2,1,0:T(8,128)(2,1)} %get-tuple-element.154), channel_id=1, source_target_pairs={{0,1},{1,0},{2,3},{3,2},{4,5},{5,4},{6,7},{7,6},{8,9},{9,8},{10,11... | collective-permute-start | bytes 294920 | tf_op jit(solution)/shard_map/ppermute | solution.py:589
  92.9 3.6 %collective-permute-start.23 = (bf16[3,64,256]{2,1,0:T(8,128)(2,1)S(1)}, bf16[3,64,256]{2,1,0:T(8,128)(2,1)S(1)}, u32[]{:S(2)}, u32[]{:S(2)}) collective-permute-start(bf16[3,64,256]{2,1,0:T(8,128)(2,1)S(1)} %copy-done.38), channel_id=1, source_target_pairs={{0,2},{1,3},{2,0},{3,1},{4,6},{5,7},{6,4},{7,5},{8,10},{9,11},{10,... | collective-permute-start | bytes 294920 | tf_op jit(solution)/shard_map/ppermute | solution.py:589
  96.5 1.4 collective-permute-start.24
  97.9 1.9 %collective-permute-done.23.refs_2_ = bf16[3,64,256]{2,1,0:T(8,128)(2,1)S(1)} collective-permute-done((bf16[3,64,256]{2,1,0:T(8,128)(2,1)S(1)}, bf16[3,64,256]{2,1,0:T(8,128)(2,1)S(1)}, u32[]{:S(2)}, u32[]{:S(2)}) %collective-permute-start.23) | collective-permute-done | bytes 98336 | tf_op jit(solution)/shard_map/ppermute | solution.py:589
  99.8 5.6 %collective-permute-done.24.refs_3_ = bf16[3,64,256]{2,1,0:T(8,128)(2,1)S(1)} collective-permute-done((bf16[3,64,256]{2,1,0:T(8,128)(2,1)S(1)}, bf16[3,64,256]{2,1,0:T(8,128)(2,1)S(1)}, u32[]{:S(2)}, u32[]{:S(2)}) %collective-permute-start.24) | collective-permute-done | bytes 98336 | tf_op jit(solution)/shard_map/ppermute | solution.py:589
  105.5 1.4 embedded_back.3
  112.8 4.1 %embed_grad.2 = (bf16[2,320,512]{2,1,0:T(8,128)(2,1)S(1)}, bf16[2,320,512]{2,1,0:T(8,128)(2,1)S(1)}) custom-call(s32[15]{0:T(128)S(1)} %copy-done.23, bf16[4,320,384]{2,1,0:T(8,128)(2,1)S(1)} %copy-done.43, bf16[4,320,384]{2,1,0:T(8,128)(2,1)} %collective-permute-done.18.refs_1_, bf16[192,1024]{1,0:T(8,128)(2,1)S(1)} %copy-done.32, ...), custom_call_target="tpu_custom_call" | custom-call | flops 1006632960 | bytes 4063232 | tf_op jit(solution)/shard_map/embed_grad/pallas_call | solution.py:555
  116.9 1.7 %collective-permute-start.29 = (bf16[2,320,512]{2,1,0:T(8,128)(2,1)S(1)}, bf16[2,320,512]{2,1,0:T(8,128)(2,1)S(1)}, u32[]{:S(2)}, u32[]{:S(2)}) collective-permute-start(bf16[2,320,512]{2,1,0:T(8,128)(2,1)S(1)} %get-tuple-element.183), channel_id=1, source_target_pairs={{0,16},{4,20},{8,24},{12,28},{16,0},{20,4},{24,8},{28,12},{1,17},{... | collective-permute-start | bytes 1966088 | tf_op jit(solution)/shard_map/ppermute | solution.py:583
  118.7 1.5 collective-permute-start.27
  120.1 4.1 %embed_grad.3 = (bf16[2,320,512]{2,1,0:T(8,128)(2,1)S(1)}, bf16[2,320,512]{2,1,0:T(8,128)(2,1)S(1)}) custom-call(s32[15]{0:T(128)S(1)} %copy-done.23, bf16[4,320,384]{2,1,0:T(8,128)(2,1)S(1)} %copy-done.44, bf16[4,320,384]{2,1,0:T(8,128)(2,1)} %collective-permute-done.18.refs_1_, bf16[192,1024]{1,0:T(8,128)(2,1)S(1)} %copy-done.32, ...), custom_call_target="tpu_custom_call" | custom-call | flops 1006632960 | bytes 4063232 | tf_op jit(solution)/shard_map/embed_grad/pallas_call | solution.py:555
  125.5 1.7 %collective-permute-start.31 = (bf16[224,256]{1,0:T(8,128)(2,1)S(1)}, bf16[224,256]{1,0:T(8,128)(2,1)S(1)}, u32[]{:S(2)}, u32[]{:S(2)}) collective-permute-start(bf16[224,256]{1,0:T(8,128)(2,1)S(1)} %get-tuple-element.184.refs_0_), channel_id=1, source_target_pairs={{0,1},{1,0},{2,3},{3,2},{4,5},{5,4},{6,7},{7,6},{8,9},{9,8},{10,11... | collective-permute-start | bytes 344072 | tf_op jit(solution)/shard_map/ppermute | solution.py:589
  127.2 1.6 collective-permute-start.32
  128.9 1.5 collective-permute-start.33
  130.3 3.7 %collective-permute-done.29 = bf16[2,320,512]{2,1,0:T(8,128)(2,1)S(1)} collective-permute-done((bf16[2,320,512]{2,1,0:T(8,128)(2,1)S(1)}, bf16[2,320,512]{2,1,0:T(8,128)(2,1)S(1)}, u32[]{:S(2)}, u32[]{:S(2)}) %collective-permute-start.29) | collective-permute-done | bytes 655392 | tf_op jit(solution)/shard_map/ppermute | solution.py:583
  134.2 1.7 %collective-permute-start.30 = (bf16[1,320,512]{2,1,0:T(8,128)(2,1)S(1)}, bf16[1,320,512]{2,1,0:T(8,128)(2,1)S(1)}, u32[]{:S(2)}, u32[]{:S(2)}) collective-permute-start(bf16[1,320,512]{2,1,0:T(8,128)(2,1)S(1)} %slice.21), channel_id=1, source_target_pairs={{0,8},{4,12},{8,0},{12,4},{16,24},{20,28},{24,16},{28,20},{1,9},{5... | collective-permute-start | bytes 983048 | tf_op jit(solution)/shard_map/ppermute | solution.py:583
  136.2 1.5 collective-permute-start.28
  139.4 4.1 %collective-permute-done.30 = bf16[1,320,512]{2,1,0:T(8,128)(2,1)S(1)} collective-permute-done((bf16[1,320,512]{2,1,0:T(8,128)(2,1)S(1)}, bf16[1,320,512]{2,1,0:T(8,128)(2,1)S(1)}, u32[]{:S(2)}, u32[]{:S(2)}) %collective-permute-start.30) | collective-permute-done | bytes 327712 | tf_op jit(solution)/shard_map/ppermute | solution.py:583
  143.6 1.7 %collective-permute-done.28 = bf16[1,320,512]{2,1,0:T(8,128)(2,1)} collective-permute-done((bf16[1,320,512]{2,1,0:T(8,128)(2,1)S(1)}, bf16[1,320,512]{2,1,0:T(8,128)(2,1)}, u32[]{:S(2)}, u32[]{:S(2)}) %collective-permute-start.28) | collective-permute-done | bytes 327712 | tf_op jit(solution)/shard_map/ppermute | solution.py:583
  146.4 1.8 %collective-permute-start.34 = (bf16[2,80,1024]{2,1,0:T(8,128)(2,1)S(1)}, bf16[2,80,1024]{2,1,0:T(8,128)(2,1)S(1)}, u32[]{:S(2)}, u32[]{:S(2)}) collective-permute-start(bf16[2,80,1024]{2,1,0:T(8,128)(2,1)S(1)} %dynamic-slice_bitcast_fusion), channel_id=1, source_target_pairs={{0,1},{1,0},{2,3},{3,2},{4,5},{5,4},{6,7},{7,6},{8,9},{9,8},{10,11... | collective-permute-start | bytes 983048 | tf_op jit(solution)/shard_map/ppermute | solution.py:623
  150.2 1.5 collective-permute-start.38
  151.7 2.8 %collective-permute-done.34 = bf16[2,80,1024]{2,1,0:T(8,128)(2,1)S(1)} collective-permute-done((bf16[2,80,1024]{2,1,0:T(8,128)(2,1)S(1)}, bf16[2,80,1024]{2,1,0:T(8,128)(2,1)S(1)}, u32[]{:S(2)}, u32[]{:S(2)}) %collective-permute-start.34) | collective-permute-done | bytes 327712 | tf_op jit(solution)/shard_map/ppermute | solution.py:623
  154.6 3.8 %collective-permute-start.35 = (bf16[1,80,1024]{2,1,0:T(8,128)(2,1)S(1)}, bf16[1,80,1024]{2,1,0:T(8,128)(2,1)S(1)}, u32[]{:S(2)}, u32[]{:S(2)}) collective-permute-start(bf16[1,80,1024]{2,1,0:T(8,128)(2,1)S(1)} %constant_dynamic-slice_fusion), channel_id=1, source_target_pairs={{0,2},{1,3},{2,0},{3,1},{4,6},{5,7},{6,4},{7,5},{8,10},{9,11},{10,... | collective-permute-start | bytes 491528 | tf_op jit(solution)/shard_map/ppermute | solution.py:623
  160.6 2.8 %collective-permute-done.35 = bf16[1,80,1024]{2,1,0:T(8,128)(2,1)S(1)} collective-permute-done((bf16[1,80,1024]{2,1,0:T(8,128)(2,1)S(1)}, bf16[1,80,1024]{2,1,0:T(8,128)(2,1)S(1)}, u32[]{:S(2)}, u32[]{:S(2)}) %collective-permute-start.35) | collective-permute-done | bytes 163872 | tf_op jit(solution)/shard_map/ppermute | solution.py:623
  164.2 2.5 %assembled.1 = (f32[1024,256]{1,0:T(8,128)}, f32[2,2,8,128,128]{4,3,2,1,0:T(8,128)}, f32[2,2,8,128]{3,2,1,0:T(8,128)}, f32[1,1024]{1,0:T(1,128)}, f32[1,1024]{1,0:T(1,128)}, /*index=5*/f32[1,256]{1,0:T(1,128)}) custom-call(s32[15]{0:T(128)S(1)} %copy-done.23, bf16[448,256]{1,0:T(8,128)(2,1)S(1)} %shard_sums.1.refs_0_, ...), custom_call_target="tpu_custom_call" | custom-call | tf_op jit(solution)/shard_map/assembled/pallas_call | solution.py:790
  (175 shorter events, 35.8 us)
Async XLA Ops:
  2.0 25.9 %copy-start.2 = (bf16[2,2,8,128,128]{4,3,2,1,0:T(8,128)(2,1)S(1)}, bf16[2,2,8,128,128]{4,3,2,1,0:T(8,128)(2,1)}, u32[]{:S(2)}) copy-start(bf16[2,2,8,128,128]{4,3,2,1,0:T(8,128)(2,1)} %w_ref.15) | copy-start | bytes 3145732
  2.0 25.9 %copy-start.4 = (bf16[3,512,256]{2,1,0:T(8,128)(2,1)S(1)}, bf16[3,512,256]{2,1,0:T(8,128)(2,1)}, u32[]{:S(2)}) copy-start(bf16[3,512,256]{2,1,0:T(8,128)(2,1)} %constant.76.clone.t_ref) | copy-start | bytes 2359300
  2.0 25.9 %copy-start.23 = (s32[15]{0:T(128)S(1)}, s32[15]{0:T(128)}, u32[]{:S(2)}) copy-start(s32[15]{0:T(128)} %concatenate.12.scal_ref) | copy-start | bytes 184
  2.0 25.9 %copy-start.41 = (f32[2,2,8,128]{3,2,1,0:T(8,128)S(1)}, f32[2,2,8,128]{3,2,1,0:T(8,128)}, u32[]{:S(2)}) copy-start(f32[2,2,8,128]{3,2,1,0:T(8,128)} %b_ref.3) | copy-start | bytes 49156
  12.1 12.2 %collective-permute-start.10 = (bf16[3,64,256]{2,1,0:T(8,128)(2,1)}, bf16[3,64,256]{2,1,0:T(8,128)(2,1)S(1)}, u32[]{:S(2)}, u32[]{:S(2)}) collective-permute-start(bf16[3,64,256]{2,1,0:T(8,128)(2,1)} %get-tuple-element.120), channel_id=1, source_target_pairs={{0,2},{1,3},{2,0},{3,1},{4,6},{5,7},{6,4},{7,5},{8,10},{9,11},{10,... | collective-permute-start | bytes 294920 | tf_op jit(solution)/shard_map/ppermute | solution.py:589
  16.2 11.7 %collective-permute-start.11 = (bf16[3,64,256]{2,1,0:T(8,128)(2,1)}, bf16[3,64,256]{2,1,0:T(8,128)(2,1)S(1)}, u32[]{:S(2)}, u32[]{:S(2)}) collective-permute-start(bf16[3,64,256]{2,1,0:T(8,128)(2,1)} %get-tuple-element.121), channel_id=1, source_target_pairs={{0,3},{1,2},{2,1},{3,0},{4,7},{5,6},{6,5},{7,4},{8,11},{9,10},{10,... | collective-permute-start | bytes 294920 | tf_op jit(solution)/shard_map/ppermute | solution.py:589
  17.5 10.3 %collective-permute-start.9 = (bf16[3,64,256]{2,1,0:T(8,128)(2,1)}, bf16[3,64,256]{2,1,0:T(8,128)(2,1)S(1)}, u32[]{:S(2)}, u32[]{:S(2)}) collective-permute-start(bf16[3,64,256]{2,1,0:T(8,128)(2,1)} %get-tuple-element.119), channel_id=1, source_target_pairs={{0,1},{1,0},{2,3},{3,2},{4,5},{5,4},{6,7},{7,6},{8,9},{9,8},{10,11... | collective-permute-start | bytes 294920 | tf_op jit(solution)/shard_map/ppermute | solution.py:589
  17.8 15.1 %collective-permute-start = (bf16[3,64,256]{2,1,0:T(8,128)(2,1)}, bf16[3,64,256]{2,1,0:T(8,128)(2,1)S(1)}, u32[]{:S(2)}, u32[]{:S(2)}) collective-permute-start(bf16[3,64,256]{2,1,0:T(8,128)(2,1)} %get-tuple-element.105), channel_id=1, source_target_pairs={{0,1},{1,0},{2,3},{3,2},{4,5},{5,4},{6,7},{7,6},{8,9},{9,8},{10,11... | collective-permute-start | bytes 294920 | tf_op jit(solution)/shard_map/ppermute | solution.py:589
  19.5 16.0 %collective-permute-start.1 = (bf16[3,64,256]{2,1,0:T(8,128)(2,1)}, bf16[3,64,256]{2,1,0:T(8,128)(2,1)S(1)}, u32[]{:S(2)}, u32[]{:S(2)}) collective-permute-start(bf16[3,64,256]{2,1,0:T(8,128)(2,1)} %get-tuple-element.106), channel_id=1, source_target_pairs={{0,2},{1,3},{2,0},{3,1},{4,6},{5,7},{6,4},{7,5},{8,10},{9,11},{10,... | collective-permute-start | bytes 294920 | tf_op jit(solution)/shard_map/ppermute | solution.py:589
  24.3 11.3 %collective-permute-start.2 = (bf16[3,64,256]{2,1,0:T(8,128)(2,1)}, bf16[3,64,256]{2,1,0:T(8,128)(2,1)S(1)}, u32[]{:S(2)}, u32[]{:S(2)}) collective-permute-start(bf16[3,64,256]{2,1,0:T(8,128)(2,1)} %get-tuple-element.107), channel_id=1, source_target_pairs={{0,3},{1,2},{2,1},{3,0},{4,7},{5,6},{6,5},{7,4},{8,11},{9,10},{10,... | collective-permute-start | bytes 294920 | tf_op jit(solution)/shard_map/ppermute | solution.py:589
  31.1 11.9 %collective-permute-start.12 = (bf16[3,64,256]{2,1,0:T(8,128)(2,1)S(1)}, bf16[3,64,256]{2,1,0:T(8,128)(2,1)S(1)}, u32[]{:S(2)}, u32[]{:S(2)}) collective-permute-start(bf16[3,64,256]{2,1,0:T(8,128)(2,1)S(1)} %get-tuple-element.126), channel_id=1, source_target_pairs={{0,1},{1,0},{2,3},{3,2},{4,5},{5,4},{6,7},{7,6},{8,9},{9,8},{10,11... | collective-permute-start | bytes 294920 | tf_op jit(solution)/shard_map/ppermute | solution.py:589
  31.3 14.4 %collective-permute-start.13 = (bf16[3,64,256]{2,1,0:T(8,128)(2,1)S(1)}, bf16[3,64,256]{2,1,0:T(8,128)(2,1)S(1)}, u32[]{:S(2)}, u32[]{:S(2)}) collective-permute-start(bf16[3,64,256]{2,1,0:T(8,128)(2,1)S(1)} %get-tuple-element.127), channel_id=1, source_target_pairs={{0,2},{1,3},{2,0},{3,1},{4,6},{5,7},{6,4},{7,5},{8,10},{9,11},{10,... | collective-permute-start | bytes 294920 | tf_op jit(solution)/shard_map/ppermute | solution.py:589
  32.9 12.9 %collective-permute-start.14 = (bf16[3,64,256]{2,1,0:T(8,128)(2,1)S(1)}, bf16[3,64,256]{2,1,0:T(8,128)(2,1)S(1)}, u32[]{:S(2)}, u32[]{:S(2)}) collective-permute-start(bf16[3,64,256]{2,1,0:T(8,128)(2,1)S(1)} %get-tuple-element.128), channel_id=1, source_target_pairs={{0,3},{1,2},{2,1},{3,0},{4,7},{5,6},{6,5},{7,4},{8,11},{9,10},{10,... | collective-permute-start | bytes 294920 | tf_op jit(solution)/shard_map/ppermute | solution.py:589
  41.1 7.4 %collective-permute-start.3 = (bf16[3,64,256]{2,1,0:T(8,128)(2,1)S(1)}, bf16[3,64,256]{2,1,0:T(8,128)(2,1)S(1)}, u32[]{:S(2)}, u32[]{:S(2)}) collective-permute-start(bf16[3,64,256]{2,1,0:T(8,128)(2,1)S(1)} %get-tuple-element.114), channel_id=1, source_target_pairs={{0,1},{1,0},{2,3},{3,2},{4,5},{5,4},{6,7},{7,6},{8,9},{9,8},{10,11... | collective-permute-start | bytes 294920 | tf_op jit(solution)/shard_map/ppermute | solution.py:589
  41.3 10.6 %collective-permute-start.4 = (bf16[3,64,256]{2,1,0:T(8,128)(2,1)S(1)}, bf16[3,64,256]{2,1,0:T(8,128)(2,1)S(1)}, u32[]{:S(2)}, u32[]{:S(2)}) collective-permute-start(bf16[3,64,256]{2,1,0:T(8,128)(2,1)S(1)} %get-tuple-element.115), channel_id=1, source_target_pairs={{0,2},{1,3},{2,0},{3,1},{4,6},{5,7},{6,4},{7,5},{8,10},{9,11},{10,... | collective-permute-start | bytes 294920 | tf_op jit(solution)/shard_map/ppermute | solution.py:589
  43.0 9.2 %collective-permute-start.5 = (bf16[3,64,256]{2,1,0:T(8,128)(2,1)S(1)}, bf16[3,64,256]{2,1,0:T(8,128)(2,1)S(1)}, u32[]{:S(2)}, u32[]{:S(2)}) collective-permute-start(bf16[3,64,256]{2,1,0:T(8,128)(2,1)S(1)} %get-tuple-element.116), channel_id=1, source_target_pairs={{0,3},{1,2},{2,1},{3,0},{4,7},{5,6},{6,5},{7,4},{8,11},{9,10},{10,... | collective-permute-start | bytes 294920 | tf_op jit(solution)/shard_map/ppermute | solution.py:589
  46.8 13.9 %collective-permute-start.15 = (bf16[3,64,256]{2,1,0:T(8,128)(2,1)S(1)}, bf16[3,64,256]{2,1,0:T(8,128)(2,1)S(1)}, u32[]{:S(2)}, u32[]{:S(2)}) collective-permute-start(bf16[3,64,256]{2,1,0:T(8,128)(2,1)S(1)} %get-tuple-element.132.refs_2_.refs_0_.res_ref), channel_id=1, source_target_pairs={{0,1},{1,0},{2,3},{3,2},{4,5},{5,4},{6,7},{7,6},{8,9},{9,8},{10,11... | collective-permute-start | bytes 294920 | tf_op jit(solution)/shard_map/ppermute | solution.py:589
  46.8 15.8 %collective-permute-start.16 = (bf16[3,64,256]{2,1,0:T(8,128)(2,1)S(1)}, bf16[3,64,256]{2,1,0:T(8,128)(2,1)S(1)}, u32[]{:S(2)}, u32[]{:S(2)}) collective-permute-start(bf16[3,64,256]{2,1,0:T(8,128)(2,1)S(1)} %get-tuple-element.132.refs_2_.refs_0_.res_ref), channel_id=1, source_target_pairs={{0,2},{1,3},{2,0},{3,1},{4,6},{5,7},{6,4},{7,5},{8,10},{9,11},{10,... | collective-permute-start | bytes 294920 | tf_op jit(solution)/shard_map/ppermute | solution.py:589
  48.5 14.2 %collective-permute-start.17 = (bf16[3,64,256]{2,1,0:T(8,128)(2,1)S(1)}, bf16[3,64,256]{2,1,0:T(8,128)(2,1)S(1)}, u32[]{:S(2)}, u32[]{:S(2)}) collective-permute-start(bf16[3,64,256]{2,1,0:T(8,128)(2,1)S(1)} %get-tuple-element.132.refs_2_.refs_0_.res_ref), channel_id=1, source_target_pairs={{0,3},{1,2},{2,1},{3,0},{4,7},{5,6},{6,5},{7,4},{8,11},{9,10},{10,... | collective-permute-start | bytes 294920 | tf_op jit(solution)/shard_map/ppermute | solution.py:589
  53.2 16.2 %collective-permute-start.6 = (bf16[3,64,256]{2,1,0:T(8,128)(2,1)S(1)}, bf16[3,64,256]{2,1,0:T(8,128)(2,1)S(1)}, u32[]{:S(2)}, u32[]{:S(2)}) collective-permute-start(bf16[3,64,256]{2,1,0:T(8,128)(2,1)S(1)} %get-tuple-element.117.refs_3_.refs_0_.res_ref), channel_id=1, source_target_pairs={{0,1},{1,0},{2,3},{3,2},{4,5},{5,4},{6,7},{7,6},{8,9},{9,8},{10,11... | collective-permute-start | bytes 294920 | tf_op jit(solution)/shard_map/ppermute | solution.py:589
  59.7 11.2 %collective-permute-start.7 = (bf16[3,64,256]{2,1,0:T(8,128)(2,1)S(1)}, bf16[3,64,256]{2,1,0:T(8,128)(2,1)S(1)}, u32[]{:S(2)}, u32[]{:S(2)}) collective-permute-start(bf16[3,64,256]{2,1,0:T(8,128)(2,1)S(1)} %get-tuple-element.117.refs_3_.refs_0_.res_ref), channel_id=1, source_target_pairs={{0,2},{1,3},{2,0},{3,1},{4,6},{5,7},{6,4},{7,5},{8,10},{9,11},{10,... | collective-permute-start | bytes 294920 | tf_op jit(solution)/shard_map/ppermute | solution.py:589
  60.7 10.2 %collective-permute-start.8 = (bf16[3,64,256]{2,1,0:T(8,128)(2,1)S(1)}, bf16[3,64,256]{2,1,0:T(8,128)(2,1)S(1)}, u32[]{:S(2)}, u32[]{:S(2)}) collective-permute-start(bf16[3,64,256]{2,1,0:T(8,128)(2,1)S(1)} %get-tuple-element.117.refs_3_.refs_0_.res_ref), channel_id=1, source_target_pairs={{0,3},{1,2},{2,1},{3,0},{4,7},{5,6},{6,5},{7,4},{8,11},{9,10},{10,... | collective-permute-start | bytes 294920 | tf_op jit(solution)/shard_map/ppermute | solution.py:589
  66.5 12.3 %collective-permute-start.19 = (bf16[3,64,256]{2,1,0:T(8,128)(2,1)}, bf16[3,64,256]{2,1,0:T(8,128)(2,1)}, u32[]{:S(2)}, u32[]{:S(2)}) collective-permute-start(bf16[3,64,256]{2,1,0:T(8,128)(2,1)} %get-tuple-element.146), channel_id=1, source_target_pairs={{0,1},{1,0},{2,3},{3,2},{4,5},{5,4},{6,7},{7,6},{8,9},{9,8},{10,11... | collective-permute-start | bytes 294920 | tf_op jit(solution)/shard_map/ppermute | solution.py:589
  67.6 11.2 %collective-permute-start.20 = (bf16[3,64,256]{2,1,0:T(8,128)(2,1)}, bf16[3,64,256]{2,1,0:T(8,128)(2,1)}, u32[]{:S(2)}, u32[]{:S(2)}) collective-permute-start(bf16[3,64,256]{2,1,0:T(8,128)(2,1)} %get-tuple-element.147), channel_id=1, source_target_pairs={{0,2},{1,3},{2,0},{3,1},{4,6},{5,7},{6,4},{7,5},{8,10},{9,11},{10,... | collective-permute-start | bytes 294920 | tf_op jit(solution)/shard_map/ppermute | solution.py:589
  69.4 9.4 %collective-permute-start.21 = (bf16[3,64,256]{2,1,0:T(8,128)(2,1)}, bf16[3,64,256]{2,1,0:T(8,128)(2,1)}, u32[]{:S(2)}, u32[]{:S(2)}) collective-permute-start(bf16[3,64,256]{2,1,0:T(8,128)(2,1)} %get-tuple-element.148), channel_id=1, source_target_pairs={{0,3},{1,2},{2,1},{3,0},{4,7},{5,6},{6,5},{7,4},{8,11},{9,10},{10,... | collective-permute-start | bytes 294920 | tf_op jit(solution)/shard_map/ppermute | solution.py:589
  77.3 32.3 %collective-permute-start.18 = (bf16[4,320,384]{2,1,0:T(8,128)(2,1)}, bf16[4,320,384]{2,1,0:T(8,128)(2,1)}, u32[]{:S(2)}, u32[]{:S(2)}) collective-permute-start(bf16[4,320,384]{2,1,0:T(8,128)(2,1)} %get-tuple-element.143), channel_id=1, source_target_pairs={{0,4},{4,0},{8,12},{12,8},{16,20},{20,16},{24,28},{28,24},{1,5},{5... | collective-permute-start | bytes 2949128 | tf_op jit(solution)/shard_map/ppermute | solution.py:583
  86.7 22.9 %all-to-all-start = ((bf16[8,256,256]{2,1,0:T(8,128)(2,1)}), bf16[8,256,256]{2,1,0:T(8,128)(2,1)S(1)}, u32[]{:S(2)}, u32[]{:S(2)}) async-start(bf16[8,256,256]{2,1,0:T(8,128)(2,1)} %packed.1), calls=%async_computation | async-start | bytes 2097152 | tf_op jit(solution)/shard_map/all_to_all | solution.py:879
  90.6 7.3 %collective-permute-start.22 = (bf16[3,64,256]{2,1,0:T(8,128)(2,1)}, bf16[3,64,256]{2,1,0:T(8,128)(2,1)S(1)}, u32[]{:S(2)}, u32[]{:S(2)}) collective-permute-start(bf16[3,64,256]{2,1,0:T(8,128)(2,1)} %get-tuple-element.154), channel_id=1, source_target_pairs={{0,1},{1,0},{2,3},{3,2},{4,5},{5,4},{6,7},{7,6},{8,9},{9,8},{10,11... | collective-permute-start | bytes 294920 | tf_op jit(solution)/shard_map/ppermute | solution.py:589
  92.9 7.0 %collective-permute-start.23 = (bf16[3,64,256]{2,1,0:T(8,128)(2,1)S(1)}, bf16[3,64,256]{2,1,0:T(8,128)(2,1)S(1)}, u32[]{:S(2)}, u32[]{:S(2)}) collective-permute-start(bf16[3,64,256]{2,1,0:T(8,128)(2,1)S(1)} %copy-done.38), channel_id=1, source_target_pairs={{0,2},{1,3},{2,0},{3,1},{4,6},{5,7},{6,4},{7,5},{8,10},{9,11},{10,... | collective-permute-start | bytes 294920 | tf_op jit(solution)/shard_map/ppermute | solution.py:589
  96.5 9.0 %collective-permute-start.24 = (bf16[3,64,256]{2,1,0:T(8,128)(2,1)S(1)}, bf16[3,64,256]{2,1,0:T(8,128)(2,1)S(1)}, u32[]{:S(2)}, u32[]{:S(2)}) collective-permute-start(bf16[3,64,256]{2,1,0:T(8,128)(2,1)S(1)} %copy-done.36), channel_id=1, source_target_pairs={{0,3},{1,2},{2,1},{3,0},{4,7},{5,6},{6,5},{7,4},{8,11},{9,10},{10,... | collective-permute-start | bytes 294920 | tf_op jit(solution)/shard_map/ppermute | solution.py:589
  107.0 1.8 %collective-permute-start.26 = (bf16[192,1024]{1,0:T(8,128)(2,1)S(1)}, bf16[192,1024]{1,0:T(8,128)(2,1)S(1)}, u32[]{:S(2)}, u32[]{:S(2)}) collective-permute-start(bf16[192,1024]{1,0:T(8,128)(2,1)S(1)} %get-tuple-element.163.refs_3_), channel_id=1, source_target_pairs={{0,4},{4,0},{8,12},{12,8},{16,20},{20,16},{24,28},{28,24},{1,5},{5... | collective-permute-start | bytes 1179656 | tf_op jit(solution)/shard_map/ppermute | solution.py:583
  107.8 1.8 %collective-permute-start.25 = (bf16[192,1024]{1,0:T(8,128)(2,1)S(1)}, bf16[192,1024]{1,0:T(8,128)(2,1)S(1)}, u32[]{:S(2)}, u32[]{:S(2)}) collective-permute-start(bf16[192,1024]{1,0:T(8,128)(2,1)S(1)} %copy-done.31), channel_id=1, source_target_pairs={{0,4},{4,0},{8,12},{12,8},{16,20},{20,16},{24,28},{28,24},{1,5},{5... | collective-permute-start | bytes 1179656 | tf_op jit(solution)/shard_map/ppermute | solution.py:583
  116.9 17.1 %collective-permute-start.29 = (bf16[2,320,512]{2,1,0:T(8,128)(2,1)S(1)}, bf16[2,320,512]{2,1,0:T(8,128)(2,1)S(1)}, u32[]{:S(2)}, u32[]{:S(2)}) collective-permute-start(bf16[2,320,512]{2,1,0:T(8,128)(2,1)S(1)} %get-tuple-element.183), channel_id=1, source_target_pairs={{0,16},{4,20},{8,24},{12,28},{16,0},{20,4},{24,8},{28,12},{1,17},{... | collective-permute-start | bytes 1966088 | tf_op jit(solution)/shard_map/ppermute | solution.py:583
  118.7 17.3 %collective-permute-start.27 = (bf16[2,320,512]{2,1,0:T(8,128)(2,1)S(1)}, bf16[2,320,512]{2,1,0:T(8,128)(2,1)S(1)}, u32[]{:S(2)}, u32[]{:S(2)}) collective-permute-start(bf16[2,320,512]{2,1,0:T(8,128)(2,1)S(1)} %get-tuple-element.181), channel_id=1, source_target_pairs={{0,8},{4,12},{8,0},{12,4},{16,24},{20,28},{24,16},{28,20},{1,9},{5... | collective-permute-start | bytes 1966088 | tf_op jit(solution)/shard_map/ppermute | solution.py:583
  125.5 12.2 %collective-permute-start.31 = (bf16[224,256]{1,0:T(8,128)(2,1)S(1)}, bf16[224,256]{1,0:T(8,128)(2,1)S(1)}, u32[]{:S(2)}, u32[]{:S(2)}) collective-permute-start(bf16[224,256]{1,0:T(8,128)(2,1)S(1)} %get-tuple-element.184.refs_0_), channel_id=1, source_target_pairs={{0,1},{1,0},{2,3},{3,2},{4,5},{5,4},{6,7},{7,6},{8,9},{9,8},{10,11... | collective-permute-start | bytes 344072 | tf_op jit(solution)/shard_map/ppermute | solution.py:589
  127.2 11.6 %collective-permute-start.32 = (bf16[224,256]{1,0:T(8,128)(2,1)S(1)}, bf16[224,256]{1,0:T(8,128)(2,1)S(1)}, u32[]{:S(2)}, u32[]{:S(2)}) collective-permute-start(bf16[224,256]{1,0:T(8,128)(2,1)S(1)} %get-tuple-element.184.refs_0_), channel_id=1, source_target_pairs={{0,2},{1,3},{2,0},{3,1},{4,6},{5,7},{6,4},{7,5},{8,10},{9,11},{10,... | collective-permute-start | bytes 344072 | tf_op jit(solution)/shard_map/ppermute | solution.py:589
  128.9 10.0 %collective-permute-start.33 = (bf16[224,256]{1,0:T(8,128)(2,1)S(1)}, bf16[224,256]{1,0:T(8,128)(2,1)S(1)}, u32[]{:S(2)}, u32[]{:S(2)}) collective-permute-start(bf16[224,256]{1,0:T(8,128)(2,1)S(1)} %get-tuple-element.184.refs_0_), channel_id=1, source_target_pairs={{0,3},{1,2},{2,1},{3,0},{4,7},{5,6},{6,5},{7,4},{8,11},{9,10},{10,... | collective-permute-start | bytes 344072 | tf_op jit(solution)/shard_map/ppermute | solution.py:589
  134.2 9.2 %collective-permute-start.30 = (bf16[1,320,512]{2,1,0:T(8,128)(2,1)S(1)}, bf16[1,320,512]{2,1,0:T(8,128)(2,1)S(1)}, u32[]{:S(2)}, u32[]{:S(2)}) collective-permute-start(bf16[1,320,512]{2,1,0:T(8,128)(2,1)S(1)} %slice.21), channel_id=1, source_target_pairs={{0,8},{4,12},{8,0},{12,4},{16,24},{20,28},{24,16},{28,20},{1,9},{5... | collective-permute-start | bytes 983048 | tf_op jit(solution)/shard_map/ppermute | solution.py:583
  136.2 9.1 %collective-permute-start.28 = (bf16[1,320,512]{2,1,0:T(8,128)(2,1)S(1)}, bf16[1,320,512]{2,1,0:T(8,128)(2,1)}, u32[]{:S(2)}, u32[]{:S(2)}) collective-permute-start(bf16[1,320,512]{2,1,0:T(8,128)(2,1)S(1)} %slice_bitcast_fusion), channel_id=1, source_target_pairs={{0,16},{4,20},{8,24},{12,28},{16,0},{20,4},{24,8},{28,12},{1,17},{... | collective-permute-start | bytes 983048 | tf_op jit(solution)/shard_map/ppermute | solution.py:583
  146.4 8.0 %collective-permute-start.34 = (bf16[2,80,1024]{2,1,0:T(8,128)(2,1)S(1)}, bf16[2,80,1024]{2,1,0:T(8,128)(2,1)S(1)}, u32[]{:S(2)}, u32[]{:S(2)}) collective-permute-start(bf16[2,80,1024]{2,1,0:T(8,128)(2,1)S(1)} %dynamic-slice_bitcast_fusion), channel_id=1, source_target_pairs={{0,1},{1,0},{2,3},{3,2},{4,5},{5,4},{6,7},{7,6},{8,9},{9,8},{10,11... | collective-permute-start | bytes 983048 | tf_op jit(solution)/shard_map/ppermute | solution.py:623
  148.2 10.2 %collective-permute-start.36 = (bf16[448,256]{1,0:T(8,128)(2,1)S(1)}, bf16[448,256]{1,0:T(8,128)(2,1)S(1)}, u32[]{:S(2)}, u32[]{:S(2)}) collective-permute-start(bf16[448,256]{1,0:T(8,128)(2,1)S(1)} %shard_sums.1.refs_0_), channel_id=1, source_target_pairs={{0,8},{4,12},{8,0},{12,4},{16,24},{20,28},{24,16},{28,20},{1,9},{5... | collective-permute-start | bytes 688136 | tf_op jit(solution)/shard_map/ppermute | solution.py:629
  149.1 9.3 %collective-permute-start.37 = (bf16[448,256]{1,0:T(8,128)(2,1)S(1)}, bf16[448,256]{1,0:T(8,128)(2,1)S(1)}, u32[]{:S(2)}, u32[]{:S(2)}) collective-permute-start(bf16[448,256]{1,0:T(8,128)(2,1)S(1)} %shard_sums.1.refs_0_), channel_id=1, source_target_pairs={{0,16},{4,20},{8,24},{12,28},{16,0},{20,4},{24,8},{28,12},{1,17},{... | collective-permute-start | bytes 688136 | tf_op jit(solution)/shard_map/ppermute | solution.py:629
  150.2 9.4 %collective-permute-start.38 = (bf16[448,256]{1,0:T(8,128)(2,1)S(1)}, bf16[448,256]{1,0:T(8,128)(2,1)S(1)}, u32[]{:S(2)}, u32[]{:S(2)}) collective-permute-start(bf16[448,256]{1,0:T(8,128)(2,1)S(1)} %shard_sums.1.refs_0_), channel_id=1, source_target_pairs={{0,24},{4,28},{8,16},{12,20},{16,8},{20,12},{24,0},{28,4},{1,25},{... | collective-permute-start | bytes 688136 | tf_op jit(solution)/shard_map/ppermute | solution.py:629
  154.6 8.9 %collective-permute-start.35 = (bf16[1,80,1024]{2,1,0:T(8,128)(2,1)S(1)}, bf16[1,80,1024]{2,1,0:T(8,128)(2,1)S(1)}, u32[]{:S(2)}, u32[]{:S(2)}) collective-permute-start(bf16[1,80,1024]{2,1,0:T(8,128)(2,1)S(1)} %constant_dynamic-slice_fusion), channel_id=1, source_target_pairs={{0,2},{1,3},{2,0},{3,1},{4,6},{5,7},{6,4},{7,5},{8,10},{9,11},{10,... | collective-permute-start | bytes 491528 | tf_op jit(solution)/shard_map/ppermute | solution.py:623
  159.6 4.6 %collective-permute-start.39 = (bf16[448,256]{1,0:T(8,128)(2,1)S(1)}, bf16[448,256]{1,0:T(8,128)(2,1)S(1)}, u32[]{:S(2)}, u32[]{:S(2)}) collective-permute-start(bf16[448,256]{1,0:T(8,128)(2,1)S(1)} %shard_sums.1.refs_0_), channel_id=1, source_target_pairs={{0,4},{4,0},{8,12},{12,8},{16,20},{20,16},{24,28},{28,24},{1,5},{5... | collective-permute-start | bytes 688136 | tf_op jit(solution)/shard_map/ppermute | solution.py:583
  159.6 4.6 %collective-permute-start.40 = (bf16[448,256]{1,0:T(8,128)(2,1)S(1)}, bf16[448,256]{1,0:T(8,128)(2,1)S(1)}, u32[]{:S(2)}, u32[]{:S(2)}) collective-permute-start(bf16[448,256]{1,0:T(8,128)(2,1)S(1)} %collective-permute-done.36.refs_2_), channel_id=1, source_target_pairs={{0,4},{4,0},{8,12},{12,8},{16,20},{20,16},{24,28},{28,24},{1,5},{5... | collective-permute-start | bytes 688136 | tf_op jit(solution)/shard_map/ppermute | solution.py:583
  160.1 4.1 %collective-permute-start.41 = (bf16[448,256]{1,0:T(8,128)(2,1)S(1)}, bf16[448,256]{1,0:T(8,128)(2,1)S(1)}, u32[]{:S(2)}, u32[]{:S(2)}) collective-permute-start(bf16[448,256]{1,0:T(8,128)(2,1)S(1)} %collective-permute-done.37.refs_4_), channel_id=1, source_target_pairs={{0,4},{4,0},{8,12},{12,8},{16,20},{20,16},{24,28},{28,24},{1,5},{5... | collective-permute-start | bytes 688136 | tf_op jit(solution)/shard_map/ppermute | solution.py:583
  160.1 4.1 %collective-permute-start.42 = (bf16[448,256]{1,0:T(8,128)(2,1)S(1)}, bf16[448,256]{1,0:T(8,128)(2,1)S(1)}, u32[]{:S(2)}, u32[]{:S(2)}) collective-permute-start(bf16[448,256]{1,0:T(8,128)(2,1)S(1)} %collective-permute-done.38.refs_6_), channel_id=1, source_target_pairs={{0,4},{4,0},{8,12},{12,8},{16,20},{20,16},{24,28},{28,24},{1,5},{5... | collective-permute-start | bytes 688136 | tf_op jit(solution)/shard_map/ppermute | solution.py:583
  (45 other events, 281.0 us)

commit v9 on v7

--- a/solution.py
+++ b/solution.py
@@ -871,6 +871,7 @@
     width = spec_w.shape[-1]
     blocks = spec_w.shape[2] // shards
     head_rows = head_w.shape[0] // groups
+    _, head_grad, spec_grad = lax.optimization_barrier((spec_back[-1][1], head_grad, spec_grad))
     weight_sums = lax.all_to_all(
         packed(routes, head_grad, spec_grad, predicted, groups), "grp", split_axis=0, concat_axis=0, tiled=True
     )
@@ -893,7 +894,7 @@
     predictions = predictions.reshape(targets.shape)
     spec_rows = spec_grad.shape[0] // groups
     outgoing = shard_sums(routes, across([small] * shards), head_rows, spec_rows, spec_bias.shape[0])
-    _, outgoing = lax.optimization_barrier((ends, outgoing))
+    ends, outgoing = lax.optimization_barrier((ends, outgoing))
     part = jnp.concatenate(ends, axis=-1)
     part = part.reshape(shards, part.shape[0] // shards, -1)
     part = scatter_step(part, 1, shards, shard_at)

time: 181 us -> 168 us (0.928)
  waiting for transfers between devices: 48.3 us -> 35.4 us
  starting transfers between devices: 66.5 us -> 69.1 us
  other arithmetic: 5.17 us -> 3.26 us
    ppermute x11, waiting for transfers between devices: 16.9 us -> 9.54 us  [swap_bit(): lax.ppermute(values, 'grp', [(g, g ^ 1 << bit) for g in range(groups)])]
    ppermute x27, waiting for transfers between devices: 24.2 us -> 18.6 us  [across(): lax.ppermute(pieces[k], 'fft', [(z, z ^ k) for z in range(shards)])]
    ppermute x2, waiting for transfers between devices: 0.01 us -> 4.68 us  [scatter_step(): received = lax.ppermute(send, 'fft', [(z, z ^ bit) for z in range(shards)])]
    ppermute x3, waiting for transfers between devices: 7.19 us -> 2.58 us  [from_same_core(): lax.ppermute(values, 'grp', [(g, g ^ k) for g in range(groups)])]
    ppermute x2, starting transfers between devices: 1.8 us -> 4.41 us  [scatter_step(): received = lax.ppermute(send, 'fft', [(z, z ^ bit) for z in range(shards)])]
    convert_element_type x3 -> x1, other arithmetic: 2.33 us -> 0.18 us  [add_half(): return (left.astype(FULL) + right.astype(FULL)).astype(HALF)]
    unnamed x94 -> x90, local copies, waits for them, and re-layouts: 16.4 us -> 14.7 us
  transfers between devices with their start and end apart: 44 -> 44, of which waited for: 15 -> 15; matrix products, arithmetic and copies ran while one was open for 2% -> 2% of each run, Pallas kernels for 12% -> 13%
where the time goes in v9:
time: 168 us; the launch traced here: 167 us
  starting transfers between devices  69.1 us (41%)
  Pallas kernels  41.7 us (25%)
  waiting for transfers between devices  35.4 us (21%)
  local copies, waits for them, and re-layouts  16.1 us (10%)
  other arithmetic  3.26 us (2%)
    ppermute x27, starting transfers between devices, across(): lax.ppermute(pieces[k], 'fft', [(z, z ^ k) for z in range(shards)])  49.3 us
    ppermute x27, waiting for transfers between devices, across(): lax.ppermute(pieces[k], 'fft', [(z, z ^ k) for z in range(shards)])  18.6 us
    unnamed x90, local copies, waits for them, and re-layouts  14.7 us
    pallas_call x1, Pallas kernels, embed(): pl.pallas_call(body, grid_spec=pltpu.PrefetchScalarGridSpec(num_scalar_pr...  10.1 us
    ppermute x11, waiting for transfers between devices, swap_bit(): lax.ppermute(values, 'grp', [(g, g ^ 1 << bit) for g in range(groups)])  9.54 us
    pallas_call x2, Pallas kernels, embed_grad_parts(): pl.pallas_call(body, grid_spec=pltpu.PrefetchScalarGridSpec(num_scalar_pr...  8.18 us
    ppermute x11, starting transfers between devices, swap_bit(): lax.ppermute(values, 'grp', [(g, g ^ 1 << bit) for g in range(groups)])  8.01 us
    pallas_call x2, Pallas kernels, spectral_back_chunk(): pl.pallas_call(body, grid_spec=pltpu.PrefetchScalarGridSpec(num_scalar_pr...  7.43 us
  transfers between devices with their start and end apart: 44, of which 15 were waited for; matrix products, arithmetic and copies ran while one was open for 2% of the time, Pallas kernels for 13%

profile of v9, /device:TPU:0, one launch (start us, length us, event | category | flops | bytes accessed | tf_op | source)
XLA Modules:
  0.0 166.7 jit_solution(10190871115794316993)
XLA Ops:
  2.0 10.1 %embed.1 = (bf16[384,1024]{1,0:T(8,128)(2,1)}, bf16[384,1024]{1,0:T(8,128)(2,1)}, f32[384,256]{1,0:T(8,128)}, bf16[4,320,384]{2,1,0:T(8,128)(2,1)}, bf16[4,320,3...) custom-call(s32[15]{0:T(128)} %concatenate.12.scal_ref, ...), custom_call_target="tpu_custom_call" | custom-call | flops 2013265920 | bytes 7208960 | tf_op jit(solution)/shard_map/embed/pallas_call | solution.py:157
  12.1 4.1 %collective-permute-start.10 = (bf16[3,64,256]{2,1,0:T(8,128)(2,1)}, bf16[3,64,256]{2,1,0:T(8,128)(2,1)S(1)}, u32[]{:S(2)}, u32[]{:S(2)}) collective-permute-start(bf16[3,64,256]{2,1,0:T(8,128)(2,1)} %get-tuple-element.119), channel_id=1, source_target_pairs={{0,2},{1,3},{2,0},{3,1},{4,6},{5,7},{6,4},{7,5},{8,10},{9,11},{10,... | collective-permute-start | bytes 294920 | tf_op jit(solution)/shard_map/ppermute | solution.py:589
  17.8 1.8 %collective-permute-start = (bf16[3,64,256]{2,1,0:T(8,128)(2,1)}, bf16[3,64,256]{2,1,0:T(8,128)(2,1)S(1)}, u32[]{:S(2)}, u32[]{:S(2)}) collective-permute-start(bf16[3,64,256]{2,1,0:T(8,128)(2,1)} %get-tuple-element.104), channel_id=1, source_target_pairs={{0,1},{1,0},{2,3},{3,2},{4,5},{5,4},{6,7},{7,6},{8,9},{9,8},{10,11... | collective-permute-start | bytes 294920 | tf_op jit(solution)/shard_map/ppermute | solution.py:589
  19.5 1.7 %collective-permute-start.1 = (bf16[3,64,256]{2,1,0:T(8,128)(2,1)}, bf16[3,64,256]{2,1,0:T(8,128)(2,1)S(1)}, u32[]{:S(2)}, u32[]{:S(2)}) collective-permute-start(bf16[3,64,256]{2,1,0:T(8,128)(2,1)} %get-tuple-element.105), channel_id=1, source_target_pairs={{0,2},{1,3},{2,0},{3,1},{4,6},{5,7},{6,4},{7,5},{8,10},{9,11},{10,... | collective-permute-start | bytes 294920 | tf_op jit(solution)/shard_map/ppermute | solution.py:589
  21.2 3.0 %collective-permute-done.10.refs_2_ = bf16[3,64,256]{2,1,0:T(8,128)(2,1)S(1)} collective-permute-done((bf16[3,64,256]{2,1,0:T(8,128)(2,1)}, bf16[3,64,256]{2,1,0:T(8,128)(2,1)S(1)}, u32[]{:S(2)}, u32[]{:S(2)}) %collective-permute-start.10) | collective-permute-done | bytes 98336 | tf_op jit(solution)/shard_map/ppermute | solution.py:589
  24.3 2.8 %collective-permute-start.2 = (bf16[3,64,256]{2,1,0:T(8,128)(2,1)}, bf16[3,64,256]{2,1,0:T(8,128)(2,1)S(1)}, u32[]{:S(2)}, u32[]{:S(2)}) collective-permute-start(bf16[3,64,256]{2,1,0:T(8,128)(2,1)} %get-tuple-element.106), channel_id=1, source_target_pairs={{0,3},{1,2},{2,1},{3,0},{4,7},{5,6},{6,5},{7,4},{8,11},{9,10},{10,... | collective-permute-start | bytes 294920 | tf_op jit(solution)/shard_map/ppermute | solution.py:589
  28.8 2.3 %spectral.3 = (bf16[3,64,256]{2,1,0:T(8,128)(2,1)S(1)}, bf16[3,64,256]{2,1,0:T(8,128)(2,1)S(1)}, bf16[3,64,256]{2,1,0:T(8,128)(2,1)S(1)}, bf16[3,64,256]{2,1,0:T...) custom-call(s32[15]{0:T(128)S(1)} %copy-done.17, ...), custom_call_target="tpu_custom_call" | custom-call | flops 704643072 | bytes 3145728 | tf_op jit(solution)/shard_map/spectral/pallas_call | solution.py:277
  31.3 1.6 collective-permute-start.13
  32.9 2.7 %collective-permute-start.14 = (bf16[3,64,256]{2,1,0:T(8,128)(2,1)S(1)}, bf16[3,64,256]{2,1,0:T(8,128)(2,1)S(1)}, u32[]{:S(2)}, u32[]{:S(2)}) collective-permute-start(bf16[3,64,256]{2,1,0:T(8,128)(2,1)S(1)} %get-tuple-element.127), channel_id=1, source_target_pairs={{0,3},{1,2},{2,1},{3,0},{4,7},{5,6},{6,5},{7,4},{8,11},{9,10},{10,... | collective-permute-start | bytes 294920 | tf_op jit(solution)/shard_map/ppermute | solution.py:589
  38.8 2.3 %spectral.2 = (bf16[3,64,256]{2,1,0:T(8,128)(2,1)S(1)}, bf16[3,64,256]{2,1,0:T(8,128)(2,1)S(1)}, bf16[3,64,256]{2,1,0:T(8,128)(2,1)S(1)}, bf16[3,64,256]{2,1,0:T...) custom-call(s32[15]{0:T(128)S(1)} %copy-done.17, ...), custom_call_target="tpu_custom_call" | custom-call | flops 704643072 | bytes 3145728 | tf_op jit(solution)/shard_map/spectral/pallas_call | solution.py:277
  41.3 1.7 %collective-permute-start.4 = (bf16[3,64,256]{2,1,0:T(8,128)(2,1)S(1)}, bf16[3,64,256]{2,1,0:T(8,128)(2,1)S(1)}, u32[]{:S(2)}, u32[]{:S(2)}) collective-permute-start(bf16[3,64,256]{2,1,0:T(8,128)(2,1)S(1)} %get-tuple-element.114), channel_id=1, source_target_pairs={{0,2},{1,3},{2,0},{3,1},{4,6},{5,7},{6,4},{7,5},{8,10},{9,11},{10,... | collective-permute-start | bytes 294920 | tf_op jit(solution)/shard_map/ppermute | solution.py:589
  43.0 2.7 %collective-permute-start.5 = (bf16[3,64,256]{2,1,0:T(8,128)(2,1)S(1)}, bf16[3,64,256]{2,1,0:T(8,128)(2,1)S(1)}, u32[]{:S(2)}, u32[]{:S(2)}) collective-permute-start(bf16[3,64,256]{2,1,0:T(8,128)(2,1)S(1)} %get-tuple-element.115), channel_id=1, source_target_pairs={{0,3},{1,2},{2,1},{3,0},{4,7},{5,6},{6,5},{7,4},{8,11},{9,10},{10,... | collective-permute-start | bytes 294920 | tf_op jit(solution)/shard_map/ppermute | solution.py:589
  46.8 1.7 %collective-permute-start.16 = (bf16[3,64,256]{2,1,0:T(8,128)(2,1)S(1)}, bf16[3,64,256]{2,1,0:T(8,128)(2,1)S(1)}, u32[]{:S(2)}, u32[]{:S(2)}) collective-permute-start(bf16[3,64,256]{2,1,0:T(8,128)(2,1)S(1)} %get-tuple-element.131.refs_2_.refs_0_.res_ref), channel_id=1, source_target_pairs={{0,2},{1,3},{2,0},{3,1},{4,6},{5,7},{6,4},{7,5},{8,10},{9,11},{10,... | collective-permute-start | bytes 294920 | tf_op jit(solution)/shard_map/ppermute | solution.py:589
  48.5 2.7 %collective-permute-start.17 = (bf16[3,64,256]{2,1,0:T(8,128)(2,1)S(1)}, bf16[3,64,256]{2,1,0:T(8,128)(2,1)S(1)}, u32[]{:S(2)}, u32[]{:S(2)}) collective-permute-start(bf16[3,64,256]{2,1,0:T(8,128)(2,1)S(1)} %get-tuple-element.131.refs_2_.refs_0_.res_ref), channel_id=1, source_target_pairs={{0,3},{1,2},{2,1},{3,0},{4,7},{5,6},{6,5},{7,4},{8,11},{9,10},{10,... | collective-permute-start | bytes 294920 | tf_op jit(solution)/shard_map/ppermute | solution.py:589
  53.2 6.5 %collective-permute-start.6 = (bf16[3,64,256]{2,1,0:T(8,128)(2,1)S(1)}, bf16[3,64,256]{2,1,0:T(8,128)(2,1)S(1)}, u32[]{:S(2)}, u32[]{:S(2)}) collective-permute-start(bf16[3,64,256]{2,1,0:T(8,128)(2,1)S(1)} %get-tuple-element.116.refs_3_.refs_0_.res_ref), channel_id=1, source_target_pairs={{0,1},{1,0},{2,3},{3,2},{4,5},{5,4},{6,7},{7,6},{8,9},{9,8},{10,11... | collective-permute-start | bytes 294920 | tf_op jit(solution)/shard_map/ppermute | solution.py:589
  60.6 1.5 collective-permute-start.8
  62.7 3.7 %spectral_back.2 = (bf16[3,64,256]{2,1,0:T(8,128)(2,1)S(1)}, bf16[3,64,256]{2,1,0:T(8,128)(2,1)}, bf16[3,64,256]{2,1,0:T(8,128)(2,1)S(1)}, bf16[3,64,256]{2,1,0:...) custom-call(s32[15]{0:T(128)S(1)} %copy-done.17, bf16[3,512,256]{2,1,0:T(8,128)(2,1)S(1)} %copy-done.4, ...), custom_call_target="tpu_custom_call" | custom-call | flops 1006632960 | bytes 3145728 | tf_op jit(solution)/shard_map/spectral_back/pallas_call | solution.py:440
  67.0 2.1 %collective-permute-done.7.refs_2_ = bf16[3,64,256]{2,1,0:T(8,128)(2,1)S(1)} collective-permute-done((bf16[3,64,256]{2,1,0:T(8,128)(2,1)S(1)}, bf16[3,64,256]{2,1,0:T(8,128)(2,1)S(1)}, u32[]{:S(2)}, u32[]{:S(2)}) %collective-permute-start.7) | collective-permute-done | bytes 98336 | tf_op jit(solution)/shard_map/ppermute | solution.py:589
  69.1 3.8 %spectral_back.3 = (bf16[3,64,256]{2,1,0:T(8,128)(2,1)S(1)}, bf16[3,64,256]{2,1,0:T(8,128)(2,1)}, bf16[3,64,256]{2,1,0:T(8,128)(2,1)}, bf16[3,64,256]{2,1,0:T(8,...) custom-call(s32[15]{0:T(128)S(1)} %copy-done.17, bf16[3,512,256]{2,1,0:T(8,128)(2,1)S(1)} %copy-done.4, ...), custom_call_target="tpu_custom_call" | custom-call | flops 1006632960 | bytes 3145728 | tf_op jit(solution)/shard_map/spectral_back/pallas_call | solution.py:440
  74.2 1.6 collective-permute-start.22
  76.0 3.0 %collective-permute-done.22.refs_1_ = bf16[3,64,256]{2,1,0:T(8,128)(2,1)S(1)} collective-permute-done((bf16[3,64,256]{2,1,0:T(8,128)(2,1)}, bf16[3,64,256]{2,1,0:T(8,128)(2,1)S(1)}, u32[]{:S(2)}, u32[]{:S(2)}) %collective-permute-start.22) | collective-permute-done | bytes 98336 | tf_op jit(solution)/shard_map/ppermute | solution.py:589
  81.9 1.7 %packed.1 = bf16[8,256,256]{2,1,0:T(8,128)(2,1)} custom-call(s32[17]{0:T(128)S(1)} %concatenate.11.routes_ref, bf16[1024,256]{1,0:T(8,128)(2,1)S(1)} %copy-done.6, bf16[512,256]{1,0:T(8,128)(2,1)S(1)} %copy-done.10, bf16[3,64,256]{2,1,0:T(8,128)(2,1)S(1)} %get-tuple-element.158.refs_0_, bf16[3,64,256]{2,1,0:T(8,128)(2,1)S(1)} %copy-done.12), custom_call_target="tpu_custom_call" | custom-call | tf_op jit(solution)/shard_map/packed/pallas_call | solution.py:645
  83.6 3.9 %all-to-all-start = ((bf16[8,256,256]{2,1,0:T(8,128)(2,1)}), bf16[8,256,256]{2,1,0:T(8,128)(2,1)S(1)}, u32[]{:S(2)}, u32[]{:S(2)}) async-start(bf16[8,256,256]{2,1,0:T(8,128)(2,1)} %packed.1), calls=%async_computation | async-start | bytes 2097152 | tf_op jit(solution)/shard_map/all_to_all | solution.py:875
  87.5 2.7 %collective-permute-start.23 = (bf16[3,64,256]{2,1,0:T(8,128)(2,1)}, bf16[3,64,256]{2,1,0:T(8,128)(2,1)S(1)}, u32[]{:S(2)}, u32[]{:S(2)}) collective-permute-start(bf16[3,64,256]{2,1,0:T(8,128)(2,1)} %get-tuple-element.151), channel_id=1, source_target_pairs={{0,2},{1,3},{2,0},{3,1},{4,6},{5,7},{6,4},{7,5},{8,10},{9,11},{10,... | collective-permute-start | bytes 294920 | tf_op jit(solution)/shard_map/ppermute | solution.py:589
  91.5 3.0 %collective-permute-start.20 = (bf16[3,64,256]{2,1,0:T(8,128)(2,1)}, bf16[3,64,256]{2,1,0:T(8,128)(2,1)S(1)}, u32[]{:S(2)}, u32[]{:S(2)}) collective-permute-start(bf16[3,64,256]{2,1,0:T(8,128)(2,1)} %copy-done.34), channel_id=1, source_target_pairs={{0,2},{1,3},{2,0},{3,1},{4,6},{5,7},{6,4},{7,5},{8,10},{9,11},{10,... | collective-permute-start | bytes 294920 | tf_op jit(solution)/shard_map/ppermute | solution.py:589
  94.5 4.2 %collective-permute-done.23.refs_2_ = bf16[3,64,256]{2,1,0:T(8,128)(2,1)S(1)} collective-permute-done((bf16[3,64,256]{2,1,0:T(8,128)(2,1)}, bf16[3,64,256]{2,1,0:T(8,128)(2,1)S(1)}, u32[]{:S(2)}, u32[]{:S(2)}) %collective-permute-start.23) | collective-permute-done | bytes 98336 | tf_op jit(solution)/shard_map/ppermute | solution.py:589
  98.7 2.0 %collective-permute-start.21 = (bf16[3,64,256]{2,1,0:T(8,128)(2,1)}, bf16[3,64,256]{2,1,0:T(8,128)(2,1)S(1)}, u32[]{:S(2)}, u32[]{:S(2)}) collective-permute-start(bf16[3,64,256]{2,1,0:T(8,128)(2,1)} %copy-done.33), channel_id=1, source_target_pairs={{0,3},{1,2},{2,1},{3,0},{4,7},{5,6},{6,5},{7,4},{8,11},{9,10},{10,... | collective-permute-start | bytes 294920 | tf_op jit(solution)/shard_map/ppermute | solution.py:589
  100.7 1.4 embedded_back.3
  102.3 4.7 %collective-permute-done.20.refs_2_ = bf16[3,64,256]{2,1,0:T(8,128)(2,1)S(1)} collective-permute-done((bf16[3,64,256]{2,1,0:T(8,128)(2,1)}, bf16[3,64,256]{2,1,0:T(8,128)(2,1)S(1)}, u32[]{:S(2)}, u32[]{:S(2)}) %collective-permute-start.20) | collective-permute-done | bytes 98336 | tf_op jit(solution)/shard_map/ppermute | solution.py:589
  106.9 1.4 embedded_back.2
  114.4 4.1 %embed_grad.2 = (bf16[2,320,512]{2,1,0:T(8,128)(2,1)S(1)}, bf16[2,320,512]{2,1,0:T(8,128)(2,1)S(1)}) custom-call(s32[15]{0:T(128)S(1)} %copy-done.17, bf16[4,320,384]{2,1,0:T(8,128)(2,1)S(1)} %copy-done.39, bf16[4,320,384]{2,1,0:T(8,128)(2,1)} %collective-permute-done.18.refs_1_, bf16[192,1024]{1,0:T(8,128)(2,1)S(1)} %copy-done.32, ...), custom_call_target="tpu_custom_call" | custom-call | flops 1006632960 | bytes 4063232 | tf_op jit(solution)/shard_map/embed_grad/pallas_call | solution.py:555
  118.5 2.0 %collective-permute-start.29 = (bf16[2,320,512]{2,1,0:T(8,128)(2,1)S(1)}, bf16[2,320,512]{2,1,0:T(8,128)(2,1)S(1)}, u32[]{:S(2)}, u32[]{:S(2)}) collective-permute-start(bf16[2,320,512]{2,1,0:T(8,128)(2,1)S(1)} %get-tuple-element.181), channel_id=1, source_target_pairs={{0,16},{4,20},{8,24},{12,28},{16,0},{20,4},{24,8},{28,12},{1,17},{... | collective-permute-start | bytes 1966088 | tf_op jit(solution)/shard_map/ppermute | solution.py:583
  120.6 1.5 collective-permute-start.27
  122.0 4.1 %embed_grad.3 = (bf16[2,320,512]{2,1,0:T(8,128)(2,1)S(1)}, bf16[2,320,512]{2,1,0:T(8,128)(2,1)S(1)}) custom-call(s32[15]{0:T(128)S(1)} %copy-done.17, bf16[4,320,384]{2,1,0:T(8,128)(2,1)S(1)} %copy-done.39, bf16[4,320,384]{2,1,0:T(8,128)(2,1)} %collective-permute-done.18.refs_1_, bf16[192,1024]{1,0:T(8,128)(2,1)S(1)} %copy-done.32, ...), custom_call_target="tpu_custom_call" | custom-call | flops 1006632960 | bytes 4063232 | tf_op jit(solution)/shard_map/embed_grad/pallas_call | solution.py:555
  127.5 1.9 %collective-permute-start.31 = (bf16[224,256]{1,0:T(8,128)(2,1)S(1)}, bf16[224,256]{1,0:T(8,128)(2,1)S(1)}, u32[]{:S(2)}, u32[]{:S(2)}) collective-permute-start(bf16[224,256]{1,0:T(8,128)(2,1)S(1)} %get-tuple-element.182.refs_0_), channel_id=1, source_target_pairs={{0,1},{1,0},{2,3},{3,2},{4,5},{5,4},{6,7},{7,6},{8,9},{9,8},{10,11... | collective-permute-start | bytes 344072 | tf_op jit(solution)/shard_map/ppermute | solution.py:589
  130.1 1.7 %collective-permute-start.33 = (bf16[224,256]{1,0:T(8,128)(2,1)S(1)}, bf16[224,256]{1,0:T(8,128)(2,1)S(1)}, u32[]{:S(2)}, u32[]{:S(2)}) collective-permute-start(bf16[224,256]{1,0:T(8,128)(2,1)S(1)} %get-tuple-element.182.refs_0_), channel_id=1, source_target_pairs={{0,3},{1,2},{2,1},{3,0},{4,7},{5,6},{6,5},{7,4},{8,11},{9,10},{10,... | collective-permute-start | bytes 344072 | tf_op jit(solution)/shard_map/ppermute | solution.py:589
  131.8 3.9 %collective-permute-done.29 = bf16[2,320,512]{2,1,0:T(8,128)(2,1)S(1)} collective-permute-done((bf16[2,320,512]{2,1,0:T(8,128)(2,1)S(1)}, bf16[2,320,512]{2,1,0:T(8,128)(2,1)S(1)}, u32[]{:S(2)}, u32[]{:S(2)}) %collective-permute-start.29) | collective-permute-done | bytes 655392 | tf_op jit(solution)/shard_map/ppermute | solution.py:583
  136.0 1.8 %collective-permute-start.30 = (bf16[1,320,512]{2,1,0:T(8,128)(2,1)S(1)}, bf16[1,320,512]{2,1,0:T(8,128)(2,1)S(1)}, u32[]{:S(2)}, u32[]{:S(2)}) collective-permute-start(bf16[1,320,512]{2,1,0:T(8,128)(2,1)S(1)} %slice.21), channel_id=1, source_target_pairs={{0,8},{4,12},{8,0},{12,4},{16,24},{20,28},{24,16},{28,20},{1,9},{5... | collective-permute-start | bytes 983048 | tf_op jit(solution)/shard_map/ppermute | solution.py:583
  138.0 1.5 collective-permute-start.28
  141.4 4.0 %collective-permute-done.30 = bf16[1,320,512]{2,1,0:T(8,128)(2,1)S(1)} collective-permute-done((bf16[1,320,512]{2,1,0:T(8,128)(2,1)S(1)}, bf16[1,320,512]{2,1,0:T(8,128)(2,1)S(1)}, u32[]{:S(2)}, u32[]{:S(2)}) %collective-permute-start.30) | collective-permute-done | bytes 327712 | tf_op jit(solution)/shard_map/ppermute | solution.py:583
  145.5 1.4 collective-permute-done.28
  147.1 1.9 %collective-permute-start.34 = (bf16[2,80,1024]{2,1,0:T(8,128)(2,1)S(1)}, bf16[2,80,1024]{2,1,0:T(8,128)(2,1)S(1)}, u32[]{:S(2)}, u32[]{:S(2)}) collective-permute-start(bf16[2,80,1024]{2,1,0:T(8,128)(2,1)S(1)} %dynamic-slice_bitcast_fusion), channel_id=1, source_target_pairs={{0,1},{1,0},{2,3},{3,2},{4,5},{5,4},{6,7},{7,6},{8,9},{9,8},{10,11... | collective-permute-start | bytes 983048 | tf_op jit(solution)/shard_map/ppermute | solution.py:623
  151.1 1.5 collective-permute-start.38
  152.5 2.7 %collective-permute-done.34 = bf16[2,80,1024]{2,1,0:T(8,128)(2,1)S(1)} collective-permute-done((bf16[2,80,1024]{2,1,0:T(8,128)(2,1)S(1)}, bf16[2,80,1024]{2,1,0:T(8,128)(2,1)S(1)}, u32[]{:S(2)}, u32[]{:S(2)}) %collective-permute-start.34) | collective-permute-done | bytes 327712 | tf_op jit(solution)/shard_map/ppermute | solution.py:623
  155.3 2.5 %collective-permute-start.35 = (bf16[1,80,1024]{2,1,0:T(8,128)(2,1)S(1)}, bf16[1,80,1024]{2,1,0:T(8,128)(2,1)S(1)}, u32[]{:S(2)}, u32[]{:S(2)}) collective-permute-start(bf16[1,80,1024]{2,1,0:T(8,128)(2,1)S(1)} %constant_dynamic-slice_fusion), channel_id=1, source_target_pairs={{0,2},{1,3},{2,0},{3,1},{4,6},{5,7},{6,4},{7,5},{8,10},{9,11},{10,... | collective-permute-start | bytes 491528 | tf_op jit(solution)/shard_map/ppermute | solution.py:623
  158.8 1.6 collective-permute-done.38.refs_6_
  161.4 2.0 %collective-permute-done.35 = bf16[1,80,1024]{2,1,0:T(8,128)(2,1)S(1)} collective-permute-done((bf16[1,80,1024]{2,1,0:T(8,128)(2,1)S(1)}, bf16[1,80,1024]{2,1,0:T(8,128)(2,1)S(1)}, u32[]{:S(2)}, u32[]{:S(2)}) %collective-permute-start.35) | collective-permute-done | bytes 163872 | tf_op jit(solution)/shard_map/ppermute | solution.py:623
  164.2 2.5 %assembled.1 = (f32[1024,256]{1,0:T(8,128)}, f32[2,2,8,128,128]{4,3,2,1,0:T(8,128)}, f32[2,2,8,128]{3,2,1,0:T(8,128)}, f32[1,1024]{1,0:T(1,128)}, f32[1,1024]{1,0:T(1,128)}, /*index=5*/f32[1,256]{1,0:T(1,128)}) custom-call(s32[15]{0:T(128)S(1)} %copy-done.17, bf16[448,256]{1,0:T(8,128)(2,1)S(1)} %shard_sums.1.refs_0_, ...), custom_call_target="tpu_custom_call" | custom-call | tf_op jit(solution)/shard_map/assembled/pallas_call | solution.py:790
  (167 shorter events, 34.7 us)
Async XLA Ops:
  2.0 25.9 %copy-start.2 = (bf16[2,2,8,128,128]{4,3,2,1,0:T(8,128)(2,1)S(1)}, bf16[2,2,8,128,128]{4,3,2,1,0:T(8,128)(2,1)}, u32[]{:S(2)}) copy-start(bf16[2,2,8,128,128]{4,3,2,1,0:T(8,128)(2,1)} %w_ref.15) | copy-start | bytes 3145732
  2.0 25.9 %copy-start.4 = (bf16[3,512,256]{2,1,0:T(8,128)(2,1)S(1)}, bf16[3,512,256]{2,1,0:T(8,128)(2,1)}, u32[]{:S(2)}) copy-start(bf16[3,512,256]{2,1,0:T(8,128)(2,1)} %constant.76.clone.t_ref) | copy-start | bytes 2359300
  2.0 25.9 %copy-start.17 = (s32[15]{0:T(128)S(1)}, s32[15]{0:T(128)}, u32[]{:S(2)}) copy-start(s32[15]{0:T(128)} %concatenate.12.scal_ref) | copy-start | bytes 184
  2.0 25.9 %copy-start.37 = (f32[2,2,8,128]{3,2,1,0:T(8,128)S(1)}, f32[2,2,8,128]{3,2,1,0:T(8,128)}, u32[]{:S(2)}) copy-start(f32[2,2,8,128]{3,2,1,0:T(8,128)} %b_ref.3) | copy-start | bytes 49156
  12.1 12.2 %collective-permute-start.10 = (bf16[3,64,256]{2,1,0:T(8,128)(2,1)}, bf16[3,64,256]{2,1,0:T(8,128)(2,1)S(1)}, u32[]{:S(2)}, u32[]{:S(2)}) collective-permute-start(bf16[3,64,256]{2,1,0:T(8,128)(2,1)} %get-tuple-element.119), channel_id=1, source_target_pairs={{0,2},{1,3},{2,0},{3,1},{4,6},{5,7},{6,4},{7,5},{8,10},{9,11},{10,... | collective-permute-start | bytes 294920 | tf_op jit(solution)/shard_map/ppermute | solution.py:589
  16.2 11.7 %collective-permute-start.11 = (bf16[3,64,256]{2,1,0:T(8,128)(2,1)}, bf16[3,64,256]{2,1,0:T(8,128)(2,1)S(1)}, u32[]{:S(2)}, u32[]{:S(2)}) collective-permute-start(bf16[3,64,256]{2,1,0:T(8,128)(2,1)} %get-tuple-element.120), channel_id=1, source_target_pairs={{0,3},{1,2},{2,1},{3,0},{4,7},{5,6},{6,5},{7,4},{8,11},{9,10},{10,... | collective-permute-start | bytes 294920 | tf_op jit(solution)/shard_map/ppermute | solution.py:589
  17.5 10.3 %collective-permute-start.9 = (bf16[3,64,256]{2,1,0:T(8,128)(2,1)}, bf16[3,64,256]{2,1,0:T(8,128)(2,1)S(1)}, u32[]{:S(2)}, u32[]{:S(2)}) collective-permute-start(bf16[3,64,256]{2,1,0:T(8,128)(2,1)} %get-tuple-element.118), channel_id=1, source_target_pairs={{0,1},{1,0},{2,3},{3,2},{4,5},{5,4},{6,7},{7,6},{8,9},{9,8},{10,11... | collective-permute-start | bytes 294920 | tf_op jit(solution)/shard_map/ppermute | solution.py:589
  17.8 15.1 %collective-permute-start = (bf16[3,64,256]{2,1,0:T(8,128)(2,1)}, bf16[3,64,256]{2,1,0:T(8,128)(2,1)S(1)}, u32[]{:S(2)}, u32[]{:S(2)}) collective-permute-start(bf16[3,64,256]{2,1,0:T(8,128)(2,1)} %get-tuple-element.104), channel_id=1, source_target_pairs={{0,1},{1,0},{2,3},{3,2},{4,5},{5,4},{6,7},{7,6},{8,9},{9,8},{10,11... | collective-permute-start | bytes 294920 | tf_op jit(solution)/shard_map/ppermute | solution.py:589
  19.5 16.0 %collective-permute-start.1 = (bf16[3,64,256]{2,1,0:T(8,128)(2,1)}, bf16[3,64,256]{2,1,0:T(8,128)(2,1)S(1)}, u32[]{:S(2)}, u32[]{:S(2)}) collective-permute-start(bf16[3,64,256]{2,1,0:T(8,128)(2,1)} %get-tuple-element.105), channel_id=1, source_target_pairs={{0,2},{1,3},{2,0},{3,1},{4,6},{5,7},{6,4},{7,5},{8,10},{9,11},{10,... | collective-permute-start | bytes 294920 | tf_op jit(solution)/shard_map/ppermute | solution.py:589
  24.3 11.3 %collective-permute-start.2 = (bf16[3,64,256]{2,1,0:T(8,128)(2,1)}, bf16[3,64,256]{2,1,0:T(8,128)(2,1)S(1)}, u32[]{:S(2)}, u32[]{:S(2)}) collective-permute-start(bf16[3,64,256]{2,1,0:T(8,128)(2,1)} %get-tuple-element.106), channel_id=1, source_target_pairs={{0,3},{1,2},{2,1},{3,0},{4,7},{5,6},{6,5},{7,4},{8,11},{9,10},{10,... | collective-permute-start | bytes 294920 | tf_op jit(solution)/shard_map/ppermute | solution.py:589
  31.1 11.9 %collective-permute-start.12 = (bf16[3,64,256]{2,1,0:T(8,128)(2,1)S(1)}, bf16[3,64,256]{2,1,0:T(8,128)(2,1)S(1)}, u32[]{:S(2)}, u32[]{:S(2)}) collective-permute-start(bf16[3,64,256]{2,1,0:T(8,128)(2,1)S(1)} %get-tuple-element.125), channel_id=1, source_target_pairs={{0,1},{1,0},{2,3},{3,2},{4,5},{5,4},{6,7},{7,6},{8,9},{9,8},{10,11... | collective-permute-start | bytes 294920 | tf_op jit(solution)/shard_map/ppermute | solution.py:589
  31.3 14.4 %collective-permute-start.13 = (bf16[3,64,256]{2,1,0:T(8,128)(2,1)S(1)}, bf16[3,64,256]{2,1,0:T(8,128)(2,1)S(1)}, u32[]{:S(2)}, u32[]{:S(2)}) collective-permute-start(bf16[3,64,256]{2,1,0:T(8,128)(2,1)S(1)} %get-tuple-element.126), channel_id=1, source_target_pairs={{0,2},{1,3},{2,0},{3,1},{4,6},{5,7},{6,4},{7,5},{8,10},{9,11},{10,... | collective-permute-start | bytes 294920 | tf_op jit(solution)/shard_map/ppermute | solution.py:589
  32.9 12.8 %collective-permute-start.14 = (bf16[3,64,256]{2,1,0:T(8,128)(2,1)S(1)}, bf16[3,64,256]{2,1,0:T(8,128)(2,1)S(1)}, u32[]{:S(2)}, u32[]{:S(2)}) collective-permute-start(bf16[3,64,256]{2,1,0:T(8,128)(2,1)S(1)} %get-tuple-element.127), channel_id=1, source_target_pairs={{0,3},{1,2},{2,1},{3,0},{4,7},{5,6},{6,5},{7,4},{8,11},{9,10},{10,... | collective-permute-start | bytes 294920 | tf_op jit(solution)/shard_map/ppermute | solution.py:589
  41.1 7.4 %collective-permute-start.3 = (bf16[3,64,256]{2,1,0:T(8,128)(2,1)S(1)}, bf16[3,64,256]{2,1,0:T(8,128)(2,1)S(1)}, u32[]{:S(2)}, u32[]{:S(2)}) collective-permute-start(bf16[3,64,256]{2,1,0:T(8,128)(2,1)S(1)} %get-tuple-element.113), channel_id=1, source_target_pairs={{0,1},{1,0},{2,3},{3,2},{4,5},{5,4},{6,7},{7,6},{8,9},{9,8},{10,11... | collective-permute-start | bytes 294920 | tf_op jit(solution)/shard_map/ppermute | solution.py:589
  41.3 10.6 %collective-permute-start.4 = (bf16[3,64,256]{2,1,0:T(8,128)(2,1)S(1)}, bf16[3,64,256]{2,1,0:T(8,128)(2,1)S(1)}, u32[]{:S(2)}, u32[]{:S(2)}) collective-permute-start(bf16[3,64,256]{2,1,0:T(8,128)(2,1)S(1)} %get-tuple-element.114), channel_id=1, source_target_pairs={{0,2},{1,3},{2,0},{3,1},{4,6},{5,7},{6,4},{7,5},{8,10},{9,11},{10,... | collective-permute-start | bytes 294920 | tf_op jit(solution)/shard_map/ppermute | solution.py:589
  43.0 9.2 %collective-permute-start.5 = (bf16[3,64,256]{2,1,0:T(8,128)(2,1)S(1)}, bf16[3,64,256]{2,1,0:T(8,128)(2,1)S(1)}, u32[]{:S(2)}, u32[]{:S(2)}) collective-permute-start(bf16[3,64,256]{2,1,0:T(8,128)(2,1)S(1)} %get-tuple-element.115), channel_id=1, source_target_pairs={{0,3},{1,2},{2,1},{3,0},{4,7},{5,6},{6,5},{7,4},{8,11},{9,10},{10,... | collective-permute-start | bytes 294920 | tf_op jit(solution)/shard_map/ppermute | solution.py:589
  46.7 13.9 %collective-permute-start.15 = (bf16[3,64,256]{2,1,0:T(8,128)(2,1)S(1)}, bf16[3,64,256]{2,1,0:T(8,128)(2,1)S(1)}, u32[]{:S(2)}, u32[]{:S(2)}) collective-permute-start(bf16[3,64,256]{2,1,0:T(8,128)(2,1)S(1)} %get-tuple-element.131.refs_2_.refs_0_.res_ref), channel_id=1, source_target_pairs={{0,1},{1,0},{2,3},{3,2},{4,5},{5,4},{6,7},{7,6},{8,9},{9,8},{10,11... | collective-permute-start | bytes 294920 | tf_op jit(solution)/shard_map/ppermute | solution.py:589
  46.8 15.8 %collective-permute-start.16 = (bf16[3,64,256]{2,1,0:T(8,128)(2,1)S(1)}, bf16[3,64,256]{2,1,0:T(8,128)(2,1)S(1)}, u32[]{:S(2)}, u32[]{:S(2)}) collective-permute-start(bf16[3,64,256]{2,1,0:T(8,128)(2,1)S(1)} %get-tuple-element.131.refs_2_.refs_0_.res_ref), channel_id=1, source_target_pairs={{0,2},{1,3},{2,0},{3,1},{4,6},{5,7},{6,4},{7,5},{8,10},{9,11},{10,... | collective-permute-start | bytes 294920 | tf_op jit(solution)/shard_map/ppermute | solution.py:589
  48.5 14.2 %collective-permute-start.17 = (bf16[3,64,256]{2,1,0:T(8,128)(2,1)S(1)}, bf16[3,64,256]{2,1,0:T(8,128)(2,1)S(1)}, u32[]{:S(2)}, u32[]{:S(2)}) collective-permute-start(bf16[3,64,256]{2,1,0:T(8,128)(2,1)S(1)} %get-tuple-element.131.refs_2_.refs_0_.res_ref), channel_id=1, source_target_pairs={{0,3},{1,2},{2,1},{3,0},{4,7},{5,6},{6,5},{7,4},{8,11},{9,10},{10,... | collective-permute-start | bytes 294920 | tf_op jit(solution)/shard_map/ppermute | solution.py:589
  53.2 13.8 %collective-permute-start.6 = (bf16[3,64,256]{2,1,0:T(8,128)(2,1)S(1)}, bf16[3,64,256]{2,1,0:T(8,128)(2,1)S(1)}, u32[]{:S(2)}, u32[]{:S(2)}) collective-permute-start(bf16[3,64,256]{2,1,0:T(8,128)(2,1)S(1)} %get-tuple-element.116.refs_3_.refs_0_.res_ref), channel_id=1, source_target_pairs={{0,1},{1,0},{2,3},{3,2},{4,5},{5,4},{6,7},{7,6},{8,9},{9,8},{10,11... | collective-permute-start | bytes 294920 | tf_op jit(solution)/shard_map/ppermute | solution.py:589
  59.7 9.4 %collective-permute-start.7 = (bf16[3,64,256]{2,1,0:T(8,128)(2,1)S(1)}, bf16[3,64,256]{2,1,0:T(8,128)(2,1)S(1)}, u32[]{:S(2)}, u32[]{:S(2)}) collective-permute-start(bf16[3,64,256]{2,1,0:T(8,128)(2,1)S(1)} %get-tuple-element.116.refs_3_.refs_0_.res_ref), channel_id=1, source_target_pairs={{0,2},{1,3},{2,0},{3,1},{4,6},{5,7},{6,4},{7,5},{8,10},{9,11},{10,... | collective-permute-start | bytes 294920 | tf_op jit(solution)/shard_map/ppermute | solution.py:589
  60.6 8.4 %collective-permute-start.8 = (bf16[3,64,256]{2,1,0:T(8,128)(2,1)S(1)}, bf16[3,64,256]{2,1,0:T(8,128)(2,1)S(1)}, u32[]{:S(2)}, u32[]{:S(2)}) collective-permute-start(bf16[3,64,256]{2,1,0:T(8,128)(2,1)S(1)} %get-tuple-element.116.refs_3_.refs_0_.res_ref), channel_id=1, source_target_pairs={{0,3},{1,2},{2,1},{3,0},{4,7},{5,6},{6,5},{7,4},{8,11},{9,10},{10,... | collective-permute-start | bytes 294920 | tf_op jit(solution)/shard_map/ppermute | solution.py:589
  74.2 4.8 %collective-permute-start.22 = (bf16[3,64,256]{2,1,0:T(8,128)(2,1)}, bf16[3,64,256]{2,1,0:T(8,128)(2,1)S(1)}, u32[]{:S(2)}, u32[]{:S(2)}) collective-permute-start(bf16[3,64,256]{2,1,0:T(8,128)(2,1)} %get-tuple-element.150), channel_id=1, source_target_pairs={{0,1},{1,0},{2,3},{3,2},{4,5},{5,4},{6,7},{7,6},{8,9},{9,8},{10,11... | collective-permute-start | bytes 294920 | tf_op jit(solution)/shard_map/ppermute | solution.py:589
  75.8 34.4 %collective-permute-start.18 = (bf16[4,320,384]{2,1,0:T(8,128)(2,1)}, bf16[4,320,384]{2,1,0:T(8,128)(2,1)}, u32[]{:S(2)}, u32[]{:S(2)}) collective-permute-start(bf16[4,320,384]{2,1,0:T(8,128)(2,1)} %get-tuple-element.142), channel_id=1, source_target_pairs={{0,4},{4,0},{8,12},{12,8},{16,20},{20,16},{24,28},{28,24},{1,5},{5... | collective-permute-start | bytes 2949128 | tf_op jit(solution)/shard_map/ppermute | solution.py:583
  83.6 26.6 %all-to-all-start = ((bf16[8,256,256]{2,1,0:T(8,128)(2,1)}), bf16[8,256,256]{2,1,0:T(8,128)(2,1)S(1)}, u32[]{:S(2)}, u32[]{:S(2)}) async-start(bf16[8,256,256]{2,1,0:T(8,128)(2,1)} %packed.1), calls=%async_computation | async-start | bytes 2097152 | tf_op jit(solution)/shard_map/all_to_all | solution.py:875
  87.5 11.2 %collective-permute-start.23 = (bf16[3,64,256]{2,1,0:T(8,128)(2,1)}, bf16[3,64,256]{2,1,0:T(8,128)(2,1)S(1)}, u32[]{:S(2)}, u32[]{:S(2)}) collective-permute-start(bf16[3,64,256]{2,1,0:T(8,128)(2,1)} %get-tuple-element.151), channel_id=1, source_target_pairs={{0,2},{1,3},{2,0},{3,1},{4,6},{5,7},{6,4},{7,5},{8,10},{9,11},{10,... | collective-permute-start | bytes 294920 | tf_op jit(solution)/shard_map/ppermute | solution.py:589
  90.1 10.6 %collective-permute-start.24 = (bf16[3,64,256]{2,1,0:T(8,128)(2,1)}, bf16[3,64,256]{2,1,0:T(8,128)(2,1)S(1)}, u32[]{:S(2)}, u32[]{:S(2)}) collective-permute-start(bf16[3,64,256]{2,1,0:T(8,128)(2,1)} %get-tuple-element.152), channel_id=1, source_target_pairs={{0,3},{1,2},{2,1},{3,0},{4,7},{5,6},{6,5},{7,4},{8,11},{9,10},{10,... | collective-permute-start | bytes 294920 | tf_op jit(solution)/shard_map/ppermute | solution.py:589
  91.5 10.8 %collective-permute-start.19 = (bf16[3,64,256]{2,1,0:T(8,128)(2,1)}, bf16[3,64,256]{2,1,0:T(8,128)(2,1)S(1)}, u32[]{:S(2)}, u32[]{:S(2)}) collective-permute-start(bf16[3,64,256]{2,1,0:T(8,128)(2,1)} %get-tuple-element.145), channel_id=1, source_target_pairs={{0,1},{1,0},{2,3},{3,2},{4,5},{5,4},{6,7},{7,6},{8,9},{9,8},{10,11... | collective-permute-start | bytes 294920 | tf_op jit(solution)/shard_map/ppermute | solution.py:589
  91.5 15.4 %collective-permute-start.20 = (bf16[3,64,256]{2,1,0:T(8,128)(2,1)}, bf16[3,64,256]{2,1,0:T(8,128)(2,1)S(1)}, u32[]{:S(2)}, u32[]{:S(2)}) collective-permute-start(bf16[3,64,256]{2,1,0:T(8,128)(2,1)} %copy-done.34), channel_id=1, source_target_pairs={{0,2},{1,3},{2,0},{3,1},{4,6},{5,7},{6,4},{7,5},{8,10},{9,11},{10,... | collective-permute-start | bytes 294920 | tf_op jit(solution)/shard_map/ppermute | solution.py:589
  98.7 8.2 %collective-permute-start.21 = (bf16[3,64,256]{2,1,0:T(8,128)(2,1)}, bf16[3,64,256]{2,1,0:T(8,128)(2,1)S(1)}, u32[]{:S(2)}, u32[]{:S(2)}) collective-permute-start(bf16[3,64,256]{2,1,0:T(8,128)(2,1)} %copy-done.33), channel_id=1, source_target_pairs={{0,3},{1,2},{2,1},{3,0},{4,7},{5,6},{6,5},{7,4},{8,11},{9,10},{10,... | collective-permute-start | bytes 294920 | tf_op jit(solution)/shard_map/ppermute | solution.py:589
  102.2 7.0 %collective-permute-start.26 = (bf16[192,1024]{1,0:T(8,128)(2,1)S(1)}, bf16[192,1024]{1,0:T(8,128)(2,1)S(1)}, u32[]{:S(2)}, u32[]{:S(2)}) collective-permute-start(bf16[192,1024]{1,0:T(8,128)(2,1)S(1)} %get-tuple-element.161.refs_3_), channel_id=1, source_target_pairs={{0,4},{4,0},{8,12},{12,8},{16,20},{20,16},{24,28},{28,24},{1,5},{5... | collective-permute-start | bytes 1179656 | tf_op jit(solution)/shard_map/ppermute | solution.py:583
  108.4 1.8 %collective-permute-start.25 = (bf16[192,1024]{1,0:T(8,128)(2,1)S(1)}, bf16[192,1024]{1,0:T(8,128)(2,1)S(1)}, u32[]{:S(2)}, u32[]{:S(2)}) collective-permute-start(bf16[192,1024]{1,0:T(8,128)(2,1)S(1)} %get-tuple-element.160.refs_2_), channel_id=1, source_target_pairs={{0,4},{4,0},{8,12},{12,8},{16,20},{20,16},{24,28},{28,24},{1,5},{5... | collective-permute-start | bytes 1179656 | tf_op jit(solution)/shard_map/ppermute | solution.py:583
  118.5 17.2 %collective-permute-start.29 = (bf16[2,320,512]{2,1,0:T(8,128)(2,1)S(1)}, bf16[2,320,512]{2,1,0:T(8,128)(2,1)S(1)}, u32[]{:S(2)}, u32[]{:S(2)}) collective-permute-start(bf16[2,320,512]{2,1,0:T(8,128)(2,1)S(1)} %get-tuple-element.181), channel_id=1, source_target_pairs={{0,16},{4,20},{8,24},{12,28},{16,0},{20,4},{24,8},{28,12},{1,17},{... | collective-permute-start | bytes 1966088 | tf_op jit(solution)/shard_map/ppermute | solution.py:583
  120.6 17.2 %collective-permute-start.27 = (bf16[2,320,512]{2,1,0:T(8,128)(2,1)S(1)}, bf16[2,320,512]{2,1,0:T(8,128)(2,1)S(1)}, u32[]{:S(2)}, u32[]{:S(2)}) collective-permute-start(bf16[2,320,512]{2,1,0:T(8,128)(2,1)S(1)} %get-tuple-element.179), channel_id=1, source_target_pairs={{0,8},{4,12},{8,0},{12,4},{16,24},{20,28},{24,16},{28,20},{1,9},{5... | collective-permute-start | bytes 1966088 | tf_op jit(solution)/shard_map/ppermute | solution.py:583
  127.5 12.1 %collective-permute-start.31 = (bf16[224,256]{1,0:T(8,128)(2,1)S(1)}, bf16[224,256]{1,0:T(8,128)(2,1)S(1)}, u32[]{:S(2)}, u32[]{:S(2)}) collective-permute-start(bf16[224,256]{1,0:T(8,128)(2,1)S(1)} %get-tuple-element.182.refs_0_), channel_id=1, source_target_pairs={{0,1},{1,0},{2,3},{3,2},{4,5},{5,4},{6,7},{7,6},{8,9},{9,8},{10,11... | collective-permute-start | bytes 344072 | tf_op jit(solution)/shard_map/ppermute | solution.py:589
  129.3 11.5 %collective-permute-start.32 = (bf16[224,256]{1,0:T(8,128)(2,1)S(1)}, bf16[224,256]{1,0:T(8,128)(2,1)S(1)}, u32[]{:S(2)}, u32[]{:S(2)}) collective-permute-start(bf16[224,256]{1,0:T(8,128)(2,1)S(1)} %get-tuple-element.182.refs_0_), channel_id=1, source_target_pairs={{0,2},{1,3},{2,0},{3,1},{4,6},{5,7},{6,4},{7,5},{8,10},{9,11},{10,... | collective-permute-start | bytes 344072 | tf_op jit(solution)/shard_map/ppermute | solution.py:589
  130.1 10.7 %collective-permute-start.33 = (bf16[224,256]{1,0:T(8,128)(2,1)S(1)}, bf16[224,256]{1,0:T(8,128)(2,1)S(1)}, u32[]{:S(2)}, u32[]{:S(2)}) collective-permute-start(bf16[224,256]{1,0:T(8,128)(2,1)S(1)} %get-tuple-element.182.refs_0_), channel_id=1, source_target_pairs={{0,3},{1,2},{2,1},{3,0},{4,7},{5,6},{6,5},{7,4},{8,11},{9,10},{10,... | collective-permute-start | bytes 344072 | tf_op jit(solution)/shard_map/ppermute | solution.py:589
  136.0 9.4 %collective-permute-start.30 = (bf16[1,320,512]{2,1,0:T(8,128)(2,1)S(1)}, bf16[1,320,512]{2,1,0:T(8,128)(2,1)S(1)}, u32[]{:S(2)}, u32[]{:S(2)}) collective-permute-start(bf16[1,320,512]{2,1,0:T(8,128)(2,1)S(1)} %slice.21), channel_id=1, source_target_pairs={{0,8},{4,12},{8,0},{12,4},{16,24},{20,28},{24,16},{28,20},{1,9},{5... | collective-permute-start | bytes 983048 | tf_op jit(solution)/shard_map/ppermute | solution.py:583
  138.0 8.9 %collective-permute-start.28 = (bf16[1,320,512]{2,1,0:T(8,128)(2,1)S(1)}, bf16[1,320,512]{2,1,0:T(8,128)(2,1)S(1)}, u32[]{:S(2)}, u32[]{:S(2)}) collective-permute-start(bf16[1,320,512]{2,1,0:T(8,128)(2,1)S(1)} %slice_bitcast_fusion), channel_id=1, source_target_pairs={{0,16},{4,20},{8,24},{12,28},{16,0},{20,4},{24,8},{28,12},{1,17},{... | collective-permute-start | bytes 983048 | tf_op jit(solution)/shard_map/ppermute | solution.py:583
  147.1 8.1 %collective-permute-start.34 = (bf16[2,80,1024]{2,1,0:T(8,128)(2,1)S(1)}, bf16[2,80,1024]{2,1,0:T(8,128)(2,1)S(1)}, u32[]{:S(2)}, u32[]{:S(2)}) collective-permute-start(bf16[2,80,1024]{2,1,0:T(8,128)(2,1)S(1)} %dynamic-slice_bitcast_fusion), channel_id=1, source_target_pairs={{0,1},{1,0},{2,3},{3,2},{4,5},{5,4},{6,7},{7,6},{8,9},{9,8},{10,11... | collective-permute-start | bytes 983048 | tf_op jit(solution)/shard_map/ppermute | solution.py:623
  149.1 8.8 %collective-permute-start.36 = (bf16[448,256]{1,0:T(8,128)(2,1)S(1)}, bf16[448,256]{1,0:T(8,128)(2,1)S(1)}, u32[]{:S(2)}, u32[]{:S(2)}) collective-permute-start(bf16[448,256]{1,0:T(8,128)(2,1)S(1)} %shard_sums.1.refs_0_), channel_id=1, source_target_pairs={{0,8},{4,12},{8,0},{12,4},{16,24},{20,28},{24,16},{28,20},{1,9},{5... | collective-permute-start | bytes 688136 | tf_op jit(solution)/shard_map/ppermute | solution.py:629
  149.9 8.9 %collective-permute-start.37 = (bf16[448,256]{1,0:T(8,128)(2,1)S(1)}, bf16[448,256]{1,0:T(8,128)(2,1)S(1)}, u32[]{:S(2)}, u32[]{:S(2)}) collective-permute-start(bf16[448,256]{1,0:T(8,128)(2,1)S(1)} %shard_sums.1.refs_0_), channel_id=1, source_target_pairs={{0,16},{4,20},{8,24},{12,28},{16,0},{20,4},{24,8},{28,12},{1,17},{... | collective-permute-start | bytes 688136 | tf_op jit(solution)/shard_map/ppermute | solution.py:629
  151.1 9.3 %collective-permute-start.38 = (bf16[448,256]{1,0:T(8,128)(2,1)S(1)}, bf16[448,256]{1,0:T(8,128)(2,1)S(1)}, u32[]{:S(2)}, u32[]{:S(2)}) collective-permute-start(bf16[448,256]{1,0:T(8,128)(2,1)S(1)} %shard_sums.1.refs_0_), channel_id=1, source_target_pairs={{0,24},{4,28},{8,16},{12,20},{16,8},{20,12},{24,0},{28,4},{1,25},{... | collective-permute-start | bytes 688136 | tf_op jit(solution)/shard_map/ppermute | solution.py:629
  155.3 8.1 %collective-permute-start.35 = (bf16[1,80,1024]{2,1,0:T(8,128)(2,1)S(1)}, bf16[1,80,1024]{2,1,0:T(8,128)(2,1)S(1)}, u32[]{:S(2)}, u32[]{:S(2)}) collective-permute-start(bf16[1,80,1024]{2,1,0:T(8,128)(2,1)S(1)} %constant_dynamic-slice_fusion), channel_id=1, source_target_pairs={{0,2},{1,3},{2,0},{3,1},{4,6},{5,7},{6,4},{7,5},{8,10},{9,11},{10,... | collective-permute-start | bytes 491528 | tf_op jit(solution)/shard_map/ppermute | solution.py:623
  160.4 3.8 %collective-permute-start.39 = (bf16[448,256]{1,0:T(8,128)(2,1)S(1)}, bf16[448,256]{1,0:T(8,128)(2,1)S(1)}, u32[]{:S(2)}, u32[]{:S(2)}) collective-permute-start(bf16[448,256]{1,0:T(8,128)(2,1)S(1)} %shard_sums.1.refs_0_), channel_id=1, source_target_pairs={{0,4},{4,0},{8,12},{12,8},{16,20},{20,16},{24,28},{28,24},{1,5},{5... | collective-permute-start | bytes 688136 | tf_op jit(solution)/shard_map/ppermute | solution.py:583
  160.4 3.8 %collective-permute-start.40 = (bf16[448,256]{1,0:T(8,128)(2,1)S(1)}, bf16[448,256]{1,0:T(8,128)(2,1)S(1)}, u32[]{:S(2)}, u32[]{:S(2)}) collective-permute-start(bf16[448,256]{1,0:T(8,128)(2,1)S(1)} %collective-permute-done.36.refs_2_), channel_id=1, source_target_pairs={{0,4},{4,0},{8,12},{12,8},{16,20},{20,16},{24,28},{28,24},{1,5},{5... | collective-permute-start | bytes 688136 | tf_op jit(solution)/shard_map/ppermute | solution.py:583
  160.9 3.3 %collective-permute-start.41 = (bf16[448,256]{1,0:T(8,128)(2,1)S(1)}, bf16[448,256]{1,0:T(8,128)(2,1)S(1)}, u32[]{:S(2)}, u32[]{:S(2)}) collective-permute-start(bf16[448,256]{1,0:T(8,128)(2,1)S(1)} %collective-permute-done.37.refs_4_), channel_id=1, source_target_pairs={{0,4},{4,0},{8,12},{12,8},{16,20},{20,16},{24,28},{28,24},{1,5},{5... | collective-permute-start | bytes 688136 | tf_op jit(solution)/shard_map/ppermute | solution.py:583
  160.9 3.3 %collective-permute-start.42 = (bf16[448,256]{1,0:T(8,128)(2,1)S(1)}, bf16[448,256]{1,0:T(8,128)(2,1)S(1)}, u32[]{:S(2)}, u32[]{:S(2)}) collective-permute-start(bf16[448,256]{1,0:T(8,128)(2,1)S(1)} %collective-permute-done.38.refs_6_), channel_id=1, source_target_pairs={{0,4},{4,0},{8,12},{12,8},{16,20},{20,16},{24,28},{28,24},{1,5},{5... | collective-permute-start | bytes 688136 | tf_op jit(solution)/shard_map/ppermute | solution.py:583
  (41 other events, 232.6 us)

commit v10 on v8

--- a/solution.py
+++ b/solution.py
@@ -883,7 +883,6 @@
         other_grads.append(swap_bit(grad, 0, groups))
         row_sums.append(row_sum)
     grads = own_grads + other_grads
-    grads, weight_sums = lax.optimization_barrier((grads, weight_sums))
     sent = embed_grad_parts(scal, turned, grads, groups, 1)
     sent, kept_turned = lax.optimization_barrier((sent, turned))
     top_bit = groups.bit_length() - 2

time: 168 us -> 165 us (0.982)
  local copies, waits for them, and re-layouts: 17.1 us -> 1.89 us
  waiting for transfers between devices: 29.6 us -> 44.4 us
  starting transfers between devices: 71.8 us -> 68.6 us
    unnamed x98 -> x32, local copies, waits for them, and re-layouts: 15 us -> 0.95 us
    ppermute x27, waiting for transfers between devices: 12 us -> 18.3 us  [across(): lax.ppermute(pieces[k], 'fft', [(z, z ^ k) for z in range(shards)])]
    ppermute x11, waiting for transfers between devices: 10.8 us -> 15.4 us  [swap_bit(): lax.ppermute(values, 'grp', [(g, g ^ 1 << bit) for g in range(groups)])]
    all_to_all x1, waiting for transfers between devices: 0.01 us -> 2.34 us  [on_device(): lax.all_to_all(packed(routes, head_grad, spec_grad, predicted, groups), '...]
    pallas_call x2, Pallas kernels: 8.18 us -> 10.1 us  [embed_grad_parts(): pl.pallas_call(body, grid_spec=pltpu.PrefetchScalarGridSpec(num_scalar_pr...]
  transfers between devices with their start and end apart: 44 -> 44, of which waited for: 13 -> 13; matrix products, arithmetic and copies ran while one was open for 2% -> 3% of each run, Pallas kernels for 16% -> 17%
where the time goes in v10:
time: 165 us; the launch traced here: 164 us
  starting transfers between devices  68.6 us (42%)
  waiting for transfers between devices  44.4 us (27%)
  Pallas kernels  43.8 us (27%)
  other arithmetic  4.84 us (3%)
  local copies, waits for them, and re-layouts  1.89 us (1%)
    ppermute x27, starting transfers between devices, across(): lax.ppermute(pieces[k], 'fft', [(z, z ^ k) for z in range(shards)])  49.6 us
    ppermute x27, waiting for transfers between devices, across(): lax.ppermute(pieces[k], 'fft', [(z, z ^ k) for z in range(shards)])  18.3 us
    ppermute x11, waiting for transfers between devices, swap_bit(): lax.ppermute(values, 'grp', [(g, g ^ 1 << bit) for g in range(groups)])  15.4 us
    pallas_call x2, Pallas kernels, embed_grad_parts(): pl.pallas_call(body, grid_spec=pltpu.PrefetchScalarGridSpec(num_scalar_pr...  10.1 us
    pallas_call x1, Pallas kernels, embed(): pl.pallas_call(body, grid_spec=pltpu.PrefetchScalarGridSpec(num_scalar_pr...  10 us
    ppermute x11, starting transfers between devices, swap_bit(): lax.ppermute(values, 'grp', [(g, g ^ 1 << bit) for g in range(groups)])  7.03 us
    ppermute x2, waiting for transfers between devices, scatter_step(): received = lax.ppermute(send, 'fft', [(z, z ^ bit) for z in range(shards)])  6.82 us
    pallas_call x2, Pallas kernels, spectral_back_chunk(): pl.pallas_call(body, grid_spec=pltpu.PrefetchScalarGridSpec(num_scalar_pr...  6.05 us
  transfers between devices with their start and end apart: 44, of which 13 were waited for; matrix products, arithmetic and copies ran while one was open for 3% of the time, Pallas kernels for 17%

profile of v10, /device:TPU:0, one launch (start us, length us, event | category | flops | bytes accessed | tf_op | source)
XLA Modules:
  0.0 164.5 jit_solution(8323350611040184931)
XLA Ops:
  2.0 10.0 %embed.1 = (bf16[384,1024]{1,0:T(8,128)(2,1)}, bf16[384,1024]{1,0:T(8,128)(2,1)}, f32[384,256]{1,0:T(8,128)}, bf16[4,320,384]{2,1,0:T(8,128)(2,1)}, bf16[4,320,3...) custom-call(s32[15]{0:T(128)} %concatenate.12.scal_ref, ...), custom_call_target="tpu_custom_call" | custom-call | flops 2013265920 | bytes 7208960 | tf_op jit(solution)/shard_map/embed/pallas_call | solution.py:157
  12.0 4.1 %collective-permute-start.10 = (bf16[3,64,256]{2,1,0:T(8,128)(2,1)}, bf16[3,64,256]{2,1,0:T(8,128)(2,1)S(1)}, u32[]{:S(2)}, u32[]{:S(2)}) collective-permute-start(bf16[3,64,256]{2,1,0:T(8,128)(2,1)} %get-tuple-element.115), channel_id=1, source_target_pairs={{0,2},{1,3},{2,0},{3,1},{4,6},{5,7},{6,4},{7,5},{8,10},{9,11},{10,... | collective-permute-start | bytes 294920 | tf_op jit(solution)/shard_map/ppermute | solution.py:589
  17.7 1.8 %collective-permute-start = (bf16[3,64,256]{2,1,0:T(8,128)(2,1)}, bf16[3,64,256]{2,1,0:T(8,128)(2,1)S(1)}, u32[]{:S(2)}, u32[]{:S(2)}) collective-permute-start(bf16[3,64,256]{2,1,0:T(8,128)(2,1)} %get-tuple-element.100), channel_id=1, source_target_pairs={{0,1},{1,0},{2,3},{3,2},{4,5},{5,4},{6,7},{7,6},{8,9},{9,8},{10,11... | collective-permute-start | bytes 294920 | tf_op jit(solution)/shard_map/ppermute | solution.py:589
  19.5 1.7 %collective-permute-start.1 = (bf16[3,64,256]{2,1,0:T(8,128)(2,1)}, bf16[3,64,256]{2,1,0:T(8,128)(2,1)S(1)}, u32[]{:S(2)}, u32[]{:S(2)}) collective-permute-start(bf16[3,64,256]{2,1,0:T(8,128)(2,1)} %get-tuple-element.101), channel_id=1, source_target_pairs={{0,2},{1,3},{2,0},{3,1},{4,6},{5,7},{6,4},{7,5},{8,10},{9,11},{10,... | collective-permute-start | bytes 294920 | tf_op jit(solution)/shard_map/ppermute | solution.py:589
  21.2 3.0 %collective-permute-done.10.refs_2_ = bf16[3,64,256]{2,1,0:T(8,128)(2,1)S(1)} collective-permute-done((bf16[3,64,256]{2,1,0:T(8,128)(2,1)}, bf16[3,64,256]{2,1,0:T(8,128)(2,1)S(1)}, u32[]{:S(2)}, u32[]{:S(2)}) %collective-permute-start.10) | collective-permute-done | bytes 98336 | tf_op jit(solution)/shard_map/ppermute | solution.py:589
  24.2 2.8 %collective-permute-start.2 = (bf16[3,64,256]{2,1,0:T(8,128)(2,1)}, bf16[3,64,256]{2,1,0:T(8,128)(2,1)S(1)}, u32[]{:S(2)}, u32[]{:S(2)}) collective-permute-start(bf16[3,64,256]{2,1,0:T(8,128)(2,1)} %get-tuple-element.102), channel_id=1, source_target_pairs={{0,3},{1,2},{2,1},{3,0},{4,7},{5,6},{6,5},{7,4},{8,11},{9,10},{10,... | collective-permute-start | bytes 294920 | tf_op jit(solution)/shard_map/ppermute | solution.py:589
  27.9 2.3 %spectral.3 = (bf16[3,64,256]{2,1,0:T(8,128)(2,1)S(1)}, bf16[3,64,256]{2,1,0:T(8,128)(2,1)S(1)}, bf16[3,64,256]{2,1,0:T(8,128)(2,1)S(1)}, bf16[3,64,256]{2,1,0:T...) custom-call(s32[15]{0:T(128)S(1)} %copy-done.7, ...), custom_call_target="tpu_custom_call" | custom-call | flops 704643072 | bytes 3145728 | tf_op jit(solution)/shard_map/spectral/pallas_call | solution.py:277
  31.3 1.6 collective-permute-start.13
  32.8 1.9 %collective-permute-start.14 = (bf16[3,64,256]{2,1,0:T(8,128)(2,1)S(1)}, bf16[3,64,256]{2,1,0:T(8,128)(2,1)S(1)}, u32[]{:S(2)}, u32[]{:S(2)}) collective-permute-start(bf16[3,64,256]{2,1,0:T(8,128)(2,1)S(1)} %get-tuple-element.123), channel_id=1, source_target_pairs={{0,3},{1,2},{2,1},{3,0},{4,7},{5,6},{6,5},{7,4},{8,11},{9,10},{10,... | collective-permute-start | bytes 294920 | tf_op jit(solution)/shard_map/ppermute | solution.py:589
  34.8 2.3 %spectral.2 = (bf16[3,64,256]{2,1,0:T(8,128)(2,1)S(1)}, bf16[3,64,256]{2,1,0:T(8,128)(2,1)S(1)}, bf16[3,64,256]{2,1,0:T(8,128)(2,1)S(1)}, bf16[3,64,256]{2,1,0:T...) custom-call(s32[15]{0:T(128)S(1)} %copy-done.7, ...), custom_call_target="tpu_custom_call" | custom-call | flops 704643072 | bytes 3145728 | tf_op jit(solution)/shard_map/spectral/pallas_call | solution.py:277
  37.5 2.2 %collective-permute-start.4 = (bf16[3,64,256]{2,1,0:T(8,128)(2,1)S(1)}, bf16[3,64,256]{2,1,0:T(8,128)(2,1)S(1)}, u32[]{:S(2)}, u32[]{:S(2)}) collective-permute-start(bf16[3,64,256]{2,1,0:T(8,128)(2,1)S(1)} %get-tuple-element.110), channel_id=1, source_target_pairs={{0,2},{1,3},{2,0},{3,1},{4,6},{5,7},{6,4},{7,5},{8,10},{9,11},{10,... | collective-permute-start | bytes 294920 | tf_op jit(solution)/shard_map/ppermute | solution.py:589
  39.7 1.8 %collective-permute-start.5 = (bf16[3,64,256]{2,1,0:T(8,128)(2,1)S(1)}, bf16[3,64,256]{2,1,0:T(8,128)(2,1)S(1)}, u32[]{:S(2)}, u32[]{:S(2)}) collective-permute-start(bf16[3,64,256]{2,1,0:T(8,128)(2,1)S(1)} %get-tuple-element.111), channel_id=1, source_target_pairs={{0,3},{1,2},{2,1},{3,0},{4,7},{5,6},{6,5},{7,4},{8,11},{9,10},{10,... | collective-permute-start | bytes 294920 | tf_op jit(solution)/shard_map/ppermute | solution.py:589
  42.8 6.9 %collective-permute-start.15 = (bf16[3,64,256]{2,1,0:T(8,128)(2,1)S(1)}, bf16[3,64,256]{2,1,0:T(8,128)(2,1)S(1)}, u32[]{:S(2)}, u32[]{:S(2)}) collective-permute-start(bf16[3,64,256]{2,1,0:T(8,128)(2,1)S(1)} %get-tuple-element.127.refs_2_.refs_0_.res_ref), channel_id=1, source_target_pairs={{0,1},{1,0},{2,3},{3,2},{4,5},{5,4},{6,7},{7,6},{8,9},{9,8},{10,11... | collective-permute-start | bytes 294920 | tf_op jit(solution)/shard_map/ppermute | solution.py:589
  50.7 1.5 collective-permute-start.17
  54.2 1.8 %collective-permute-start.7 = (bf16[3,64,256]{2,1,0:T(8,128)(2,1)S(1)}, bf16[3,64,256]{2,1,0:T(8,128)(2,1)S(1)}, u32[]{:S(2)}, u32[]{:S(2)}) collective-permute-start(bf16[3,64,256]{2,1,0:T(8,128)(2,1)S(1)} %get-tuple-element.112.refs_3_.refs_0_.res_ref), channel_id=1, source_target_pairs={{0,2},{1,3},{2,0},{3,1},{4,6},{5,7},{6,4},{7,5},{8,10},{9,11},{10,... | collective-permute-start | bytes 294920 | tf_op jit(solution)/shard_map/ppermute | solution.py:589
  56.0 1.5 collective-permute-start.8
  58.1 2.4 %collective-permute-done.16.refs_2_ = bf16[3,64,256]{2,1,0:T(8,128)(2,1)S(1)} collective-permute-done((bf16[3,64,256]{2,1,0:T(8,128)(2,1)S(1)}, bf16[3,64,256]{2,1,0:T(8,128)(2,1)S(1)}, u32[]{:S(2)}, u32[]{:S(2)}) %collective-permute-start.16) | collective-permute-done | bytes 98336 | tf_op jit(solution)/shard_map/ppermute | solution.py:589
  60.5 3.0 %spectral_back.2 = (bf16[3,64,256]{2,1,0:T(8,128)(2,1)S(1)}, bf16[3,64,256]{2,1,0:T(8,128)(2,1)S(1)}, bf16[3,64,256]{2,1,0:T(8,128)(2,1)S(1)}, bf16[3,64,256]{2,...) custom-call(s32[15]{0:T(128)S(1)} %copy-done.7, bf16[3,512,256]{2,1,0:T(8,128)(2,1)S(1)} %copy-done.4, ...), custom_call_target="tpu_custom_call" | custom-call | flops 1006632960 | bytes 3145728 | tf_op jit(solution)/shard_map/spectral_back/pallas_call | solution.py:440
  63.5 4.3 %collective-permute-done.7.refs_2_ = bf16[3,64,256]{2,1,0:T(8,128)(2,1)S(1)} collective-permute-done((bf16[3,64,256]{2,1,0:T(8,128)(2,1)S(1)}, bf16[3,64,256]{2,1,0:T(8,128)(2,1)S(1)}, u32[]{:S(2)}, u32[]{:S(2)}) %collective-permute-start.7) | collective-permute-done | bytes 98336 | tf_op jit(solution)/shard_map/ppermute | solution.py:589
  67.8 3.1 %spectral_back.3 = (bf16[3,64,256]{2,1,0:T(8,128)(2,1)S(1)}, bf16[3,64,256]{2,1,0:T(8,128)(2,1)S(1)}, bf16[3,64,256]{2,1,0:T(8,128)(2,1)S(1)}, bf16[3,64,256]{2,...) custom-call(s32[15]{0:T(128)S(1)} %copy-done.7, bf16[3,512,256]{2,1,0:T(8,128)(2,1)S(1)} %copy-done.4, ...), custom_call_target="tpu_custom_call" | custom-call | flops 1006632960 | bytes 3145728 | tf_op jit(solution)/shard_map/spectral_back/pallas_call | solution.py:440
  70.9 1.8 %collective-permute-start.19 = (bf16[3,64,256]{2,1,0:T(8,128)(2,1)S(1)}, bf16[3,64,256]{2,1,0:T(8,128)(2,1)S(1)}, u32[]{:S(2)}, u32[]{:S(2)}) collective-permute-start(bf16[3,64,256]{2,1,0:T(8,128)(2,1)S(1)} %get-tuple-element.141), channel_id=1, source_target_pairs={{0,1},{1,0},{2,3},{3,2},{4,5},{5,4},{6,7},{7,6},{8,9},{9,8},{10,11... | collective-permute-start | bytes 294920 | tf_op jit(solution)/shard_map/ppermute | solution.py:589
  73.7 1.7 %collective-permute-start.21 = (bf16[3,64,256]{2,1,0:T(8,128)(2,1)S(1)}, bf16[3,64,256]{2,1,0:T(8,128)(2,1)S(1)}, u32[]{:S(2)}, u32[]{:S(2)}) collective-permute-start(bf16[3,64,256]{2,1,0:T(8,128)(2,1)S(1)} %get-tuple-element.143), channel_id=1, source_target_pairs={{0,3},{1,2},{2,1},{3,0},{4,7},{5,6},{6,5},{7,4},{8,11},{9,10},{10,... | collective-permute-start | bytes 294920 | tf_op jit(solution)/shard_map/ppermute | solution.py:589
  76.3 2.9 %collective-permute-start.23 = (bf16[3,64,256]{2,1,0:T(8,128)(2,1)S(1)}, bf16[3,64,256]{2,1,0:T(8,128)(2,1)S(1)}, u32[]{:S(2)}, u32[]{:S(2)}) collective-permute-start(bf16[3,64,256]{2,1,0:T(8,128)(2,1)S(1)} %get-tuple-element.150), channel_id=1, source_target_pairs={{0,2},{1,3},{2,0},{3,1},{4,6},{5,7},{6,4},{7,5},{8,10},{9,11},{10,... | collective-permute-start | bytes 294920 | tf_op jit(solution)/shard_map/ppermute | solution.py:589
  79.2 4.4 %collective-permute-done.20.refs_2_ = bf16[3,64,256]{2,1,0:T(8,128)(2,1)S(1)} collective-permute-done((bf16[3,64,256]{2,1,0:T(8,128)(2,1)S(1)}, bf16[3,64,256]{2,1,0:T(8,128)(2,1)S(1)}, u32[]{:S(2)}, u32[]{:S(2)}) %collective-permute-start.20) | collective-permute-done | bytes 98336 | tf_op jit(solution)/shard_map/ppermute | solution.py:589
  83.5 2.3 %collective-permute-start.24 = (bf16[3,64,256]{2,1,0:T(8,128)(2,1)S(1)}, bf16[3,64,256]{2,1,0:T(8,128)(2,1)S(1)}, u32[]{:S(2)}, u32[]{:S(2)}) collective-permute-start(bf16[3,64,256]{2,1,0:T(8,128)(2,1)S(1)} %get-tuple-element.151), channel_id=1, source_target_pairs={{0,3},{1,2},{2,1},{3,0},{4,7},{5,6},{6,5},{7,4},{8,11},{9,10},{10,... | collective-permute-start | bytes 294920 | tf_op jit(solution)/shard_map/ppermute | solution.py:589
  85.9 2.2 %embedded_back.2 = (bf16[192,1024]{1,0:T(8,128)(2,1)}, f32[8,1024]{1,0:T(8,128)S(1)}) custom-call(s32[15]{0:T(128)S(1)} %copy-done.7, bf16[384,1024]{1,0:T(8,128)(2,1)S(1)} %copy-done.1, f32[384,256]{1,0:T(8,128)S(1)} %copy-done.5, bf16[3,64,256]{2,1,0:T(8,128)(2,1)S(1)} %get-tuple-element.127.refs_2_.refs_0_.res_ref, bf16[1024,256]{1,0:T(8,128)(2,1)S(1)} %copy-done, ...), custom_call_target="tpu_custom_call" | custom-call | flops 100663296 | bytes 1179648 | tf_op jit(solution)/shard_map/embedded_back/pallas_call | solution.py:497
  88.1 3.8 %collective-permute-done.23.refs_2_ = bf16[3,64,256]{2,1,0:T(8,128)(2,1)S(1)} collective-permute-done((bf16[3,64,256]{2,1,0:T(8,128)(2,1)S(1)}, bf16[3,64,256]{2,1,0:T(8,128)(2,1)S(1)}, u32[]{:S(2)}, u32[]{:S(2)}) %collective-permute-start.23) | collective-permute-done | bytes 98336 | tf_op jit(solution)/shard_map/ppermute | solution.py:589
  92.0 2.4 %embedded_back.3 = (bf16[192,1024]{1,0:T(8,128)(2,1)}, f32[8,1024]{1,0:T(8,128)S(1)}) custom-call(s32[15]{0:T(128)S(1)} %copy-done.7, bf16[384,1024]{1,0:T(8,128)(2,1)S(1)} %copy-done.1, f32[384,256]{1,0:T(8,128)S(1)} %copy-done.5, bf16[3,64,256]{2,1,0:T(8,128)(2,1)S(1)} %get-tuple-element.112.refs_3_.refs_0_.res_ref, bf16[1024,256]{1,0:T(8,128)(2,1)S(1)} %copy-done, ...), custom_call_target="tpu_custom_call" | custom-call | flops 100663296 | bytes 1179648 | tf_op jit(solution)/shard_map/embedded_back/pallas_call | solution.py:497
  95.5 1.7 %packed.1 = bf16[8,256,256]{2,1,0:T(8,128)(2,1)} custom-call(s32[17]{0:T(128)S(1)} %concatenate.11.routes_ref, bf16[1024,256]{1,0:T(8,128)(2,1)S(1)} %head_gradient.1.head_ref, bf16[512,256]{1,0:T(8,128)(2,1)S(1)} %get-tuple-element.160.spec_ref, bf16[3,64,256]{2,1,0:T(8,128)(2,1)S(1)} %get-tuple-element.161.refs_0_, ...), custom_call_target="tpu_custom_call" | custom-call | tf_op jit(solution)/shard_map/packed/pallas_call | solution.py:645
  97.2 4.0 %all-to-all-start = ((bf16[8,256,256]{2,1,0:T(8,128)(2,1)}), bf16[8,256,256]{2,1,0:T(8,128)(2,1)S(1)}, u32[]{:S(2)}, u32[]{:S(2)}) async-start(bf16[8,256,256]{2,1,0:T(8,128)(2,1)} %packed.1), calls=%async_computation | async-start | bytes 2097152 | tf_op jit(solution)/shard_map/all_to_all | solution.py:879
  101.3 5.5 %embed_grad.2 = (bf16[2,320,512]{2,1,0:T(8,128)(2,1)}, bf16[2,320,512]{2,1,0:T(8,128)(2,1)}) custom-call(s32[15]{0:T(128)S(1)} %copy-done.7, bf16[4,320,384]{2,1,0:T(8,128)(2,1)S(1)} %copy-done.11, bf16[4,320,384]{2,1,0:T(8,128)(2,1)S(1)} %collective-permute-done.18.refs_1_, bf16[192,1024]{1,0:T(8,128)(2,1)} %get-tuple-element.147.refs_2_, ...), custom_call_target="tpu_custom_call" | custom-call | flops 1006632960 | bytes 4063232 | tf_op jit(solution)/shard_map/embed_grad/pallas_call | solution.py:555
  106.7 2.0 %collective-permute-start.29 = (bf16[2,320,512]{2,1,0:T(8,128)(2,1)}, bf16[2,320,512]{2,1,0:T(8,128)(2,1)}, u32[]{:S(2)}, u32[]{:S(2)}) collective-permute-start(bf16[2,320,512]{2,1,0:T(8,128)(2,1)} %get-tuple-element.173), channel_id=1, source_target_pairs={{0,16},{4,20},{8,24},{12,28},{16,0},{20,4},{24,8},{28,12},{1,17},{... | collective-permute-start | bytes 1966088 | tf_op jit(solution)/shard_map/ppermute | solution.py:583
  108.8 1.5 collective-permute-start.27
  110.2 4.6 %embed_grad.3 = (bf16[2,320,512]{2,1,0:T(8,128)(2,1)S(1)}, bf16[2,320,512]{2,1,0:T(8,128)(2,1)S(1)}) custom-call(s32[15]{0:T(128)S(1)} %copy-done.7, bf16[4,320,384]{2,1,0:T(8,128)(2,1)S(1)} %copy-done.12, bf16[4,320,384]{2,1,0:T(8,128)(2,1)S(1)} %collective-permute-done.18.refs_1_, bf16[192,1024]{1,0:T(8,128)(2,1)} %get-tuple-element.147.refs_2_, ...), custom_call_target="tpu_custom_call" | custom-call | flops 1006632960 | bytes 4063232 | tf_op jit(solution)/shard_map/embed_grad/pallas_call | solution.py:555
  114.8 2.3 %all-to-all-done.moved_ref = bf16[8,256,256]{2,1,0:T(8,128)(2,1)S(1)} async-done(((bf16[8,256,256]{2,1,0:T(8,128)(2,1)}), bf16[8,256,256]{2,1,0:T(8,128)(2,1)S(1)}, u32[]{:S(2)}, u32[]{:S(2)}) %all-to-all-start) | async-done | bytes 1048608 | tf_op jit(solution)/shard_map/all_to_all | solution.py:879
  118.4 1.9 %collective-permute-start.31 = (bf16[224,256]{1,0:T(8,128)(2,1)S(1)}, bf16[224,256]{1,0:T(8,128)(2,1)S(1)}, u32[]{:S(2)}, u32[]{:S(2)}) collective-permute-start(bf16[224,256]{1,0:T(8,128)(2,1)S(1)} %get-tuple-element.174.refs_0_), channel_id=1, source_target_pairs={{0,1},{1,0},{2,3},{3,2},{4,5},{5,4},{6,7},{7,6},{8,9},{9,8},{10,11... | collective-permute-start | bytes 344072 | tf_op jit(solution)/shard_map/ppermute | solution.py:589
  121.1 1.7 %collective-permute-start.33 = (bf16[224,256]{1,0:T(8,128)(2,1)S(1)}, bf16[224,256]{1,0:T(8,128)(2,1)S(1)}, u32[]{:S(2)}, u32[]{:S(2)}) collective-permute-start(bf16[224,256]{1,0:T(8,128)(2,1)S(1)} %get-tuple-element.174.refs_0_), channel_id=1, source_target_pairs={{0,3},{1,2},{2,1},{3,0},{4,7},{5,6},{6,5},{7,4},{8,11},{9,10},{10,... | collective-permute-start | bytes 344072 | tf_op jit(solution)/shard_map/ppermute | solution.py:589
  122.8 7.0 %collective-permute-done.29 = bf16[2,320,512]{2,1,0:T(8,128)(2,1)} collective-permute-done((bf16[2,320,512]{2,1,0:T(8,128)(2,1)}, bf16[2,320,512]{2,1,0:T(8,128)(2,1)}, u32[]{:S(2)}, u32[]{:S(2)}) %collective-permute-start.29) | collective-permute-done | bytes 655392 | tf_op jit(solution)/shard_map/ppermute | solution.py:583
  131.1 1.5 collective-permute-start.30
  135.0 5.6 %collective-permute-done.30 = bf16[1,320,512]{2,1,0:T(8,128)(2,1)S(1)} collective-permute-done((bf16[1,320,512]{2,1,0:T(8,128)(2,1)S(1)}, bf16[1,320,512]{2,1,0:T(8,128)(2,1)S(1)}, u32[]{:S(2)}, u32[]{:S(2)}) %collective-permute-start.30) | collective-permute-done | bytes 327712 | tf_op jit(solution)/shard_map/ppermute | solution.py:583
  140.7 2.7 %collective-permute-done.28 = bf16[1,320,512]{2,1,0:T(8,128)(2,1)S(1)} collective-permute-done((bf16[1,320,512]{2,1,0:T(8,128)(2,1)S(1)}, bf16[1,320,512]{2,1,0:T(8,128)(2,1)S(1)}, u32[]{:S(2)}, u32[]{:S(2)}) %collective-permute-start.28) | collective-permute-done | bytes 327712 | tf_op jit(solution)/shard_map/ppermute | solution.py:583
  143.6 2.0 %collective-permute-start.34 = (bf16[2,80,1024]{2,1,0:T(8,128)(2,1)S(1)}, bf16[2,80,1024]{2,1,0:T(8,128)(2,1)S(1)}, u32[]{:S(2)}, u32[]{:S(2)}) collective-permute-start(bf16[2,80,1024]{2,1,0:T(8,128)(2,1)S(1)} %dynamic-slice_bitcast_fusion), channel_id=1, source_target_pairs={{0,1},{1,0},{2,3},{3,2},{4,5},{5,4},{6,7},{7,6},{8,9},{9,8},{10,11... | collective-permute-start | bytes 983048 | tf_op jit(solution)/shard_map/ppermute | solution.py:623
  146.4 2.7 %collective-permute-start.38 = (bf16[448,256]{1,0:T(8,128)(2,1)S(1)}, bf16[448,256]{1,0:T(8,128)(2,1)S(1)}, u32[]{:S(2)}, u32[]{:S(2)}) collective-permute-start(bf16[448,256]{1,0:T(8,128)(2,1)S(1)} %shard_sums.1.refs_0_), channel_id=1, source_target_pairs={{0,24},{4,28},{8,16},{12,20},{16,8},{20,12},{24,0},{28,4},{1,25},{... | collective-permute-start | bytes 688136 | tf_op jit(solution)/shard_map/ppermute | solution.py:629
  149.1 3.3 %collective-permute-done.34 = bf16[2,80,1024]{2,1,0:T(8,128)(2,1)S(1)} collective-permute-done((bf16[2,80,1024]{2,1,0:T(8,128)(2,1)S(1)}, bf16[2,80,1024]{2,1,0:T(8,128)(2,1)S(1)}, u32[]{:S(2)}, u32[]{:S(2)}) %collective-permute-start.34) | collective-permute-done | bytes 327712 | tf_op jit(solution)/shard_map/ppermute | solution.py:623
  152.5 2.6 %collective-permute-start.35 = (bf16[1,80,1024]{2,1,0:T(8,128)(2,1)S(1)}, bf16[1,80,1024]{2,1,0:T(8,128)(2,1)S(1)}, u32[]{:S(2)}, u32[]{:S(2)}) collective-permute-start(bf16[1,80,1024]{2,1,0:T(8,128)(2,1)S(1)} %constant_dynamic-slice_fusion), channel_id=1, source_target_pairs={{0,2},{1,3},{2,0},{3,1},{4,6},{5,7},{6,4},{7,5},{8,10},{9,11},{10,... | collective-permute-start | bytes 491528 | tf_op jit(solution)/shard_map/ppermute | solution.py:623
  155.0 1.6 collective-permute-done.37.refs_4_
  157.7 3.5 %collective-permute-done.35 = bf16[1,80,1024]{2,1,0:T(8,128)(2,1)S(1)} collective-permute-done((bf16[1,80,1024]{2,1,0:T(8,128)(2,1)S(1)}, bf16[1,80,1024]{2,1,0:T(8,128)(2,1)S(1)}, u32[]{:S(2)}, u32[]{:S(2)}) %collective-permute-start.35) | collective-permute-done | bytes 163872 | tf_op jit(solution)/shard_map/ppermute | solution.py:623
  162.0 2.5 %assembled.1 = (f32[1024,256]{1,0:T(8,128)}, f32[2,2,8,128,128]{4,3,2,1,0:T(8,128)}, f32[2,2,8,128]{3,2,1,0:T(8,128)}, f32[1,1024]{1,0:T(1,128)}, f32[1,1024]{1,0:T(1,128)}, /*index=5*/f32[1,256]{1,0:T(1,128)}) custom-call(s32[15]{0:T(128)S(1)} %copy-done.7, bf16[448,256]{1,0:T(8,128)(2,1)S(1)} %shard_sums.1.refs_0_, ...), custom_call_target="tpu_custom_call" | custom-call | tf_op jit(solution)/shard_map/assembled/pallas_call | solution.py:790
  (109 shorter events, 21.8 us)
Async XLA Ops:
  2.0 25.0 %copy-start.2 = (bf16[2,2,8,128,128]{4,3,2,1,0:T(8,128)(2,1)S(1)}, bf16[2,2,8,128,128]{4,3,2,1,0:T(8,128)(2,1)}, u32[]{:S(2)}) copy-start(bf16[2,2,8,128,128]{4,3,2,1,0:T(8,128)(2,1)} %w_ref.15) | copy-start | bytes 3145732
  2.0 25.0 %copy-start.4 = (bf16[3,512,256]{2,1,0:T(8,128)(2,1)S(1)}, bf16[3,512,256]{2,1,0:T(8,128)(2,1)}, u32[]{:S(2)}) copy-start(bf16[3,512,256]{2,1,0:T(8,128)(2,1)} %constant.76.clone.t_ref) | copy-start | bytes 2359300
  2.0 25.0 %copy-start.7 = (s32[15]{0:T(128)S(1)}, s32[15]{0:T(128)}, u32[]{:S(2)}) copy-start(s32[15]{0:T(128)} %concatenate.12.scal_ref) | copy-start | bytes 184
  2.0 25.1 %copy-start.10 = (f32[2,2,8,128]{3,2,1,0:T(8,128)S(1)}, f32[2,2,8,128]{3,2,1,0:T(8,128)}, u32[]{:S(2)}) copy-start(f32[2,2,8,128]{3,2,1,0:T(8,128)} %b_ref.3) | copy-start | bytes 49156
  12.0 12.2 %collective-permute-start.10 = (bf16[3,64,256]{2,1,0:T(8,128)(2,1)}, bf16[3,64,256]{2,1,0:T(8,128)(2,1)S(1)}, u32[]{:S(2)}, u32[]{:S(2)}) collective-permute-start(bf16[3,64,256]{2,1,0:T(8,128)(2,1)} %get-tuple-element.115), channel_id=1, source_target_pairs={{0,2},{1,3},{2,0},{3,1},{4,6},{5,7},{6,4},{7,5},{8,10},{9,11},{10,... | collective-permute-start | bytes 294920 | tf_op jit(solution)/shard_map/ppermute | solution.py:589
  16.1 10.9 %collective-permute-start.11 = (bf16[3,64,256]{2,1,0:T(8,128)(2,1)}, bf16[3,64,256]{2,1,0:T(8,128)(2,1)S(1)}, u32[]{:S(2)}, u32[]{:S(2)}) collective-permute-start(bf16[3,64,256]{2,1,0:T(8,128)(2,1)} %get-tuple-element.116), channel_id=1, source_target_pairs={{0,3},{1,2},{2,1},{3,0},{4,7},{5,6},{6,5},{7,4},{8,11},{9,10},{10,... | collective-permute-start | bytes 294920 | tf_op jit(solution)/shard_map/ppermute | solution.py:589
  17.5 9.5 %collective-permute-start.9 = (bf16[3,64,256]{2,1,0:T(8,128)(2,1)}, bf16[3,64,256]{2,1,0:T(8,128)(2,1)S(1)}, u32[]{:S(2)}, u32[]{:S(2)}) collective-permute-start(bf16[3,64,256]{2,1,0:T(8,128)(2,1)} %get-tuple-element.114), channel_id=1, source_target_pairs={{0,1},{1,0},{2,3},{3,2},{4,5},{5,4},{6,7},{7,6},{8,9},{9,8},{10,11... | collective-permute-start | bytes 294920 | tf_op jit(solution)/shard_map/ppermute | solution.py:589
  17.7 15.1 %collective-permute-start = (bf16[3,64,256]{2,1,0:T(8,128)(2,1)}, bf16[3,64,256]{2,1,0:T(8,128)(2,1)S(1)}, u32[]{:S(2)}, u32[]{:S(2)}) collective-permute-start(bf16[3,64,256]{2,1,0:T(8,128)(2,1)} %get-tuple-element.100), channel_id=1, source_target_pairs={{0,1},{1,0},{2,3},{3,2},{4,5},{5,4},{6,7},{7,6},{8,9},{9,8},{10,11... | collective-permute-start | bytes 294920 | tf_op jit(solution)/shard_map/ppermute | solution.py:589
  19.5 15.2 %collective-permute-start.1 = (bf16[3,64,256]{2,1,0:T(8,128)(2,1)}, bf16[3,64,256]{2,1,0:T(8,128)(2,1)S(1)}, u32[]{:S(2)}, u32[]{:S(2)}) collective-permute-start(bf16[3,64,256]{2,1,0:T(8,128)(2,1)} %get-tuple-element.101), channel_id=1, source_target_pairs={{0,2},{1,3},{2,0},{3,1},{4,6},{5,7},{6,4},{7,5},{8,10},{9,11},{10,... | collective-permute-start | bytes 294920 | tf_op jit(solution)/shard_map/ppermute | solution.py:589
  24.2 10.5 %collective-permute-start.2 = (bf16[3,64,256]{2,1,0:T(8,128)(2,1)}, bf16[3,64,256]{2,1,0:T(8,128)(2,1)S(1)}, u32[]{:S(2)}, u32[]{:S(2)}) collective-permute-start(bf16[3,64,256]{2,1,0:T(8,128)(2,1)} %get-tuple-element.102), channel_id=1, source_target_pairs={{0,3},{1,2},{2,1},{3,0},{4,7},{5,6},{6,5},{7,4},{8,11},{9,10},{10,... | collective-permute-start | bytes 294920 | tf_op jit(solution)/shard_map/ppermute | solution.py:589
  30.2 9.5 %collective-permute-start.12 = (bf16[3,64,256]{2,1,0:T(8,128)(2,1)S(1)}, bf16[3,64,256]{2,1,0:T(8,128)(2,1)S(1)}, u32[]{:S(2)}, u32[]{:S(2)}) collective-permute-start(bf16[3,64,256]{2,1,0:T(8,128)(2,1)S(1)} %get-tuple-element.121), channel_id=1, source_target_pairs={{0,1},{1,0},{2,3},{3,2},{4,5},{5,4},{6,7},{7,6},{8,9},{9,8},{10,11... | collective-permute-start | bytes 294920 | tf_op jit(solution)/shard_map/ppermute | solution.py:589
  31.3 10.6 %collective-permute-start.13 = (bf16[3,64,256]{2,1,0:T(8,128)(2,1)S(1)}, bf16[3,64,256]{2,1,0:T(8,128)(2,1)S(1)}, u32[]{:S(2)}, u32[]{:S(2)}) collective-permute-start(bf16[3,64,256]{2,1,0:T(8,128)(2,1)S(1)} %get-tuple-element.122), channel_id=1, source_target_pairs={{0,2},{1,3},{2,0},{3,1},{4,6},{5,7},{6,4},{7,5},{8,10},{9,11},{10,... | collective-permute-start | bytes 294920 | tf_op jit(solution)/shard_map/ppermute | solution.py:589
  32.8 9.0 %collective-permute-start.14 = (bf16[3,64,256]{2,1,0:T(8,128)(2,1)S(1)}, bf16[3,64,256]{2,1,0:T(8,128)(2,1)S(1)}, u32[]{:S(2)}, u32[]{:S(2)}) collective-permute-start(bf16[3,64,256]{2,1,0:T(8,128)(2,1)S(1)} %get-tuple-element.123), channel_id=1, source_target_pairs={{0,3},{1,2},{2,1},{3,0},{4,7},{5,6},{6,5},{7,4},{8,11},{9,10},{10,... | collective-permute-start | bytes 294920 | tf_op jit(solution)/shard_map/ppermute | solution.py:589
  37.1 13.6 %collective-permute-start.3 = (bf16[3,64,256]{2,1,0:T(8,128)(2,1)S(1)}, bf16[3,64,256]{2,1,0:T(8,128)(2,1)S(1)}, u32[]{:S(2)}, u32[]{:S(2)}) collective-permute-start(bf16[3,64,256]{2,1,0:T(8,128)(2,1)S(1)} %get-tuple-element.109), channel_id=1, source_target_pairs={{0,1},{1,0},{2,3},{3,2},{4,5},{5,4},{6,7},{7,6},{8,9},{9,8},{10,11... | collective-permute-start | bytes 294920 | tf_op jit(solution)/shard_map/ppermute | solution.py:589
  37.5 14.7 %collective-permute-start.4 = (bf16[3,64,256]{2,1,0:T(8,128)(2,1)S(1)}, bf16[3,64,256]{2,1,0:T(8,128)(2,1)S(1)}, u32[]{:S(2)}, u32[]{:S(2)}) collective-permute-start(bf16[3,64,256]{2,1,0:T(8,128)(2,1)S(1)} %get-tuple-element.110), channel_id=1, source_target_pairs={{0,2},{1,3},{2,0},{3,1},{4,6},{5,7},{6,4},{7,5},{8,10},{9,11},{10,... | collective-permute-start | bytes 294920 | tf_op jit(solution)/shard_map/ppermute | solution.py:589
  39.7 12.4 %collective-permute-start.5 = (bf16[3,64,256]{2,1,0:T(8,128)(2,1)S(1)}, bf16[3,64,256]{2,1,0:T(8,128)(2,1)S(1)}, u32[]{:S(2)}, u32[]{:S(2)}) collective-permute-start(bf16[3,64,256]{2,1,0:T(8,128)(2,1)S(1)} %get-tuple-element.111), channel_id=1, source_target_pairs={{0,3},{1,2},{2,1},{3,0},{4,7},{5,6},{6,5},{7,4},{8,11},{9,10},{10,... | collective-permute-start | bytes 294920 | tf_op jit(solution)/shard_map/ppermute | solution.py:589
  42.8 13.2 %collective-permute-start.15 = (bf16[3,64,256]{2,1,0:T(8,128)(2,1)S(1)}, bf16[3,64,256]{2,1,0:T(8,128)(2,1)S(1)}, u32[]{:S(2)}, u32[]{:S(2)}) collective-permute-start(bf16[3,64,256]{2,1,0:T(8,128)(2,1)S(1)} %get-tuple-element.127.refs_2_.refs_0_.res_ref), channel_id=1, source_target_pairs={{0,1},{1,0},{2,3},{3,2},{4,5},{5,4},{6,7},{7,6},{8,9},{9,8},{10,11... | collective-permute-start | bytes 294920 | tf_op jit(solution)/shard_map/ppermute | solution.py:589
  49.7 10.8 %collective-permute-start.16 = (bf16[3,64,256]{2,1,0:T(8,128)(2,1)S(1)}, bf16[3,64,256]{2,1,0:T(8,128)(2,1)S(1)}, u32[]{:S(2)}, u32[]{:S(2)}) collective-permute-start(bf16[3,64,256]{2,1,0:T(8,128)(2,1)S(1)} %get-tuple-element.127.refs_2_.refs_0_.res_ref), channel_id=1, source_target_pairs={{0,2},{1,3},{2,0},{3,1},{4,6},{5,7},{6,4},{7,5},{8,10},{9,11},{10,... | collective-permute-start | bytes 294920 | tf_op jit(solution)/shard_map/ppermute | solution.py:589
  50.7 9.9 %collective-permute-start.17 = (bf16[3,64,256]{2,1,0:T(8,128)(2,1)S(1)}, bf16[3,64,256]{2,1,0:T(8,128)(2,1)S(1)}, u32[]{:S(2)}, u32[]{:S(2)}) collective-permute-start(bf16[3,64,256]{2,1,0:T(8,128)(2,1)S(1)} %get-tuple-element.127.refs_2_.refs_0_.res_ref), channel_id=1, source_target_pairs={{0,3},{1,2},{2,1},{3,0},{4,7},{5,6},{6,5},{7,4},{8,11},{9,10},{10,... | collective-permute-start | bytes 294920 | tf_op jit(solution)/shard_map/ppermute | solution.py:589
  53.1 10.4 %collective-permute-start.6 = (bf16[3,64,256]{2,1,0:T(8,128)(2,1)S(1)}, bf16[3,64,256]{2,1,0:T(8,128)(2,1)S(1)}, u32[]{:S(2)}, u32[]{:S(2)}) collective-permute-start(bf16[3,64,256]{2,1,0:T(8,128)(2,1)S(1)} %get-tuple-element.112.refs_3_.refs_0_.res_ref), channel_id=1, source_target_pairs={{0,1},{1,0},{2,3},{3,2},{4,5},{5,4},{6,7},{7,6},{8,9},{9,8},{10,11... | collective-permute-start | bytes 294920 | tf_op jit(solution)/shard_map/ppermute | solution.py:589
  54.2 13.6 %collective-permute-start.7 = (bf16[3,64,256]{2,1,0:T(8,128)(2,1)S(1)}, bf16[3,64,256]{2,1,0:T(8,128)(2,1)S(1)}, u32[]{:S(2)}, u32[]{:S(2)}) collective-permute-start(bf16[3,64,256]{2,1,0:T(8,128)(2,1)S(1)} %get-tuple-element.112.refs_3_.refs_0_.res_ref), channel_id=1, source_target_pairs={{0,2},{1,3},{2,0},{3,1},{4,6},{5,7},{6,4},{7,5},{8,10},{9,11},{10,... | collective-permute-start | bytes 294920 | tf_op jit(solution)/shard_map/ppermute | solution.py:589
  56.0 11.8 %collective-permute-start.8 = (bf16[3,64,256]{2,1,0:T(8,128)(2,1)S(1)}, bf16[3,64,256]{2,1,0:T(8,128)(2,1)S(1)}, u32[]{:S(2)}, u32[]{:S(2)}) collective-permute-start(bf16[3,64,256]{2,1,0:T(8,128)(2,1)S(1)} %get-tuple-element.112.refs_3_.refs_0_.res_ref), channel_id=1, source_target_pairs={{0,3},{1,2},{2,1},{3,0},{4,7},{5,6},{6,5},{7,4},{8,11},{9,10},{10,... | collective-permute-start | bytes 294920 | tf_op jit(solution)/shard_map/ppermute | solution.py:589
  70.9 30.4 %collective-permute-start.18 = (bf16[4,320,384]{2,1,0:T(8,128)(2,1)}, bf16[4,320,384]{2,1,0:T(8,128)(2,1)S(1)}, u32[]{:S(2)}, u32[]{:S(2)}) collective-permute-start(bf16[4,320,384]{2,1,0:T(8,128)(2,1)} %get-tuple-element.138), channel_id=1, source_target_pairs={{0,4},{4,0},{8,12},{12,8},{16,20},{20,16},{24,28},{28,24},{1,5},{5... | collective-permute-start | bytes 2949128 | tf_op jit(solution)/shard_map/ppermute | solution.py:583
  70.9 5.3 %collective-permute-start.19 = (bf16[3,64,256]{2,1,0:T(8,128)(2,1)S(1)}, bf16[3,64,256]{2,1,0:T(8,128)(2,1)S(1)}, u32[]{:S(2)}, u32[]{:S(2)}) collective-permute-start(bf16[3,64,256]{2,1,0:T(8,128)(2,1)S(1)} %get-tuple-element.141), channel_id=1, source_target_pairs={{0,1},{1,0},{2,3},{3,2},{4,5},{5,4},{6,7},{7,6},{8,9},{9,8},{10,11... | collective-permute-start | bytes 294920 | tf_op jit(solution)/shard_map/ppermute | solution.py:589
  72.8 10.8 %collective-permute-start.20 = (bf16[3,64,256]{2,1,0:T(8,128)(2,1)S(1)}, bf16[3,64,256]{2,1,0:T(8,128)(2,1)S(1)}, u32[]{:S(2)}, u32[]{:S(2)}) collective-permute-start(bf16[3,64,256]{2,1,0:T(8,128)(2,1)S(1)} %get-tuple-element.142), channel_id=1, source_target_pairs={{0,2},{1,3},{2,0},{3,1},{4,6},{5,7},{6,4},{7,5},{8,10},{9,11},{10,... | collective-permute-start | bytes 294920 | tf_op jit(solution)/shard_map/ppermute | solution.py:589
  73.7 12.2 %collective-permute-start.21 = (bf16[3,64,256]{2,1,0:T(8,128)(2,1)S(1)}, bf16[3,64,256]{2,1,0:T(8,128)(2,1)S(1)}, u32[]{:S(2)}, u32[]{:S(2)}) collective-permute-start(bf16[3,64,256]{2,1,0:T(8,128)(2,1)S(1)} %get-tuple-element.143), channel_id=1, source_target_pairs={{0,3},{1,2},{2,1},{3,0},{4,7},{5,6},{6,5},{7,4},{8,11},{9,10},{10,... | collective-permute-start | bytes 294920 | tf_op jit(solution)/shard_map/ppermute | solution.py:589
  75.4 12.7 %collective-permute-start.22 = (bf16[3,64,256]{2,1,0:T(8,128)(2,1)S(1)}, bf16[3,64,256]{2,1,0:T(8,128)(2,1)S(1)}, u32[]{:S(2)}, u32[]{:S(2)}) collective-permute-start(bf16[3,64,256]{2,1,0:T(8,128)(2,1)S(1)} %get-tuple-element.149), channel_id=1, source_target_pairs={{0,1},{1,0},{2,3},{3,2},{4,5},{5,4},{6,7},{7,6},{8,9},{9,8},{10,11... | collective-permute-start | bytes 294920 | tf_op jit(solution)/shard_map/ppermute | solution.py:589
  76.3 15.7 %collective-permute-start.23 = (bf16[3,64,256]{2,1,0:T(8,128)(2,1)S(1)}, bf16[3,64,256]{2,1,0:T(8,128)(2,1)S(1)}, u32[]{:S(2)}, u32[]{:S(2)}) collective-permute-start(bf16[3,64,256]{2,1,0:T(8,128)(2,1)S(1)} %get-tuple-element.150), channel_id=1, source_target_pairs={{0,2},{1,3},{2,0},{3,1},{4,6},{5,7},{6,4},{7,5},{8,10},{9,11},{10,... | collective-permute-start | bytes 294920 | tf_op jit(solution)/shard_map/ppermute | solution.py:589
  83.5 8.4 %collective-permute-start.24 = (bf16[3,64,256]{2,1,0:T(8,128)(2,1)S(1)}, bf16[3,64,256]{2,1,0:T(8,128)(2,1)S(1)}, u32[]{:S(2)}, u32[]{:S(2)}) collective-permute-start(bf16[3,64,256]{2,1,0:T(8,128)(2,1)S(1)} %get-tuple-element.151), channel_id=1, source_target_pairs={{0,3},{1,2},{2,1},{3,0},{4,7},{5,6},{6,5},{7,4},{8,11},{9,10},{10,... | collective-permute-start | bytes 294920 | tf_op jit(solution)/shard_map/ppermute | solution.py:589
  94.3 6.9 %collective-permute-start.26 = (bf16[192,1024]{1,0:T(8,128)(2,1)}, bf16[192,1024]{1,0:T(8,128)(2,1)}, u32[]{:S(2)}, u32[]{:S(2)}) collective-permute-start(bf16[192,1024]{1,0:T(8,128)(2,1)} %get-tuple-element.152.refs_3_), channel_id=1, source_target_pairs={{0,4},{4,0},{8,12},{12,8},{16,20},{20,16},{24,28},{28,24},{1,5},{5... | collective-permute-start | bytes 1179656 | tf_op jit(solution)/shard_map/ppermute | solution.py:583
  94.4 6.9 %collective-permute-start.25 = (bf16[192,1024]{1,0:T(8,128)(2,1)}, bf16[192,1024]{1,0:T(8,128)(2,1)}, u32[]{:S(2)}, u32[]{:S(2)}) collective-permute-start(bf16[192,1024]{1,0:T(8,128)(2,1)} %get-tuple-element.147.refs_2_), channel_id=1, source_target_pairs={{0,4},{4,0},{8,12},{12,8},{16,20},{20,16},{24,28},{28,24},{1,5},{5... | collective-permute-start | bytes 1179656 | tf_op jit(solution)/shard_map/ppermute | solution.py:583
  97.2 19.9 %all-to-all-start = ((bf16[8,256,256]{2,1,0:T(8,128)(2,1)}), bf16[8,256,256]{2,1,0:T(8,128)(2,1)S(1)}, u32[]{:S(2)}, u32[]{:S(2)}) async-start(bf16[8,256,256]{2,1,0:T(8,128)(2,1)} %packed.1), calls=%async_computation | async-start | bytes 2097152 | tf_op jit(solution)/shard_map/all_to_all | solution.py:879
  106.7 23.1 %collective-permute-start.29 = (bf16[2,320,512]{2,1,0:T(8,128)(2,1)}, bf16[2,320,512]{2,1,0:T(8,128)(2,1)}, u32[]{:S(2)}, u32[]{:S(2)}) collective-permute-start(bf16[2,320,512]{2,1,0:T(8,128)(2,1)} %get-tuple-element.173), channel_id=1, source_target_pairs={{0,16},{4,20},{8,24},{12,28},{16,0},{20,4},{24,8},{28,12},{1,17},{... | collective-permute-start | bytes 1966088 | tf_op jit(solution)/shard_map/ppermute | solution.py:583
  108.8 23.9 %collective-permute-start.27 = (bf16[2,320,512]{2,1,0:T(8,128)(2,1)}, bf16[2,320,512]{2,1,0:T(8,128)(2,1)}, u32[]{:S(2)}, u32[]{:S(2)}) collective-permute-start(bf16[2,320,512]{2,1,0:T(8,128)(2,1)} %get-tuple-element.171), channel_id=1, source_target_pairs={{0,8},{4,12},{8,0},{12,4},{16,24},{20,28},{24,16},{28,20},{1,9},{5... | collective-permute-start | bytes 1966088 | tf_op jit(solution)/shard_map/ppermute | solution.py:583
  118.4 16.0 %collective-permute-start.31 = (bf16[224,256]{1,0:T(8,128)(2,1)S(1)}, bf16[224,256]{1,0:T(8,128)(2,1)S(1)}, u32[]{:S(2)}, u32[]{:S(2)}) collective-permute-start(bf16[224,256]{1,0:T(8,128)(2,1)S(1)} %get-tuple-element.174.refs_0_), channel_id=1, source_target_pairs={{0,1},{1,0},{2,3},{3,2},{4,5},{5,4},{6,7},{7,6},{8,9},{9,8},{10,11... | collective-permute-start | bytes 344072 | tf_op jit(solution)/shard_map/ppermute | solution.py:589
  120.3 14.1 %collective-permute-start.32 = (bf16[224,256]{1,0:T(8,128)(2,1)S(1)}, bf16[224,256]{1,0:T(8,128)(2,1)S(1)}, u32[]{:S(2)}, u32[]{:S(2)}) collective-permute-start(bf16[224,256]{1,0:T(8,128)(2,1)S(1)} %get-tuple-element.174.refs_0_), channel_id=1, source_target_pairs={{0,2},{1,3},{2,0},{3,1},{4,6},{5,7},{6,4},{7,5},{8,10},{9,11},{10,... | collective-permute-start | bytes 344072 | tf_op jit(solution)/shard_map/ppermute | solution.py:589
  121.1 13.3 %collective-permute-start.33 = (bf16[224,256]{1,0:T(8,128)(2,1)S(1)}, bf16[224,256]{1,0:T(8,128)(2,1)S(1)}, u32[]{:S(2)}, u32[]{:S(2)}) collective-permute-start(bf16[224,256]{1,0:T(8,128)(2,1)S(1)} %get-tuple-element.174.refs_0_), channel_id=1, source_target_pairs={{0,3},{1,2},{2,1},{3,0},{4,7},{5,6},{6,5},{7,4},{8,11},{9,10},{10,... | collective-permute-start | bytes 344072 | tf_op jit(solution)/shard_map/ppermute | solution.py:589
  131.1 9.5 %collective-permute-start.30 = (bf16[1,320,512]{2,1,0:T(8,128)(2,1)S(1)}, bf16[1,320,512]{2,1,0:T(8,128)(2,1)S(1)}, u32[]{:S(2)}, u32[]{:S(2)}) collective-permute-start(bf16[1,320,512]{2,1,0:T(8,128)(2,1)S(1)} %slice.21), channel_id=1, source_target_pairs={{0,8},{4,12},{8,0},{12,4},{16,24},{20,28},{24,16},{28,20},{1,9},{5... | collective-permute-start | bytes 983048 | tf_op jit(solution)/shard_map/ppermute | solution.py:583
  133.9 9.5 %collective-permute-start.28 = (bf16[1,320,512]{2,1,0:T(8,128)(2,1)S(1)}, bf16[1,320,512]{2,1,0:T(8,128)(2,1)S(1)}, u32[]{:S(2)}, u32[]{:S(2)}) collective-permute-start(bf16[1,320,512]{2,1,0:T(8,128)(2,1)S(1)} %slice_bitcast_fusion), channel_id=1, source_target_pairs={{0,16},{4,20},{8,24},{12,28},{16,0},{20,4},{24,8},{28,12},{1,17},{... | collective-permute-start | bytes 983048 | tf_op jit(solution)/shard_map/ppermute | solution.py:583
  143.6 8.7 %collective-permute-start.34 = (bf16[2,80,1024]{2,1,0:T(8,128)(2,1)S(1)}, bf16[2,80,1024]{2,1,0:T(8,128)(2,1)S(1)}, u32[]{:S(2)}, u32[]{:S(2)}) collective-permute-start(bf16[2,80,1024]{2,1,0:T(8,128)(2,1)S(1)} %dynamic-slice_bitcast_fusion), channel_id=1, source_target_pairs={{0,1},{1,0},{2,3},{3,2},{4,5},{5,4},{6,7},{7,6},{8,9},{9,8},{10,11... | collective-permute-start | bytes 983048 | tf_op jit(solution)/shard_map/ppermute | solution.py:623
  145.6 9.5 %collective-permute-start.36 = (bf16[448,256]{1,0:T(8,128)(2,1)S(1)}, bf16[448,256]{1,0:T(8,128)(2,1)S(1)}, u32[]{:S(2)}, u32[]{:S(2)}) collective-permute-start(bf16[448,256]{1,0:T(8,128)(2,1)S(1)} %shard_sums.1.refs_0_), channel_id=1, source_target_pairs={{0,8},{4,12},{8,0},{12,4},{16,24},{20,28},{24,16},{28,20},{1,9},{5... | collective-permute-start | bytes 688136 | tf_op jit(solution)/shard_map/ppermute | solution.py:629
  145.9 10.8 %collective-permute-start.37 = (bf16[448,256]{1,0:T(8,128)(2,1)S(1)}, bf16[448,256]{1,0:T(8,128)(2,1)S(1)}, u32[]{:S(2)}, u32[]{:S(2)}) collective-permute-start(bf16[448,256]{1,0:T(8,128)(2,1)S(1)} %shard_sums.1.refs_0_), channel_id=1, source_target_pairs={{0,16},{4,20},{8,24},{12,28},{16,0},{20,4},{24,8},{28,12},{1,17},{... | collective-permute-start | bytes 688136 | tf_op jit(solution)/shard_map/ppermute | solution.py:629
  146.4 10.3 %collective-permute-start.38 = (bf16[448,256]{1,0:T(8,128)(2,1)S(1)}, bf16[448,256]{1,0:T(8,128)(2,1)S(1)}, u32[]{:S(2)}, u32[]{:S(2)}) collective-permute-start(bf16[448,256]{1,0:T(8,128)(2,1)S(1)} %shard_sums.1.refs_0_), channel_id=1, source_target_pairs={{0,24},{4,28},{8,16},{12,20},{16,8},{20,12},{24,0},{28,4},{1,25},{... | collective-permute-start | bytes 688136 | tf_op jit(solution)/shard_map/ppermute | solution.py:629
  152.5 8.7 %collective-permute-start.35 = (bf16[1,80,1024]{2,1,0:T(8,128)(2,1)S(1)}, bf16[1,80,1024]{2,1,0:T(8,128)(2,1)S(1)}, u32[]{:S(2)}, u32[]{:S(2)}) collective-permute-start(bf16[1,80,1024]{2,1,0:T(8,128)(2,1)S(1)} %constant_dynamic-slice_fusion), channel_id=1, source_target_pairs={{0,2},{1,3},{2,0},{3,1},{4,6},{5,7},{6,4},{7,5},{8,10},{9,11},{10,... | collective-permute-start | bytes 491528 | tf_op jit(solution)/shard_map/ppermute | solution.py:623
  156.6 5.3 %collective-permute-start.39 = (bf16[448,256]{1,0:T(8,128)(2,1)S(1)}, bf16[448,256]{1,0:T(8,128)(2,1)S(1)}, u32[]{:S(2)}, u32[]{:S(2)}) collective-permute-start(bf16[448,256]{1,0:T(8,128)(2,1)S(1)} %shard_sums.1.refs_0_), channel_id=1, source_target_pairs={{0,4},{4,0},{8,12},{12,8},{16,20},{20,16},{24,28},{28,24},{1,5},{5... | collective-permute-start | bytes 688136 | tf_op jit(solution)/shard_map/ppermute | solution.py:583
  156.6 5.3 %collective-permute-start.40 = (bf16[448,256]{1,0:T(8,128)(2,1)S(1)}, bf16[448,256]{1,0:T(8,128)(2,1)S(1)}, u32[]{:S(2)}, u32[]{:S(2)}) collective-permute-start(bf16[448,256]{1,0:T(8,128)(2,1)S(1)} %collective-permute-done.36.refs_2_), channel_id=1, source_target_pairs={{0,4},{4,0},{8,12},{12,8},{16,20},{20,16},{24,28},{28,24},{1,5},{5... | collective-permute-start | bytes 688136 | tf_op jit(solution)/shard_map/ppermute | solution.py:583
  157.2 4.8 %collective-permute-start.41 = (bf16[448,256]{1,0:T(8,128)(2,1)S(1)}, bf16[448,256]{1,0:T(8,128)(2,1)S(1)}, u32[]{:S(2)}, u32[]{:S(2)}) collective-permute-start(bf16[448,256]{1,0:T(8,128)(2,1)S(1)} %collective-permute-done.37.refs_4_), channel_id=1, source_target_pairs={{0,4},{4,0},{8,12},{12,8},{16,20},{20,16},{24,28},{28,24},{1,5},{5... | collective-permute-start | bytes 688136 | tf_op jit(solution)/shard_map/ppermute | solution.py:583
  157.2 4.8 %collective-permute-start.42 = (bf16[448,256]{1,0:T(8,128)(2,1)S(1)}, bf16[448,256]{1,0:T(8,128)(2,1)S(1)}, u32[]{:S(2)}, u32[]{:S(2)}) collective-permute-start(bf16[448,256]{1,0:T(8,128)(2,1)S(1)} %collective-permute-done.38.refs_6_), channel_id=1, source_target_pairs={{0,4},{4,0},{8,12},{12,8},{16,20},{20,16},{24,28},{28,24},{1,5},{5... | collective-permute-start | bytes 688136 | tf_op jit(solution)/shard_map/ppermute | solution.py:583
  (12 other events, 120.7 us)

commit v11 on v10

--- a/solution.py
+++ b/solution.py
@@ -873,18 +873,19 @@
     head_rows = head_w.shape[0] // groups
     own_grads, other_grads, row_sums = [], [], []
     for first, res, back in zip(firsts, residual, spec_back):
+        if first == firsts[-1]:
+            back, _ = lax.optimization_barrier((back, outgoing_sums))
         grad, row_sum = embedded_back_chunk(scal, embedded, stats, res, head_w, gain_row, back, first, cells)
         if first == firsts[0]:
             grad, head_grad, spec_grad = lax.optimization_barrier((grad, head_grad, spec_grad))
-            weight_sums = lax.all_to_all(
-                packed(routes, head_grad, spec_grad, predicted, groups), "grp", split_axis=0, concat_axis=0, tiled=True
-            )
+            outgoing_sums = packed(routes, head_grad, spec_grad, predicted, groups)
+            weight_sums = lax.all_to_all(outgoing_sums, "grp", split_axis=0, concat_axis=0, tiled=True)
         own_grads.append(grad)
         other_grads.append(swap_bit(grad, 0, groups))
         row_sums.append(row_sum)
     grads = own_grads + other_grads
     sent = embed_grad_parts(scal, turned, grads, groups, 1)
-    sent, kept_turned = lax.optimization_barrier((sent, turned))
+    _, kept_turned, weight_sums = lax.optimization_barrier((sent, turned, weight_sums))
     top_bit = groups.bit_length() - 2
     received = [swap_bit(sent[0], 1, groups), swap_bit(sent[1], top_bit, groups)]
     kept = embed_grad_parts(scal, kept_turned, grads, groups, 0)

time: 165 us -> 169 us (1.024)
  local copies, waits for them, and re-layouts: 1.89 us -> 21.4 us
  waiting for transfers between devices: 44.4 us -> 30.9 us
  Pallas kernels: 43.8 us -> 40.3 us
    unnamed x32 -> x108, local copies, waits for them, and re-layouts: 0.95 us -> 20.4 us
    ppermute x11, waiting for transfers between devices: 15.4 us -> 3.57 us  [swap_bit(): lax.ppermute(values, 'grp', [(g, g ^ 1 << bit) for g in range(groups)])]
    ppermute x2, waiting for transfers between devices: 6.82 us -> 4.45 us  [scatter_step(): received = lax.ppermute(send, 'fft', [(z, z ^ bit) for z in range(shards)])]
    pallas_call x2, Pallas kernels: 10.1 us -> 8.17 us  [embed_grad_parts(): pl.pallas_call(body, grid_spec=pltpu.PrefetchScalarGridSpec(num_scalar_pr...]
    pallas_call x2, Pallas kernels: 4.59 us -> 2.87 us  [embedded_back_chunk(): pl.pallas_call(body, grid_spec=pltpu.PrefetchScalarGridSpec(num_scalar_pr...]
  transfers between devices with their start and end apart: 44 -> 44, of which waited for: 13 -> 12; matrix products, arithmetic and copies ran while one was open for 3% -> 3% of each run, Pallas kernels for 17% -> 15%
where the time goes in v11:
time: 169 us; the launch traced here: 168 us
  starting transfers between devices  68.7 us (41%)
  Pallas kernels  40.3 us (24%)
  waiting for transfers between devices  30.9 us (18%)
  local copies, waits for them, and re-layouts  21.4 us (13%)
  other arithmetic  5.82 us (3%)
    ppermute x27, starting transfers between devices, across(): lax.ppermute(pieces[k], 'fft', [(z, z ^ k) for z in range(shards)])  51 us
    unnamed x108, local copies, waits for them, and re-layouts  20.4 us
    ppermute x27, waiting for transfers between devices, across(): lax.ppermute(pieces[k], 'fft', [(z, z ^ k) for z in range(shards)])  18.4 us
    pallas_call x1, Pallas kernels, embed(): pl.pallas_call(body, grid_spec=pltpu.PrefetchScalarGridSpec(num_scalar_pr...  10 us
    pallas_call x2, Pallas kernels, embed_grad_parts(): pl.pallas_call(body, grid_spec=pltpu.PrefetchScalarGridSpec(num_scalar_pr...  8.17 us
    ppermute x11, starting transfers between devices, swap_bit(): lax.ppermute(values, 'grp', [(g, g ^ 1 << bit) for g in range(groups)])  6.25 us
    pallas_call x2, Pallas kernels, spectral_back_chunk(): pl.pallas_call(body, grid_spec=pltpu.PrefetchScalarGridSpec(num_scalar_pr...  6.05 us
    pallas_call x2, Pallas kernels, spectral_chunk(): pl.pallas_call(body, grid_spec=pltpu.PrefetchScalarGridSpec(num_scalar_pr...  4.6 us
  transfers between devices with their start and end apart: 44, of which 12 were waited for; matrix products, arithmetic and copies ran while one was open for 3% of the time, Pallas kernels for 15%

profile of v11, /device:TPU:0, one launch (start us, length us, event | category | flops | bytes accessed | tf_op | source)
XLA Modules:
  0.0 168.3 jit_solution(10712678702918629863)
XLA Ops:
  2.0 10.0 %embed.1 = (bf16[384,1024]{1,0:T(8,128)(2,1)}, bf16[384,1024]{1,0:T(8,128)(2,1)}, f32[384,256]{1,0:T(8,128)}, bf16[4,320,384]{2,1,0:T(8,128)(2,1)}, bf16[4,320,3...) custom-call(s32[15]{0:T(128)} %concatenate.12.scal_ref, ...), custom_call_target="tpu_custom_call" | custom-call | flops 2013265920 | bytes 7208960 | tf_op jit(solution)/shard_map/embed/pallas_call | solution.py:157
  12.0 4.1 %collective-permute-start.10 = (bf16[3,64,256]{2,1,0:T(8,128)(2,1)}, bf16[3,64,256]{2,1,0:T(8,128)(2,1)S(1)}, u32[]{:S(2)}, u32[]{:S(2)}) collective-permute-start(bf16[3,64,256]{2,1,0:T(8,128)(2,1)} %get-tuple-element.118), channel_id=1, source_target_pairs={{0,2},{1,3},{2,0},{3,1},{4,6},{5,7},{6,4},{7,5},{8,10},{9,11},{10,... | collective-permute-start | bytes 294920 | tf_op jit(solution)/shard_map/ppermute | solution.py:589
  16.1 1.3 collective-permute-start.11
  17.7 1.8 %collective-permute-start = (bf16[3,64,256]{2,1,0:T(8,128)(2,1)}, bf16[3,64,256]{2,1,0:T(8,128)(2,1)S(1)}, u32[]{:S(2)}, u32[]{:S(2)}) collective-permute-start(bf16[3,64,256]{2,1,0:T(8,128)(2,1)} %get-tuple-element.103), channel_id=1, source_target_pairs={{0,1},{1,0},{2,3},{3,2},{4,5},{5,4},{6,7},{7,6},{8,9},{9,8},{10,11... | collective-permute-start | bytes 294920 | tf_op jit(solution)/shard_map/ppermute | solution.py:589
  19.5 1.7 %collective-permute-start.1 = (bf16[3,64,256]{2,1,0:T(8,128)(2,1)}, bf16[3,64,256]{2,1,0:T(8,128)(2,1)S(1)}, u32[]{:S(2)}, u32[]{:S(2)}) collective-permute-start(bf16[3,64,256]{2,1,0:T(8,128)(2,1)} %get-tuple-element.104), channel_id=1, source_target_pairs={{0,2},{1,3},{2,0},{3,1},{4,6},{5,7},{6,4},{7,5},{8,10},{9,11},{10,... | collective-permute-start | bytes 294920 | tf_op jit(solution)/shard_map/ppermute | solution.py:589
  21.2 3.0 %collective-permute-done.10.refs_2_ = bf16[3,64,256]{2,1,0:T(8,128)(2,1)S(1)} collective-permute-done((bf16[3,64,256]{2,1,0:T(8,128)(2,1)}, bf16[3,64,256]{2,1,0:T(8,128)(2,1)S(1)}, u32[]{:S(2)}, u32[]{:S(2)}) %collective-permute-start.10) | collective-permute-done | bytes 98336 | tf_op jit(solution)/shard_map/ppermute | solution.py:589
  24.2 2.8 %collective-permute-start.2 = (bf16[3,64,256]{2,1,0:T(8,128)(2,1)}, bf16[3,64,256]{2,1,0:T(8,128)(2,1)S(1)}, u32[]{:S(2)}, u32[]{:S(2)}) collective-permute-start(bf16[3,64,256]{2,1,0:T(8,128)(2,1)} %get-tuple-element.105), channel_id=1, source_target_pairs={{0,3},{1,2},{2,1},{3,0},{4,7},{5,6},{6,5},{7,4},{8,11},{9,10},{10,... | collective-permute-start | bytes 294920 | tf_op jit(solution)/shard_map/ppermute | solution.py:589
  27.9 2.3 %spectral.3 = (bf16[3,64,256]{2,1,0:T(8,128)(2,1)S(1)}, bf16[3,64,256]{2,1,0:T(8,128)(2,1)S(1)}, bf16[3,64,256]{2,1,0:T(8,128)(2,1)S(1)}, bf16[3,64,256]{2,1,0:T...) custom-call(s32[15]{0:T(128)S(1)} %copy-done.23, ...), custom_call_target="tpu_custom_call" | custom-call | flops 704643072 | bytes 3145728 | tf_op jit(solution)/shard_map/spectral/pallas_call | solution.py:277
  31.3 1.6 collective-permute-start.13
  32.8 1.9 %collective-permute-start.14 = (bf16[3,64,256]{2,1,0:T(8,128)(2,1)S(1)}, bf16[3,64,256]{2,1,0:T(8,128)(2,1)S(1)}, u32[]{:S(2)}, u32[]{:S(2)}) collective-permute-start(bf16[3,64,256]{2,1,0:T(8,128)(2,1)S(1)} %get-tuple-element.126), channel_id=1, source_target_pairs={{0,3},{1,2},{2,1},{3,0},{4,7},{5,6},{6,5},{7,4},{8,11},{9,10},{10,... | collective-permute-start | bytes 294920 | tf_op jit(solution)/shard_map/ppermute | solution.py:589
  34.8 2.3 %spectral.2 = (bf16[3,64,256]{2,1,0:T(8,128)(2,1)S(1)}, bf16[3,64,256]{2,1,0:T(8,128)(2,1)S(1)}, bf16[3,64,256]{2,1,0:T(8,128)(2,1)S(1)}, bf16[3,64,256]{2,1,0:T...) custom-call(s32[15]{0:T(128)S(1)} %copy-done.23, ...), custom_call_target="tpu_custom_call" | custom-call | flops 704643072 | bytes 3145728 | tf_op jit(solution)/shard_map/spectral/pallas_call | solution.py:277
  37.5 2.2 %collective-permute-start.4 = (bf16[3,64,256]{2,1,0:T(8,128)(2,1)S(1)}, bf16[3,64,256]{2,1,0:T(8,128)(2,1)S(1)}, u32[]{:S(2)}, u32[]{:S(2)}) collective-permute-start(bf16[3,64,256]{2,1,0:T(8,128)(2,1)S(1)} %get-tuple-element.113), channel_id=1, source_target_pairs={{0,2},{1,3},{2,0},{3,1},{4,6},{5,7},{6,4},{7,5},{8,10},{9,11},{10,... | collective-permute-start | bytes 294920 | tf_op jit(solution)/shard_map/ppermute | solution.py:589
  39.7 1.8 %collective-permute-start.5 = (bf16[3,64,256]{2,1,0:T(8,128)(2,1)S(1)}, bf16[3,64,256]{2,1,0:T(8,128)(2,1)S(1)}, u32[]{:S(2)}, u32[]{:S(2)}) collective-permute-start(bf16[3,64,256]{2,1,0:T(8,128)(2,1)S(1)} %get-tuple-element.114), channel_id=1, source_target_pairs={{0,3},{1,2},{2,1},{3,0},{4,7},{5,6},{6,5},{7,4},{8,11},{9,10},{10,... | collective-permute-start | bytes 294920 | tf_op jit(solution)/shard_map/ppermute | solution.py:589
  42.8 6.9 %collective-permute-start.15 = (bf16[3,64,256]{2,1,0:T(8,128)(2,1)S(1)}, bf16[3,64,256]{2,1,0:T(8,128)(2,1)S(1)}, u32[]{:S(2)}, u32[]{:S(2)}) collective-permute-start(bf16[3,64,256]{2,1,0:T(8,128)(2,1)S(1)} %get-tuple-element.130.refs_2_.refs_0_.res_ref), channel_id=1, source_target_pairs={{0,1},{1,0},{2,3},{3,2},{4,5},{5,4},{6,7},{7,6},{8,9},{9,8},{10,11... | collective-permute-start | bytes 294920 | tf_op jit(solution)/shard_map/ppermute | solution.py:589
  50.7 1.5 collective-permute-start.17
  54.3 1.8 %collective-permute-start.7 = (bf16[3,64,256]{2,1,0:T(8,128)(2,1)S(1)}, bf16[3,64,256]{2,1,0:T(8,128)(2,1)S(1)}, u32[]{:S(2)}, u32[]{:S(2)}) collective-permute-start(bf16[3,64,256]{2,1,0:T(8,128)(2,1)S(1)} %get-tuple-element.115.refs_3_.refs_0_.res_ref), channel_id=1, source_target_pairs={{0,2},{1,3},{2,0},{3,1},{4,6},{5,7},{6,4},{7,5},{8,10},{9,11},{10,... | collective-permute-start | bytes 294920 | tf_op jit(solution)/shard_map/ppermute | solution.py:589
  56.1 1.5 collective-permute-start.8
  58.1 2.4 %collective-permute-done.16.refs_2_ = bf16[3,64,256]{2,1,0:T(8,128)(2,1)S(1)} collective-permute-done((bf16[3,64,256]{2,1,0:T(8,128)(2,1)S(1)}, bf16[3,64,256]{2,1,0:T(8,128)(2,1)S(1)}, u32[]{:S(2)}, u32[]{:S(2)}) %collective-permute-start.16) | collective-permute-done | bytes 98336 | tf_op jit(solution)/shard_map/ppermute | solution.py:589
  60.5 3.0 %spectral_back.2 = (bf16[3,64,256]{2,1,0:T(8,128)(2,1)S(1)}, bf16[3,64,256]{2,1,0:T(8,128)(2,1)S(1)}, bf16[3,64,256]{2,1,0:T(8,128)(2,1)S(1)}, bf16[3,64,256]{2,...) custom-call(s32[15]{0:T(128)S(1)} %copy-done.23, bf16[3,512,256]{2,1,0:T(8,128)(2,1)S(1)} %copy-done.4, ...), custom_call_target="tpu_custom_call" | custom-call | flops 1006632960 | bytes 3145728 | tf_op jit(solution)/shard_map/spectral_back/pallas_call | solution.py:440
  63.6 4.2 %collective-permute-done.7.refs_2_ = bf16[3,64,256]{2,1,0:T(8,128)(2,1)S(1)} collective-permute-done((bf16[3,64,256]{2,1,0:T(8,128)(2,1)S(1)}, bf16[3,64,256]{2,1,0:T(8,128)(2,1)S(1)}, u32[]{:S(2)}, u32[]{:S(2)}) %collective-permute-start.7) | collective-permute-done | bytes 98336 | tf_op jit(solution)/shard_map/ppermute | solution.py:589
  67.8 3.0 %spectral_back.3 = (bf16[3,64,256]{2,1,0:T(8,128)(2,1)S(1)}, bf16[3,64,256]{2,1,0:T(8,128)(2,1)S(1)}, bf16[3,64,256]{2,1,0:T(8,128)(2,1)S(1)}, bf16[3,64,256]{2,...) custom-call(s32[15]{0:T(128)S(1)} %copy-done.23, bf16[3,512,256]{2,1,0:T(8,128)(2,1)S(1)} %copy-done.4, ...), custom_call_target="tpu_custom_call" | custom-call | flops 1006632960 | bytes 3145728 | tf_op jit(solution)/shard_map/spectral_back/pallas_call | solution.py:440
  75.2 1.9 %collective-permute-start.19 = (bf16[3,64,256]{2,1,0:T(8,128)(2,1)}, bf16[3,64,256]{2,1,0:T(8,128)(2,1)S(1)}, u32[]{:S(2)}, u32[]{:S(2)}) collective-permute-start(bf16[3,64,256]{2,1,0:T(8,128)(2,1)} %copy-done.47), channel_id=1, source_target_pairs={{0,1},{1,0},{2,3},{3,2},{4,5},{5,4},{6,7},{7,6},{8,9},{9,8},{10,11... | collective-permute-start | bytes 294920 | tf_op jit(solution)/shard_map/ppermute | solution.py:589
  78.1 1.7 %collective-permute-start.21 = (bf16[3,64,256]{2,1,0:T(8,128)(2,1)}, bf16[3,64,256]{2,1,0:T(8,128)(2,1)S(1)}, u32[]{:S(2)}, u32[]{:S(2)}) collective-permute-start(bf16[3,64,256]{2,1,0:T(8,128)(2,1)} %copy-done.44), channel_id=1, source_target_pairs={{0,3},{1,2},{2,1},{3,0},{4,7},{5,6},{6,5},{7,4},{8,11},{9,10},{10,... | collective-permute-start | bytes 294920 | tf_op jit(solution)/shard_map/ppermute | solution.py:589
  80.8 2.9 %collective-permute-start.23 = (bf16[3,64,256]{2,1,0:T(8,128)(2,1)}, bf16[3,64,256]{2,1,0:T(8,128)(2,1)S(1)}, u32[]{:S(2)}, u32[]{:S(2)}) collective-permute-start(bf16[3,64,256]{2,1,0:T(8,128)(2,1)} %copy-done.43), channel_id=1, source_target_pairs={{0,2},{1,3},{2,0},{3,1},{4,6},{5,7},{6,4},{7,5},{8,10},{9,11},{10,... | collective-permute-start | bytes 294920 | tf_op jit(solution)/shard_map/ppermute | solution.py:589
  83.6 4.4 %collective-permute-done.20.refs_2_ = bf16[3,64,256]{2,1,0:T(8,128)(2,1)S(1)} collective-permute-done((bf16[3,64,256]{2,1,0:T(8,128)(2,1)}, bf16[3,64,256]{2,1,0:T(8,128)(2,1)S(1)}, u32[]{:S(2)}, u32[]{:S(2)}) %collective-permute-start.20) | collective-permute-done | bytes 98336 | tf_op jit(solution)/shard_map/ppermute | solution.py:589
  88.0 2.2 %collective-permute-start.24 = (bf16[3,64,256]{2,1,0:T(8,128)(2,1)}, bf16[3,64,256]{2,1,0:T(8,128)(2,1)S(1)}, u32[]{:S(2)}, u32[]{:S(2)}) collective-permute-start(bf16[3,64,256]{2,1,0:T(8,128)(2,1)} %copy-done.42), channel_id=1, source_target_pairs={{0,3},{1,2},{2,1},{3,0},{4,7},{5,6},{6,5},{7,4},{8,11},{9,10},{10,... | collective-permute-start | bytes 294920 | tf_op jit(solution)/shard_map/ppermute | solution.py:589
  92.3 1.4 embedded_back.2
  95.7 1.9 %packed.1 = bf16[8,256,256]{2,1,0:T(8,128)(2,1)} custom-call(s32[17]{0:T(128)S(1)} %concatenate.11.routes_ref, bf16[1024,256]{1,0:T(8,128)(2,1)S(1)} %copy-done.6, bf16[512,256]{1,0:T(8,128)(2,1)S(1)} %copy-done.14, bf16[3,64,256]{2,1,0:T(8,128)(2,1)S(1)} %copy-done.16, bf16[3,64,256]{2,1,0:T(8,128)(2,1)S(1)} %copy-done.18), custom_call_target="tpu_custom_call" | custom-call | tf_op jit(solution)/shard_map/packed/pallas_call | solution.py:645
  97.6 1.4 embedded_back.3
  99.6 3.8 %all-to-all-start = ((bf16[8,256,256]{2,1,0:T(8,128)(2,1)}), bf16[8,256,256]{2,1,0:T(8,128)(2,1)S(1)}, u32[]{:S(2)}, u32[]{:S(2)}) async-start(bf16[8,256,256]{2,1,0:T(8,128)(2,1)} %packed.1), calls=%async_computation | async-start | bytes 2097152 | tf_op jit(solution)/shard_map/all_to_all | solution.py:882
  110.1 4.1 %embed_grad.2 = (bf16[2,320,512]{2,1,0:T(8,128)(2,1)S(1)}, bf16[2,320,512]{2,1,0:T(8,128)(2,1)S(1)}) custom-call(s32[15]{0:T(128)S(1)} %copy-done.23, bf16[4,320,384]{2,1,0:T(8,128)(2,1)S(1)} %copy-done.49, bf16[4,320,384]{2,1,0:T(8,128)(2,1)} %collective-permute-done.18.refs_1_, bf16[192,1024]{1,0:T(8,128)(2,1)S(1)} %copy-done.31, ...), custom_call_target="tpu_custom_call" | custom-call | flops 1006632960 | bytes 4063232 | tf_op jit(solution)/shard_map/embed_grad/pallas_call | solution.py:555
  114.2 2.1 %collective-permute-start.29 = (bf16[2,320,512]{2,1,0:T(8,128)(2,1)S(1)}, bf16[2,320,512]{2,1,0:T(8,128)(2,1)}, u32[]{:S(2)}, u32[]{:S(2)}) collective-permute-start(bf16[2,320,512]{2,1,0:T(8,128)(2,1)S(1)} %get-tuple-element.165), channel_id=1, source_target_pairs={{0,16},{4,20},{8,24},{12,28},{16,0},{20,4},{24,8},{28,12},{1,17},{... | collective-permute-start | bytes 1966088 | tf_op jit(solution)/shard_map/ppermute | solution.py:583
  116.3 1.5 collective-permute-start.27
  124.2 4.1 %embed_grad.3 = (bf16[2,320,512]{2,1,0:T(8,128)(2,1)S(1)}, bf16[2,320,512]{2,1,0:T(8,128)(2,1)S(1)}) custom-call(s32[15]{0:T(128)S(1)} %copy-done.23, bf16[4,320,384]{2,1,0:T(8,128)(2,1)S(1)} %copy-done.50, bf16[4,320,384]{2,1,0:T(8,128)(2,1)} %collective-permute-done.18.refs_1_, bf16[192,1024]{1,0:T(8,128)(2,1)S(1)} %copy-done.32, ...), custom_call_target="tpu_custom_call" | custom-call | flops 1006632960 | bytes 4063232 | tf_op jit(solution)/shard_map/embed_grad/pallas_call | solution.py:555
  128.3 1.3 group_sums.1
  129.6 3.5 %collective-permute-start.31 = (bf16[224,256]{1,0:T(8,128)(2,1)S(1)}, bf16[224,256]{1,0:T(8,128)(2,1)S(1)}, u32[]{:S(2)}, u32[]{:S(2)}) collective-permute-start(bf16[224,256]{1,0:T(8,128)(2,1)S(1)} %get-tuple-element.180.refs_0_), channel_id=1, source_target_pairs={{0,1},{1,0},{2,3},{3,2},{4,5},{5,4},{6,7},{7,6},{8,9},{9,8},{10,11... | collective-permute-start | bytes 344072 | tf_op jit(solution)/shard_map/ppermute | solution.py:589
  133.7 1.7 collective-permute-start.33
  135.4 1.3 add_convert_fusion
  139.1 4.0 %collective-permute-done.32.refs_2_ = bf16[224,256]{1,0:T(8,128)(2,1)S(1)} collective-permute-done((bf16[224,256]{1,0:T(8,128)(2,1)S(1)}, bf16[224,256]{1,0:T(8,128)(2,1)S(1)}, u32[]{:S(2)}, u32[]{:S(2)}) %collective-permute-start.32) | collective-permute-done | bytes 114720 | tf_op jit(solution)/shard_map/ppermute | solution.py:589
  144.6 2.8 %collective-permute-done.28 = bf16[1,320,512]{2,1,0:T(8,128)(2,1)} collective-permute-done((bf16[1,320,512]{2,1,0:T(8,128)(2,1)S(1)}, bf16[1,320,512]{2,1,0:T(8,128)(2,1)}, u32[]{:S(2)}, u32[]{:S(2)}) %collective-permute-start.28) | collective-permute-done | bytes 327712 | tf_op jit(solution)/shard_map/ppermute | solution.py:583
  148.6 1.6 collective-permute-start.34
  150.2 1.7 %collective-permute-start.36 = (bf16[448,256]{1,0:T(8,128)(2,1)S(1)}, bf16[448,256]{1,0:T(8,128)(2,1)S(1)}, u32[]{:S(2)}, u32[]{:S(2)}) collective-permute-start(bf16[448,256]{1,0:T(8,128)(2,1)S(1)} %shard_sums.1.refs_0_), channel_id=1, source_target_pairs={{0,8},{4,12},{8,0},{12,4},{16,24},{20,28},{24,16},{28,20},{1,9},{5... | collective-permute-start | bytes 688136 | tf_op jit(solution)/shard_map/ppermute | solution.py:629
  152.2 1.5 collective-permute-start.38
  153.7 3.1 %collective-permute-done.34 = bf16[2,80,1024]{2,1,0:T(8,128)(2,1)S(1)} collective-permute-done((bf16[2,80,1024]{2,1,0:T(8,128)(2,1)S(1)}, bf16[2,80,1024]{2,1,0:T(8,128)(2,1)S(1)}, u32[]{:S(2)}, u32[]{:S(2)}) %collective-permute-start.34) | collective-permute-done | bytes 327712 | tf_op jit(solution)/shard_map/ppermute | solution.py:623
  156.9 2.5 %collective-permute-start.35 = (bf16[1,80,1024]{2,1,0:T(8,128)(2,1)S(1)}, bf16[1,80,1024]{2,1,0:T(8,128)(2,1)S(1)}, u32[]{:S(2)}, u32[]{:S(2)}) collective-permute-start(bf16[1,80,1024]{2,1,0:T(8,128)(2,1)S(1)} %constant_dynamic-slice_fusion), channel_id=1, source_target_pairs={{0,2},{1,3},{2,0},{3,1},{4,6},{5,7},{6,4},{7,5},{8,10},{9,11},{10,... | collective-permute-start | bytes 491528 | tf_op jit(solution)/shard_map/ppermute | solution.py:623
  159.4 3.2 %collective-permute-done.37.refs_4_ = bf16[448,256]{1,0:T(8,128)(2,1)S(1)} collective-permute-done((bf16[448,256]{1,0:T(8,128)(2,1)S(1)}, bf16[448,256]{1,0:T(8,128)(2,1)S(1)}, u32[]{:S(2)}, u32[]{:S(2)}) %collective-permute-start.37) | collective-permute-done | bytes 229408 | tf_op jit(solution)/shard_map/ppermute | solution.py:629
  163.6 1.4 collective-permute-done.35
  165.8 2.5 %assembled.1 = (f32[1024,256]{1,0:T(8,128)}, f32[2,2,8,128,128]{4,3,2,1,0:T(8,128)}, f32[2,2,8,128]{3,2,1,0:T(8,128)}, f32[1,1024]{1,0:T(1,128)}, f32[1,1024]{1,0:T(1,128)}, /*index=5*/f32[1,256]{1,0:T(1,128)}) custom-call(s32[15]{0:T(128)S(1)} %copy-done.23, bf16[448,256]{1,0:T(8,128)(2,1)S(1)} %shard_sums.1.refs_0_, ...), custom_call_target="tpu_custom_call" | custom-call | tf_op jit(solution)/shard_map/assembled/pallas_call | solution.py:790
  (185 shorter events, 40.3 us)
Async XLA Ops:
  2.0 25.0 %copy-start.2 = (bf16[2,2,8,128,128]{4,3,2,1,0:T(8,128)(2,1)S(1)}, bf16[2,2,8,128,128]{4,3,2,1,0:T(8,128)(2,1)}, u32[]{:S(2)}) copy-start(bf16[2,2,8,128,128]{4,3,2,1,0:T(8,128)(2,1)} %w_ref.15) | copy-start | bytes 3145732
  2.0 25.0 %copy-start.4 = (bf16[3,512,256]{2,1,0:T(8,128)(2,1)S(1)}, bf16[3,512,256]{2,1,0:T(8,128)(2,1)}, u32[]{:S(2)}) copy-start(bf16[3,512,256]{2,1,0:T(8,128)(2,1)} %constant.76.clone.t_ref) | copy-start | bytes 2359300
  2.0 25.0 %copy-start.23 = (s32[15]{0:T(128)S(1)}, s32[15]{0:T(128)}, u32[]{:S(2)}) copy-start(s32[15]{0:T(128)} %concatenate.12.scal_ref) | copy-start | bytes 184
  2.0 25.1 %copy-start.48 = (f32[2,2,8,128]{3,2,1,0:T(8,128)S(1)}, f32[2,2,8,128]{3,2,1,0:T(8,128)}, u32[]{:S(2)}) copy-start(f32[2,2,8,128]{3,2,1,0:T(8,128)} %b_ref.3) | copy-start | bytes 49156
  12.0 12.2 %collective-permute-start.10 = (bf16[3,64,256]{2,1,0:T(8,128)(2,1)}, bf16[3,64,256]{2,1,0:T(8,128)(2,1)S(1)}, u32[]{:S(2)}, u32[]{:S(2)}) collective-permute-start(bf16[3,64,256]{2,1,0:T(8,128)(2,1)} %get-tuple-element.118), channel_id=1, source_target_pairs={{0,2},{1,3},{2,0},{3,1},{4,6},{5,7},{6,4},{7,5},{8,10},{9,11},{10,... | collective-permute-start | bytes 294920 | tf_op jit(solution)/shard_map/ppermute | solution.py:589
  16.1 10.9 %collective-permute-start.11 = (bf16[3,64,256]{2,1,0:T(8,128)(2,1)}, bf16[3,64,256]{2,1,0:T(8,128)(2,1)S(1)}, u32[]{:S(2)}, u32[]{:S(2)}) collective-permute-start(bf16[3,64,256]{2,1,0:T(8,128)(2,1)} %get-tuple-element.119), channel_id=1, source_target_pairs={{0,3},{1,2},{2,1},{3,0},{4,7},{5,6},{6,5},{7,4},{8,11},{9,10},{10,... | collective-permute-start | bytes 294920 | tf_op jit(solution)/shard_map/ppermute | solution.py:589
  17.5 9.5 %collective-permute-start.9 = (bf16[3,64,256]{2,1,0:T(8,128)(2,1)}, bf16[3,64,256]{2,1,0:T(8,128)(2,1)S(1)}, u32[]{:S(2)}, u32[]{:S(2)}) collective-permute-start(bf16[3,64,256]{2,1,0:T(8,128)(2,1)} %get-tuple-element.117), channel_id=1, source_target_pairs={{0,1},{1,0},{2,3},{3,2},{4,5},{5,4},{6,7},{7,6},{8,9},{9,8},{10,11... | collective-permute-start | bytes 294920 | tf_op jit(solution)/shard_map/ppermute | solution.py:589
  17.7 15.1 %collective-permute-start = (bf16[3,64,256]{2,1,0:T(8,128)(2,1)}, bf16[3,64,256]{2,1,0:T(8,128)(2,1)S(1)}, u32[]{:S(2)}, u32[]{:S(2)}) collective-permute-start(bf16[3,64,256]{2,1,0:T(8,128)(2,1)} %get-tuple-element.103), channel_id=1, source_target_pairs={{0,1},{1,0},{2,3},{3,2},{4,5},{5,4},{6,7},{7,6},{8,9},{9,8},{10,11... | collective-permute-start | bytes 294920 | tf_op jit(solution)/shard_map/ppermute | solution.py:589
  19.5 15.2 %collective-permute-start.1 = (bf16[3,64,256]{2,1,0:T(8,128)(2,1)}, bf16[3,64,256]{2,1,0:T(8,128)(2,1)S(1)}, u32[]{:S(2)}, u32[]{:S(2)}) collective-permute-start(bf16[3,64,256]{2,1,0:T(8,128)(2,1)} %get-tuple-element.104), channel_id=1, source_target_pairs={{0,2},{1,3},{2,0},{3,1},{4,6},{5,7},{6,4},{7,5},{8,10},{9,11},{10,... | collective-permute-start | bytes 294920 | tf_op jit(solution)/shard_map/ppermute | solution.py:589
  24.2 10.5 %collective-permute-start.2 = (bf16[3,64,256]{2,1,0:T(8,128)(2,1)}, bf16[3,64,256]{2,1,0:T(8,128)(2,1)S(1)}, u32[]{:S(2)}, u32[]{:S(2)}) collective-permute-start(bf16[3,64,256]{2,1,0:T(8,128)(2,1)} %get-tuple-element.105), channel_id=1, source_target_pairs={{0,3},{1,2},{2,1},{3,0},{4,7},{5,6},{6,5},{7,4},{8,11},{9,10},{10,... | collective-permute-start | bytes 294920 | tf_op jit(solution)/shard_map/ppermute | solution.py:589
  30.2 9.5 %collective-permute-start.12 = (bf16[3,64,256]{2,1,0:T(8,128)(2,1)S(1)}, bf16[3,64,256]{2,1,0:T(8,128)(2,1)S(1)}, u32[]{:S(2)}, u32[]{:S(2)}) collective-permute-start(bf16[3,64,256]{2,1,0:T(8,128)(2,1)S(1)} %get-tuple-element.124), channel_id=1, source_target_pairs={{0,1},{1,0},{2,3},{3,2},{4,5},{5,4},{6,7},{7,6},{8,9},{9,8},{10,11... | collective-permute-start | bytes 294920 | tf_op jit(solution)/shard_map/ppermute | solution.py:589
  31.3 10.6 %collective-permute-start.13 = (bf16[3,64,256]{2,1,0:T(8,128)(2,1)S(1)}, bf16[3,64,256]{2,1,0:T(8,128)(2,1)S(1)}, u32[]{:S(2)}, u32[]{:S(2)}) collective-permute-start(bf16[3,64,256]{2,1,0:T(8,128)(2,1)S(1)} %get-tuple-element.125), channel_id=1, source_target_pairs={{0,2},{1,3},{2,0},{3,1},{4,6},{5,7},{6,4},{7,5},{8,10},{9,11},{10,... | collective-permute-start | bytes 294920 | tf_op jit(solution)/shard_map/ppermute | solution.py:589
  32.8 9.0 %collective-permute-start.14 = (bf16[3,64,256]{2,1,0:T(8,128)(2,1)S(1)}, bf16[3,64,256]{2,1,0:T(8,128)(2,1)S(1)}, u32[]{:S(2)}, u32[]{:S(2)}) collective-permute-start(bf16[3,64,256]{2,1,0:T(8,128)(2,1)S(1)} %get-tuple-element.126), channel_id=1, source_target_pairs={{0,3},{1,2},{2,1},{3,0},{4,7},{5,6},{6,5},{7,4},{8,11},{9,10},{10,... | collective-permute-start | bytes 294920 | tf_op jit(solution)/shard_map/ppermute | solution.py:589
  37.1 13.6 %collective-permute-start.3 = (bf16[3,64,256]{2,1,0:T(8,128)(2,1)S(1)}, bf16[3,64,256]{2,1,0:T(8,128)(2,1)S(1)}, u32[]{:S(2)}, u32[]{:S(2)}) collective-permute-start(bf16[3,64,256]{2,1,0:T(8,128)(2,1)S(1)} %get-tuple-element.112), channel_id=1, source_target_pairs={{0,1},{1,0},{2,3},{3,2},{4,5},{5,4},{6,7},{7,6},{8,9},{9,8},{10,11... | collective-permute-start | bytes 294920 | tf_op jit(solution)/shard_map/ppermute | solution.py:589
  37.5 14.7 %collective-permute-start.4 = (bf16[3,64,256]{2,1,0:T(8,128)(2,1)S(1)}, bf16[3,64,256]{2,1,0:T(8,128)(2,1)S(1)}, u32[]{:S(2)}, u32[]{:S(2)}) collective-permute-start(bf16[3,64,256]{2,1,0:T(8,128)(2,1)S(1)} %get-tuple-element.113), channel_id=1, source_target_pairs={{0,2},{1,3},{2,0},{3,1},{4,6},{5,7},{6,4},{7,5},{8,10},{9,11},{10,... | collective-permute-start | bytes 294920 | tf_op jit(solution)/shard_map/ppermute | solution.py:589
  39.7 12.5 %collective-permute-start.5 = (bf16[3,64,256]{2,1,0:T(8,128)(2,1)S(1)}, bf16[3,64,256]{2,1,0:T(8,128)(2,1)S(1)}, u32[]{:S(2)}, u32[]{:S(2)}) collective-permute-start(bf16[3,64,256]{2,1,0:T(8,128)(2,1)S(1)} %get-tuple-element.114), channel_id=1, source_target_pairs={{0,3},{1,2},{2,1},{3,0},{4,7},{5,6},{6,5},{7,4},{8,11},{9,10},{10,... | collective-permute-start | bytes 294920 | tf_op jit(solution)/shard_map/ppermute | solution.py:589
  42.8 13.3 %collective-permute-start.15 = (bf16[3,64,256]{2,1,0:T(8,128)(2,1)S(1)}, bf16[3,64,256]{2,1,0:T(8,128)(2,1)S(1)}, u32[]{:S(2)}, u32[]{:S(2)}) collective-permute-start(bf16[3,64,256]{2,1,0:T(8,128)(2,1)S(1)} %get-tuple-element.130.refs_2_.refs_0_.res_ref), channel_id=1, source_target_pairs={{0,1},{1,0},{2,3},{3,2},{4,5},{5,4},{6,7},{7,6},{8,9},{9,8},{10,11... | collective-permute-start | bytes 294920 | tf_op jit(solution)/shard_map/ppermute | solution.py:589
  49.8 10.8 %collective-permute-start.16 = (bf16[3,64,256]{2,1,0:T(8,128)(2,1)S(1)}, bf16[3,64,256]{2,1,0:T(8,128)(2,1)S(1)}, u32[]{:S(2)}, u32[]{:S(2)}) collective-permute-start(bf16[3,64,256]{2,1,0:T(8,128)(2,1)S(1)} %get-tuple-element.130.refs_2_.refs_0_.res_ref), channel_id=1, source_target_pairs={{0,2},{1,3},{2,0},{3,1},{4,6},{5,7},{6,4},{7,5},{8,10},{9,11},{10,... | collective-permute-start | bytes 294920 | tf_op jit(solution)/shard_map/ppermute | solution.py:589
  50.7 9.8 %collective-permute-start.17 = (bf16[3,64,256]{2,1,0:T(8,128)(2,1)S(1)}, bf16[3,64,256]{2,1,0:T(8,128)(2,1)S(1)}, u32[]{:S(2)}, u32[]{:S(2)}) collective-permute-start(bf16[3,64,256]{2,1,0:T(8,128)(2,1)S(1)} %get-tuple-element.130.refs_2_.refs_0_.res_ref), channel_id=1, source_target_pairs={{0,3},{1,2},{2,1},{3,0},{4,7},{5,6},{6,5},{7,4},{8,11},{9,10},{10,... | collective-permute-start | bytes 294920 | tf_op jit(solution)/shard_map/ppermute | solution.py:589
  53.1 10.5 %collective-permute-start.6 = (bf16[3,64,256]{2,1,0:T(8,128)(2,1)S(1)}, bf16[3,64,256]{2,1,0:T(8,128)(2,1)S(1)}, u32[]{:S(2)}, u32[]{:S(2)}) collective-permute-start(bf16[3,64,256]{2,1,0:T(8,128)(2,1)S(1)} %get-tuple-element.115.refs_3_.refs_0_.res_ref), channel_id=1, source_target_pairs={{0,1},{1,0},{2,3},{3,2},{4,5},{5,4},{6,7},{7,6},{8,9},{9,8},{10,11... | collective-permute-start | bytes 294920 | tf_op jit(solution)/shard_map/ppermute | solution.py:589
  54.3 13.5 %collective-permute-start.7 = (bf16[3,64,256]{2,1,0:T(8,128)(2,1)S(1)}, bf16[3,64,256]{2,1,0:T(8,128)(2,1)S(1)}, u32[]{:S(2)}, u32[]{:S(2)}) collective-permute-start(bf16[3,64,256]{2,1,0:T(8,128)(2,1)S(1)} %get-tuple-element.115.refs_3_.refs_0_.res_ref), channel_id=1, source_target_pairs={{0,2},{1,3},{2,0},{3,1},{4,6},{5,7},{6,4},{7,5},{8,10},{9,11},{10,... | collective-permute-start | bytes 294920 | tf_op jit(solution)/shard_map/ppermute | solution.py:589
  56.1 11.7 %collective-permute-start.8 = (bf16[3,64,256]{2,1,0:T(8,128)(2,1)S(1)}, bf16[3,64,256]{2,1,0:T(8,128)(2,1)S(1)}, u32[]{:S(2)}, u32[]{:S(2)}) collective-permute-start(bf16[3,64,256]{2,1,0:T(8,128)(2,1)S(1)} %get-tuple-element.115.refs_3_.refs_0_.res_ref), channel_id=1, source_target_pairs={{0,3},{1,2},{2,1},{3,0},{4,7},{5,6},{6,5},{7,4},{8,11},{9,10},{10,... | collective-permute-start | bytes 294920 | tf_op jit(solution)/shard_map/ppermute | solution.py:589
  74.8 30.2 %collective-permute-start.18 = (bf16[4,320,384]{2,1,0:T(8,128)(2,1)}, bf16[4,320,384]{2,1,0:T(8,128)(2,1)}, u32[]{:S(2)}, u32[]{:S(2)}) collective-permute-start(bf16[4,320,384]{2,1,0:T(8,128)(2,1)} %get-tuple-element.141), channel_id=1, source_target_pairs={{0,4},{4,0},{8,12},{12,8},{16,20},{20,16},{24,28},{28,24},{1,5},{5... | collective-permute-start | bytes 2949128 | tf_op jit(solution)/shard_map/ppermute | solution.py:583
  75.2 5.6 %collective-permute-start.19 = (bf16[3,64,256]{2,1,0:T(8,128)(2,1)}, bf16[3,64,256]{2,1,0:T(8,128)(2,1)S(1)}, u32[]{:S(2)}, u32[]{:S(2)}) collective-permute-start(bf16[3,64,256]{2,1,0:T(8,128)(2,1)} %copy-done.47), channel_id=1, source_target_pairs={{0,1},{1,0},{2,3},{3,2},{4,5},{5,4},{6,7},{7,6},{8,9},{9,8},{10,11... | collective-permute-start | bytes 294920 | tf_op jit(solution)/shard_map/ppermute | solution.py:589
  77.1 11.0 %collective-permute-start.20 = (bf16[3,64,256]{2,1,0:T(8,128)(2,1)}, bf16[3,64,256]{2,1,0:T(8,128)(2,1)S(1)}, u32[]{:S(2)}, u32[]{:S(2)}) collective-permute-start(bf16[3,64,256]{2,1,0:T(8,128)(2,1)} %copy-done.46), channel_id=1, source_target_pairs={{0,2},{1,3},{2,0},{3,1},{4,6},{5,7},{6,4},{7,5},{8,10},{9,11},{10,... | collective-permute-start | bytes 294920 | tf_op jit(solution)/shard_map/ppermute | solution.py:589
  78.1 12.4 %collective-permute-start.21 = (bf16[3,64,256]{2,1,0:T(8,128)(2,1)}, bf16[3,64,256]{2,1,0:T(8,128)(2,1)S(1)}, u32[]{:S(2)}, u32[]{:S(2)}) collective-permute-start(bf16[3,64,256]{2,1,0:T(8,128)(2,1)} %copy-done.44), channel_id=1, source_target_pairs={{0,3},{1,2},{2,1},{3,0},{4,7},{5,6},{6,5},{7,4},{8,11},{9,10},{10,... | collective-permute-start | bytes 294920 | tf_op jit(solution)/shard_map/ppermute | solution.py:589
  79.8 17.8 %collective-permute-start.22 = (bf16[3,64,256]{2,1,0:T(8,128)(2,1)}, bf16[3,64,256]{2,1,0:T(8,128)(2,1)S(1)}, u32[]{:S(2)}, u32[]{:S(2)}) collective-permute-start(bf16[3,64,256]{2,1,0:T(8,128)(2,1)} %copy-done.45), channel_id=1, source_target_pairs={{0,1},{1,0},{2,3},{3,2},{4,5},{5,4},{6,7},{7,6},{8,9},{9,8},{10,11... | collective-permute-start | bytes 294920 | tf_op jit(solution)/shard_map/ppermute | solution.py:589
  80.8 16.8 %collective-permute-start.23 = (bf16[3,64,256]{2,1,0:T(8,128)(2,1)}, bf16[3,64,256]{2,1,0:T(8,128)(2,1)S(1)}, u32[]{:S(2)}, u32[]{:S(2)}) collective-permute-start(bf16[3,64,256]{2,1,0:T(8,128)(2,1)} %copy-done.43), channel_id=1, source_target_pairs={{0,2},{1,3},{2,0},{3,1},{4,6},{5,7},{6,4},{7,5},{8,10},{9,11},{10,... | collective-permute-start | bytes 294920 | tf_op jit(solution)/shard_map/ppermute | solution.py:589
  88.0 9.5 %collective-permute-start.24 = (bf16[3,64,256]{2,1,0:T(8,128)(2,1)}, bf16[3,64,256]{2,1,0:T(8,128)(2,1)S(1)}, u32[]{:S(2)}, u32[]{:S(2)}) collective-permute-start(bf16[3,64,256]{2,1,0:T(8,128)(2,1)} %copy-done.42), channel_id=1, source_target_pairs={{0,3},{1,2},{2,1},{3,0},{4,7},{5,6},{6,5},{7,4},{8,11},{9,10},{10,... | collective-permute-start | bytes 294920 | tf_op jit(solution)/shard_map/ppermute | solution.py:589
  99.0 4.4 %collective-permute-start.26 = (bf16[192,1024]{1,0:T(8,128)(2,1)S(1)}, bf16[192,1024]{1,0:T(8,128)(2,1)S(1)}, u32[]{:S(2)}, u32[]{:S(2)}) collective-permute-start(bf16[192,1024]{1,0:T(8,128)(2,1)S(1)} %get-tuple-element.163.refs_3_), channel_id=1, source_target_pairs={{0,4},{4,0},{8,12},{12,8},{16,20},{20,16},{24,28},{28,24},{1,5},{5... | collective-permute-start | bytes 1179656 | tf_op jit(solution)/shard_map/ppermute | solution.py:583
  99.1 5.0 %collective-permute-start.25 = (bf16[192,1024]{1,0:T(8,128)(2,1)S(1)}, bf16[192,1024]{1,0:T(8,128)(2,1)S(1)}, u32[]{:S(2)}, u32[]{:S(2)}) collective-permute-start(bf16[192,1024]{1,0:T(8,128)(2,1)S(1)} %get-tuple-element.150.refs_2_), channel_id=1, source_target_pairs={{0,4},{4,0},{8,12},{12,8},{16,20},{20,16},{24,28},{28,24},{1,5},{5... | collective-permute-start | bytes 1179656 | tf_op jit(solution)/shard_map/ppermute | solution.py:583
  99.6 19.4 %all-to-all-start = ((bf16[8,256,256]{2,1,0:T(8,128)(2,1)}), bf16[8,256,256]{2,1,0:T(8,128)(2,1)S(1)}, u32[]{:S(2)}, u32[]{:S(2)}) async-start(bf16[8,256,256]{2,1,0:T(8,128)(2,1)} %packed.1), calls=%async_computation | async-start | bytes 2097152 | tf_op jit(solution)/shard_map/all_to_all | solution.py:882
  114.2 21.2 %collective-permute-start.29 = (bf16[2,320,512]{2,1,0:T(8,128)(2,1)S(1)}, bf16[2,320,512]{2,1,0:T(8,128)(2,1)}, u32[]{:S(2)}, u32[]{:S(2)}) collective-permute-start(bf16[2,320,512]{2,1,0:T(8,128)(2,1)S(1)} %get-tuple-element.165), channel_id=1, source_target_pairs={{0,16},{4,20},{8,24},{12,28},{16,0},{20,4},{24,8},{28,12},{1,17},{... | collective-permute-start | bytes 1966088 | tf_op jit(solution)/shard_map/ppermute | solution.py:583
  116.3 20.9 %collective-permute-start.27 = (bf16[2,320,512]{2,1,0:T(8,128)(2,1)S(1)}, bf16[2,320,512]{2,1,0:T(8,128)(2,1)}, u32[]{:S(2)}, u32[]{:S(2)}) collective-permute-start(bf16[2,320,512]{2,1,0:T(8,128)(2,1)S(1)} %get-tuple-element.164), channel_id=1, source_target_pairs={{0,8},{4,12},{8,0},{12,4},{16,24},{20,28},{24,16},{28,20},{1,9},{5... | collective-permute-start | bytes 1966088 | tf_op jit(solution)/shard_map/ppermute | solution.py:583
  129.6 9.6 %collective-permute-start.31 = (bf16[224,256]{1,0:T(8,128)(2,1)S(1)}, bf16[224,256]{1,0:T(8,128)(2,1)S(1)}, u32[]{:S(2)}, u32[]{:S(2)}) collective-permute-start(bf16[224,256]{1,0:T(8,128)(2,1)S(1)} %get-tuple-element.180.refs_0_), channel_id=1, source_target_pairs={{0,1},{1,0},{2,3},{3,2},{4,5},{5,4},{6,7},{7,6},{8,9},{9,8},{10,11... | collective-permute-start | bytes 344072 | tf_op jit(solution)/shard_map/ppermute | solution.py:589
  133.0 10.1 %collective-permute-start.32 = (bf16[224,256]{1,0:T(8,128)(2,1)S(1)}, bf16[224,256]{1,0:T(8,128)(2,1)S(1)}, u32[]{:S(2)}, u32[]{:S(2)}) collective-permute-start(bf16[224,256]{1,0:T(8,128)(2,1)S(1)} %get-tuple-element.180.refs_0_), channel_id=1, source_target_pairs={{0,2},{1,3},{2,0},{3,1},{4,6},{5,7},{6,4},{7,5},{8,10},{9,11},{10,... | collective-permute-start | bytes 344072 | tf_op jit(solution)/shard_map/ppermute | solution.py:589
  133.7 9.4 %collective-permute-start.33 = (bf16[224,256]{1,0:T(8,128)(2,1)S(1)}, bf16[224,256]{1,0:T(8,128)(2,1)S(1)}, u32[]{:S(2)}, u32[]{:S(2)}) collective-permute-start(bf16[224,256]{1,0:T(8,128)(2,1)S(1)} %get-tuple-element.180.refs_0_), channel_id=1, source_target_pairs={{0,3},{1,2},{2,1},{3,0},{4,7},{5,6},{6,5},{7,4},{8,11},{9,10},{10,... | collective-permute-start | bytes 344072 | tf_op jit(solution)/shard_map/ppermute | solution.py:589
  136.7 7.8 %collective-permute-start.30 = (bf16[1,320,512]{2,1,0:T(8,128)(2,1)S(1)}, bf16[1,320,512]{2,1,0:T(8,128)(2,1)S(1)}, u32[]{:S(2)}, u32[]{:S(2)}) collective-permute-start(bf16[1,320,512]{2,1,0:T(8,128)(2,1)S(1)} %slice.21), channel_id=1, source_target_pairs={{0,8},{4,12},{8,0},{12,4},{16,24},{20,28},{24,16},{28,20},{1,9},{5... | collective-permute-start | bytes 983048 | tf_op jit(solution)/shard_map/ppermute | solution.py:583
  138.5 9.0 %collective-permute-start.28 = (bf16[1,320,512]{2,1,0:T(8,128)(2,1)S(1)}, bf16[1,320,512]{2,1,0:T(8,128)(2,1)}, u32[]{:S(2)}, u32[]{:S(2)}) collective-permute-start(bf16[1,320,512]{2,1,0:T(8,128)(2,1)S(1)} %slice_bitcast_fusion), channel_id=1, source_target_pairs={{0,16},{4,20},{8,24},{12,28},{16,0},{20,4},{24,8},{28,12},{1,17},{... | collective-permute-start | bytes 983048 | tf_op jit(solution)/shard_map/ppermute | solution.py:583
  148.6 8.2 %collective-permute-start.34 = (bf16[2,80,1024]{2,1,0:T(8,128)(2,1)S(1)}, bf16[2,80,1024]{2,1,0:T(8,128)(2,1)S(1)}, u32[]{:S(2)}, u32[]{:S(2)}) collective-permute-start(bf16[2,80,1024]{2,1,0:T(8,128)(2,1)S(1)} %dynamic-slice_bitcast_fusion), channel_id=1, source_target_pairs={{0,1},{1,0},{2,3},{3,2},{4,5},{5,4},{6,7},{7,6},{8,9},{9,8},{10,11... | collective-permute-start | bytes 983048 | tf_op jit(solution)/shard_map/ppermute | solution.py:623
  150.2 9.2 %collective-permute-start.36 = (bf16[448,256]{1,0:T(8,128)(2,1)S(1)}, bf16[448,256]{1,0:T(8,128)(2,1)S(1)}, u32[]{:S(2)}, u32[]{:S(2)}) collective-permute-start(bf16[448,256]{1,0:T(8,128)(2,1)S(1)} %shard_sums.1.refs_0_), channel_id=1, source_target_pairs={{0,8},{4,12},{8,0},{12,4},{16,24},{20,28},{24,16},{28,20},{1,9},{5... | collective-permute-start | bytes 688136 | tf_op jit(solution)/shard_map/ppermute | solution.py:629
  152.0 10.7 %collective-permute-start.37 = (bf16[448,256]{1,0:T(8,128)(2,1)S(1)}, bf16[448,256]{1,0:T(8,128)(2,1)S(1)}, u32[]{:S(2)}, u32[]{:S(2)}) collective-permute-start(bf16[448,256]{1,0:T(8,128)(2,1)S(1)} %shard_sums.1.refs_0_), channel_id=1, source_target_pairs={{0,16},{4,20},{8,24},{12,28},{16,0},{20,4},{24,8},{28,12},{1,17},{... | collective-permute-start | bytes 688136 | tf_op jit(solution)/shard_map/ppermute | solution.py:629
  152.2 10.4 %collective-permute-start.38 = (bf16[448,256]{1,0:T(8,128)(2,1)S(1)}, bf16[448,256]{1,0:T(8,128)(2,1)S(1)}, u32[]{:S(2)}, u32[]{:S(2)}) collective-permute-start(bf16[448,256]{1,0:T(8,128)(2,1)S(1)} %shard_sums.1.refs_0_), channel_id=1, source_target_pairs={{0,24},{4,28},{8,16},{12,20},{16,8},{20,12},{24,0},{28,4},{1,25},{... | collective-permute-start | bytes 688136 | tf_op jit(solution)/shard_map/ppermute | solution.py:629
  156.9 8.1 %collective-permute-start.35 = (bf16[1,80,1024]{2,1,0:T(8,128)(2,1)S(1)}, bf16[1,80,1024]{2,1,0:T(8,128)(2,1)S(1)}, u32[]{:S(2)}, u32[]{:S(2)}) collective-permute-start(bf16[1,80,1024]{2,1,0:T(8,128)(2,1)S(1)} %constant_dynamic-slice_fusion), channel_id=1, source_target_pairs={{0,2},{1,3},{2,0},{3,1},{4,6},{5,7},{6,4},{7,5},{8,10},{9,11},{10,... | collective-permute-start | bytes 491528 | tf_op jit(solution)/shard_map/ppermute | solution.py:623
  162.6 3.2 %collective-permute-start.39 = (bf16[448,256]{1,0:T(8,128)(2,1)S(1)}, bf16[448,256]{1,0:T(8,128)(2,1)S(1)}, u32[]{:S(2)}, u32[]{:S(2)}) collective-permute-start(bf16[448,256]{1,0:T(8,128)(2,1)S(1)} %shard_sums.1.refs_0_), channel_id=1, source_target_pairs={{0,4},{4,0},{8,12},{12,8},{16,20},{20,16},{24,28},{28,24},{1,5},{5... | collective-permute-start | bytes 688136 | tf_op jit(solution)/shard_map/ppermute | solution.py:583
  162.6 3.2 %collective-permute-start.40 = (bf16[448,256]{1,0:T(8,128)(2,1)S(1)}, bf16[448,256]{1,0:T(8,128)(2,1)S(1)}, u32[]{:S(2)}, u32[]{:S(2)}) collective-permute-start(bf16[448,256]{1,0:T(8,128)(2,1)S(1)} %collective-permute-done.36.refs_2_), channel_id=1, source_target_pairs={{0,4},{4,0},{8,12},{12,8},{16,20},{20,16},{24,28},{28,24},{1,5},{5... | collective-permute-start | bytes 688136 | tf_op jit(solution)/shard_map/ppermute | solution.py:583
  163.1 2.7 %collective-permute-start.41 = (bf16[448,256]{1,0:T(8,128)(2,1)S(1)}, bf16[448,256]{1,0:T(8,128)(2,1)S(1)}, u32[]{:S(2)}, u32[]{:S(2)}) collective-permute-start(bf16[448,256]{1,0:T(8,128)(2,1)S(1)} %collective-permute-done.37.refs_4_), channel_id=1, source_target_pairs={{0,4},{4,0},{8,12},{12,8},{16,20},{20,16},{24,28},{28,24},{1,5},{5... | collective-permute-start | bytes 688136 | tf_op jit(solution)/shard_map/ppermute | solution.py:583
  163.1 2.7 %collective-permute-start.42 = (bf16[448,256]{1,0:T(8,128)(2,1)S(1)}, bf16[448,256]{1,0:T(8,128)(2,1)S(1)}, u32[]{:S(2)}, u32[]{:S(2)}) collective-permute-start(bf16[448,256]{1,0:T(8,128)(2,1)S(1)} %collective-permute-done.38.refs_6_), channel_id=1, source_target_pairs={{0,4},{4,0},{8,12},{12,8},{16,20},{20,16},{24,28},{28,24},{1,5},{5... | collective-permute-start | bytes 688136 | tf_op jit(solution)/shard_map/ppermute | solution.py:583
  (50 other events, 288.4 us)

commit v12 on v9

--- a/solution.py
+++ b/solution.py
@@ -9,7 +9,7 @@
 
 EPSILON = 1e-05
 SHRINK = 0.01
-CHUNKS = 2
+CHUNKS = 1
 VMEM_BYTES = 24 * 1024 * 1024
 SLOTS = 6
 SHARD, FIRST_ROW, GROUP, SIDES = 0, 1, 2, 3
@@ -871,7 +871,6 @@
     width = spec_w.shape[-1]
     blocks = spec_w.shape[2] // shards
     head_rows = head_w.shape[0] // groups
-    _, head_grad, spec_grad = lax.optimization_barrier((spec_back[-1][1], head_grad, spec_grad))
     weight_sums = lax.all_to_all(
         packed(routes, head_grad, spec_grad, predicted, groups), "grp", split_axis=0, concat_axis=0, tiled=True
     )

time: 168 us -> 177 us (1.054)
  waiting for transfers between devices: 35.4 us -> 65.3 us
  starting transfers between devices: 69.1 us -> 53.1 us
  local copies, waits for them, and re-layouts: 16.1 us -> 13.7 us
    ppermute x27 -> x15, waiting for transfers between devices: 18.6 us -> 53.2 us  [across(): lax.ppermute(pieces[k], 'fft', [(z, z ^ k) for z in range(shards)])]
    ppermute x27 -> x15, starting transfers between devices: 49.3 us -> 29.9 us  [across(): lax.ppermute(pieces[k], 'fft', [(z, z ^ k) for z in range(shards)])]
    ppermute x11 -> x10, waiting for transfers between devices: 9.54 us -> 3.99 us  [swap_bit(): lax.ppermute(values, 'grp', [(g, g ^ 1 << bit) for g in range(groups)])]
    ppermute x2, starting transfers between devices: 4.41 us -> 8.58 us  [scatter_step(): received = lax.ppermute(send, 'fft', [(z, z ^ bit) for z in range(shards)])]
    unnamed x90 -> x60, local copies, waits for them, and re-layouts: 14.7 us -> 12.2 us
    all_to_all x1, waiting for transfers between devices: 0.01 us -> 1.79 us  [on_device(): lax.all_to_all(packed(routes, head_grad, spec_grad, predicted, groups), '...]
    pallas_call x2 -> x1, Pallas kernels: 7.43 us -> 6.14 us  [spectral_back_chunk(): pl.pallas_call(body, grid_spec=pltpu.PrefetchScalarGridSpec(num_scalar_pr...]
    pallas_call x2 -> x1, Pallas kernels: 2.89 us -> 3.92 us  [embedded_back_chunk(): pl.pallas_call(body, grid_spec=pltpu.PrefetchScalarGridSpec(num_scalar_pr...]
  transfers between devices with their start and end apart: 44 -> 31, of which waited for: 15 -> 17; matrix products, arithmetic and copies ran while one was open for 2% -> 1% of each run, Pallas kernels for 13% -> 7%
where the time goes in v12:
time: 177 us; the launch traced here: 176 us
  waiting for transfers between devices  65.3 us (37%)
  starting transfers between devices  53.1 us (30%)
  Pallas kernels  40.7 us (23%)
  local copies, waits for them, and re-layouts  13.7 us (8%)
  other arithmetic  2.68 us (2%)
    ppermute x15, waiting for transfers between devices, across(): lax.ppermute(pieces[k], 'fft', [(z, z ^ k) for z in range(shards)])  53.2 us
    ppermute x15, starting transfers between devices, across(): lax.ppermute(pieces[k], 'fft', [(z, z ^ k) for z in range(shards)])  29.9 us
    unnamed x60, local copies, waits for them, and re-layouts  12.2 us
    pallas_call x1, Pallas kernels, embed(): pl.pallas_call(body, grid_spec=pltpu.PrefetchScalarGridSpec(num_scalar_pr...  10 us
    pallas_call x2, Pallas kernels, embed_grad_parts(): pl.pallas_call(body, grid_spec=pltpu.PrefetchScalarGridSpec(num_scalar_pr...  8.59 us
    ppermute x2, starting transfers between devices, scatter_step(): received = lax.ppermute(send, 'fft', [(z, z ^ bit) for z in range(shards)])  8.58 us
    ppermute x10, starting transfers between devices, swap_bit(): lax.ppermute(values, 'grp', [(g, g ^ 1 << bit) for g in range(groups)])  7.25 us
    pallas_call x1, Pallas kernels, spectral_back_chunk(): pl.pallas_call(body, grid_spec=pltpu.PrefetchScalarGridSpec(num_scalar_pr...  6.14 us
  transfers between devices with their start and end apart: 31, of which 17 were waited for; matrix products, arithmetic and copies ran while one was open for 1% of the time, Pallas kernels for 7%

profile of v12, /device:TPU:0, one launch (start us, length us, event | category | flops | bytes accessed | tf_op | source)
XLA Modules:
  0.0 176.4 jit_solution(998935976548811906)
XLA Ops:
  2.0 10.0 %embed.1 = (bf16[384,1024]{1,0:T(8,128)(2,1)}, bf16[384,1024]{1,0:T(8,128)(2,1)}, f32[384,256]{1,0:T(8,128)}, bf16[4,320,384]{2,1,0:T(8,128)(2,1)}, bf16[4,320,3...) custom-call(s32[15]{0:T(128)} %concatenate.12.scal_ref, ...), custom_call_target="tpu_custom_call" | custom-call | flops 2013265920 | bytes 7208960 | tf_op jit(solution)/shard_map/embed/pallas_call | solution.py:157
  12.0 3.1 %collective-permute-start = (bf16[6,64,256]{2,1,0:T(8,128)(2,1)}, bf16[6,64,256]{2,1,0:T(8,128)(2,1)S(1)}, u32[]{:S(2)}, u32[]{:S(2)}) collective-permute-start(bf16[6,64,256]{2,1,0:T(8,128)(2,1)} %get-tuple-element.77), channel_id=1, source_target_pairs={{0,1},{1,0},{2,3},{3,2},{4,5},{5,4},{6,7},{7,6},{8,9},{9,8},{10,11... | collective-permute-start | bytes 589832 | tf_op jit(solution)/shard_map/ppermute | solution.py:589
  15.1 2.6 %collective-permute-start.1 = (bf16[6,64,256]{2,1,0:T(8,128)(2,1)}, bf16[6,64,256]{2,1,0:T(8,128)(2,1)S(1)}, u32[]{:S(2)}, u32[]{:S(2)}) collective-permute-start(bf16[6,64,256]{2,1,0:T(8,128)(2,1)} %get-tuple-element.78), channel_id=1, source_target_pairs={{0,2},{1,3},{2,0},{3,1},{4,6},{5,7},{6,4},{7,5},{8,10},{9,11},{10,... | collective-permute-start | bytes 589832 | tf_op jit(solution)/shard_map/ppermute | solution.py:589
  18.3 5.3 %collective-permute-done.refs_1_ = bf16[6,64,256]{2,1,0:T(8,128)(2,1)S(1)} collective-permute-done((bf16[6,64,256]{2,1,0:T(8,128)(2,1)}, bf16[6,64,256]{2,1,0:T(8,128)(2,1)S(1)}, u32[]{:S(2)}, u32[]{:S(2)}) %collective-permute-start) | collective-permute-done | bytes 196640 | tf_op jit(solution)/shard_map/ppermute | solution.py:589
  23.6 8.9 %collective-permute-done.1.refs_2_ = bf16[6,64,256]{2,1,0:T(8,128)(2,1)S(1)} collective-permute-done((bf16[6,64,256]{2,1,0:T(8,128)(2,1)}, bf16[6,64,256]{2,1,0:T(8,128)(2,1)S(1)}, u32[]{:S(2)}, u32[]{:S(2)}) %collective-permute-start.1) | collective-permute-done | bytes 196640 | tf_op jit(solution)/shard_map/ppermute | solution.py:589
  34.6 4.3 %spectral.1 = (bf16[6,64,256]{2,1,0:T(8,128)(2,1)S(1)}, bf16[6,64,256]{2,1,0:T(8,128)(2,1)}, bf16[6,64,256]{2,1,0:T(8,128)(2,1)}, bf16[6,64,256]{2,1,0:T(8,128)(...) custom-call(s32[15]{0:T(128)S(1)} %copy-done.19, ...), custom_call_target="tpu_custom_call" | custom-call | flops 1409286144 | bytes 6291456 | tf_op jit(solution)/shard_map/spectral/pallas_call | solution.py:277
  38.9 1.1 copy-done.2
  40.1 1.2 copy-done.4
  41.2 1.1 copy-done.6
  43.1 3.3 %collective-permute-start.3 = (bf16[6,64,256]{2,1,0:T(8,128)(2,1)}, bf16[6,64,256]{2,1,0:T(8,128)(2,1)S(1)}, u32[]{:S(2)}, u32[]{:S(2)}) collective-permute-start(bf16[6,64,256]{2,1,0:T(8,128)(2,1)} %get-tuple-element.86), channel_id=1, source_target_pairs={{0,1},{1,0},{2,3},{3,2},{4,5},{5,4},{6,7},{7,6},{8,9},{9,8},{10,11... | collective-permute-start | bytes 589832 | tf_op jit(solution)/shard_map/ppermute | solution.py:589
  47.4 1.5 collective-permute-start.5
  49.1 3.7 %collective-permute-done.3.refs_1_ = bf16[6,64,256]{2,1,0:T(8,128)(2,1)S(1)} collective-permute-done((bf16[6,64,256]{2,1,0:T(8,128)(2,1)}, bf16[6,64,256]{2,1,0:T(8,128)(2,1)S(1)}, u32[]{:S(2)}, u32[]{:S(2)}) %collective-permute-start.3) | collective-permute-done | bytes 196640 | tf_op jit(solution)/shard_map/ppermute | solution.py:589
  52.8 10.4 %collective-permute-done.4.refs_2_ = bf16[6,64,256]{2,1,0:T(8,128)(2,1)S(1)} collective-permute-done((bf16[6,64,256]{2,1,0:T(8,128)(2,1)}, bf16[6,64,256]{2,1,0:T(8,128)(2,1)S(1)}, u32[]{:S(2)}, u32[]{:S(2)}) %collective-permute-start.4) | collective-permute-done | bytes 196640 | tf_op jit(solution)/shard_map/ppermute | solution.py:589
  64.2 1.2 head.1
  65.4 2.7 %collective-permute-start.6 = (bf16[6,64,256]{2,1,0:T(8,128)(2,1)S(1)}, bf16[6,64,256]{2,1,0:T(8,128)(2,1)S(1)}, u32[]{:S(2)}, u32[]{:S(2)}) collective-permute-start(bf16[6,64,256]{2,1,0:T(8,128)(2,1)S(1)} %get-tuple-element.91.refs_1_.refs_0_.res_ref), channel_id=1, source_target_pairs={{0,1},{1,0},{2,3},{3,2},{4,5},{5,4},{6,7},{7,6},{8,9},{9,8},{10,11... | collective-permute-start | bytes 589832 | tf_op jit(solution)/shard_map/ppermute | solution.py:589
  69.2 1.4 collective-permute-start.8
  71.3 2.2 %collective-permute-done.6.refs_1_ = bf16[6,64,256]{2,1,0:T(8,128)(2,1)S(1)} collective-permute-done((bf16[6,64,256]{2,1,0:T(8,128)(2,1)S(1)}, bf16[6,64,256]{2,1,0:T(8,128)(2,1)S(1)}, u32[]{:S(2)}, u32[]{:S(2)}) %collective-permute-start.6) | collective-permute-done | bytes 196640 | tf_op jit(solution)/shard_map/ppermute | solution.py:589
  73.5 10.3 %collective-permute-done.7.refs_2_ = bf16[6,64,256]{2,1,0:T(8,128)(2,1)S(1)} collective-permute-done((bf16[6,64,256]{2,1,0:T(8,128)(2,1)S(1)}, bf16[6,64,256]{2,1,0:T(8,128)(2,1)S(1)}, u32[]{:S(2)}, u32[]{:S(2)}) %collective-permute-start.7) | collective-permute-done | bytes 196640 | tf_op jit(solution)/shard_map/ppermute | solution.py:589
  83.8 1.4 copy-done.7
  86.3 6.1 %spectral_back.1 = (bf16[6,64,256]{2,1,0:T(8,128)(2,1)S(1)}, bf16[6,64,256]{2,1,0:T(8,128)(2,1)}, bf16[6,64,256]{2,1,0:T(8,128)(2,1)}, bf16[6,64,256]{2,1,0:T(8,...) custom-call(s32[15]{0:T(128)S(1)} %copy-done.19, bf16[3,512,256]{2,1,0:T(8,128)(2,1)S(1)} %copy-done.12, ...), custom_call_target="tpu_custom_call" | custom-call | flops 2013265920 | bytes 6291456 | tf_op jit(solution)/shard_map/spectral_back/pallas_call | solution.py:440
  92.5 2.7 %collective-permute-start.10 = (bf16[6,64,256]{2,1,0:T(8,128)(2,1)}, bf16[6,64,256]{2,1,0:T(8,128)(2,1)S(1)}, u32[]{:S(2)}, u32[]{:S(2)}) collective-permute-start(bf16[6,64,256]{2,1,0:T(8,128)(2,1)} %get-tuple-element.103), channel_id=1, source_target_pairs={{0,1},{1,0},{2,3},{3,2},{4,5},{5,4},{6,7},{7,6},{8,9},{9,8},{10,11... | collective-permute-start | bytes 589832 | tf_op jit(solution)/shard_map/ppermute | solution.py:589
  95.1 1.8 %collective-permute-start.11 = (bf16[6,64,256]{2,1,0:T(8,128)(2,1)}, bf16[6,64,256]{2,1,0:T(8,128)(2,1)S(1)}, u32[]{:S(2)}, u32[]{:S(2)}) collective-permute-start(bf16[6,64,256]{2,1,0:T(8,128)(2,1)} %get-tuple-element.104), channel_id=1, source_target_pairs={{0,2},{1,3},{2,0},{3,1},{4,6},{5,7},{6,4},{7,5},{8,10},{9,11},{10,... | collective-permute-start | bytes 589832 | tf_op jit(solution)/shard_map/ppermute | solution.py:589
  97.0 1.4 collective-permute-start.12
  98.6 1.7 packed.1
  100.2 3.9 %all-to-all-start = ((bf16[8,256,256]{2,1,0:T(8,128)(2,1)}), bf16[8,256,256]{2,1,0:T(8,128)(2,1)S(1)}, u32[]{:S(2)}, u32[]{:S(2)}) async-start(bf16[8,256,256]{2,1,0:T(8,128)(2,1)} %packed.1), calls=%async_computation | async-start | bytes 2097152 | tf_op jit(solution)/shard_map/all_to_all | solution.py:874
  105.1 7.4 %collective-permute-done.11.refs_2_ = bf16[6,64,256]{2,1,0:T(8,128)(2,1)S(1)} collective-permute-done((bf16[6,64,256]{2,1,0:T(8,128)(2,1)}, bf16[6,64,256]{2,1,0:T(8,128)(2,1)S(1)}, u32[]{:S(2)}, u32[]{:S(2)}) %collective-permute-start.11) | collective-permute-done | bytes 196640 | tf_op jit(solution)/shard_map/ppermute | solution.py:589
  113.2 3.9 %embedded_back.1 = (bf16[384,1024]{1,0:T(8,128)(2,1)}, f32[8,1024]{1,0:T(8,128)S(1)}) custom-call(s32[15]{0:T(128)S(1)} %copy-done.19, bf16[384,1024]{1,0:T(8,128)(2,1)S(1)} %copy-done.1, f32[384,256]{1,0:T(8,128)S(1)} %copy-done.13, bf16[6,64,256]{2,1,0:T(8,128)(2,1)S(1)} %get-tuple-element.91.refs_1_.refs_0_.res_ref, bf16[1024,256]{1,0:T(8,128)(2,1)S(1)} %copy-done, ...), custom_call_target="tpu_custom_call" | custom-call | flops 201326592 | bytes 2359296 | tf_op jit(solution)/shard_map/embedded_back/pallas_call | solution.py:497
  117.7 1.8 %all-to-all-done.moved_ref = bf16[8,256,256]{2,1,0:T(8,128)(2,1)S(1)} async-done(((bf16[8,256,256]{2,1,0:T(8,128)(2,1)}), bf16[8,256,256]{2,1,0:T(8,128)(2,1)S(1)}, u32[]{:S(2)}, u32[]{:S(2)}) %all-to-all-start) | async-done | bytes 1048608 | tf_op jit(solution)/shard_map/all_to_all | solution.py:874
  120.2 1.2 copy-done.25
  121.4 4.3 %embed_grad.2 = (bf16[2,320,512]{2,1,0:T(8,128)(2,1)S(1)}, bf16[2,320,512]{2,1,0:T(8,128)(2,1)S(1)}) custom-call(s32[15]{0:T(128)S(1)} %copy-done.19, bf16[4,320,384]{2,1,0:T(8,128)(2,1)S(1)} %copy-done.25, bf16[4,320,384]{2,1,0:T(8,128)(2,1)} %collective-permute-done.9.refs_1_, bf16[384,1024]{1,0:T(8,128)(2,1)} %get-tuple-element.110.refs_2_, ...), custom_call_target="tpu_custom_call" | custom-call | flops 1006632960 | bytes 4063232 | tf_op jit(solution)/shard_map/embed_grad/pallas_call | solution.py:555
  125.8 1.6 collective-permute-start.14
  127.3 1.5 collective-permute-start.16
  128.8 4.3 %embed_grad.3 = (bf16[2,320,512]{2,1,0:T(8,128)(2,1)S(1)}, bf16[2,320,512]{2,1,0:T(8,128)(2,1)S(1)}) custom-call(s32[15]{0:T(128)S(1)} %copy-done.19, bf16[4,320,384]{2,1,0:T(8,128)(2,1)S(1)} %copy-done.26, bf16[4,320,384]{2,1,0:T(8,128)(2,1)} %collective-permute-done.9.refs_1_, bf16[384,1024]{1,0:T(8,128)(2,1)} %get-tuple-element.110.refs_2_, ...), custom_call_target="tpu_custom_call" | custom-call | flops 1006632960 | bytes 4063232 | tf_op jit(solution)/shard_map/embed_grad/pallas_call | solution.py:555
  133.2 1.3 group_sums.1
  134.4 4.1 %collective-permute-start.18 = (bf16[224,256]{1,0:T(8,128)(2,1)S(1)}, bf16[224,256]{1,0:T(8,128)(2,1)S(1)}, u32[]{:S(2)}, u32[]{:S(2)}) collective-permute-start(bf16[224,256]{1,0:T(8,128)(2,1)S(1)} %get-tuple-element.128.refs_0_), channel_id=1, source_target_pairs={{0,1},{1,0},{2,3},{3,2},{4,5},{5,4},{6,7},{7,6},{8,9},{9,8},{10,11... | collective-permute-start | bytes 344072 | tf_op jit(solution)/shard_map/ppermute | solution.py:589
  138.6 1.8 %collective-permute-start.19 = (bf16[224,256]{1,0:T(8,128)(2,1)S(1)}, bf16[224,256]{1,0:T(8,128)(2,1)S(1)}, u32[]{:S(2)}, u32[]{:S(2)}) collective-permute-start(bf16[224,256]{1,0:T(8,128)(2,1)S(1)} %get-tuple-element.128.refs_0_), channel_id=1, source_target_pairs={{0,2},{1,3},{2,0},{3,1},{4,6},{5,7},{6,4},{7,5},{8,10},{9,11},{10,... | collective-permute-start | bytes 344072 | tf_op jit(solution)/shard_map/ppermute | solution.py:589
  140.3 1.5 collective-permute-start.20
  142.8 1.6 collective-permute-start.15
  144.6 1.6 collective-permute-start.17
  146.2 4.0 %collective-permute-done.19.refs_2_ = bf16[224,256]{1,0:T(8,128)(2,1)S(1)} collective-permute-done((bf16[224,256]{1,0:T(8,128)(2,1)S(1)}, bf16[224,256]{1,0:T(8,128)(2,1)S(1)}, u32[]{:S(2)}, u32[]{:S(2)}) %collective-permute-start.19) | collective-permute-done | bytes 114720 | tf_op jit(solution)/shard_map/ppermute | solution.py:589
  151.9 1.4 collective-permute-done.17
  153.5 4.2 %collective-permute-start.21 = (bf16[2,80,1024]{2,1,0:T(8,128)(2,1)S(1)}, bf16[2,80,1024]{2,1,0:T(8,128)(2,1)S(1)}, u32[]{:S(2)}, u32[]{:S(2)}) collective-permute-start(bf16[2,80,1024]{2,1,0:T(8,128)(2,1)S(1)} %dynamic-slice_bitcast_fusion), channel_id=1, source_target_pairs={{0,1},{1,0},{2,3},{3,2},{4,5},{5,4},{6,7},{7,6},{8,9},{9,8},{10,11... | collective-permute-start | bytes 983048 | tf_op jit(solution)/shard_map/ppermute | solution.py:623
  157.7 1.5 collective-permute-start.23
  159.7 1.5 collective-permute-start.25
  161.2 2.5 %collective-permute-done.21 = bf16[2,80,1024]{2,1,0:T(8,128)(2,1)S(1)} collective-permute-done((bf16[2,80,1024]{2,1,0:T(8,128)(2,1)S(1)}, bf16[2,80,1024]{2,1,0:T(8,128)(2,1)S(1)}, u32[]{:S(2)}, u32[]{:S(2)}) %collective-permute-start.21) | collective-permute-done | bytes 327712 | tf_op jit(solution)/shard_map/ppermute | solution.py:623
  163.8 4.4 %collective-permute-start.22 = (bf16[1,80,1024]{2,1,0:T(8,128)(2,1)S(1)}, bf16[1,80,1024]{2,1,0:T(8,128)(2,1)S(1)}, u32[]{:S(2)}, u32[]{:S(2)}) collective-permute-start(bf16[1,80,1024]{2,1,0:T(8,128)(2,1)S(1)} %constant_dynamic-slice_fusion), channel_id=1, source_target_pairs={{0,2},{1,3},{2,0},{3,1},{4,6},{5,7},{6,4},{7,5},{8,10},{9,11},{10,... | collective-permute-start | bytes 491528 | tf_op jit(solution)/shard_map/ppermute | solution.py:623
  170.2 2.8 %collective-permute-done.22 = bf16[1,80,1024]{2,1,0:T(8,128)(2,1)S(1)} collective-permute-done((bf16[1,80,1024]{2,1,0:T(8,128)(2,1)S(1)}, bf16[1,80,1024]{2,1,0:T(8,128)(2,1)S(1)}, u32[]{:S(2)}, u32[]{:S(2)}) %collective-permute-start.22) | collective-permute-done | bytes 163872 | tf_op jit(solution)/shard_map/ppermute | solution.py:623
  173.8 2.5 %assembled.1 = (f32[1024,256]{1,0:T(8,128)}, f32[2,2,8,128,128]{4,3,2,1,0:T(8,128)}, f32[2,2,8,128]{3,2,1,0:T(8,128)}, f32[1,1024]{1,0:T(1,128)}, f32[1,1024]{1,0:T(1,128)}, /*index=5*/f32[1,256]{1,0:T(1,128)}) custom-call(s32[15]{0:T(128)S(1)} %copy-done.19, bf16[448,256]{1,0:T(8,128)(2,1)S(1)} %shard_sums.1.refs_0_, ...), custom_call_target="tpu_custom_call" | custom-call | tf_op jit(solution)/shard_map/assembled/pallas_call | solution.py:790
  (107 shorter events, 19.5 us)
Async XLA Ops:
  2.0 15.7 %copy-start.28 = (s32[48]{0:T(128)S(1)}, s32[48]{0:T(128)}, u32[]{:S(2)}) copy-start(s32[48]{0:T(128)} %param.15) | copy-start | bytes 580
  2.0 30.5 %copy-start.8 = (bf16[2,2,8,128,128]{4,3,2,1,0:T(8,128)(2,1)S(1)}, bf16[2,2,8,128,128]{4,3,2,1,0:T(8,128)(2,1)}, u32[]{:S(2)}) copy-start(bf16[2,2,8,128,128]{4,3,2,1,0:T(8,128)(2,1)} %w_ref.8) | copy-start | bytes 3145732
  2.0 30.5 %copy-start.19 = (s32[15]{0:T(128)S(1)}, s32[15]{0:T(128)}, u32[]{:S(2)}) copy-start(s32[15]{0:T(128)} %concatenate.12.scal_ref) | copy-start | bytes 184
  2.0 30.5 %copy-start.24 = (f32[2,2,8,128]{3,2,1,0:T(8,128)S(1)}, f32[2,2,8,128]{3,2,1,0:T(8,128)}, u32[]{:S(2)}) copy-start(f32[2,2,8,128]{3,2,1,0:T(8,128)} %b_ref.1) | copy-start | bytes 49156
  12.0 11.5 %collective-permute-start = (bf16[6,64,256]{2,1,0:T(8,128)(2,1)}, bf16[6,64,256]{2,1,0:T(8,128)(2,1)S(1)}, u32[]{:S(2)}, u32[]{:S(2)}) collective-permute-start(bf16[6,64,256]{2,1,0:T(8,128)(2,1)} %get-tuple-element.77), channel_id=1, source_target_pairs={{0,1},{1,0},{2,3},{3,2},{4,5},{5,4},{6,7},{7,6},{8,9},{9,8},{10,11... | collective-permute-start | bytes 589832 | tf_op jit(solution)/shard_map/ppermute | solution.py:589
  15.1 17.4 %collective-permute-start.1 = (bf16[6,64,256]{2,1,0:T(8,128)(2,1)}, bf16[6,64,256]{2,1,0:T(8,128)(2,1)S(1)}, u32[]{:S(2)}, u32[]{:S(2)}) collective-permute-start(bf16[6,64,256]{2,1,0:T(8,128)(2,1)} %get-tuple-element.78), channel_id=1, source_target_pairs={{0,2},{1,3},{2,0},{3,1},{4,6},{5,7},{6,4},{7,5},{8,10},{9,11},{10,... | collective-permute-start | bytes 589832 | tf_op jit(solution)/shard_map/ppermute | solution.py:589
  17.7 14.8 %collective-permute-start.2 = (bf16[6,64,256]{2,1,0:T(8,128)(2,1)}, bf16[6,64,256]{2,1,0:T(8,128)(2,1)S(1)}, u32[]{:S(2)}, u32[]{:S(2)}) collective-permute-start(bf16[6,64,256]{2,1,0:T(8,128)(2,1)} %get-tuple-element.79), channel_id=1, source_target_pairs={{0,3},{1,2},{2,1},{3,0},{4,7},{5,6},{6,5},{7,4},{8,11},{9,10},{10,... | collective-permute-start | bytes 589832 | tf_op jit(solution)/shard_map/ppermute | solution.py:589
  34.6 28.7 %copy-start = (bf16[1024,256]{1,0:T(8,128)(2,1)S(1)}, bf16[1024,256]{1,0:T(8,128)(2,1)}, u32[]{:S(2)}) copy-start(bf16[1024,256]{1,0:T(8,128)(2,1)} %w_ref.9) | copy-start | bytes 1572868
  34.6 28.7 %copy-start.1 = (bf16[384,1024]{1,0:T(8,128)(2,1)S(1)}, bf16[384,1024]{1,0:T(8,128)(2,1)}, u32[]{:S(2)}) copy-start(bf16[384,1024]{1,0:T(8,128)(2,1)} %get-tuple-element.83.emb_ref) | copy-start | bytes 2359300
  34.6 28.7 %copy-start.10 = (bf16[384,1024]{1,0:T(8,128)(2,1)S(1)}, bf16[384,1024]{1,0:T(8,128)(2,1)}, u32[]{:S(2)}) copy-start(bf16[384,1024]{1,0:T(8,128)(2,1)} %get-tuple-element.84.norm_ref) | copy-start | bytes 2359300
  34.6 28.7 %copy-start.14 = (bf16[6,4,16,256]{3,2,1,0:T(8,128)(2,1)S(1)}, bf16[6,4,16,256]{3,2,1,0:T(8,128)(2,1)}, u32[]{:S(2)}) copy-start(bf16[6,4,16,256]{3,2,1,0:T(8,128)(2,1)} %param.13) | copy-start | bytes 589828
  34.6 28.7 %copy-start.23 = (f32[256]{0:T(256)S(1)}, f32[256]{0:T(256)}, u32[]{:S(2)}) copy-start(f32[256]{0:T(256)} %param.22) | copy-start | bytes 3076
  43.1 9.8 %collective-permute-start.3 = (bf16[6,64,256]{2,1,0:T(8,128)(2,1)}, bf16[6,64,256]{2,1,0:T(8,128)(2,1)S(1)}, u32[]{:S(2)}, u32[]{:S(2)}) collective-permute-start(bf16[6,64,256]{2,1,0:T(8,128)(2,1)} %get-tuple-element.86), channel_id=1, source_target_pairs={{0,1},{1,0},{2,3},{3,2},{4,5},{5,4},{6,7},{7,6},{8,9},{9,8},{10,11... | collective-permute-start | bytes 589832 | tf_op jit(solution)/shard_map/ppermute | solution.py:589
  46.4 16.9 %collective-permute-start.4 = (bf16[6,64,256]{2,1,0:T(8,128)(2,1)}, bf16[6,64,256]{2,1,0:T(8,128)(2,1)S(1)}, u32[]{:S(2)}, u32[]{:S(2)}) collective-permute-start(bf16[6,64,256]{2,1,0:T(8,128)(2,1)} %get-tuple-element.87), channel_id=1, source_target_pairs={{0,2},{1,3},{2,0},{3,1},{4,6},{5,7},{6,4},{7,5},{8,10},{9,11},{10,... | collective-permute-start | bytes 589832 | tf_op jit(solution)/shard_map/ppermute | solution.py:589
  47.4 15.9 %collective-permute-start.5 = (bf16[6,64,256]{2,1,0:T(8,128)(2,1)S(1)}, bf16[6,64,256]{2,1,0:T(8,128)(2,1)S(1)}, u32[]{:S(2)}, u32[]{:S(2)}) collective-permute-start(bf16[6,64,256]{2,1,0:T(8,128)(2,1)S(1)} %get-tuple-element.88), channel_id=1, source_target_pairs={{0,3},{1,2},{2,1},{3,0},{4,7},{5,6},{6,5},{7,4},{8,11},{9,10},{10,... | collective-permute-start | bytes 589832 | tf_op jit(solution)/shard_map/ppermute | solution.py:589
  64.2 19.6 %copy-start.3 = (bf16[2,1536,256]{2,1,0:T(8,128)(2,1)S(1)}, bf16[2,1536,256]{2,1,0:T(8,128)(2,1)}, u32[]{:S(2)}) copy-start(bf16[2,1536,256]{2,1,0:T(8,128)(2,1)} %copy-done.2) | copy-start | bytes 4718596
  64.2 19.6 %copy-start.5 = (bf16[2,1536,256]{2,1,0:T(8,128)(2,1)S(1)}, bf16[2,1536,256]{2,1,0:T(8,128)(2,1)}, u32[]{:S(2)}) copy-start(bf16[2,1536,256]{2,1,0:T(8,128)(2,1)} %copy-done.4) | copy-start | bytes 4718596
  65.4 18.4 %copy-start.9 = (bf16[2,2,8,128,128]{4,3,2,1,0:T(8,128)(2,1)S(1)}, bf16[2,2,8,128,128]{4,3,2,1,0:T(8,128)(2,1)}, u32[]{:S(2)}) copy-start(bf16[2,2,8,128,128]{4,3,2,1,0:T(8,128)(2,1)} %w_ref.8) | copy-start | bytes 3145732
  65.4 8.1 %collective-permute-start.6 = (bf16[6,64,256]{2,1,0:T(8,128)(2,1)S(1)}, bf16[6,64,256]{2,1,0:T(8,128)(2,1)S(1)}, u32[]{:S(2)}, u32[]{:S(2)}) collective-permute-start(bf16[6,64,256]{2,1,0:T(8,128)(2,1)S(1)} %get-tuple-element.91.refs_1_.refs_0_.res_ref), channel_id=1, source_target_pairs={{0,1},{1,0},{2,3},{3,2},{4,5},{5,4},{6,7},{7,6},{8,9},{9,8},{10,11... | collective-permute-start | bytes 589832 | tf_op jit(solution)/shard_map/ppermute | solution.py:589
  68.1 15.6 %collective-permute-start.7 = (bf16[6,64,256]{2,1,0:T(8,128)(2,1)S(1)}, bf16[6,64,256]{2,1,0:T(8,128)(2,1)S(1)}, u32[]{:S(2)}, u32[]{:S(2)}) collective-permute-start(bf16[6,64,256]{2,1,0:T(8,128)(2,1)S(1)} %get-tuple-element.91.refs_1_.refs_0_.res_ref), channel_id=1, source_target_pairs={{0,2},{1,3},{2,0},{3,1},{4,6},{5,7},{6,4},{7,5},{8,10},{9,11},{10,... | collective-permute-start | bytes 589832 | tf_op jit(solution)/shard_map/ppermute | solution.py:589
  69.2 14.6 %collective-permute-start.8 = (bf16[6,64,256]{2,1,0:T(8,128)(2,1)S(1)}, bf16[6,64,256]{2,1,0:T(8,128)(2,1)S(1)}, u32[]{:S(2)}, u32[]{:S(2)}) collective-permute-start(bf16[6,64,256]{2,1,0:T(8,128)(2,1)S(1)} %get-tuple-element.91.refs_1_.refs_0_.res_ref), channel_id=1, source_target_pairs={{0,3},{1,2},{2,1},{3,0},{4,7},{5,6},{6,5},{7,4},{8,11},{9,10},{10,... | collective-permute-start | bytes 589832 | tf_op jit(solution)/shard_map/ppermute | solution.py:589
  86.3 12.0 %copy-start.29 = (s32[6]{0:T(128)S(1)}, s32[6]{0:T(128)}, u32[]{:S(2)}) copy-start(s32[6]{0:T(128)} %dynamic_slice.16) | copy-start | bytes 76
  92.5 27.7 %collective-permute-start.9 = (bf16[4,320,384]{2,1,0:T(8,128)(2,1)}, bf16[4,320,384]{2,1,0:T(8,128)(2,1)}, u32[]{:S(2)}, u32[]{:S(2)}) collective-permute-start(bf16[4,320,384]{2,1,0:T(8,128)(2,1)} %get-tuple-element.100), channel_id=1, source_target_pairs={{0,4},{4,0},{8,12},{12,8},{16,20},{20,16},{24,28},{28,24},{1,5},{5... | collective-permute-start | bytes 2949128 | tf_op jit(solution)/shard_map/ppermute | solution.py:583
  92.5 12.6 %collective-permute-start.10 = (bf16[6,64,256]{2,1,0:T(8,128)(2,1)}, bf16[6,64,256]{2,1,0:T(8,128)(2,1)S(1)}, u32[]{:S(2)}, u32[]{:S(2)}) collective-permute-start(bf16[6,64,256]{2,1,0:T(8,128)(2,1)} %get-tuple-element.103), channel_id=1, source_target_pairs={{0,1},{1,0},{2,3},{3,2},{4,5},{5,4},{6,7},{7,6},{8,9},{9,8},{10,11... | collective-permute-start | bytes 589832 | tf_op jit(solution)/shard_map/ppermute | solution.py:589
  95.1 17.3 %collective-permute-start.11 = (bf16[6,64,256]{2,1,0:T(8,128)(2,1)}, bf16[6,64,256]{2,1,0:T(8,128)(2,1)S(1)}, u32[]{:S(2)}, u32[]{:S(2)}) collective-permute-start(bf16[6,64,256]{2,1,0:T(8,128)(2,1)} %get-tuple-element.104), channel_id=1, source_target_pairs={{0,2},{1,3},{2,0},{3,1},{4,6},{5,7},{6,4},{7,5},{8,10},{9,11},{10,... | collective-permute-start | bytes 589832 | tf_op jit(solution)/shard_map/ppermute | solution.py:589
  97.0 15.5 %collective-permute-start.12 = (bf16[6,64,256]{2,1,0:T(8,128)(2,1)}, bf16[6,64,256]{2,1,0:T(8,128)(2,1)}, u32[]{:S(2)}, u32[]{:S(2)}) collective-permute-start(bf16[6,64,256]{2,1,0:T(8,128)(2,1)} %get-tuple-element.105), channel_id=1, source_target_pairs={{0,3},{1,2},{2,1},{3,0},{4,7},{5,6},{6,5},{7,4},{8,11},{9,10},{10,... | collective-permute-start | bytes 589832 | tf_op jit(solution)/shard_map/ppermute | solution.py:589
  100.2 12.3 %copy-start.13 = (f32[384,256]{1,0:T(8,128)S(1)}, f32[384,256]{1,0:T(8,128)}, u32[]{:S(2)}) copy-start(f32[384,256]{1,0:T(8,128)} %get-tuple-element.101.stat_ref) | copy-start | bytes 1179652
  100.2 19.3 %all-to-all-start = ((bf16[8,256,256]{2,1,0:T(8,128)(2,1)}), bf16[8,256,256]{2,1,0:T(8,128)(2,1)S(1)}, u32[]{:S(2)}, u32[]{:S(2)}) async-start(bf16[8,256,256]{2,1,0:T(8,128)(2,1)} %packed.1), calls=%async_computation | async-start | bytes 2097152 | tf_op jit(solution)/shard_map/all_to_all | solution.py:874
  117.7 2.5 %collective-permute-start.13 = (bf16[384,1024]{1,0:T(8,128)(2,1)}, bf16[384,1024]{1,0:T(8,128)(2,1)S(1)}, u32[]{:S(2)}, u32[]{:S(2)}) collective-permute-start(bf16[384,1024]{1,0:T(8,128)(2,1)} %get-tuple-element.110.refs_2_), channel_id=1, source_target_pairs={{0,4},{4,0},{8,12},{12,8},{16,20},{20,16},{24,28},{28,24},{1,5},{5... | collective-permute-start | bytes 2359304 | tf_op jit(solution)/shard_map/ppermute | solution.py:583
  121.4 7.4 %copy-start.26 = (bf16[4,320,384]{2,1,0:T(8,128)(2,1)S(1)}, bf16[4,320,384]{2,1,0:T(8,128)(2,1)}, u32[]{:S(2)}) copy-start(bf16[4,320,384]{2,1,0:T(8,128)(2,1)} %get-tuple-element.114.refs_0_) | copy-start | bytes 2949124
  125.7 7.4 %copy-start.18 = (f32[8,1024]{1,0:T(8,128)S(1)}, f32[8,1024]{1,0:T(8,128)}, u32[]{:S(2)}) copy-start(f32[8,1024]{1,0:T(8,128)} %copy-done.17) | copy-start | bytes 98308
  125.7 7.4 %copy-start.22 = (f32[4,256]{1,0:T(4,128)S(1)}, f32[4,256]{1,0:T(4,128)}, u32[]{:S(2)}) copy-start(f32[4,256]{1,0:T(4,128)} %copy-done.21) | copy-start | bytes 12292
  125.8 16.8 %collective-permute-start.14 = (bf16[2,320,512]{2,1,0:T(8,128)(2,1)S(1)}, bf16[2,320,512]{2,1,0:T(8,128)(2,1)S(1)}, u32[]{:S(2)}, u32[]{:S(2)}) collective-permute-start(bf16[2,320,512]{2,1,0:T(8,128)(2,1)S(1)} %get-tuple-element.125), channel_id=1, source_target_pairs={{0,8},{4,12},{8,0},{12,4},{16,24},{20,28},{24,16},{28,20},{1,9},{5... | collective-permute-start | bytes 1966088 | tf_op jit(solution)/shard_map/ppermute | solution.py:583
  127.3 17.1 %collective-permute-start.16 = (bf16[2,320,512]{2,1,0:T(8,128)(2,1)S(1)}, bf16[2,320,512]{2,1,0:T(8,128)(2,1)S(1)}, u32[]{:S(2)}, u32[]{:S(2)}) collective-permute-start(bf16[2,320,512]{2,1,0:T(8,128)(2,1)S(1)} %get-tuple-element.127), channel_id=1, source_target_pairs={{0,16},{4,20},{8,24},{12,28},{16,0},{20,4},{24,8},{28,12},{1,17},{... | collective-permute-start | bytes 1966088 | tf_op jit(solution)/shard_map/ppermute | solution.py:583
  134.4 11.7 %collective-permute-start.18 = (bf16[224,256]{1,0:T(8,128)(2,1)S(1)}, bf16[224,256]{1,0:T(8,128)(2,1)S(1)}, u32[]{:S(2)}, u32[]{:S(2)}) collective-permute-start(bf16[224,256]{1,0:T(8,128)(2,1)S(1)} %get-tuple-element.128.refs_0_), channel_id=1, source_target_pairs={{0,1},{1,0},{2,3},{3,2},{4,5},{5,4},{6,7},{7,6},{8,9},{9,8},{10,11... | collective-permute-start | bytes 344072 | tf_op jit(solution)/shard_map/ppermute | solution.py:589
  138.6 11.6 %collective-permute-start.19 = (bf16[224,256]{1,0:T(8,128)(2,1)S(1)}, bf16[224,256]{1,0:T(8,128)(2,1)S(1)}, u32[]{:S(2)}, u32[]{:S(2)}) collective-permute-start(bf16[224,256]{1,0:T(8,128)(2,1)S(1)} %get-tuple-element.128.refs_0_), channel_id=1, source_target_pairs={{0,2},{1,3},{2,0},{3,1},{4,6},{5,7},{6,4},{7,5},{8,10},{9,11},{10,... | collective-permute-start | bytes 344072 | tf_op jit(solution)/shard_map/ppermute | solution.py:589
  140.3 9.8 %collective-permute-start.20 = (bf16[224,256]{1,0:T(8,128)(2,1)S(1)}, bf16[224,256]{1,0:T(8,128)(2,1)S(1)}, u32[]{:S(2)}, u32[]{:S(2)}) collective-permute-start(bf16[224,256]{1,0:T(8,128)(2,1)S(1)} %get-tuple-element.128.refs_0_), channel_id=1, source_target_pairs={{0,3},{1,2},{2,1},{3,0},{4,7},{5,6},{6,5},{7,4},{8,11},{9,10},{10,... | collective-permute-start | bytes 344072 | tf_op jit(solution)/shard_map/ppermute | solution.py:589
  142.8 9.0 %collective-permute-start.15 = (bf16[1,320,512]{2,1,0:T(8,128)(2,1)S(1)}, bf16[1,320,512]{2,1,0:T(8,128)(2,1)S(1)}, u32[]{:S(2)}, u32[]{:S(2)}) collective-permute-start(bf16[1,320,512]{2,1,0:T(8,128)(2,1)S(1)} %slice_bitcast_fusion), channel_id=1, source_target_pairs={{0,16},{4,20},{8,24},{12,28},{16,0},{20,4},{24,8},{28,12},{1,17},{... | collective-permute-start | bytes 983048 | tf_op jit(solution)/shard_map/ppermute | solution.py:583
  144.6 8.7 %collective-permute-start.17 = (bf16[1,320,512]{2,1,0:T(8,128)(2,1)S(1)}, bf16[1,320,512]{2,1,0:T(8,128)(2,1)S(1)}, u32[]{:S(2)}, u32[]{:S(2)}) collective-permute-start(bf16[1,320,512]{2,1,0:T(8,128)(2,1)S(1)} %slice.21), channel_id=1, source_target_pairs={{0,8},{4,12},{8,0},{12,4},{16,24},{20,28},{24,16},{28,20},{1,9},{5... | collective-permute-start | bytes 983048 | tf_op jit(solution)/shard_map/ppermute | solution.py:583
  153.5 10.2 %collective-permute-start.21 = (bf16[2,80,1024]{2,1,0:T(8,128)(2,1)S(1)}, bf16[2,80,1024]{2,1,0:T(8,128)(2,1)S(1)}, u32[]{:S(2)}, u32[]{:S(2)}) collective-permute-start(bf16[2,80,1024]{2,1,0:T(8,128)(2,1)S(1)} %dynamic-slice_bitcast_fusion), channel_id=1, source_target_pairs={{0,1},{1,0},{2,3},{3,2},{4,5},{5,4},{6,7},{7,6},{8,9},{9,8},{10,11... | collective-permute-start | bytes 983048 | tf_op jit(solution)/shard_map/ppermute | solution.py:623
  157.7 10.5 %collective-permute-start.23 = (bf16[448,256]{1,0:T(8,128)(2,1)S(1)}, bf16[448,256]{1,0:T(8,128)(2,1)S(1)}, u32[]{:S(2)}, u32[]{:S(2)}) collective-permute-start(bf16[448,256]{1,0:T(8,128)(2,1)S(1)} %shard_sums.1.refs_0_), channel_id=1, source_target_pairs={{0,8},{4,12},{8,0},{12,4},{16,24},{20,28},{24,16},{28,20},{1,9},{5... | collective-permute-start | bytes 688136 | tf_op jit(solution)/shard_map/ppermute | solution.py:629
  159.2 10.0 %collective-permute-start.24 = (bf16[448,256]{1,0:T(8,128)(2,1)S(1)}, bf16[448,256]{1,0:T(8,128)(2,1)S(1)}, u32[]{:S(2)}, u32[]{:S(2)}) collective-permute-start(bf16[448,256]{1,0:T(8,128)(2,1)S(1)} %shard_sums.1.refs_0_), channel_id=1, source_target_pairs={{0,16},{4,20},{8,24},{12,28},{16,0},{20,4},{24,8},{28,12},{1,17},{... | collective-permute-start | bytes 688136 | tf_op jit(solution)/shard_map/ppermute | solution.py:629
  159.7 9.5 %collective-permute-start.25 = (bf16[448,256]{1,0:T(8,128)(2,1)S(1)}, bf16[448,256]{1,0:T(8,128)(2,1)S(1)}, u32[]{:S(2)}, u32[]{:S(2)}) collective-permute-start(bf16[448,256]{1,0:T(8,128)(2,1)S(1)} %shard_sums.1.refs_0_), channel_id=1, source_target_pairs={{0,24},{4,28},{8,16},{12,20},{16,8},{20,12},{24,0},{28,4},{1,25},{... | collective-permute-start | bytes 688136 | tf_op jit(solution)/shard_map/ppermute | solution.py:629
  163.8 9.2 %collective-permute-start.22 = (bf16[1,80,1024]{2,1,0:T(8,128)(2,1)S(1)}, bf16[1,80,1024]{2,1,0:T(8,128)(2,1)S(1)}, u32[]{:S(2)}, u32[]{:S(2)}) collective-permute-start(bf16[1,80,1024]{2,1,0:T(8,128)(2,1)S(1)} %constant_dynamic-slice_fusion), channel_id=1, source_target_pairs={{0,2},{1,3},{2,0},{3,1},{4,6},{5,7},{6,4},{7,5},{8,10},{9,11},{10,... | collective-permute-start | bytes 491528 | tf_op jit(solution)/shard_map/ppermute | solution.py:623
  169.2 4.6 %collective-permute-start.26 = (bf16[448,256]{1,0:T(8,128)(2,1)S(1)}, bf16[448,256]{1,0:T(8,128)(2,1)S(1)}, u32[]{:S(2)}, u32[]{:S(2)}) collective-permute-start(bf16[448,256]{1,0:T(8,128)(2,1)S(1)} %shard_sums.1.refs_0_), channel_id=1, source_target_pairs={{0,4},{4,0},{8,12},{12,8},{16,20},{20,16},{24,28},{28,24},{1,5},{5... | collective-permute-start | bytes 688136 | tf_op jit(solution)/shard_map/ppermute | solution.py:583
  169.2 4.6 %collective-permute-start.27 = (bf16[448,256]{1,0:T(8,128)(2,1)S(1)}, bf16[448,256]{1,0:T(8,128)(2,1)S(1)}, u32[]{:S(2)}, u32[]{:S(2)}) collective-permute-start(bf16[448,256]{1,0:T(8,128)(2,1)S(1)} %collective-permute-done.23.refs_2_), channel_id=1, source_target_pairs={{0,4},{4,0},{8,12},{12,8},{16,20},{20,16},{24,28},{28,24},{1,5},{5... | collective-permute-start | bytes 688136 | tf_op jit(solution)/shard_map/ppermute | solution.py:583
  169.7 4.1 %collective-permute-start.28 = (bf16[448,256]{1,0:T(8,128)(2,1)S(1)}, bf16[448,256]{1,0:T(8,128)(2,1)S(1)}, u32[]{:S(2)}, u32[]{:S(2)}) collective-permute-start(bf16[448,256]{1,0:T(8,128)(2,1)S(1)} %collective-permute-done.24.refs_4_), channel_id=1, source_target_pairs={{0,4},{4,0},{8,12},{12,8},{16,20},{20,16},{24,28},{28,24},{1,5},{5... | collective-permute-start | bytes 688136 | tf_op jit(solution)/shard_map/ppermute | solution.py:583
  169.7 4.1 %collective-permute-start.29 = (bf16[448,256]{1,0:T(8,128)(2,1)S(1)}, bf16[448,256]{1,0:T(8,128)(2,1)S(1)}, u32[]{:S(2)}, u32[]{:S(2)}) collective-permute-start(bf16[448,256]{1,0:T(8,128)(2,1)S(1)} %collective-permute-done.25.refs_6_), channel_id=1, source_target_pairs={{0,4},{4,0},{8,12},{12,8},{16,20},{20,16},{24,28},{28,24},{1,5},{5... | collective-permute-start | bytes 688136 | tf_op jit(solution)/shard_map/ppermute | solution.py:583
  (13 other events, 18.1 us)

commit v13 on v11

--- a/solution.py
+++ b/solution.py
@@ -885,7 +885,7 @@
         row_sums.append(row_sum)
     grads = own_grads + other_grads
     sent = embed_grad_parts(scal, turned, grads, groups, 1)
-    _, kept_turned, weight_sums = lax.optimization_barrier((sent, turned, weight_sums))
+    sent, kept_turned = lax.optimization_barrier((sent, turned))
     top_bit = groups.bit_length() - 2
     received = [swap_bit(sent[0], 1, groups), swap_bit(sent[1], top_bit, groups)]
     kept = embed_grad_parts(scal, kept_turned, grads, groups, 0)

time: 169 us -> 169 us (level)
  local copies, waits for them, and re-layouts: 21.4 us -> 14.5 us
  waiting for transfers between devices: 30.9 us -> 34.3 us
  starting transfers between devices: 68.7 us -> 71.5 us
    ppermute x11, waiting for transfers between devices: 3.57 us -> 10.8 us  [swap_bit(): lax.ppermute(values, 'grp', [(g, g ^ 1 << bit) for g in range(groups)])]
    unnamed x108 -> x104, local copies, waits for them, and re-layouts: 20.4 us -> 13.6 us
    ppermute x27, waiting for transfers between devices: 18.4 us -> 14.8 us  [across(): lax.ppermute(pieces[k], 'fft', [(z, z ^ k) for z in range(shards)])]
    ppermute x2, waiting for transfers between devices: 4.45 us -> 6.75 us  [scatter_step(): received = lax.ppermute(send, 'fft', [(z, z ^ bit) for z in range(shards)])]
    ppermute x2, starting transfers between devices: 4.12 us -> 6.03 us  [scatter_step(): received = lax.ppermute(send, 'fft', [(z, z ^ bit) for z in range(shards)])]
where the time goes in v13:
time: 169 us
  starting transfers between devices  71.5 us (42%)
  Pallas kernels  41 us (24%)
  waiting for transfers between devices  34.3 us (20%)
  local copies, waits for them, and re-layouts  14.5 us (9%)
  other arithmetic  5.9 us (3%)
    ppermute x27, starting transfers between devices, across(): lax.ppermute(pieces[k], 'fft', [(z, z ^ k) for z in range(shards)])  51 us
    ppermute x27, waiting for transfers between devices, across(): lax.ppermute(pieces[k], 'fft', [(z, z ^ k) for z in range(shards)])  14.8 us
    unnamed x104, local copies, waits for them, and re-layouts  13.6 us
    ppermute x11, waiting for transfers between devices, swap_bit(): lax.ppermute(values, 'grp', [(g, g ^ 1 << bit) for g in range(groups)])  10.8 us
    pallas_call x1, Pallas kernels, embed(): pl.pallas_call(body, grid_spec=pltpu.PrefetchScalarGridSpec(num_scalar_pr...  10 us
    pallas_call x2, Pallas kernels, embed_grad_parts(): pl.pallas_call(body, grid_spec=pltpu.PrefetchScalarGridSpec(num_scalar_pr...  8.9 us
    ppermute x11, starting transfers between devices, swap_bit(): lax.ppermute(values, 'grp', [(g, g ^ 1 << bit) for g in range(groups)])  7.07 us
    ppermute x2, waiting for transfers between devices, scatter_step(): received = lax.ppermute(send, 'fft', [(z, z ^ bit) for z in range(shards)])  6.75 us
  transfers between devices with their start and end apart: 44, of which 12 were waited for; matrix products, arithmetic and copies ran while one was open for 3% of the time, Pallas kernels for 15%

profile of v13, /device:TPU:0, one launch (start us, length us, event | category | flops | bytes accessed | tf_op | source)
XLA Modules:
  0.0 168.6 jit_solution(10116515557834540399)
XLA Ops:
  2.0 10.0 %embed.1 = (bf16[384,1024]{1,0:T(8,128)(2,1)}, bf16[384,1024]{1,0:T(8,128)(2,1)}, f32[384,256]{1,0:T(8,128)}, bf16[4,320,384]{2,1,0:T(8,128)(2,1)}, bf16[4,320,3...) custom-call(s32[15]{0:T(128)} %concatenate.12.scal_ref, ...), custom_call_target="tpu_custom_call" | custom-call | flops 2013265920 | bytes 7208960 | tf_op jit(solution)/shard_map/embed/pallas_call | solution.py:157
  12.0 4.1 %collective-permute-start.10 = (bf16[3,64,256]{2,1,0:T(8,128)(2,1)}, bf16[3,64,256]{2,1,0:T(8,128)(2,1)S(1)}, u32[]{:S(2)}, u32[]{:S(2)}) collective-permute-start(bf16[3,64,256]{2,1,0:T(8,128)(2,1)} %get-tuple-element.119), channel_id=1, source_target_pairs={{0,2},{1,3},{2,0},{3,1},{4,6},{5,7},{6,4},{7,5},{8,10},{9,11},{10,... | collective-permute-start | bytes 294920 | tf_op jit(solution)/shard_map/ppermute | solution.py:589
  16.1 1.3 collective-permute-start.11
  17.7 1.8 %collective-permute-start = (bf16[3,64,256]{2,1,0:T(8,128)(2,1)}, bf16[3,64,256]{2,1,0:T(8,128)(2,1)S(1)}, u32[]{:S(2)}, u32[]{:S(2)}) collective-permute-start(bf16[3,64,256]{2,1,0:T(8,128)(2,1)} %get-tuple-element.104), channel_id=1, source_target_pairs={{0,1},{1,0},{2,3},{3,2},{4,5},{5,4},{6,7},{7,6},{8,9},{9,8},{10,11... | collective-permute-start | bytes 294920 | tf_op jit(solution)/shard_map/ppermute | solution.py:589
  19.5 1.7 %collective-permute-start.1 = (bf16[3,64,256]{2,1,0:T(8,128)(2,1)}, bf16[3,64,256]{2,1,0:T(8,128)(2,1)S(1)}, u32[]{:S(2)}, u32[]{:S(2)}) collective-permute-start(bf16[3,64,256]{2,1,0:T(8,128)(2,1)} %get-tuple-element.105), channel_id=1, source_target_pairs={{0,2},{1,3},{2,0},{3,1},{4,6},{5,7},{6,4},{7,5},{8,10},{9,11},{10,... | collective-permute-start | bytes 294920 | tf_op jit(solution)/shard_map/ppermute | solution.py:589
  21.2 3.0 %collective-permute-done.10.refs_2_ = bf16[3,64,256]{2,1,0:T(8,128)(2,1)S(1)} collective-permute-done((bf16[3,64,256]{2,1,0:T(8,128)(2,1)}, bf16[3,64,256]{2,1,0:T(8,128)(2,1)S(1)}, u32[]{:S(2)}, u32[]{:S(2)}) %collective-permute-start.10) | collective-permute-done | bytes 98336 | tf_op jit(solution)/shard_map/ppermute | solution.py:589
  24.2 2.8 %collective-permute-start.2 = (bf16[3,64,256]{2,1,0:T(8,128)(2,1)}, bf16[3,64,256]{2,1,0:T(8,128)(2,1)S(1)}, u32[]{:S(2)}, u32[]{:S(2)}) collective-permute-start(bf16[3,64,256]{2,1,0:T(8,128)(2,1)} %get-tuple-element.106), channel_id=1, source_target_pairs={{0,3},{1,2},{2,1},{3,0},{4,7},{5,6},{6,5},{7,4},{8,11},{9,10},{10,... | collective-permute-start | bytes 294920 | tf_op jit(solution)/shard_map/ppermute | solution.py:589
  28.0 2.3 %spectral.3 = (bf16[3,64,256]{2,1,0:T(8,128)(2,1)S(1)}, bf16[3,64,256]{2,1,0:T(8,128)(2,1)S(1)}, bf16[3,64,256]{2,1,0:T(8,128)(2,1)S(1)}, bf16[3,64,256]{2,1,0:T...) custom-call(s32[15]{0:T(128)S(1)} %copy-done.23, ...), custom_call_target="tpu_custom_call" | custom-call | flops 704643072 | bytes 3145728 | tf_op jit(solution)/shard_map/spectral/pallas_call | solution.py:277
  31.3 1.6 collective-permute-start.13
  32.8 1.9 %collective-permute-start.14 = (bf16[3,64,256]{2,1,0:T(8,128)(2,1)S(1)}, bf16[3,64,256]{2,1,0:T(8,128)(2,1)S(1)}, u32[]{:S(2)}, u32[]{:S(2)}) collective-permute-start(bf16[3,64,256]{2,1,0:T(8,128)(2,1)S(1)} %get-tuple-element.127), channel_id=1, source_target_pairs={{0,3},{1,2},{2,1},{3,0},{4,7},{5,6},{6,5},{7,4},{8,11},{9,10},{10,... | collective-permute-start | bytes 294920 | tf_op jit(solution)/shard_map/ppermute | solution.py:589
  34.8 2.3 %spectral.2 = (bf16[3,64,256]{2,1,0:T(8,128)(2,1)S(1)}, bf16[3,64,256]{2,1,0:T(8,128)(2,1)S(1)}, bf16[3,64,256]{2,1,0:T(8,128)(2,1)S(1)}, bf16[3,64,256]{2,1,0:T...) custom-call(s32[15]{0:T(128)S(1)} %copy-done.23, ...), custom_call_target="tpu_custom_call" | custom-call | flops 704643072 | bytes 3145728 | tf_op jit(solution)/shard_map/spectral/pallas_call | solution.py:277
  37.5 2.2 %collective-permute-start.4 = (bf16[3,64,256]{2,1,0:T(8,128)(2,1)S(1)}, bf16[3,64,256]{2,1,0:T(8,128)(2,1)S(1)}, u32[]{:S(2)}, u32[]{:S(2)}) collective-permute-start(bf16[3,64,256]{2,1,0:T(8,128)(2,1)S(1)} %get-tuple-element.114), channel_id=1, source_target_pairs={{0,2},{1,3},{2,0},{3,1},{4,6},{5,7},{6,4},{7,5},{8,10},{9,11},{10,... | collective-permute-start | bytes 294920 | tf_op jit(solution)/shard_map/ppermute | solution.py:589
  39.8 1.8 %collective-permute-start.5 = (bf16[3,64,256]{2,1,0:T(8,128)(2,1)S(1)}, bf16[3,64,256]{2,1,0:T(8,128)(2,1)S(1)}, u32[]{:S(2)}, u32[]{:S(2)}) collective-permute-start(bf16[3,64,256]{2,1,0:T(8,128)(2,1)S(1)} %get-tuple-element.115), channel_id=1, source_target_pairs={{0,3},{1,2},{2,1},{3,0},{4,7},{5,6},{6,5},{7,4},{8,11},{9,10},{10,... | collective-permute-start | bytes 294920 | tf_op jit(solution)/shard_map/ppermute | solution.py:589
  42.8 6.9 %collective-permute-start.15 = (bf16[3,64,256]{2,1,0:T(8,128)(2,1)S(1)}, bf16[3,64,256]{2,1,0:T(8,128)(2,1)S(1)}, u32[]{:S(2)}, u32[]{:S(2)}) collective-permute-start(bf16[3,64,256]{2,1,0:T(8,128)(2,1)S(1)} %get-tuple-element.131.refs_2_.refs_0_.res_ref), channel_id=1, source_target_pairs={{0,1},{1,0},{2,3},{3,2},{4,5},{5,4},{6,7},{7,6},{8,9},{9,8},{10,11... | collective-permute-start | bytes 294920 | tf_op jit(solution)/shard_map/ppermute | solution.py:589
  50.7 1.5 collective-permute-start.17
  54.3 1.8 %collective-permute-start.7 = (bf16[3,64,256]{2,1,0:T(8,128)(2,1)S(1)}, bf16[3,64,256]{2,1,0:T(8,128)(2,1)S(1)}, u32[]{:S(2)}, u32[]{:S(2)}) collective-permute-start(bf16[3,64,256]{2,1,0:T(8,128)(2,1)S(1)} %get-tuple-element.116.refs_3_.refs_0_.res_ref), channel_id=1, source_target_pairs={{0,2},{1,3},{2,0},{3,1},{4,6},{5,7},{6,4},{7,5},{8,10},{9,11},{10,... | collective-permute-start | bytes 294920 | tf_op jit(solution)/shard_map/ppermute | solution.py:589
  56.1 1.5 collective-permute-start.8
  58.1 2.4 %collective-permute-done.16.refs_2_ = bf16[3,64,256]{2,1,0:T(8,128)(2,1)S(1)} collective-permute-done((bf16[3,64,256]{2,1,0:T(8,128)(2,1)S(1)}, bf16[3,64,256]{2,1,0:T(8,128)(2,1)S(1)}, u32[]{:S(2)}, u32[]{:S(2)}) %collective-permute-start.16) | collective-permute-done | bytes 98336 | tf_op jit(solution)/shard_map/ppermute | solution.py:589
  60.5 3.0 %spectral_back.2 = (bf16[3,64,256]{2,1,0:T(8,128)(2,1)S(1)}, bf16[3,64,256]{2,1,0:T(8,128)(2,1)S(1)}, bf16[3,64,256]{2,1,0:T(8,128)(2,1)S(1)}, bf16[3,64,256]{2,...) custom-call(s32[15]{0:T(128)S(1)} %copy-done.23, bf16[3,512,256]{2,1,0:T(8,128)(2,1)S(1)} %copy-done.4, ...), custom_call_target="tpu_custom_call" | custom-call | flops 1006632960 | bytes 3145728 | tf_op jit(solution)/shard_map/spectral_back/pallas_call | solution.py:440
  63.6 4.2 %collective-permute-done.7.refs_2_ = bf16[3,64,256]{2,1,0:T(8,128)(2,1)S(1)} collective-permute-done((bf16[3,64,256]{2,1,0:T(8,128)(2,1)S(1)}, bf16[3,64,256]{2,1,0:T(8,128)(2,1)S(1)}, u32[]{:S(2)}, u32[]{:S(2)}) %collective-permute-start.7) | collective-permute-done | bytes 98336 | tf_op jit(solution)/shard_map/ppermute | solution.py:589
  67.8 3.0 %spectral_back.3 = (bf16[3,64,256]{2,1,0:T(8,128)(2,1)S(1)}, bf16[3,64,256]{2,1,0:T(8,128)(2,1)S(1)}, bf16[3,64,256]{2,1,0:T(8,128)(2,1)S(1)}, bf16[3,64,256]{2,...) custom-call(s32[15]{0:T(128)S(1)} %copy-done.23, bf16[3,512,256]{2,1,0:T(8,128)(2,1)S(1)} %copy-done.4, ...), custom_call_target="tpu_custom_call" | custom-call | flops 1006632960 | bytes 3145728 | tf_op jit(solution)/shard_map/spectral_back/pallas_call | solution.py:440
  75.2 1.9 %collective-permute-start.19 = (bf16[3,64,256]{2,1,0:T(8,128)(2,1)}, bf16[3,64,256]{2,1,0:T(8,128)(2,1)S(1)}, u32[]{:S(2)}, u32[]{:S(2)}) collective-permute-start(bf16[3,64,256]{2,1,0:T(8,128)(2,1)} %copy-done.45), channel_id=1, source_target_pairs={{0,1},{1,0},{2,3},{3,2},{4,5},{5,4},{6,7},{7,6},{8,9},{9,8},{10,11... | collective-permute-start | bytes 294920 | tf_op jit(solution)/shard_map/ppermute | solution.py:589
  78.1 1.7 %collective-permute-start.21 = (bf16[3,64,256]{2,1,0:T(8,128)(2,1)}, bf16[3,64,256]{2,1,0:T(8,128)(2,1)S(1)}, u32[]{:S(2)}, u32[]{:S(2)}) collective-permute-start(bf16[3,64,256]{2,1,0:T(8,128)(2,1)} %copy-done.42), channel_id=1, source_target_pairs={{0,3},{1,2},{2,1},{3,0},{4,7},{5,6},{6,5},{7,4},{8,11},{9,10},{10,... | collective-permute-start | bytes 294920 | tf_op jit(solution)/shard_map/ppermute | solution.py:589
  80.8 2.9 %collective-permute-start.23 = (bf16[3,64,256]{2,1,0:T(8,128)(2,1)}, bf16[3,64,256]{2,1,0:T(8,128)(2,1)S(1)}, u32[]{:S(2)}, u32[]{:S(2)}) collective-permute-start(bf16[3,64,256]{2,1,0:T(8,128)(2,1)} %copy-done.41), channel_id=1, source_target_pairs={{0,2},{1,3},{2,0},{3,1},{4,6},{5,7},{6,4},{7,5},{8,10},{9,11},{10,... | collective-permute-start | bytes 294920 | tf_op jit(solution)/shard_map/ppermute | solution.py:589
  83.6 4.4 %collective-permute-done.20.refs_2_ = bf16[3,64,256]{2,1,0:T(8,128)(2,1)S(1)} collective-permute-done((bf16[3,64,256]{2,1,0:T(8,128)(2,1)}, bf16[3,64,256]{2,1,0:T(8,128)(2,1)S(1)}, u32[]{:S(2)}, u32[]{:S(2)}) %collective-permute-start.20) | collective-permute-done | bytes 98336 | tf_op jit(solution)/shard_map/ppermute | solution.py:589
  88.1 2.2 %collective-permute-start.24 = (bf16[3,64,256]{2,1,0:T(8,128)(2,1)}, bf16[3,64,256]{2,1,0:T(8,128)(2,1)S(1)}, u32[]{:S(2)}, u32[]{:S(2)}) collective-permute-start(bf16[3,64,256]{2,1,0:T(8,128)(2,1)} %copy-done.40), channel_id=1, source_target_pairs={{0,3},{1,2},{2,1},{3,0},{4,7},{5,6},{6,5},{7,4},{8,11},{9,10},{10,... | collective-permute-start | bytes 294920 | tf_op jit(solution)/shard_map/ppermute | solution.py:589
  92.3 1.4 embedded_back.2
  95.7 1.9 %packed.1 = bf16[8,256,256]{2,1,0:T(8,128)(2,1)} custom-call(s32[17]{0:T(128)S(1)} %concatenate.11.routes_ref, bf16[1024,256]{1,0:T(8,128)(2,1)S(1)} %copy-done.6, bf16[512,256]{1,0:T(8,128)(2,1)S(1)} %copy-done.14, bf16[3,64,256]{2,1,0:T(8,128)(2,1)S(1)} %copy-done.16, bf16[3,64,256]{2,1,0:T(8,128)(2,1)S(1)} %copy-done.18), custom_call_target="tpu_custom_call" | custom-call | tf_op jit(solution)/shard_map/packed/pallas_call | solution.py:645
  97.6 1.4 embedded_back.3
  99.7 3.9 %all-to-all-start = ((bf16[8,256,256]{2,1,0:T(8,128)(2,1)}), bf16[8,256,256]{2,1,0:T(8,128)(2,1)S(1)}, u32[]{:S(2)}, u32[]{:S(2)}) async-start(bf16[8,256,256]{2,1,0:T(8,128)(2,1)} %packed.1), calls=%async_computation | async-start | bytes 2097152 | tf_op jit(solution)/shard_map/all_to_all | solution.py:882
  106.6 4.8 %embed_grad.2 = (bf16[2,320,512]{2,1,0:T(8,128)(2,1)S(1)}, bf16[2,320,512]{2,1,0:T(8,128)(2,1)}) custom-call(s32[15]{0:T(128)S(1)} %copy-done.23, bf16[4,320,384]{2,1,0:T(8,128)(2,1)S(1)} %copy-done.47, bf16[4,320,384]{2,1,0:T(8,128)(2,1)} %collective-permute-done.18.refs_1_, bf16[192,1024]{1,0:T(8,128)(2,1)S(1)} %copy-done.31, ...), custom_call_target="tpu_custom_call" | custom-call | flops 1006632960 | bytes 4063232 | tf_op jit(solution)/shard_map/embed_grad/pallas_call | solution.py:555
  111.5 2.1 %collective-permute-start.29 = (bf16[2,320,512]{2,1,0:T(8,128)(2,1)}, bf16[2,320,512]{2,1,0:T(8,128)(2,1)}, u32[]{:S(2)}, u32[]{:S(2)}) collective-permute-start(bf16[2,320,512]{2,1,0:T(8,128)(2,1)} %get-tuple-element.181), channel_id=1, source_target_pairs={{0,16},{4,20},{8,24},{12,28},{16,0},{20,4},{24,8},{28,12},{1,17},{... | collective-permute-start | bytes 1966088 | tf_op jit(solution)/shard_map/ppermute | solution.py:583
  113.5 1.5 collective-permute-start.27
  117.0 4.1 %embed_grad.3 = (bf16[2,320,512]{2,1,0:T(8,128)(2,1)S(1)}, bf16[2,320,512]{2,1,0:T(8,128)(2,1)S(1)}) custom-call(s32[15]{0:T(128)S(1)} %copy-done.23, bf16[4,320,384]{2,1,0:T(8,128)(2,1)S(1)} %copy-done.47, bf16[4,320,384]{2,1,0:T(8,128)(2,1)} %collective-permute-done.18.refs_1_, bf16[192,1024]{1,0:T(8,128)(2,1)S(1)} %copy-done.32, ...), custom_call_target="tpu_custom_call" | custom-call | flops 1006632960 | bytes 4063232 | tf_op jit(solution)/shard_map/embed_grad/pallas_call | solution.py:555
  121.1 1.3 group_sums.1
  122.4 3.5 %collective-permute-start.31 = (bf16[224,256]{1,0:T(8,128)(2,1)S(1)}, bf16[224,256]{1,0:T(8,128)(2,1)S(1)}, u32[]{:S(2)}, u32[]{:S(2)}) collective-permute-start(bf16[224,256]{1,0:T(8,128)(2,1)S(1)} %get-tuple-element.182.refs_0_), channel_id=1, source_target_pairs={{0,1},{1,0},{2,3},{3,2},{4,5},{5,4},{6,7},{7,6},{8,9},{9,8},{10,11... | collective-permute-start | bytes 344072 | tf_op jit(solution)/shard_map/ppermute | solution.py:589
  126.5 1.7 collective-permute-start.33
  128.2 4.0 %collective-permute-done.29 = bf16[2,320,512]{2,1,0:T(8,128)(2,1)} collective-permute-done((bf16[2,320,512]{2,1,0:T(8,128)(2,1)}, bf16[2,320,512]{2,1,0:T(8,128)(2,1)}, u32[]{:S(2)}, u32[]{:S(2)}) %collective-permute-start.29) | collective-permute-done | bytes 655392 | tf_op jit(solution)/shard_map/ppermute | solution.py:583
  133.5 1.5 collective-permute-start.30
  137.8 5.3 %collective-permute-done.30 = bf16[1,320,512]{2,1,0:T(8,128)(2,1)} collective-permute-done((bf16[1,320,512]{2,1,0:T(8,128)(2,1)S(1)}, bf16[1,320,512]{2,1,0:T(8,128)(2,1)}, u32[]{:S(2)}, u32[]{:S(2)}) %collective-permute-start.30) | collective-permute-done | bytes 327712 | tf_op jit(solution)/shard_map/ppermute | solution.py:583
  144.2 1.6 collective-permute-done.28
  146.0 3.5 %collective-permute-start.34 = (bf16[2,80,1024]{2,1,0:T(8,128)(2,1)S(1)}, bf16[2,80,1024]{2,1,0:T(8,128)(2,1)S(1)}, u32[]{:S(2)}, u32[]{:S(2)}) collective-permute-start(bf16[2,80,1024]{2,1,0:T(8,128)(2,1)S(1)} %dynamic-slice_bitcast_fusion), channel_id=1, source_target_pairs={{0,1},{1,0},{2,3},{3,2},{4,5},{5,4},{6,7},{7,6},{8,9},{9,8},{10,11... | collective-permute-start | bytes 983048 | tf_op jit(solution)/shard_map/ppermute | solution.py:623
  150.9 2.2 %collective-permute-start.38 = (bf16[448,256]{1,0:T(8,128)(2,1)S(1)}, bf16[448,256]{1,0:T(8,128)(2,1)S(1)}, u32[]{:S(2)}, u32[]{:S(2)}) collective-permute-start(bf16[448,256]{1,0:T(8,128)(2,1)S(1)} %shard_sums.1.refs_0_), channel_id=1, source_target_pairs={{0,24},{4,28},{8,16},{12,20},{16,8},{20,12},{24,0},{28,4},{1,25},{... | collective-permute-start | bytes 688136 | tf_op jit(solution)/shard_map/ppermute | solution.py:629
  153.0 3.3 %collective-permute-done.34 = bf16[2,80,1024]{2,1,0:T(8,128)(2,1)S(1)} collective-permute-done((bf16[2,80,1024]{2,1,0:T(8,128)(2,1)S(1)}, bf16[2,80,1024]{2,1,0:T(8,128)(2,1)S(1)}, u32[]{:S(2)}, u32[]{:S(2)}) %collective-permute-start.34) | collective-permute-done | bytes 327712 | tf_op jit(solution)/shard_map/ppermute | solution.py:623
  156.4 2.5 %collective-permute-start.35 = (bf16[1,80,1024]{2,1,0:T(8,128)(2,1)S(1)}, bf16[1,80,1024]{2,1,0:T(8,128)(2,1)S(1)}, u32[]{:S(2)}, u32[]{:S(2)}) collective-permute-start(bf16[1,80,1024]{2,1,0:T(8,128)(2,1)S(1)} %constant_dynamic-slice_fusion), channel_id=1, source_target_pairs={{0,2},{1,3},{2,0},{3,1},{4,6},{5,7},{6,4},{7,5},{8,10},{9,11},{10,... | collective-permute-start | bytes 491528 | tf_op jit(solution)/shard_map/ppermute | solution.py:623
  158.9 1.9 %collective-permute-done.37.refs_4_ = bf16[448,256]{1,0:T(8,128)(2,1)S(1)} collective-permute-done((bf16[448,256]{1,0:T(8,128)(2,1)S(1)}, bf16[448,256]{1,0:T(8,128)(2,1)S(1)}, u32[]{:S(2)}, u32[]{:S(2)}) %collective-permute-start.37) | collective-permute-done | bytes 229408 | tf_op jit(solution)/shard_map/ppermute | solution.py:629
  161.8 3.5 %collective-permute-done.35 = bf16[1,80,1024]{2,1,0:T(8,128)(2,1)S(1)} collective-permute-done((bf16[1,80,1024]{2,1,0:T(8,128)(2,1)S(1)}, bf16[1,80,1024]{2,1,0:T(8,128)(2,1)S(1)}, u32[]{:S(2)}, u32[]{:S(2)}) %collective-permute-start.35) | collective-permute-done | bytes 163872 | tf_op jit(solution)/shard_map/ppermute | solution.py:623
  166.1 2.5 %assembled.1 = (f32[1024,256]{1,0:T(8,128)}, f32[2,2,8,128,128]{4,3,2,1,0:T(8,128)}, f32[2,2,8,128]{3,2,1,0:T(8,128)}, f32[1,1024]{1,0:T(1,128)}, f32[1,1024]{1,0:T(1,128)}, /*index=5*/f32[1,256]{1,0:T(1,128)}) custom-call(s32[15]{0:T(128)S(1)} %copy-done.23, bf16[448,256]{1,0:T(8,128)(2,1)S(1)} %shard_sums.1.refs_0_, ...), custom_call_target="tpu_custom_call" | custom-call | tf_op jit(solution)/shard_map/assembled/pallas_call | solution.py:790
  (181 shorter events, 33.7 us)
Async XLA Ops:
  2.0 25.0 %copy-start.2 = (bf16[2,2,8,128,128]{4,3,2,1,0:T(8,128)(2,1)S(1)}, bf16[2,2,8,128,128]{4,3,2,1,0:T(8,128)(2,1)}, u32[]{:S(2)}) copy-start(bf16[2,2,8,128,128]{4,3,2,1,0:T(8,128)(2,1)} %w_ref.15) | copy-start | bytes 3145732
  2.0 25.0 %copy-start.4 = (bf16[3,512,256]{2,1,0:T(8,128)(2,1)S(1)}, bf16[3,512,256]{2,1,0:T(8,128)(2,1)}, u32[]{:S(2)}) copy-start(bf16[3,512,256]{2,1,0:T(8,128)(2,1)} %constant.76.clone.t_ref) | copy-start | bytes 2359300
  2.0 25.1 %copy-start.23 = (s32[15]{0:T(128)S(1)}, s32[15]{0:T(128)}, u32[]{:S(2)}) copy-start(s32[15]{0:T(128)} %concatenate.12.scal_ref) | copy-start | bytes 184
  2.0 25.1 %copy-start.46 = (f32[2,2,8,128]{3,2,1,0:T(8,128)S(1)}, f32[2,2,8,128]{3,2,1,0:T(8,128)}, u32[]{:S(2)}) copy-start(f32[2,2,8,128]{3,2,1,0:T(8,128)} %b_ref.3) | copy-start | bytes 49156
  12.0 12.2 %collective-permute-start.10 = (bf16[3,64,256]{2,1,0:T(8,128)(2,1)}, bf16[3,64,256]{2,1,0:T(8,128)(2,1)S(1)}, u32[]{:S(2)}, u32[]{:S(2)}) collective-permute-start(bf16[3,64,256]{2,1,0:T(8,128)(2,1)} %get-tuple-element.119), channel_id=1, source_target_pairs={{0,2},{1,3},{2,0},{3,1},{4,6},{5,7},{6,4},{7,5},{8,10},{9,11},{10,... | collective-permute-start | bytes 294920 | tf_op jit(solution)/shard_map/ppermute | solution.py:589
  16.1 10.9 %collective-permute-start.11 = (bf16[3,64,256]{2,1,0:T(8,128)(2,1)}, bf16[3,64,256]{2,1,0:T(8,128)(2,1)S(1)}, u32[]{:S(2)}, u32[]{:S(2)}) collective-permute-start(bf16[3,64,256]{2,1,0:T(8,128)(2,1)} %get-tuple-element.120), channel_id=1, source_target_pairs={{0,3},{1,2},{2,1},{3,0},{4,7},{5,6},{6,5},{7,4},{8,11},{9,10},{10,... | collective-permute-start | bytes 294920 | tf_op jit(solution)/shard_map/ppermute | solution.py:589
  17.5 9.5 %collective-permute-start.9 = (bf16[3,64,256]{2,1,0:T(8,128)(2,1)}, bf16[3,64,256]{2,1,0:T(8,128)(2,1)S(1)}, u32[]{:S(2)}, u32[]{:S(2)}) collective-permute-start(bf16[3,64,256]{2,1,0:T(8,128)(2,1)} %get-tuple-element.118), channel_id=1, source_target_pairs={{0,1},{1,0},{2,3},{3,2},{4,5},{5,4},{6,7},{7,6},{8,9},{9,8},{10,11... | collective-permute-start | bytes 294920 | tf_op jit(solution)/shard_map/ppermute | solution.py:589
  17.7 15.1 %collective-permute-start = (bf16[3,64,256]{2,1,0:T(8,128)(2,1)}, bf16[3,64,256]{2,1,0:T(8,128)(2,1)S(1)}, u32[]{:S(2)}, u32[]{:S(2)}) collective-permute-start(bf16[3,64,256]{2,1,0:T(8,128)(2,1)} %get-tuple-element.104), channel_id=1, source_target_pairs={{0,1},{1,0},{2,3},{3,2},{4,5},{5,4},{6,7},{7,6},{8,9},{9,8},{10,11... | collective-permute-start | bytes 294920 | tf_op jit(solution)/shard_map/ppermute | solution.py:589
  19.5 15.2 %collective-permute-start.1 = (bf16[3,64,256]{2,1,0:T(8,128)(2,1)}, bf16[3,64,256]{2,1,0:T(8,128)(2,1)S(1)}, u32[]{:S(2)}, u32[]{:S(2)}) collective-permute-start(bf16[3,64,256]{2,1,0:T(8,128)(2,1)} %get-tuple-element.105), channel_id=1, source_target_pairs={{0,2},{1,3},{2,0},{3,1},{4,6},{5,7},{6,4},{7,5},{8,10},{9,11},{10,... | collective-permute-start | bytes 294920 | tf_op jit(solution)/shard_map/ppermute | solution.py:589
  24.2 10.5 %collective-permute-start.2 = (bf16[3,64,256]{2,1,0:T(8,128)(2,1)}, bf16[3,64,256]{2,1,0:T(8,128)(2,1)S(1)}, u32[]{:S(2)}, u32[]{:S(2)}) collective-permute-start(bf16[3,64,256]{2,1,0:T(8,128)(2,1)} %get-tuple-element.106), channel_id=1, source_target_pairs={{0,3},{1,2},{2,1},{3,0},{4,7},{5,6},{6,5},{7,4},{8,11},{9,10},{10,... | collective-permute-start | bytes 294920 | tf_op jit(solution)/shard_map/ppermute | solution.py:589
  30.3 9.5 %collective-permute-start.12 = (bf16[3,64,256]{2,1,0:T(8,128)(2,1)S(1)}, bf16[3,64,256]{2,1,0:T(8,128)(2,1)S(1)}, u32[]{:S(2)}, u32[]{:S(2)}) collective-permute-start(bf16[3,64,256]{2,1,0:T(8,128)(2,1)S(1)} %get-tuple-element.125), channel_id=1, source_target_pairs={{0,1},{1,0},{2,3},{3,2},{4,5},{5,4},{6,7},{7,6},{8,9},{9,8},{10,11... | collective-permute-start | bytes 294920 | tf_op jit(solution)/shard_map/ppermute | solution.py:589
  31.3 10.6 %collective-permute-start.13 = (bf16[3,64,256]{2,1,0:T(8,128)(2,1)S(1)}, bf16[3,64,256]{2,1,0:T(8,128)(2,1)S(1)}, u32[]{:S(2)}, u32[]{:S(2)}) collective-permute-start(bf16[3,64,256]{2,1,0:T(8,128)(2,1)S(1)} %get-tuple-element.126), channel_id=1, source_target_pairs={{0,2},{1,3},{2,0},{3,1},{4,6},{5,7},{6,4},{7,5},{8,10},{9,11},{10,... | collective-permute-start | bytes 294920 | tf_op jit(solution)/shard_map/ppermute | solution.py:589
  32.8 9.0 %collective-permute-start.14 = (bf16[3,64,256]{2,1,0:T(8,128)(2,1)S(1)}, bf16[3,64,256]{2,1,0:T(8,128)(2,1)S(1)}, u32[]{:S(2)}, u32[]{:S(2)}) collective-permute-start(bf16[3,64,256]{2,1,0:T(8,128)(2,1)S(1)} %get-tuple-element.127), channel_id=1, source_target_pairs={{0,3},{1,2},{2,1},{3,0},{4,7},{5,6},{6,5},{7,4},{8,11},{9,10},{10,... | collective-permute-start | bytes 294920 | tf_op jit(solution)/shard_map/ppermute | solution.py:589
  37.1 13.6 %collective-permute-start.3 = (bf16[3,64,256]{2,1,0:T(8,128)(2,1)S(1)}, bf16[3,64,256]{2,1,0:T(8,128)(2,1)S(1)}, u32[]{:S(2)}, u32[]{:S(2)}) collective-permute-start(bf16[3,64,256]{2,1,0:T(8,128)(2,1)S(1)} %get-tuple-element.113), channel_id=1, source_target_pairs={{0,1},{1,0},{2,3},{3,2},{4,5},{5,4},{6,7},{7,6},{8,9},{9,8},{10,11... | collective-permute-start | bytes 294920 | tf_op jit(solution)/shard_map/ppermute | solution.py:589
  37.5 14.7 %collective-permute-start.4 = (bf16[3,64,256]{2,1,0:T(8,128)(2,1)S(1)}, bf16[3,64,256]{2,1,0:T(8,128)(2,1)S(1)}, u32[]{:S(2)}, u32[]{:S(2)}) collective-permute-start(bf16[3,64,256]{2,1,0:T(8,128)(2,1)S(1)} %get-tuple-element.114), channel_id=1, source_target_pairs={{0,2},{1,3},{2,0},{3,1},{4,6},{5,7},{6,4},{7,5},{8,10},{9,11},{10,... | collective-permute-start | bytes 294920 | tf_op jit(solution)/shard_map/ppermute | solution.py:589
  39.8 12.5 %collective-permute-start.5 = (bf16[3,64,256]{2,1,0:T(8,128)(2,1)S(1)}, bf16[3,64,256]{2,1,0:T(8,128)(2,1)S(1)}, u32[]{:S(2)}, u32[]{:S(2)}) collective-permute-start(bf16[3,64,256]{2,1,0:T(8,128)(2,1)S(1)} %get-tuple-element.115), channel_id=1, source_target_pairs={{0,3},{1,2},{2,1},{3,0},{4,7},{5,6},{6,5},{7,4},{8,11},{9,10},{10,... | collective-permute-start | bytes 294920 | tf_op jit(solution)/shard_map/ppermute | solution.py:589
  42.8 13.3 %collective-permute-start.15 = (bf16[3,64,256]{2,1,0:T(8,128)(2,1)S(1)}, bf16[3,64,256]{2,1,0:T(8,128)(2,1)S(1)}, u32[]{:S(2)}, u32[]{:S(2)}) collective-permute-start(bf16[3,64,256]{2,1,0:T(8,128)(2,1)S(1)} %get-tuple-element.131.refs_2_.refs_0_.res_ref), channel_id=1, source_target_pairs={{0,1},{1,0},{2,3},{3,2},{4,5},{5,4},{6,7},{7,6},{8,9},{9,8},{10,11... | collective-permute-start | bytes 294920 | tf_op jit(solution)/shard_map/ppermute | solution.py:589
  49.8 10.8 %collective-permute-start.16 = (bf16[3,64,256]{2,1,0:T(8,128)(2,1)S(1)}, bf16[3,64,256]{2,1,0:T(8,128)(2,1)S(1)}, u32[]{:S(2)}, u32[]{:S(2)}) collective-permute-start(bf16[3,64,256]{2,1,0:T(8,128)(2,1)S(1)} %get-tuple-element.131.refs_2_.refs_0_.res_ref), channel_id=1, source_target_pairs={{0,2},{1,3},{2,0},{3,1},{4,6},{5,7},{6,4},{7,5},{8,10},{9,11},{10,... | collective-permute-start | bytes 294920 | tf_op jit(solution)/shard_map/ppermute | solution.py:589
  50.7 9.8 %collective-permute-start.17 = (bf16[3,64,256]{2,1,0:T(8,128)(2,1)S(1)}, bf16[3,64,256]{2,1,0:T(8,128)(2,1)S(1)}, u32[]{:S(2)}, u32[]{:S(2)}) collective-permute-start(bf16[3,64,256]{2,1,0:T(8,128)(2,1)S(1)} %get-tuple-element.131.refs_2_.refs_0_.res_ref), channel_id=1, source_target_pairs={{0,3},{1,2},{2,1},{3,0},{4,7},{5,6},{6,5},{7,4},{8,11},{9,10},{10,... | collective-permute-start | bytes 294920 | tf_op jit(solution)/shard_map/ppermute | solution.py:589
  53.2 10.5 %collective-permute-start.6 = (bf16[3,64,256]{2,1,0:T(8,128)(2,1)S(1)}, bf16[3,64,256]{2,1,0:T(8,128)(2,1)S(1)}, u32[]{:S(2)}, u32[]{:S(2)}) collective-permute-start(bf16[3,64,256]{2,1,0:T(8,128)(2,1)S(1)} %get-tuple-element.116.refs_3_.refs_0_.res_ref), channel_id=1, source_target_pairs={{0,1},{1,0},{2,3},{3,2},{4,5},{5,4},{6,7},{7,6},{8,9},{9,8},{10,11... | collective-permute-start | bytes 294920 | tf_op jit(solution)/shard_map/ppermute | solution.py:589
  54.3 13.5 %collective-permute-start.7 = (bf16[3,64,256]{2,1,0:T(8,128)(2,1)S(1)}, bf16[3,64,256]{2,1,0:T(8,128)(2,1)S(1)}, u32[]{:S(2)}, u32[]{:S(2)}) collective-permute-start(bf16[3,64,256]{2,1,0:T(8,128)(2,1)S(1)} %get-tuple-element.116.refs_3_.refs_0_.res_ref), channel_id=1, source_target_pairs={{0,2},{1,3},{2,0},{3,1},{4,6},{5,7},{6,4},{7,5},{8,10},{9,11},{10,... | collective-permute-start | bytes 294920 | tf_op jit(solution)/shard_map/ppermute | solution.py:589
  56.1 11.7 %collective-permute-start.8 = (bf16[3,64,256]{2,1,0:T(8,128)(2,1)S(1)}, bf16[3,64,256]{2,1,0:T(8,128)(2,1)S(1)}, u32[]{:S(2)}, u32[]{:S(2)}) collective-permute-start(bf16[3,64,256]{2,1,0:T(8,128)(2,1)S(1)} %get-tuple-element.116.refs_3_.refs_0_.res_ref), channel_id=1, source_target_pairs={{0,3},{1,2},{2,1},{3,0},{4,7},{5,6},{6,5},{7,4},{8,11},{9,10},{10,... | collective-permute-start | bytes 294920 | tf_op jit(solution)/shard_map/ppermute | solution.py:589
  74.8 29.6 %collective-permute-start.18 = (bf16[4,320,384]{2,1,0:T(8,128)(2,1)}, bf16[4,320,384]{2,1,0:T(8,128)(2,1)}, u32[]{:S(2)}, u32[]{:S(2)}) collective-permute-start(bf16[4,320,384]{2,1,0:T(8,128)(2,1)} %get-tuple-element.142), channel_id=1, source_target_pairs={{0,4},{4,0},{8,12},{12,8},{16,20},{20,16},{24,28},{28,24},{1,5},{5... | collective-permute-start | bytes 2949128 | tf_op jit(solution)/shard_map/ppermute | solution.py:583
  75.2 5.6 %collective-permute-start.19 = (bf16[3,64,256]{2,1,0:T(8,128)(2,1)}, bf16[3,64,256]{2,1,0:T(8,128)(2,1)S(1)}, u32[]{:S(2)}, u32[]{:S(2)}) collective-permute-start(bf16[3,64,256]{2,1,0:T(8,128)(2,1)} %copy-done.45), channel_id=1, source_target_pairs={{0,1},{1,0},{2,3},{3,2},{4,5},{5,4},{6,7},{7,6},{8,9},{9,8},{10,11... | collective-permute-start | bytes 294920 | tf_op jit(solution)/shard_map/ppermute | solution.py:589
  77.1 11.0 %collective-permute-start.20 = (bf16[3,64,256]{2,1,0:T(8,128)(2,1)}, bf16[3,64,256]{2,1,0:T(8,128)(2,1)S(1)}, u32[]{:S(2)}, u32[]{:S(2)}) collective-permute-start(bf16[3,64,256]{2,1,0:T(8,128)(2,1)} %copy-done.44), channel_id=1, source_target_pairs={{0,2},{1,3},{2,0},{3,1},{4,6},{5,7},{6,4},{7,5},{8,10},{9,11},{10,... | collective-permute-start | bytes 294920 | tf_op jit(solution)/shard_map/ppermute | solution.py:589
  78.1 12.4 %collective-permute-start.21 = (bf16[3,64,256]{2,1,0:T(8,128)(2,1)}, bf16[3,64,256]{2,1,0:T(8,128)(2,1)S(1)}, u32[]{:S(2)}, u32[]{:S(2)}) collective-permute-start(bf16[3,64,256]{2,1,0:T(8,128)(2,1)} %copy-done.42), channel_id=1, source_target_pairs={{0,3},{1,2},{2,1},{3,0},{4,7},{5,6},{6,5},{7,4},{8,11},{9,10},{10,... | collective-permute-start | bytes 294920 | tf_op jit(solution)/shard_map/ppermute | solution.py:589
  79.8 17.8 %collective-permute-start.22 = (bf16[3,64,256]{2,1,0:T(8,128)(2,1)}, bf16[3,64,256]{2,1,0:T(8,128)(2,1)S(1)}, u32[]{:S(2)}, u32[]{:S(2)}) collective-permute-start(bf16[3,64,256]{2,1,0:T(8,128)(2,1)} %copy-done.43), channel_id=1, source_target_pairs={{0,1},{1,0},{2,3},{3,2},{4,5},{5,4},{6,7},{7,6},{8,9},{9,8},{10,11... | collective-permute-start | bytes 294920 | tf_op jit(solution)/shard_map/ppermute | solution.py:589
  80.8 16.8 %collective-permute-start.23 = (bf16[3,64,256]{2,1,0:T(8,128)(2,1)}, bf16[3,64,256]{2,1,0:T(8,128)(2,1)S(1)}, u32[]{:S(2)}, u32[]{:S(2)}) collective-permute-start(bf16[3,64,256]{2,1,0:T(8,128)(2,1)} %copy-done.41), channel_id=1, source_target_pairs={{0,2},{1,3},{2,0},{3,1},{4,6},{5,7},{6,4},{7,5},{8,10},{9,11},{10,... | collective-permute-start | bytes 294920 | tf_op jit(solution)/shard_map/ppermute | solution.py:589
  88.1 9.5 %collective-permute-start.24 = (bf16[3,64,256]{2,1,0:T(8,128)(2,1)}, bf16[3,64,256]{2,1,0:T(8,128)(2,1)S(1)}, u32[]{:S(2)}, u32[]{:S(2)}) collective-permute-start(bf16[3,64,256]{2,1,0:T(8,128)(2,1)} %copy-done.40), channel_id=1, source_target_pairs={{0,3},{1,2},{2,1},{3,0},{4,7},{5,6},{6,5},{7,4},{8,11},{9,10},{10,... | collective-permute-start | bytes 294920 | tf_op jit(solution)/shard_map/ppermute | solution.py:589
  99.1 4.5 %collective-permute-start.26 = (bf16[192,1024]{1,0:T(8,128)(2,1)S(1)}, bf16[192,1024]{1,0:T(8,128)(2,1)S(1)}, u32[]{:S(2)}, u32[]{:S(2)}) collective-permute-start(bf16[192,1024]{1,0:T(8,128)(2,1)S(1)} %get-tuple-element.164.refs_3_), channel_id=1, source_target_pairs={{0,4},{4,0},{8,12},{12,8},{16,20},{20,16},{24,28},{28,24},{1,5},{5... | collective-permute-start | bytes 1179656 | tf_op jit(solution)/shard_map/ppermute | solution.py:583
  99.2 4.4 %collective-permute-start.25 = (bf16[192,1024]{1,0:T(8,128)(2,1)S(1)}, bf16[192,1024]{1,0:T(8,128)(2,1)S(1)}, u32[]{:S(2)}, u32[]{:S(2)}) collective-permute-start(bf16[192,1024]{1,0:T(8,128)(2,1)S(1)} %get-tuple-element.151.refs_2_), channel_id=1, source_target_pairs={{0,4},{4,0},{8,12},{12,8},{16,20},{20,16},{24,28},{28,24},{1,5},{5... | collective-permute-start | bytes 1179656 | tf_op jit(solution)/shard_map/ppermute | solution.py:583
  99.7 21.4 %all-to-all-start = ((bf16[8,256,256]{2,1,0:T(8,128)(2,1)}), bf16[8,256,256]{2,1,0:T(8,128)(2,1)S(1)}, u32[]{:S(2)}, u32[]{:S(2)}) async-start(bf16[8,256,256]{2,1,0:T(8,128)(2,1)} %packed.1), calls=%async_computation | async-start | bytes 2097152 | tf_op jit(solution)/shard_map/all_to_all | solution.py:882
  111.5 20.7 %collective-permute-start.29 = (bf16[2,320,512]{2,1,0:T(8,128)(2,1)}, bf16[2,320,512]{2,1,0:T(8,128)(2,1)}, u32[]{:S(2)}, u32[]{:S(2)}) collective-permute-start(bf16[2,320,512]{2,1,0:T(8,128)(2,1)} %get-tuple-element.181), channel_id=1, source_target_pairs={{0,16},{4,20},{8,24},{12,28},{16,0},{20,4},{24,8},{28,12},{1,17},{... | collective-permute-start | bytes 1966088 | tf_op jit(solution)/shard_map/ppermute | solution.py:583
  113.5 21.5 %collective-permute-start.27 = (bf16[2,320,512]{2,1,0:T(8,128)(2,1)S(1)}, bf16[2,320,512]{2,1,0:T(8,128)(2,1)}, u32[]{:S(2)}, u32[]{:S(2)}) collective-permute-start(bf16[2,320,512]{2,1,0:T(8,128)(2,1)S(1)} %get-tuple-element.179), channel_id=1, source_target_pairs={{0,8},{4,12},{8,0},{12,4},{16,24},{20,28},{24,16},{28,20},{1,9},{5... | collective-permute-start | bytes 1966088 | tf_op jit(solution)/shard_map/ppermute | solution.py:583
  122.4 14.4 %collective-permute-start.31 = (bf16[224,256]{1,0:T(8,128)(2,1)S(1)}, bf16[224,256]{1,0:T(8,128)(2,1)S(1)}, u32[]{:S(2)}, u32[]{:S(2)}) collective-permute-start(bf16[224,256]{1,0:T(8,128)(2,1)S(1)} %get-tuple-element.182.refs_0_), channel_id=1, source_target_pairs={{0,1},{1,0},{2,3},{3,2},{4,5},{5,4},{6,7},{7,6},{8,9},{9,8},{10,11... | collective-permute-start | bytes 344072 | tf_op jit(solution)/shard_map/ppermute | solution.py:589
  125.8 11.3 %collective-permute-start.32 = (bf16[224,256]{1,0:T(8,128)(2,1)S(1)}, bf16[224,256]{1,0:T(8,128)(2,1)S(1)}, u32[]{:S(2)}, u32[]{:S(2)}) collective-permute-start(bf16[224,256]{1,0:T(8,128)(2,1)S(1)} %get-tuple-element.182.refs_0_), channel_id=1, source_target_pairs={{0,2},{1,3},{2,0},{3,1},{4,6},{5,7},{6,4},{7,5},{8,10},{9,11},{10,... | collective-permute-start | bytes 344072 | tf_op jit(solution)/shard_map/ppermute | solution.py:589
  126.5 10.6 %collective-permute-start.33 = (bf16[224,256]{1,0:T(8,128)(2,1)S(1)}, bf16[224,256]{1,0:T(8,128)(2,1)S(1)}, u32[]{:S(2)}, u32[]{:S(2)}) collective-permute-start(bf16[224,256]{1,0:T(8,128)(2,1)S(1)} %get-tuple-element.182.refs_0_), channel_id=1, source_target_pairs={{0,3},{1,2},{2,1},{3,0},{4,7},{5,6},{6,5},{7,4},{8,11},{9,10},{10,... | collective-permute-start | bytes 344072 | tf_op jit(solution)/shard_map/ppermute | solution.py:589
  133.5 9.6 %collective-permute-start.30 = (bf16[1,320,512]{2,1,0:T(8,128)(2,1)S(1)}, bf16[1,320,512]{2,1,0:T(8,128)(2,1)}, u32[]{:S(2)}, u32[]{:S(2)}) collective-permute-start(bf16[1,320,512]{2,1,0:T(8,128)(2,1)S(1)} %slice.21), channel_id=1, source_target_pairs={{0,8},{4,12},{8,0},{12,4},{16,24},{20,28},{24,16},{28,20},{1,9},{5... | collective-permute-start | bytes 983048 | tf_op jit(solution)/shard_map/ppermute | solution.py:583
  136.3 9.5 %collective-permute-start.28 = (bf16[1,320,512]{2,1,0:T(8,128)(2,1)S(1)}, bf16[1,320,512]{2,1,0:T(8,128)(2,1)S(1)}, u32[]{:S(2)}, u32[]{:S(2)}) collective-permute-start(bf16[1,320,512]{2,1,0:T(8,128)(2,1)S(1)} %slice_bitcast_fusion), channel_id=1, source_target_pairs={{0,16},{4,20},{8,24},{12,28},{16,0},{20,4},{24,8},{28,12},{1,17},{... | collective-permute-start | bytes 983048 | tf_op jit(solution)/shard_map/ppermute | solution.py:583
  146.0 10.3 %collective-permute-start.34 = (bf16[2,80,1024]{2,1,0:T(8,128)(2,1)S(1)}, bf16[2,80,1024]{2,1,0:T(8,128)(2,1)S(1)}, u32[]{:S(2)}, u32[]{:S(2)}) collective-permute-start(bf16[2,80,1024]{2,1,0:T(8,128)(2,1)S(1)} %dynamic-slice_bitcast_fusion), channel_id=1, source_target_pairs={{0,1},{1,0},{2,3},{3,2},{4,5},{5,4},{6,7},{7,6},{8,9},{9,8},{10,11... | collective-permute-start | bytes 983048 | tf_op jit(solution)/shard_map/ppermute | solution.py:623
  149.5 9.4 %collective-permute-start.36 = (bf16[448,256]{1,0:T(8,128)(2,1)S(1)}, bf16[448,256]{1,0:T(8,128)(2,1)S(1)}, u32[]{:S(2)}, u32[]{:S(2)}) collective-permute-start(bf16[448,256]{1,0:T(8,128)(2,1)S(1)} %shard_sums.1.refs_0_), channel_id=1, source_target_pairs={{0,8},{4,12},{8,0},{12,4},{16,24},{20,28},{24,16},{28,20},{1,9},{5... | collective-permute-start | bytes 688136 | tf_op jit(solution)/shard_map/ppermute | solution.py:629
  150.0 10.9 %collective-permute-start.37 = (bf16[448,256]{1,0:T(8,128)(2,1)S(1)}, bf16[448,256]{1,0:T(8,128)(2,1)S(1)}, u32[]{:S(2)}, u32[]{:S(2)}) collective-permute-start(bf16[448,256]{1,0:T(8,128)(2,1)S(1)} %shard_sums.1.refs_0_), channel_id=1, source_target_pairs={{0,16},{4,20},{8,24},{12,28},{16,0},{20,4},{24,8},{28,12},{1,17},{... | collective-permute-start | bytes 688136 | tf_op jit(solution)/shard_map/ppermute | solution.py:629
  150.9 9.9 %collective-permute-start.38 = (bf16[448,256]{1,0:T(8,128)(2,1)S(1)}, bf16[448,256]{1,0:T(8,128)(2,1)S(1)}, u32[]{:S(2)}, u32[]{:S(2)}) collective-permute-start(bf16[448,256]{1,0:T(8,128)(2,1)S(1)} %shard_sums.1.refs_0_), channel_id=1, source_target_pairs={{0,24},{4,28},{8,16},{12,20},{16,8},{20,12},{24,0},{28,4},{1,25},{... | collective-permute-start | bytes 688136 | tf_op jit(solution)/shard_map/ppermute | solution.py:629
  156.4 8.8 %collective-permute-start.35 = (bf16[1,80,1024]{2,1,0:T(8,128)(2,1)S(1)}, bf16[1,80,1024]{2,1,0:T(8,128)(2,1)S(1)}, u32[]{:S(2)}, u32[]{:S(2)}) collective-permute-start(bf16[1,80,1024]{2,1,0:T(8,128)(2,1)S(1)} %constant_dynamic-slice_fusion), channel_id=1, source_target_pairs={{0,2},{1,3},{2,0},{3,1},{4,6},{5,7},{6,4},{7,5},{8,10},{9,11},{10,... | collective-permute-start | bytes 491528 | tf_op jit(solution)/shard_map/ppermute | solution.py:623
  160.8 5.2 %collective-permute-start.39 = (bf16[448,256]{1,0:T(8,128)(2,1)S(1)}, bf16[448,256]{1,0:T(8,128)(2,1)S(1)}, u32[]{:S(2)}, u32[]{:S(2)}) collective-permute-start(bf16[448,256]{1,0:T(8,128)(2,1)S(1)} %shard_sums.1.refs_0_), channel_id=1, source_target_pairs={{0,4},{4,0},{8,12},{12,8},{16,20},{20,16},{24,28},{28,24},{1,5},{5... | collective-permute-start | bytes 688136 | tf_op jit(solution)/shard_map/ppermute | solution.py:583
  160.8 5.2 %collective-permute-start.40 = (bf16[448,256]{1,0:T(8,128)(2,1)S(1)}, bf16[448,256]{1,0:T(8,128)(2,1)S(1)}, u32[]{:S(2)}, u32[]{:S(2)}) collective-permute-start(bf16[448,256]{1,0:T(8,128)(2,1)S(1)} %collective-permute-done.36.refs_2_), channel_id=1, source_target_pairs={{0,4},{4,0},{8,12},{12,8},{16,20},{20,16},{24,28},{28,24},{1,5},{5... | collective-permute-start | bytes 688136 | tf_op jit(solution)/shard_map/ppermute | solution.py:583
  161.3 4.7 %collective-permute-start.41 = (bf16[448,256]{1,0:T(8,128)(2,1)S(1)}, bf16[448,256]{1,0:T(8,128)(2,1)S(1)}, u32[]{:S(2)}, u32[]{:S(2)}) collective-permute-start(bf16[448,256]{1,0:T(8,128)(2,1)S(1)} %collective-permute-done.37.refs_4_), channel_id=1, source_target_pairs={{0,4},{4,0},{8,12},{12,8},{16,20},{20,16},{24,28},{28,24},{1,5},{5... | collective-permute-start | bytes 688136 | tf_op jit(solution)/shard_map/ppermute | solution.py:583
  161.3 4.7 %collective-permute-start.42 = (bf16[448,256]{1,0:T(8,128)(2,1)S(1)}, bf16[448,256]{1,0:T(8,128)(2,1)S(1)}, u32[]{:S(2)}, u32[]{:S(2)}) collective-permute-start(bf16[448,256]{1,0:T(8,128)(2,1)S(1)} %collective-permute-done.38.refs_6_), channel_id=1, source_target_pairs={{0,4},{4,0},{8,12},{12,8},{16,20},{20,16},{24,28},{28,24},{1,5},{5... | collective-permute-start | bytes 688136 | tf_op jit(solution)/shard_map/ppermute | solution.py:583
  (48 other events, 315.6 us)

commit v14 on v10

--- a/solution.py
+++ b/solution.py
@@ -874,11 +874,6 @@
     own_grads, other_grads, row_sums = [], [], []
     for first, res, back in zip(firsts, residual, spec_back):
         grad, row_sum = embedded_back_chunk(scal, embedded, stats, res, head_w, gain_row, back, first, cells)
-        if first == firsts[0]:
-            grad, head_grad, spec_grad = lax.optimization_barrier((grad, head_grad, spec_grad))
-            weight_sums = lax.all_to_all(
-                packed(routes, head_grad, spec_grad, predicted, groups), "grp", split_axis=0, concat_axis=0, tiled=True
-            )
         own_grads.append(grad)
         other_grads.append(swap_bit(grad, 0, groups))
         row_sums.append(row_sum)
@@ -888,6 +883,10 @@
     top_bit = groups.bit_length() - 2
     received = [swap_bit(sent[0], 1, groups), swap_bit(sent[1], top_bit, groups)]
     kept = embed_grad_parts(scal, kept_turned, grads, groups, 0)
+    _, head_grad, spec_grad = lax.optimization_barrier((sent, head_grad, spec_grad))
+    weight_sums = lax.all_to_all(
+        packed(routes, head_grad, spec_grad, predicted, groups), "grp", split_axis=0, concat_axis=0, tiled=True
+    )
     kept, weight_sums = lax.optimization_barrier((kept, weight_sums))
     ends = scatter_start(received, kept, groups)
     small, predictions = group_sums(routes, weight_sums, spec_bias, head_sums, row_sums, slot_count, per_sample)

time: 165 us -> 171 us (1.036)
  local copies, waits for them, and re-layouts: 1.89 us -> 7.3 us
  waiting for transfers between devices: 44.4 us -> 48.1 us
  Pallas kernels: 43.8 us -> 41.2 us
    unnamed x32 -> x44, local copies, waits for them, and re-layouts: 0.95 us -> 6.35 us
    all_to_all x1, waiting for transfers between devices: 2.34 us -> 4.23 us  [on_device(): lax.all_to_all(packed(routes, head_grad, spec_grad, predicted, groups), '...]
  transfers between devices with their start and end apart: 44 -> 44, of which waited for: 13 -> 14; matrix products, arithmetic and copies ran while one was open for 3% -> 2% of each run, Pallas kernels for 17% -> 11%
where the time goes in v14:
time: 171 us
  starting transfers between devices  68.1 us (40%)
  waiting for transfers between devices  48.1 us (28%)
  Pallas kernels  41.2 us (24%)
  local copies, waits for them, and re-layouts  7.3 us (4%)
  other arithmetic  4.84 us (3%)
    ppermute x27, starting transfers between devices, across(): lax.ppermute(pieces[k], 'fft', [(z, z ^ k) for z in range(shards)])  49.6 us
    ppermute x27, waiting for transfers between devices, across(): lax.ppermute(pieces[k], 'fft', [(z, z ^ k) for z in range(shards)])  19 us
    ppermute x11, waiting for transfers between devices, swap_bit(): lax.ppermute(values, 'grp', [(g, g ^ 1 << bit) for g in range(groups)])  16.5 us
    pallas_call x1, Pallas kernels, embed(): pl.pallas_call(body, grid_spec=pltpu.PrefetchScalarGridSpec(num_scalar_pr...  10 us
    pallas_call x2, Pallas kernels, embed_grad_parts(): pl.pallas_call(body, grid_spec=pltpu.PrefetchScalarGridSpec(num_scalar_pr...  8.98 us
    ppermute x2, waiting for transfers between devices, scatter_step(): received = lax.ppermute(send, 'fft', [(z, z ^ bit) for z in range(shards)])  6.82 us
    ppermute x11, starting transfers between devices, swap_bit(): lax.ppermute(values, 'grp', [(g, g ^ 1 << bit) for g in range(groups)])  6.67 us
    unnamed x44, local copies, waits for them, and re-layouts  6.35 us
  transfers between devices with their start and end apart: 44, of which 14 were waited for; matrix products, arithmetic and copies ran while one was open for 2% of the time, Pallas kernels for 11%

profile of v14, /device:TPU:0, one launch (start us, length us, event | category | flops | bytes accessed | tf_op | source)
XLA Modules:
  0.0 170.6 jit_solution(199055246138635178)
XLA Ops:
  2.0 10.0 %embed.1 = (bf16[384,1024]{1,0:T(8,128)(2,1)}, bf16[384,1024]{1,0:T(8,128)(2,1)}, f32[384,256]{1,0:T(8,128)}, bf16[4,320,384]{2,1,0:T(8,128)(2,1)}, bf16[4,320,3...) custom-call(s32[15]{0:T(128)} %concatenate.12.scal_ref, ...), custom_call_target="tpu_custom_call" | custom-call | flops 2013265920 | bytes 7208960 | tf_op jit(solution)/shard_map/embed/pallas_call | solution.py:157
  12.0 4.1 %collective-permute-start.10 = (bf16[3,64,256]{2,1,0:T(8,128)(2,1)}, bf16[3,64,256]{2,1,0:T(8,128)(2,1)S(1)}, u32[]{:S(2)}, u32[]{:S(2)}) collective-permute-start(bf16[3,64,256]{2,1,0:T(8,128)(2,1)} %get-tuple-element.114), channel_id=1, source_target_pairs={{0,2},{1,3},{2,0},{3,1},{4,6},{5,7},{6,4},{7,5},{8,10},{9,11},{10,... | collective-permute-start | bytes 294920 | tf_op jit(solution)/shard_map/ppermute | solution.py:589
  17.7 1.8 %collective-permute-start = (bf16[3,64,256]{2,1,0:T(8,128)(2,1)}, bf16[3,64,256]{2,1,0:T(8,128)(2,1)S(1)}, u32[]{:S(2)}, u32[]{:S(2)}) collective-permute-start(bf16[3,64,256]{2,1,0:T(8,128)(2,1)} %get-tuple-element.99), channel_id=1, source_target_pairs={{0,1},{1,0},{2,3},{3,2},{4,5},{5,4},{6,7},{7,6},{8,9},{9,8},{10,11... | collective-permute-start | bytes 294920 | tf_op jit(solution)/shard_map/ppermute | solution.py:589
  19.5 1.7 collective-permute-start.1
  21.2 3.0 %collective-permute-done.10.refs_2_ = bf16[3,64,256]{2,1,0:T(8,128)(2,1)S(1)} collective-permute-done((bf16[3,64,256]{2,1,0:T(8,128)(2,1)}, bf16[3,64,256]{2,1,0:T(8,128)(2,1)S(1)}, u32[]{:S(2)}, u32[]{:S(2)}) %collective-permute-start.10) | collective-permute-done | bytes 98336 | tf_op jit(solution)/shard_map/ppermute | solution.py:589
  24.2 2.8 %collective-permute-start.2 = (bf16[3,64,256]{2,1,0:T(8,128)(2,1)}, bf16[3,64,256]{2,1,0:T(8,128)(2,1)S(1)}, u32[]{:S(2)}, u32[]{:S(2)}) collective-permute-start(bf16[3,64,256]{2,1,0:T(8,128)(2,1)} %get-tuple-element.101), channel_id=1, source_target_pairs={{0,3},{1,2},{2,1},{3,0},{4,7},{5,6},{6,5},{7,4},{8,11},{9,10},{10,... | collective-permute-start | bytes 294920 | tf_op jit(solution)/shard_map/ppermute | solution.py:589
  27.9 2.3 %spectral.3 = (bf16[3,64,256]{2,1,0:T(8,128)(2,1)S(1)}, bf16[3,64,256]{2,1,0:T(8,128)(2,1)S(1)}, bf16[3,64,256]{2,1,0:T(8,128)(2,1)S(1)}, bf16[3,64,256]{2,1,0:T...) custom-call(s32[15]{0:T(128)S(1)} %copy-done.7, ...), custom_call_target="tpu_custom_call" | custom-call | flops 704643072 | bytes 3145728 | tf_op jit(solution)/shard_map/spectral/pallas_call | solution.py:277
  31.3 1.6 collective-permute-start.13
  32.8 1.9 %collective-permute-start.14 = (bf16[3,64,256]{2,1,0:T(8,128)(2,1)S(1)}, bf16[3,64,256]{2,1,0:T(8,128)(2,1)S(1)}, u32[]{:S(2)}, u32[]{:S(2)}) collective-permute-start(bf16[3,64,256]{2,1,0:T(8,128)(2,1)S(1)} %get-tuple-element.122), channel_id=1, source_target_pairs={{0,3},{1,2},{2,1},{3,0},{4,7},{5,6},{6,5},{7,4},{8,11},{9,10},{10,... | collective-permute-start | bytes 294920 | tf_op jit(solution)/shard_map/ppermute | solution.py:589
  34.8 2.3 %spectral.2 = (bf16[3,64,256]{2,1,0:T(8,128)(2,1)S(1)}, bf16[3,64,256]{2,1,0:T(8,128)(2,1)S(1)}, bf16[3,64,256]{2,1,0:T(8,128)(2,1)S(1)}, bf16[3,64,256]{2,1,0:T...) custom-call(s32[15]{0:T(128)S(1)} %copy-done.7, ...), custom_call_target="tpu_custom_call" | custom-call | flops 704643072 | bytes 3145728 | tf_op jit(solution)/shard_map/spectral/pallas_call | solution.py:277
  37.5 2.2 %collective-permute-start.4 = (bf16[3,64,256]{2,1,0:T(8,128)(2,1)S(1)}, bf16[3,64,256]{2,1,0:T(8,128)(2,1)S(1)}, u32[]{:S(2)}, u32[]{:S(2)}) collective-permute-start(bf16[3,64,256]{2,1,0:T(8,128)(2,1)S(1)} %get-tuple-element.109), channel_id=1, source_target_pairs={{0,2},{1,3},{2,0},{3,1},{4,6},{5,7},{6,4},{7,5},{8,10},{9,11},{10,... | collective-permute-start | bytes 294920 | tf_op jit(solution)/shard_map/ppermute | solution.py:589
  39.7 1.8 %collective-permute-start.5 = (bf16[3,64,256]{2,1,0:T(8,128)(2,1)S(1)}, bf16[3,64,256]{2,1,0:T(8,128)(2,1)S(1)}, u32[]{:S(2)}, u32[]{:S(2)}) collective-permute-start(bf16[3,64,256]{2,1,0:T(8,128)(2,1)S(1)} %get-tuple-element.110), channel_id=1, source_target_pairs={{0,3},{1,2},{2,1},{3,0},{4,7},{5,6},{6,5},{7,4},{8,11},{9,10},{10,... | collective-permute-start | bytes 294920 | tf_op jit(solution)/shard_map/ppermute | solution.py:589
  42.8 6.9 %collective-permute-start.15 = (bf16[3,64,256]{2,1,0:T(8,128)(2,1)S(1)}, bf16[3,64,256]{2,1,0:T(8,128)(2,1)S(1)}, u32[]{:S(2)}, u32[]{:S(2)}) collective-permute-start(bf16[3,64,256]{2,1,0:T(8,128)(2,1)S(1)} %get-tuple-element.126.refs_2_.refs_0_.res_ref), channel_id=1, source_target_pairs={{0,1},{1,0},{2,3},{3,2},{4,5},{5,4},{6,7},{7,6},{8,9},{9,8},{10,11... | collective-permute-start | bytes 294920 | tf_op jit(solution)/shard_map/ppermute | solution.py:589
  50.7 1.5 collective-permute-start.17
  54.2 1.8 %collective-permute-start.7 = (bf16[3,64,256]{2,1,0:T(8,128)(2,1)S(1)}, bf16[3,64,256]{2,1,0:T(8,128)(2,1)S(1)}, u32[]{:S(2)}, u32[]{:S(2)}) collective-permute-start(bf16[3,64,256]{2,1,0:T(8,128)(2,1)S(1)} %get-tuple-element.111.refs_3_.refs_0_.res_ref), channel_id=1, source_target_pairs={{0,2},{1,3},{2,0},{3,1},{4,6},{5,7},{6,4},{7,5},{8,10},{9,11},{10,... | collective-permute-start | bytes 294920 | tf_op jit(solution)/shard_map/ppermute | solution.py:589
  56.0 1.5 collective-permute-start.8
  58.1 2.4 %collective-permute-done.16.refs_2_ = bf16[3,64,256]{2,1,0:T(8,128)(2,1)S(1)} collective-permute-done((bf16[3,64,256]{2,1,0:T(8,128)(2,1)S(1)}, bf16[3,64,256]{2,1,0:T(8,128)(2,1)S(1)}, u32[]{:S(2)}, u32[]{:S(2)}) %collective-permute-start.16) | collective-permute-done | bytes 98336 | tf_op jit(solution)/shard_map/ppermute | solution.py:589
  60.5 3.0 %spectral_back.2 = (bf16[3,64,256]{2,1,0:T(8,128)(2,1)S(1)}, bf16[3,64,256]{2,1,0:T(8,128)(2,1)S(1)}, bf16[3,64,256]{2,1,0:T(8,128)(2,1)S(1)}, bf16[3,64,256]{2,...) custom-call(s32[15]{0:T(128)S(1)} %copy-done.7, bf16[3,512,256]{2,1,0:T(8,128)(2,1)S(1)} %copy-done.4, ...), custom_call_target="tpu_custom_call" | custom-call | flops 1006632960 | bytes 3145728 | tf_op jit(solution)/shard_map/spectral_back/pallas_call | solution.py:440
  63.5 4.3 %collective-permute-done.7.refs_2_ = bf16[3,64,256]{2,1,0:T(8,128)(2,1)S(1)} collective-permute-done((bf16[3,64,256]{2,1,0:T(8,128)(2,1)S(1)}, bf16[3,64,256]{2,1,0:T(8,128)(2,1)S(1)}, u32[]{:S(2)}, u32[]{:S(2)}) %collective-permute-start.7) | collective-permute-done | bytes 98336 | tf_op jit(solution)/shard_map/ppermute | solution.py:589
  67.8 3.0 %spectral_back.3 = (bf16[3,64,256]{2,1,0:T(8,128)(2,1)S(1)}, bf16[3,64,256]{2,1,0:T(8,128)(2,1)S(1)}, bf16[3,64,256]{2,1,0:T(8,128)(2,1)S(1)}, bf16[3,64,256]{2,...) custom-call(s32[15]{0:T(128)S(1)} %copy-done.7, bf16[3,512,256]{2,1,0:T(8,128)(2,1)S(1)} %copy-done.4, ...), custom_call_target="tpu_custom_call" | custom-call | flops 1006632960 | bytes 3145728 | tf_op jit(solution)/shard_map/spectral_back/pallas_call | solution.py:440
  70.9 1.9 %collective-permute-start.22 = (bf16[3,64,256]{2,1,0:T(8,128)(2,1)S(1)}, bf16[3,64,256]{2,1,0:T(8,128)(2,1)S(1)}, u32[]{:S(2)}, u32[]{:S(2)}) collective-permute-start(bf16[3,64,256]{2,1,0:T(8,128)(2,1)S(1)} %get-tuple-element.145), channel_id=1, source_target_pairs={{0,1},{1,0},{2,3},{3,2},{4,5},{5,4},{6,7},{7,6},{8,9},{9,8},{10,11... | collective-permute-start | bytes 294920 | tf_op jit(solution)/shard_map/ppermute | solution.py:589
  73.7 1.6 collective-permute-start.24
  76.3 2.9 %collective-permute-start.20 = (bf16[3,64,256]{2,1,0:T(8,128)(2,1)S(1)}, bf16[3,64,256]{2,1,0:T(8,128)(2,1)S(1)}, u32[]{:S(2)}, u32[]{:S(2)}) collective-permute-start(bf16[3,64,256]{2,1,0:T(8,128)(2,1)S(1)} %get-tuple-element.141), channel_id=1, source_target_pairs={{0,2},{1,3},{2,0},{3,1},{4,6},{5,7},{6,4},{7,5},{8,10},{9,11},{10,... | collective-permute-start | bytes 294920 | tf_op jit(solution)/shard_map/ppermute | solution.py:589
  79.2 4.4 %collective-permute-done.23.refs_2_ = bf16[3,64,256]{2,1,0:T(8,128)(2,1)S(1)} collective-permute-done((bf16[3,64,256]{2,1,0:T(8,128)(2,1)S(1)}, bf16[3,64,256]{2,1,0:T(8,128)(2,1)S(1)}, u32[]{:S(2)}, u32[]{:S(2)}) %collective-permute-start.23) | collective-permute-done | bytes 98336 | tf_op jit(solution)/shard_map/ppermute | solution.py:589
  83.5 2.3 %collective-permute-start.21 = (bf16[3,64,256]{2,1,0:T(8,128)(2,1)S(1)}, bf16[3,64,256]{2,1,0:T(8,128)(2,1)S(1)}, u32[]{:S(2)}, u32[]{:S(2)}) collective-permute-start(bf16[3,64,256]{2,1,0:T(8,128)(2,1)S(1)} %get-tuple-element.142), channel_id=1, source_target_pairs={{0,3},{1,2},{2,1},{3,0},{4,7},{5,6},{6,5},{7,4},{8,11},{9,10},{10,... | collective-permute-start | bytes 294920 | tf_op jit(solution)/shard_map/ppermute | solution.py:589
  85.8 1.5 embedded_back.3
  87.4 4.6 %collective-permute-done.20.refs_2_ = bf16[3,64,256]{2,1,0:T(8,128)(2,1)S(1)} collective-permute-done((bf16[3,64,256]{2,1,0:T(8,128)(2,1)S(1)}, bf16[3,64,256]{2,1,0:T(8,128)(2,1)S(1)}, u32[]{:S(2)}, u32[]{:S(2)}) %collective-permute-start.20) | collective-permute-done | bytes 98336 | tf_op jit(solution)/shard_map/ppermute | solution.py:589
  92.0 1.6 embedded_back.2
  96.8 5.0 %embed_grad.2 = (bf16[2,320,512]{2,1,0:T(8,128)(2,1)}, bf16[2,320,512]{2,1,0:T(8,128)(2,1)}) custom-call(s32[15]{0:T(128)S(1)} %copy-done.7, bf16[4,320,384]{2,1,0:T(8,128)(2,1)S(1)} %copy-done.17, bf16[4,320,384]{2,1,0:T(8,128)(2,1)S(1)} %collective-permute-done.18.refs_1_, bf16[192,1024]{1,0:T(8,128)(2,1)S(1)} %get-tuple-element.143.refs_2_, ...), custom_call_target="tpu_custom_call" | custom-call | flops 1006632960 | bytes 4063232 | tf_op jit(solution)/shard_map/embed_grad/pallas_call | solution.py:555
  101.7 1.7 packed.1
  103.4 3.8 %all-to-all-start = ((bf16[8,256,256]{2,1,0:T(8,128)(2,1)}), bf16[8,256,256]{2,1,0:T(8,128)(2,1)S(1)}, u32[]{:S(2)}, u32[]{:S(2)}) async-start(bf16[8,256,256]{2,1,0:T(8,128)(2,1)} %packed.1), calls=%async_computation | async-start | bytes 2097152 | tf_op jit(solution)/shard_map/all_to_all | solution.py:887
  107.3 2.0 %collective-permute-start.29 = (bf16[2,320,512]{2,1,0:T(8,128)(2,1)}, bf16[2,320,512]{2,1,0:T(8,128)(2,1)}, u32[]{:S(2)}, u32[]{:S(2)}) collective-permute-start(bf16[2,320,512]{2,1,0:T(8,128)(2,1)} %get-tuple-element.156), channel_id=1, source_target_pairs={{0,16},{4,20},{8,24},{12,28},{16,0},{20,4},{24,8},{28,12},{1,17},{... | collective-permute-start | bytes 1966088 | tf_op jit(solution)/shard_map/ppermute | solution.py:583
  109.3 1.5 collective-permute-start.27
  115.0 4.0 %embed_grad.3 = (bf16[2,320,512]{2,1,0:T(8,128)(2,1)S(1)}, bf16[2,320,512]{2,1,0:T(8,128)(2,1)S(1)}) custom-call(s32[15]{0:T(128)S(1)} %copy-done.7, bf16[4,320,384]{2,1,0:T(8,128)(2,1)S(1)} %copy-done.18, bf16[4,320,384]{2,1,0:T(8,128)(2,1)S(1)} %collective-permute-done.18.refs_1_, bf16[192,1024]{1,0:T(8,128)(2,1)S(1)} %copy-done.15, ...), custom_call_target="tpu_custom_call" | custom-call | flops 1006632960 | bytes 4063232 | tf_op jit(solution)/shard_map/embed_grad/pallas_call | solution.py:555
  119.0 4.2 %all-to-all-done.moved_ref = bf16[8,256,256]{2,1,0:T(8,128)(2,1)S(1)} async-done(((bf16[8,256,256]{2,1,0:T(8,128)(2,1)}), bf16[8,256,256]{2,1,0:T(8,128)(2,1)S(1)}, u32[]{:S(2)}, u32[]{:S(2)}) %all-to-all-start) | async-done | bytes 1048608 | tf_op jit(solution)/shard_map/all_to_all | solution.py:887
  124.5 1.9 %collective-permute-start.31 = (bf16[224,256]{1,0:T(8,128)(2,1)S(1)}, bf16[224,256]{1,0:T(8,128)(2,1)S(1)}, u32[]{:S(2)}, u32[]{:S(2)}) collective-permute-start(bf16[224,256]{1,0:T(8,128)(2,1)S(1)} %get-tuple-element.172.refs_0_), channel_id=1, source_target_pairs={{0,1},{1,0},{2,3},{3,2},{4,5},{5,4},{6,7},{7,6},{8,9},{9,8},{10,11... | collective-permute-start | bytes 344072 | tf_op jit(solution)/shard_map/ppermute | solution.py:589
  127.2 1.7 collective-permute-start.33
  128.9 7.0 %collective-permute-done.29 = bf16[2,320,512]{2,1,0:T(8,128)(2,1)} collective-permute-done((bf16[2,320,512]{2,1,0:T(8,128)(2,1)}, bf16[2,320,512]{2,1,0:T(8,128)(2,1)}, u32[]{:S(2)}, u32[]{:S(2)}) %collective-permute-start.29) | collective-permute-done | bytes 655392 | tf_op jit(solution)/shard_map/ppermute | solution.py:583
  137.2 1.5 collective-permute-start.30
  141.1 5.6 %collective-permute-done.30 = bf16[1,320,512]{2,1,0:T(8,128)(2,1)S(1)} collective-permute-done((bf16[1,320,512]{2,1,0:T(8,128)(2,1)S(1)}, bf16[1,320,512]{2,1,0:T(8,128)(2,1)S(1)}, u32[]{:S(2)}, u32[]{:S(2)}) %collective-permute-start.30) | collective-permute-done | bytes 327712 | tf_op jit(solution)/shard_map/ppermute | solution.py:583
  146.7 2.7 %collective-permute-done.28 = bf16[1,320,512]{2,1,0:T(8,128)(2,1)S(1)} collective-permute-done((bf16[1,320,512]{2,1,0:T(8,128)(2,1)S(1)}, bf16[1,320,512]{2,1,0:T(8,128)(2,1)S(1)}, u32[]{:S(2)}, u32[]{:S(2)}) %collective-permute-start.28) | collective-permute-done | bytes 327712 | tf_op jit(solution)/shard_map/ppermute | solution.py:583
  149.7 2.0 %collective-permute-start.34 = (bf16[2,80,1024]{2,1,0:T(8,128)(2,1)S(1)}, bf16[2,80,1024]{2,1,0:T(8,128)(2,1)S(1)}, u32[]{:S(2)}, u32[]{:S(2)}) collective-permute-start(bf16[2,80,1024]{2,1,0:T(8,128)(2,1)S(1)} %dynamic-slice_bitcast_fusion), channel_id=1, source_target_pairs={{0,1},{1,0},{2,3},{3,2},{4,5},{5,4},{6,7},{7,6},{8,9},{9,8},{10,11... | collective-permute-start | bytes 983048 | tf_op jit(solution)/shard_map/ppermute | solution.py:623
  152.4 2.7 %collective-permute-start.38 = (bf16[448,256]{1,0:T(8,128)(2,1)S(1)}, bf16[448,256]{1,0:T(8,128)(2,1)S(1)}, u32[]{:S(2)}, u32[]{:S(2)}) collective-permute-start(bf16[448,256]{1,0:T(8,128)(2,1)S(1)} %shard_sums.1.refs_0_), channel_id=1, source_target_pairs={{0,24},{4,28},{8,16},{12,20},{16,8},{20,12},{24,0},{28,4},{1,25},{... | collective-permute-start | bytes 688136 | tf_op jit(solution)/shard_map/ppermute | solution.py:629
  155.1 3.3 %collective-permute-done.34 = bf16[2,80,1024]{2,1,0:T(8,128)(2,1)S(1)} collective-permute-done((bf16[2,80,1024]{2,1,0:T(8,128)(2,1)S(1)}, bf16[2,80,1024]{2,1,0:T(8,128)(2,1)S(1)}, u32[]{:S(2)}, u32[]{:S(2)}) %collective-permute-start.34) | collective-permute-done | bytes 327712 | tf_op jit(solution)/shard_map/ppermute | solution.py:623
  158.6 2.6 %collective-permute-start.35 = (bf16[1,80,1024]{2,1,0:T(8,128)(2,1)S(1)}, bf16[1,80,1024]{2,1,0:T(8,128)(2,1)S(1)}, u32[]{:S(2)}, u32[]{:S(2)}) collective-permute-start(bf16[1,80,1024]{2,1,0:T(8,128)(2,1)S(1)} %constant_dynamic-slice_fusion), channel_id=1, source_target_pairs={{0,2},{1,3},{2,0},{3,1},{4,6},{5,7},{6,4},{7,5},{8,10},{9,11},{10,... | collective-permute-start | bytes 491528 | tf_op jit(solution)/shard_map/ppermute | solution.py:623
  161.1 1.6 collective-permute-done.37.refs_4_
  163.7 3.5 %collective-permute-done.35 = bf16[1,80,1024]{2,1,0:T(8,128)(2,1)S(1)} collective-permute-done((bf16[1,80,1024]{2,1,0:T(8,128)(2,1)S(1)}, bf16[1,80,1024]{2,1,0:T(8,128)(2,1)S(1)}, u32[]{:S(2)}, u32[]{:S(2)}) %collective-permute-start.35) | collective-permute-done | bytes 163872 | tf_op jit(solution)/shard_map/ppermute | solution.py:623
  168.1 2.5 %assembled.1 = (f32[1024,256]{1,0:T(8,128)}, f32[2,2,8,128,128]{4,3,2,1,0:T(8,128)}, f32[2,2,8,128]{3,2,1,0:T(8,128)}, f32[1,1024]{1,0:T(1,128)}, f32[1,1024]{1,0:T(1,128)}, /*index=5*/f32[1,256]{1,0:T(1,128)}) custom-call(s32[15]{0:T(128)S(1)} %copy-done.7, bf16[448,256]{1,0:T(8,128)(2,1)S(1)} %shard_sums.1.refs_0_, ...), custom_call_target="tpu_custom_call" | custom-call | tf_op jit(solution)/shard_map/assembled/pallas_call | solution.py:790
  (121 shorter events, 27.9 us)
Async XLA Ops:
  2.0 25.0 %copy-start.2 = (bf16[2,2,8,128,128]{4,3,2,1,0:T(8,128)(2,1)S(1)}, bf16[2,2,8,128,128]{4,3,2,1,0:T(8,128)(2,1)}, u32[]{:S(2)}) copy-start(bf16[2,2,8,128,128]{4,3,2,1,0:T(8,128)(2,1)} %w_ref.15) | copy-start | bytes 3145732
  2.0 25.0 %copy-start.4 = (bf16[3,512,256]{2,1,0:T(8,128)(2,1)S(1)}, bf16[3,512,256]{2,1,0:T(8,128)(2,1)}, u32[]{:S(2)}) copy-start(bf16[3,512,256]{2,1,0:T(8,128)(2,1)} %constant.76.clone.t_ref) | copy-start | bytes 2359300
  2.0 25.1 %copy-start.7 = (s32[15]{0:T(128)S(1)}, s32[15]{0:T(128)}, u32[]{:S(2)}) copy-start(s32[15]{0:T(128)} %concatenate.12.scal_ref) | copy-start | bytes 184
  2.0 25.1 %copy-start.16 = (f32[2,2,8,128]{3,2,1,0:T(8,128)S(1)}, f32[2,2,8,128]{3,2,1,0:T(8,128)}, u32[]{:S(2)}) copy-start(f32[2,2,8,128]{3,2,1,0:T(8,128)} %b_ref.3) | copy-start | bytes 49156
  12.0 12.2 %collective-permute-start.10 = (bf16[3,64,256]{2,1,0:T(8,128)(2,1)}, bf16[3,64,256]{2,1,0:T(8,128)(2,1)S(1)}, u32[]{:S(2)}, u32[]{:S(2)}) collective-permute-start(bf16[3,64,256]{2,1,0:T(8,128)(2,1)} %get-tuple-element.114), channel_id=1, source_target_pairs={{0,2},{1,3},{2,0},{3,1},{4,6},{5,7},{6,4},{7,5},{8,10},{9,11},{10,... | collective-permute-start | bytes 294920 | tf_op jit(solution)/shard_map/ppermute | solution.py:589
  16.1 10.9 %collective-permute-start.11 = (bf16[3,64,256]{2,1,0:T(8,128)(2,1)}, bf16[3,64,256]{2,1,0:T(8,128)(2,1)S(1)}, u32[]{:S(2)}, u32[]{:S(2)}) collective-permute-start(bf16[3,64,256]{2,1,0:T(8,128)(2,1)} %get-tuple-element.115), channel_id=1, source_target_pairs={{0,3},{1,2},{2,1},{3,0},{4,7},{5,6},{6,5},{7,4},{8,11},{9,10},{10,... | collective-permute-start | bytes 294920 | tf_op jit(solution)/shard_map/ppermute | solution.py:589
  17.5 9.5 %collective-permute-start.9 = (bf16[3,64,256]{2,1,0:T(8,128)(2,1)}, bf16[3,64,256]{2,1,0:T(8,128)(2,1)S(1)}, u32[]{:S(2)}, u32[]{:S(2)}) collective-permute-start(bf16[3,64,256]{2,1,0:T(8,128)(2,1)} %get-tuple-element.113), channel_id=1, source_target_pairs={{0,1},{1,0},{2,3},{3,2},{4,5},{5,4},{6,7},{7,6},{8,9},{9,8},{10,11... | collective-permute-start | bytes 294920 | tf_op jit(solution)/shard_map/ppermute | solution.py:589
  17.7 15.1 %collective-permute-start = (bf16[3,64,256]{2,1,0:T(8,128)(2,1)}, bf16[3,64,256]{2,1,0:T(8,128)(2,1)S(1)}, u32[]{:S(2)}, u32[]{:S(2)}) collective-permute-start(bf16[3,64,256]{2,1,0:T(8,128)(2,1)} %get-tuple-element.99), channel_id=1, source_target_pairs={{0,1},{1,0},{2,3},{3,2},{4,5},{5,4},{6,7},{7,6},{8,9},{9,8},{10,11... | collective-permute-start | bytes 294920 | tf_op jit(solution)/shard_map/ppermute | solution.py:589
  19.5 15.2 %collective-permute-start.1 = (bf16[3,64,256]{2,1,0:T(8,128)(2,1)}, bf16[3,64,256]{2,1,0:T(8,128)(2,1)S(1)}, u32[]{:S(2)}, u32[]{:S(2)}) collective-permute-start(bf16[3,64,256]{2,1,0:T(8,128)(2,1)} %get-tuple-element.100), channel_id=1, source_target_pairs={{0,2},{1,3},{2,0},{3,1},{4,6},{5,7},{6,4},{7,5},{8,10},{9,11},{10,... | collective-permute-start | bytes 294920 | tf_op jit(solution)/shard_map/ppermute | solution.py:589
  24.2 10.5 %collective-permute-start.2 = (bf16[3,64,256]{2,1,0:T(8,128)(2,1)}, bf16[3,64,256]{2,1,0:T(8,128)(2,1)S(1)}, u32[]{:S(2)}, u32[]{:S(2)}) collective-permute-start(bf16[3,64,256]{2,1,0:T(8,128)(2,1)} %get-tuple-element.101), channel_id=1, source_target_pairs={{0,3},{1,2},{2,1},{3,0},{4,7},{5,6},{6,5},{7,4},{8,11},{9,10},{10,... | collective-permute-start | bytes 294920 | tf_op jit(solution)/shard_map/ppermute | solution.py:589
  30.3 9.5 %collective-permute-start.12 = (bf16[3,64,256]{2,1,0:T(8,128)(2,1)S(1)}, bf16[3,64,256]{2,1,0:T(8,128)(2,1)S(1)}, u32[]{:S(2)}, u32[]{:S(2)}) collective-permute-start(bf16[3,64,256]{2,1,0:T(8,128)(2,1)S(1)} %get-tuple-element.120), channel_id=1, source_target_pairs={{0,1},{1,0},{2,3},{3,2},{4,5},{5,4},{6,7},{7,6},{8,9},{9,8},{10,11... | collective-permute-start | bytes 294920 | tf_op jit(solution)/shard_map/ppermute | solution.py:589
  31.3 10.6 %collective-permute-start.13 = (bf16[3,64,256]{2,1,0:T(8,128)(2,1)S(1)}, bf16[3,64,256]{2,1,0:T(8,128)(2,1)S(1)}, u32[]{:S(2)}, u32[]{:S(2)}) collective-permute-start(bf16[3,64,256]{2,1,0:T(8,128)(2,1)S(1)} %get-tuple-element.121), channel_id=1, source_target_pairs={{0,2},{1,3},{2,0},{3,1},{4,6},{5,7},{6,4},{7,5},{8,10},{9,11},{10,... | collective-permute-start | bytes 294920 | tf_op jit(solution)/shard_map/ppermute | solution.py:589
  32.8 9.0 %collective-permute-start.14 = (bf16[3,64,256]{2,1,0:T(8,128)(2,1)S(1)}, bf16[3,64,256]{2,1,0:T(8,128)(2,1)S(1)}, u32[]{:S(2)}, u32[]{:S(2)}) collective-permute-start(bf16[3,64,256]{2,1,0:T(8,128)(2,1)S(1)} %get-tuple-element.122), channel_id=1, source_target_pairs={{0,3},{1,2},{2,1},{3,0},{4,7},{5,6},{6,5},{7,4},{8,11},{9,10},{10,... | collective-permute-start | bytes 294920 | tf_op jit(solution)/shard_map/ppermute | solution.py:589
  37.1 13.6 %collective-permute-start.3 = (bf16[3,64,256]{2,1,0:T(8,128)(2,1)S(1)}, bf16[3,64,256]{2,1,0:T(8,128)(2,1)S(1)}, u32[]{:S(2)}, u32[]{:S(2)}) collective-permute-start(bf16[3,64,256]{2,1,0:T(8,128)(2,1)S(1)} %get-tuple-element.108), channel_id=1, source_target_pairs={{0,1},{1,0},{2,3},{3,2},{4,5},{5,4},{6,7},{7,6},{8,9},{9,8},{10,11... | collective-permute-start | bytes 294920 | tf_op jit(solution)/shard_map/ppermute | solution.py:589
  37.5 14.7 %collective-permute-start.4 = (bf16[3,64,256]{2,1,0:T(8,128)(2,1)S(1)}, bf16[3,64,256]{2,1,0:T(8,128)(2,1)S(1)}, u32[]{:S(2)}, u32[]{:S(2)}) collective-permute-start(bf16[3,64,256]{2,1,0:T(8,128)(2,1)S(1)} %get-tuple-element.109), channel_id=1, source_target_pairs={{0,2},{1,3},{2,0},{3,1},{4,6},{5,7},{6,4},{7,5},{8,10},{9,11},{10,... | collective-permute-start | bytes 294920 | tf_op jit(solution)/shard_map/ppermute | solution.py:589
  39.7 12.4 %collective-permute-start.5 = (bf16[3,64,256]{2,1,0:T(8,128)(2,1)S(1)}, bf16[3,64,256]{2,1,0:T(8,128)(2,1)S(1)}, u32[]{:S(2)}, u32[]{:S(2)}) collective-permute-start(bf16[3,64,256]{2,1,0:T(8,128)(2,1)S(1)} %get-tuple-element.110), channel_id=1, source_target_pairs={{0,3},{1,2},{2,1},{3,0},{4,7},{5,6},{6,5},{7,4},{8,11},{9,10},{10,... | collective-permute-start | bytes 294920 | tf_op jit(solution)/shard_map/ppermute | solution.py:589
  42.8 13.2 %collective-permute-start.15 = (bf16[3,64,256]{2,1,0:T(8,128)(2,1)S(1)}, bf16[3,64,256]{2,1,0:T(8,128)(2,1)S(1)}, u32[]{:S(2)}, u32[]{:S(2)}) collective-permute-start(bf16[3,64,256]{2,1,0:T(8,128)(2,1)S(1)} %get-tuple-element.126.refs_2_.refs_0_.res_ref), channel_id=1, source_target_pairs={{0,1},{1,0},{2,3},{3,2},{4,5},{5,4},{6,7},{7,6},{8,9},{9,8},{10,11... | collective-permute-start | bytes 294920 | tf_op jit(solution)/shard_map/ppermute | solution.py:589
  49.7 10.8 %collective-permute-start.16 = (bf16[3,64,256]{2,1,0:T(8,128)(2,1)S(1)}, bf16[3,64,256]{2,1,0:T(8,128)(2,1)S(1)}, u32[]{:S(2)}, u32[]{:S(2)}) collective-permute-start(bf16[3,64,256]{2,1,0:T(8,128)(2,1)S(1)} %get-tuple-element.126.refs_2_.refs_0_.res_ref), channel_id=1, source_target_pairs={{0,2},{1,3},{2,0},{3,1},{4,6},{5,7},{6,4},{7,5},{8,10},{9,11},{10,... | collective-permute-start | bytes 294920 | tf_op jit(solution)/shard_map/ppermute | solution.py:589
  50.7 9.9 %collective-permute-start.17 = (bf16[3,64,256]{2,1,0:T(8,128)(2,1)S(1)}, bf16[3,64,256]{2,1,0:T(8,128)(2,1)S(1)}, u32[]{:S(2)}, u32[]{:S(2)}) collective-permute-start(bf16[3,64,256]{2,1,0:T(8,128)(2,1)S(1)} %get-tuple-element.126.refs_2_.refs_0_.res_ref), channel_id=1, source_target_pairs={{0,3},{1,2},{2,1},{3,0},{4,7},{5,6},{6,5},{7,4},{8,11},{9,10},{10,... | collective-permute-start | bytes 294920 | tf_op jit(solution)/shard_map/ppermute | solution.py:589
  53.1 10.4 %collective-permute-start.6 = (bf16[3,64,256]{2,1,0:T(8,128)(2,1)S(1)}, bf16[3,64,256]{2,1,0:T(8,128)(2,1)S(1)}, u32[]{:S(2)}, u32[]{:S(2)}) collective-permute-start(bf16[3,64,256]{2,1,0:T(8,128)(2,1)S(1)} %get-tuple-element.111.refs_3_.refs_0_.res_ref), channel_id=1, source_target_pairs={{0,1},{1,0},{2,3},{3,2},{4,5},{5,4},{6,7},{7,6},{8,9},{9,8},{10,11... | collective-permute-start | bytes 294920 | tf_op jit(solution)/shard_map/ppermute | solution.py:589
  54.2 13.6 %collective-permute-start.7 = (bf16[3,64,256]{2,1,0:T(8,128)(2,1)S(1)}, bf16[3,64,256]{2,1,0:T(8,128)(2,1)S(1)}, u32[]{:S(2)}, u32[]{:S(2)}) collective-permute-start(bf16[3,64,256]{2,1,0:T(8,128)(2,1)S(1)} %get-tuple-element.111.refs_3_.refs_0_.res_ref), channel_id=1, source_target_pairs={{0,2},{1,3},{2,0},{3,1},{4,6},{5,7},{6,4},{7,5},{8,10},{9,11},{10,... | collective-permute-start | bytes 294920 | tf_op jit(solution)/shard_map/ppermute | solution.py:589
  56.0 11.8 %collective-permute-start.8 = (bf16[3,64,256]{2,1,0:T(8,128)(2,1)S(1)}, bf16[3,64,256]{2,1,0:T(8,128)(2,1)S(1)}, u32[]{:S(2)}, u32[]{:S(2)}) collective-permute-start(bf16[3,64,256]{2,1,0:T(8,128)(2,1)S(1)} %get-tuple-element.111.refs_3_.refs_0_.res_ref), channel_id=1, source_target_pairs={{0,3},{1,2},{2,1},{3,0},{4,7},{5,6},{6,5},{7,4},{8,11},{9,10},{10,... | collective-permute-start | bytes 294920 | tf_op jit(solution)/shard_map/ppermute | solution.py:589
  70.9 24.7 %collective-permute-start.18 = (bf16[4,320,384]{2,1,0:T(8,128)(2,1)}, bf16[4,320,384]{2,1,0:T(8,128)(2,1)S(1)}, u32[]{:S(2)}, u32[]{:S(2)}) collective-permute-start(bf16[4,320,384]{2,1,0:T(8,128)(2,1)} %get-tuple-element.137), channel_id=1, source_target_pairs={{0,4},{4,0},{8,12},{12,8},{16,20},{20,16},{24,28},{28,24},{1,5},{5... | collective-permute-start | bytes 2949128 | tf_op jit(solution)/shard_map/ppermute | solution.py:583
  70.9 5.3 %collective-permute-start.22 = (bf16[3,64,256]{2,1,0:T(8,128)(2,1)S(1)}, bf16[3,64,256]{2,1,0:T(8,128)(2,1)S(1)}, u32[]{:S(2)}, u32[]{:S(2)}) collective-permute-start(bf16[3,64,256]{2,1,0:T(8,128)(2,1)S(1)} %get-tuple-element.145), channel_id=1, source_target_pairs={{0,1},{1,0},{2,3},{3,2},{4,5},{5,4},{6,7},{7,6},{8,9},{9,8},{10,11... | collective-permute-start | bytes 294920 | tf_op jit(solution)/shard_map/ppermute | solution.py:589
  72.8 10.8 %collective-permute-start.23 = (bf16[3,64,256]{2,1,0:T(8,128)(2,1)S(1)}, bf16[3,64,256]{2,1,0:T(8,128)(2,1)S(1)}, u32[]{:S(2)}, u32[]{:S(2)}) collective-permute-start(bf16[3,64,256]{2,1,0:T(8,128)(2,1)S(1)} %get-tuple-element.146), channel_id=1, source_target_pairs={{0,2},{1,3},{2,0},{3,1},{4,6},{5,7},{6,4},{7,5},{8,10},{9,11},{10,... | collective-permute-start | bytes 294920 | tf_op jit(solution)/shard_map/ppermute | solution.py:589
  73.7 12.1 %collective-permute-start.24 = (bf16[3,64,256]{2,1,0:T(8,128)(2,1)S(1)}, bf16[3,64,256]{2,1,0:T(8,128)(2,1)S(1)}, u32[]{:S(2)}, u32[]{:S(2)}) collective-permute-start(bf16[3,64,256]{2,1,0:T(8,128)(2,1)S(1)} %get-tuple-element.147), channel_id=1, source_target_pairs={{0,3},{1,2},{2,1},{3,0},{4,7},{5,6},{6,5},{7,4},{8,11},{9,10},{10,... | collective-permute-start | bytes 294920 | tf_op jit(solution)/shard_map/ppermute | solution.py:589
  75.4 12.0 %collective-permute-start.19 = (bf16[3,64,256]{2,1,0:T(8,128)(2,1)S(1)}, bf16[3,64,256]{2,1,0:T(8,128)(2,1)S(1)}, u32[]{:S(2)}, u32[]{:S(2)}) collective-permute-start(bf16[3,64,256]{2,1,0:T(8,128)(2,1)S(1)} %get-tuple-element.140), channel_id=1, source_target_pairs={{0,1},{1,0},{2,3},{3,2},{4,5},{5,4},{6,7},{7,6},{8,9},{9,8},{10,11... | collective-permute-start | bytes 294920 | tf_op jit(solution)/shard_map/ppermute | solution.py:589
  76.3 15.7 %collective-permute-start.20 = (bf16[3,64,256]{2,1,0:T(8,128)(2,1)S(1)}, bf16[3,64,256]{2,1,0:T(8,128)(2,1)S(1)}, u32[]{:S(2)}, u32[]{:S(2)}) collective-permute-start(bf16[3,64,256]{2,1,0:T(8,128)(2,1)S(1)} %get-tuple-element.141), channel_id=1, source_target_pairs={{0,2},{1,3},{2,0},{3,1},{4,6},{5,7},{6,4},{7,5},{8,10},{9,11},{10,... | collective-permute-start | bytes 294920 | tf_op jit(solution)/shard_map/ppermute | solution.py:589
  83.5 8.4 %collective-permute-start.21 = (bf16[3,64,256]{2,1,0:T(8,128)(2,1)S(1)}, bf16[3,64,256]{2,1,0:T(8,128)(2,1)S(1)}, u32[]{:S(2)}, u32[]{:S(2)}) collective-permute-start(bf16[3,64,256]{2,1,0:T(8,128)(2,1)S(1)} %get-tuple-element.142), channel_id=1, source_target_pairs={{0,3},{1,2},{2,1},{3,0},{4,7},{5,6},{6,5},{7,4},{8,11},{9,10},{10,... | collective-permute-start | bytes 294920 | tf_op jit(solution)/shard_map/ppermute | solution.py:589
  87.3 7.1 %collective-permute-start.26 = (bf16[192,1024]{1,0:T(8,128)(2,1)S(1)}, bf16[192,1024]{1,0:T(8,128)(2,1)S(1)}, u32[]{:S(2)}, u32[]{:S(2)}) collective-permute-start(bf16[192,1024]{1,0:T(8,128)(2,1)S(1)} %get-tuple-element.148.refs_3_), channel_id=1, source_target_pairs={{0,4},{4,0},{8,12},{12,8},{16,20},{20,16},{24,28},{28,24},{1,5},{5... | collective-permute-start | bytes 1179656 | tf_op jit(solution)/shard_map/ppermute | solution.py:583
  93.6 1.9 %collective-permute-start.25 = (bf16[192,1024]{1,0:T(8,128)(2,1)S(1)}, bf16[192,1024]{1,0:T(8,128)(2,1)}, u32[]{:S(2)}, u32[]{:S(2)}) collective-permute-start(bf16[192,1024]{1,0:T(8,128)(2,1)S(1)} %get-tuple-element.143.refs_2_), channel_id=1, source_target_pairs={{0,4},{4,0},{8,12},{12,8},{16,20},{20,16},{24,28},{28,24},{1,5},{5... | collective-permute-start | bytes 1179656 | tf_op jit(solution)/shard_map/ppermute | solution.py:583
  103.4 19.8 %all-to-all-start = ((bf16[8,256,256]{2,1,0:T(8,128)(2,1)}), bf16[8,256,256]{2,1,0:T(8,128)(2,1)S(1)}, u32[]{:S(2)}, u32[]{:S(2)}) async-start(bf16[8,256,256]{2,1,0:T(8,128)(2,1)} %packed.1), calls=%async_computation | async-start | bytes 2097152 | tf_op jit(solution)/shard_map/all_to_all | solution.py:887
  107.3 28.6 %collective-permute-start.29 = (bf16[2,320,512]{2,1,0:T(8,128)(2,1)}, bf16[2,320,512]{2,1,0:T(8,128)(2,1)}, u32[]{:S(2)}, u32[]{:S(2)}) collective-permute-start(bf16[2,320,512]{2,1,0:T(8,128)(2,1)} %get-tuple-element.156), channel_id=1, source_target_pairs={{0,16},{4,20},{8,24},{12,28},{16,0},{20,4},{24,8},{28,12},{1,17},{... | collective-permute-start | bytes 1966088 | tf_op jit(solution)/shard_map/ppermute | solution.py:583
  109.3 29.4 %collective-permute-start.27 = (bf16[2,320,512]{2,1,0:T(8,128)(2,1)}, bf16[2,320,512]{2,1,0:T(8,128)(2,1)}, u32[]{:S(2)}, u32[]{:S(2)}) collective-permute-start(bf16[2,320,512]{2,1,0:T(8,128)(2,1)} %get-tuple-element.155), channel_id=1, source_target_pairs={{0,8},{4,12},{8,0},{12,4},{16,24},{20,28},{24,16},{28,20},{1,9},{5... | collective-permute-start | bytes 1966088 | tf_op jit(solution)/shard_map/ppermute | solution.py:583
  124.5 16.0 %collective-permute-start.31 = (bf16[224,256]{1,0:T(8,128)(2,1)S(1)}, bf16[224,256]{1,0:T(8,128)(2,1)S(1)}, u32[]{:S(2)}, u32[]{:S(2)}) collective-permute-start(bf16[224,256]{1,0:T(8,128)(2,1)S(1)} %get-tuple-element.172.refs_0_), channel_id=1, source_target_pairs={{0,1},{1,0},{2,3},{3,2},{4,5},{5,4},{6,7},{7,6},{8,9},{9,8},{10,11... | collective-permute-start | bytes 344072 | tf_op jit(solution)/shard_map/ppermute | solution.py:589
  126.4 14.1 %collective-permute-start.32 = (bf16[224,256]{1,0:T(8,128)(2,1)S(1)}, bf16[224,256]{1,0:T(8,128)(2,1)S(1)}, u32[]{:S(2)}, u32[]{:S(2)}) collective-permute-start(bf16[224,256]{1,0:T(8,128)(2,1)S(1)} %get-tuple-element.172.refs_0_), channel_id=1, source_target_pairs={{0,2},{1,3},{2,0},{3,1},{4,6},{5,7},{6,4},{7,5},{8,10},{9,11},{10,... | collective-permute-start | bytes 344072 | tf_op jit(solution)/shard_map/ppermute | solution.py:589
  127.2 13.3 %collective-permute-start.33 = (bf16[224,256]{1,0:T(8,128)(2,1)S(1)}, bf16[224,256]{1,0:T(8,128)(2,1)S(1)}, u32[]{:S(2)}, u32[]{:S(2)}) collective-permute-start(bf16[224,256]{1,0:T(8,128)(2,1)S(1)} %get-tuple-element.172.refs_0_), channel_id=1, source_target_pairs={{0,3},{1,2},{2,1},{3,0},{4,7},{5,6},{6,5},{7,4},{8,11},{9,10},{10,... | collective-permute-start | bytes 344072 | tf_op jit(solution)/shard_map/ppermute | solution.py:589
  137.2 9.5 %collective-permute-start.30 = (bf16[1,320,512]{2,1,0:T(8,128)(2,1)S(1)}, bf16[1,320,512]{2,1,0:T(8,128)(2,1)S(1)}, u32[]{:S(2)}, u32[]{:S(2)}) collective-permute-start(bf16[1,320,512]{2,1,0:T(8,128)(2,1)S(1)} %slice.21), channel_id=1, source_target_pairs={{0,8},{4,12},{8,0},{12,4},{16,24},{20,28},{24,16},{28,20},{1,9},{5... | collective-permute-start | bytes 983048 | tf_op jit(solution)/shard_map/ppermute | solution.py:583
  140.0 9.5 %collective-permute-start.28 = (bf16[1,320,512]{2,1,0:T(8,128)(2,1)S(1)}, bf16[1,320,512]{2,1,0:T(8,128)(2,1)S(1)}, u32[]{:S(2)}, u32[]{:S(2)}) collective-permute-start(bf16[1,320,512]{2,1,0:T(8,128)(2,1)S(1)} %slice_bitcast_fusion), channel_id=1, source_target_pairs={{0,16},{4,20},{8,24},{12,28},{16,0},{20,4},{24,8},{28,12},{1,17},{... | collective-permute-start | bytes 983048 | tf_op jit(solution)/shard_map/ppermute | solution.py:583
  149.7 8.7 %collective-permute-start.34 = (bf16[2,80,1024]{2,1,0:T(8,128)(2,1)S(1)}, bf16[2,80,1024]{2,1,0:T(8,128)(2,1)S(1)}, u32[]{:S(2)}, u32[]{:S(2)}) collective-permute-start(bf16[2,80,1024]{2,1,0:T(8,128)(2,1)S(1)} %dynamic-slice_bitcast_fusion), channel_id=1, source_target_pairs={{0,1},{1,0},{2,3},{3,2},{4,5},{5,4},{6,7},{7,6},{8,9},{9,8},{10,11... | collective-permute-start | bytes 983048 | tf_op jit(solution)/shard_map/ppermute | solution.py:623
  151.6 9.5 %collective-permute-start.36 = (bf16[448,256]{1,0:T(8,128)(2,1)S(1)}, bf16[448,256]{1,0:T(8,128)(2,1)S(1)}, u32[]{:S(2)}, u32[]{:S(2)}) collective-permute-start(bf16[448,256]{1,0:T(8,128)(2,1)S(1)} %shard_sums.1.refs_0_), channel_id=1, source_target_pairs={{0,8},{4,12},{8,0},{12,4},{16,24},{20,28},{24,16},{28,20},{1,9},{5... | collective-permute-start | bytes 688136 | tf_op jit(solution)/shard_map/ppermute | solution.py:629
  151.9 10.8 %collective-permute-start.37 = (bf16[448,256]{1,0:T(8,128)(2,1)S(1)}, bf16[448,256]{1,0:T(8,128)(2,1)S(1)}, u32[]{:S(2)}, u32[]{:S(2)}) collective-permute-start(bf16[448,256]{1,0:T(8,128)(2,1)S(1)} %shard_sums.1.refs_0_), channel_id=1, source_target_pairs={{0,16},{4,20},{8,24},{12,28},{16,0},{20,4},{24,8},{28,12},{1,17},{... | collective-permute-start | bytes 688136 | tf_op jit(solution)/shard_map/ppermute | solution.py:629
  152.4 10.3 %collective-permute-start.38 = (bf16[448,256]{1,0:T(8,128)(2,1)S(1)}, bf16[448,256]{1,0:T(8,128)(2,1)S(1)}, u32[]{:S(2)}, u32[]{:S(2)}) collective-permute-start(bf16[448,256]{1,0:T(8,128)(2,1)S(1)} %shard_sums.1.refs_0_), channel_id=1, source_target_pairs={{0,24},{4,28},{8,16},{12,20},{16,8},{20,12},{24,0},{28,4},{1,25},{... | collective-permute-start | bytes 688136 | tf_op jit(solution)/shard_map/ppermute | solution.py:629
  158.6 8.7 %collective-permute-start.35 = (bf16[1,80,1024]{2,1,0:T(8,128)(2,1)S(1)}, bf16[1,80,1024]{2,1,0:T(8,128)(2,1)S(1)}, u32[]{:S(2)}, u32[]{:S(2)}) collective-permute-start(bf16[1,80,1024]{2,1,0:T(8,128)(2,1)S(1)} %constant_dynamic-slice_fusion), channel_id=1, source_target_pairs={{0,2},{1,3},{2,0},{3,1},{4,6},{5,7},{6,4},{7,5},{8,10},{9,11},{10,... | collective-permute-start | bytes 491528 | tf_op jit(solution)/shard_map/ppermute | solution.py:623
  162.7 5.3 %collective-permute-start.39 = (bf16[448,256]{1,0:T(8,128)(2,1)S(1)}, bf16[448,256]{1,0:T(8,128)(2,1)S(1)}, u32[]{:S(2)}, u32[]{:S(2)}) collective-permute-start(bf16[448,256]{1,0:T(8,128)(2,1)S(1)} %shard_sums.1.refs_0_), channel_id=1, source_target_pairs={{0,4},{4,0},{8,12},{12,8},{16,20},{20,16},{24,28},{28,24},{1,5},{5... | collective-permute-start | bytes 688136 | tf_op jit(solution)/shard_map/ppermute | solution.py:583
  162.7 5.3 %collective-permute-start.40 = (bf16[448,256]{1,0:T(8,128)(2,1)S(1)}, bf16[448,256]{1,0:T(8,128)(2,1)S(1)}, u32[]{:S(2)}, u32[]{:S(2)}) collective-permute-start(bf16[448,256]{1,0:T(8,128)(2,1)S(1)} %collective-permute-done.36.refs_2_), channel_id=1, source_target_pairs={{0,4},{4,0},{8,12},{12,8},{16,20},{20,16},{24,28},{28,24},{1,5},{5... | collective-permute-start | bytes 688136 | tf_op jit(solution)/shard_map/ppermute | solution.py:583
  163.2 4.8 %collective-permute-start.41 = (bf16[448,256]{1,0:T(8,128)(2,1)S(1)}, bf16[448,256]{1,0:T(8,128)(2,1)S(1)}, u32[]{:S(2)}, u32[]{:S(2)}) collective-permute-start(bf16[448,256]{1,0:T(8,128)(2,1)S(1)} %collective-permute-done.37.refs_4_), channel_id=1, source_target_pairs={{0,4},{4,0},{8,12},{12,8},{16,20},{20,16},{24,28},{28,24},{1,5},{5... | collective-permute-start | bytes 688136 | tf_op jit(solution)/shard_map/ppermute | solution.py:583
  163.2 4.8 %collective-permute-start.42 = (bf16[448,256]{1,0:T(8,128)(2,1)S(1)}, bf16[448,256]{1,0:T(8,128)(2,1)S(1)}, u32[]{:S(2)}, u32[]{:S(2)}) collective-permute-start(bf16[448,256]{1,0:T(8,128)(2,1)S(1)} %collective-permute-done.38.refs_6_), channel_id=1, source_target_pairs={{0,4},{4,0},{8,12},{12,8},{16,20},{20,16},{24,28},{28,24},{1,5},{5... | collective-permute-start | bytes 688136 | tf_op jit(solution)/shard_map/ppermute | solution.py:583
  (18 other events, 131.1 us)
